TPU v7x, 32 devices: a whole 2x2x4 slice. The times are simulated.
32 devices in a mesh: replica: 4 (over y, x), fsdp: 8 (over z, core).
Axes of the slice: x: 2, y: 2, z: 4, core: 2. Of those that a mesh axis runs over, the one named last changes fastest.
Arguments:
- tokens: bfloat16 [4, 8192, 4096], P('replica', 'fsdp'), may hold values from -6 to 6
- norm_gain: float32 [4096], replicated, may hold values from 0.25 to 1.75
- value_weight: bfloat16 [4, 4096, 512], P('replica', 'fsdp'), may hold values from -0.09375 to 0.09375
- output_weight: bfloat16 [4, 4096, 512], P('replica', 'fsdp'), may hold values from -0.25 to 0.25
- out_cotangent: bfloat16 [4, 8192, 4096], P('replica', 'fsdp'), may hold values from -0.21875 to 0.21875
- base_params: bfloat16 [65536, 128], P('fsdp'), may hold values from -6 to 6
- outer_momentum: float32 [65536, 128], P('fsdp'), may hold values from -4 to 4
- delta_values: bfloat16 [4, 65536, 128], P('replica', 'fsdp'), may hold values from -8 to 8
- delta_exponents: int32 [4, 65536], P('replica', 'fsdp'), may hold values from -3 to 1
Outputs:
- value_grad: float32 [4, 4096, 512], P('replica', 'fsdp')
- output_grad: float32 [4, 4096, 512], P('replica', 'fsdp')
- new_base: bfloat16 [65536, 128], P('fsdp')
- new_momentum: float32 [65536, 128], P('fsdp')
All inputs are finite; a program needn't handle non-finite values.
Results may differ from a plain program's by a relative error of at most 0.015.
Values may be sent and summed in bfloat16 or wider, within the bound.
No kernel may reach another device: no remote copies, remote signals or barrier semaphores. Data moves between devices by JAX's collectives and lax.ppermute only.
A program may use at most 128 MiB of HBM per device.

v0:
```python
import jax
import jax.numpy as jnp
from jax import lax
from jax.sharding import PartitionSpec as P


def nesterov(delta, base_part, momentum_part):
    momentum_next = 0.9 * momentum_part + delta
    base_next = (base_part.astype(jnp.float32) - 0.7 * (delta + 0.9 * momentum_next)).astype(
        jnp.bfloat16
    )
    return (base_next, momentum_next)


def per_device(
    tokens,
    norm_gain,
    value_weight,
    output_weight,
    out_cotangent,
    base_params,
    outer_momentum,
    delta_values,
    delta_exponents,
):
    replicas = lax.axis_size("replica")
    xf = tokens[0].astype(jnp.float32)
    scale = lax.rsqrt(jnp.mean(xf * xf, axis=1, keepdims=True) + 1e-05)
    normed = (xf * scale * norm_gain).astype(jnp.bfloat16)
    cotangent = out_cotangent[0]
    normed_cols = normed
    cot_cols = cotangent
    first = jnp.dot(
        normed_cols,
        lax.all_gather(value_weight[0], "fsdp", axis=0, tiled=True),
        preferred_element_type=jnp.float32,
    )
    second = jnp.dot(
        cot_cols,
        lax.all_gather(output_weight[0], "fsdp", axis=0, tiled=True),
        preferred_element_type=jnp.float32,
    )
    values = first.astype(jnp.bfloat16)
    value_cot = second.astype(jnp.bfloat16)
    cot_cols = cotangent
    output_grad = lax.psum_scatter(
        lax.dot_general(
            cot_cols, values, (((0,), (0,)), ((), ())), preferred_element_type=jnp.float32
        ).astype(jnp.bfloat16),
        "fsdp",
        scatter_dimension=0,
        tiled=True,
    ).astype(jnp.float32)
    normed_cols = normed
    value_grad = lax.psum_scatter(
        lax.dot_general(
            normed_cols, value_cot, (((0,), (0,)), ((), ())), preferred_element_type=jnp.float32
        ).astype(jnp.bfloat16),
        "fsdp",
        scatter_dimension=0,
        tiled=True,
    ).astype(jnp.float32)
    scaled = (
        delta_values[0].astype(jnp.float32)
        * jnp.exp2(delta_exponents[0].astype(jnp.float32))[:, None]
    )
    delta = lax.psum(scaled.astype(jnp.bfloat16), "replica").astype(jnp.float32) * (1.0 / replicas)
    new_base, new_momentum = nesterov(delta, base_params, outer_momentum)
    return (value_grad[None], output_grad[None], new_base, new_momentum)


def solution(mesh):
    return jax.shard_map(
        per_device,
        mesh=mesh,
        in_specs=(
            P("replica", "fsdp", None),
            P(),
            P("replica", "fsdp", None),
            P("replica", "fsdp", None),
            P("replica", "fsdp", None),
            P("fsdp", None),
            P("fsdp", None),
            P("replica", "fsdp", None),
            P("replica", "fsdp"),
        ),
        out_specs=(
            P("replica", "fsdp", None),
            P("replica", "fsdp", None),
            P("fsdp", None),
            P("fsdp", None),
        ),
        check_vma=False,
    )
```

profile of v0, /device:TPU:0, one launch (start us, length us, event | category | flops | bytes accessed | tf_op | source)
XLA Modules:
  0.0 218.5 jit_solution(17830927267866350845)
XLA Ops:
  8.0 0.0 all-gather.7.cloned.1.call-start
  8.0 0.7 all-gather.7.cloned.1.call-update
  8.7 0.0 all-gather.5.cloned.1.call-start
  8.8 0.7 all-gather.5.cloned.1.call-update
  9.5 0.0 all-reduce.2.cloned.1.call-start
  9.5 0.8 multiply_exponential_fusion
  10.3 3.4 %fusion.13 = bf16[8192,128]{1,0:T(8,128)(2,1)} fusion(bf16[1,8192,128]{2,1,0:T(8,128)(2,1)} %param.16, f32[8192]{0:T(1024)S(1)} %bitcast.49), kind=kLoop, calls=%fused_computation.13 | loop fusion | flops 3145728 | bytes 4227072 | tf_op jit(solution)/shard_map/convert_element_type | solution.py:67
  13.8 0.0 all-reduce.2.cloned.1.call-update
  13.8 0.0 copy-start.1
  13.8 0.0 reduce-scatter.5.cloned.1.call-start
  13.9 5.1 %fusion = f32[1024]{0:T(1024)S(1)} fusion(bf16[1,1024,4096]{2,1,0:T(8,128)(2,1)} %param.9), kind=kLoop, calls=%fused_computation.2 | loop fusion | flops 12581888 | bytes 8392704 | tf_op jit(solution)/shard_map/reduce_sum | solution.py:28
  19.0 41.4 %all-gather.7.cloned.1.call-done = bf16[1,4096,512]{2,1,0:T(8,128)(2,1)} async-done(((bf16[1,512,512]{2,1,0:T(8,128)(2,1)}), bf16[1,4096,512]{2,1,0:T(8,128)(2,1)}) %all-gather.7.cloned.1.call-update) | async-done | bytes 4194320 | tf_op jit(solution)/shard_map/all_gather | solution.py:35
  60.3 0.0 copy-done.1
  60.3 18.1 %fusion.10 = bf16[4096,512]{0,1:T(8,128)(2,1)} fusion(bf16[1,1024,4096]{2,1,0:T(8,128)(2,1)} %param.13, bf16[1,4096,512]{2,1,0:T(8,128)(2,1)} %all-gather.7.cloned.1.call-done, bf16[1,1024,4096]{2,1,0:T(8,128)(2,1)} %param.9, f32[4096]{0:T(1024)S(1)} %copy-done.1, f32[1024]{0:T(1024)S(1)} %add_rsqrt_fusion), kind=kOutput, calls=%fused_computation.11 | convolution fusion | flops 8609333248 | bytes 25186304 | tf_op jit(solution)/shard_map/dot_general | solution.py:47
  78.4 0.0 reduce-scatter.5.cloned.1.call-update
  78.4 0.2 reduce-scatter.3.cloned.1.call-start
  78.6 29.2 %all-gather.5.cloned.1.call-done = bf16[1,4096,512]{2,1,0:T(8,128)(2,1)} async-done(((bf16[1,512,512]{2,1,0:T(8,128)(2,1)}), bf16[1,4096,512]{2,1,0:T(8,128)(2,1)}) %all-gather.5.cloned.1.call-update) | async-done | bytes 4194320 | tf_op jit(solution)/shard_map/all_gather | solution.py:40
  107.8 18.2 %convolution_convert_fusion = bf16[4096,512]{1,0:T(8,128)(2,1)} fusion(bf16[1,1024,4096]{2,1,0:T(8,128)(2,1)} %param.9, f32[4096]{0:T(1024)S(1)} %copy-done.1, f32[1024]{0:T(1024)S(1)} %add_rsqrt_fusion, bf16[1,4096,512]{2,1,0:T(8,128)(2,1)} %all-gather.5.cloned.1.call-done, bf16[1,1024,4096]{2,1,0:T(8,128)(2,1)} %param.13), kind=kOutput, calls=%fused_computation.10 | convolution fusion | flops 8609333248 | bytes 25186304 | tf_op jit(solution)/shard_map/dot_general | solution.py:56
  126.0 0.0 copy-start
  126.0 0.0 reduce-scatter.3.cloned.1.call-update
  126.0 0.0 all-reduce.2.cloned.1.call-done
  126.1 1.6 copy-done
  127.6 6.9 %subtract_convert_fusion = (bf16[8192,128]{1,0:T(8,128)(2,1)}, f32[8192,128]{1,0:T(8,128)}) fusion(bf16[8192,128]{1,0:T(8,128)(2,1)} %all-reduce.2.cloned.1.call-done, bf16[8192,128]{1,0:T(8,128)(2,1)S(1)} %copy-done, f32[8192,128]{1,0:T(8,128)} %param.15), kind=kLoop, calls=%fused_computation.17 | loop fusion | flops 10485760 | bytes 14680064 | tf_op jit(solution)/shard_map/convert_element_type | solution.py:9
  134.6 24.3 %reduce-scatter.5.cloned.1.call-done = bf16[512,512]{0,1:T(8,128)(2,1)} async-done(((bf16[4096,512]{0,1:T(8,128)(2,1)}), bf16[512,512]{0,1:T(8,128)(2,1)}) %reduce-scatter.5.cloned.1.call-update) | async-done | bytes 524304 | tf_op jit(solution)/shard_map/reduce_scatter | solution.py:46
  158.9 1.2 bitcast_convert_fusion
  160.0 1.3 copy.13
  161.4 47.8 %reduce-scatter.3.cloned.1.call-done = bf16[512,512]{1,0:T(8,128)(2,1)} async-done(((bf16[4096,512]{1,0:T(8,128)(2,1)}), bf16[512,512]{1,0:T(8,128)(2,1)}) %reduce-scatter.3.cloned.1.call-update) | async-done | bytes 524304 | tf_op jit(solution)/shard_map/reduce_scatter | solution.py:55
  209.2 2.1 bitcast_convert_fusion.1
  (1 shorter events, 0.0 us)
Async XLA Ops:
  8.0 52.3 %all-gather.7.cloned.1.call-start = ((), (), s32[]{:S(2)}) async-start(), calls=%async_computation.6 | async-start | bytes 4718592 | tf_op jit(solution)/shard_map/all_gather | solution.py:35
  8.7 99.1 %all-gather.5.cloned.1.call-start = ((), (), s32[]{:S(2)}) async-start(), calls=%async_computation.5 | async-start | bytes 4718592 | tf_op jit(solution)/shard_map/all_gather | solution.py:40
  9.5 116.6 %all-reduce.2.cloned.1.call-start = ((), (), s32[]{:S(2)}) async-start(), calls=%async_computation.4 | async-start | bytes 4194304 | tf_op jit(solution)/shard_map/psum | solution.py:67
  13.8 46.5 %copy-start.1 = (f32[4096]{0:T(1024)S(1)}, f32[4096]{0:T(1024)}, u32[]{:S(2)}) copy-start(f32[4096]{0:T(1024)} %param.10) | copy-start | bytes 49156
  13.8 145.1 %reduce-scatter.5.cloned.1.call-start = ((), (), s32[]{:S(2)}) async-start(), calls=%async_computation.3 | async-start | bytes 4718592 | tf_op jit(solution)/shard_map/reduce_scatter | solution.py:46
  78.4 130.8 %reduce-scatter.3.cloned.1.call-start = ((), (), s32[]{:S(2)}) async-start(), calls=%async_computation.2 | async-start | bytes 4718592 | tf_op jit(solution)/shard_map/reduce_scatter | solution.py:55
  126.0 1.6 copy-start
Sparse Core Ops, SparseCore 0:
  10.4 49.8 all-gather.6
  61.9 45.8 all-gather.4
  110.1 48.7 reduce-scatter.4
  161.0 48.1 reduce-scatter.2
Sparse Core Ops, SparseCore 1:
  13.9 71.9 all-reduce.1
where the time goes:
time: 219 us; the launch traced here: 218 us
  waiting for transfers between devices  144 us (66%)
  matrix products  36.2 us (17%)
  other arithmetic  19.6 us (9%)
  between operations  15.2 us (7%)
  local copies, waits for them, and re-layouts  2.89 us (1%)
    reduce_scatter x1, waiting for transfers between devices, per_device(): lax.psum_scatter(lax.dot_general(normed_cols, value_cot, (((0,), (0,)), (...  47.8 us
    all_gather x1, waiting for transfers between devices, per_device(): lax.all_gather(value_weight[0], 'fsdp', axis=0, tiled=True)  41.4 us
    all_gather x1, waiting for transfers between devices, per_device(): lax.all_gather(output_weight[0], 'fsdp', axis=0, tiled=True)  29.2 us
    reduce_scatter x1, waiting for transfers between devices, per_device(): lax.psum_scatter(lax.dot_general(cot_cols, values, (((0,), (0,)), ((), ()...  24.3 us
    dot_general x1, matrix products, per_device(): lax.dot_general(normed_cols, value_cot, (((0,), (0,)), ((), ())), preferr...  18.2 us
    dot_general x1, matrix products, per_device(): lax.dot_general(cot_cols, values, (((0,), (0,)), ((), ())), preferred_ele...  18.1 us
    convert_element_type x1, other arithmetic, nesterov(): (base_part.astype(jnp.float32) - 0.7 * (delta + 0.9 * momentum_next)).ast...  6.95 us
    reduce_sum x1, other arithmetic, per_device(): scale = lax.rsqrt(jnp.mean(xf * xf, axis=1, keepdims=True) + 1e-05)  5.07 us
  transfers between devices with their start and end apart: 5, of which 4 were waited for; matrix products, arithmetic and copies ran while one was open for 25% of the time, Pallas kernels for 0%

commit v1 on v0

v1 whole, which is shorter than its diff:
```python
import jax
import jax.numpy as jnp
from jax import lax
from jax.experimental import pallas as pl
from jax.experimental.pallas import tpu as pltpu
from jax.sharding import PartitionSpec as P

CHUNKS = 2
ROW_TILE = 128


def nesterov(delta, base_part, momentum_part):
    momentum_next = 0.9 * momentum_part + delta
    base_next = (base_part.astype(jnp.float32) - 0.7 * (delta + 0.9 * momentum_next)).astype(
        jnp.bfloat16
    )
    return (base_next, momentum_next)


def prepare_kernel(blocks, width, order_ref, tokens_ref, cot_ref, gain_ref, n0, n1, c0, c1):
    xf = tokens_ref[...].astype(jnp.float32)
    scale = lax.rsqrt(jnp.mean(xf * xf, axis=1, keepdims=True) + 1e-05)
    for place in range(blocks):
        for core, (n_out, c_out) in enumerate(((n0, c0), (n1, c1))):
            start = pl.multiple_of(order_ref[core * blocks + place] * width, width)
            cols = pl.ds(start, width)
            to = slice(place * width, (place + 1) * width)
            part = tokens_ref[:, cols].astype(jnp.float32)
            n_out[:, to] = (part * scale * gain_ref[:, cols]).astype(jnp.bfloat16)
            c_out[:, to] = cot_ref[:, cols]


def prepare(tokens, cotangent, gain, order):
    rows, model = tokens.shape
    blocks = order.shape[0] // 2
    half = model // 2

    def kernel(*refs):
        prepare_kernel(blocks, half // blocks, *refs)

    wide = pl.BlockSpec((ROW_TILE, model), lambda i, order_ref: (i, 0))
    out = pl.BlockSpec((ROW_TILE, half), lambda i, order_ref: (i, 0))
    return pl.pallas_call(
        kernel,
        grid_spec=pltpu.PrefetchScalarGridSpec(
            num_scalar_prefetch=1,
            grid=(rows // ROW_TILE,),
            in_specs=[wide, wide, pl.BlockSpec((1, model), lambda i, order_ref: (0, 0))],
            out_specs=[out] * 4,
        ),
        out_shape=[jax.ShapeDtypeStruct((rows, half), jnp.bfloat16)] * 4,
        compiler_params=pltpu.CompilerParams(vmem_limit_bytes=32 * 1024 * 1024),
        cost_estimate=pl.CostEstimate(
            flops=6 * rows * model, bytes_accessed=8 * rows * model, transcendentals=rows
        ),
    )(order, tokens, cotangent, gain[None])


def tie(value, after):
    return lax.optimization_barrier((value, after))[0]


def line_perm(chips, senders, shift):
    return [(2 * z + c, 2 * (z + shift) + c) for z in senders for c in (0, 1)]


def gather_line(own, chips, after):
    right, left = [own], [own]
    for step in range(1, chips):
        to_right, to_left = right[-1], left[-1]
        if step == 1 and after is not None:
            to_right, to_left = tie(to_right, after), tie(to_left, after)
        right.append(
            lax.ppermute(to_right, "fsdp", line_perm(chips, range(step - 1, chips - 1), 1))
        )
        left.append(
            lax.ppermute(to_left, "fsdp", line_perm(chips, range(1, chips - step + 1), -1))
        )
    places = [own] + [right[s] + left[chips - s] for s in range(1, chips)]
    return (jnp.concatenate(places, axis=0), right[chips - 2])


def scatter_line(keep, other, chips, width):
    def term(place):
        cols = slice(place * width, (place + 1) * width)
        return keep[:, cols].astype(jnp.float32) + other[:, cols].astype(jnp.float32)

    right = left = None
    for step in range(1, chips):
        to_right, to_left = term(step), term(chips - step)
        if right is not None:
            to_right, to_left = to_right + right, to_left + left
        right = lax.ppermute(
            to_right.astype(jnp.bfloat16), "fsdp", line_perm(chips, range(0, step), 1)
        ).astype(jnp.float32)
        left = lax.ppermute(
            to_left.astype(jnp.bfloat16), "fsdp", line_perm(chips, range(chips - step, chips), -1)
        ).astype(jnp.float32)
    return term(0) + right + left


def per_device(
    tokens,
    norm_gain,
    value_weight,
    output_weight,
    out_cotangent,
    base_params,
    outer_momentum,
    delta_values,
    delta_exponents,
):
    replicas = lax.axis_size("replica")
    devices = lax.axis_size("fsdp")
    chips = devices // 2
    me = lax.axis_index("fsdp")
    chip, core = me // 2, me % 2
    swap = [(i, i ^ 1) for i in range(devices)]
    width = tokens.shape[2] // devices

    scaled = (
        delta_values[0].astype(jnp.float32)
        * jnp.exp2(delta_exponents[0].astype(jnp.float32))[:, None]
    )
    delta = lax.psum(scaled.astype(jnp.bfloat16), "replica").astype(jnp.float32) * (1.0 / replicas)

    source = (chip - jnp.arange(chips, dtype=jnp.int32) + chips) % chips
    order = jnp.concatenate([2 * source + core, 2 * source + 1 - core]).astype(jnp.int32)
    normed0, normed1, cot0, cot1 = prepare(tokens[0], out_cotangent[0], norm_gain, order)

    features = value_weight.shape[2]
    piece = features // CHUNKS
    after = None
    sums = {}
    for name, weight, (in0, in1), (out0, out1) in (
        ("output", value_weight[0], (normed0, normed1), (cot0, cot1)),
        ("value", output_weight[0], (cot0, cot1), (normed0, normed1)),
    ):
        parts = []
        for chunk in range(CHUNKS):
            own = weight[:, chunk * piece : (chunk + 1) * piece]
            w0, after = gather_line(own, chips, after)
            w1 = lax.ppermute(w0, "fsdp", swap)
            mid = (
                jnp.dot(in0, w0, preferred_element_type=jnp.float32)
                + jnp.dot(in1, w1, preferred_element_type=jnp.float32)
            ).astype(jnp.bfloat16)

            def grad(out):
                return lax.dot_general(
                    mid, out, (((0,), (0,)), ((), ())), preferred_element_type=jnp.float32
                ).astype(jnp.bfloat16)

            other = lax.ppermute(grad(out1), "fsdp", swap)
            keep = grad(out0)
            parts.append(scatter_line(keep, other, chips, width).T)
        sums[name] = jnp.concatenate(parts, axis=1)

    new_base, new_momentum = nesterov(delta, base_params, outer_momentum)
    return (sums["value"][None], sums["output"][None], new_base, new_momentum)


def solution(mesh):
    return jax.shard_map(
        per_device,
        mesh=mesh,
        in_specs=(
            P("replica", "fsdp", None),
            P(),
            P("replica", "fsdp", None),
            P("replica", "fsdp", None),
            P("replica", "fsdp", None),
            P("fsdp", None),
            P("fsdp", None),
            P("replica", "fsdp", None),
            P("replica", "fsdp"),
        ),
        out_specs=(
            P("replica", "fsdp", None),
            P("replica", "fsdp", None),
            P("fsdp", None),
            P("fsdp", None),
        ),
        check_vma=False,
    )
```

time: 219 us -> 274 us (1.25)
  starting transfers between devices: 0.38 us -> 116 us
  waiting for transfers between devices: 144 us -> 68.8 us
  matrix products: 36.2 us -> 25.4 us
  Pallas kernels: 0 us -> 10.5 us
  other arithmetic: 19.6 us -> 29.9 us
  local copies, waits for them, and re-layouts: 2.89 us -> 5.8 us
    ppermute x0 -> x56, starting transfers between devices: none -> 116 us  [the longest x12 54 us: scatter_line(): lax.ppermute(to_right.astype(jnp.bfloat16), 'fsdp', line_perm(chips, rang...]
    reduce_scatter x2 -> x0, waiting for transfers between devices: 72.1 us -> none  [the longest x1 47.8 us: per_device(): lax.psum_scatter(lax.dot_general(normed_cols, value_cot, (((0,), (0,)), (...]
    all_gather x2 -> x0, waiting for transfers between devices: 70.5 us -> none  [the longest x1 41.4 us: per_device(): lax.all_gather(value_weight[0], 'fsdp', axis=0, tiled=True)]
    ppermute x0 -> x56, waiting for transfers between devices: none -> 51 us  [the longest x12 22.7 us: gather_line(): lax.ppermute(to_left, 'fsdp', line_perm(chips, range(1, chips - step + 1)...]
    psum x1, waiting for transfers between devices: 0.03 us -> 17.8 us  [per_device(): lax.psum(scaled.astype(jnp.bfloat16), 'replica').astype(jnp.float32)]
    dot_general x2 -> x16, matrix products: 36.2 us -> 25.4 us  [the longest x8 11.1 us: grad(): lax.dot_general(mid, out, (((0,), (0,)), ((), ())), preferred_element_typ...]
    pallas_call x0 -> x1, Pallas kernels: none -> 10.5 us  [prepare(): pl.pallas_call(kernel, grid_spec=pltpu.PrefetchScalarGridSpec(num_scalar_...]
    add x0 -> x12, other arithmetic: none -> 8.52 us  [gather_line(): places = [own] + [right[s] + left[chips - s] for s in range(1, chips)]]
  transfers between devices with their start and end apart: 5 -> 57, of which waited for: 4 -> 15; matrix products, arithmetic and copies ran while one was open for 25% -> 21% of each run, Pallas kernels for 0% -> 4%
where the time goes in v1:
time: 274 us; the launch traced here: 272 us
  starting transfers between devices  116 us (42%)
  waiting for transfers between devices  68.8 us (25%)
  other arithmetic  29.9 us (11%)
  matrix products  25.4 us (9%)
  between operations  15.4 us (6%)
  Pallas kernels  10.5 us (4%)
  local copies, waits for them, and re-layouts  5.8 us (2%)
    ppermute x12, starting transfers between devices, scatter_line(): lax.ppermute(to_right.astype(jnp.bfloat16), 'fsdp', line_perm(chips, rang...  54 us
    ppermute x12, starting transfers between devices, gather_line(): lax.ppermute(to_right, 'fsdp', line_perm(chips, range(step - 1, chips - 1...  34.2 us
    ppermute x12, waiting for transfers between devices, gather_line(): lax.ppermute(to_left, 'fsdp', line_perm(chips, range(1, chips - step + 1)...  22.7 us
    psum x1, waiting for transfers between devices, per_device(): lax.psum(scaled.astype(jnp.bfloat16), 'replica').astype(jnp.float32)  17.8 us
    ppermute x12, starting transfers between devices, gather_line(): lax.ppermute(to_left, 'fsdp', line_perm(chips, range(1, chips - step + 1)...  15.4 us
    ppermute x12, waiting for transfers between devices, scatter_line(): lax.ppermute(to_left.astype(jnp.bfloat16), 'fsdp', line_perm(chips, range...  13.2 us
    ppermute x12, starting transfers between devices, scatter_line(): lax.ppermute(to_left.astype(jnp.bfloat16), 'fsdp', line_perm(chips, range...  11.2 us
    dot_general x8, matrix products, grad(): lax.dot_general(mid, out, (((0,), (0,)), ((), ())), preferred_element_typ...  11.1 us
  transfers between devices with their start and end apart: 57, of which 15 were waited for; matrix products, arithmetic and copies ran while one was open for 21% of the time, Pallas kernels for 4%

profile of v1, /device:TPU:0, one launch (start us, length us, event | category | flops | bytes accessed | tf_op | source)
XLA Modules:
  0.0 271.8 jit_solution(4836343740346776101)
XLA Ops:
  8.3 4.9 %collective-permute-start = (bf16[512,256]{1,0:T(8,128)(2,1)S(1)}, bf16[512,256]{1,0:T(8,128)(2,1)S(1)}, u32[]{:S(2)}, u32[]{:S(2)}) collective-permute-start(bf16[512,256]{1,0:T(8,128)(2,1)S(1)} %get-tuple-element.32), channel_id=1, source_target_pairs={{0,2},{1,3},{2,4},{3,5},{4,6},{5,7},{8,10},{9,11},{10,12},{11,13},... | collective-permute-start | bytes 786440 | tf_op jit(solution)/shard_map/ppermute | solution.py:74
  13.2 1.3 collective-permute-start.32
  14.5 4.2 %collective-permute-done = bf16[512,256]{1,0:T(8,128)(2,1)S(1)} collective-permute-done((bf16[512,256]{1,0:T(8,128)(2,1)S(1)}, bf16[512,256]{1,0:T(8,128)(2,1)S(1)}, u32[]{:S(2)}, u32[]{:S(2)}) %collective-permute-start) | collective-permute-done | bytes 262176 | tf_op jit(solution)/shard_map/ppermute | solution.py:74
  19.4 3.5 %collective-permute-done.32 = bf16[512,256]{1,0:T(8,128)(2,1)S(1)} collective-permute-done((bf16[512,256]{1,0:T(8,128)(2,1)S(1)}, bf16[512,256]{1,0:T(8,128)(2,1)S(1)}, u32[]{:S(2)}, u32[]{:S(2)}) %collective-permute-start.32) | collective-permute-done | bytes 262176 | tf_op jit(solution)/shard_map/ppermute | solution.py:77
  24.2 7.1 %collective-permute-start.2 = (bf16[512,256]{1,0:T(8,128)(2,1)S(1)}, bf16[512,256]{1,0:T(8,128)(2,1)S(1)}, u32[]{:S(2)}, u32[]{:S(2)}) collective-permute-start(bf16[512,256]{1,0:T(8,128)(2,1)S(1)} %get-tuple-element.12), channel_id=1, source_target_pairs={{0,2},{1,3},{2,4},{3,5},{4,6},{5,7},{8,10},{9,11},{10,12},{11,13},... | collective-permute-start | bytes 786440 | tf_op jit(solution)/shard_map/ppermute | solution.py:74
  31.3 1.3 collective-permute-start.44
  33.3 1.3 collective-permute-start.34
  35.4 1.4 collective-permute-start.3
  36.8 5.9 %collective-permute-done.44 = bf16[512,256]{1,0:T(8,128)(2,1)S(1)} collective-permute-done((bf16[512,256]{1,0:T(8,128)(2,1)S(1)}, bf16[512,256]{1,0:T(8,128)(2,1)S(1)}, u32[]{:S(2)}, u32[]{:S(2)}) %collective-permute-start.44) | collective-permute-done | bytes 262176 | tf_op jit(solution)/shard_map/ppermute | solution.py:77
  46.2 5.4 %collective-permute-start.4 = (bf16[512,256]{1,0:T(8,128)(2,1)S(1)}, bf16[512,256]{1,0:T(8,128)(2,1)}, u32[]{:S(2)}, u32[]{:S(2)}) collective-permute-start(bf16[512,256]{1,0:T(8,128)(2,1)S(1)} %get-tuple-element.13), channel_id=1, source_target_pairs={{0,2},{1,3},{2,4},{3,5},{4,6},{5,7},{8,10},{9,11},{10,12},{11,13},... | collective-permute-start | bytes 786440 | tf_op jit(solution)/shard_map/ppermute | solution.py:74
  52.9 1.4 collective-permute-start.47
  55.6 2.2 fusion
  58.5 4.2 %collective-permute-done.5 = bf16[512,256]{1,0:T(8,128)(2,1)} collective-permute-done((bf16[512,256]{1,0:T(8,128)(2,1)S(1)}, bf16[512,256]{1,0:T(8,128)(2,1)}, u32[]{:S(2)}, u32[]{:S(2)}) %collective-permute-start.5) | collective-permute-done | bytes 262176 | tf_op jit(solution)/shard_map/ppermute | solution.py:77
  64.1 10.5 %shard_map.120 = (bf16[1024,2048]{1,0:T(8,128)(2,1)S(1)}, bf16[1024,2048]{1,0:T(8,128)(2,1)S(1)}, bf16[1024,2048]{1,0:T(8,128)(2,1)S(1)}, bf16[1024,2048]{1,0:T(8,128)(2,1)S(1)}) custom-call(s32[8]{0:T(128)S(1)} %pad_add_fusion.refs_0_, bf16[1024,4096]{1,0:T(8,128)(2,1)} %bitcast.50, bf16[1024,4096]{1,0:T(8,128)(2,1)} %bitcast.51, f32[1,4096]{1,0:T(1,128)S(1)} %bitcast.49), custom_call_target="tpu_custom_call" | custom-call | flops 25165824 | bytes 33554432 | tf_op jit(solution)/shard_map/pallas_call | solution.py:43
  74.6 1.5 add.260
  78.6 1.9 pad_maximum_fusion.3
  81.8 9.0 %collective-permute-start.18 = (bf16[512,256]{1,0:T(8,128)(2,1)S(1)}, bf16[512,256]{1,0:T(8,128)(2,1)}, u32[]{:S(2)}, u32[]{:S(2)}) collective-permute-start(bf16[512,256]{1,0:T(8,128)(2,1)S(1)} %get-tuple-element.17), channel_id=1, source_target_pairs={{0,2},{1,3},{2,4},{3,5},{4,6},{5,7},{8,10},{9,11},{10,12},{11,13},... | collective-permute-start | bytes 786440 | tf_op jit(solution)/shard_map/ppermute | solution.py:74
  92.9 2.5 fusion.19
  96.7 2.2 convolution_convert_fusion.2
  100.2 1.7 collective-permute-done.7
  103.1 1.3 collective-permute-start.20
  104.4 1.4 collective-permute-start.22
  107.1 6.7 %collective-permute-done.20 = bf16[512,256]{1,0:T(8,128)(2,1)} collective-permute-done((bf16[512,256]{1,0:T(8,128)(2,1)S(1)}, bf16[512,256]{1,0:T(8,128)(2,1)}, u32[]{:S(2)}, u32[]{:S(2)}) %collective-permute-start.20) | collective-permute-done | bytes 262176 | tf_op jit(solution)/shard_map/ppermute | solution.py:77
  115.1 17.8 %all-reduce.2.cloned.1.call-done = bf16[8192,128]{1,0:T(8,128)(2,1)} async-done(((bf16[8192,128]{1,0:T(8,128)(2,1)}), bf16[8192,128]{1,0:T(8,128)(2,1)}) %all-reduce.2.cloned.1.call-update) | async-done | bytes 2097168 | tf_op jit(solution)/shard_map/psum | solution.py:125
  132.9 7.6 %subtract_convert_fusion = (bf16[8192,128]{1,0:T(8,128)(2,1)}, f32[8192,128]{1,0:T(8,128)}) fusion(bf16[8192,128]{1,0:T(8,128)(2,1)} %all-reduce.2.cloned.1.call-done, bf16[8192,128]{1,0:T(8,128)(2,1)} %param.14, f32[8192,128]{1,0:T(8,128)} %param.15), kind=kLoop, calls=%fused_computation.2 | loop fusion | flops 10485760 | bytes 14680064 | tf_op jit(solution)/shard_map/convert_element_type | solution.py:14
  142.7 3.0 %fusion.20 = f32[1024,256]{1,0:T(8,128)S(1)} fusion(bf16[1024,2048]{1,0:T(8,128)(2,1)S(1)} %copy-done.2, bf16[2048,256]{1,0:T(8,128)(2,1)} %collective-permute-done.48), kind=kOutput, calls=%fused_computation.81 | convolution fusion | flops 1073741824 | bytes 6291456 | tf_op jit(solution)/shard_map/dot_general | solution.py:146
  152.6 3.5 %collective-permute-start.38 = (bf16[256,512]{1,0:T(8,128)(2,1)S(1)}, bf16[256,512]{1,0:T(8,128)(2,1)S(1)}, u32[]{:S(2)}, u32[]{:S(2)}) collective-permute-start(bf16[256,512]{1,0:T(8,128)(2,1)S(1)} %fusion.10), channel_id=1, source_target_pairs={{0,2},{1,3},{8,10},{9,11},{16,18},{17,19},{24,26},{25,27}} | collective-permute-start | bytes 786440 | tf_op jit(solution)/shard_map/ppermute | solution.py:93
  156.1 2.5 fusion.17
  162.0 4.5 %collective-permute-start.39 = (bf16[256,512]{1,0:T(8,128)(2,1)S(1)}, bf16[256,512]{1,0:T(8,128)(2,1)S(1)}, u32[]{:S(2)}, u32[]{:S(2)}) collective-permute-start(bf16[256,512]{1,0:T(8,128)(2,1)S(1)} %add_convert_fusion.7), channel_id=1, source_target_pairs={{0,2},{1,3},{2,4},{3,5},{8,10},{9,11},{10,12},{11,13},{16,18},{17,... | collective-permute-start | bytes 786440 | tf_op jit(solution)/shard_map/ppermute | solution.py:93
  167.8 3.6 %collective-permute-done.39 = bf16[256,512]{1,0:T(8,128)(2,1)S(1)} collective-permute-done((bf16[256,512]{1,0:T(8,128)(2,1)S(1)}, bf16[256,512]{1,0:T(8,128)(2,1)S(1)}, u32[]{:S(2)}, u32[]{:S(2)}) %collective-permute-start.39) | collective-permute-done | bytes 262176 | tf_op jit(solution)/shard_map/ppermute | solution.py:93
  172.4 4.6 %collective-permute-start.50 = (bf16[256,512]{1,0:T(8,128)(2,1)S(1)}, bf16[256,512]{1,0:T(8,128)(2,1)S(1)}, u32[]{:S(2)}, u32[]{:S(2)}) collective-permute-start(bf16[256,512]{1,0:T(8,128)(2,1)S(1)} %fusion.12), channel_id=1, source_target_pairs={{0,2},{1,3},{8,10},{9,11},{16,18},{17,19},{24,26},{25,27}} | collective-permute-start | bytes 786440 | tf_op jit(solution)/shard_map/ppermute | solution.py:93
  181.0 4.3 %collective-permute-start.51 = (bf16[256,512]{1,0:T(8,128)(2,1)S(1)}, bf16[256,512]{1,0:T(8,128)(2,1)S(1)}, u32[]{:S(2)}, u32[]{:S(2)}) collective-permute-start(bf16[256,512]{1,0:T(8,128)(2,1)S(1)} %add_convert_fusion.3), channel_id=1, source_target_pairs={{0,2},{1,3},{2,4},{3,5},{8,10},{9,11},{10,12},{11,13},{16,18},{17,... | collective-permute-start | bytes 786440 | tf_op jit(solution)/shard_map/ppermute | solution.py:93
  186.7 1.9 collective-permute-start.40
  189.5 2.2 collective-permute-done.51
  192.6 4.4 %collective-permute-start.12 = (bf16[256,512]{1,0:T(8,128)(2,1)S(1)}, bf16[256,512]{1,0:T(8,128)(2,1)S(1)}, u32[]{:S(2)}, u32[]{:S(2)}) collective-permute-start(bf16[256,512]{1,0:T(8,128)(2,1)S(1)} %fusion.6), channel_id=1, source_target_pairs={{0,2},{1,3},{8,10},{9,11},{16,18},{17,19},{24,26},{25,27}} | collective-permute-start | bytes 786440 | tf_op jit(solution)/shard_map/ppermute | solution.py:93
  198.5 4.9 %collective-permute-start.52 = (bf16[256,512]{1,0:T(8,128)(2,1)S(1)}, bf16[256,512]{1,0:T(8,128)(2,1)S(1)}, u32[]{:S(2)}, u32[]{:S(2)}) collective-permute-start(bf16[256,512]{1,0:T(8,128)(2,1)S(1)} %get-tuple-element.26), channel_id=1, source_target_pairs={{0,2},{1,3},{2,4},{3,5},{4,6},{5,7},{8,10},{9,11},{10,12},{11,13},... | collective-permute-start | bytes 786440 | tf_op jit(solution)/shard_map/ppermute | solution.py:93
  204.4 6.0 %collective-permute-start.13 = (bf16[256,512]{1,0:T(8,128)(2,1)S(1)}, bf16[256,512]{1,0:T(8,128)(2,1)S(1)}, u32[]{:S(2)}, u32[]{:S(2)}) collective-permute-start(bf16[256,512]{1,0:T(8,128)(2,1)S(1)} %add_convert_fusion.15), channel_id=1, source_target_pairs={{0,2},{1,3},{2,4},{3,5},{8,10},{9,11},{10,12},{11,13},{16,18},{17,... | collective-permute-start | bytes 786440 | tf_op jit(solution)/shard_map/ppermute | solution.py:93
  210.5 4.6 %collective-permute-start.26 = (bf16[256,512]{1,0:T(8,128)(2,1)S(1)}, bf16[256,512]{1,0:T(8,128)(2,1)S(1)}, u32[]{:S(2)}, u32[]{:S(2)}) collective-permute-start(bf16[256,512]{1,0:T(8,128)(2,1)S(1)} %fusion.8), channel_id=1, source_target_pairs={{0,2},{1,3},{8,10},{9,11},{16,18},{17,19},{24,26},{25,27}} | collective-permute-start | bytes 786440 | tf_op jit(solution)/shard_map/ppermute | solution.py:93
  215.2 1.4 collective-permute-done.13
  217.4 2.6 collective-permute-done.26
  220.2 4.4 %collective-permute-start.27 = (bf16[256,512]{1,0:T(8,128)(2,1)S(1)}, bf16[256,512]{1,0:T(8,128)(2,1)S(1)}, u32[]{:S(2)}, u32[]{:S(2)}) collective-permute-start(bf16[256,512]{1,0:T(8,128)(2,1)S(1)} %add_convert_fusion.11), channel_id=1, source_target_pairs={{0,2},{1,3},{2,4},{3,5},{8,10},{9,11},{10,12},{11,13},{16,18},{17,... | collective-permute-start | bytes 786440 | tf_op jit(solution)/shard_map/ppermute | solution.py:93
  226.0 5.3 %collective-permute-start.14 = (bf16[256,512]{1,0:T(8,128)(2,1)S(1)}, bf16[256,512]{1,0:T(8,128)(2,1)}, u32[]{:S(2)}, u32[]{:S(2)}) collective-permute-start(bf16[256,512]{1,0:T(8,128)(2,1)S(1)} %get-tuple-element.28), channel_id=1, source_target_pairs={{0,2},{1,3},{2,4},{3,5},{4,6},{5,7},{8,10},{9,11},{10,12},{11,13},... | collective-permute-start | bytes 786440 | tf_op jit(solution)/shard_map/ppermute | solution.py:93
  234.7 1.4 collective-permute-start.30
  238.3 1.3 copy.14
  239.6 5.5 %collective-permute-start.28 = (bf16[256,512]{1,0:T(8,128)(2,1)}, bf16[256,512]{1,0:T(8,128)(2,1)S(1)}, u32[]{:S(2)}, u32[]{:S(2)}) collective-permute-start(bf16[256,512]{1,0:T(8,128)(2,1)} %get-tuple-element.30), channel_id=1, source_target_pairs={{0,2},{1,3},{2,4},{3,5},{4,6},{5,7},{8,10},{9,11},{10,12},{11,13},... | collective-permute-start | bytes 786440 | tf_op jit(solution)/shard_map/ppermute | solution.py:93
  246.3 1.3 collective-permute-start.31
  249.2 13.1 %collective-permute-done.31 = bf16[256,512]{1,0:T(8,128)(2,1)S(1)} collective-permute-done((bf16[256,512]{1,0:T(8,128)(2,1)S(1)}, bf16[256,512]{1,0:T(8,128)(2,1)S(1)}, u32[]{:S(2)}, u32[]{:S(2)}) %collective-permute-start.31) | collective-permute-done | bytes 262176 | tf_op jit(solution)/shard_map/ppermute | solution.py:96
  263.6 1.3 copy.13
  (203 shorter events, 60.4 us)
Async XLA Ops:
  7.2 125.8 %all-reduce.2.cloned.1.call-start = ((), (), s32[]{:S(2)}) async-start(), calls=%async_computation | async-start | bytes 4194304 | tf_op jit(solution)/shard_map/psum | solution.py:125
  8.3 10.5 %collective-permute-start = (bf16[512,256]{1,0:T(8,128)(2,1)S(1)}, bf16[512,256]{1,0:T(8,128)(2,1)S(1)}, u32[]{:S(2)}, u32[]{:S(2)}) collective-permute-start(bf16[512,256]{1,0:T(8,128)(2,1)S(1)} %get-tuple-element.32), channel_id=1, source_target_pairs={{0,2},{1,3},{2,4},{3,5},{4,6},{5,7},{8,10},{9,11},{10,12},{11,13},... | collective-permute-start | bytes 786440 | tf_op jit(solution)/shard_map/ppermute | solution.py:74
  13.2 9.7 %collective-permute-start.32 = (bf16[512,256]{1,0:T(8,128)(2,1)S(1)}, bf16[512,256]{1,0:T(8,128)(2,1)S(1)}, u32[]{:S(2)}, u32[]{:S(2)}) collective-permute-start(bf16[512,256]{1,0:T(8,128)(2,1)S(1)} %get-tuple-element.32), channel_id=1, source_target_pairs={{2,0},{3,1},{4,2},{5,3},{6,4},{7,5},{10,8},{11,9},{12,10},{13,11},... | collective-permute-start | bytes 786440 | tf_op jit(solution)/shard_map/ppermute | solution.py:77
  22.9 10.4 %collective-permute-start.33 = (bf16[512,256]{1,0:T(8,128)(2,1)S(1)}, bf16[512,256]{1,0:T(8,128)(2,1)S(1)}, u32[]{:S(2)}, u32[]{:S(2)}) collective-permute-start(bf16[512,256]{1,0:T(8,128)(2,1)S(1)} %collective-permute-done.32), channel_id=1, source_target_pairs={{2,0},{3,1},{4,2},{5,3},{10,8},{11,9},{12,10},{13,11},{18,16},{19,... | collective-permute-start | bytes 786440 | tf_op jit(solution)/shard_map/ppermute | solution.py:77
  24.2 11.2 %collective-permute-start.2 = (bf16[512,256]{1,0:T(8,128)(2,1)S(1)}, bf16[512,256]{1,0:T(8,128)(2,1)S(1)}, u32[]{:S(2)}, u32[]{:S(2)}) collective-permute-start(bf16[512,256]{1,0:T(8,128)(2,1)S(1)} %get-tuple-element.12), channel_id=1, source_target_pairs={{0,2},{1,3},{2,4},{3,5},{4,6},{5,7},{8,10},{9,11},{10,12},{11,13},... | collective-permute-start | bytes 786440 | tf_op jit(solution)/shard_map/ppermute | solution.py:74
  31.3 11.4 %collective-permute-start.44 = (bf16[512,256]{1,0:T(8,128)(2,1)S(1)}, bf16[512,256]{1,0:T(8,128)(2,1)S(1)}, u32[]{:S(2)}, u32[]{:S(2)}) collective-permute-start(bf16[512,256]{1,0:T(8,128)(2,1)S(1)} %get-tuple-element.12), channel_id=1, source_target_pairs={{2,0},{3,1},{4,2},{5,3},{6,4},{7,5},{10,8},{11,9},{12,10},{13,11},... | collective-permute-start | bytes 786440 | tf_op jit(solution)/shard_map/ppermute | solution.py:77
  32.6 12.6 %collective-permute-start.35 = (bf16[512,256]{1,0:T(8,128)(2,1)S(1)}, bf16[512,256]{1,0:T(8,128)(2,1)S(1)}, u32[]{:S(2)}, u32[]{:S(2)}) collective-permute-start(bf16[512,256]{1,0:T(8,128)(2,1)S(1)} %collective-permute-done.1), channel_id=1, source_target_pairs={{4,6},{5,7},{12,14},{13,15},{20,22},{21,23},{28,30},{29,31}} | collective-permute-start | bytes 786440 | tf_op jit(solution)/shard_map/ppermute | solution.py:74
  33.3 12.6 %collective-permute-start.34 = (bf16[512,256]{1,0:T(8,128)(2,1)S(1)}, bf16[512,256]{1,0:T(8,128)(2,1)S(1)}, u32[]{:S(2)}, u32[]{:S(2)}) collective-permute-start(bf16[512,256]{1,0:T(8,128)(2,1)S(1)} %collective-permute-done.33), channel_id=1, source_target_pairs={{2,0},{3,1},{10,8},{11,9},{18,16},{19,17},{26,24},{27,25}} | collective-permute-start | bytes 786440 | tf_op jit(solution)/shard_map/ppermute | solution.py:77
  35.4 10.8 %collective-permute-start.3 = (bf16[512,256]{1,0:T(8,128)(2,1)S(1)}, bf16[512,256]{1,0:T(8,128)(2,1)}, u32[]{:S(2)}, u32[]{:S(2)}) collective-permute-start(bf16[512,256]{1,0:T(8,128)(2,1)S(1)} %collective-permute-done.2), channel_id=1, source_target_pairs={{2,4},{3,5},{4,6},{5,7},{10,12},{11,13},{12,14},{13,15},{18,20},{1... | collective-permute-start | bytes 786440 | tf_op jit(solution)/shard_map/ppermute | solution.py:74
  42.7 11.5 %collective-permute-start.45 = (bf16[512,256]{1,0:T(8,128)(2,1)S(1)}, bf16[512,256]{1,0:T(8,128)(2,1)}, u32[]{:S(2)}, u32[]{:S(2)}) collective-permute-start(bf16[512,256]{1,0:T(8,128)(2,1)S(1)} %collective-permute-done.44), channel_id=1, source_target_pairs={{2,0},{3,1},{4,2},{5,3},{10,8},{11,9},{12,10},{13,11},{18,16},{19,... | collective-permute-start | bytes 786440 | tf_op jit(solution)/shard_map/ppermute | solution.py:77
  46.1 45.5 %collective-permute-start.36 = (bf16[2048,256]{1,0:T(8,128)(2,1)S(1)}, bf16[2048,256]{1,0:T(8,128)(2,1)}, u32[]{:S(2)}, u32[]{:S(2)}) collective-permute-start(bf16[2048,256]{1,0:T(8,128)(2,1)S(1)} %pad_maximum_fusion.2), channel_id=1, source_target_pairs={{0,1},{1,0},{2,3},{3,2},{4,5},{5,4},{6,7},{7,6},{8,9},{9,8},{10,11... | collective-permute-start | bytes 3145736 | tf_op jit(solution)/shard_map/ppermute | solution.py:143
  46.2 11.6 %collective-permute-start.4 = (bf16[512,256]{1,0:T(8,128)(2,1)S(1)}, bf16[512,256]{1,0:T(8,128)(2,1)}, u32[]{:S(2)}, u32[]{:S(2)}) collective-permute-start(bf16[512,256]{1,0:T(8,128)(2,1)S(1)} %get-tuple-element.13), channel_id=1, source_target_pairs={{0,2},{1,3},{2,4},{3,5},{4,6},{5,7},{8,10},{9,11},{10,12},{11,13},... | collective-permute-start | bytes 786440 | tf_op jit(solution)/shard_map/ppermute | solution.py:74
  51.6 11.1 %collective-permute-start.5 = (bf16[512,256]{1,0:T(8,128)(2,1)S(1)}, bf16[512,256]{1,0:T(8,128)(2,1)}, u32[]{:S(2)}, u32[]{:S(2)}) collective-permute-start(bf16[512,256]{1,0:T(8,128)(2,1)S(1)} %get-tuple-element.13), channel_id=1, source_target_pairs={{2,0},{3,1},{4,2},{5,3},{6,4},{7,5},{10,8},{11,9},{12,10},{13,11},... | collective-permute-start | bytes 786440 | tf_op jit(solution)/shard_map/ppermute | solution.py:77
  52.9 23.2 %collective-permute-start.47 = (bf16[512,256]{1,0:T(8,128)(2,1)}, bf16[512,256]{1,0:T(8,128)(2,1)}, u32[]{:S(2)}, u32[]{:S(2)}) collective-permute-start(bf16[512,256]{1,0:T(8,128)(2,1)} %collective-permute-done.3), channel_id=1, source_target_pairs={{4,6},{5,7},{12,14},{13,15},{20,22},{21,23},{28,30},{29,31}} | collective-permute-start | bytes 786440 | tf_op jit(solution)/shard_map/ppermute | solution.py:74
  54.3 23.1 %collective-permute-start.46 = (bf16[512,256]{1,0:T(8,128)(2,1)}, bf16[512,256]{1,0:T(8,128)(2,1)}, u32[]{:S(2)}, u32[]{:S(2)}) collective-permute-start(bf16[512,256]{1,0:T(8,128)(2,1)} %collective-permute-done.45), channel_id=1, source_target_pairs={{2,0},{3,1},{10,8},{11,9},{18,16},{19,17},{26,24},{27,25}} | collective-permute-start | bytes 786440 | tf_op jit(solution)/shard_map/ppermute | solution.py:77
  57.8 22.7 %collective-permute-start.8 = (bf16[512,256]{1,0:T(8,128)(2,1)}, bf16[512,256]{1,0:T(8,128)(2,1)S(1)}, u32[]{:S(2)}, u32[]{:S(2)}) collective-permute-start(bf16[512,256]{1,0:T(8,128)(2,1)} %collective-permute-done.4), channel_id=1, source_target_pairs={{2,4},{3,5},{4,6},{5,7},{10,12},{11,13},{12,14},{13,15},{18,20},{1... | collective-permute-start | bytes 786440 | tf_op jit(solution)/shard_map/ppermute | solution.py:74
  62.7 28.1 %collective-permute-start.6 = (bf16[512,256]{1,0:T(8,128)(2,1)}, bf16[512,256]{1,0:T(8,128)(2,1)S(1)}, u32[]{:S(2)}, u32[]{:S(2)}) collective-permute-start(bf16[512,256]{1,0:T(8,128)(2,1)} %collective-permute-done.5), channel_id=1, source_target_pairs={{2,0},{3,1},{4,2},{5,3},{10,8},{11,9},{12,10},{13,11},{18,16},{19,... | collective-permute-start | bytes 786440 | tf_op jit(solution)/shard_map/ppermute | solution.py:77
  80.5 62.2 %collective-permute-start.48 = (bf16[2048,256]{1,0:T(8,128)(2,1)}, bf16[2048,256]{1,0:T(8,128)(2,1)}, u32[]{:S(2)}, u32[]{:S(2)}) collective-permute-start(bf16[2048,256]{1,0:T(8,128)(2,1)} %pad_maximum_fusion.3), channel_id=1, source_target_pairs={{0,1},{1,0},{2,3},{3,2},{4,5},{5,4},{6,7},{7,6},{8,9},{9,8},{10,11... | collective-permute-start | bytes 3145736 | tf_op jit(solution)/shard_map/ppermute | solution.py:143
  80.5 22.6 %collective-permute-start.19 = (bf16[512,256]{1,0:T(8,128)(2,1)S(1)}, bf16[512,256]{1,0:T(8,128)(2,1)S(1)}, u32[]{:S(2)}, u32[]{:S(2)}) collective-permute-start(bf16[512,256]{1,0:T(8,128)(2,1)S(1)} %get-tuple-element.17), channel_id=1, source_target_pairs={{2,0},{3,1},{4,2},{5,3},{6,4},{7,5},{10,8},{11,9},{12,10},{13,11},... | collective-permute-start | bytes 786440 | tf_op jit(solution)/shard_map/ppermute | solution.py:77
  81.8 22.6 %collective-permute-start.18 = (bf16[512,256]{1,0:T(8,128)(2,1)S(1)}, bf16[512,256]{1,0:T(8,128)(2,1)}, u32[]{:S(2)}, u32[]{:S(2)}) collective-permute-start(bf16[512,256]{1,0:T(8,128)(2,1)S(1)} %get-tuple-element.17), channel_id=1, source_target_pairs={{0,2},{1,3},{2,4},{3,5},{4,6},{5,7},{8,10},{9,11},{10,12},{11,13},... | collective-permute-start | bytes 786440 | tf_op jit(solution)/shard_map/ppermute | solution.py:74
  91.6 10.3 %collective-permute-start.7 = (bf16[512,256]{1,0:T(8,128)(2,1)S(1)}, bf16[512,256]{1,0:T(8,128)(2,1)S(1)}, u32[]{:S(2)}, u32[]{:S(2)}) collective-permute-start(bf16[512,256]{1,0:T(8,128)(2,1)S(1)} %collective-permute-done.6), channel_id=1, source_target_pairs={{2,0},{3,1},{10,8},{11,9},{18,16},{19,17},{26,24},{27,25}} | collective-permute-start | bytes 786440 | tf_op jit(solution)/shard_map/ppermute | solution.py:77
  99.0 53.5 %collective-permute-start.37 = (bf16[256,2048]{1,0:T(8,128)(2,1)}, bf16[256,2048]{1,0:T(8,128)(2,1)S(1)}, u32[]{:S(2)}, u32[]{:S(2)}) collective-permute-start(bf16[256,2048]{1,0:T(8,128)(2,1)} %convolution_convert_fusion.2), channel_id=1, source_target_pairs={{0,1},{1,0},{2,3},{3,2},{4,5},{5,4},{6,7},{7,6},{8,9},{9,8},{10,11... | collective-permute-start | bytes 3145736 | tf_op jit(solution)/shard_map/ppermute | solution.py:154
  103.0 53.1 %collective-permute-start.10 = (bf16[2048,256]{1,0:T(8,128)(2,1)S(1)}, bf16[2048,256]{1,0:T(8,128)(2,1)}, u32[]{:S(2)}, u32[]{:S(2)}) collective-permute-start(bf16[2048,256]{1,0:T(8,128)(2,1)S(1)} %pad_maximum_fusion), channel_id=1, source_target_pairs={{0,1},{1,0},{2,3},{3,2},{4,5},{5,4},{6,7},{7,6},{8,9},{9,8},{10,11... | collective-permute-start | bytes 3145736 | tf_op jit(solution)/shard_map/ppermute | solution.py:143
  103.1 10.7 %collective-permute-start.20 = (bf16[512,256]{1,0:T(8,128)(2,1)S(1)}, bf16[512,256]{1,0:T(8,128)(2,1)}, u32[]{:S(2)}, u32[]{:S(2)}) collective-permute-start(bf16[512,256]{1,0:T(8,128)(2,1)S(1)} %collective-permute-done.19), channel_id=1, source_target_pairs={{2,0},{3,1},{4,2},{5,3},{10,8},{11,9},{12,10},{13,11},{18,16},{19,... | collective-permute-start | bytes 786440 | tf_op jit(solution)/shard_map/ppermute | solution.py:77
  104.4 36.1 %collective-permute-start.22 = (bf16[512,256]{1,0:T(8,128)(2,1)}, bf16[512,256]{1,0:T(8,128)(2,1)}, u32[]{:S(2)}, u32[]{:S(2)}) collective-permute-start(bf16[512,256]{1,0:T(8,128)(2,1)} %collective-permute-done.18), channel_id=1, source_target_pairs={{2,4},{3,5},{4,6},{5,7},{10,12},{11,13},{12,14},{13,15},{18,20},{1... | collective-permute-start | bytes 786440 | tf_op jit(solution)/shard_map/ppermute | solution.py:74
  113.8 35.5 %collective-permute-start.21 = (bf16[512,256]{1,0:T(8,128)(2,1)}, bf16[512,256]{1,0:T(8,128)(2,1)}, u32[]{:S(2)}, u32[]{:S(2)}) collective-permute-start(bf16[512,256]{1,0:T(8,128)(2,1)} %collective-permute-done.20), channel_id=1, source_target_pairs={{2,0},{3,1},{10,8},{11,9},{18,16},{19,17},{26,24},{27,25}} | collective-permute-start | bytes 786440 | tf_op jit(solution)/shard_map/ppermute | solution.py:77
  149.2 23.1 %collective-permute-start.49 = (bf16[256,2048]{1,0:T(8,128)(2,1)S(1)}, bf16[256,2048]{1,0:T(8,128)(2,1)S(1)}, u32[]{:S(2)}, u32[]{:S(2)}) collective-permute-start(bf16[256,2048]{1,0:T(8,128)(2,1)S(1)} %convolution_convert_fusion), channel_id=1, source_target_pairs={{0,1},{1,0},{2,3},{3,2},{4,5},{5,4},{6,7},{7,6},{8,9},{9,8},{10,11... | collective-permute-start | bytes 3145736 | tf_op jit(solution)/shard_map/ppermute | solution.py:154
  150.7 26.4 %collective-permute-start.24 = (bf16[2048,256]{1,0:T(8,128)(2,1)S(1)}, bf16[2048,256]{1,0:T(8,128)(2,1)S(1)}, u32[]{:S(2)}, u32[]{:S(2)}) collective-permute-start(bf16[2048,256]{1,0:T(8,128)(2,1)S(1)} %pad_maximum_fusion.1), channel_id=1, source_target_pairs={{0,1},{1,0},{2,3},{3,2},{4,5},{5,4},{6,7},{7,6},{8,9},{9,8},{10,11... | collective-permute-start | bytes 3145736 | tf_op jit(solution)/shard_map/ppermute | solution.py:143
  152.6 9.3 %collective-permute-start.38 = (bf16[256,512]{1,0:T(8,128)(2,1)S(1)}, bf16[256,512]{1,0:T(8,128)(2,1)S(1)}, u32[]{:S(2)}, u32[]{:S(2)}) collective-permute-start(bf16[256,512]{1,0:T(8,128)(2,1)S(1)} %fusion.10), channel_id=1, source_target_pairs={{0,2},{1,3},{8,10},{9,11},{16,18},{17,19},{24,26},{25,27}} | collective-permute-start | bytes 786440 | tf_op jit(solution)/shard_map/ppermute | solution.py:93
  161.2 31.3 %collective-permute-start.11 = (bf16[256,2048]{1,0:T(8,128)(2,1)S(1)}, bf16[256,2048]{1,0:T(8,128)(2,1)S(1)}, u32[]{:S(2)}, u32[]{:S(2)}) collective-permute-start(bf16[256,2048]{1,0:T(8,128)(2,1)S(1)} %convolution_convert_fusion.6), channel_id=1, source_target_pairs={{0,1},{1,0},{2,3},{3,2},{4,5},{5,4},{6,7},{7,6},{8,9},{9,8},{10,11... | collective-permute-start | bytes 3145736 | tf_op jit(solution)/shard_map/ppermute | solution.py:154
  162.0 9.5 %collective-permute-start.39 = (bf16[256,512]{1,0:T(8,128)(2,1)S(1)}, bf16[256,512]{1,0:T(8,128)(2,1)S(1)}, u32[]{:S(2)}, u32[]{:S(2)}) collective-permute-start(bf16[256,512]{1,0:T(8,128)(2,1)S(1)} %add_convert_fusion.7), channel_id=1, source_target_pairs={{0,2},{1,3},{2,4},{3,5},{8,10},{9,11},{10,12},{11,13},{16,18},{17,... | collective-permute-start | bytes 786440 | tf_op jit(solution)/shard_map/ppermute | solution.py:93
  171.6 17.0 %collective-permute-start.41 = (bf16[256,512]{1,0:T(8,128)(2,1)S(1)}, bf16[256,512]{1,0:T(8,128)(2,1)S(1)}, u32[]{:S(2)}, u32[]{:S(2)}) collective-permute-start(bf16[256,512]{1,0:T(8,128)(2,1)S(1)} %get-tuple-element.25), channel_id=1, source_target_pairs={{6,4},{7,5},{14,12},{15,13},{22,20},{23,21},{30,28},{31,29}} | collective-permute-start | bytes 786440 | tf_op jit(solution)/shard_map/ppermute | solution.py:96
  181.0 10.7 %collective-permute-start.51 = (bf16[256,512]{1,0:T(8,128)(2,1)S(1)}, bf16[256,512]{1,0:T(8,128)(2,1)S(1)}, u32[]{:S(2)}, u32[]{:S(2)}) collective-permute-start(bf16[256,512]{1,0:T(8,128)(2,1)S(1)} %add_convert_fusion.3), channel_id=1, source_target_pairs={{0,2},{1,3},{2,4},{3,5},{8,10},{9,11},{10,12},{11,13},{16,18},{17,... | collective-permute-start | bytes 786440 | tf_op jit(solution)/shard_map/ppermute | solution.py:93
  186.7 23.8 %collective-permute-start.40 = (bf16[256,512]{1,0:T(8,128)(2,1)S(1)}, bf16[256,512]{1,0:T(8,128)(2,1)S(1)}, u32[]{:S(2)}, u32[]{:S(2)}) collective-permute-start(bf16[256,512]{1,0:T(8,128)(2,1)S(1)} %get-tuple-element.24), channel_id=1, source_target_pairs={{0,2},{1,3},{2,4},{3,5},{4,6},{5,7},{8,10},{9,11},{10,12},{11,13},... | collective-permute-start | bytes 786440 | tf_op jit(solution)/shard_map/ppermute | solution.py:93
  188.6 15.8 %collective-permute-start.25 = (bf16[256,2048]{1,0:T(8,128)(2,1)S(1)}, bf16[256,2048]{1,0:T(8,128)(2,1)S(1)}, u32[]{:S(2)}, u32[]{:S(2)}) collective-permute-start(bf16[256,2048]{1,0:T(8,128)(2,1)S(1)} %convolution_convert_fusion.4), channel_id=1, source_target_pairs={{0,1},{1,0},{2,3},{3,2},{4,5},{5,4},{6,7},{7,6},{8,9},{9,8},{10,11... | collective-permute-start | bytes 3145736 | tf_op jit(solution)/shard_map/ppermute | solution.py:154
  192.6 10.9 %collective-permute-start.12 = (bf16[256,512]{1,0:T(8,128)(2,1)S(1)}, bf16[256,512]{1,0:T(8,128)(2,1)S(1)}, u32[]{:S(2)}, u32[]{:S(2)}) collective-permute-start(bf16[256,512]{1,0:T(8,128)(2,1)S(1)} %fusion.6), channel_id=1, source_target_pairs={{0,2},{1,3},{8,10},{9,11},{16,18},{17,19},{24,26},{25,27}} | collective-permute-start | bytes 786440 | tf_op jit(solution)/shard_map/ppermute | solution.py:93
  197.2 17.9 %collective-permute-start.43 = (bf16[256,512]{1,0:T(8,128)(2,1)S(1)}, bf16[256,512]{1,0:T(8,128)(2,1)S(1)}, u32[]{:S(2)}, u32[]{:S(2)}) collective-permute-start(bf16[256,512]{1,0:T(8,128)(2,1)S(1)} %add_convert_fusion.4), channel_id=1, source_target_pairs={{2,0},{3,1},{4,2},{5,3},{6,4},{7,5},{10,8},{11,9},{12,10},{13,11},... | collective-permute-start | bytes 786440 | tf_op jit(solution)/shard_map/ppermute | solution.py:96
  198.5 35.2 %collective-permute-start.52 = (bf16[256,512]{1,0:T(8,128)(2,1)S(1)}, bf16[256,512]{1,0:T(8,128)(2,1)S(1)}, u32[]{:S(2)}, u32[]{:S(2)}) collective-permute-start(bf16[256,512]{1,0:T(8,128)(2,1)S(1)} %get-tuple-element.26), channel_id=1, source_target_pairs={{0,2},{1,3},{2,4},{3,5},{4,6},{5,7},{8,10},{9,11},{10,12},{11,13},... | collective-permute-start | bytes 786440 | tf_op jit(solution)/shard_map/ppermute | solution.py:93
  203.6 21.0 %collective-permute-start.54 = (bf16[256,512]{1,0:T(8,128)(2,1)S(1)}, bf16[256,512]{1,0:T(8,128)(2,1)S(1)}, u32[]{:S(2)}, u32[]{:S(2)}) collective-permute-start(bf16[256,512]{1,0:T(8,128)(2,1)S(1)} %add_convert_fusion.1), channel_id=1, source_target_pairs={{4,2},{5,3},{6,4},{7,5},{12,10},{13,11},{14,12},{15,13},{20,18},{2... | collective-permute-start | bytes 786440 | tf_op jit(solution)/shard_map/ppermute | solution.py:96
  204.4 12.2 %collective-permute-start.13 = (bf16[256,512]{1,0:T(8,128)(2,1)S(1)}, bf16[256,512]{1,0:T(8,128)(2,1)S(1)}, u32[]{:S(2)}, u32[]{:S(2)}) collective-permute-start(bf16[256,512]{1,0:T(8,128)(2,1)S(1)} %add_convert_fusion.15), channel_id=1, source_target_pairs={{0,2},{1,3},{2,4},{3,5},{8,10},{9,11},{10,12},{11,13},{16,18},{17,... | collective-permute-start | bytes 786440 | tf_op jit(solution)/shard_map/ppermute | solution.py:93
  210.5 9.6 %collective-permute-start.26 = (bf16[256,512]{1,0:T(8,128)(2,1)S(1)}, bf16[256,512]{1,0:T(8,128)(2,1)S(1)}, u32[]{:S(2)}, u32[]{:S(2)}) collective-permute-start(bf16[256,512]{1,0:T(8,128)(2,1)S(1)} %fusion.8), channel_id=1, source_target_pairs={{0,2},{1,3},{8,10},{9,11},{16,18},{17,19},{24,26},{25,27}} | collective-permute-start | bytes 786440 | tf_op jit(solution)/shard_map/ppermute | solution.py:93
  216.8 14.6 %collective-permute-start.15 = (bf16[256,512]{1,0:T(8,128)(2,1)S(1)}, bf16[256,512]{1,0:T(8,128)(2,1)S(1)}, u32[]{:S(2)}, u32[]{:S(2)}) collective-permute-start(bf16[256,512]{1,0:T(8,128)(2,1)S(1)} %get-tuple-element.29), channel_id=1, source_target_pairs={{6,4},{7,5},{14,12},{15,13},{22,20},{23,21},{30,28},{31,29}} | collective-permute-start | bytes 786440 | tf_op jit(solution)/shard_map/ppermute | solution.py:96
  220.2 12.0 %collective-permute-start.27 = (bf16[256,512]{1,0:T(8,128)(2,1)S(1)}, bf16[256,512]{1,0:T(8,128)(2,1)S(1)}, u32[]{:S(2)}, u32[]{:S(2)}) collective-permute-start(bf16[256,512]{1,0:T(8,128)(2,1)S(1)} %add_convert_fusion.11), channel_id=1, source_target_pairs={{0,2},{1,3},{2,4},{3,5},{8,10},{9,11},{10,12},{11,13},{16,18},{17,... | collective-permute-start | bytes 786440 | tf_op jit(solution)/shard_map/ppermute | solution.py:93
  226.0 21.6 %collective-permute-start.14 = (bf16[256,512]{1,0:T(8,128)(2,1)S(1)}, bf16[256,512]{1,0:T(8,128)(2,1)}, u32[]{:S(2)}, u32[]{:S(2)}) collective-permute-start(bf16[256,512]{1,0:T(8,128)(2,1)S(1)} %get-tuple-element.28), channel_id=1, source_target_pairs={{0,2},{1,3},{2,4},{3,5},{4,6},{5,7},{8,10},{9,11},{10,12},{11,13},... | collective-permute-start | bytes 786440 | tf_op jit(solution)/shard_map/ppermute | solution.py:93
  234.7 10.4 %collective-permute-start.30 = (bf16[256,512]{1,0:T(8,128)(2,1)}, bf16[256,512]{1,0:T(8,128)(2,1)}, u32[]{:S(2)}, u32[]{:S(2)}) collective-permute-start(bf16[256,512]{1,0:T(8,128)(2,1)} %add_convert_fusion.9), channel_id=1, source_target_pairs={{4,2},{5,3},{6,4},{7,5},{12,10},{13,11},{14,12},{15,13},{20,18},{2... | collective-permute-start | bytes 786440 | tf_op jit(solution)/shard_map/ppermute | solution.py:96
  236.9 10.7 %collective-permute-start.17 = (bf16[256,512]{1,0:T(8,128)(2,1)}, bf16[256,512]{1,0:T(8,128)(2,1)}, u32[]{:S(2)}, u32[]{:S(2)}) collective-permute-start(bf16[256,512]{1,0:T(8,128)(2,1)} %add_convert_fusion.12), channel_id=1, source_target_pairs={{2,0},{3,1},{4,2},{5,3},{6,4},{7,5},{10,8},{11,9},{12,10},{13,11},... | collective-permute-start | bytes 786440 | tf_op jit(solution)/shard_map/ppermute | solution.py:96
  239.6 9.7 %collective-permute-start.28 = (bf16[256,512]{1,0:T(8,128)(2,1)}, bf16[256,512]{1,0:T(8,128)(2,1)S(1)}, u32[]{:S(2)}, u32[]{:S(2)}) collective-permute-start(bf16[256,512]{1,0:T(8,128)(2,1)} %get-tuple-element.30), channel_id=1, source_target_pairs={{0,2},{1,3},{2,4},{3,5},{4,6},{5,7},{8,10},{9,11},{10,12},{11,13},... | collective-permute-start | bytes 786440 | tf_op jit(solution)/shard_map/ppermute | solution.py:93
  246.3 16.1 %collective-permute-start.31 = (bf16[256,512]{1,0:T(8,128)(2,1)S(1)}, bf16[256,512]{1,0:T(8,128)(2,1)S(1)}, u32[]{:S(2)}, u32[]{:S(2)}) collective-permute-start(bf16[256,512]{1,0:T(8,128)(2,1)S(1)} %add_convert_fusion.8), channel_id=1, source_target_pairs={{2,0},{3,1},{4,2},{5,3},{6,4},{7,5},{10,8},{11,9},{12,10},{13,11},... | collective-permute-start | bytes 786440 | tf_op jit(solution)/shard_map/ppermute | solution.py:96
  (43 other events, 625.6 us)
Sparse Core Ops, SparseCore 0:
  57.9 74.9 all-reduce.1

commit v2 on v0

v2 whole, which is shorter than its diff:
```python
import jax
import jax.numpy as jnp
from jax import lax
from jax.experimental import pallas as pl
from jax.experimental.pallas import tpu as pltpu
from jax.sharding import PartitionSpec as P

STREAMS = 2
ROW_TILE = 128
MIB = 1024 * 1024


def nesterov(delta, base_part, momentum_part):
    momentum_next = 0.9 * momentum_part + delta
    base_next = (base_part.astype(jnp.float32) - 0.7 * (delta + 0.9 * momentum_next)).astype(
        jnp.bfloat16
    )
    return (base_next, momentum_next)


def move_perm(chips, active):
    pairs = []
    for z in range(chips):
        if z < chips - 1 and active(z):
            pairs.append((2 * z, 2 * z + 2))
        if z > 0 and active(chips - 1 - z):
            pairs.append((2 * z + 1, 2 * z - 1))
    return pairs


def call(kernel, place, grid, in_specs, out_specs, out_shape, flops, moved, scratch=(), vmem=32):
    return pl.pallas_call(
        kernel,
        grid_spec=pltpu.PrefetchScalarGridSpec(
            num_scalar_prefetch=1,
            grid=grid,
            in_specs=in_specs,
            out_specs=out_specs,
            scratch_shapes=scratch,
        ),
        out_shape=out_shape,
        compiler_params=pltpu.CompilerParams(vmem_limit_bytes=vmem * MIB),
        cost_estimate=pl.CostEstimate(flops=flops, bytes_accessed=moved, transcendentals=0),
    )


def normalise(tokens, gain):
    rows, model = tokens.shape

    def kernel(tokens_ref, gain_ref, out_ref):
        xf = tokens_ref[...].astype(jnp.float32)
        scale = lax.rsqrt(jnp.mean(xf * xf, axis=1, keepdims=True) + 1e-05)
        out_ref[...] = (xf * scale * gain_ref[...]).astype(jnp.bfloat16)

    tile = pl.BlockSpec((ROW_TILE, model), lambda i: (i, 0))
    return pl.pallas_call(
        kernel,
        grid=(rows // ROW_TILE,),
        in_specs=[tile, pl.BlockSpec((1, model), lambda i: (0, 0))],
        out_specs=tile,
        out_shape=jax.ShapeDtypeStruct((rows, model), jnp.bfloat16),
        compiler_params=pltpu.CompilerParams(vmem_limit_bytes=32 * MIB),
        cost_estimate=pl.CostEstimate(
            flops=6 * rows * model, bytes_accessed=4 * rows * model, transcendentals=rows
        ),
    )(tokens, gain[None])


def join_cores(place, own, partner, stream, piece, after):
    rows = own.shape[0]

    def kernel(place_ref, own_ref, partner_ref, *rest):
        core = place_ref[place_ref.shape[0] - 1]
        out_ref = rest[-1]
        out_ref[pl.ds(pl.multiple_of(core * rows, rows), rows), :] = own_ref[...]
        out_ref[pl.ds(pl.multiple_of((1 - core) * rows, rows), rows), :] = partner_ref[...]

    part = pl.BlockSpec((rows, piece), lambda i, place_ref: (0, stream))
    return call(
        kernel,
        place,
        (1,),
        [part, part] + [pl.BlockSpec(memory_space=pl.ANY)] * len(after),
        pl.BlockSpec((2 * rows, piece), lambda i, place_ref: (0, 0)),
        jax.ShapeDtypeStruct((2 * rows, piece), jnp.bfloat16),
        0,
        8 * rows * piece,
    )(place, own, partner, *after)


def project(place, x, pieces, other, chips):
    rows, model = x.shape
    block = model // chips
    piece = pieces[0].shape[1]

    def kernel(place_ref, x_ref, *refs):
        piece_refs, other_ref, out_ref, weight, total = refs[:chips], *refs[chips:]
        step = pl.program_id(0)
        position = place_ref[chips]

        @pl.when(step == 0)
        def _():
            total[...] = jnp.zeros_like(total)
            weight[0] = piece_refs[0][...]
            for p in range(1, chips):

                @pl.when(position >= p)
                def _():
                    weight[p] = piece_refs[p][...]

                @pl.when(position < p)
                def _():
                    weight[p] = other_ref[chips - p - 1]

        total[...] += jnp.dot(x_ref[...], weight[step], preferred_element_type=jnp.float32)

        @pl.when(step == chips - 1)
        def _():
            out_ref[...] = total[...].astype(jnp.bfloat16).T

    whole = pl.BlockSpec((block, piece), lambda i, place_ref: (0, 0))
    return call(
        kernel,
        place,
        (chips,),
        [pl.BlockSpec((rows, block), lambda i, place_ref: (0, place_ref[i]))]
        + [whole] * chips
        + [pl.BlockSpec((chips - 1, block, piece), lambda i, place_ref: (0, 0, 0))],
        pl.BlockSpec((piece, rows), lambda i, place_ref: (0, 0)),
        jax.ShapeDtypeStruct((piece, rows), jnp.bfloat16),
        2 * rows * model * piece,
        2 * rows * model + 4 * model * piece,
        [pltpu.VMEM((chips, block, piece), jnp.bfloat16), pltpu.VMEM((rows, piece), jnp.float32)],
    )(place, x, *pieces, other)


def gradient(place, mid, x, chips, first, count):
    piece, rows = mid.shape
    block = x.shape[1] // chips

    def kernel(place_ref, mid_ref, x_ref, out_ref):
        term = jnp.dot(mid_ref[...], x_ref[...], preferred_element_type=jnp.float32)
        out_ref[0] = term.astype(jnp.bfloat16).T

    return call(
        kernel,
        place,
        (count,),
        [
            pl.BlockSpec((piece, rows), lambda i, place_ref: (0, 0)),
            pl.BlockSpec((rows, block), lambda i, place_ref: (0, place_ref[first + i])),
        ],
        pl.BlockSpec((1, block, piece), lambda i, place_ref: (i, 0, 0)),
        jax.ShapeDtypeStruct((count, block, piece), jnp.bfloat16),
        2 * rows * block * count * piece,
        2 * rows * block * count + 2 * count * block * piece,
    )(place, mid, x)


def per_device(
    tokens,
    norm_gain,
    value_weight,
    output_weight,
    out_cotangent,
    base_params,
    outer_momentum,
    delta_values,
    delta_exponents,
):
    replicas = lax.axis_size("replica")
    devices = lax.axis_size("fsdp")
    chips = devices // 2
    me = lax.axis_index("fsdp")
    chip, core = me // 2, me % 2
    position = jnp.where(core == 0, chip, chips - 1 - chip)
    back = jnp.arange(chips, dtype=jnp.int32)
    behind = jnp.where(core == 0, chip - back + chips, chip + back) % chips
    place = jnp.concatenate([behind, position[None], core[None]]).astype(jnp.int32)

    def swap(value):
        return lax.ppermute(value, "fsdp", [(i, i ^ 1) for i in range(devices)])

    def move(value, active=lambda y: True):
        return lax.ppermute(value, "fsdp", move_perm(chips, active))

    shard = value_weight.shape[1]
    piece = value_weight.shape[2] // STREAMS
    streams = range(STREAMS)
    first_own, second_own = value_weight[0], output_weight[0]
    first_partner, second_partner = swap(first_own), swap(second_own)

    scaled = (
        delta_values[0].astype(jnp.float32)
        * jnp.exp2(delta_exponents[0].astype(jnp.float32))[:, None]
    )
    delta = lax.psum(scaled.astype(jnp.bfloat16), "replica").astype(jnp.float32) * (1.0 / replicas)

    normed = normalise(tokens[0], norm_gain)
    cotangent = out_cotangent[0]

    def partial(rest, other, step, received):
        term = rest[step - 1].astype(jnp.float32) + other[chips - step - 1].astype(jnp.float32)
        if received is not None:
            term = term + received.astype(jnp.float32)
        return term.astype(jnp.bfloat16)

    def terms(x_in, x_out, pieces):
        other = swap(jnp.stack(pieces[1:]))
        mid = project(place, x_in, pieces, other, chips)
        rest = gradient(place, mid, x_out, chips, 1, chips - 1)
        return (rest, swap(rest), gradient(place, mid, x_out, chips, 0, 1)[0])

    def finish(here, received):
        whole = here.astype(jnp.float32) + received.astype(jnp.float32)
        mine = lax.dynamic_slice_in_dim(whole, core * shard, shard, 0)
        partners = lax.dynamic_slice_in_dim(whole, (1 - core) * shard, shard, 0)
        return mine + swap(partners.astype(jnp.bfloat16)).astype(jnp.float32)

    held = [[join_cores(place, first_own, first_partner, j, piece, ())] for j in streams]
    for step in range(1, chips):
        for j in streams:
            held[j].append(move(held[j][-1], lambda y: y >= step - 1))
    sent = [
        join_cores(place, second_own, second_partner, j, piece, (held[j][-1],)) for j in streams
    ]
    first = [terms(normed, cotangent, held[j]) for j in streams]
    later = [[sent[j]] for j in streams]
    received = [move(sent[j]) for j in streams]
    for step in range(1, chips):
        for j in streams:
            later[j].append(received[j])
            rest, other, _ = first[j]
            message = jnp.where(
                position >= step, received[j], partial(rest, other, step, received[j])
            )
            received[j] = move(message)
    output_grad = [finish(first[j][2], received[j]) for j in streams]
    second = [terms(cotangent, normed, later[j]) for j in streams]
    received = [None] * STREAMS
    for step in range(1, chips):
        for j in streams:
            rest, other, _ = second[j]
            message = partial(rest, other, step, received[j])
            received[j] = move(message, lambda y: y <= step - 1)
    value_grad = [finish(second[j][2], received[j]) for j in streams]

    new_base, new_momentum = nesterov(delta, base_params, outer_momentum)
    return (
        jnp.concatenate(value_grad, axis=1)[None],
        jnp.concatenate(output_grad, axis=1)[None],
        new_base,
        new_momentum,
    )


def solution(mesh):
    return jax.shard_map(
        per_device,
        mesh=mesh,
        in_specs=(
            P("replica", "fsdp", None),
            P(),
            P("replica", "fsdp", None),
            P("replica", "fsdp", None),
            P("replica", "fsdp", None),
            P("fsdp", None),
            P("fsdp", None),
            P("replica", "fsdp", None),
            P("replica", "fsdp"),
        ),
        out_specs=(
            P("replica", "fsdp", None),
            P("replica", "fsdp", None),
            P("fsdp", None),
            P("fsdp", None),
        ),
        check_vma=False,
    )
```

time: 219 us -> 270 us (1.23)
  waiting for transfers between devices: 144 us -> 47.6 us
  starting transfers between devices: 0.38 us -> 89.2 us
  Pallas kernels: 0 us -> 49.8 us
  matrix products: 36.2 us -> 0 us
  local copies, waits for them, and re-layouts: 2.89 us -> 25.7 us
  other arithmetic: 19.6 us -> 41.6 us
    ppermute x0 -> x34, starting transfers between devices: none -> 89.2 us  [the longest x20 67.8 us: move(): return lax.ppermute(value, 'fsdp', move_perm(chips, active))]
    reduce_scatter x2 -> x0, waiting for transfers between devices: 72.1 us -> none  [the longest x1 47.8 us: per_device(): lax.psum_scatter(lax.dot_general(normed_cols, value_cot, (((0,), (0,)), (...]
    all_gather x2 -> x0, waiting for transfers between devices: 70.5 us -> none  [the longest x1 41.4 us: per_device(): lax.all_gather(value_weight[0], 'fsdp', axis=0, tiled=True)]
    pallas_call x0 -> x17, Pallas kernels: none -> 49.8 us  [the longest x4 21.3 us: project(): call(kernel, place, (chips,), [pl.BlockSpec((rows, block), lambda i, plac...]
    dot_general x2 -> x0, matrix products: 36.2 us -> none  [the longest x1 18.2 us: per_device(): lax.dot_general(normed_cols, value_cot, (((0,), (0,)), ((), ())), preferr...]
    psum x1, waiting for transfers between devices: 0.03 us -> 28.1 us  [per_device(): lax.psum(scaled.astype(jnp.bfloat16), 'replica').astype(jnp.float32)]
    unnamed x5 -> x70, local copies, waits for them, and re-layouts: 2.89 us -> 25.6 us
    ppermute x0 -> x34, waiting for transfers between devices: none -> 19.6 us  [the longest x20 17.5 us: move(): return lax.ppermute(value, 'fsdp', move_perm(chips, active))]
  transfers between devices with their start and end apart: 5 -> 35, of which waited for: 4 -> 10; matrix products, arithmetic and copies ran while one was open for 25% -> 15% of each run, Pallas kernels for 0% -> 18%
where the time goes in v2:
time: 270 us; the launch traced here: 269 us
  starting transfers between devices  89.2 us (33%)
  Pallas kernels  49.8 us (18%)
  waiting for transfers between devices  47.6 us (18%)
  other arithmetic  41.6 us (15%)
  local copies, waits for them, and re-layouts  25.7 us (10%)
  between operations  14.8 us (5%)
    ppermute x20, starting transfers between devices, move(): return lax.ppermute(value, 'fsdp', move_perm(chips, active))  67.8 us
    psum x1, waiting for transfers between devices, per_device(): lax.psum(scaled.astype(jnp.bfloat16), 'replica').astype(jnp.float32)  28.1 us
    unnamed x70, local copies, waits for them, and re-layouts  25.6 us
    ppermute x14, starting transfers between devices, swap(): return lax.ppermute(value, 'fsdp', [(i, i ^ 1) for i in range(devices)])  21.4 us
    pallas_call x4, Pallas kernels, project(): call(kernel, place, (chips,), [pl.BlockSpec((rows, block), lambda i, plac...  21.3 us
    pallas_call x8, Pallas kernels, gradient(): call(kernel, place, (count,), [pl.BlockSpec((piece, rows), lambda i, plac...  19.8 us
    ppermute x20, waiting for transfers between devices, move(): return lax.ppermute(value, 'fsdp', move_perm(chips, active))  17.5 us
    select_n x6, other arithmetic, per_device(): jnp.where(position >= step, received[j], partial(rest, other, step, recei...  11.8 us
  transfers between devices with their start and end apart: 35, of which 10 were waited for; matrix products, arithmetic and copies ran while one was open for 15% of the time, Pallas kernels for 18%

profile of v2, /device:TPU:0, one launch (start us, length us, event | category | flops | bytes accessed | tf_op | source)
XLA Modules:
  0.0 269.0 jit_solution(2606983996092576732)
XLA Ops:
  7.8 1.7 collective-permute-done.1.partner_ref
  11.1 4.9 %collective-permute-start.2 = (bf16[1024,256]{1,0:T(8,128)(2,1)S(1)}, bf16[1024,256]{1,0:T(8,128)(2,1)S(1)}, u32[]{:S(2)}, u32[]{:S(2)}) collective-permute-start(bf16[1024,256]{1,0:T(8,128)(2,1)S(1)} %shard_map.120.refs_0_), channel_id=1, source_target_pairs={{0,2},{2,4},{3,1},{4,6},{5,3},{7,5},{8,10},{10,12},{11,9},{12,14},... | collective-permute-start | bytes 1572872 | tf_op jit(solution)/shard_map/ppermute | solution.py:185
  16.6 3.5 %collective-permute-start.16 = (bf16[1024,256]{1,0:T(8,128)(2,1)S(1)}, bf16[1024,256]{1,0:T(8,128)(2,1)S(1)}, u32[]{:S(2)}, u32[]{:S(2)}) collective-permute-start(bf16[1024,256]{1,0:T(8,128)(2,1)S(1)} %shard_map.128.refs_0_), channel_id=1, source_target_pairs={{0,2},{2,4},{3,1},{4,6},{5,3},{7,5},{8,10},{10,12},{11,9},{12,14},... | collective-permute-start | bytes 1572872 | tf_op jit(solution)/shard_map/ppermute | solution.py:185
  20.1 2.6 collective-permute-done.2.refs_1_
  23.3 4.9 %collective-permute-done.16.refs_1_ = bf16[1024,256]{1,0:T(8,128)(2,1)S(1)} collective-permute-done((bf16[1024,256]{1,0:T(8,128)(2,1)S(1)}, bf16[1024,256]{1,0:T(8,128)(2,1)S(1)}, u32[]{:S(2)}, u32[]{:S(2)}) %collective-permute-start.16) | collective-permute-done | bytes 524320 | tf_op jit(solution)/shard_map/ppermute | solution.py:185
  31.7 14.5 %collective-permute-start.6 = (bf16[3,1024,256]{2,1,0:T(8,128)(2,1)}, bf16[3,1024,256]{2,1,0:T(8,128)(2,1)S(1)}, u32[]{:S(2)}, u32[]{:S(2)}) collective-permute-start(bf16[3,1024,256]{2,1,0:T(8,128)(2,1)} %pad_maximum_fusion), channel_id=1, source_target_pairs={{0,1},{1,0},{2,3},{3,2},{4,5},{5,4},{6,7},{7,6},{8,9},{9,8},{10,11... | collective-permute-start | bytes 4718600 | tf_op jit(solution)/shard_map/ppermute | solution.py:182
  47.5 4.3 %collective-permute-start.20 = (bf16[3,1024,256]{2,1,0:T(8,128)(2,1)}, bf16[3,1024,256]{2,1,0:T(8,128)(2,1)S(1)}, u32[]{:S(2)}, u32[]{:S(2)}) collective-permute-start(bf16[3,1024,256]{2,1,0:T(8,128)(2,1)} %pad_maximum_fusion.2), channel_id=1, source_target_pairs={{0,1},{1,0},{2,3},{3,2},{4,5},{5,4},{6,7},{7,6},{8,9},{9,8},{10,11... | collective-permute-start | bytes 4718600 | tf_op jit(solution)/shard_map/ppermute | solution.py:182
  51.8 3.4 %copy-done.6 = bf16[1,1024,4096]{2,1,0:T(8,128)(2,1)S(1)} copy-done((bf16[1,1024,4096]{2,1,0:T(8,128)(2,1)S(1)}, bf16[1,1024,4096]{2,1,0:T(8,128)(2,1)}, u32[]{:S(2)}) %copy-start.6) | copy-done | bytes 8388632
  55.2 4.8 %shard_map.122.x_ref = bf16[1024,4096]{1,0:T(8,128)(2,1)S(1)} custom-call(bf16[1024,4096]{1,0:T(8,128)(2,1)S(1)} %bitcast.107, f32[1,4096]{1,0:T(1,128)S(1)} %bitcast.122), custom_call_target="tpu_custom_call" | custom-call | flops 25165824 | bytes 16777216 | tf_op jit(solution)/shard_map/pallas_call | solution.py:56
  60.0 4.4 %shard_map.123.mid_ref = bf16[256,1024]{1,0:T(8,128)(2,1)S(1)} custom-call(s32[6]{0:T(128)S(1)} %pad_add_fusion.place_ref, bf16[1024,4096]{1,0:T(8,128)(2,1)S(1)} %shard_map.122.x_ref, bf16[1024,256]{1,0:T(8,128)(2,1)S(1)} %shard_map.120.refs_0_, bf16[1024,256]{1,0:T(8,128)(2,1)S(1)} %collective-permute-done.2.refs_1_, ...), custom_call_target="tpu_custom_call" | custom-call | flops 2147483648 | bytes 12582912 | tf_op jit(solution)/shard_map/pallas_call | solution.py:122
  64.5 3.4 %shard_map.124 = bf16[3,1024,256]{2,1,0:T(8,128)(2,1)S(1)} custom-call(s32[6]{0:T(128)S(1)} %pad_add_fusion.place_ref, bf16[256,1024]{1,0:T(8,128)(2,1)S(1)} %shard_map.123.mid_ref, bf16[1024,4096]{1,0:T(8,128)(2,1)S(1)} %bitcast.101), custom_call_target="tpu_custom_call" | custom-call | flops 1610612736 | bytes 7864320 | tf_op jit(solution)/shard_map/pallas_call | solution.py:145
  68.8 4.4 %shard_map.130.mid_ref = bf16[256,1024]{1,0:T(8,128)(2,1)S(1)} custom-call(s32[6]{0:T(128)S(1)} %pad_add_fusion.place_ref, bf16[1024,4096]{1,0:T(8,128)(2,1)S(1)} %shard_map.122.x_ref, bf16[1024,256]{1,0:T(8,128)(2,1)S(1)} %shard_map.128.refs_0_, bf16[1024,256]{1,0:T(8,128)(2,1)S(1)} %collective-permute-done.16.refs_1_, ...), custom_call_target="tpu_custom_call" | custom-call | flops 2147483648 | bytes 12582912 | tf_op jit(solution)/shard_map/pallas_call | solution.py:122
  73.3 3.4 %shard_map.131 = bf16[3,1024,256]{2,1,0:T(8,128)(2,1)S(1)} custom-call(s32[6]{0:T(128)S(1)} %pad_add_fusion.place_ref, bf16[256,1024]{1,0:T(8,128)(2,1)S(1)} %shard_map.130.mid_ref, bf16[1024,4096]{1,0:T(8,128)(2,1)S(1)} %bitcast.102), custom_call_target="tpu_custom_call" | custom-call | flops 1610612736 | bytes 7864320 | tf_op jit(solution)/shard_map/pallas_call | solution.py:145
  78.6 2.6 collective-permute-start.5
  85.6 5.6 %collective-permute-start.19 = (bf16[1024,256]{1,0:T(8,128)(2,1)}, bf16[1024,256]{1,0:T(8,128)(2,1)}, u32[]{:S(2)}, u32[]{:S(2)}) collective-permute-start(bf16[1024,256]{1,0:T(8,128)(2,1)} %shard_map.129.refs_0_), channel_id=1, source_target_pairs={{0,2},{2,4},{3,1},{4,6},{5,3},{7,5},{8,10},{10,12},{11,9},{12,14},... | collective-permute-start | bytes 1572872 | tf_op jit(solution)/shard_map/ppermute | solution.py:185
  91.2 2.4 fusion.11
  93.6 4.4 %collective-permute-start.8 = (bf16[1024,256]{1,0:T(8,128)(2,1)}, bf16[1024,256]{1,0:T(8,128)(2,1)}, u32[]{:S(2)}, u32[]{:S(2)}) collective-permute-start(bf16[1024,256]{1,0:T(8,128)(2,1)} %fusion.11), channel_id=1, source_target_pairs={{0,2},{2,4},{3,1},{4,6},{5,3},{7,5},{8,10},{10,12},{11,9},{12,14},... | collective-permute-start | bytes 1572872 | tf_op jit(solution)/shard_map/ppermute | solution.py:185
  98.0 1.6 fusion.13
  99.6 3.8 %collective-permute-start.22 = (bf16[1024,256]{1,0:T(8,128)(2,1)S(1)}, bf16[1024,256]{1,0:T(8,128)(2,1)S(1)}, u32[]{:S(2)}, u32[]{:S(2)}) collective-permute-start(bf16[1024,256]{1,0:T(8,128)(2,1)S(1)} %fusion.13), channel_id=1, source_target_pairs={{0,2},{2,4},{3,1},{4,6},{5,3},{7,5},{8,10},{10,12},{11,9},{12,14},... | collective-permute-start | bytes 1572872 | tf_op jit(solution)/shard_map/ppermute | solution.py:185
  104.2 1.6 fusion.12
  105.8 4.4 %collective-permute-start.9 = (bf16[1024,256]{1,0:T(8,128)(2,1)S(1)}, bf16[1024,256]{1,0:T(8,128)(2,1)S(1)}, u32[]{:S(2)}, u32[]{:S(2)}) collective-permute-start(bf16[1024,256]{1,0:T(8,128)(2,1)S(1)} %fusion.12), channel_id=1, source_target_pairs={{0,2},{2,4},{3,1},{4,6},{5,3},{7,5},{8,10},{10,12},{11,9},{12,14},... | collective-permute-start | bytes 1572872 | tf_op jit(solution)/shard_map/ppermute | solution.py:185
  111.1 2.1 fusion.14
  113.2 4.9 %collective-permute-start.23 = (bf16[1024,256]{1,0:T(8,128)(2,1)}, bf16[1024,256]{1,0:T(8,128)(2,1)}, u32[]{:S(2)}, u32[]{:S(2)}) collective-permute-start(bf16[1024,256]{1,0:T(8,128)(2,1)} %fusion.14), channel_id=1, source_target_pairs={{0,2},{2,4},{3,1},{4,6},{5,3},{7,5},{8,10},{10,12},{11,9},{12,14},... | collective-permute-start | bytes 1572872 | tf_op jit(solution)/shard_map/ppermute | solution.py:185
  118.1 2.8 %pad_maximum_fusion.1 = bf16[3,1024,256]{2,1,0:T(8,128)(2,1)} fusion(bf16[1,1024,256]{2,1,0:T(8,128)(2,1)S(1)} %bitcast.109, bf16[1,1024,256]{2,1,0:T(8,128)(2,1)} %bitcast.13, bf16[1,1024,256]{2,1,0:T(8,128)(2,1)} %bitcast.12), kind=kLoop, calls=%fused_computation.6 | loop fusion | flops 1572864 | bytes 3145728 | tf_op jit(solution)/shard_map/stack | solution.py:209
  120.9 2.2 fusion
  124.3 2.7 pad_maximum_fusion.3
  127.0 2.5 fusion.15
  129.5 5.2 %collective-permute-start.30 = (bf16[1024,256]{1,0:T(8,128)(2,1)}, bf16[1024,256]{1,0:T(8,128)(2,1)}, u32[]{:S(2)}, u32[]{:S(2)}) collective-permute-start(bf16[1024,256]{1,0:T(8,128)(2,1)} %fusion.15), channel_id=1, source_target_pairs={{0,2},{2,4},{3,1},{4,6},{5,3},{7,5},{8,10},{10,12},{11,9},{12,14},... | collective-permute-start | bytes 1572872 | tf_op jit(solution)/shard_map/ppermute | solution.py:185
  134.7 3.5 %copy-done.2 = bf16[1,1024,4096]{2,1,0:T(8,128)(2,1)S(1)} copy-done((bf16[1,1024,4096]{2,1,0:T(8,128)(2,1)S(1)}, bf16[1,1024,4096]{2,1,0:T(8,128)(2,1)}, u32[]{:S(2)}) %copy-start.2) | copy-done | bytes 8388632
  138.2 6.2 %shard_map.125.mid_ref = bf16[256,1024]{1,0:T(8,128)(2,1)S(1)} custom-call(s32[6]{0:T(128)S(1)} %pad_add_fusion.place_ref, bf16[1024,4096]{1,0:T(8,128)(2,1)S(1)} %bitcast.103, bf16[1024,256]{1,0:T(8,128)(2,1)} %shard_map.121.refs_0_, bf16[1024,256]{1,0:T(8,128)(2,1)} %collective-permute-done.5.refs_1_, bf16[1024,256]{1,0:T(8,128)(2,1)} %collective-permute-done.8.refs_2_, ...), custom_call_target="tpu_custom_call" | custom-call | flops 2147483648 | bytes 12582912 | tf_op jit(solution)/shard_map/pallas_call | solution.py:122
  144.4 3.4 %copy-done.1 = bf16[1024,4096]{1,0:T(8,128)(2,1)S(1)} copy-done((bf16[1024,4096]{1,0:T(8,128)(2,1)S(1)}, bf16[1024,4096]{1,0:T(8,128)(2,1)}, u32[]{:S(2)}) %copy-start.1) | copy-done | bytes 8388632
  147.8 3.4 %shard_map.127 = bf16[3,1024,256]{2,1,0:T(8,128)(2,1)S(1)} custom-call(s32[6]{0:T(128)S(1)} %pad_add_fusion.place_ref, bf16[256,1024]{1,0:T(8,128)(2,1)S(1)} %shard_map.125.mid_ref, bf16[1024,4096]{1,0:T(8,128)(2,1)S(1)} %copy-done.1), custom_call_target="tpu_custom_call" | custom-call | flops 1610612736 | bytes 7864320 | tf_op jit(solution)/shard_map/pallas_call | solution.py:145
  151.4 3.5 %copy-done.3 = bf16[1,1024,4096]{2,1,0:T(8,128)(2,1)S(1)} copy-done((bf16[1,1024,4096]{2,1,0:T(8,128)(2,1)S(1)}, bf16[1,1024,4096]{2,1,0:T(8,128)(2,1)}, u32[]{:S(2)}) %copy-start.3) | copy-done | bytes 8388632
  154.9 6.2 %shard_map.132.mid_ref = bf16[256,1024]{1,0:T(8,128)(2,1)S(1)} custom-call(s32[6]{0:T(128)S(1)} %pad_add_fusion.place_ref, bf16[1024,4096]{1,0:T(8,128)(2,1)S(1)} %bitcast.104, bf16[1024,256]{1,0:T(8,128)(2,1)} %shard_map.129.refs_0_, bf16[1024,256]{1,0:T(8,128)(2,1)} %collective-permute-done.19.refs_1_, bf16[1024,256]{1,0:T(8,128)(2,1)S(1)} %copy-done.8, ...), custom_call_target="tpu_custom_call" | custom-call | flops 2147483648 | bytes 12582912 | tf_op jit(solution)/shard_map/pallas_call | solution.py:122
  161.2 4.3 %shard_map.134 = bf16[3,1024,256]{2,1,0:T(8,128)(2,1)} custom-call(s32[6]{0:T(128)S(1)} %pad_add_fusion.place_ref, bf16[256,1024]{1,0:T(8,128)(2,1)S(1)} %shard_map.132.mid_ref, bf16[1024,4096]{1,0:T(8,128)(2,1)S(1)} %bitcast.96), custom_call_target="tpu_custom_call" | custom-call | flops 1610612736 | bytes 7864320 | tf_op jit(solution)/shard_map/pallas_call | solution.py:145
  165.8 28.1 %all-reduce.2.cloned.1.call-done = bf16[8192,128]{1,0:T(8,128)(2,1)} async-done(((bf16[8192,128]{1,0:T(8,128)(2,1)}), bf16[8192,128]{1,0:T(8,128)(2,1)}) %all-reduce.2.cloned.1.call-update) | async-done | bytes 2097168 | tf_op jit(solution)/shard_map/psum | solution.py:197
  193.9 7.6 %subtract_convert_fusion = (bf16[8192,128]{1,0:T(8,128)(2,1)}, f32[8192,128]{1,0:T(8,128)}) fusion(bf16[8192,128]{1,0:T(8,128)(2,1)} %all-reduce.2.cloned.1.call-done, bf16[8192,128]{1,0:T(8,128)(2,1)} %param.14, f32[8192,128]{1,0:T(8,128)} %param.15), kind=kLoop, calls=%fused_computation.2 | loop fusion | flops 10485760 | bytes 14680064 | tf_op jit(solution)/shard_map/convert_element_type | solution.py:15
  201.5 3.4 %copy-done.4 = bf16[1,1024,4096]{2,1,0:T(8,128)(2,1)S(1)} copy-done((bf16[1,1024,4096]{2,1,0:T(8,128)(2,1)S(1)}, bf16[1,1024,4096]{2,1,0:T(8,128)(2,1)}, u32[]{:S(2)}) %copy-start.4) | copy-done | bytes 8388632
  206.2 3.4 %copy-done.5 = bf16[1,1024,4096]{2,1,0:T(8,128)(2,1)S(1)} copy-done((bf16[1,1024,4096]{2,1,0:T(8,128)(2,1)S(1)}, bf16[1,1024,4096]{2,1,0:T(8,128)(2,1)}, u32[]{:S(2)}) %copy-start.5) | copy-done | bytes 8388632
  210.9 1.6 fusion.16
  212.5 3.4 %collective-permute-start.32 = (bf16[1024,256]{1,0:T(8,128)(2,1)S(1)}, bf16[1024,256]{1,0:T(8,128)(2,1)S(1)}, u32[]{:S(2)}, u32[]{:S(2)}) collective-permute-start(bf16[1024,256]{1,0:T(8,128)(2,1)S(1)} %fusion.16), channel_id=1, source_target_pairs={{0,2},{2,4},{3,1},{4,6},{5,3},{7,5},{8,10},{10,12},{11,9},{12,14},... | collective-permute-start | bytes 1572872 | tf_op jit(solution)/shard_map/ppermute | solution.py:185
  218.4 3.4 %collective-permute-start.12 = (bf16[1024,256]{1,0:T(8,128)(2,1)S(1)}, bf16[1024,256]{1,0:T(8,128)(2,1)S(1)}, u32[]{:S(2)}, u32[]{:S(2)}) collective-permute-start(bf16[1024,256]{1,0:T(8,128)(2,1)S(1)} %fusion.17), channel_id=1, source_target_pairs={{0,2},{7,5},{8,10},{15,13},{16,18},{23,21},{24,26},{31,29}} | collective-permute-start | bytes 1572872 | tf_op jit(solution)/shard_map/ppermute | solution.py:185
  224.9 3.6 %collective-permute-done.12 = bf16[1024,256]{1,0:T(8,128)(2,1)S(1)} collective-permute-done((bf16[1024,256]{1,0:T(8,128)(2,1)S(1)}, bf16[1024,256]{1,0:T(8,128)(2,1)S(1)}, u32[]{:S(2)}, u32[]{:S(2)}) %collective-permute-start.12) | collective-permute-done | bytes 524320 | tf_op jit(solution)/shard_map/ppermute | solution.py:185
  229.7 4.7 %collective-permute-start.13 = (bf16[1024,256]{1,0:T(8,128)(2,1)S(1)}, bf16[1024,256]{1,0:T(8,128)(2,1)S(1)}, u32[]{:S(2)}, u32[]{:S(2)}) collective-permute-start(bf16[1024,256]{1,0:T(8,128)(2,1)S(1)} %fusion.7), channel_id=1, source_target_pairs={{0,2},{2,4},{5,3},{7,5},{8,10},{10,12},{13,11},{15,13},{16,18},{18... | collective-permute-start | bytes 1572872 | tf_op jit(solution)/shard_map/ppermute | solution.py:185
  235.8 4.1 %collective-permute-start.27 = (bf16[1024,256]{1,0:T(8,128)(2,1)S(1)}, bf16[1024,256]{1,0:T(8,128)(2,1)S(1)}, u32[]{:S(2)}, u32[]{:S(2)}) collective-permute-start(bf16[1024,256]{1,0:T(8,128)(2,1)S(1)} %fusion.3), channel_id=1, source_target_pairs={{0,2},{2,4},{5,3},{7,5},{8,10},{10,12},{13,11},{15,13},{16,18},{18... | collective-permute-start | bytes 1572872 | tf_op jit(solution)/shard_map/ppermute | solution.py:185
  242.3 4.5 %collective-permute-start.14 = (bf16[1024,256]{1,0:T(8,128)(2,1)S(1)}, bf16[1024,256]{1,0:T(8,128)(2,1)S(1)}, u32[]{:S(2)}, u32[]{:S(2)}) collective-permute-start(bf16[1024,256]{1,0:T(8,128)(2,1)S(1)} %fusion.8), channel_id=1, source_target_pairs={{0,2},{2,4},{3,1},{4,6},{5,3},{7,5},{8,10},{10,12},{11,9},{12,14},... | collective-permute-start | bytes 1572872 | tf_op jit(solution)/shard_map/ppermute | solution.py:185
  248.3 4.2 %collective-permute-start.28 = (bf16[1024,256]{1,0:T(8,128)(2,1)S(1)}, bf16[1024,256]{1,0:T(8,128)(2,1)S(1)}, u32[]{:S(2)}, u32[]{:S(2)}) collective-permute-start(bf16[1024,256]{1,0:T(8,128)(2,1)S(1)} %fusion.4), channel_id=1, source_target_pairs={{0,2},{2,4},{3,1},{4,6},{5,3},{7,5},{8,10},{10,12},{11,9},{12,14},... | collective-permute-start | bytes 1572872 | tf_op jit(solution)/shard_map/ppermute | solution.py:185
  255.6 3.6 %collective-permute-done.28 = bf16[1024,256]{1,0:T(8,128)(2,1)S(1)} collective-permute-done((bf16[1024,256]{1,0:T(8,128)(2,1)S(1)}, bf16[1024,256]{1,0:T(8,128)(2,1)S(1)}, u32[]{:S(2)}, u32[]{:S(2)}) %collective-permute-start.28) | collective-permute-done | bytes 524320 | tf_op jit(solution)/shard_map/ppermute | solution.py:185
  (148 shorter events, 39.2 us)
Async XLA Ops:
  7.2 186.7 %all-reduce.2.cloned.1.call-start = ((), (), s32[]{:S(2)}) async-start(), calls=%async_computation | async-start | bytes 4194304 | tf_op jit(solution)/shard_map/psum | solution.py:197
  7.2 2.3 collective-permute-start.1
  11.1 11.5 %collective-permute-start.2 = (bf16[1024,256]{1,0:T(8,128)(2,1)S(1)}, bf16[1024,256]{1,0:T(8,128)(2,1)S(1)}, u32[]{:S(2)}, u32[]{:S(2)}) collective-permute-start(bf16[1024,256]{1,0:T(8,128)(2,1)S(1)} %shard_map.120.refs_0_), channel_id=1, source_target_pairs={{0,2},{2,4},{3,1},{4,6},{5,3},{7,5},{8,10},{10,12},{11,9},{12,14},... | collective-permute-start | bytes 1572872 | tf_op jit(solution)/shard_map/ppermute | solution.py:185
  16.6 11.7 %collective-permute-start.16 = (bf16[1024,256]{1,0:T(8,128)(2,1)S(1)}, bf16[1024,256]{1,0:T(8,128)(2,1)S(1)}, u32[]{:S(2)}, u32[]{:S(2)}) collective-permute-start(bf16[1024,256]{1,0:T(8,128)(2,1)S(1)} %shard_map.128.refs_0_), channel_id=1, source_target_pairs={{0,2},{2,4},{3,1},{4,6},{5,3},{7,5},{8,10},{10,12},{11,9},{12,14},... | collective-permute-start | bytes 1572872 | tf_op jit(solution)/shard_map/ppermute | solution.py:185
  22.6 6.3 %collective-permute-start.3 = (bf16[1024,256]{1,0:T(8,128)(2,1)S(1)}, bf16[1024,256]{1,0:T(8,128)(2,1)S(1)}, u32[]{:S(2)}, u32[]{:S(2)}) collective-permute-start(bf16[1024,256]{1,0:T(8,128)(2,1)S(1)} %collective-permute-done.2.refs_1_), channel_id=1, source_target_pairs={{2,4},{3,1},{4,6},{5,3},{10,12},{11,9},{12,14},{13,11},{18,20},{19... | collective-permute-start | bytes 1572872 | tf_op jit(solution)/shard_map/ppermute | solution.py:185
  28.3 1.4 collective-permute-start.17
  29.0 1.4 collective-permute-start.4
  29.7 16.5 %collective-permute-start.18 = (bf16[1024,256]{1,0:T(8,128)(2,1)S(1)}, bf16[1024,256]{1,0:T(8,128)(2,1)S(1)}, u32[]{:S(2)}, u32[]{:S(2)}) collective-permute-start(bf16[1024,256]{1,0:T(8,128)(2,1)S(1)} %collective-permute-done.17.refs_2_), channel_id=1, source_target_pairs={{3,1},{4,6},{11,9},{12,14},{19,17},{20,22},{27,25},{28,30}} | collective-permute-start | bytes 1572872 | tf_op jit(solution)/shard_map/ppermute | solution.py:185
  30.4 21.4 %copy-start.26 = (f32[4096]{0:T(1024)S(1)}, f32[4096]{0:T(1024)}, u32[]{:S(2)}) copy-start(f32[4096]{0:T(1024)} %param.10) | copy-start | bytes 49156
  31.7 28.3 %collective-permute-start.6 = (bf16[3,1024,256]{2,1,0:T(8,128)(2,1)}, bf16[3,1024,256]{2,1,0:T(8,128)(2,1)S(1)}, u32[]{:S(2)}, u32[]{:S(2)}) collective-permute-start(bf16[3,1024,256]{2,1,0:T(8,128)(2,1)} %pad_maximum_fusion), channel_id=1, source_target_pairs={{0,1},{1,0},{2,3},{3,2},{4,5},{5,4},{6,7},{7,6},{8,9},{9,8},{10,11... | collective-permute-start | bytes 4718600 | tf_op jit(solution)/shard_map/ppermute | solution.py:182
  46.2 22.6 %copy-start.11 = (bf16[1024,256]{1,0:T(8,128)(2,1)}, bf16[1024,256]{1,0:T(8,128)(2,1)S(1)}, u32[]{:S(2)}) copy-start(bf16[1024,256]{1,0:T(8,128)(2,1)S(1)} %collective-permute-done.18.rest_0_.refs_3_) | copy-start | bytes 1572868
  46.2 18.3 %slice-start.4 = ((s8[8388608]{0:T(1024)(128)(4,1)}), s8[4194304]{0:T(1024)(128)(4,1)S(1)}, s32[]{:S(2)}) async-start(s8[8388608]{0:T(1024)(128)(4,1)} %bitcast.99), calls=%async_computation.5 | async-start | bytes 8388608
  47.5 21.3 %collective-permute-start.20 = (bf16[3,1024,256]{2,1,0:T(8,128)(2,1)}, bf16[3,1024,256]{2,1,0:T(8,128)(2,1)S(1)}, u32[]{:S(2)}, u32[]{:S(2)}) collective-permute-start(bf16[3,1024,256]{2,1,0:T(8,128)(2,1)} %pad_maximum_fusion.2), channel_id=1, source_target_pairs={{0,1},{1,0},{2,3},{3,2},{4,5},{5,4},{6,7},{7,6},{8,9},{9,8},{10,11... | collective-permute-start | bytes 4718600 | tf_op jit(solution)/shard_map/ppermute | solution.py:182
  55.2 9.3 %slice-start.5 = ((s8[8388608]{0:T(1024)(128)(4,1)}), s8[4194304]{0:T(1024)(128)(4,1)S(1)}, s32[]{:S(2)}) async-start(s8[8388608]{0:T(1024)(128)(4,1)} %bitcast.99), calls=%async_computation.6 | async-start | bytes 8388608
  60.0 8.8 %copy-start = (bf16[1024,4096]{1,0:T(8,128)(2,1)}, bf16[1024,4096]{1,0:T(8,128)(2,1)S(1)}, u32[]{:S(2)}) copy-start(bf16[1024,4096]{1,0:T(8,128)(2,1)S(1)} %shard_map.122.x_ref) | copy-start | bytes 25165828
  67.9 23.2 %collective-permute-start.7 = (bf16[3,1024,256]{2,1,0:T(8,128)(2,1)S(1)}, bf16[3,1024,256]{2,1,0:T(8,128)(2,1)}, u32[]{:S(2)}, u32[]{:S(2)}) collective-permute-start(bf16[3,1024,256]{2,1,0:T(8,128)(2,1)S(1)} %shard_map.124), channel_id=1, source_target_pairs={{0,1},{1,0},{2,3},{3,2},{4,5},{5,4},{6,7},{7,6},{8,9},{9,8},{10,11... | collective-permute-start | bytes 4718600 | tf_op jit(solution)/shard_map/ppermute | solution.py:182
  68.7 8.5 %collective-permute-start = (bf16[512,512]{1,0:T(8,128)(2,1)S(1)}, bf16[512,512]{1,0:T(8,128)(2,1)S(1)}, u32[]{:S(2)}, u32[]{:S(2)}) collective-permute-start(bf16[512,512]{1,0:T(8,128)(2,1)S(1)} %bitcast.112), channel_id=1, source_target_pairs={{0,1},{1,0},{2,3},{3,2},{4,5},{5,4},{6,7},{7,6},{8,9},{9,8},{10,11... | collective-permute-start | bytes 1572872 | tf_op jit(solution)/shard_map/ppermute | solution.py:182
  76.7 21.3 %collective-permute-start.21 = (bf16[3,1024,256]{2,1,0:T(8,128)(2,1)S(1)}, bf16[3,1024,256]{2,1,0:T(8,128)(2,1)}, u32[]{:S(2)}, u32[]{:S(2)}) collective-permute-start(bf16[3,1024,256]{2,1,0:T(8,128)(2,1)S(1)} %shard_map.131), channel_id=1, source_target_pairs={{0,1},{1,0},{2,3},{3,2},{4,5},{5,4},{6,7},{7,6},{8,9},{9,8},{10,11... | collective-permute-start | bytes 4718600 | tf_op jit(solution)/shard_map/ppermute | solution.py:182
  78.6 12.6 %collective-permute-start.5 = (bf16[1024,256]{1,0:T(8,128)(2,1)}, bf16[1024,256]{1,0:T(8,128)(2,1)}, u32[]{:S(2)}, u32[]{:S(2)}) collective-permute-start(bf16[1024,256]{1,0:T(8,128)(2,1)} %shard_map.121.refs_0_), channel_id=1, source_target_pairs={{0,2},{2,4},{3,1},{4,6},{5,3},{7,5},{8,10},{10,12},{11,9},{12,14},... | collective-permute-start | bytes 1572872 | tf_op jit(solution)/shard_map/ppermute | solution.py:185
  85.6 12.4 %collective-permute-start.19 = (bf16[1024,256]{1,0:T(8,128)(2,1)}, bf16[1024,256]{1,0:T(8,128)(2,1)}, u32[]{:S(2)}, u32[]{:S(2)}) collective-permute-start(bf16[1024,256]{1,0:T(8,128)(2,1)} %shard_map.129.refs_0_), channel_id=1, source_target_pairs={{0,2},{2,4},{3,1},{4,6},{5,3},{7,5},{8,10},{10,12},{11,9},{12,14},... | collective-permute-start | bytes 1572872 | tf_op jit(solution)/shard_map/ppermute | solution.py:185
  93.6 10.6 %collective-permute-start.8 = (bf16[1024,256]{1,0:T(8,128)(2,1)}, bf16[1024,256]{1,0:T(8,128)(2,1)}, u32[]{:S(2)}, u32[]{:S(2)}) collective-permute-start(bf16[1024,256]{1,0:T(8,128)(2,1)} %fusion.11), channel_id=1, source_target_pairs={{0,2},{2,4},{3,1},{4,6},{5,3},{7,5},{8,10},{10,12},{11,9},{12,14},... | collective-permute-start | bytes 1572872 | tf_op jit(solution)/shard_map/ppermute | solution.py:185
  99.6 10.6 %copy-start.28 = (s32[1,8192]{1,0:T(1,128)S(1)}, s32[1,8192]{1,0:T(1,128)}, u32[]{:S(2)}) copy-start(s32[1,8192]{1,0:T(1,128)} %param.17) | copy-start | bytes 98308
  99.6 10.7 %collective-permute-start.22 = (bf16[1024,256]{1,0:T(8,128)(2,1)S(1)}, bf16[1024,256]{1,0:T(8,128)(2,1)S(1)}, u32[]{:S(2)}, u32[]{:S(2)}) collective-permute-start(bf16[1024,256]{1,0:T(8,128)(2,1)S(1)} %fusion.13), channel_id=1, source_target_pairs={{0,2},{2,4},{3,1},{4,6},{5,3},{7,5},{8,10},{10,12},{11,9},{12,14},... | collective-permute-start | bytes 1572872 | tf_op jit(solution)/shard_map/ppermute | solution.py:185
  105.8 12.3 %collective-permute-start.9 = (bf16[1024,256]{1,0:T(8,128)(2,1)S(1)}, bf16[1024,256]{1,0:T(8,128)(2,1)S(1)}, u32[]{:S(2)}, u32[]{:S(2)}) collective-permute-start(bf16[1024,256]{1,0:T(8,128)(2,1)S(1)} %fusion.12), channel_id=1, source_target_pairs={{0,2},{2,4},{3,1},{4,6},{5,3},{7,5},{8,10},{10,12},{11,9},{12,14},... | collective-permute-start | bytes 1572872 | tf_op jit(solution)/shard_map/ppermute | solution.py:185
  113.2 11.1 %collective-permute-start.23 = (bf16[1024,256]{1,0:T(8,128)(2,1)}, bf16[1024,256]{1,0:T(8,128)(2,1)}, u32[]{:S(2)}, u32[]{:S(2)}) collective-permute-start(bf16[1024,256]{1,0:T(8,128)(2,1)} %fusion.14), channel_id=1, source_target_pairs={{0,2},{2,4},{3,1},{4,6},{5,3},{7,5},{8,10},{10,12},{11,9},{12,14},... | collective-permute-start | bytes 1572872 | tf_op jit(solution)/shard_map/ppermute | solution.py:185
  120.9 13.8 %collective-permute-start.10 = (bf16[3,1024,256]{2,1,0:T(8,128)(2,1)}, bf16[3,1024,256]{2,1,0:T(8,128)(2,1)}, u32[]{:S(2)}, u32[]{:S(2)}) collective-permute-start(bf16[3,1024,256]{2,1,0:T(8,128)(2,1)} %pad_maximum_fusion.1), channel_id=1, source_target_pairs={{0,1},{1,0},{2,3},{3,2},{4,5},{5,4},{6,7},{7,6},{8,9},{9,8},{10,11... | collective-permute-start | bytes 4718600 | tf_op jit(solution)/shard_map/ppermute | solution.py:182
  127.0 24.3 %collective-permute-start.24 = (bf16[3,1024,256]{2,1,0:T(8,128)(2,1)}, bf16[3,1024,256]{2,1,0:T(8,128)(2,1)}, u32[]{:S(2)}, u32[]{:S(2)}) collective-permute-start(bf16[3,1024,256]{2,1,0:T(8,128)(2,1)} %pad_maximum_fusion.3), channel_id=1, source_target_pairs={{0,1},{1,0},{2,3},{3,2},{4,5},{5,4},{6,7},{7,6},{8,9},{9,8},{10,11... | collective-permute-start | bytes 4718600 | tf_op jit(solution)/shard_map/ppermute | solution.py:182
  127.0 7.7 %copy-start.10 = (bf16[1024,256]{1,0:T(8,128)(2,1)S(1)}, bf16[1024,256]{1,0:T(8,128)(2,1)}, u32[]{:S(2)}) copy-start(bf16[1024,256]{1,0:T(8,128)(2,1)} %copy-done.9) | copy-start | bytes 1572868
  129.5 86.5 %collective-permute-start.30 = (bf16[1024,256]{1,0:T(8,128)(2,1)}, bf16[1024,256]{1,0:T(8,128)(2,1)}, u32[]{:S(2)}, u32[]{:S(2)}) collective-permute-start(bf16[1024,256]{1,0:T(8,128)(2,1)} %fusion.15), channel_id=1, source_target_pairs={{0,2},{2,4},{3,1},{4,6},{5,3},{7,5},{8,10},{10,12},{11,9},{12,14},... | collective-permute-start | bytes 1572872 | tf_op jit(solution)/shard_map/ppermute | solution.py:185
  147.8 13.3 %slice-start = ((s8[8388608]{0:T(1024)(128)(4,1)}), s8[4194304]{0:T(1024)(128)(4,1)S(1)}, s32[]{:S(2)}) async-start(s8[8388608]{0:T(1024)(128)(4,1)} %bitcast.95), calls=%async_computation.1 | async-start | bytes 8388608
  151.2 9.9 %slice-start.1 = ((s8[8388608]{0:T(1024)(128)(4,1)}), s8[4194304]{0:T(1024)(128)(4,1)S(1)}, s32[]{:S(2)}) async-start(s8[8388608]{0:T(1024)(128)(4,1)} %bitcast.95), calls=%async_computation.2 | async-start | bytes 8388608
  151.3 66.0 %collective-permute-start.11 = (bf16[3,1024,256]{2,1,0:T(8,128)(2,1)S(1)}, bf16[3,1024,256]{2,1,0:T(8,128)(2,1)}, u32[]{:S(2)}, u32[]{:S(2)}) collective-permute-start(bf16[3,1024,256]{2,1,0:T(8,128)(2,1)S(1)} %shard_map.127), channel_id=1, source_target_pairs={{0,1},{1,0},{2,3},{3,2},{4,5},{5,4},{6,7},{7,6},{8,9},{9,8},{10,11... | collective-permute-start | bytes 4718600 | tf_op jit(solution)/shard_map/ppermute | solution.py:182
  165.4 56.4 %collective-permute-start.25 = (bf16[3,1024,256]{2,1,0:T(8,128)(2,1)}, bf16[3,1024,256]{2,1,0:T(8,128)(2,1)}, u32[]{:S(2)}, u32[]{:S(2)}) collective-permute-start(bf16[3,1024,256]{2,1,0:T(8,128)(2,1)} %shard_map.134), channel_id=1, source_target_pairs={{0,1},{1,0},{2,3},{3,2},{4,5},{5,4},{6,7},{7,6},{8,9},{9,8},{10,11... | collective-permute-start | bytes 4718600 | tf_op jit(solution)/shard_map/ppermute | solution.py:182
  193.9 7.6 %copy-start.14 = (bf16[256,1024]{1,0:T(8,128)(2,1)S(1)}, bf16[256,1024]{1,0:T(8,128)(2,1)}, u32[]{:S(2)}) copy-start(bf16[256,1024]{1,0:T(8,128)(2,1)} %copy-done.13) | copy-start | bytes 1572868
  212.5 12.3 %collective-permute-start.32 = (bf16[1024,256]{1,0:T(8,128)(2,1)S(1)}, bf16[1024,256]{1,0:T(8,128)(2,1)S(1)}, u32[]{:S(2)}, u32[]{:S(2)}) collective-permute-start(bf16[1024,256]{1,0:T(8,128)(2,1)S(1)} %fusion.16), channel_id=1, source_target_pairs={{0,2},{2,4},{3,1},{4,6},{5,3},{7,5},{8,10},{10,12},{11,9},{12,14},... | collective-permute-start | bytes 1572872 | tf_op jit(solution)/shard_map/ppermute | solution.py:185
  217.2 22.9 %collective-permute-start.31 = (bf16[512,256]{1,0:T(8,128)(2,1)S(1)}, bf16[512,256]{1,0:T(8,128)(2,1)S(1)}, u32[]{:S(2)}, u32[]{:S(2)}) collective-permute-start(bf16[512,256]{1,0:T(8,128)(2,1)S(1)} %dynamic-slice_convert_fusion.1), channel_id=1, source_target_pairs={{0,1},{1,0},{2,3},{3,2},{4,5},{5,4},{6,7},{7,6},{8,9},{9,8},{10,11... | collective-permute-start | bytes 786440 | tf_op jit(solution)/shard_map/ppermute | solution.py:182
  218.4 10.1 %collective-permute-start.12 = (bf16[1024,256]{1,0:T(8,128)(2,1)S(1)}, bf16[1024,256]{1,0:T(8,128)(2,1)S(1)}, u32[]{:S(2)}, u32[]{:S(2)}) collective-permute-start(bf16[1024,256]{1,0:T(8,128)(2,1)S(1)} %fusion.17), channel_id=1, source_target_pairs={{0,2},{7,5},{8,10},{15,13},{16,18},{23,21},{24,26},{31,29}} | collective-permute-start | bytes 1572872 | tf_op jit(solution)/shard_map/ppermute | solution.py:185
  221.9 30.7 %slice-start.2 = ((s8[8388608]{0:T(1024)(128)(4,1)}), s8[4194304]{0:T(1024)(128)(4,1)S(1)}, s32[]{:S(2)}) async-start(s8[8388608]{0:T(1024)(128)(4,1)} %bitcast.97), calls=%async_computation.3 | async-start | bytes 8388608
  223.4 11.1 %collective-permute-start.26 = (bf16[1024,256]{1,0:T(8,128)(2,1)S(1)}, bf16[1024,256]{1,0:T(8,128)(2,1)S(1)}, u32[]{:S(2)}, u32[]{:S(2)}) collective-permute-start(bf16[1024,256]{1,0:T(8,128)(2,1)S(1)} %fusion.18), channel_id=1, source_target_pairs={{0,2},{7,5},{8,10},{15,13},{16,18},{23,21},{24,26},{31,29}} | collective-permute-start | bytes 1572872 | tf_op jit(solution)/shard_map/ppermute | solution.py:185
  229.7 22.9 %slice-start.3 = ((s8[8388608]{0:T(1024)(128)(4,1)}), s8[4194304]{0:T(1024)(128)(4,1)S(1)}, s32[]{:S(2)}) async-start(s8[8388608]{0:T(1024)(128)(4,1)} %bitcast.97), calls=%async_computation.4 | async-start | bytes 8388608
  229.7 11.3 %collective-permute-start.13 = (bf16[1024,256]{1,0:T(8,128)(2,1)S(1)}, bf16[1024,256]{1,0:T(8,128)(2,1)S(1)}, u32[]{:S(2)}, u32[]{:S(2)}) collective-permute-start(bf16[1024,256]{1,0:T(8,128)(2,1)S(1)} %fusion.7), channel_id=1, source_target_pairs={{0,2},{2,4},{5,3},{7,5},{8,10},{10,12},{13,11},{15,13},{16,18},{18... | collective-permute-start | bytes 1572872 | tf_op jit(solution)/shard_map/ppermute | solution.py:185
  235.8 11.0 %collective-permute-start.27 = (bf16[1024,256]{1,0:T(8,128)(2,1)S(1)}, bf16[1024,256]{1,0:T(8,128)(2,1)S(1)}, u32[]{:S(2)}, u32[]{:S(2)}) collective-permute-start(bf16[1024,256]{1,0:T(8,128)(2,1)S(1)} %fusion.3), channel_id=1, source_target_pairs={{0,2},{2,4},{5,3},{7,5},{8,10},{10,12},{13,11},{15,13},{16,18},{18... | collective-permute-start | bytes 1572872 | tf_op jit(solution)/shard_map/ppermute | solution.py:185
  240.0 12.5 %collective-permute-start.33 = (bf16[512,256]{1,0:T(8,128)(2,1)S(1)}, bf16[512,256]{1,0:T(8,128)(2,1)S(1)}, u32[]{:S(2)}, u32[]{:S(2)}) collective-permute-start(bf16[512,256]{1,0:T(8,128)(2,1)S(1)} %dynamic-slice_convert_fusion), channel_id=1, source_target_pairs={{0,1},{1,0},{2,3},{3,2},{4,5},{5,4},{6,7},{7,6},{8,9},{9,8},{10,11... | collective-permute-start | bytes 786440 | tf_op jit(solution)/shard_map/ppermute | solution.py:182
  242.3 10.3 %copy-start.18 = (bf16[256,1024]{1,0:T(8,128)(2,1)S(1)}, bf16[256,1024]{1,0:T(8,128)(2,1)}, u32[]{:S(2)}) copy-start(bf16[256,1024]{1,0:T(8,128)(2,1)} %copy-done.17) | copy-start | bytes 1572868
  242.3 13.0 %collective-permute-start.14 = (bf16[1024,256]{1,0:T(8,128)(2,1)S(1)}, bf16[1024,256]{1,0:T(8,128)(2,1)S(1)}, u32[]{:S(2)}, u32[]{:S(2)}) collective-permute-start(bf16[1024,256]{1,0:T(8,128)(2,1)S(1)} %fusion.8), channel_id=1, source_target_pairs={{0,2},{2,4},{3,1},{4,6},{5,3},{7,5},{8,10},{10,12},{11,9},{12,14},... | collective-permute-start | bytes 1572872 | tf_op jit(solution)/shard_map/ppermute | solution.py:185
  248.3 10.9 %collective-permute-start.28 = (bf16[1024,256]{1,0:T(8,128)(2,1)S(1)}, bf16[1024,256]{1,0:T(8,128)(2,1)S(1)}, u32[]{:S(2)}, u32[]{:S(2)}) collective-permute-start(bf16[1024,256]{1,0:T(8,128)(2,1)S(1)} %fusion.4), channel_id=1, source_target_pairs={{0,2},{2,4},{3,1},{4,6},{5,3},{7,5},{8,10},{10,12},{11,9},{12,14},... | collective-permute-start | bytes 1572872 | tf_op jit(solution)/shard_map/ppermute | solution.py:185
  255.5 5.0 %collective-permute-start.15 = (bf16[512,256]{1,0:T(8,128)(2,1)S(1)}, bf16[512,256]{1,0:T(8,128)(2,1)S(1)}, u32[]{:S(2)}, u32[]{:S(2)}) collective-permute-start(bf16[512,256]{1,0:T(8,128)(2,1)S(1)} %dynamic-slice_convert_fusion.3), channel_id=1, source_target_pairs={{0,1},{1,0},{2,3},{3,2},{4,5},{5,4},{6,7},{7,6},{8,9},{9,8},{10,11... | collective-permute-start | bytes 786440 | tf_op jit(solution)/shard_map/ppermute | solution.py:182
  259.3 1.6 collective-permute-start.29
  (22 other events, 57.6 us)
Sparse Core Ops, SparseCore 0:
  123.3 70.5 all-reduce.1

commit v3 on v0

v3 whole, which is shorter than its diff:
```python
import jax
import jax.numpy as jnp
from jax import lax
from jax.experimental import pallas as pl
from jax.experimental.pallas import tpu as pltpu
from jax.sharding import PartitionSpec as P

HALVES = 2
ROW_TILE = 128
KERNEL_FLOPS = 20 * 10**9
ANY = pl.BlockSpec(memory_space=pl.ANY)


def move_perm(chips, active):
    pairs = []
    for z in range(chips):
        if z < chips - 1 and active(z):
            pairs.append((2 * z, 2 * z + 2))
        if z > 0 and active(chips - 1 - z):
            pairs.append((2 * z + 1, 2 * z - 1))
    return pairs


class Order:
    def __init__(self, place):
        self.place = place
        self.last = ()

    def __call__(
        self, kernel, args, in_specs, out_shape, scratch, vmem, after=(), aliases=None, grid=1,
        out_specs=None,
    ):
        after = self.last + tuple(after)
        count = len(args)

        def ordered(place_ref, *refs):
            kernel(place_ref, *refs[:count], *refs[count + len(after) :])

        result = pl.pallas_call(
            ordered,
            grid_spec=pltpu.PrefetchScalarGridSpec(
                num_scalar_prefetch=1,
                grid=(grid,),
                in_specs=in_specs + [ANY] * len(after),
                out_specs=out_specs or [ANY] * len(out_shape),
                scratch_shapes=scratch,
            ),
            out_shape=out_shape,
            input_output_aliases={1 + i: o for i, o in (aliases or {}).items()},
            compiler_params=pltpu.CompilerParams(vmem_limit_bytes=vmem * 1024 * 1024),
            cost_estimate=pl.CostEstimate(flops=KERNEL_FLOPS, bytes_accessed=1, transcendentals=0),
            name=kernel.__qualname__.split(".")[0],
        )(self.place, *args, *after)
        self.last = (result[0],)
        return result


def copies(pairs, sems):
    started = [pltpu.make_async_copy(a, b, sems.at[i]) for i, (a, b) in enumerate(pairs)]
    for copy in started:
        copy.start()
    return started


def fence(order, *values, after=()):
    def fence(*refs):
        pass

    shapes = [jax.ShapeDtypeStruct(v.shape, v.dtype) for v in values]
    aliases = {i: i for i in range(len(values))}
    return order(fence, values, [ANY] * len(values), shapes, [], 4, after, aliases)


def normalise(order, tokens, gain, after=()):
    rows, model = tokens.shape

    def run(_, tokens_ref, gain_ref, out_ref):
        xf = tokens_ref[...].astype(jnp.float32)
        scale = lax.rsqrt(jnp.mean(xf * xf, axis=1, keepdims=True) + 1e-05)
        out_ref[...] = (xf * scale * gain_ref[...]).astype(jnp.bfloat16)

    tile = pl.BlockSpec((ROW_TILE, model), lambda i, _: (i, 0))
    return order(
        run,
        (tokens, gain[None]),
        [tile, pl.BlockSpec((1, model), lambda i, _: (0, 0))],
        [jax.ShapeDtypeStruct((rows, model), jnp.bfloat16)],
        [],
        16,
        after,
        grid=rows // ROW_TILE,
        out_specs=[tile],
    )[0]


def join_cores(order, own, partner, after=()):
    rows, features = own.shape
    piece = features // HALVES

    def run(place_ref, own_ref, partner_ref, *refs):
        out_refs, sems = refs[:HALVES], refs[HALVES]
        core = place_ref[place_ref.shape[0] - 1]
        pairs = []
        for j, out_ref in enumerate(out_refs):
            cols = pl.ds(j * piece, piece)
            for source, where in ((own_ref, core), (partner_ref, 1 - core)):
                target = out_ref.at[pl.ds(pl.multiple_of(where * rows, rows), rows)]
                pairs.append((source.at[:, cols], target))
        for copy in copies(pairs, sems):
            copy.wait()

    return order(
        run,
        (own, partner),
        [ANY, ANY],
        [jax.ShapeDtypeStruct((2 * rows, piece), jnp.bfloat16)] * HALVES,
        [pltpu.SemaphoreType.DMA((2 * HALVES,))],
        4,
        after,
    )


def join_cores_across(order, own, partner, after=()):
    features, rows = own.shape

    def run(place_ref, own_ref, partner_ref, out_ref, sems):
        core = place_ref[place_ref.shape[0] - 1]
        pairs = []
        for source, where in ((own_ref, core), (partner_ref, 1 - core)):
            cols = pl.ds(pl.multiple_of(where * rows, rows), rows)
            pairs.append((source, out_ref.at[:, cols]))
        for copy in copies(pairs, sems):
            copy.wait()

    return order(
        run,
        (own, partner),
        [ANY, ANY],
        [jax.ShapeDtypeStruct((features, 2 * rows), jnp.bfloat16)],
        [pltpu.SemaphoreType.DMA((2,))],
        4,
        after,
    )[0]


def assemble(order, pieces, others, across, after=()):
    chips, parts = len(pieces), len(pieces[0])
    first, second = pieces[0][0].shape
    shape = (first * parts, second * chips) if across else (first * chips, second * parts)

    def run(place_ref, *refs):
        piece_refs = [refs[p * parts : (p + 1) * parts] for p in range(chips)]
        rest = refs[chips * parts :]
        other_refs = [rest[p * parts : (p + 1) * parts] for p in range(chips - 1)]
        out_ref, sems = rest[(chips - 1) * parts :]
        position = place_ref[chips]

        def pairs(p, source):
            for j in range(parts):
                if across:
                    at = pl.ds(pl.multiple_of(place_ref[p] * second, second), second)
                    target = out_ref.at[pl.ds(j * first, first), at]
                else:
                    at = pl.ds(pl.multiple_of(place_ref[p] * first, first), first)
                    target = out_ref.at[at, pl.ds(j * second, second)]
                yield pltpu.make_async_copy(source[j], target, sems.at[p * parts + j])

        def begin(p, source):
            for copy in pairs(p, source):
                copy.start()

        begin(0, piece_refs[0])
        for p in range(1, chips):
            pl.when(position >= p)(lambda p=p: begin(p, piece_refs[p]))
            pl.when(position < p)(lambda p=p: begin(p, other_refs[chips - p - 1]))
        for p in range(chips):
            for copy in pairs(p, piece_refs[0]):
                copy.wait()

    arrays = [part for shard in (*pieces, *others) for part in shard]
    return order(
        run,
        tuple(arrays),
        [ANY] * len(arrays),
        [jax.ShapeDtypeStruct(shape, jnp.bfloat16)],
        [pltpu.SemaphoreType.DMA((chips * parts,))],
        4,
        after,
    )[0]


def nesterov(delta, base_part, momentum_part):
    momentum_next = 0.9 * momentum_part + delta
    base_next = (base_part.astype(jnp.float32) - 0.7 * (delta + 0.9 * momentum_next)).astype(
        jnp.bfloat16
    )
    return (base_next, momentum_next)


def per_device(
    tokens,
    norm_gain,
    value_weight,
    output_weight,
    out_cotangent,
    base_params,
    outer_momentum,
    delta_values,
    delta_exponents,
):
    replicas = lax.axis_size("replica")
    devices = lax.axis_size("fsdp")
    chips = devices // 2
    me = lax.axis_index("fsdp")
    chip, core = me // 2, me % 2
    position = jnp.where(core == 0, chip, chips - 1 - chip)
    steps = jnp.arange(chips, dtype=jnp.int32)
    behind = jnp.where(core == 0, chip - steps + chips, chip + steps) % chips
    order = Order(jnp.concatenate([behind, position[None], core[None]]).astype(jnp.int32))
    shard = value_weight.shape[1]
    block = 2 * shard
    cotangent = out_cotangent[0]
    bf16, f32 = jnp.bfloat16, jnp.float32

    def swap(value):
        return lax.ppermute(value, "fsdp", [(i, i ^ 1) for i in range(devices)])

    def move(value, active=lambda y: True):
        return lax.ppermute(value, "fsdp", move_perm(chips, active))

    class Gradient:
        def __init__(self, mid, x):
            terms = lax.dot_general(mid, x, (((0,), (0,)), ((), ())), preferred_element_type=f32)
            self.terms = terms.astype(bf16)
            self.across = [None] + [swap(self.block(behind[chips - s])) for s in range(1, chips)]
            self.arrived = None

        def block(self, where):
            return lax.dynamic_slice_in_dim(self.terms, where * block, block, 1)

        def message(self, step):
            term = self.block(behind[step]).astype(f32) + self.across[step].astype(f32)
            if self.arrived is not None:
                term = term + self.arrived.astype(f32)
            return term.astype(bf16)

        def reduce(self, step):
            message = self.message(step)
            self.arrived = move(message, lambda y: y <= step - 1)
            return message

        def finish(self):
            whole = self.block(chip).astype(f32) + self.arrived.astype(f32)
            mine = lax.dynamic_slice_in_dim(whole, core * shard, shard, 1)
            partners = lax.dynamic_slice_in_dim(whole, (1 - core) * shard, shard, 1)
            return (mine + swap(partners.astype(bf16)).astype(f32)).T

    first_own, second_own = value_weight[0], output_weight[0].T
    first_partner, second_partner = swap(first_own), swap(second_own)

    along = list(join_cores(order, first_own, first_partner, (second_partner,)))
    pieces, others = [list(along)], []
    normed = normalise(order, tokens[0], norm_gain)
    for step in range(1, chips):
        along = [move(part, lambda y: y >= step - 1) for part in along]
        if step == 1:
            along = [fence(order, along[0])[0], *along[1:]]
        pieces.append(list(along))
        others.append([swap(part) for part in along])
    weight = assemble(order, pieces, others, False)
    values = jnp.dot(normed, weight, preferred_element_type=f32).astype(bf16)

    message = join_cores_across(order, second_own, second_partner, (pieces[-1][0],))
    arrived = move(message)
    values = fence(order, values, after=(arrived,))[0]
    first = Gradient(values, cotangent)
    pieces, others = [[message]], []
    for step in range(1, chips):
        pieces.append([arrived])
        others.append([swap(arrived)])
        first.arrived = arrived
        message = jnp.where(position >= step, arrived, first.message(step))
        arrived = move(message)
    first.arrived = arrived
    weight = assemble(order, pieces, others, True, (message,))

    half = weight.shape[0] // HALVES
    second = []
    for j in range(HALVES):
        part = weight[j * half : (j + 1) * half]
        mid = lax.dot_general(
            cotangent, part, (((1,), (1,)), ((), ())), preferred_element_type=f32
        ).astype(bf16)
        if j == HALVES - 1:
            mid = fence(order, mid, after=(arrived,))[0]
        second.append(Gradient(mid, normed))
    for step in range(1, chips):
        for gradient in second:
            gradient.reduce(step)
    output_grad = first.finish()

    bits = replicas.bit_length() - 1
    if replicas != 1 << bits or bits < 1:
        raise ValueError("replicas")
    half = base_params.shape[0] // 2
    sums = []
    for index in range(2):
        rows = slice(index * half, (index + 1) * half)
        scale = jnp.exp2(delta_exponents[0, rows].astype(f32))[:, None]
        total = delta_values[0, rows].astype(f32) * scale
        for turn in range(bits):
            mine = total.astype(bf16)
            bit = 1 << ((turn + index) % bits)
            theirs = lax.ppermute(mine, "replica", [(i, i ^ bit) for i in range(replicas)])
            total = mine.astype(f32) + theirs.astype(f32)
        sums.append(total)
    delta = jnp.concatenate(sums) * (1.0 / replicas)
    new_base, new_momentum = nesterov(delta, base_params, outer_momentum)
    value_grad = jnp.concatenate([gradient.finish() for gradient in second], axis=1)
    return (value_grad[None], output_grad[None], new_base, new_momentum)


def solution(mesh):
    return jax.shard_map(
        per_device,
        mesh=mesh,
        in_specs=(
            P("replica", "fsdp", None),
            P(),
            P("replica", "fsdp", None),
            P("replica", "fsdp", None),
            P("replica", "fsdp", None),
            P("fsdp", None),
            P("fsdp", None),
            P("replica", "fsdp", None),
            P("replica", "fsdp"),
        ),
        out_specs=(
            P("replica", "fsdp", None),
            P("replica", "fsdp", None),
            P("fsdp", None),
            P("fsdp", None),
        ),
        check_vma=False,
    )
```

time: 219 us -> 207 us (0.945)
  waiting for transfers between devices: 144 us -> 31.3 us
  starting transfers between devices: 0.38 us -> 78 us
  local copies, waits for them, and re-layouts: 2.89 us -> 20.6 us
  Pallas kernels: 0 us -> 11.9 us
  between operations: 15.2 us -> 3.52 us
  other arithmetic: 19.6 us -> 30.3 us
  matrix products: 36.2 us -> 29.9 us
    ppermute x0 -> x43, starting transfers between devices: none -> 78 us  [the longest x16 50.1 us: move(): return lax.ppermute(value, 'fsdp', move_perm(chips, active))]
    reduce_scatter x2 -> x0, waiting for transfers between devices: 72.1 us -> none  [the longest x1 47.8 us: per_device(): lax.psum_scatter(lax.dot_general(normed_cols, value_cot, (((0,), (0,)), (...]
    all_gather x2 -> x0, waiting for transfers between devices: 70.5 us -> none  [the longest x1 41.4 us: per_device(): lax.all_gather(value_weight[0], 'fsdp', axis=0, tiled=True)]
    ppermute x0 -> x43, waiting for transfers between devices: none -> 31.3 us  [the longest x16 21.6 us: move(): return lax.ppermute(value, 'fsdp', move_perm(chips, active))]
    unnamed x5 -> x63, local copies, waits for them, and re-layouts: 2.89 us -> 18.1 us
    pallas_call x0 -> x8, Pallas kernels: none -> 11.9 us  [__call__(): pl.pallas_call(ordered, grid_spec=pltpu.PrefetchScalarGridSpec(num_scalar...]
    select_n x0 -> x4, other arithmetic: none -> 8.12 us  [the longest x3 8.11 us: per_device(): message = jnp.where(position >= step, arrived, first.message(step))]
    convert_element_type x1 -> x9, other arithmetic: 3.44 us -> 10.2 us  [the longest x3 8.72 us: per_device(): mine = total.astype(bf16)]
  transfers between devices with their start and end apart: 5 -> 43, of which waited for: 4 -> 12; matrix products, arithmetic and copies ran while one was open for 25% -> 28% of each run, Pallas kernels for 0% -> 4%
where the time goes in v3:
time: 207 us; the launch traced here: 206 us
  starting transfers between devices  78 us (38%)
  waiting for transfers between devices  31.3 us (15%)
  other arithmetic  30.3 us (15%)
  matrix products  29.9 us (14%)
  local copies, waits for them, and re-layouts  20.6 us (10%)
  Pallas kernels  11.9 us (6%)
  between operations  3.52 us (2%)
    ppermute x16, starting transfers between devices, move(): return lax.ppermute(value, 'fsdp', move_perm(chips, active))  50.1 us
    ppermute x23, starting transfers between devices, swap(): return lax.ppermute(value, 'fsdp', [(i, i ^ 1) for i in range(devices)])  21.7 us
    ppermute x16, waiting for transfers between devices, move(): return lax.ppermute(value, 'fsdp', move_perm(chips, active))  21.6 us
    dot_general x3, matrix products, __init__(): lax.dot_general(mid, x, (((0,), (0,)), ((), ())), preferred_element_type=...  18.4 us
    unnamed x63, local copies, waits for them, and re-layouts  18.1 us
    pallas_call x8, Pallas kernels, __call__(): pl.pallas_call(ordered, grid_spec=pltpu.PrefetchScalarGridSpec(num_scalar...  11.9 us
    convert_element_type x3, other arithmetic, per_device(): mine = total.astype(bf16)  8.72 us
    select_n x3, other arithmetic, per_device(): message = jnp.where(position >= step, arrived, first.message(step))  8.11 us
  transfers between devices with their start and end apart: 43, of which 12 were waited for; matrix products, arithmetic and copies ran while one was open for 28% of the time, Pallas kernels for 4%

profile of v3, /device:TPU:0, one launch (start us, length us, event | category | flops | bytes accessed | tf_op | source)
XLA Modules:
  0.0 205.6 jit_solution(11368509015851470756)
XLA Ops:
  6.7 4.9 %collective-permute-start.2 = (bf16[1024,256]{1,0:T(8,128)(2,1)S(1)}, bf16[1024,256]{1,0:T(8,128)(2,1)S(1)}, u32[]{:S(2)}, u32[]{:S(2)}) collective-permute-start(bf16[1024,256]{1,0:T(8,128)(2,1)S(1)} %get-tuple-element.6.refs_2_.refs_0_), channel_id=1, source_target_pairs={{0,2},{2,4},{3,1},{4,6},{5,3},{7,5},{8,10},{10,12},{11,9},{12,14},... | collective-permute-start | bytes 1572872 | tf_op jit(solution)/shard_map/ppermute | solution.py:229
  11.6 3.5 %collective-permute-start.3 = (bf16[1024,256]{1,0:T(8,128)(2,1)S(1)}, bf16[1024,256]{1,0:T(8,128)(2,1)S(1)}, u32[]{:S(2)}, u32[]{:S(2)}) collective-permute-start(bf16[1024,256]{1,0:T(8,128)(2,1)S(1)} %get-tuple-element.7.refs_1_), channel_id=1, source_target_pairs={{0,2},{2,4},{3,1},{4,6},{5,3},{7,5},{8,10},{10,12},{11,9},{12,14},... | collective-permute-start | bytes 1572872 | tf_op jit(solution)/shard_map/ppermute | solution.py:229
  15.1 5.4 %normalise.1.refs_1_ = bf16[1024,4096]{1,0:T(8,128)(2,1)S(1)} custom-call(s32[6]{0:T(128)S(1)} %pad_add_fusion.place_ref, bf16[1024,4096]{1,0:T(8,128)(2,1)S(1)} %bitcast.60, f32[1,4096]{1,0:T(1,128)S(1)} %bitcast.63, bf16[1024,256]{1,0:T(8,128)(2,1)S(1)} %get-tuple-element.6.refs_2_.refs_0_), custom_call_target="tpu_custom_call" | custom-call | flops 20000000000 | bytes 1 | tf_op jit(solution)/shard_map/normalise/pallas_call | solution.py:39
  21.1 2.8 %copy-done = bf16[1024,4096]{1,0:T(8,128)(2,1)} copy-done((bf16[1024,4096]{1,0:T(8,128)(2,1)}, bf16[1024,4096]{1,0:T(8,128)(2,1)S(1)}, u32[]{:S(2)}) %copy-start) | copy-done | bytes 8388632
  29.8 7.8 %collective-permute-start.9 = (bf16[1024,256]{1,0:T(8,128)(2,1)S(1)}, bf16[1024,256]{1,0:T(8,128)(2,1)}, u32[]{:S(2)}, u32[]{:S(2)}) collective-permute-start(bf16[1024,256]{1,0:T(8,128)(2,1)S(1)} %collective-permute-done.3.refs_3_), channel_id=1, source_target_pairs={{0,1},{1,0},{2,3},{3,2},{4,5},{5,4},{6,7},{7,6},{8,9},{9,8},{10,11... | collective-permute-start | bytes 1572872 | tf_op jit(solution)/shard_map/ppermute | solution.py:226
  39.0 3.0 %collective-permute-start.12 = (bf16[1024,256]{1,0:T(8,128)(2,1)}, bf16[1024,256]{1,0:T(8,128)(2,1)}, u32[]{:S(2)}, u32[]{:S(2)}) collective-permute-start(bf16[1024,256]{1,0:T(8,128)(2,1)} %collective-permute-done.6.refs_6_.refs_3_), channel_id=1, source_target_pairs={{0,1},{1,0},{2,3},{3,2},{4,5},{5,4},{6,7},{7,6},{8,9},{9,8},{10,11... | collective-permute-start | bytes 1572872 | tf_op jit(solution)/shard_map/ppermute | solution.py:226
  41.9 5.6 %collective-permute-start.13 = (bf16[1024,256]{1,0:T(8,128)(2,1)}, bf16[1024,256]{1,0:T(8,128)(2,1)}, u32[]{:S(2)}, u32[]{:S(2)}) collective-permute-start(bf16[1024,256]{1,0:T(8,128)(2,1)} %collective-permute-done.7.refs_7_), channel_id=1, source_target_pairs={{0,1},{1,0},{2,3},{3,2},{4,5},{5,4},{6,7},{7,6},{8,9},{9,8},{10,11... | collective-permute-start | bytes 1572872 | tf_op jit(solution)/shard_map/ppermute | solution.py:226
  51.6 2.4 %assemble.2.refs_2_ = bf16[4096,512]{1,0:T(8,128)(2,1)S(1)} custom-call(s32[6]{0:T(128)S(1)} %pad_add_fusion.place_ref, bf16[1024,256]{1,0:T(8,128)(2,1)S(1)} %get-tuple-element.6.refs_2_.refs_0_, bf16[1024,256]{1,0:T(8,128)(2,1)S(1)} %get-tuple-element.7.refs_1_, bf16[1024,256]{1,0:T(8,128)(2,1)S(1)} %copy-done.10, ...), custom_call_target="tpu_custom_call" | custom-call | flops 20000000000 | bytes 1 | tf_op jit(solution)/shard_map/assemble/pallas_call | solution.py:39
  54.8 2.0 collective-permute-start.14
  57.8 4.5 %convolution_convert_fusion.2.refs_0_ = bf16[1024,512]{1,0:T(8,128)(2,1)S(1)} fusion(bf16[1024,4096]{1,0:T(8,128)(2,1)S(1)} %copy-done.1, bf16[4096,512]{1,0:T(8,128)(2,1)S(1)} %assemble.2.refs_2_), kind=kOutput, calls=%fused_computation.29 | convolution fusion | flops 4295491584 | bytes 13631488 | tf_op jit(solution)/shard_map/dot_general | solution.py:271
  62.3 6.7 %collective-permute-done.14.refs_2_.refs_1_ = bf16[512,1024]{1,0:T(8,128)(2,1)S(1)} collective-permute-done((bf16[512,1024]{1,0:T(8,128)(2,1)S(1)}, bf16[512,1024]{1,0:T(8,128)(2,1)S(1)}, u32[]{:S(2)}, u32[]{:S(2)}) %collective-permute-start.14) | collective-permute-done | bytes 1048608 | tf_op jit(solution)/shard_map/ppermute | solution.py:229
  69.6 4.9 %fusion.6 = bf16[512,4096]{1,0:T(8,128)(2,1)S(1)} fusion(bf16[1024,512]{1,0:T(8,128)(2,1)S(1)} %fence.4.refs_7_, bf16[1,1024,4096]{2,1,0:T(8,128)(2,1)S(1)} %bitcast.67), kind=kOutput, calls=%fused_computation.6 | convolution fusion | flops 4297064448 | bytes 13631488 | tf_op jit(solution)/shard_map/dot_general | solution.py:233
  74.8 1.9 copy-done.18
  76.7 1.6 collective-permute-start.15
  79.1 1.6 collective-permute-done.15
  80.7 3.6 %fusion.13 = (bf16[512,1024]{1,0:T(8,128)(2,1)}, bf16[512,1024]{1,0:T(8,128)(2,1)}) fusion(bf16[512,1024]{1,0:T(8,128)(2,1)S(1)} %collective-permute-done.14.refs_2_.refs_1_, bf16[512,1024]{1,0:T(8,128)(2,1)} %collective-permute-done.15, pred[]{:T(512)S(6)} %ge.9, bf16[512,4096]{1,0:T(8,128)(2,1)} %copy-done.18, s32[]{:T(128)S(6)} %select_n.94), kind=kLoop, calls=%fused_computation.26 | loop fusion | flops 3670016 | bytes 5242885 | tf_op jit(solution)/shard_map/jit(_where)/select_n | solution.py:282
  84.3 4.5 %collective-permute-start.16 = (bf16[512,1024]{1,0:T(8,128)(2,1)}, bf16[512,1024]{1,0:T(8,128)(2,1)S(1)}, u32[]{:S(2)}, u32[]{:S(2)}) collective-permute-start(bf16[512,1024]{1,0:T(8,128)(2,1)} %get-tuple-element.18), channel_id=1, source_target_pairs={{0,2},{2,4},{3,1},{4,6},{5,3},{7,5},{8,10},{10,12},{11,9},{12,14},... | collective-permute-start | bytes 3145736 | tf_op jit(solution)/shard_map/ppermute | solution.py:229
  88.8 3.2 %fusion.12 = (bf16[4096,128]{1,0:T(8,128)(2,1)}, bf16[4096,128]{1,0:T(8,128)(2,1)}) fusion(f32[4096]{0:T(1024)S(1)} %bitcast.64, bf16[1,8192,128]{2,1,0:T(8,128)(2,1)S(1)} %copy-done.21, f32[4096]{0:T(1024)S(1)} %bitcast.65), kind=kLoop, calls=%fused_computation.17 | loop fusion | flops 3145728 | bytes 4227072 | tf_op jit(solution)/shard_map/convert_element_type | solution.py:312
  92.0 1.5 collective-permute-start.41
  93.5 1.5 collective-permute-start.39
  95.0 6.4 %collective-permute-done.16.refs_2_ = bf16[512,1024]{1,0:T(8,128)(2,1)S(1)} collective-permute-done((bf16[512,1024]{1,0:T(8,128)(2,1)}, bf16[512,1024]{1,0:T(8,128)(2,1)S(1)}, u32[]{:S(2)}, u32[]{:S(2)}) %collective-permute-start.16) | collective-permute-done | bytes 1048608 | tf_op jit(solution)/shard_map/ppermute | solution.py:229
  101.3 2.9 %fusion.14 = bf16[512,1024]{1,0:T(8,128)(2,1)} fusion(bf16[512,1024]{1,0:T(8,128)(2,1)S(1)} %collective-permute-done.16.refs_2_, bf16[512,1024]{1,0:T(8,128)(2,1)} %collective-permute-done.17, bf16[512,1024]{1,0:T(8,128)(2,1)S(1)} %get-tuple-element.20, pred[]{:T(512)S(6)} %ge.10), kind=kLoop, calls=%fused_computation.27 | loop fusion | flops 3670016 | bytes 4194305 | tf_op jit(solution)/shard_map/jit(_where)/select_n | solution.py:282
  104.2 4.8 %collective-permute-start.18 = (bf16[512,1024]{1,0:T(8,128)(2,1)}, bf16[512,1024]{1,0:T(8,128)(2,1)S(1)}, u32[]{:S(2)}, u32[]{:S(2)}) collective-permute-start(bf16[512,1024]{1,0:T(8,128)(2,1)} %fusion.14), channel_id=1, source_target_pairs={{0,2},{2,4},{3,1},{4,6},{5,3},{7,5},{8,10},{10,12},{11,9},{12,14},... | collective-permute-start | bytes 3145736 | tf_op jit(solution)/shard_map/ppermute | solution.py:229
  109.1 5.4 %collective-permute-done.41 = bf16[4096,128]{1,0:T(8,128)(2,1)} collective-permute-done((bf16[4096,128]{1,0:T(8,128)(2,1)}, bf16[4096,128]{1,0:T(8,128)(2,1)}, u32[]{:S(2)}, u32[]{:S(2)}) %collective-permute-start.41) | collective-permute-done | bytes 1048608 | tf_op jit(solution)/shard_map/ppermute | solution.py:314
  114.5 2.8 %add_convert_fusion = bf16[4096,128]{1,0:T(8,128)(2,1)} fusion(bf16[4096,128]{1,0:T(8,128)(2,1)} %collective-permute-done.41, bf16[4096,128]{1,0:T(8,128)(2,1)} %get-tuple-element.23), kind=kLoop, calls=%fused_computation.19 | loop fusion | flops 2097152 | bytes 3145728 | tf_op jit(solution)/shard_map/convert_element_type | solution.py:312
  117.3 1.6 collective-permute-start.42
  119.5 1.9 collective-permute-done.18.refs_3_
  121.3 2.8 %add_convert_fusion.1 = bf16[4096,128]{1,0:T(8,128)(2,1)} fusion(bf16[4096,128]{1,0:T(8,128)(2,1)} %collective-permute-done.39, bf16[4096,128]{1,0:T(8,128)(2,1)} %get-tuple-element.22), kind=kLoop, calls=%fused_computation.21 | loop fusion | flops 2097152 | bytes 3145728 | tf_op jit(solution)/shard_map/convert_element_type | solution.py:312
  124.1 1.6 collective-permute-start.40
  125.7 1.6 fusion.15.refs_8_
  127.4 4.4 %collective-permute-start.30 = (bf16[512,1024]{1,0:T(8,128)(2,1)}, bf16[512,1024]{1,0:T(8,128)(2,1)S(1)}, u32[]{:S(2)}, u32[]{:S(2)}) collective-permute-start(bf16[512,1024]{1,0:T(8,128)(2,1)} %fusion.15.refs_8_), channel_id=1, source_target_pairs={{0,2},{2,4},{3,1},{4,6},{5,3},{7,5},{8,10},{10,12},{11,9},{12,14},... | collective-permute-start | bytes 3145736 | tf_op jit(solution)/shard_map/ppermute | solution.py:229
  133.1 2.0 copy-done.14
  135.1 10.9 %convolution_convert_fusion.1 = bf16[256,4096]{1,0:T(8,128)(2,1)S(1)} fusion(bf16[1024,4096]{1,0:T(8,128)(2,1)} %copy-done, bf16[1,1024,4096]{2,1,0:T(8,128)(2,1)} %param.13, bf16[512,4096]{1,0:T(8,128)(2,1)} %copy-done.14), kind=kOutput, calls=%fused_computation.8 | convolution fusion | flops 4296278016 | bytes 20971520 | tf_op jit(solution)/shard_map/dot_general | solution.py:233
  146.2 7.1 %fusion.26.refs_0_ = bf16[1024,256]{1,0:T(8,128)(2,1)S(1)} fusion(bf16[1,1024,4096]{2,1,0:T(8,128)(2,1)} %param.13, bf16[512,4096]{1,0:T(8,128)(2,1)} %copy-done.14), kind=kOutput, calls=%fused_computation.32 | convolution fusion | flops 2147745792 | bytes 11010048 | tf_op jit(solution)/shard_map/dot_general | solution.py:291
  153.9 1.6 slice-done.1
  155.5 2.5 %convolution_convert_fusion = bf16[256,4096]{1,0:T(8,128)(2,1)S(1)} fusion(bf16[1024,256]{1,0:T(8,128)(2,1)S(1)} %fence.5, bf16[1024,4096]{1,0:T(8,128)(2,1)S(1)} %bitcast.55), kind=kOutput, calls=%fused_computation.7 | convolution fusion | flops 2148532224 | bytes 11010048 | tf_op jit(solution)/shard_map/dot_general | solution.py:233
  158.2 1.7 convert_add_fusion
  160.8 4.2 %collective-permute-start.26 = (bf16[256,1024]{1,0:T(8,128)(2,1)S(1)}, bf16[256,1024]{1,0:T(8,128)(2,1)S(1)}, u32[]{:S(2)}, u32[]{:S(2)}) collective-permute-start(bf16[256,1024]{1,0:T(8,128)(2,1)S(1)} %get-tuple-element.14), channel_id=1, source_target_pairs={{0,2},{7,5},{8,10},{15,13},{16,18},{23,21},{24,26},{31,29}} | collective-permute-start | bytes 1572872 | tf_op jit(solution)/shard_map/ppermute | solution.py:229
  165.3 1.5 collective-permute-start.34
  166.8 1.9 convert_add_fusion.1
  169.3 2.4 %collective-permute-done.26 = bf16[256,1024]{1,0:T(8,128)(2,1)S(1)} collective-permute-done((bf16[256,1024]{1,0:T(8,128)(2,1)S(1)}, bf16[256,1024]{1,0:T(8,128)(2,1)S(1)}, u32[]{:S(2)}, u32[]{:S(2)}) %collective-permute-start.26) | collective-permute-done | bytes 524320 | tf_op jit(solution)/shard_map/ppermute | solution.py:229
  172.0 4.4 %collective-permute-start.27 = (bf16[256,1024]{1,0:T(8,128)(2,1)S(1)}, bf16[256,1024]{1,0:T(8,128)(2,1)S(1)}, u32[]{:S(2)}, u32[]{:S(2)}) collective-permute-start(bf16[256,1024]{1,0:T(8,128)(2,1)S(1)} %add_convert_fusion.9), channel_id=1, source_target_pairs={{0,2},{2,4},{5,3},{7,5},{8,10},{10,12},{13,11},{15,13},{16,18},{18... | collective-permute-start | bytes 1572872 | tf_op jit(solution)/shard_map/ppermute | solution.py:229
  177.6 4.4 %collective-permute-start.35 = (bf16[256,1024]{1,0:T(8,128)(2,1)S(1)}, bf16[256,1024]{1,0:T(8,128)(2,1)S(1)}, u32[]{:S(2)}, u32[]{:S(2)}) collective-permute-start(bf16[256,1024]{1,0:T(8,128)(2,1)S(1)} %add_convert_fusion.6), channel_id=1, source_target_pairs={{0,2},{2,4},{5,3},{7,5},{8,10},{10,12},{13,11},{15,13},{16,18},{18... | collective-permute-start | bytes 1572872 | tf_op jit(solution)/shard_map/ppermute | solution.py:229
  182.0 3.9 %subtract_convert_fusion = (bf16[8192,128]{1,0:T(8,128)(2,1)}, f32[8192,128]{1,0:T(8,128)}) fusion(bf16[8192,128]{1,0:T(8,128)(2,1)S(1)} %copy-done.22, f32[4096,128]{1,0:T(8,128)S(1)} %convert_add_fusion, f32[4096,128]{1,0:T(8,128)S(1)} %convert_add_fusion.1, f32[8192,128]{1,0:T(8,128)S(1)} %copy-done.19), kind=kLoop, calls=%fused_computation.10 | loop fusion | flops 10485760 | bytes 16777216 | tf_op jit(solution)/shard_map/convert_element_type | solution.py:194
  186.2 1.9 collective-permute-start.28
  188.9 4.4 %collective-permute-start.36 = (bf16[256,1024]{1,0:T(8,128)(2,1)S(1)}, bf16[256,1024]{1,0:T(8,128)(2,1)S(1)}, u32[]{:S(2)}, u32[]{:S(2)}) collective-permute-start(bf16[256,1024]{1,0:T(8,128)(2,1)S(1)} %add_convert_fusion.5), channel_id=1, source_target_pairs={{0,2},{2,4},{3,1},{4,6},{5,3},{7,5},{8,10},{10,12},{11,9},{12,14},... | collective-permute-start | bytes 1572872 | tf_op jit(solution)/shard_map/ppermute | solution.py:229
  193.4 1.6 convert_add_fusion.2
  197.6 2.8 %collective-permute-done.36 = bf16[256,1024]{1,0:T(8,128)(2,1)S(1)} collective-permute-done((bf16[256,1024]{1,0:T(8,128)(2,1)S(1)}, bf16[256,1024]{1,0:T(8,128)(2,1)S(1)}, u32[]{:S(2)}, u32[]{:S(2)}) %collective-permute-start.36) | collective-permute-done | bytes 524320 | tf_op jit(solution)/shard_map/ppermute | solution.py:229
  (149 shorter events, 33.7 us)
Async XLA Ops:
  1.9 2.1 collective-permute-start
  2.4 2.5 %collective-permute-start.1 = (bf16[512,512]{1,0:T(8,128)(2,1)}, bf16[512,512]{1,0:T(8,128)(2,1)S(1)}, u32[]{:S(2)}, u32[]{:S(2)}) collective-permute-start(bf16[512,512]{1,0:T(8,128)(2,1)} %bitcast.61), channel_id=1, source_target_pairs={{0,1},{1,0},{2,3},{3,2},{4,5},{5,4},{6,7},{7,6},{8,9},{9,8},{10,11... | collective-permute-start | bytes 1572872 | tf_op jit(solution)/shard_map/ppermute | solution.py:226
  6.7 13.9 %collective-permute-start.2 = (bf16[1024,256]{1,0:T(8,128)(2,1)S(1)}, bf16[1024,256]{1,0:T(8,128)(2,1)S(1)}, u32[]{:S(2)}, u32[]{:S(2)}) collective-permute-start(bf16[1024,256]{1,0:T(8,128)(2,1)S(1)} %get-tuple-element.6.refs_2_.refs_0_), channel_id=1, source_target_pairs={{0,2},{2,4},{3,1},{4,6},{5,3},{7,5},{8,10},{10,12},{11,9},{12,14},... | collective-permute-start | bytes 1572872 | tf_op jit(solution)/shard_map/ppermute | solution.py:229
  11.6 13.0 %collective-permute-start.3 = (bf16[1024,256]{1,0:T(8,128)(2,1)S(1)}, bf16[1024,256]{1,0:T(8,128)(2,1)S(1)}, u32[]{:S(2)}, u32[]{:S(2)}) collective-permute-start(bf16[1024,256]{1,0:T(8,128)(2,1)S(1)} %get-tuple-element.7.refs_1_), channel_id=1, source_target_pairs={{0,2},{2,4},{3,1},{4,6},{5,3},{7,5},{8,10},{10,12},{11,9},{12,14},... | collective-permute-start | bytes 1572872 | tf_op jit(solution)/shard_map/ppermute | solution.py:229
  23.9 3.0 %collective-permute-start.4 = (bf16[1024,256]{1,0:T(8,128)(2,1)S(1)}, bf16[1024,256]{1,0:T(8,128)(2,1)S(1)}, u32[]{:S(2)}, u32[]{:S(2)}) collective-permute-start(bf16[1024,256]{1,0:T(8,128)(2,1)S(1)} %fence.3.refs_2_.refs_14_), channel_id=1, source_target_pairs={{2,4},{3,1},{4,6},{5,3},{10,12},{11,9},{12,14},{13,11},{18,20},{19... | collective-permute-start | bytes 1572872 | tf_op jit(solution)/shard_map/ppermute | solution.py:229
  24.6 3.7 %collective-permute-start.5 = (bf16[1024,256]{1,0:T(8,128)(2,1)S(1)}, bf16[1024,256]{1,0:T(8,128)(2,1)}, u32[]{:S(2)}, u32[]{:S(2)}) collective-permute-start(bf16[1024,256]{1,0:T(8,128)(2,1)S(1)} %collective-permute-done.3.refs_3_), channel_id=1, source_target_pairs={{2,4},{3,1},{4,6},{5,3},{10,12},{11,9},{12,14},{13,11},{18,20},{19... | collective-permute-start | bytes 1572872 | tf_op jit(solution)/shard_map/ppermute | solution.py:229
  26.1 11.7 %collective-permute-start.8 = (bf16[1024,256]{1,0:T(8,128)(2,1)S(1)}, bf16[1024,256]{1,0:T(8,128)(2,1)S(1)}, u32[]{:S(2)}, u32[]{:S(2)}) collective-permute-start(bf16[1024,256]{1,0:T(8,128)(2,1)S(1)} %fence.3.refs_2_.refs_14_), channel_id=1, source_target_pairs={{0,1},{1,0},{2,3},{3,2},{4,5},{5,4},{6,7},{7,6},{8,9},{9,8},{10,11... | collective-permute-start | bytes 1572872 | tf_op jit(solution)/shard_map/ppermute | solution.py:226
  26.9 12.1 %collective-permute-start.6 = (bf16[1024,256]{1,0:T(8,128)(2,1)S(1)}, bf16[1024,256]{1,0:T(8,128)(2,1)}, u32[]{:S(2)}, u32[]{:S(2)}) collective-permute-start(bf16[1024,256]{1,0:T(8,128)(2,1)S(1)} %collective-permute-done.4.refs_4_), channel_id=1, source_target_pairs={{3,1},{4,6},{11,9},{12,14},{19,17},{20,22},{27,25},{28,30}} | collective-permute-start | bytes 1572872 | tf_op jit(solution)/shard_map/ppermute | solution.py:229
  28.3 13.6 %collective-permute-start.7 = (bf16[1024,256]{1,0:T(8,128)(2,1)}, bf16[1024,256]{1,0:T(8,128)(2,1)}, u32[]{:S(2)}, u32[]{:S(2)}) collective-permute-start(bf16[1024,256]{1,0:T(8,128)(2,1)} %collective-permute-done.5.refs_5_), channel_id=1, source_target_pairs={{3,1},{4,6},{11,9},{12,14},{19,17},{20,22},{27,25},{28,30}} | collective-permute-start | bytes 1572872 | tf_op jit(solution)/shard_map/ppermute | solution.py:229
  29.8 19.7 %collective-permute-start.9 = (bf16[1024,256]{1,0:T(8,128)(2,1)S(1)}, bf16[1024,256]{1,0:T(8,128)(2,1)}, u32[]{:S(2)}, u32[]{:S(2)}) collective-permute-start(bf16[1024,256]{1,0:T(8,128)(2,1)S(1)} %collective-permute-done.3.refs_3_), channel_id=1, source_target_pairs={{0,1},{1,0},{2,3},{3,2},{4,5},{5,4},{6,7},{7,6},{8,9},{9,8},{10,11... | collective-permute-start | bytes 1572872 | tf_op jit(solution)/shard_map/ppermute | solution.py:226
  37.6 11.9 %collective-permute-start.10 = (bf16[1024,256]{1,0:T(8,128)(2,1)S(1)}, bf16[1024,256]{1,0:T(8,128)(2,1)}, u32[]{:S(2)}, u32[]{:S(2)}) collective-permute-start(bf16[1024,256]{1,0:T(8,128)(2,1)S(1)} %collective-permute-done.4.refs_4_), channel_id=1, source_target_pairs={{0,1},{1,0},{2,3},{3,2},{4,5},{5,4},{6,7},{7,6},{8,9},{9,8},{10,11... | collective-permute-start | bytes 1572872 | tf_op jit(solution)/shard_map/ppermute | solution.py:226
  38.5 11.0 %collective-permute-start.11 = (bf16[1024,256]{1,0:T(8,128)(2,1)}, bf16[1024,256]{1,0:T(8,128)(2,1)}, u32[]{:S(2)}, u32[]{:S(2)}) collective-permute-start(bf16[1024,256]{1,0:T(8,128)(2,1)} %collective-permute-done.5.refs_5_), channel_id=1, source_target_pairs={{0,1},{1,0},{2,3},{3,2},{4,5},{5,4},{6,7},{7,6},{8,9},{9,8},{10,11... | collective-permute-start | bytes 1572872 | tf_op jit(solution)/shard_map/ppermute | solution.py:226
  39.0 10.6 %collective-permute-start.12 = (bf16[1024,256]{1,0:T(8,128)(2,1)}, bf16[1024,256]{1,0:T(8,128)(2,1)}, u32[]{:S(2)}, u32[]{:S(2)}) collective-permute-start(bf16[1024,256]{1,0:T(8,128)(2,1)} %collective-permute-done.6.refs_6_.refs_3_), channel_id=1, source_target_pairs={{0,1},{1,0},{2,3},{3,2},{4,5},{5,4},{6,7},{7,6},{8,9},{9,8},{10,11... | collective-permute-start | bytes 1572872 | tf_op jit(solution)/shard_map/ppermute | solution.py:226
  41.9 7.6 %collective-permute-start.13 = (bf16[1024,256]{1,0:T(8,128)(2,1)}, bf16[1024,256]{1,0:T(8,128)(2,1)}, u32[]{:S(2)}, u32[]{:S(2)}) collective-permute-start(bf16[1024,256]{1,0:T(8,128)(2,1)} %collective-permute-done.7.refs_7_), channel_id=1, source_target_pairs={{0,1},{1,0},{2,3},{3,2},{4,5},{5,4},{6,7},{7,6},{8,9},{9,8},{10,11... | collective-permute-start | bytes 1572872 | tf_op jit(solution)/shard_map/ppermute | solution.py:226
  54.8 14.2 %copy-start.4 = (bf16[512,1024]{1,0:T(8,128)(2,1)}, bf16[512,1024]{1,0:T(8,128)(2,1)S(1)}, u32[]{:S(2)}) copy-start(bf16[512,1024]{1,0:T(8,128)(2,1)S(1)} %join_cores_across.1.refs_1_.refs_0_) | copy-start | bytes 3145732
  54.8 14.2 %collective-permute-start.14 = (bf16[512,1024]{1,0:T(8,128)(2,1)S(1)}, bf16[512,1024]{1,0:T(8,128)(2,1)S(1)}, u32[]{:S(2)}, u32[]{:S(2)}) collective-permute-start(bf16[512,1024]{1,0:T(8,128)(2,1)S(1)} %join_cores_across.1.refs_1_.refs_0_), channel_id=1, source_target_pairs={{0,2},{2,4},{3,1},{4,6},{5,3},{7,5},{8,10},{10,12},{11,9},{12,14},... | collective-permute-start | bytes 3145736 | tf_op jit(solution)/shard_map/ppermute | solution.py:229
  69.0 49.9 %copy-start.2 = (bf16[512,1024]{1,0:T(8,128)(2,1)}, bf16[512,1024]{1,0:T(8,128)(2,1)S(1)}, u32[]{:S(2)}) copy-start(bf16[512,1024]{1,0:T(8,128)(2,1)S(1)} %collective-permute-done.14.refs_2_.refs_1_) | copy-start | bytes 3145732
  76.7 4.0 %collective-permute-start.15 = (bf16[512,1024]{1,0:T(8,128)(2,1)S(1)}, bf16[512,1024]{1,0:T(8,128)(2,1)}, u32[]{:S(2)}, u32[]{:S(2)}) collective-permute-start(bf16[512,1024]{1,0:T(8,128)(2,1)S(1)} %get-tuple-element.21), channel_id=1, source_target_pairs={{0,1},{1,0},{2,3},{3,2},{4,5},{5,4},{6,7},{7,6},{8,9},{9,8},{10,11... | collective-permute-start | bytes 3145736 | tf_op jit(solution)/shard_map/ppermute | solution.py:226
  79.1 15.9 %collective-permute-start.17 = (bf16[512,1024]{1,0:T(8,128)(2,1)S(1)}, bf16[512,1024]{1,0:T(8,128)(2,1)}, u32[]{:S(2)}, u32[]{:S(2)}) collective-permute-start(bf16[512,1024]{1,0:T(8,128)(2,1)S(1)} %get-tuple-element.20), channel_id=1, source_target_pairs={{0,1},{1,0},{2,3},{3,2},{4,5},{5,4},{6,7},{7,6},{8,9},{9,8},{10,11... | collective-permute-start | bytes 3145736 | tf_op jit(solution)/shard_map/ppermute | solution.py:226
  84.3 17.0 %collective-permute-start.16 = (bf16[512,1024]{1,0:T(8,128)(2,1)}, bf16[512,1024]{1,0:T(8,128)(2,1)S(1)}, u32[]{:S(2)}, u32[]{:S(2)}) collective-permute-start(bf16[512,1024]{1,0:T(8,128)(2,1)} %get-tuple-element.18), channel_id=1, source_target_pairs={{0,2},{2,4},{3,1},{4,6},{5,3},{7,5},{8,10},{10,12},{11,9},{12,14},... | collective-permute-start | bytes 3145736 | tf_op jit(solution)/shard_map/ppermute | solution.py:229
  92.0 22.6 %collective-permute-start.41 = (bf16[4096,128]{1,0:T(8,128)(2,1)}, bf16[4096,128]{1,0:T(8,128)(2,1)}, u32[]{:S(2)}, u32[]{:S(2)}) collective-permute-start(bf16[4096,128]{1,0:T(8,128)(2,1)} %get-tuple-element.23), channel_id=1, source_target_pairs={{0,16},{8,24},{16,0},{24,8},{1,17},{9,25},{17,1},{25,9},{2,18},{10... | collective-permute-start | bytes 3145736 | tf_op jit(solution)/shard_map/ppermute | solution.py:314
  93.5 25.5 %collective-permute-start.39 = (bf16[4096,128]{1,0:T(8,128)(2,1)}, bf16[4096,128]{1,0:T(8,128)(2,1)}, u32[]{:S(2)}, u32[]{:S(2)}) collective-permute-start(bf16[4096,128]{1,0:T(8,128)(2,1)} %get-tuple-element.22), channel_id=1, source_target_pairs={{0,8},{8,0},{16,24},{24,16},{1,9},{9,1},{17,25},{25,17},{2,10},{10... | collective-permute-start | bytes 3145736 | tf_op jit(solution)/shard_map/ppermute | solution.py:314
  104.2 17.1 %collective-permute-start.18 = (bf16[512,1024]{1,0:T(8,128)(2,1)}, bf16[512,1024]{1,0:T(8,128)(2,1)S(1)}, u32[]{:S(2)}, u32[]{:S(2)}) collective-permute-start(bf16[512,1024]{1,0:T(8,128)(2,1)} %fusion.14), channel_id=1, source_target_pairs={{0,2},{2,4},{3,1},{4,6},{5,3},{7,5},{8,10},{10,12},{11,9},{12,14},... | collective-permute-start | bytes 3145736 | tf_op jit(solution)/shard_map/ppermute | solution.py:229
  109.0 15.1 %collective-permute-start.22 = (bf16[512,1024]{1,0:T(8,128)(2,1)}, bf16[512,1024]{1,0:T(8,128)(2,1)S(1)}, u32[]{:S(2)}, u32[]{:S(2)}) collective-permute-start(bf16[512,1024]{1,0:T(8,128)(2,1)} %get-tuple-element.19), channel_id=1, source_target_pairs={{0,1},{1,0},{2,3},{3,2},{4,5},{5,4},{6,7},{7,6},{8,9},{9,8},{10,11... | collective-permute-start | bytes 3145736 | tf_op jit(solution)/shard_map/ppermute | solution.py:226
  117.3 40.9 %collective-permute-start.42 = (bf16[4096,128]{1,0:T(8,128)(2,1)}, bf16[4096,128]{1,0:T(8,128)(2,1)}, u32[]{:S(2)}, u32[]{:S(2)}) collective-permute-start(bf16[4096,128]{1,0:T(8,128)(2,1)} %add_convert_fusion), channel_id=1, source_target_pairs={{0,8},{8,0},{16,24},{24,16},{1,9},{9,1},{17,25},{25,17},{2,10},{10... | collective-permute-start | bytes 3145736 | tf_op jit(solution)/shard_map/ppermute | solution.py:314
  118.9 8.4 %collective-permute-start.19 = (bf16[512,1024]{1,0:T(8,128)(2,1)S(1)}, bf16[512,1024]{1,0:T(8,128)(2,1)S(1)}, u32[]{:S(2)}, u32[]{:S(2)}) collective-permute-start(bf16[512,1024]{1,0:T(8,128)(2,1)S(1)} %collective-permute-done.14.refs_2_.refs_1_), channel_id=1, source_target_pairs={{0,1},{1,0},{2,3},{3,2},{4,5},{5,4},{6,7},{7,6},{8,9},{9,8},{10,11... | collective-permute-start | bytes 3145736 | tf_op jit(solution)/shard_map/ppermute | solution.py:226
  119.0 12.9 %collective-permute-start.20 = (bf16[512,1024]{1,0:T(8,128)(2,1)S(1)}, bf16[512,1024]{1,0:T(8,128)(2,1)S(1)}, u32[]{:S(2)}, u32[]{:S(2)}) collective-permute-start(bf16[512,1024]{1,0:T(8,128)(2,1)S(1)} %collective-permute-done.16.refs_2_), channel_id=1, source_target_pairs={{0,1},{1,0},{2,3},{3,2},{4,5},{5,4},{6,7},{7,6},{8,9},{9,8},{10,11... | collective-permute-start | bytes 3145736 | tf_op jit(solution)/shard_map/ppermute | solution.py:226
  121.3 10.5 %collective-permute-start.21 = (bf16[512,1024]{1,0:T(8,128)(2,1)S(1)}, bf16[512,1024]{1,0:T(8,128)(2,1)S(1)}, u32[]{:S(2)}, u32[]{:S(2)}) collective-permute-start(bf16[512,1024]{1,0:T(8,128)(2,1)S(1)} %collective-permute-done.18.refs_3_), channel_id=1, source_target_pairs={{0,1},{1,0},{2,3},{3,2},{4,5},{5,4},{6,7},{7,6},{8,9},{9,8},{10,11... | collective-permute-start | bytes 3145736 | tf_op jit(solution)/shard_map/ppermute | solution.py:226
  124.1 42.6 %collective-permute-start.40 = (bf16[4096,128]{1,0:T(8,128)(2,1)}, bf16[4096,128]{1,0:T(8,128)(2,1)}, u32[]{:S(2)}, u32[]{:S(2)}) collective-permute-start(bf16[4096,128]{1,0:T(8,128)(2,1)} %add_convert_fusion.1), channel_id=1, source_target_pairs={{0,16},{8,24},{16,0},{24,8},{1,17},{9,25},{17,1},{25,9},{2,18},{10... | collective-permute-start | bytes 3145736 | tf_op jit(solution)/shard_map/ppermute | solution.py:314
  127.4 25.9 %collective-permute-start.30 = (bf16[512,1024]{1,0:T(8,128)(2,1)}, bf16[512,1024]{1,0:T(8,128)(2,1)S(1)}, u32[]{:S(2)}, u32[]{:S(2)}) collective-permute-start(bf16[512,1024]{1,0:T(8,128)(2,1)} %fusion.15.refs_8_), channel_id=1, source_target_pairs={{0,2},{2,4},{3,1},{4,6},{5,3},{7,5},{8,10},{10,12},{11,9},{12,14},... | collective-permute-start | bytes 3145736 | tf_op jit(solution)/shard_map/ppermute | solution.py:229
  146.0 14.6 %copy-start.20 = (bf16[256,4096]{1,0:T(8,128)(2,1)}, bf16[256,4096]{1,0:T(8,128)(2,1)S(1)}, u32[]{:S(2)}) copy-start(bf16[256,4096]{1,0:T(8,128)(2,1)S(1)} %convolution_convert_fusion.1) | copy-start | bytes 6291460
  146.1 14.5 %collective-permute-start.25 = (bf16[256,1024]{1,0:T(8,128)(2,1)S(1)}, bf16[256,1024]{1,0:T(8,128)(2,1)S(1)}, u32[]{:S(2)}, u32[]{:S(2)}) collective-permute-start(bf16[256,1024]{1,0:T(8,128)(2,1)S(1)} %get-tuple-element.25), channel_id=1, source_target_pairs={{0,1},{1,0},{2,3},{3,2},{4,5},{5,4},{6,7},{7,6},{8,9},{9,8},{10,11... | collective-permute-start | bytes 1572872 | tf_op jit(solution)/shard_map/ppermute | solution.py:226
  158.1 6.9 %collective-permute-start.33 = (bf16[256,1024]{1,0:T(8,128)(2,1)S(1)}, bf16[256,1024]{1,0:T(8,128)(2,1)S(1)}, u32[]{:S(2)}, u32[]{:S(2)}) collective-permute-start(bf16[256,1024]{1,0:T(8,128)(2,1)S(1)} %get-tuple-element.27), channel_id=1, source_target_pairs={{0,1},{1,0},{2,3},{3,2},{4,5},{5,4},{6,7},{7,6},{8,9},{9,8},{10,11... | collective-permute-start | bytes 1572872 | tf_op jit(solution)/shard_map/ppermute | solution.py:226
  159.9 8.9 %collective-permute-start.24 = (bf16[256,1024]{1,0:T(8,128)(2,1)S(1)}, bf16[256,1024]{1,0:T(8,128)(2,1)S(1)}, u32[]{:S(2)}, u32[]{:S(2)}) collective-permute-start(bf16[256,1024]{1,0:T(8,128)(2,1)S(1)} %get-tuple-element.24), channel_id=1, source_target_pairs={{0,1},{1,0},{2,3},{3,2},{4,5},{5,4},{6,7},{7,6},{8,9},{9,8},{10,11... | collective-permute-start | bytes 1572872 | tf_op jit(solution)/shard_map/ppermute | solution.py:226
  160.5 15.9 %collective-permute-start.32 = (bf16[256,1024]{1,0:T(8,128)(2,1)S(1)}, bf16[256,1024]{1,0:T(8,128)(2,1)S(1)}, u32[]{:S(2)}, u32[]{:S(2)}) collective-permute-start(bf16[256,1024]{1,0:T(8,128)(2,1)S(1)} %get-tuple-element.26), channel_id=1, source_target_pairs={{0,1},{1,0},{2,3},{3,2},{4,5},{5,4},{6,7},{7,6},{8,9},{9,8},{10,11... | collective-permute-start | bytes 1572872 | tf_op jit(solution)/shard_map/ppermute | solution.py:226
  160.8 10.9 %collective-permute-start.26 = (bf16[256,1024]{1,0:T(8,128)(2,1)S(1)}, bf16[256,1024]{1,0:T(8,128)(2,1)S(1)}, u32[]{:S(2)}, u32[]{:S(2)}) collective-permute-start(bf16[256,1024]{1,0:T(8,128)(2,1)S(1)} %get-tuple-element.14), channel_id=1, source_target_pairs={{0,2},{7,5},{8,10},{15,13},{16,18},{23,21},{24,26},{31,29}} | collective-permute-start | bytes 1572872 | tf_op jit(solution)/shard_map/ppermute | solution.py:229
  165.3 12.0 %collective-permute-start.34 = (bf16[256,1024]{1,0:T(8,128)(2,1)S(1)}, bf16[256,1024]{1,0:T(8,128)(2,1)S(1)}, u32[]{:S(2)}, u32[]{:S(2)}) collective-permute-start(bf16[256,1024]{1,0:T(8,128)(2,1)S(1)} %get-tuple-element.16), channel_id=1, source_target_pairs={{0,2},{7,5},{8,10},{15,13},{16,18},{23,21},{24,26},{31,29}} | collective-permute-start | bytes 1572872 | tf_op jit(solution)/shard_map/ppermute | solution.py:229
  166.8 15.2 %copy-start.22 = (bf16[8192,128]{1,0:T(8,128)(2,1)S(1)}, bf16[8192,128]{1,0:T(8,128)(2,1)}, u32[]{:S(2)}) copy-start(bf16[8192,128]{1,0:T(8,128)(2,1)} %param.14) | copy-start | bytes 6291460
  168.7 17.2 %collective-permute-start.23 = (bf16[256,1024]{1,0:T(8,128)(2,1)S(1)}, bf16[256,1024]{1,0:T(8,128)(2,1)S(1)}, u32[]{:S(2)}, u32[]{:S(2)}) collective-permute-start(bf16[256,1024]{1,0:T(8,128)(2,1)S(1)} %get-tuple-element.15), channel_id=1, source_target_pairs={{0,1},{1,0},{2,3},{3,2},{4,5},{5,4},{6,7},{7,6},{8,9},{9,8},{10,11... | collective-permute-start | bytes 1572872 | tf_op jit(solution)/shard_map/ppermute | solution.py:226
  168.8 13.2 %copy-start.19 = (f32[8192,128]{1,0:T(8,128)S(1)}, f32[8192,128]{1,0:T(8,128)}, u32[]{:S(2)}) copy-start(f32[8192,128]{1,0:T(8,128)} %param.15) | copy-start | bytes 12582916
  168.8 19.3 %collective-permute-start.31 = (bf16[256,1024]{1,0:T(8,128)(2,1)S(1)}, bf16[256,1024]{1,0:T(8,128)(2,1)S(1)}, u32[]{:S(2)}, u32[]{:S(2)}) collective-permute-start(bf16[256,1024]{1,0:T(8,128)(2,1)S(1)} %get-tuple-element.17), channel_id=1, source_target_pairs={{0,1},{1,0},{2,3},{3,2},{4,5},{5,4},{6,7},{7,6},{8,9},{9,8},{10,11... | collective-permute-start | bytes 1572872 | tf_op jit(solution)/shard_map/ppermute | solution.py:226
  172.0 14.0 %collective-permute-start.27 = (bf16[256,1024]{1,0:T(8,128)(2,1)S(1)}, bf16[256,1024]{1,0:T(8,128)(2,1)S(1)}, u32[]{:S(2)}, u32[]{:S(2)}) collective-permute-start(bf16[256,1024]{1,0:T(8,128)(2,1)S(1)} %add_convert_fusion.9), channel_id=1, source_target_pairs={{0,2},{2,4},{5,3},{7,5},{8,10},{10,12},{13,11},{15,13},{16,18},{18... | collective-permute-start | bytes 1572872 | tf_op jit(solution)/shard_map/ppermute | solution.py:229
  177.6 11.1 %collective-permute-start.35 = (bf16[256,1024]{1,0:T(8,128)(2,1)S(1)}, bf16[256,1024]{1,0:T(8,128)(2,1)S(1)}, u32[]{:S(2)}, u32[]{:S(2)}) collective-permute-start(bf16[256,1024]{1,0:T(8,128)(2,1)S(1)} %add_convert_fusion.6), channel_id=1, source_target_pairs={{0,2},{2,4},{5,3},{7,5},{8,10},{10,12},{13,11},{15,13},{16,18},{18... | collective-permute-start | bytes 1572872 | tf_op jit(solution)/shard_map/ppermute | solution.py:229
  186.2 8.9 %collective-permute-start.28 = (bf16[256,1024]{1,0:T(8,128)(2,1)S(1)}, bf16[256,1024]{1,0:T(8,128)(2,1)S(1)}, u32[]{:S(2)}, u32[]{:S(2)}) collective-permute-start(bf16[256,1024]{1,0:T(8,128)(2,1)S(1)} %add_convert_fusion.8), channel_id=1, source_target_pairs={{0,2},{2,4},{3,1},{4,6},{5,3},{7,5},{8,10},{10,12},{11,9},{12,14},... | collective-permute-start | bytes 1572872 | tf_op jit(solution)/shard_map/ppermute | solution.py:229
  188.9 11.5 %collective-permute-start.36 = (bf16[256,1024]{1,0:T(8,128)(2,1)S(1)}, bf16[256,1024]{1,0:T(8,128)(2,1)S(1)}, u32[]{:S(2)}, u32[]{:S(2)}) collective-permute-start(bf16[256,1024]{1,0:T(8,128)(2,1)S(1)} %add_convert_fusion.5), channel_id=1, source_target_pairs={{0,2},{2,4},{3,1},{4,6},{5,3},{7,5},{8,10},{10,12},{11,9},{12,14},... | collective-permute-start | bytes 1572872 | tf_op jit(solution)/shard_map/ppermute | solution.py:229
  195.1 6.3 %collective-permute-start.38 = (bf16[512,512]{1,0:T(8,128)(2,1)S(1)}, bf16[512,512]{1,0:T(8,128)(2,1)S(1)}, u32[]{:S(2)}, u32[]{:S(2)}) collective-permute-start(bf16[512,512]{1,0:T(8,128)(2,1)S(1)} %dynamic-slice_convert_fusion), channel_id=1, source_target_pairs={{0,1},{1,0},{2,3},{3,2},{4,5},{5,4},{6,7},{7,6},{8,9},{9,8},{10,11... | collective-permute-start | bytes 1572872 | tf_op jit(solution)/shard_map/ppermute | solution.py:226
  197.1 5.7 %collective-permute-start.29 = (bf16[256,512]{1,0:T(8,128)(2,1)}, bf16[256,512]{1,0:T(8,128)(2,1)S(1)}, u32[]{:S(2)}, u32[]{:S(2)}) collective-permute-start(bf16[256,512]{1,0:T(8,128)(2,1)} %dynamic-slice_convert_fusion.2), channel_id=1, source_target_pairs={{0,1},{1,0},{2,3},{3,2},{4,5},{5,4},{6,7},{7,6},{8,9},{9,8},{10,11... | collective-permute-start | bytes 786440 | tf_op jit(solution)/shard_map/ppermute | solution.py:226
  201.3 1.9 collective-permute-start.37
  (25 other events, 144.8 us)

commit v4 on v3

--- a/solution.py
+++ b/solution.py
@@ -7,7 +7,7 @@
 
 HALVES = 2
 ROW_TILE = 128
-KERNEL_FLOPS = 20 * 10**9
+FLOPS_PER_US = 10**9
 ANY = pl.BlockSpec(memory_space=pl.ANY)
 
 
@@ -28,7 +28,7 @@
 
     def __call__(
         self, kernel, args, in_specs, out_shape, scratch, vmem, after=(), aliases=None, grid=1,
-        out_specs=None,
+        out_specs=None, us=1.0,
     ):
         after = self.last + tuple(after)
         count = len(args)
@@ -48,7 +48,7 @@
             out_shape=out_shape,
             input_output_aliases={1 + i: o for i, o in (aliases or {}).items()},
             compiler_params=pltpu.CompilerParams(vmem_limit_bytes=vmem * 1024 * 1024),
-            cost_estimate=pl.CostEstimate(flops=KERNEL_FLOPS, bytes_accessed=1, transcendentals=0),
+            cost_estimate=pl.CostEstimate(flops=int(us * FLOPS_PER_US), bytes_accessed=1, transcendentals=0),
             name=kernel.__qualname__.split(".")[0],
         )(self.place, *args, *after)
         self.last = (result[0],)
@@ -90,15 +90,16 @@
         after,
         grid=rows // ROW_TILE,
         out_specs=[tile],
+        us=20.0,
     )[0]
 
 
-def join_cores(order, own, partner, after=()):
+def join_cores(order, own, partner, parts, after=()):
     rows, features = own.shape
-    piece = features // HALVES
+    piece = features // parts
 
     def run(place_ref, own_ref, partner_ref, *refs):
-        out_refs, sems = refs[:HALVES], refs[HALVES]
+        out_refs, sems = refs[:parts], refs[parts]
         core = place_ref[place_ref.shape[0] - 1]
         pairs = []
         for j, out_ref in enumerate(out_refs):
@@ -113,60 +114,38 @@
         run,
         (own, partner),
         [ANY, ANY],
-        [jax.ShapeDtypeStruct((2 * rows, piece), jnp.bfloat16)] * HALVES,
-        [pltpu.SemaphoreType.DMA((2 * HALVES,))],
+        [jax.ShapeDtypeStruct((2 * rows, piece), jnp.bfloat16)] * parts,
+        [pltpu.SemaphoreType.DMA((2 * parts,))],
         4,
         after,
     )
 
 
-def join_cores_across(order, own, partner, after=()):
-    features, rows = own.shape
-
-    def run(place_ref, own_ref, partner_ref, out_ref, sems):
-        core = place_ref[place_ref.shape[0] - 1]
-        pairs = []
-        for source, where in ((own_ref, core), (partner_ref, 1 - core)):
-            cols = pl.ds(pl.multiple_of(where * rows, rows), rows)
-            pairs.append((source, out_ref.at[:, cols]))
-        for copy in copies(pairs, sems):
-            copy.wait()
-
-    return order(
-        run,
-        (own, partner),
-        [ANY, ANY],
-        [jax.ShapeDtypeStruct((features, 2 * rows), jnp.bfloat16)],
-        [pltpu.SemaphoreType.DMA((2,))],
-        4,
-        after,
-    )[0]
-
-
-def assemble(order, pieces, others, across, after=()):
-    chips, parts = len(pieces), len(pieces[0])
-    first, second = pieces[0][0].shape
-    shape = (first * parts, second * chips) if across else (first * chips, second * parts)
+def assemble(order, pieces, others, parts, after=()):
+    chips, held = len(pieces), len(pieces[0])
+    block, width = pieces[0][0].shape
+    features = held * width
+    count = max(parts, held)
+    piece = features // count
+    wide = features // parts
 
     def run(place_ref, *refs):
-        piece_refs = [refs[p * parts : (p + 1) * parts] for p in range(chips)]
-        rest = refs[chips * parts :]
-        other_refs = [rest[p * parts : (p + 1) * parts] for p in range(chips - 1)]
-        out_ref, sems = rest[(chips - 1) * parts :]
+        piece_refs = [refs[p * held : (p + 1) * held] for p in range(chips)]
+        rest = refs[chips * held :]
+        other_refs = [rest[p * held : (p + 1) * held] for p in range(chips - 1)]
+        out_refs, sems = rest[(chips - 1) * held : -1], rest[-1]
         position = place_ref[chips]
 
-        def pairs(p, source):
-            for j in range(parts):
-                if across:
-                    at = pl.ds(pl.multiple_of(place_ref[p] * second, second), second)
-                    target = out_ref.at[pl.ds(j * first, first), at]
-                else:
-                    at = pl.ds(pl.multiple_of(place_ref[p] * first, first), first)
-                    target = out_ref.at[at, pl.ds(j * second, second)]
-                yield pltpu.make_async_copy(source[j], target, sems.at[p * parts + j])
+        def moves(p, source):
+            rows = pl.ds(pl.multiple_of(place_ref[p] * block, block), block)
+            for j in range(count):
+                at = j * piece
+                taken = source[at // width].at[:, pl.ds(at % width, piece)]
+                target = out_refs[at // wide].at[rows, pl.ds(at % wide, piece)]
+                yield pltpu.make_async_copy(taken, target, sems.at[p * count + j])
 
         def begin(p, source):
-            for copy in pairs(p, source):
+            for copy in moves(p, source):
                 copy.start()
 
         begin(0, piece_refs[0])
@@ -174,7 +153,7 @@
             pl.when(position >= p)(lambda p=p: begin(p, piece_refs[p]))
             pl.when(position < p)(lambda p=p: begin(p, other_refs[chips - p - 1]))
         for p in range(chips):
-            for copy in pairs(p, piece_refs[0]):
+            for copy in moves(p, piece_refs[0]):
                 copy.wait()
 
     arrays = [part for shard in (*pieces, *others) for part in shard]
@@ -182,11 +161,12 @@
         run,
         tuple(arrays),
         [ANY] * len(arrays),
-        [jax.ShapeDtypeStruct(shape, jnp.bfloat16)],
-        [pltpu.SemaphoreType.DMA((chips * parts,))],
+        [jax.ShapeDtypeStruct((chips * block, wide), jnp.bfloat16)] * parts,
+        [pltpu.SemaphoreType.DMA((chips * count,))],
         4,
         after,
-    )[0]
+        us=2.4,
+    )
 
 
 def nesterov(delta, base_part, momentum_part):
@@ -229,9 +209,11 @@
         return lax.ppermute(value, "fsdp", move_perm(chips, active))
 
     class Gradient:
-        def __init__(self, mid, x):
+        def __init__(self, mid, x, after=()):
             terms = lax.dot_general(mid, x, (((0,), (0,)), ((), ())), preferred_element_type=f32)
             self.terms = terms.astype(bf16)
+            if after:
+                self.terms = fence(order, self.terms, after=after)[0]
             self.across = [None] + [swap(self.block(behind[chips - s])) for s in range(1, chips)]
             self.arrived = None
 
@@ -255,44 +237,37 @@
             partners = lax.dynamic_slice_in_dim(whole, (1 - core) * shard, shard, 1)
             return (mine + swap(partners.astype(bf16)).astype(f32)).T
 
-    first_own, second_own = value_weight[0], output_weight[0].T
+    def gather(own):
+        along = list(own)
+        pieces, others = [list(along)], []
+        for step in range(1, chips):
+            along = [move(part, lambda y: y >= step - 1) for part in along]
+            pieces.append(list(along))
+            others.append([swap(part) for part in along])
+        return pieces, others
+
+    first_own, second_own = value_weight[0], output_weight[0]
     first_partner, second_partner = swap(first_own), swap(second_own)
 
-    along = list(join_cores(order, first_own, first_partner, (second_partner,)))
-    pieces, others = [list(along)], []
-    normed = normalise(order, tokens[0], norm_gain)
-    for step in range(1, chips):
-        along = [move(part, lambda y: y >= step - 1) for part in along]
-        if step == 1:
-            along = [fence(order, along[0])[0], *along[1:]]
-        pieces.append(list(along))
-        others.append([swap(part) for part in along])
-    weight = assemble(order, pieces, others, False)
+    joined = join_cores(order, first_own, first_partner, HALVES, (second_partner,))
+    normed = normalise(order, tokens[0], norm_gain, ())
+    pieces, others = gather(joined)
+    early = pieces[-1]
+
+    joined = join_cores(order, second_own, second_partner, 1, (early[0],))
+    weight = assemble(order, pieces, others, 1, ())[0]
     values = jnp.dot(normed, weight, preferred_element_type=f32).astype(bf16)
-
-    message = join_cores_across(order, second_own, second_partner, (pieces[-1][0],))
-    arrived = move(message)
-    values = fence(order, values, after=(arrived,))[0]
-    first = Gradient(values, cotangent)
-    pieces, others = [[message]], []
-    for step in range(1, chips):
-        pieces.append([arrived])
-        others.append([swap(arrived)])
-        first.arrived = arrived
-        message = jnp.where(position >= step, arrived, first.message(step))
-        arrived = move(message)
-    first.arrived = arrived
-    weight = assemble(order, pieces, others, True, (message,))
-
-    half = weight.shape[0] // HALVES
+    pieces, others = gather(joined)
+    values = fence(order, values, after=(pieces[1][0],))[0]
+    first = Gradient(values, cotangent, (pieces[2][0],))
+    sent = [first.reduce(step) for step in range(1, chips)]
+
+    parts = assemble(order, pieces, others, HALVES, (sent[1],))
     second = []
-    for j in range(HALVES):
-        part = weight[j * half : (j + 1) * half]
-        mid = lax.dot_general(
-            cotangent, part, (((1,), (1,)), ((), ())), preferred_element_type=f32
-        ).astype(bf16)
-        if j == HALVES - 1:
-            mid = fence(order, mid, after=(arrived,))[0]
+    for part in parts:
+        mid = jnp.dot(cotangent, part, preferred_element_type=f32).astype(bf16)
+        if part is parts[-1]:
+            mid = fence(order, mid, after=(sent[-1],))[0]
         second.append(Gradient(mid, normed))
     for step in range(1, chips):
         for gradient in second:
@@ -312,7 +287,7 @@
             mine = total.astype(bf16)
             bit = 1 << ((turn + index) % bits)
             theirs = lax.ppermute(mine, "replica", [(i, i ^ bit) for i in range(replicas)])
-            total = mine.astype(f32) + theirs.astype(f32)
+            total = lax.optimization_barrier(mine).astype(f32) + theirs.astype(f32)
         sums.append(total)
     delta = jnp.concatenate(sums) * (1.0 / replicas)
     new_base, new_momentum = nesterov(delta, base_params, outer_momentum)

time: 207 us -> 223 us (1.077)
  waiting for transfers between devices: 31.3 us -> 46.2 us
  starting transfers between devices: 78 us -> 89.2 us
  local copies, waits for them, and re-layouts: 20.6 us -> 15.7 us
  other arithmetic: 30.3 us -> 27.7 us
    ppermute x23, starting transfers between devices: 21.7 us -> 31.2 us  [swap(): return lax.ppermute(value, 'fsdp', [(i, i ^ 1) for i in range(devices)])]
    ppermute x16 -> x18, waiting for transfers between devices: 21.6 us -> 30.7 us  [move(): return lax.ppermute(value, 'fsdp', move_perm(chips, active))]
    select_n x3 -> x0, other arithmetic: 8.11 us -> none  [per_device(): message = jnp.where(position >= step, arrived, first.message(step))]
    ppermute x4, waiting for transfers between devices: 5.44 us -> 13.2 us  [per_device(): lax.ppermute(mine, 'replica', [(i, i ^ bit) for i in range(replicas)])]
    convert_element_type x6 -> x9, other arithmetic: 1.48 us -> 8.98 us  [message(): return term.astype(bf16)]
    unnamed x63 -> x52, local copies, waits for them, and re-layouts: 18.1 us -> 12.2 us
    dynamic_slice x3, local copies, waits for them, and re-layouts: 0.34 us -> 2.69 us  [block(): return lax.dynamic_slice_in_dim(self.terms, where * block, block, 1)]
    ppermute x16 -> x18, starting transfers between devices: 50.1 us -> 52 us  [move(): return lax.ppermute(value, 'fsdp', move_perm(chips, active))]
  transfers between devices with their start and end apart: 43 -> 45, of which waited for: 12 -> 11; matrix products, arithmetic and copies ran while one was open for 28% -> 28% of each run, Pallas kernels for 4% -> 4%
where the time goes in v4:
time: 223 us
  starting transfers between devices  89.2 us (40%)
  waiting for transfers between devices  46.2 us (21%)
  matrix products  30 us (13%)
  other arithmetic  27.7 us (12%)
  local copies, waits for them, and re-layouts  15.7 us (7%)
  Pallas kernels  10.1 us (5%)
  between operations  3.46 us (2%)
    ppermute x18, starting transfers between devices, move(): return lax.ppermute(value, 'fsdp', move_perm(chips, active))  52 us
    ppermute x23, starting transfers between devices, swap(): return lax.ppermute(value, 'fsdp', [(i, i ^ 1) for i in range(devices)])  31.2 us
    ppermute x18, waiting for transfers between devices, move(): return lax.ppermute(value, 'fsdp', move_perm(chips, active))  30.7 us
    dot_general x3, matrix products, __init__(): lax.dot_general(mid, x, (((0,), (0,)), ((), ())), preferred_element_type=...  19.7 us
    ppermute x4, waiting for transfers between devices, per_device(): lax.ppermute(mine, 'replica', [(i, i ^ bit) for i in range(replicas)])  13.2 us
    unnamed x52, local copies, waits for them, and re-layouts  12.2 us
    pallas_call x8, Pallas kernels, __call__(): pl.pallas_call(ordered, grid_spec=pltpu.PrefetchScalarGridSpec(num_scalar...  10.1 us
    convert_element_type x9, other arithmetic, message(): return term.astype(bf16)  8.98 us
  transfers between devices with their start and end apart: 45, of which 11 were waited for; matrix products, arithmetic and copies ran while one was open for 28% of the time, Pallas kernels for 4%

profile of v4, /device:TPU:0, one launch (start us, length us, event | category | flops | bytes accessed | tf_op | source)
XLA Modules:
  0.0 222.5 jit_solution(9502183813577908146)
XLA Ops:
  1.3 1.6 collective-permute-done.refs_2_.refs_1_
  5.4 4.9 %collective-permute-start.2 = (bf16[1024,256]{1,0:T(8,128)(2,1)S(1)}, bf16[1024,256]{1,0:T(8,128)(2,1)S(1)}, u32[]{:S(2)}, u32[]{:S(2)}) collective-permute-start(bf16[1024,256]{1,0:T(8,128)(2,1)S(1)} %get-tuple-element.8.refs_2_.refs_0_), channel_id=1, source_target_pairs={{0,2},{2,4},{3,1},{4,6},{5,3},{7,5},{8,10},{10,12},{11,9},{12,14},... | collective-permute-start | bytes 1572872 | tf_op jit(solution)/shard_map/ppermute | solution.py:209
  10.3 4.3 %collective-permute-start.11 = (bf16[1024,256]{1,0:T(8,128)(2,1)S(1)}, bf16[1024,256]{1,0:T(8,128)(2,1)}, u32[]{:S(2)}, u32[]{:S(2)}) collective-permute-start(bf16[1024,256]{1,0:T(8,128)(2,1)S(1)} %get-tuple-element.9.refs_1_), channel_id=1, source_target_pairs={{0,2},{2,4},{3,1},{4,6},{5,3},{7,5},{8,10},{10,12},{11,9},{12,14},... | collective-permute-start | bytes 1572872 | tf_op jit(solution)/shard_map/ppermute | solution.py:209
  14.5 2.4 %collective-permute-done.2.refs_2_ = bf16[1024,256]{1,0:T(8,128)(2,1)S(1)} collective-permute-done((bf16[1024,256]{1,0:T(8,128)(2,1)S(1)}, bf16[1024,256]{1,0:T(8,128)(2,1)S(1)}, u32[]{:S(2)}, u32[]{:S(2)}) %collective-permute-start.2) | collective-permute-done | bytes 524320 | tf_op jit(solution)/shard_map/ppermute | solution.py:209
  16.9 1.4 collective-permute-start.3
  18.4 4.2 %collective-permute-done.11.refs_3_ = bf16[1024,256]{1,0:T(8,128)(2,1)} collective-permute-done((bf16[1024,256]{1,0:T(8,128)(2,1)S(1)}, bf16[1024,256]{1,0:T(8,128)(2,1)}, u32[]{:S(2)}, u32[]{:S(2)}) %collective-permute-start.11) | collective-permute-done | bytes 524320 | tf_op jit(solution)/shard_map/ppermute | solution.py:209
  22.5 1.5 collective-permute-start.12
  27.5 7.5 %collective-permute-start.15 = (bf16[1024,256]{1,0:T(8,128)(2,1)}, bf16[1024,256]{1,0:T(8,128)(2,1)S(1)}, u32[]{:S(2)}, u32[]{:S(2)}) collective-permute-start(bf16[1024,256]{1,0:T(8,128)(2,1)} %collective-permute-done.11.refs_3_), channel_id=1, source_target_pairs={{0,1},{1,0},{2,3},{3,2},{4,5},{5,4},{6,7},{7,6},{8,9},{9,8},{10,11... | collective-permute-start | bytes 1572872 | tf_op jit(solution)/shard_map/ppermute | solution.py:206
  35.5 4.1 %collective-permute-start.18 = (bf16[1024,256]{1,0:T(8,128)(2,1)S(1)}, bf16[1024,256]{1,0:T(8,128)(2,1)S(1)}, u32[]{:S(2)}, u32[]{:S(2)}) collective-permute-start(bf16[1024,256]{1,0:T(8,128)(2,1)S(1)} %collective-permute-done.4.refs_3_.refs_6_), channel_id=1, source_target_pairs={{0,1},{1,0},{2,3},{3,2},{4,5},{5,4},{6,7},{7,6},{8,9},{9,8},{10,11... | collective-permute-start | bytes 1572872 | tf_op jit(solution)/shard_map/ppermute | solution.py:206
  39.7 5.6 %collective-permute-start.19 = (bf16[1024,256]{1,0:T(8,128)(2,1)S(1)}, bf16[1024,256]{1,0:T(8,128)(2,1)S(1)}, u32[]{:S(2)}, u32[]{:S(2)}) collective-permute-start(bf16[1024,256]{1,0:T(8,128)(2,1)S(1)} %collective-permute-done.13.refs_7_), channel_id=1, source_target_pairs={{0,1},{1,0},{2,3},{3,2},{4,5},{5,4},{6,7},{7,6},{8,9},{9,8},{10,11... | collective-permute-start | bytes 1572872 | tf_op jit(solution)/shard_map/ppermute | solution.py:206
  45.3 3.4 %copy-done.8 = bf16[1,1024,4096]{2,1,0:T(8,128)(2,1)S(1)} copy-done((bf16[1,1024,4096]{2,1,0:T(8,128)(2,1)S(1)}, bf16[1,1024,4096]{2,1,0:T(8,128)(2,1)}, u32[]{:S(2)}) %copy-start.8) | copy-done | bytes 8388632
  48.7 5.3 %normalise.1.refs_2_ = bf16[1024,4096]{1,0:T(8,128)(2,1)S(1)} custom-call(s32[6]{0:T(128)S(1)} %pad_add_fusion.place_ref, bf16[1024,4096]{1,0:T(8,128)(2,1)S(1)} %bitcast.58, f32[1,4096]{1,0:T(1,128)S(1)} %bitcast.61, bf16[1024,256]{1,0:T(8,128)(2,1)S(1)} %get-tuple-element.8.refs_2_.refs_0_), custom_call_target="tpu_custom_call" | custom-call | flops 20000000000 | bytes 1 | tf_op jit(solution)/shard_map/normalise/pallas_call | solution.py:39
  54.7 1.9 collective-permute-start.5
  58.9 4.5 %convolution_convert_fusion.2.refs_0_ = bf16[1024,512]{1,0:T(8,128)(2,1)S(1)} fusion(bf16[1024,4096]{1,0:T(8,128)(2,1)S(1)} %normalise.1.refs_2_, bf16[4096,512]{1,0:T(8,128)(2,1)S(1)} %assemble.2.refs_1_), kind=kOutput, calls=%fused_computation.24 | convolution fusion | flops 4295491584 | bytes 13631488 | tf_op jit(solution)/shard_map/dot_general | solution.py:259
  63.3 5.5 %collective-permute-done.5.refs_2_.refs_1_ = bf16[1024,512]{1,0:T(8,128)(2,1)S(1)} collective-permute-done((bf16[1024,512]{1,0:T(8,128)(2,1)S(1)}, bf16[1024,512]{1,0:T(8,128)(2,1)S(1)}, u32[]{:S(2)}, u32[]{:S(2)}) %collective-permute-start.5) | collective-permute-done | bytes 1048608 | tf_op jit(solution)/shard_map/ppermute | solution.py:209
  68.8 1.6 collective-permute-start.6
  71.1 4.8 %fusion.6.refs_0_ = bf16[512,4096]{1,0:T(8,128)(2,1)S(1)} fusion(bf16[1024,512]{1,0:T(8,128)(2,1)S(1)} %fence.3.refs_1_, bf16[1,1024,4096]{2,1,0:T(8,128)(2,1)S(1)} %bitcast.65), kind=kOutput, calls=%fused_computation.6 | convolution fusion | flops 4297064448 | bytes 13631488 | tf_op jit(solution)/shard_map/dot_general | solution.py:213
  78.9 10.3 %collective-permute-start.21 = (bf16[512,1024]{1,0:T(8,128)(2,1)S(1)}, bf16[512,1024]{1,0:T(8,128)(2,1)}, u32[]{:S(2)}, u32[]{:S(2)}) collective-permute-start(bf16[512,1024]{1,0:T(8,128)(2,1)S(1)} %get-tuple-element.25), channel_id=1, source_target_pairs={{0,1},{1,0},{2,3},{3,2},{4,5},{5,4},{6,7},{7,6},{8,9},{9,8},{10,11... | collective-permute-start | bytes 3145736 | tf_op jit(solution)/shard_map/ppermute | solution.py:206
  89.2 3.1 %fusion.10 = (bf16[4096,128]{1,0:T(8,128)(2,1)}, bf16[4096,128]{1,0:T(8,128)(2,1)}) fusion(f32[4096]{0:T(1024)S(1)} %bitcast.62, bf16[1,8192,128]{2,1,0:T(8,128)(2,1)S(1)} %copy-done.18, f32[4096]{0:T(1024)S(1)} %bitcast.63), kind=kLoop, calls=%fused_computation.15 | loop fusion | flops 3145728 | bytes 4227072 | tf_op jit(solution)/shard_map/convert_element_type | solution.py:287
  92.3 1.5 collective-permute-start.43
  93.8 1.5 collective-permute-start.41
  96.9 3.1 %add_convert_fusion.4 = (bf16[512,1024]{1,0:T(8,128)(2,1)S(1)}, bf16[512,1024]{1,0:T(8,128)(2,1)}) fusion(bf16[512,1024]{1,0:T(8,128)(2,1)} %collective-permute-done.21, bf16[512,4096]{1,0:T(8,128)(2,1)} %copy-done.1, s32[]{:T(128)S(6)} %select_n.74), kind=kLoop, calls=%fused_computation.23 | loop fusion | flops 2097152 | bytes 4194308 | tf_op jit(solution)/shard_map/convert_element_type | solution.py:227
  100.0 5.2 %collective-permute-start.22 = (bf16[512,1024]{1,0:T(8,128)(2,1)S(1)}, bf16[512,1024]{1,0:T(8,128)(2,1)S(1)}, u32[]{:S(2)}, u32[]{:S(2)}) collective-permute-start(bf16[512,1024]{1,0:T(8,128)(2,1)S(1)} %get-tuple-element.22), channel_id=1, source_target_pairs={{0,2},{7,5},{8,10},{15,13},{16,18},{23,21},{24,26},{31,29}} | collective-permute-start | bytes 3145736 | tf_op jit(solution)/shard_map/ppermute | solution.py:209
  105.2 13.2 %collective-permute-done.43 = bf16[4096,128]{1,0:T(8,128)(2,1)} collective-permute-done((bf16[4096,128]{1,0:T(8,128)(2,1)}, bf16[4096,128]{1,0:T(8,128)(2,1)}, u32[]{:S(2)}, u32[]{:S(2)}) %collective-permute-start.43) | collective-permute-done | bytes 1048608 | tf_op jit(solution)/shard_map/ppermute | solution.py:289
  118.3 2.8 %add_convert_fusion = bf16[4096,128]{1,0:T(8,128)(2,1)} fusion(bf16[4096,128]{1,0:T(8,128)(2,1)} %collective-permute-done.43, bf16[4096,128]{1,0:T(8,128)(2,1)} %get-tuple-element.27), kind=kLoop, calls=%fused_computation.17 | loop fusion | flops 2097152 | bytes 3145728 | tf_op jit(solution)/shard_map/convert_element_type | solution.py:287
  121.7 2.8 %add_convert_fusion.1 = bf16[4096,128]{1,0:T(8,128)(2,1)} fusion(bf16[4096,128]{1,0:T(8,128)(2,1)} %collective-permute-done.41, bf16[4096,128]{1,0:T(8,128)(2,1)} %get-tuple-element.26), kind=kLoop, calls=%fused_computation.19 | loop fusion | flops 2097152 | bytes 3145728 | tf_op jit(solution)/shard_map/convert_element_type | solution.py:287
  124.5 1.5 collective-permute-start.44
  126.0 1.5 collective-permute-start.42
  128.3 5.4 %collective-permute-start.31 = (bf16[512,1024]{1,0:T(8,128)(2,1)S(1)}, bf16[512,1024]{1,0:T(8,128)(2,1)}, u32[]{:S(2)}, u32[]{:S(2)}) collective-permute-start(bf16[512,1024]{1,0:T(8,128)(2,1)S(1)} %add_convert_fusion.3.refs_8_), channel_id=1, source_target_pairs={{0,2},{2,4},{5,3},{7,5},{8,10},{10,12},{13,11},{15,13},{16,18},{18... | collective-permute-start | bytes 3145736 | tf_op jit(solution)/shard_map/ppermute | solution.py:209
  137.3 12.4 %convolution_convert_fusion.1 = bf16[256,4096]{1,0:T(8,128)(2,1)} fusion(bf16[1024,4096]{1,0:T(8,128)(2,1)} %copy-done, bf16[4096,256]{1,0:T(8,128)(2,1)} %copy-done.3, bf16[1,1024,4096]{2,1,0:T(8,128)(2,1)} %param.13), kind=kOutput, calls=%fused_computation.8 | convolution fusion | flops 4296278016 | bytes 20971520 | tf_op jit(solution)/shard_map/dot_general | solution.py:213
  149.7 1.4 constant_dynamic-slice_fusion.3
  151.2 5.9 %fusion.17.refs_0_ = bf16[1024,256]{1,0:T(8,128)(2,1)S(1)} fusion(bf16[4096,256]{1,0:T(8,128)(2,1)S(1)} %copy-done.10, bf16[1,1024,4096]{2,1,0:T(8,128)(2,1)} %param.13), kind=kOutput, calls=%fused_computation.27 | convolution fusion | flops 2147745792 | bytes 11010048 | tf_op jit(solution)/shard_map/dot_general | solution.py:268
  157.9 3.9 %collective-permute-start.26 = (bf16[256,1024]{1,0:T(8,128)(2,1)S(1)}, bf16[256,1024]{1,0:T(8,128)(2,1)S(1)}, u32[]{:S(2)}, u32[]{:S(2)}) collective-permute-start(bf16[256,1024]{1,0:T(8,128)(2,1)S(1)} %get-tuple-element.18), channel_id=1, source_target_pairs={{0,2},{7,5},{8,10},{15,13},{16,18},{23,21},{24,26},{31,29}} | collective-permute-start | bytes 1572872 | tf_op jit(solution)/shard_map/ppermute | solution.py:209
  161.8 2.2 add_convert_fusion.2.refs_2_
  164.5 2.5 %convolution_convert_fusion = bf16[256,4096]{1,0:T(8,128)(2,1)S(1)} fusion(bf16[1024,256]{1,0:T(8,128)(2,1)S(1)} %fence.5, bf16[1024,4096]{1,0:T(8,128)(2,1)S(1)} %bitcast.55), kind=kOutput, calls=%fused_computation.7 | convolution fusion | flops 2148532224 | bytes 11010048 | tf_op jit(solution)/shard_map/dot_general | solution.py:213
  167.2 1.7 convert_add_fusion
  169.9 3.2 %collective-permute-start.27 = (bf16[256,1024]{1,0:T(8,128)(2,1)S(1)}, bf16[256,1024]{1,0:T(8,128)(2,1)S(1)}, u32[]{:S(2)}, u32[]{:S(2)}) collective-permute-start(bf16[256,1024]{1,0:T(8,128)(2,1)S(1)} %add_convert_fusion.9), channel_id=1, source_target_pairs={{0,2},{2,4},{5,3},{7,5},{8,10},{10,12},{13,11},{15,13},{16,18},{18... | collective-permute-start | bytes 1572872 | tf_op jit(solution)/shard_map/ppermute | solution.py:209
  173.3 1.9 collective-permute-start.35
  175.3 1.9 convert_add_fusion.1
  177.2 1.6 collective-permute-start.39
  180.8 4.4 %collective-permute-start.28 = (bf16[256,1024]{1,0:T(8,128)(2,1)}, bf16[256,1024]{1,0:T(8,128)(2,1)S(1)}, u32[]{:S(2)}, u32[]{:S(2)}) collective-permute-start(bf16[256,1024]{1,0:T(8,128)(2,1)} %add_convert_fusion.8), channel_id=1, source_target_pairs={{0,2},{2,4},{3,1},{4,6},{5,3},{7,5},{8,10},{10,12},{11,9},{12,14},... | collective-permute-start | bytes 1572872 | tf_op jit(solution)/shard_map/ppermute | solution.py:209
  186.4 4.4 %collective-permute-start.36 = (bf16[256,1024]{1,0:T(8,128)(2,1)}, bf16[256,1024]{1,0:T(8,128)(2,1)S(1)}, u32[]{:S(2)}, u32[]{:S(2)}) collective-permute-start(bf16[256,1024]{1,0:T(8,128)(2,1)} %add_convert_fusion.6), channel_id=1, source_target_pairs={{0,2},{2,4},{5,3},{7,5},{8,10},{10,12},{13,11},{15,13},{16,18},{18... | collective-permute-start | bytes 1572872 | tf_op jit(solution)/shard_map/ppermute | solution.py:209
  190.9 3.9 %subtract_convert_fusion = (bf16[8192,128]{1,0:T(8,128)(2,1)}, f32[8192,128]{1,0:T(8,128)}) fusion(bf16[8192,128]{1,0:T(8,128)(2,1)S(1)} %copy-done.19, f32[4096,128]{1,0:T(8,128)S(1)} %convert_add_fusion, f32[4096,128]{1,0:T(8,128)S(1)} %convert_add_fusion.1, f32[8192,128]{1,0:T(8,128)S(1)} %copy-done.16), kind=kLoop, calls=%fused_computation.10 | loop fusion | flops 10485760 | bytes 16777216 | tf_op jit(solution)/shard_map/convert_element_type | solution.py:174
  194.8 7.5 %collective-permute-done.28 = bf16[256,1024]{1,0:T(8,128)(2,1)S(1)} collective-permute-done((bf16[256,1024]{1,0:T(8,128)(2,1)}, bf16[256,1024]{1,0:T(8,128)(2,1)S(1)}, u32[]{:S(2)}, u32[]{:S(2)}) %collective-permute-start.28) | collective-permute-done | bytes 524320 | tf_op jit(solution)/shard_map/ppermute | solution.py:209
  202.7 5.3 %collective-permute-done.36 = bf16[256,1024]{1,0:T(8,128)(2,1)S(1)} collective-permute-done((bf16[256,1024]{1,0:T(8,128)(2,1)}, bf16[256,1024]{1,0:T(8,128)(2,1)S(1)}, u32[]{:S(2)}, u32[]{:S(2)}) %collective-permute-start.36) | collective-permute-done | bytes 524320 | tf_op jit(solution)/shard_map/ppermute | solution.py:209
  208.2 4.3 %collective-permute-start.37 = (bf16[256,1024]{1,0:T(8,128)(2,1)S(1)}, bf16[256,1024]{1,0:T(8,128)(2,1)S(1)}, u32[]{:S(2)}, u32[]{:S(2)}) collective-permute-start(bf16[256,1024]{1,0:T(8,128)(2,1)S(1)} %add_convert_fusion.5), channel_id=1, source_target_pairs={{0,2},{2,4},{3,1},{4,6},{5,3},{7,5},{8,10},{10,12},{11,9},{12,14},... | collective-permute-start | bytes 1572872 | tf_op jit(solution)/shard_map/ppermute | solution.py:209
  212.6 1.6 convert_add_fusion.2
  214.4 4.8 %collective-permute-done.37 = bf16[256,1024]{1,0:T(8,128)(2,1)S(1)} collective-permute-done((bf16[256,1024]{1,0:T(8,128)(2,1)S(1)}, bf16[256,1024]{1,0:T(8,128)(2,1)S(1)}, u32[]{:S(2)}, u32[]{:S(2)}) %collective-permute-start.37) | collective-permute-done | bytes 524320 | tf_op jit(solution)/shard_map/ppermute | solution.py:209
  (141 shorter events, 27.9 us)
Async XLA Ops:
  0.6 26.8 %copy-start.20 = (s32[1,8192]{1,0:T(1,128)S(1)}, s32[1,8192]{1,0:T(1,128)}, u32[]{:S(2)}) copy-start(s32[1,8192]{1,0:T(1,128)} %param.17) | copy-start | bytes 98308
  0.6 44.6 %copy-start.12 = (f32[4096]{0:T(1024)S(1)}, f32[4096]{0:T(1024)}, u32[]{:S(2)}) copy-start(f32[4096]{0:T(1024)} %param.10) | copy-start | bytes 49156
  0.7 2.3 %collective-permute-start = (bf16[512,512]{1,0:T(8,128)(2,1)}, bf16[512,512]{1,0:T(8,128)(2,1)S(1)}, u32[]{:S(2)}, u32[]{:S(2)}) collective-permute-start(bf16[512,512]{1,0:T(8,128)(2,1)} %bitcast.56), channel_id=1, source_target_pairs={{0,1},{1,0},{2,3},{3,2},{4,5},{5,4},{6,7},{7,6},{8,9},{9,8},{10,11... | collective-permute-start | bytes 1572872 | tf_op jit(solution)/shard_map/ppermute | solution.py:206
  1.2 2.5 %collective-permute-start.1 = (bf16[512,512]{1,0:T(8,128)(2,1)}, bf16[512,512]{1,0:T(8,128)(2,1)S(1)}, u32[]{:S(2)}, u32[]{:S(2)}) collective-permute-start(bf16[512,512]{1,0:T(8,128)(2,1)} %bitcast.59), channel_id=1, source_target_pairs={{0,1},{1,0},{2,3},{3,2},{4,5},{5,4},{6,7},{7,6},{8,9},{9,8},{10,11... | collective-permute-start | bytes 1572872 | tf_op jit(solution)/shard_map/ppermute | solution.py:206
  5.4 11.5 %collective-permute-start.2 = (bf16[1024,256]{1,0:T(8,128)(2,1)S(1)}, bf16[1024,256]{1,0:T(8,128)(2,1)S(1)}, u32[]{:S(2)}, u32[]{:S(2)}) collective-permute-start(bf16[1024,256]{1,0:T(8,128)(2,1)S(1)} %get-tuple-element.8.refs_2_.refs_0_), channel_id=1, source_target_pairs={{0,2},{2,4},{3,1},{4,6},{5,3},{7,5},{8,10},{10,12},{11,9},{12,14},... | collective-permute-start | bytes 1572872 | tf_op jit(solution)/shard_map/ppermute | solution.py:209
  10.3 12.3 %collective-permute-start.11 = (bf16[1024,256]{1,0:T(8,128)(2,1)S(1)}, bf16[1024,256]{1,0:T(8,128)(2,1)}, u32[]{:S(2)}, u32[]{:S(2)}) collective-permute-start(bf16[1024,256]{1,0:T(8,128)(2,1)S(1)} %get-tuple-element.9.refs_1_), channel_id=1, source_target_pairs={{0,2},{2,4},{3,1},{4,6},{5,3},{7,5},{8,10},{10,12},{11,9},{12,14},... | collective-permute-start | bytes 1572872 | tf_op jit(solution)/shard_map/ppermute | solution.py:209
  16.9 37.1 %copy-start.6 = (bf16[1024,256]{1,0:T(8,128)(2,1)}, bf16[1024,256]{1,0:T(8,128)(2,1)S(1)}, u32[]{:S(2)}) copy-start(bf16[1024,256]{1,0:T(8,128)(2,1)S(1)} %collective-permute-done.2.refs_2_) | copy-start | bytes 1572868
  16.9 9.1 %collective-permute-start.3 = (bf16[1024,256]{1,0:T(8,128)(2,1)S(1)}, bf16[1024,256]{1,0:T(8,128)(2,1)}, u32[]{:S(2)}, u32[]{:S(2)}) collective-permute-start(bf16[1024,256]{1,0:T(8,128)(2,1)S(1)} %collective-permute-done.2.refs_2_), channel_id=1, source_target_pairs={{2,4},{3,1},{4,6},{5,3},{10,12},{11,9},{12,14},{13,11},{18,20},{19... | collective-permute-start | bytes 1572872 | tf_op jit(solution)/shard_map/ppermute | solution.py:209
  22.5 4.2 %collective-permute-start.12 = (bf16[1024,256]{1,0:T(8,128)(2,1)}, bf16[1024,256]{1,0:T(8,128)(2,1)}, u32[]{:S(2)}, u32[]{:S(2)}) collective-permute-start(bf16[1024,256]{1,0:T(8,128)(2,1)} %collective-permute-done.11.refs_3_), channel_id=1, source_target_pairs={{2,4},{3,1},{4,6},{5,3},{10,12},{11,9},{12,14},{13,11},{18,20},{19... | collective-permute-start | bytes 1572872 | tf_op jit(solution)/shard_map/ppermute | solution.py:209
  25.9 9.2 %collective-permute-start.14 = (bf16[1024,256]{1,0:T(8,128)(2,1)S(1)}, bf16[1024,256]{1,0:T(8,128)(2,1)S(1)}, u32[]{:S(2)}, u32[]{:S(2)}) collective-permute-start(bf16[1024,256]{1,0:T(8,128)(2,1)S(1)} %collective-permute-done.2.refs_2_), channel_id=1, source_target_pairs={{0,1},{1,0},{2,3},{3,2},{4,5},{5,4},{6,7},{7,6},{8,9},{9,8},{10,11... | collective-permute-start | bytes 1572872 | tf_op jit(solution)/shard_map/ppermute | solution.py:206
  26.0 9.6 %collective-permute-start.4 = (bf16[1024,256]{1,0:T(8,128)(2,1)}, bf16[1024,256]{1,0:T(8,128)(2,1)S(1)}, u32[]{:S(2)}, u32[]{:S(2)}) collective-permute-start(bf16[1024,256]{1,0:T(8,128)(2,1)} %collective-permute-done.3.refs_4_), channel_id=1, source_target_pairs={{3,1},{4,6},{11,9},{12,14},{19,17},{20,22},{27,25},{28,30}} | collective-permute-start | bytes 1572872 | tf_op jit(solution)/shard_map/ppermute | solution.py:209
  26.7 13.0 %collective-permute-start.13 = (bf16[1024,256]{1,0:T(8,128)(2,1)}, bf16[1024,256]{1,0:T(8,128)(2,1)S(1)}, u32[]{:S(2)}, u32[]{:S(2)}) collective-permute-start(bf16[1024,256]{1,0:T(8,128)(2,1)} %collective-permute-done.12.refs_5_), channel_id=1, source_target_pairs={{3,1},{4,6},{11,9},{12,14},{19,17},{20,22},{27,25},{28,30}} | collective-permute-start | bytes 1572872 | tf_op jit(solution)/shard_map/ppermute | solution.py:209
  27.5 27.2 %collective-permute-start.15 = (bf16[1024,256]{1,0:T(8,128)(2,1)}, bf16[1024,256]{1,0:T(8,128)(2,1)S(1)}, u32[]{:S(2)}, u32[]{:S(2)}) collective-permute-start(bf16[1024,256]{1,0:T(8,128)(2,1)} %collective-permute-done.11.refs_3_), channel_id=1, source_target_pairs={{0,1},{1,0},{2,3},{3,2},{4,5},{5,4},{6,7},{7,6},{8,9},{9,8},{10,11... | collective-permute-start | bytes 1572872 | tf_op jit(solution)/shard_map/ppermute | solution.py:206
  35.0 21.6 %collective-permute-start.16 = (bf16[1024,256]{1,0:T(8,128)(2,1)}, bf16[1024,256]{1,0:T(8,128)(2,1)S(1)}, u32[]{:S(2)}, u32[]{:S(2)}) collective-permute-start(bf16[1024,256]{1,0:T(8,128)(2,1)} %collective-permute-done.3.refs_4_), channel_id=1, source_target_pairs={{0,1},{1,0},{2,3},{3,2},{4,5},{5,4},{6,7},{7,6},{8,9},{9,8},{10,11... | collective-permute-start | bytes 1572872 | tf_op jit(solution)/shard_map/ppermute | solution.py:206
  35.1 21.5 %collective-permute-start.17 = (bf16[1024,256]{1,0:T(8,128)(2,1)}, bf16[1024,256]{1,0:T(8,128)(2,1)S(1)}, u32[]{:S(2)}, u32[]{:S(2)}) collective-permute-start(bf16[1024,256]{1,0:T(8,128)(2,1)} %collective-permute-done.12.refs_5_), channel_id=1, source_target_pairs={{0,1},{1,0},{2,3},{3,2},{4,5},{5,4},{6,7},{7,6},{8,9},{9,8},{10,11... | collective-permute-start | bytes 1572872 | tf_op jit(solution)/shard_map/ppermute | solution.py:206
  35.5 21.1 %collective-permute-start.18 = (bf16[1024,256]{1,0:T(8,128)(2,1)S(1)}, bf16[1024,256]{1,0:T(8,128)(2,1)S(1)}, u32[]{:S(2)}, u32[]{:S(2)}) collective-permute-start(bf16[1024,256]{1,0:T(8,128)(2,1)S(1)} %collective-permute-done.4.refs_3_.refs_6_), channel_id=1, source_target_pairs={{0,1},{1,0},{2,3},{3,2},{4,5},{5,4},{6,7},{7,6},{8,9},{9,8},{10,11... | collective-permute-start | bytes 1572872 | tf_op jit(solution)/shard_map/ppermute | solution.py:206
  39.7 17.0 %collective-permute-start.19 = (bf16[1024,256]{1,0:T(8,128)(2,1)S(1)}, bf16[1024,256]{1,0:T(8,128)(2,1)S(1)}, u32[]{:S(2)}, u32[]{:S(2)}) collective-permute-start(bf16[1024,256]{1,0:T(8,128)(2,1)S(1)} %collective-permute-done.13.refs_7_), channel_id=1, source_target_pairs={{0,1},{1,0},{2,3},{3,2},{4,5},{5,4},{6,7},{7,6},{8,9},{9,8},{10,11... | collective-permute-start | bytes 1572872 | tf_op jit(solution)/shard_map/ppermute | solution.py:206
  54.7 14.2 %collective-permute-start.5 = (bf16[1024,512]{1,0:T(8,128)(2,1)S(1)}, bf16[1024,512]{1,0:T(8,128)(2,1)S(1)}, u32[]{:S(2)}, u32[]{:S(2)}) collective-permute-start(bf16[1024,512]{1,0:T(8,128)(2,1)S(1)} %join_cores.3.refs_14_.refs_0_), channel_id=1, source_target_pairs={{0,2},{2,4},{3,1},{4,6},{5,3},{7,5},{8,10},{10,12},{11,9},{12,14},... | collective-permute-start | bytes 3145736 | tf_op jit(solution)/shard_map/ppermute | solution.py:209
  68.8 7.0 %collective-permute-start.6 = (bf16[1024,512]{1,0:T(8,128)(2,1)S(1)}, bf16[1024,512]{1,0:T(8,128)(2,1)}, u32[]{:S(2)}, u32[]{:S(2)}) collective-permute-start(bf16[1024,512]{1,0:T(8,128)(2,1)S(1)} %collective-permute-done.5.refs_2_.refs_1_), channel_id=1, source_target_pairs={{2,4},{3,1},{4,6},{5,3},{10,12},{11,9},{12,14},{13,11},{18,20},{19... | collective-permute-start | bytes 3145736 | tf_op jit(solution)/shard_map/ppermute | solution.py:209
  78.9 18.0 %collective-permute-start.21 = (bf16[512,1024]{1,0:T(8,128)(2,1)S(1)}, bf16[512,1024]{1,0:T(8,128)(2,1)}, u32[]{:S(2)}, u32[]{:S(2)}) collective-permute-start(bf16[512,1024]{1,0:T(8,128)(2,1)S(1)} %get-tuple-element.25), channel_id=1, source_target_pairs={{0,1},{1,0},{2,3},{3,2},{4,5},{5,4},{6,7},{7,6},{8,9},{9,8},{10,11... | collective-permute-start | bytes 3145736 | tf_op jit(solution)/shard_map/ppermute | solution.py:206
  92.3 26.0 %collective-permute-start.43 = (bf16[4096,128]{1,0:T(8,128)(2,1)}, bf16[4096,128]{1,0:T(8,128)(2,1)}, u32[]{:S(2)}, u32[]{:S(2)}) collective-permute-start(bf16[4096,128]{1,0:T(8,128)(2,1)} %get-tuple-element.27), channel_id=1, source_target_pairs={{0,16},{8,24},{16,0},{24,8},{1,17},{9,25},{17,1},{25,9},{2,18},{10... | collective-permute-start | bytes 3145736 | tf_op jit(solution)/shard_map/ppermute | solution.py:289
  93.8 27.3 %collective-permute-start.41 = (bf16[4096,128]{1,0:T(8,128)(2,1)}, bf16[4096,128]{1,0:T(8,128)(2,1)}, u32[]{:S(2)}, u32[]{:S(2)}) collective-permute-start(bf16[4096,128]{1,0:T(8,128)(2,1)} %get-tuple-element.26), channel_id=1, source_target_pairs={{0,8},{8,0},{16,24},{24,16},{1,9},{9,1},{17,25},{25,17},{2,10},{10... | collective-permute-start | bytes 3145736 | tf_op jit(solution)/shard_map/ppermute | solution.py:289
  96.0 28.5 %collective-permute-start.20 = (bf16[512,1024]{1,0:T(8,128)(2,1)}, bf16[512,1024]{1,0:T(8,128)(2,1)S(1)}, u32[]{:S(2)}, u32[]{:S(2)}) collective-permute-start(bf16[512,1024]{1,0:T(8,128)(2,1)} %get-tuple-element.24), channel_id=1, source_target_pairs={{0,1},{1,0},{2,3},{3,2},{4,5},{5,4},{6,7},{7,6},{8,9},{9,8},{10,11... | collective-permute-start | bytes 3145736 | tf_op jit(solution)/shard_map/ppermute | solution.py:206
  96.2 25.5 %collective-permute-start.7 = (bf16[1024,512]{1,0:T(8,128)(2,1)}, bf16[1024,512]{1,0:T(8,128)(2,1)S(1)}, u32[]{:S(2)}, u32[]{:S(2)}) collective-permute-start(bf16[1024,512]{1,0:T(8,128)(2,1)} %collective-permute-done.6.refs_2_), channel_id=1, source_target_pairs={{3,1},{4,6},{11,9},{12,14},{19,17},{20,22},{27,25},{28,30}} | collective-permute-start | bytes 3145736 | tf_op jit(solution)/shard_map/ppermute | solution.py:209
  100.0 26.0 %collective-permute-start.22 = (bf16[512,1024]{1,0:T(8,128)(2,1)S(1)}, bf16[512,1024]{1,0:T(8,128)(2,1)S(1)}, u32[]{:S(2)}, u32[]{:S(2)}) collective-permute-start(bf16[512,1024]{1,0:T(8,128)(2,1)S(1)} %get-tuple-element.22), channel_id=1, source_target_pairs={{0,2},{7,5},{8,10},{15,13},{16,18},{23,21},{24,26},{31,29}} | collective-permute-start | bytes 3145736 | tf_op jit(solution)/shard_map/ppermute | solution.py:209
  121.1 7.0 %collective-permute-start.8 = (bf16[1024,512]{1,0:T(8,128)(2,1)S(1)}, bf16[1024,512]{1,0:T(8,128)(2,1)S(1)}, u32[]{:S(2)}, u32[]{:S(2)}) collective-permute-start(bf16[1024,512]{1,0:T(8,128)(2,1)S(1)} %collective-permute-done.5.refs_2_.refs_1_), channel_id=1, source_target_pairs={{0,1},{1,0},{2,3},{3,2},{4,5},{5,4},{6,7},{7,6},{8,9},{9,8},{10,11... | collective-permute-start | bytes 3145736 | tf_op jit(solution)/shard_map/ppermute | solution.py:206
  121.2 7.1 %collective-permute-start.9 = (bf16[1024,512]{1,0:T(8,128)(2,1)}, bf16[1024,512]{1,0:T(8,128)(2,1)S(1)}, u32[]{:S(2)}, u32[]{:S(2)}) collective-permute-start(bf16[1024,512]{1,0:T(8,128)(2,1)} %collective-permute-done.6.refs_2_), channel_id=1, source_target_pairs={{0,1},{1,0},{2,3},{3,2},{4,5},{5,4},{6,7},{7,6},{8,9},{9,8},{10,11... | collective-permute-start | bytes 3145736 | tf_op jit(solution)/shard_map/ppermute | solution.py:206
  121.7 12.0 %collective-permute-start.10 = (bf16[1024,512]{1,0:T(8,128)(2,1)S(1)}, bf16[1024,512]{1,0:T(8,128)(2,1)S(1)}, u32[]{:S(2)}, u32[]{:S(2)}) collective-permute-start(bf16[1024,512]{1,0:T(8,128)(2,1)S(1)} %collective-permute-done.7.refs_3_), channel_id=1, source_target_pairs={{0,1},{1,0},{2,3},{3,2},{4,5},{5,4},{6,7},{7,6},{8,9},{9,8},{10,11... | collective-permute-start | bytes 3145736 | tf_op jit(solution)/shard_map/ppermute | solution.py:206
  124.5 42.7 %collective-permute-start.44 = (bf16[4096,128]{1,0:T(8,128)(2,1)}, bf16[4096,128]{1,0:T(8,128)(2,1)}, u32[]{:S(2)}, u32[]{:S(2)}) collective-permute-start(bf16[4096,128]{1,0:T(8,128)(2,1)} %add_convert_fusion), channel_id=1, source_target_pairs={{0,8},{8,0},{16,24},{24,16},{1,9},{9,1},{17,25},{25,17},{2,10},{10... | collective-permute-start | bytes 3145736 | tf_op jit(solution)/shard_map/ppermute | solution.py:289
  126.0 49.3 %collective-permute-start.42 = (bf16[4096,128]{1,0:T(8,128)(2,1)}, bf16[4096,128]{1,0:T(8,128)(2,1)}, u32[]{:S(2)}, u32[]{:S(2)}) collective-permute-start(bf16[4096,128]{1,0:T(8,128)(2,1)} %add_convert_fusion.1), channel_id=1, source_target_pairs={{0,16},{8,24},{16,0},{24,8},{1,17},{9,25},{17,1},{25,9},{2,18},{10... | collective-permute-start | bytes 3145736 | tf_op jit(solution)/shard_map/ppermute | solution.py:289
  128.2 29.7 %collective-permute-start.30 = (bf16[512,1024]{1,0:T(8,128)(2,1)}, bf16[512,1024]{1,0:T(8,128)(2,1)}, u32[]{:S(2)}, u32[]{:S(2)}) collective-permute-start(bf16[512,1024]{1,0:T(8,128)(2,1)} %get-tuple-element.23), channel_id=1, source_target_pairs={{0,1},{1,0},{2,3},{3,2},{4,5},{5,4},{6,7},{7,6},{8,9},{9,8},{10,11... | collective-permute-start | bytes 3145736 | tf_op jit(solution)/shard_map/ppermute | solution.py:206
  128.3 33.5 %collective-permute-start.31 = (bf16[512,1024]{1,0:T(8,128)(2,1)S(1)}, bf16[512,1024]{1,0:T(8,128)(2,1)}, u32[]{:S(2)}, u32[]{:S(2)}) collective-permute-start(bf16[512,1024]{1,0:T(8,128)(2,1)S(1)} %add_convert_fusion.3.refs_8_), channel_id=1, source_target_pairs={{0,2},{2,4},{5,3},{7,5},{8,10},{10,12},{13,11},{15,13},{16,18},{18... | collective-permute-start | bytes 3145736 | tf_op jit(solution)/shard_map/ppermute | solution.py:209
  151.1 6.0 %collective-permute-start.25 = (bf16[256,1024]{1,0:T(8,128)(2,1)S(1)}, bf16[256,1024]{1,0:T(8,128)(2,1)S(1)}, u32[]{:S(2)}, u32[]{:S(2)}) collective-permute-start(bf16[256,1024]{1,0:T(8,128)(2,1)S(1)} %get-tuple-element.29), channel_id=1, source_target_pairs={{0,1},{1,0},{2,3},{3,2},{4,5},{5,4},{6,7},{7,6},{8,9},{9,8},{10,11... | collective-permute-start | bytes 1572872 | tf_op jit(solution)/shard_map/ppermute | solution.py:206
  157.1 12.4 %collective-permute-start.24 = (bf16[256,1024]{1,0:T(8,128)(2,1)S(1)}, bf16[256,1024]{1,0:T(8,128)(2,1)S(1)}, u32[]{:S(2)}, u32[]{:S(2)}) collective-permute-start(bf16[256,1024]{1,0:T(8,128)(2,1)S(1)} %get-tuple-element.28), channel_id=1, source_target_pairs={{0,1},{1,0},{2,3},{3,2},{4,5},{5,4},{6,7},{7,6},{8,9},{9,8},{10,11... | collective-permute-start | bytes 1572872 | tf_op jit(solution)/shard_map/ppermute | solution.py:206
  157.9 11.8 %collective-permute-start.26 = (bf16[256,1024]{1,0:T(8,128)(2,1)S(1)}, bf16[256,1024]{1,0:T(8,128)(2,1)S(1)}, u32[]{:S(2)}, u32[]{:S(2)}) collective-permute-start(bf16[256,1024]{1,0:T(8,128)(2,1)S(1)} %get-tuple-element.18), channel_id=1, source_target_pairs={{0,2},{7,5},{8,10},{15,13},{16,18},{23,21},{24,26},{31,29}} | collective-permute-start | bytes 1572872 | tf_op jit(solution)/shard_map/ppermute | solution.py:209
  167.2 6.0 %collective-permute-start.34 = (bf16[256,1024]{1,0:T(8,128)(2,1)S(1)}, bf16[256,1024]{1,0:T(8,128)(2,1)S(1)}, u32[]{:S(2)}, u32[]{:S(2)}) collective-permute-start(bf16[256,1024]{1,0:T(8,128)(2,1)S(1)} %get-tuple-element.31), channel_id=1, source_target_pairs={{0,1},{1,0},{2,3},{3,2},{4,5},{5,4},{6,7},{7,6},{8,9},{9,8},{10,11... | collective-permute-start | bytes 1572872 | tf_op jit(solution)/shard_map/ppermute | solution.py:206
  169.0 9.8 %collective-permute-start.23 = (bf16[256,1024]{1,0:T(8,128)(2,1)S(1)}, bf16[256,1024]{1,0:T(8,128)(2,1)S(1)}, u32[]{:S(2)}, u32[]{:S(2)}) collective-permute-start(bf16[256,1024]{1,0:T(8,128)(2,1)S(1)} %get-tuple-element.19), channel_id=1, source_target_pairs={{0,1},{1,0},{2,3},{3,2},{4,5},{5,4},{6,7},{7,6},{8,9},{9,8},{10,11... | collective-permute-start | bytes 1572872 | tf_op jit(solution)/shard_map/ppermute | solution.py:206
  169.6 15.7 %collective-permute-start.33 = (bf16[256,1024]{1,0:T(8,128)(2,1)S(1)}, bf16[256,1024]{1,0:T(8,128)(2,1)S(1)}, u32[]{:S(2)}, u32[]{:S(2)}) collective-permute-start(bf16[256,1024]{1,0:T(8,128)(2,1)S(1)} %get-tuple-element.30), channel_id=1, source_target_pairs={{0,1},{1,0},{2,3},{3,2},{4,5},{5,4},{6,7},{7,6},{8,9},{9,8},{10,11... | collective-permute-start | bytes 1572872 | tf_op jit(solution)/shard_map/ppermute | solution.py:206
  169.9 9.8 %collective-permute-start.27 = (bf16[256,1024]{1,0:T(8,128)(2,1)S(1)}, bf16[256,1024]{1,0:T(8,128)(2,1)S(1)}, u32[]{:S(2)}, u32[]{:S(2)}) collective-permute-start(bf16[256,1024]{1,0:T(8,128)(2,1)S(1)} %add_convert_fusion.9), channel_id=1, source_target_pairs={{0,2},{2,4},{5,3},{7,5},{8,10},{10,12},{13,11},{15,13},{16,18},{18... | collective-permute-start | bytes 1572872 | tf_op jit(solution)/shard_map/ppermute | solution.py:209
  173.3 12.0 %collective-permute-start.35 = (bf16[256,1024]{1,0:T(8,128)(2,1)S(1)}, bf16[256,1024]{1,0:T(8,128)(2,1)S(1)}, u32[]{:S(2)}, u32[]{:S(2)}) collective-permute-start(bf16[256,1024]{1,0:T(8,128)(2,1)S(1)} %get-tuple-element.20), channel_id=1, source_target_pairs={{0,2},{7,5},{8,10},{15,13},{16,18},{23,21},{24,26},{31,29}} | collective-permute-start | bytes 1572872 | tf_op jit(solution)/shard_map/ppermute | solution.py:209
  177.2 35.4 %collective-permute-start.39 = (bf16[512,1024]{1,0:T(8,128)(2,1)S(1)}, bf16[512,1024]{1,0:T(8,128)(2,1)S(1)}, u32[]{:S(2)}, u32[]{:S(2)}) collective-permute-start(bf16[512,1024]{1,0:T(8,128)(2,1)S(1)} %add_convert_fusion.2.refs_2_), channel_id=1, source_target_pairs={{0,2},{2,4},{3,1},{4,6},{5,3},{7,5},{8,10},{10,12},{11,9},{12,14},... | collective-permute-start | bytes 3145736 | tf_op jit(solution)/shard_map/ppermute | solution.py:209
  178.8 23.9 %collective-permute-start.32 = (bf16[256,1024]{1,0:T(8,128)(2,1)S(1)}, bf16[256,1024]{1,0:T(8,128)(2,1)S(1)}, u32[]{:S(2)}, u32[]{:S(2)}) collective-permute-start(bf16[256,1024]{1,0:T(8,128)(2,1)S(1)} %get-tuple-element.21), channel_id=1, source_target_pairs={{0,1},{1,0},{2,3},{3,2},{4,5},{5,4},{6,7},{7,6},{8,9},{9,8},{10,11... | collective-permute-start | bytes 1572872 | tf_op jit(solution)/shard_map/ppermute | solution.py:206
  180.8 21.5 %collective-permute-start.28 = (bf16[256,1024]{1,0:T(8,128)(2,1)}, bf16[256,1024]{1,0:T(8,128)(2,1)S(1)}, u32[]{:S(2)}, u32[]{:S(2)}) collective-permute-start(bf16[256,1024]{1,0:T(8,128)(2,1)} %add_convert_fusion.8), channel_id=1, source_target_pairs={{0,2},{2,4},{3,1},{4,6},{5,3},{7,5},{8,10},{10,12},{11,9},{12,14},... | collective-permute-start | bytes 1572872 | tf_op jit(solution)/shard_map/ppermute | solution.py:209
  186.4 21.5 %collective-permute-start.36 = (bf16[256,1024]{1,0:T(8,128)(2,1)}, bf16[256,1024]{1,0:T(8,128)(2,1)S(1)}, u32[]{:S(2)}, u32[]{:S(2)}) collective-permute-start(bf16[256,1024]{1,0:T(8,128)(2,1)} %add_convert_fusion.6), channel_id=1, source_target_pairs={{0,2},{2,4},{5,3},{7,5},{8,10},{10,12},{13,11},{15,13},{16,18},{18... | collective-permute-start | bytes 1572872 | tf_op jit(solution)/shard_map/ppermute | solution.py:209
  202.6 11.8 %collective-permute-start.29 = (bf16[256,512]{1,0:T(8,128)(2,1)S(1)}, bf16[256,512]{1,0:T(8,128)(2,1)S(1)}, u32[]{:S(2)}, u32[]{:S(2)}) collective-permute-start(bf16[256,512]{1,0:T(8,128)(2,1)S(1)} %dynamic-slice_convert_fusion.2), channel_id=1, source_target_pairs={{0,1},{1,0},{2,3},{3,2},{4,5},{5,4},{6,7},{7,6},{8,9},{9,8},{10,11... | collective-permute-start | bytes 786440 | tf_op jit(solution)/shard_map/ppermute | solution.py:206
  208.2 11.0 %collective-permute-start.37 = (bf16[256,1024]{1,0:T(8,128)(2,1)S(1)}, bf16[256,1024]{1,0:T(8,128)(2,1)S(1)}, u32[]{:S(2)}, u32[]{:S(2)}) collective-permute-start(bf16[256,1024]{1,0:T(8,128)(2,1)S(1)} %add_convert_fusion.5), channel_id=1, source_target_pairs={{0,2},{2,4},{3,1},{4,6},{5,3},{7,5},{8,10},{10,12},{11,9},{12,14},... | collective-permute-start | bytes 1572872 | tf_op jit(solution)/shard_map/ppermute | solution.py:209
  214.3 5.2 %collective-permute-start.40 = (bf16[512,512]{1,0:T(8,128)(2,1)S(1)}, bf16[512,512]{1,0:T(8,128)(2,1)S(1)}, u32[]{:S(2)}, u32[]{:S(2)}) collective-permute-start(bf16[512,512]{1,0:T(8,128)(2,1)S(1)} %dynamic-slice_convert_fusion), channel_id=1, source_target_pairs={{0,1},{1,0},{2,3},{3,2},{4,5},{5,4},{6,7},{7,6},{8,9},{9,8},{10,11... | collective-permute-start | bytes 1572872 | tf_op jit(solution)/shard_map/ppermute | solution.py:206
  219.4 1.6 collective-permute-start.38
  (22 other events, 175.0 us)

commit v5 on v4

--- a/solution.py
+++ b/solution.py
@@ -218,7 +218,11 @@
             self.arrived = None
 
         def block(self, where):
-            return lax.dynamic_slice_in_dim(self.terms, where * block, block, 1)
+            chosen = self.terms[:, :block]
+            for at in range(1, chips):
+                part = self.terms[:, at * block : (at + 1) * block]
+                chosen = jnp.where(where == at, part, chosen)
+            return chosen
 
         def message(self, step):
             term = self.block(behind[step]).astype(f32) + self.across[step].astype(f32)
@@ -233,15 +237,18 @@
 
         def finish(self):
             whole = self.block(chip).astype(f32) + self.arrived.astype(f32)
-            mine = lax.dynamic_slice_in_dim(whole, core * shard, shard, 1)
-            partners = lax.dynamic_slice_in_dim(whole, (1 - core) * shard, shard, 1)
+            first, second = whole[:, :shard], whole[:, shard:]
+            mine = jnp.where(core == 0, first, second)
+            partners = jnp.where(core == 0, second, first)
             return (mine + swap(partners.astype(bf16)).astype(f32)).T
 
-    def gather(own):
+    def gather(own, at_first=False):
         along = list(own)
         pieces, others = [list(along)], []
         for step in range(1, chips):
             along = [move(part, lambda y: y >= step - 1) for part in along]
+            if at_first and step == 1:
+                along[:1] = fence(order, along[0])
             pieces.append(list(along))
             others.append([swap(part) for part in along])
         return pieces, others
@@ -249,46 +256,47 @@
     first_own, second_own = value_weight[0], output_weight[0]
     first_partner, second_partner = swap(first_own), swap(second_own)
 
-    joined = join_cores(order, first_own, first_partner, HALVES, (second_partner,))
-    normed = normalise(order, tokens[0], norm_gain, ())
-    pieces, others = gather(joined)
-    early = pieces[-1]
-
-    joined = join_cores(order, second_own, second_partner, 1, (early[0],))
-    weight = assemble(order, pieces, others, 1, ())[0]
-    values = jnp.dot(normed, weight, preferred_element_type=f32).astype(bf16)
-    pieces, others = gather(joined)
-    values = fence(order, values, after=(pieces[1][0],))[0]
-    first = Gradient(values, cotangent, (pieces[2][0],))
-    sent = [first.reduce(step) for step in range(1, chips)]
-
-    parts = assemble(order, pieces, others, HALVES, (sent[1],))
-    second = []
-    for part in parts:
-        mid = jnp.dot(cotangent, part, preferred_element_type=f32).astype(bf16)
-        if part is parts[-1]:
-            mid = fence(order, mid, after=(sent[-1],))[0]
-        second.append(Gradient(mid, normed))
-    for step in range(1, chips):
-        for gradient in second:
-            gradient.reduce(step)
-    output_grad = first.finish()
-
     bits = replicas.bit_length() - 1
     if replicas != 1 << bits or bits < 1:
         raise ValueError("replicas")
-    half = base_params.shape[0] // 2
-    sums = []
+    rows_half = base_params.shape[0] // 2
+    sums, early = [], []
     for index in range(2):
-        rows = slice(index * half, (index + 1) * half)
+        rows = slice(index * rows_half, (index + 1) * rows_half)
         scale = jnp.exp2(delta_exponents[0, rows].astype(f32))[:, None]
         total = delta_values[0, rows].astype(f32) * scale
         for turn in range(bits):
             mine = total.astype(bf16)
             bit = 1 << ((turn + index) % bits)
             theirs = lax.ppermute(mine, "replica", [(i, i ^ bit) for i in range(replicas)])
+            if turn == 0:
+                early.append(theirs)
             total = lax.optimization_barrier(mine).astype(f32) + theirs.astype(f32)
         sums.append(total)
+
+    joined = join_cores(order, first_own, first_partner, HALVES, (second_partner,))
+    normed = normalise(order, tokens[0], norm_gain, ())
+    pieces, others = gather(joined, at_first=True)
+    last = pieces[-1]
+
+    joined = join_cores(order, second_own, second_partner, 1, (last[0],))
+    weight = assemble(order, pieces, others, 1, early)[0]
+    values = jnp.dot(normed, weight, preferred_element_type=f32).astype(bf16)
+    pieces, others = gather(joined)
+    values = fence(order, values, after=(pieces[1][0],))[0]
+    first = Gradient(values, cotangent, (pieces[2][0],))
+    sent = [first.reduce(step) for step in range(1, chips)]
+
+    weight = assemble(order, pieces, others, 1, (sent[1],))[0]
+    mid = jnp.dot(cotangent, weight, preferred_element_type=f32).astype(bf16)
+    mid = fence(order, mid, after=(sent[-1],))[0]
+    half = mid.shape[1] // HALVES
+    second = [Gradient(mid[:, j * half : (j + 1) * half], normed) for j in range(HALVES)]
+    for step in range(1, chips):
+        for gradient in second:
+            gradient.reduce(step)
+    output_grad = first.finish()
+
     delta = jnp.concatenate(sums) * (1.0 / replicas)
     new_base, new_momentum = nesterov(delta, base_params, outer_momentum)
     value_grad = jnp.concatenate([gradient.finish() for gradient in second], axis=1)

time: 223 us -> 209 us (0.937)
  waiting for transfers between devices: 46.2 us -> 32.4 us
  matrix products: 30 us -> 21.5 us
  other arithmetic: 27.7 us -> 35.7 us
  local copies, waits for them, and re-layouts: 15.7 us -> 8.08 us
  between operations: 3.46 us -> 7.21 us
  starting transfers between devices: 89.2 us -> 91.7 us
    ppermute x18, waiting for transfers between devices: 30.7 us -> 18.2 us  [move(): return lax.ppermute(value, 'fsdp', move_perm(chips, active))]
    dot_general x3, matrix products: 19.7 us -> 9.55 us  [__init__(): lax.dot_general(mid, x, (((0,), (0,)), ((), ())), preferred_element_type=...]
    unnamed x52 -> x40, local copies, waits for them, and re-layouts: 12.2 us -> 7.43 us
    convert_element_type x9, other arithmetic: 8.98 us -> 12.9 us  [message(): return term.astype(bf16)]
    add x2, other arithmetic: 3.64 us -> 0.41 us  [per_device(): total = lax.optimization_barrier(mine).astype(f32) + theirs.astype(f32)]
    select_n x0 -> x3, other arithmetic: none -> 2.73 us  [block(): chosen = jnp.where(where == at, part, chosen)]
    dynamic_slice x3 -> x0, local copies, waits for them, and re-layouts: 2.69 us -> none  [block(): return lax.dynamic_slice_in_dim(self.terms, where * block, block, 1)]
    ppermute x23, starting transfers between devices: 31.2 us -> 33.6 us  [swap(): return lax.ppermute(value, 'fsdp', [(i, i ^ 1) for i in range(devices)])]
  transfers between devices with their start and end apart: 45 -> 45, of which waited for: 11 -> 9; matrix products, arithmetic and copies ran while one was open for 28% -> 27% of each run, Pallas kernels for 4% -> 5%
where the time goes in v5:
time: 209 us; the launch traced here: 208 us
  starting transfers between devices  91.7 us (44%)
  other arithmetic  35.7 us (17%)
  waiting for transfers between devices  32.4 us (16%)
  matrix products  21.5 us (10%)
  Pallas kernels  11.7 us (6%)
  local copies, waits for them, and re-layouts  8.08 us (4%)
  between operations  7.21 us (3%)
    ppermute x18, starting transfers between devices, move(): return lax.ppermute(value, 'fsdp', move_perm(chips, active))  52.5 us
    ppermute x23, starting transfers between devices, swap(): return lax.ppermute(value, 'fsdp', [(i, i ^ 1) for i in range(devices)])  33.6 us
    ppermute x18, waiting for transfers between devices, move(): return lax.ppermute(value, 'fsdp', move_perm(chips, active))  18.2 us
    ppermute x4, waiting for transfers between devices, per_device(): lax.ppermute(mine, 'replica', [(i, i ^ bit) for i in range(replicas)])  14.1 us
    convert_element_type x9, other arithmetic, message(): return term.astype(bf16)  12.9 us
    pallas_call x9, Pallas kernels, __call__(): pl.pallas_call(ordered, grid_spec=pltpu.PrefetchScalarGridSpec(num_scalar...  11.7 us
    dot_general x3, matrix products, __init__(): lax.dot_general(mid, x, (((0,), (0,)), ((), ())), preferred_element_type=...  9.55 us
    convert_element_type x3, other arithmetic, per_device(): mine = total.astype(bf16)  7.91 us
  transfers between devices with their start and end apart: 45, of which 9 were waited for; matrix products, arithmetic and copies ran while one was open for 27% of the time, Pallas kernels for 5%

profile of v5, /device:TPU:0, one launch (start us, length us, event | category | flops | bytes accessed | tf_op | source)
XLA Modules:
  0.0 208.2 jit_solution(8079747318404312223)
XLA Ops:
  2.0 4.8 %fusion.7 = (bf16[4096,128]{1,0:T(8,128)(2,1)}, bf16[4096,128]{1,0:T(8,128)(2,1)}) fusion(f32[4096]{0:T(1024)S(1)} %bitcast.60, bf16[1,8192,128]{2,1,0:T(8,128)(2,1)} %param.16, f32[4096]{0:T(1024)S(1)} %bitcast.61), kind=kLoop, calls=%fused_computation.11 | loop fusion | flops 3145728 | bytes 4227072 | tf_op jit(solution)/shard_map/convert_element_type | solution.py:269
  6.8 2.9 %collective-permute-start.20 = (bf16[4096,128]{1,0:T(8,128)(2,1)}, bf16[4096,128]{1,0:T(8,128)(2,1)S(1)}, u32[]{:S(2)}, u32[]{:S(2)}) collective-permute-start(bf16[4096,128]{1,0:T(8,128)(2,1)} %get-tuple-element.27), channel_id=1, source_target_pairs={{0,8},{8,0},{16,24},{24,16},{1,9},{9,1},{17,25},{25,17},{2,10},{10... | collective-permute-start | bytes 3145736 | tf_op jit(solution)/shard_map/ppermute | solution.py:271
  9.7 1.5 collective-permute-start.21
  11.3 1.6 join_cores.2
  13.0 3.5 %collective-permute-start.2 = (bf16[1024,256]{1,0:T(8,128)(2,1)S(1)}, bf16[1024,256]{1,0:T(8,128)(2,1)S(1)}, u32[]{:S(2)}, u32[]{:S(2)}) collective-permute-start(bf16[1024,256]{1,0:T(8,128)(2,1)S(1)} %get-tuple-element.6.refs_2_.refs_0_), channel_id=1, source_target_pairs={{0,2},{2,4},{3,1},{4,6},{5,3},{7,5},{8,10},{10,12},{11,9},{12,14},... | collective-permute-start | bytes 1572872 | tf_op jit(solution)/shard_map/ppermute | solution.py:209
  16.5 3.5 %collective-permute-start.11 = (bf16[1024,256]{1,0:T(8,128)(2,1)S(1)}, bf16[1024,256]{1,0:T(8,128)(2,1)S(1)}, u32[]{:S(2)}, u32[]{:S(2)}) collective-permute-start(bf16[1024,256]{1,0:T(8,128)(2,1)S(1)} %get-tuple-element.7.refs_1_), channel_id=1, source_target_pairs={{0,2},{2,4},{3,1},{4,6},{5,3},{7,5},{8,10},{10,12},{11,9},{12,14},... | collective-permute-start | bytes 1572872 | tf_op jit(solution)/shard_map/ppermute | solution.py:209
  20.0 3.4 %copy-done.7 = bf16[1,1024,4096]{2,1,0:T(8,128)(2,1)S(1)} copy-done((bf16[1,1024,4096]{2,1,0:T(8,128)(2,1)S(1)}, bf16[1,1024,4096]{2,1,0:T(8,128)(2,1)}, u32[]{:S(2)}) %copy-start.7) | copy-done | bytes 8388632
  23.4 5.4 %normalise.1.refs_1_ = bf16[1024,4096]{1,0:T(8,128)(2,1)S(1)} custom-call(s32[6]{0:T(128)S(1)} %pad_add_fusion.place_ref, bf16[1024,4096]{1,0:T(8,128)(2,1)S(1)} %bitcast.54, f32[1,4096]{1,0:T(1,128)S(1)} %bitcast.59, bf16[1024,256]{1,0:T(8,128)(2,1)S(1)} %get-tuple-element.6.refs_2_.refs_0_), custom_call_target="tpu_custom_call" | custom-call | flops 20000000000 | bytes 1 | tf_op jit(solution)/shard_map/normalise/pallas_call | solution.py:39
  33.3 9.5 %collective-permute-start.15 = (bf16[1024,256]{1,0:T(8,128)(2,1)S(1)}, bf16[1024,256]{1,0:T(8,128)(2,1)S(1)}, u32[]{:S(2)}, u32[]{:S(2)}) collective-permute-start(bf16[1024,256]{1,0:T(8,128)(2,1)S(1)} %collective-permute-done.11.refs_3_), channel_id=1, source_target_pairs={{0,1},{1,0},{2,3},{3,2},{4,5},{5,4},{6,7},{7,6},{8,9},{9,8},{10,11... | collective-permute-start | bytes 1572872 | tf_op jit(solution)/shard_map/ppermute | solution.py:206
  43.3 3.7 %collective-permute-start.18 = (bf16[1024,256]{1,0:T(8,128)(2,1)S(1)}, bf16[1024,256]{1,0:T(8,128)(2,1)S(1)}, u32[]{:S(2)}, u32[]{:S(2)}) collective-permute-start(bf16[1024,256]{1,0:T(8,128)(2,1)S(1)} %collective-permute-done.4.refs_3_.refs_6_), channel_id=1, source_target_pairs={{0,1},{1,0},{2,3},{3,2},{4,5},{5,4},{6,7},{7,6},{8,9},{9,8},{10,11... | collective-permute-start | bytes 1572872 | tf_op jit(solution)/shard_map/ppermute | solution.py:206
  47.0 5.6 %collective-permute-start.19 = (bf16[1024,256]{1,0:T(8,128)(2,1)S(1)}, bf16[1024,256]{1,0:T(8,128)(2,1)S(1)}, u32[]{:S(2)}, u32[]{:S(2)}) collective-permute-start(bf16[1024,256]{1,0:T(8,128)(2,1)S(1)} %collective-permute-done.13.refs_7_), channel_id=1, source_target_pairs={{0,1},{1,0},{2,3},{3,2},{4,5},{5,4},{6,7},{7,6},{8,9},{9,8},{10,11... | collective-permute-start | bytes 1572872 | tf_op jit(solution)/shard_map/ppermute | solution.py:206
  57.9 1.8 collective-permute-start.5
  59.7 1.0 assemble.2.refs_1_
  60.8 4.5 %convolution_convert_fusion.2.refs_0_ = bf16[1024,512]{1,0:T(8,128)(2,1)S(1)} fusion(bf16[1024,4096]{1,0:T(8,128)(2,1)S(1)} %normalise.1.refs_1_, bf16[4096,512]{1,0:T(8,128)(2,1)S(1)} %assemble.2.refs_1_), kind=kOutput, calls=%fused_computation.23 | convolution fusion | flops 4295491584 | bytes 13631488 | tf_op jit(solution)/shard_map/dot_general | solution.py:284
  65.2 6.7 %collective-permute-done.5.refs_2_.refs_1_ = bf16[1024,512]{1,0:T(8,128)(2,1)S(1)} collective-permute-done((bf16[1024,512]{1,0:T(8,128)(2,1)S(1)}, bf16[1024,512]{1,0:T(8,128)(2,1)S(1)}, u32[]{:S(2)}, u32[]{:S(2)}) %collective-permute-start.5) | collective-permute-done | bytes 1048608 | tf_op jit(solution)/shard_map/ppermute | solution.py:209
  73.2 4.8 %fusion.4.refs_0_ = bf16[512,4096]{1,0:T(8,128)(2,1)S(1)} fusion(bf16[1024,512]{1,0:T(8,128)(2,1)S(1)} %fence.5.refs_1_, bf16[1,1024,4096]{2,1,0:T(8,128)(2,1)S(1)} %bitcast.63), kind=kOutput, calls=%fused_computation.4 | convolution fusion | flops 4297064448 | bytes 13631488 | tf_op jit(solution)/shard_map/dot_general | solution.py:213
  79.0 1.7 select_select_fusion.2
  80.7 0.9 copy-done.1
  81.7 11.8 %collective-permute-start.23 = (bf16[512,1024]{1,0:T(8,128)(2,1)}, bf16[512,1024]{1,0:T(8,128)(2,1)}, u32[]{:S(2)}, u32[]{:S(2)}) collective-permute-start(bf16[512,1024]{1,0:T(8,128)(2,1)} %get-tuple-element.21), channel_id=1, source_target_pairs={{0,1},{1,0},{2,3},{3,2},{4,5},{5,4},{6,7},{7,6},{8,9},{9,8},{10,11... | collective-permute-start | bytes 3145736 | tf_op jit(solution)/shard_map/ppermute | solution.py:206
  95.4 1.6 add_convert_fusion
  98.4 3.7 %add_convert_fusion.4 = (bf16[512,1024]{1,0:T(8,128)(2,1)S(1)}, bf16[512,1024]{1,0:T(8,128)(2,1)S(1)}) fusion(bf16[512,1024]{1,0:T(8,128)(2,1)} %collective-permute-done.23, bf16[512,4096]{1,0:T(8,128)(2,1)} %copy-done.1, pred[]{:T(512)} %bitcast.16, pred[]{:T(512)} %bitcast.15, pred[]{:T(512)} %bitcast.14), kind=kLoop, calls=%fused_computation.21 | loop fusion | flops 3670016 | bytes 7340035 | tf_op jit(solution)/shard_map/convert_element_type | solution.py:231
  102.1 5.3 %collective-permute-start.24 = (bf16[512,1024]{1,0:T(8,128)(2,1)S(1)}, bf16[512,1024]{1,0:T(8,128)(2,1)S(1)}, u32[]{:S(2)}, u32[]{:S(2)}) collective-permute-start(bf16[512,1024]{1,0:T(8,128)(2,1)S(1)} %get-tuple-element.18), channel_id=1, source_target_pairs={{0,2},{7,5},{8,10},{15,13},{16,18},{23,21},{24,26},{31,29}} | collective-permute-start | bytes 3145736 | tf_op jit(solution)/shard_map/ppermute | solution.py:209
  107.4 1.5 add_convert_fusion.1
  109.0 13.1 %collective-permute-done.44 = bf16[4096,128]{1,0:T(8,128)(2,1)S(1)} collective-permute-done((bf16[4096,128]{1,0:T(8,128)(2,1)S(1)}, bf16[4096,128]{1,0:T(8,128)(2,1)S(1)}, u32[]{:S(2)}, u32[]{:S(2)}) %collective-permute-start.44) | collective-permute-done | bytes 1048608 | tf_op jit(solution)/shard_map/ppermute | solution.py:271
  124.1 5.4 %collective-permute-start.26 = (bf16[512,1024]{1,0:T(8,128)(2,1)S(1)}, bf16[512,1024]{1,0:T(8,128)(2,1)S(1)}, u32[]{:S(2)}, u32[]{:S(2)}) collective-permute-start(bf16[512,1024]{1,0:T(8,128)(2,1)S(1)} %add_convert_fusion.3.refs_8_), channel_id=1, source_target_pairs={{0,2},{2,4},{5,3},{7,5},{8,10},{10,12},{13,11},{15,13},{16,18},{18... | collective-permute-start | bytes 3145736 | tf_op jit(solution)/shard_map/ppermute | solution.py:209
  130.5 7.4 %fusion.12.refs_0_ = bf16[1024,512]{1,0:T(8,128)(2,1)S(1)} fusion(bf16[4096,512]{1,0:T(8,128)(2,1)S(1)} %assemble.3.refs_1_, bf16[1,1024,4096]{2,1,0:T(8,128)(2,1)} %param.13), kind=kOutput, calls=%fused_computation.24 | convolution fusion | flops 4295491584 | bytes 13631488 | tf_op jit(solution)/shard_map/dot_general | solution.py:291
  137.9 3.8 %collective-permute-done.26 = bf16[512,1024]{1,0:T(8,128)(2,1)S(1)} collective-permute-done((bf16[512,1024]{1,0:T(8,128)(2,1)S(1)}, bf16[512,1024]{1,0:T(8,128)(2,1)S(1)}, u32[]{:S(2)}, u32[]{:S(2)}) %collective-permute-start.26) | collective-permute-done | bytes 1048608 | tf_op jit(solution)/shard_map/ppermute | solution.py:209
  141.8 1.9 add_convert_fusion.2.refs_2_
  144.2 2.4 %convolution_convert_fusion = bf16[256,4096]{1,0:T(8,128)(2,1)S(1)} fusion(bf16[1024,4096]{1,0:T(8,128)(2,1)S(1)} %bitcast.53, bf16[1024,512]{1,0:T(8,128)(2,1)S(1)} %fence.7), kind=kOutput, calls=%fused_computation.5 | convolution fusion | flops 2148532224 | bytes 11010048 | tf_op jit(solution)/shard_map/dot_general | solution.py:213
  147.5 2.4 %convolution_convert_fusion.1 = bf16[256,4096]{1,0:T(8,128)(2,1)S(1)} fusion(bf16[1024,4096]{1,0:T(8,128)(2,1)S(1)} %bitcast.53, bf16[1024,512]{1,0:T(8,128)(2,1)S(1)} %fence.7), kind=kOutput, calls=%fused_computation.6 | convolution fusion | flops 2148532224 | bytes 11010048 | tf_op jit(solution)/shard_map/dot_general | solution.py:213
  150.8 5.4 %collective-permute-start.41 = (bf16[512,1024]{1,0:T(8,128)(2,1)S(1)}, bf16[512,1024]{1,0:T(8,128)(2,1)}, u32[]{:S(2)}, u32[]{:S(2)}) collective-permute-start(bf16[512,1024]{1,0:T(8,128)(2,1)S(1)} %add_convert_fusion.2.refs_2_), channel_id=1, source_target_pairs={{0,2},{2,4},{3,1},{4,6},{5,3},{7,5},{8,10},{10,12},{11,9},{12,14},... | collective-permute-start | bytes 3145736 | tf_op jit(solution)/shard_map/ppermute | solution.py:209
  156.7 1.5 add_convert_fusion.7
  158.2 4.4 %collective-permute-start.37 = (bf16[256,1024]{1,0:T(8,128)(2,1)}, bf16[256,1024]{1,0:T(8,128)(2,1)}, u32[]{:S(2)}, u32[]{:S(2)}) collective-permute-start(bf16[256,1024]{1,0:T(8,128)(2,1)} %get-tuple-element.16), channel_id=1, source_target_pairs={{0,2},{7,5},{8,10},{15,13},{16,18},{23,21},{24,26},{31,29}} | collective-permute-start | bytes 1572872 | tf_op jit(solution)/shard_map/ppermute | solution.py:209
  162.6 1.5 add_convert_fusion.10
  164.1 2.1 %collective-permute-start.30 = (bf16[256,1024]{1,0:T(8,128)(2,1)}, bf16[256,1024]{1,0:T(8,128)(2,1)}, u32[]{:S(2)}, u32[]{:S(2)}) collective-permute-start(bf16[256,1024]{1,0:T(8,128)(2,1)} %get-tuple-element.14), channel_id=1, source_target_pairs={{0,2},{7,5},{8,10},{15,13},{16,18},{23,21},{24,26},{31,29}} | collective-permute-start | bytes 1572872 | tf_op jit(solution)/shard_map/ppermute | solution.py:209
  166.3 5.7 %subtract_convert_fusion = (bf16[8192,128]{1,0:T(8,128)(2,1)}, f32[8192,128]{1,0:T(8,128)}) fusion(bf16[8192,128]{1,0:T(8,128)(2,1)} %param.14, f32[4096,128]{1,0:T(8,128)S(1)} %convert_add_fusion, f32[4096,128]{1,0:T(8,128)S(1)} %convert_add_fusion.1, f32[8192,128]{1,0:T(8,128)S(1)} %copy-done.14), kind=kLoop, calls=%fused_computation.8 | loop fusion | flops 10485760 | bytes 16777216 | tf_op jit(solution)/shard_map/convert_element_type | solution.py:174
  172.0 1.2 collective-permute-done.37
  173.2 1.6 add_convert_fusion.6
  174.9 4.4 %collective-permute-start.38 = (bf16[256,1024]{1,0:T(8,128)(2,1)S(1)}, bf16[256,1024]{1,0:T(8,128)(2,1)S(1)}, u32[]{:S(2)}, u32[]{:S(2)}) collective-permute-start(bf16[256,1024]{1,0:T(8,128)(2,1)S(1)} %add_convert_fusion.6), channel_id=1, source_target_pairs={{0,2},{2,4},{5,3},{7,5},{8,10},{10,12},{13,11},{15,13},{16,18},{18... | collective-permute-start | bytes 1572872 | tf_op jit(solution)/shard_map/ppermute | solution.py:209
  179.3 1.5 add_convert_fusion.9
  180.8 4.0 %collective-permute-start.31 = (bf16[256,1024]{1,0:T(8,128)(2,1)S(1)}, bf16[256,1024]{1,0:T(8,128)(2,1)S(1)}, u32[]{:S(2)}, u32[]{:S(2)}) collective-permute-start(bf16[256,1024]{1,0:T(8,128)(2,1)S(1)} %add_convert_fusion.9), channel_id=1, source_target_pairs={{0,2},{2,4},{5,3},{7,5},{8,10},{10,12},{13,11},{15,13},{16,18},{18... | collective-permute-start | bytes 1572872 | tf_op jit(solution)/shard_map/ppermute | solution.py:209
  184.7 1.6 convert_add_fusion.2
  186.6 4.0 %collective-permute-start.39 = (bf16[256,1024]{1,0:T(8,128)(2,1)S(1)}, bf16[256,1024]{1,0:T(8,128)(2,1)S(1)}, u32[]{:S(2)}, u32[]{:S(2)}) collective-permute-start(bf16[256,1024]{1,0:T(8,128)(2,1)S(1)} %add_convert_fusion.5), channel_id=1, source_target_pairs={{0,2},{2,4},{3,1},{4,6},{5,3},{7,5},{8,10},{10,12},{11,9},{12,14},... | collective-permute-start | bytes 1572872 | tf_op jit(solution)/shard_map/ppermute | solution.py:209
  191.8 4.4 %collective-permute-start.32 = (bf16[256,1024]{1,0:T(8,128)(2,1)S(1)}, bf16[256,1024]{1,0:T(8,128)(2,1)S(1)}, u32[]{:S(2)}, u32[]{:S(2)}) collective-permute-start(bf16[256,1024]{1,0:T(8,128)(2,1)S(1)} %add_convert_fusion.8), channel_id=1, source_target_pairs={{0,2},{2,4},{3,1},{4,6},{5,3},{7,5},{8,10},{10,12},{11,9},{12,14},... | collective-permute-start | bytes 1572872 | tf_op jit(solution)/shard_map/ppermute | solution.py:209
  198.2 4.7 %collective-permute-done.32 = bf16[256,1024]{1,0:T(8,128)(2,1)S(1)} collective-permute-done((bf16[256,1024]{1,0:T(8,128)(2,1)S(1)}, bf16[256,1024]{1,0:T(8,128)(2,1)S(1)}, u32[]{:S(2)}, u32[]{:S(2)}) %collective-permute-start.32) | collective-permute-done | bytes 524320 | tf_op jit(solution)/shard_map/ppermute | solution.py:209
  204.2 1.3 copy.19
  205.7 1.1 add_bitcast_fusion.2
  206.9 1.3 copy.18
  (130 shorter events, 22.1 us)
Async XLA Ops:
  0.6 10.7 %collective-permute-start.1 = (bf16[512,512]{1,0:T(8,128)(2,1)}, bf16[512,512]{1,0:T(8,128)(2,1)}, u32[]{:S(2)}, u32[]{:S(2)}) collective-permute-start(bf16[512,512]{1,0:T(8,128)(2,1)} %bitcast.55), channel_id=1, source_target_pairs={{0,1},{1,0},{2,3},{3,2},{4,5},{5,4},{6,7},{7,6},{8,9},{9,8},{10,11... | collective-permute-start | bytes 1572872 | tf_op jit(solution)/shard_map/ppermute | solution.py:206
  1.1 10.2 %collective-permute-start = (bf16[512,512]{1,0:T(8,128)(2,1)}, bf16[512,512]{1,0:T(8,128)(2,1)S(1)}, u32[]{:S(2)}, u32[]{:S(2)}) collective-permute-start(bf16[512,512]{1,0:T(8,128)(2,1)} %bitcast.57), channel_id=1, source_target_pairs={{0,1},{1,0},{2,3},{3,2},{4,5},{5,4},{6,7},{7,6},{8,9},{9,8},{10,11... | collective-permute-start | bytes 1572872 | tf_op jit(solution)/shard_map/ppermute | solution.py:206
  6.8 26.5 %collective-permute-start.20 = (bf16[4096,128]{1,0:T(8,128)(2,1)}, bf16[4096,128]{1,0:T(8,128)(2,1)S(1)}, u32[]{:S(2)}, u32[]{:S(2)}) collective-permute-start(bf16[4096,128]{1,0:T(8,128)(2,1)} %get-tuple-element.27), channel_id=1, source_target_pairs={{0,8},{8,0},{16,24},{24,16},{1,9},{9,1},{17,25},{25,17},{2,10},{10... | collective-permute-start | bytes 3145736 | tf_op jit(solution)/shard_map/ppermute | solution.py:271
  9.7 33.1 %collective-permute-start.21 = (bf16[4096,128]{1,0:T(8,128)(2,1)}, bf16[4096,128]{1,0:T(8,128)(2,1)S(1)}, u32[]{:S(2)}, u32[]{:S(2)}) collective-permute-start(bf16[4096,128]{1,0:T(8,128)(2,1)} %get-tuple-element.26), channel_id=1, source_target_pairs={{0,16},{8,24},{16,0},{24,8},{1,17},{9,25},{17,1},{25,9},{2,18},{10... | collective-permute-start | bytes 3145736 | tf_op jit(solution)/shard_map/ppermute | solution.py:271
  13.0 15.8 %collective-permute-start.2 = (bf16[1024,256]{1,0:T(8,128)(2,1)S(1)}, bf16[1024,256]{1,0:T(8,128)(2,1)S(1)}, u32[]{:S(2)}, u32[]{:S(2)}) collective-permute-start(bf16[1024,256]{1,0:T(8,128)(2,1)S(1)} %get-tuple-element.6.refs_2_.refs_0_), channel_id=1, source_target_pairs={{0,2},{2,4},{3,1},{4,6},{5,3},{7,5},{8,10},{10,12},{11,9},{12,14},... | collective-permute-start | bytes 1572872 | tf_op jit(solution)/shard_map/ppermute | solution.py:209
  16.5 13.7 %collective-permute-start.11 = (bf16[1024,256]{1,0:T(8,128)(2,1)S(1)}, bf16[1024,256]{1,0:T(8,128)(2,1)S(1)}, u32[]{:S(2)}, u32[]{:S(2)}) collective-permute-start(bf16[1024,256]{1,0:T(8,128)(2,1)S(1)} %get-tuple-element.7.refs_1_), channel_id=1, source_target_pairs={{0,2},{2,4},{3,1},{4,6},{5,3},{7,5},{8,10},{10,12},{11,9},{12,14},... | collective-permute-start | bytes 1572872 | tf_op jit(solution)/shard_map/ppermute | solution.py:209
  28.8 32.0 %copy-start = (bf16[1024,4096]{1,0:T(8,128)(2,1)}, bf16[1024,4096]{1,0:T(8,128)(2,1)S(1)}, u32[]{:S(2)}) copy-start(bf16[1024,4096]{1,0:T(8,128)(2,1)S(1)} %normalise.1.refs_1_) | copy-start | bytes 25165828
  28.8 28.4 %copy-start.9 = (bf16[1,512,512]{2,1,0:T(8,128)(2,1)S(1)}, bf16[1,512,512]{2,1,0:T(8,128)(2,1)}, u32[]{:S(2)}) copy-start(bf16[1,512,512]{2,1,0:T(8,128)(2,1)} %param.12) | copy-start | bytes 1572868
  28.8 28.4 %copy-start.11 = (bf16[512,512]{1,0:T(8,128)(2,1)S(1)}, bf16[512,512]{1,0:T(8,128)(2,1)}, u32[]{:S(2)}) copy-start(bf16[512,512]{1,0:T(8,128)(2,1)} %copy-done.10) | copy-start | bytes 1572868
  29.4 1.6 collective-permute-start.3
  30.2 1.5 collective-permute-start.12
  30.9 12.0 %collective-permute-start.14 = (bf16[1024,256]{1,0:T(8,128)(2,1)S(1)}, bf16[1024,256]{1,0:T(8,128)(2,1)S(1)}, u32[]{:S(2)}, u32[]{:S(2)}) collective-permute-start(bf16[1024,256]{1,0:T(8,128)(2,1)S(1)} %fence.4.refs_2_), channel_id=1, source_target_pairs={{0,1},{1,0},{2,3},{3,2},{4,5},{5,4},{6,7},{7,6},{8,9},{9,8},{10,11... | collective-permute-start | bytes 1572872 | tf_op jit(solution)/shard_map/ppermute | solution.py:206
  31.0 12.3 %collective-permute-start.4 = (bf16[1024,256]{1,0:T(8,128)(2,1)S(1)}, bf16[1024,256]{1,0:T(8,128)(2,1)S(1)}, u32[]{:S(2)}, u32[]{:S(2)}) collective-permute-start(bf16[1024,256]{1,0:T(8,128)(2,1)S(1)} %collective-permute-done.3.refs_4_), channel_id=1, source_target_pairs={{3,1},{4,6},{11,9},{12,14},{19,17},{20,22},{27,25},{28,30}} | collective-permute-start | bytes 1572872 | tf_op jit(solution)/shard_map/ppermute | solution.py:209
  31.7 15.3 %collective-permute-start.13 = (bf16[1024,256]{1,0:T(8,128)(2,1)S(1)}, bf16[1024,256]{1,0:T(8,128)(2,1)S(1)}, u32[]{:S(2)}, u32[]{:S(2)}) collective-permute-start(bf16[1024,256]{1,0:T(8,128)(2,1)S(1)} %collective-permute-done.12.refs_5_), channel_id=1, source_target_pairs={{3,1},{4,6},{11,9},{12,14},{19,17},{20,22},{27,25},{28,30}} | collective-permute-start | bytes 1572872 | tf_op jit(solution)/shard_map/ppermute | solution.py:209
  33.3 24.5 %collective-permute-start.15 = (bf16[1024,256]{1,0:T(8,128)(2,1)S(1)}, bf16[1024,256]{1,0:T(8,128)(2,1)S(1)}, u32[]{:S(2)}, u32[]{:S(2)}) collective-permute-start(bf16[1024,256]{1,0:T(8,128)(2,1)S(1)} %collective-permute-done.11.refs_3_), channel_id=1, source_target_pairs={{0,1},{1,0},{2,3},{3,2},{4,5},{5,4},{6,7},{7,6},{8,9},{9,8},{10,11... | collective-permute-start | bytes 1572872 | tf_op jit(solution)/shard_map/ppermute | solution.py:206
  42.8 16.9 %collective-permute-start.16 = (bf16[1024,256]{1,0:T(8,128)(2,1)S(1)}, bf16[1024,256]{1,0:T(8,128)(2,1)S(1)}, u32[]{:S(2)}, u32[]{:S(2)}) collective-permute-start(bf16[1024,256]{1,0:T(8,128)(2,1)S(1)} %collective-permute-done.3.refs_4_), channel_id=1, source_target_pairs={{0,1},{1,0},{2,3},{3,2},{4,5},{5,4},{6,7},{7,6},{8,9},{9,8},{10,11... | collective-permute-start | bytes 1572872 | tf_op jit(solution)/shard_map/ppermute | solution.py:206
  42.9 16.8 %collective-permute-start.17 = (bf16[1024,256]{1,0:T(8,128)(2,1)S(1)}, bf16[1024,256]{1,0:T(8,128)(2,1)S(1)}, u32[]{:S(2)}, u32[]{:S(2)}) collective-permute-start(bf16[1024,256]{1,0:T(8,128)(2,1)S(1)} %collective-permute-done.12.refs_5_), channel_id=1, source_target_pairs={{0,1},{1,0},{2,3},{3,2},{4,5},{5,4},{6,7},{7,6},{8,9},{9,8},{10,11... | collective-permute-start | bytes 1572872 | tf_op jit(solution)/shard_map/ppermute | solution.py:206
  43.3 16.4 %collective-permute-start.18 = (bf16[1024,256]{1,0:T(8,128)(2,1)S(1)}, bf16[1024,256]{1,0:T(8,128)(2,1)S(1)}, u32[]{:S(2)}, u32[]{:S(2)}) collective-permute-start(bf16[1024,256]{1,0:T(8,128)(2,1)S(1)} %collective-permute-done.4.refs_3_.refs_6_), channel_id=1, source_target_pairs={{0,1},{1,0},{2,3},{3,2},{4,5},{5,4},{6,7},{7,6},{8,9},{9,8},{10,11... | collective-permute-start | bytes 1572872 | tf_op jit(solution)/shard_map/ppermute | solution.py:206
  47.0 12.7 %collective-permute-start.19 = (bf16[1024,256]{1,0:T(8,128)(2,1)S(1)}, bf16[1024,256]{1,0:T(8,128)(2,1)S(1)}, u32[]{:S(2)}, u32[]{:S(2)}) collective-permute-start(bf16[1024,256]{1,0:T(8,128)(2,1)S(1)} %collective-permute-done.13.refs_7_), channel_id=1, source_target_pairs={{0,1},{1,0},{2,3},{3,2},{4,5},{5,4},{6,7},{7,6},{8,9},{9,8},{10,11... | collective-permute-start | bytes 1572872 | tf_op jit(solution)/shard_map/ppermute | solution.py:206
  57.9 14.1 %collective-permute-start.5 = (bf16[1024,512]{1,0:T(8,128)(2,1)S(1)}, bf16[1024,512]{1,0:T(8,128)(2,1)S(1)}, u32[]{:S(2)}, u32[]{:S(2)}) collective-permute-start(bf16[1024,512]{1,0:T(8,128)(2,1)S(1)} %join_cores.3.refs_14_.refs_0_), channel_id=1, source_target_pairs={{0,2},{2,4},{3,1},{4,6},{5,3},{7,5},{8,10},{10,12},{11,9},{12,14},... | collective-permute-start | bytes 3145736 | tf_op jit(solution)/shard_map/ppermute | solution.py:209
  71.9 6.1 %collective-permute-start.6 = (bf16[1024,512]{1,0:T(8,128)(2,1)S(1)}, bf16[1024,512]{1,0:T(8,128)(2,1)S(1)}, u32[]{:S(2)}, u32[]{:S(2)}) collective-permute-start(bf16[1024,512]{1,0:T(8,128)(2,1)S(1)} %collective-permute-done.5.refs_2_.refs_1_), channel_id=1, source_target_pairs={{2,4},{3,1},{4,6},{5,3},{10,12},{11,9},{12,14},{13,11},{18,20},{19... | collective-permute-start | bytes 3145736 | tf_op jit(solution)/shard_map/ppermute | solution.py:209
  81.7 16.7 %collective-permute-start.23 = (bf16[512,1024]{1,0:T(8,128)(2,1)}, bf16[512,1024]{1,0:T(8,128)(2,1)}, u32[]{:S(2)}, u32[]{:S(2)}) collective-permute-start(bf16[512,1024]{1,0:T(8,128)(2,1)} %get-tuple-element.21), channel_id=1, source_target_pairs={{0,1},{1,0},{2,3},{3,2},{4,5},{5,4},{6,7},{7,6},{8,9},{9,8},{10,11... | collective-permute-start | bytes 3145736 | tf_op jit(solution)/shard_map/ppermute | solution.py:206
  97.0 25.1 %collective-permute-start.44 = (bf16[4096,128]{1,0:T(8,128)(2,1)S(1)}, bf16[4096,128]{1,0:T(8,128)(2,1)S(1)}, u32[]{:S(2)}, u32[]{:S(2)}) collective-permute-start(bf16[4096,128]{1,0:T(8,128)(2,1)S(1)} %add_convert_fusion), channel_id=1, source_target_pairs={{0,8},{8,0},{16,24},{24,16},{1,9},{9,1},{17,25},{25,17},{2,10},{10... | collective-permute-start | bytes 3145736 | tf_op jit(solution)/shard_map/ppermute | solution.py:271
  97.6 25.3 %collective-permute-start.22 = (bf16[512,1024]{1,0:T(8,128)(2,1)S(1)}, bf16[512,1024]{1,0:T(8,128)(2,1)S(1)}, u32[]{:S(2)}, u32[]{:S(2)}) collective-permute-start(bf16[512,1024]{1,0:T(8,128)(2,1)S(1)} %copy-done.13), channel_id=1, source_target_pairs={{0,1},{1,0},{2,3},{3,2},{4,5},{5,4},{6,7},{7,6},{8,9},{9,8},{10,11... | collective-permute-start | bytes 3145736 | tf_op jit(solution)/shard_map/ppermute | solution.py:206
  97.6 24.5 %collective-permute-start.7 = (bf16[1024,512]{1,0:T(8,128)(2,1)S(1)}, bf16[1024,512]{1,0:T(8,128)(2,1)S(1)}, u32[]{:S(2)}, u32[]{:S(2)}) collective-permute-start(bf16[1024,512]{1,0:T(8,128)(2,1)S(1)} %copy-done.6), channel_id=1, source_target_pairs={{3,1},{4,6},{11,9},{12,14},{19,17},{20,22},{27,25},{28,30}} | collective-permute-start | bytes 3145736 | tf_op jit(solution)/shard_map/ppermute | solution.py:209
  102.1 21.3 %collective-permute-start.24 = (bf16[512,1024]{1,0:T(8,128)(2,1)S(1)}, bf16[512,1024]{1,0:T(8,128)(2,1)S(1)}, u32[]{:S(2)}, u32[]{:S(2)}) collective-permute-start(bf16[512,1024]{1,0:T(8,128)(2,1)S(1)} %get-tuple-element.18), channel_id=1, source_target_pairs={{0,2},{7,5},{8,10},{15,13},{16,18},{23,21},{24,26},{31,29}} | collective-permute-start | bytes 3145736 | tf_op jit(solution)/shard_map/ppermute | solution.py:209
  108.9 15.2 %collective-permute-start.8 = (bf16[1024,512]{1,0:T(8,128)(2,1)S(1)}, bf16[1024,512]{1,0:T(8,128)(2,1)S(1)}, u32[]{:S(2)}, u32[]{:S(2)}) collective-permute-start(bf16[1024,512]{1,0:T(8,128)(2,1)S(1)} %copy-done.4), channel_id=1, source_target_pairs={{0,1},{1,0},{2,3},{3,2},{4,5},{5,4},{6,7},{7,6},{8,9},{9,8},{10,11... | collective-permute-start | bytes 3145736 | tf_op jit(solution)/shard_map/ppermute | solution.py:206
  122.2 7.4 %collective-permute-start.9 = (bf16[1024,512]{1,0:T(8,128)(2,1)S(1)}, bf16[1024,512]{1,0:T(8,128)(2,1)S(1)}, u32[]{:S(2)}, u32[]{:S(2)}) collective-permute-start(bf16[1024,512]{1,0:T(8,128)(2,1)S(1)} %copy-done.6), channel_id=1, source_target_pairs={{0,1},{1,0},{2,3},{3,2},{4,5},{5,4},{6,7},{7,6},{8,9},{9,8},{10,11... | collective-permute-start | bytes 3145736 | tf_op jit(solution)/shard_map/ppermute | solution.py:206
  122.2 7.4 %collective-permute-start.10 = (bf16[1024,512]{1,0:T(8,128)(2,1)S(1)}, bf16[1024,512]{1,0:T(8,128)(2,1)S(1)}, u32[]{:S(2)}, u32[]{:S(2)}) collective-permute-start(bf16[1024,512]{1,0:T(8,128)(2,1)S(1)} %collective-permute-done.7.refs_3_), channel_id=1, source_target_pairs={{0,1},{1,0},{2,3},{3,2},{4,5},{5,4},{6,7},{7,6},{8,9},{9,8},{10,11... | collective-permute-start | bytes 3145736 | tf_op jit(solution)/shard_map/ppermute | solution.py:206
  122.9 27.7 %collective-permute-start.43 = (bf16[4096,128]{1,0:T(8,128)(2,1)S(1)}, bf16[4096,128]{1,0:T(8,128)(2,1)S(1)}, u32[]{:S(2)}, u32[]{:S(2)}) collective-permute-start(bf16[4096,128]{1,0:T(8,128)(2,1)S(1)} %add_convert_fusion.1), channel_id=1, source_target_pairs={{0,16},{8,24},{16,0},{24,8},{1,17},{9,25},{17,1},{25,9},{2,18},{10... | collective-permute-start | bytes 3145736 | tf_op jit(solution)/shard_map/ppermute | solution.py:271
  123.5 14.5 %collective-permute-start.25 = (bf16[512,1024]{1,0:T(8,128)(2,1)S(1)}, bf16[512,1024]{1,0:T(8,128)(2,1)S(1)}, u32[]{:S(2)}, u32[]{:S(2)}) collective-permute-start(bf16[512,1024]{1,0:T(8,128)(2,1)S(1)} %get-tuple-element.19), channel_id=1, source_target_pairs={{0,1},{1,0},{2,3},{3,2},{4,5},{5,4},{6,7},{7,6},{8,9},{9,8},{10,11... | collective-permute-start | bytes 3145736 | tf_op jit(solution)/shard_map/ppermute | solution.py:206
  124.1 17.6 %collective-permute-start.26 = (bf16[512,1024]{1,0:T(8,128)(2,1)S(1)}, bf16[512,1024]{1,0:T(8,128)(2,1)S(1)}, u32[]{:S(2)}, u32[]{:S(2)}) collective-permute-start(bf16[512,1024]{1,0:T(8,128)(2,1)S(1)} %add_convert_fusion.3.refs_8_), channel_id=1, source_target_pairs={{0,2},{2,4},{5,3},{7,5},{8,10},{10,12},{13,11},{15,13},{16,18},{18... | collective-permute-start | bytes 3145736 | tf_op jit(solution)/shard_map/ppermute | solution.py:209
  147.5 9.2 %collective-permute-start.36 = (bf16[256,1024]{1,0:T(8,128)(2,1)S(1)}, bf16[256,1024]{1,0:T(8,128)(2,1)S(1)}, u32[]{:S(2)}, u32[]{:S(2)}) collective-permute-start(bf16[256,1024]{1,0:T(8,128)(2,1)S(1)} %get-tuple-element.25), channel_id=1, source_target_pairs={{0,1},{1,0},{2,3},{3,2},{4,5},{5,4},{6,7},{7,6},{8,9},{9,8},{10,11... | collective-permute-start | bytes 1572872 | tf_op jit(solution)/shard_map/ppermute | solution.py:206
  150.0 12.6 %collective-permute-start.29 = (bf16[256,1024]{1,0:T(8,128)(2,1)S(1)}, bf16[256,1024]{1,0:T(8,128)(2,1)S(1)}, u32[]{:S(2)}, u32[]{:S(2)}) collective-permute-start(bf16[256,1024]{1,0:T(8,128)(2,1)S(1)} %get-tuple-element.23), channel_id=1, source_target_pairs={{0,1},{1,0},{2,3},{3,2},{4,5},{5,4},{6,7},{7,6},{8,9},{9,8},{10,11... | collective-permute-start | bytes 1572872 | tf_op jit(solution)/shard_map/ppermute | solution.py:206
  150.8 33.9 %collective-permute-start.41 = (bf16[512,1024]{1,0:T(8,128)(2,1)S(1)}, bf16[512,1024]{1,0:T(8,128)(2,1)}, u32[]{:S(2)}, u32[]{:S(2)}) collective-permute-start(bf16[512,1024]{1,0:T(8,128)(2,1)S(1)} %add_convert_fusion.2.refs_2_), channel_id=1, source_target_pairs={{0,2},{2,4},{3,1},{4,6},{5,3},{7,5},{8,10},{10,12},{11,9},{12,14},... | collective-permute-start | bytes 3145736 | tf_op jit(solution)/shard_map/ppermute | solution.py:209
  156.2 15.8 %collective-permute-start.35 = (bf16[256,1024]{1,0:T(8,128)(2,1)}, bf16[256,1024]{1,0:T(8,128)(2,1)}, u32[]{:S(2)}, u32[]{:S(2)}) collective-permute-start(bf16[256,1024]{1,0:T(8,128)(2,1)} %get-tuple-element.24), channel_id=1, source_target_pairs={{0,1},{1,0},{2,3},{3,2},{4,5},{5,4},{6,7},{7,6},{8,9},{9,8},{10,11... | collective-permute-start | bytes 1572872 | tf_op jit(solution)/shard_map/ppermute | solution.py:206
  156.2 18.7 %collective-permute-start.28 = (bf16[256,1024]{1,0:T(8,128)(2,1)S(1)}, bf16[256,1024]{1,0:T(8,128)(2,1)}, u32[]{:S(2)}, u32[]{:S(2)}) collective-permute-start(bf16[256,1024]{1,0:T(8,128)(2,1)S(1)} %get-tuple-element.22), channel_id=1, source_target_pairs={{0,1},{1,0},{2,3},{3,2},{4,5},{5,4},{6,7},{7,6},{8,9},{9,8},{10,11... | collective-permute-start | bytes 1572872 | tf_op jit(solution)/shard_map/ppermute | solution.py:206
  158.2 15.0 %collective-permute-start.37 = (bf16[256,1024]{1,0:T(8,128)(2,1)}, bf16[256,1024]{1,0:T(8,128)(2,1)}, u32[]{:S(2)}, u32[]{:S(2)}) collective-permute-start(bf16[256,1024]{1,0:T(8,128)(2,1)} %get-tuple-element.16), channel_id=1, source_target_pairs={{0,2},{7,5},{8,10},{15,13},{16,18},{23,21},{24,26},{31,29}} | collective-permute-start | bytes 1572872 | tf_op jit(solution)/shard_map/ppermute | solution.py:209
  164.1 15.2 %collective-permute-start.30 = (bf16[256,1024]{1,0:T(8,128)(2,1)}, bf16[256,1024]{1,0:T(8,128)(2,1)}, u32[]{:S(2)}, u32[]{:S(2)}) collective-permute-start(bf16[256,1024]{1,0:T(8,128)(2,1)} %get-tuple-element.14), channel_id=1, source_target_pairs={{0,2},{7,5},{8,10},{15,13},{16,18},{23,21},{24,26},{31,29}} | collective-permute-start | bytes 1572872 | tf_op jit(solution)/shard_map/ppermute | solution.py:209
  172.0 14.4 %collective-permute-start.34 = (bf16[256,1024]{1,0:T(8,128)(2,1)}, bf16[256,1024]{1,0:T(8,128)(2,1)S(1)}, u32[]{:S(2)}, u32[]{:S(2)}) collective-permute-start(bf16[256,1024]{1,0:T(8,128)(2,1)} %get-tuple-element.17), channel_id=1, source_target_pairs={{0,1},{1,0},{2,3},{3,2},{4,5},{5,4},{6,7},{7,6},{8,9},{9,8},{10,11... | collective-permute-start | bytes 1572872 | tf_op jit(solution)/shard_map/ppermute | solution.py:206
  173.2 17.4 %collective-permute-start.27 = (bf16[256,1024]{1,0:T(8,128)(2,1)}, bf16[256,1024]{1,0:T(8,128)(2,1)S(1)}, u32[]{:S(2)}, u32[]{:S(2)}) collective-permute-start(bf16[256,1024]{1,0:T(8,128)(2,1)} %get-tuple-element.15), channel_id=1, source_target_pairs={{0,1},{1,0},{2,3},{3,2},{4,5},{5,4},{6,7},{7,6},{8,9},{9,8},{10,11... | collective-permute-start | bytes 1572872 | tf_op jit(solution)/shard_map/ppermute | solution.py:206
  174.9 11.5 %collective-permute-start.38 = (bf16[256,1024]{1,0:T(8,128)(2,1)S(1)}, bf16[256,1024]{1,0:T(8,128)(2,1)S(1)}, u32[]{:S(2)}, u32[]{:S(2)}) collective-permute-start(bf16[256,1024]{1,0:T(8,128)(2,1)S(1)} %add_convert_fusion.6), channel_id=1, source_target_pairs={{0,2},{2,4},{5,3},{7,5},{8,10},{10,12},{13,11},{15,13},{16,18},{18... | collective-permute-start | bytes 1572872 | tf_op jit(solution)/shard_map/ppermute | solution.py:209
  180.8 10.8 %collective-permute-start.31 = (bf16[256,1024]{1,0:T(8,128)(2,1)S(1)}, bf16[256,1024]{1,0:T(8,128)(2,1)S(1)}, u32[]{:S(2)}, u32[]{:S(2)}) collective-permute-start(bf16[256,1024]{1,0:T(8,128)(2,1)S(1)} %add_convert_fusion.9), channel_id=1, source_target_pairs={{0,2},{2,4},{5,3},{7,5},{8,10},{10,12},{13,11},{15,13},{16,18},{18... | collective-permute-start | bytes 1572872 | tf_op jit(solution)/shard_map/ppermute | solution.py:209
  186.6 10.6 %collective-permute-start.39 = (bf16[256,1024]{1,0:T(8,128)(2,1)S(1)}, bf16[256,1024]{1,0:T(8,128)(2,1)S(1)}, u32[]{:S(2)}, u32[]{:S(2)}) collective-permute-start(bf16[256,1024]{1,0:T(8,128)(2,1)S(1)} %add_convert_fusion.5), channel_id=1, source_target_pairs={{0,2},{2,4},{3,1},{4,6},{5,3},{7,5},{8,10},{10,12},{11,9},{12,14},... | collective-permute-start | bytes 1572872 | tf_op jit(solution)/shard_map/ppermute | solution.py:209
  191.8 11.1 %collective-permute-start.32 = (bf16[256,1024]{1,0:T(8,128)(2,1)S(1)}, bf16[256,1024]{1,0:T(8,128)(2,1)S(1)}, u32[]{:S(2)}, u32[]{:S(2)}) collective-permute-start(bf16[256,1024]{1,0:T(8,128)(2,1)S(1)} %add_convert_fusion.8), channel_id=1, source_target_pairs={{0,2},{2,4},{3,1},{4,6},{5,3},{7,5},{8,10},{10,12},{11,9},{12,14},... | collective-permute-start | bytes 1572872 | tf_op jit(solution)/shard_map/ppermute | solution.py:209
  196.4 7.5 %collective-permute-start.42 = (bf16[512,512]{1,0:T(8,128)(2,1)S(1)}, bf16[512,512]{1,0:T(8,128)(2,1)S(1)}, u32[]{:S(2)}, u32[]{:S(2)}) collective-permute-start(bf16[512,512]{1,0:T(8,128)(2,1)S(1)} %select_convert_fusion), channel_id=1, source_target_pairs={{0,1},{1,0},{2,3},{3,2},{4,5},{5,4},{6,7},{7,6},{8,9},{9,8},{10,11... | collective-permute-start | bytes 1572872 | tf_op jit(solution)/shard_map/ppermute | solution.py:206
  198.2 7.2 %collective-permute-start.40 = (bf16[256,512]{1,0:T(8,128)(2,1)}, bf16[256,512]{1,0:T(8,128)(2,1)S(1)}, u32[]{:S(2)}, u32[]{:S(2)}) collective-permute-start(bf16[256,512]{1,0:T(8,128)(2,1)} %select_convert_fusion.1), channel_id=1, source_target_pairs={{0,1},{1,0},{2,3},{3,2},{4,5},{5,4},{6,7},{7,6},{8,9},{9,8},{10,11... | collective-permute-start | bytes 786440 | tf_op jit(solution)/shard_map/ppermute | solution.py:206
  203.8 1.9 collective-permute-start.33
  (16 other events, 129.5 us)

commit v6 on v5

--- a/solution.py
+++ b/solution.py
@@ -193,10 +193,10 @@
     chips = devices // 2
     me = lax.axis_index("fsdp")
     chip, core = me // 2, me % 2
-    position = jnp.where(core == 0, chip, chips - 1 - chip)
-    steps = jnp.arange(chips, dtype=jnp.int32)
-    behind = jnp.where(core == 0, chip - steps + chips, chip + steps) % chips
-    order = Order(jnp.concatenate([behind, position[None], core[None]]).astype(jnp.int32))
+    position = chip + core * (chips - 1 - 2 * chip)
+    way = 1 - 2 * core
+    behind = [(chip - way * s + chips) % chips for s in range(chips)]
+    order = Order(jnp.stack([*behind, position, core]).astype(jnp.int32))
     shard = value_weight.shape[1]
     block = 2 * shard
     cotangent = out_cotangent[0]
@@ -256,6 +256,9 @@
     first_own, second_own = value_weight[0], output_weight[0]
     first_partner, second_partner = swap(first_own), swap(second_own)
 
+    joined = join_cores(order, first_own, first_partner, HALVES, (second_partner,))
+    normed = normalise(order, tokens[0], norm_gain, ())
+    exponents = fence(order, delta_exponents)[0]
     bits = replicas.bit_length() - 1
     if replicas != 1 << bits or bits < 1:
         raise ValueError("replicas")
@@ -263,7 +266,7 @@
     sums, early = [], []
     for index in range(2):
         rows = slice(index * rows_half, (index + 1) * rows_half)
-        scale = jnp.exp2(delta_exponents[0, rows].astype(f32))[:, None]
+        scale = jnp.exp2(exponents[0, rows].astype(f32))[:, None]
         total = delta_values[0, rows].astype(f32) * scale
         for turn in range(bits):
             mine = total.astype(bf16)
@@ -271,11 +274,8 @@
             theirs = lax.ppermute(mine, "replica", [(i, i ^ bit) for i in range(replicas)])
             if turn == 0:
                 early.append(theirs)
-            total = lax.optimization_barrier(mine).astype(f32) + theirs.astype(f32)
-        sums.append(total)
-
-    joined = join_cores(order, first_own, first_partner, HALVES, (second_partner,))
-    normed = normalise(order, tokens[0], norm_gain, ())
+            total = mine.astype(f32) + theirs.astype(f32)
+        sums.append((mine, theirs))
     pieces, others = gather(joined, at_first=True)
     last = pieces[-1]
 
@@ -293,11 +293,13 @@
     half = mid.shape[1] // HALVES
     second = [Gradient(mid[:, j * half : (j + 1) * half], normed) for j in range(HALVES)]
     for step in range(1, chips):
-        for gradient in second:
-            gradient.reduce(step)
+        sent = tuple(gradient.reduce(step) for gradient in second)
+        if step == 1:
+            theirs = fence(order, *(pair[1] for pair in sums), after=sent)
     output_grad = first.finish()
 
-    delta = jnp.concatenate(sums) * (1.0 / replicas)
+    total = [a.astype(f32) + b.astype(f32) for (a, _), b in zip(sums, theirs)]
+    delta = jnp.concatenate(total) * (1.0 / replicas)
     new_base, new_momentum = nesterov(delta, base_params, outer_momentum)
     value_grad = jnp.concatenate([gradient.finish() for gradient in second], axis=1)
     return (value_grad[None], output_grad[None], new_base, new_momentum)

time: 209 us -> 210 us (level)
  local copies, waits for them, and re-layouts: 8.08 us -> 24.4 us
  starting transfers between devices: 91.7 us -> 78.7 us
  waiting for transfers between devices: 32.4 us -> 38.5 us
  between operations: 7.21 us -> 1.56 us
  matrix products: 21.5 us -> 18.7 us
  other arithmetic: 35.7 us -> 33.4 us
    unnamed x40 -> x95, local copies, waits for them, and re-layouts: 7.43 us -> 24.3 us
    ppermute x23, starting transfers between devices: 33.6 us -> 20 us  [swap(): return lax.ppermute(value, 'fsdp', [(i, i ^ 1) for i in range(devices)])]
    ppermute x23, waiting for transfers between devices: 0.18 us -> 5.76 us  [swap(): return lax.ppermute(value, 'fsdp', [(i, i ^ 1) for i in range(devices)])]
    ppermute x18, waiting for transfers between devices: 18.2 us -> 21.7 us  [move(): return lax.ppermute(value, 'fsdp', move_perm(chips, active))]
    convert_element_type x3, other arithmetic: 7.91 us -> 4.67 us  [per_device(): mine = total.astype(bf16)]
    ppermute x4, waiting for transfers between devices: 14.1 us -> 11.1 us  [per_device(): lax.ppermute(mine, 'replica', [(i, i ^ bit) for i in range(replicas)])]
    dot_general x1, matrix products: 7.42 us -> 4.48 us  [per_device(): mid = jnp.dot(cotangent, weight, preferred_element_type=f32).astype(bf16)]
    add x2 -> x1, other arithmetic: 0.41 us -> 2.73 us  [per_device(): total = [a.astype(f32) + b.astype(f32) for (a, _), b in zip(sums, theirs)]]
  transfers between devices with their start and end apart: 45 -> 45, of which waited for: 9 -> 13; matrix products, arithmetic and copies ran while one was open for 27% -> 24% of each run, Pallas kernels for 5% -> 6%
where the time goes in v6:
time: 210 us; the launch traced here: 209 us
  starting transfers between devices  78.7 us (37%)
  waiting for transfers between devices  38.5 us (18%)
  other arithmetic  33.4 us (16%)
  local copies, waits for them, and re-layouts  24.4 us (12%)
  matrix products  18.7 us (9%)
  Pallas kernels  13.5 us (6%)
    ppermute x18, starting transfers between devices, move(): return lax.ppermute(value, 'fsdp', move_perm(chips, active))  54.6 us
    unnamed x95, local copies, waits for them, and re-layouts  24.3 us
    ppermute x18, waiting for transfers between devices, move(): return lax.ppermute(value, 'fsdp', move_perm(chips, active))  21.7 us
    ppermute x23, starting transfers between devices, swap(): return lax.ppermute(value, 'fsdp', [(i, i ^ 1) for i in range(devices)])  20 us
    convert_element_type x9, other arithmetic, message(): return term.astype(bf16)  14.5 us
    pallas_call x11, Pallas kernels, __call__(): pl.pallas_call(ordered, grid_spec=pltpu.PrefetchScalarGridSpec(num_scalar...  13.5 us
    ppermute x4, waiting for transfers between devices, per_device(): lax.ppermute(mine, 'replica', [(i, i ^ bit) for i in range(replicas)])  11.1 us
    dot_general x3, matrix products, __init__(): lax.dot_general(mid, x, (((0,), (0,)), ((), ())), preferred_element_type=...  9.74 us
  transfers between devices with their start and end apart: 45, of which 13 were waited for; matrix products, arithmetic and copies ran while one was open for 24% of the time, Pallas kernels for 6%

profile of v6, /device:TPU:0, one launch (start us, length us, event | category | flops | bytes accessed | tf_op | source)
XLA Modules:
  0.0 208.7 jit_solution(14489700501351927535)
XLA Ops:
  2.0 1.6 collective-permute-done.refs_2_.refs_1_
  6.1 4.9 %collective-permute-start.2 = (bf16[1024,256]{1,0:T(8,128)(2,1)S(1)}, bf16[1024,256]{1,0:T(8,128)(2,1)S(1)}, u32[]{:S(2)}, u32[]{:S(2)}) collective-permute-start(bf16[1024,256]{1,0:T(8,128)(2,1)S(1)} %get-tuple-element.8.refs_2_.refs_0_), channel_id=1, source_target_pairs={{0,2},{2,4},{3,1},{4,6},{5,3},{7,5},{8,10},{10,12},{11,9},{12,14},... | collective-permute-start | bytes 1572872 | tf_op jit(solution)/shard_map/ppermute | solution.py:209
  11.0 3.4 %copy-done.17 = bf16[1,1024,4096]{2,1,0:T(8,128)(2,1)S(1)} copy-done((bf16[1,1024,4096]{2,1,0:T(8,128)(2,1)S(1)}, bf16[1,1024,4096]{2,1,0:T(8,128)(2,1)}, u32[]{:S(2)}) %copy-start.17) | copy-done | bytes 8388632
  14.4 5.4 %normalise.1.refs_1_ = bf16[1024,4096]{1,0:T(8,128)(2,1)S(1)} custom-call(s32[6]{0:T(128)S(1)} %stack.27.place_ref, bf16[1024,4096]{1,0:T(8,128)(2,1)S(1)} %bitcast.51, f32[1,4096]{1,0:T(1,128)S(1)} %bitcast.56, bf16[1024,256]{1,0:T(8,128)(2,1)S(1)} %get-tuple-element.8.refs_2_.refs_0_), custom_call_target="tpu_custom_call" | custom-call | flops 20000000000 | bytes 1 | tf_op jit(solution)/shard_map/normalise/pallas_call | solution.py:39
  20.3 3.0 %copy-done = bf16[1024,4096]{1,0:T(8,128)(2,1)} copy-done((bf16[1024,4096]{1,0:T(8,128)(2,1)}, bf16[1024,4096]{1,0:T(8,128)(2,1)S(1)}, u32[]{:S(2)}) %copy-start) | copy-done | bytes 8388632
  23.4 4.3 %collective-permute-start.11 = (bf16[1024,256]{1,0:T(8,128)(2,1)S(1)}, bf16[1024,256]{1,0:T(8,128)(2,1)}, u32[]{:S(2)}, u32[]{:S(2)}) collective-permute-start(bf16[1024,256]{1,0:T(8,128)(2,1)S(1)} %get-tuple-element.9.refs_1_), channel_id=1, source_target_pairs={{0,2},{2,4},{3,1},{4,6},{5,3},{7,5},{8,10},{10,12},{11,9},{12,14},... | collective-permute-start | bytes 1572872 | tf_op jit(solution)/shard_map/ppermute | solution.py:209
  27.6 2.1 %fusion.7 = (bf16[4096,128]{1,0:T(8,128)(2,1)S(1)}, bf16[4096,128]{1,0:T(8,128)(2,1)S(1)}) fusion(f32[4096]{0:T(1024)S(1)} %bitcast.57, bf16[1,8192,128]{2,1,0:T(8,128)(2,1)S(1)} %copy-done.33, f32[4096]{0:T(1024)S(1)} %bitcast.58), kind=kLoop, calls=%fused_computation.11 | loop fusion | flops 3145728 | bytes 4227072 | tf_op jit(solution)/shard_map/convert_element_type | solution.py:272
  29.8 1.6 collective-permute-start.20
  31.4 1.5 collective-permute-start.21
  33.4 1.5 collective-permute-start.3
  34.9 1.5 collective-permute-start.12
  37.2 1.4 collective-permute-start.4
  38.6 1.5 collective-permute-start.13
  40.1 9.6 %collective-permute-done.20.refs_15_ = bf16[4096,128]{1,0:T(8,128)(2,1)S(1)} collective-permute-done((bf16[4096,128]{1,0:T(8,128)(2,1)S(1)}, bf16[4096,128]{1,0:T(8,128)(2,1)S(1)}, u32[]{:S(2)}, u32[]{:S(2)}) %collective-permute-start.20) | collective-permute-done | bytes 1048608 | tf_op jit(solution)/shard_map/ppermute | solution.py:274
  49.7 1.5 collective-permute-done.21.refs_16_
  52.5 3.5 %collective-permute-start.19 = (bf16[1024,256]{1,0:T(8,128)(2,1)}, bf16[1024,256]{1,0:T(8,128)(2,1)}, u32[]{:S(2)}, u32[]{:S(2)}) collective-permute-start(bf16[1024,256]{1,0:T(8,128)(2,1)} %collective-permute-done.13.refs_7_), channel_id=1, source_target_pairs={{0,1},{1,0},{2,3},{3,2},{4,5},{5,4},{6,7},{7,6},{8,9},{9,8},{10,11... | collective-permute-start | bytes 1572872 | tf_op jit(solution)/shard_map/ppermute | solution.py:206
  59.8 2.3 %collective-permute-start.5 = (bf16[1024,512]{1,0:T(8,128)(2,1)S(1)}, bf16[1024,512]{1,0:T(8,128)(2,1)S(1)}, u32[]{:S(2)}, u32[]{:S(2)}) collective-permute-start(bf16[1024,512]{1,0:T(8,128)(2,1)S(1)} %join_cores.3.refs_14_.refs_0_), channel_id=1, source_target_pairs={{0,2},{2,4},{3,1},{4,6},{5,3},{7,5},{8,10},{10,12},{11,9},{12,14},... | collective-permute-start | bytes 3145736 | tf_op jit(solution)/shard_map/ppermute | solution.py:209
  66.4 2.7 %assemble.2.refs_1_ = bf16[4096,512]{1,0:T(8,128)(2,1)S(1)} custom-call(s32[6]{0:T(128)S(1)} %stack.27.place_ref, bf16[1024,256]{1,0:T(8,128)(2,1)S(1)} %copy-done.9, bf16[1024,256]{1,0:T(8,128)(2,1)S(1)} %copy-done.11, bf16[1024,256]{1,0:T(8,128)(2,1)S(1)} %copy-done.16, bf16[1024,256]{1,0:T(8,128)(2,1)} %collective-permute-done.11.refs_3_, ...), custom_call_target="tpu_custom_call" | custom-call | flops 2400000000 | bytes 1 | tf_op jit(solution)/shard_map/assemble/pallas_call | solution.py:39
  69.1 4.5 %convolution_convert_fusion.2.refs_0_ = bf16[1024,512]{1,0:T(8,128)(2,1)S(1)} fusion(bf16[1024,4096]{1,0:T(8,128)(2,1)S(1)} %bitcast.48, bf16[4096,512]{1,0:T(8,128)(2,1)S(1)} %assemble.2.refs_1_), kind=kOutput, calls=%fused_computation.23 | convolution fusion | flops 4295491584 | bytes 13631488 | tf_op jit(solution)/shard_map/dot_general | solution.py:284
  75.7 5.0 %fusion.4.refs_0_ = bf16[512,4096]{1,0:T(8,128)(2,1)S(1)} fusion(bf16[1024,512]{1,0:T(8,128)(2,1)S(1)} %fence.8.refs_1_, bf16[1,1024,4096]{2,1,0:T(8,128)(2,1)S(1)} %bitcast.60), kind=kOutput, calls=%fused_computation.4 | convolution fusion | flops 4297064448 | bytes 13631488 | tf_op jit(solution)/shard_map/dot_general | solution.py:213
  81.6 1.7 select_select_fusion.2
  84.3 11.6 %collective-permute-start.23 = (bf16[512,1024]{1,0:T(8,128)(2,1)}, bf16[512,1024]{1,0:T(8,128)(2,1)}, u32[]{:S(2)}, u32[]{:S(2)}) collective-permute-start(bf16[512,1024]{1,0:T(8,128)(2,1)} %get-tuple-element.25), channel_id=1, source_target_pairs={{0,1},{1,0},{2,3},{3,2},{4,5},{5,4},{6,7},{7,6},{8,9},{9,8},{10,11... | collective-permute-start | bytes 3145736 | tf_op jit(solution)/shard_map/ppermute | solution.py:206
  96.8 3.2 %collective-permute-done.23 = bf16[512,1024]{1,0:T(8,128)(2,1)} collective-permute-done((bf16[512,1024]{1,0:T(8,128)(2,1)}, bf16[512,1024]{1,0:T(8,128)(2,1)}, u32[]{:S(2)}, u32[]{:S(2)}) %collective-permute-start.23) | collective-permute-done | bytes 1048608 | tf_op jit(solution)/shard_map/ppermute | solution.py:206
  100.0 3.7 %add_convert_fusion.4 = (bf16[512,1024]{1,0:T(8,128)(2,1)S(1)}, bf16[512,1024]{1,0:T(8,128)(2,1)S(1)}) fusion(bf16[512,1024]{1,0:T(8,128)(2,1)} %collective-permute-done.23, bf16[512,4096]{1,0:T(8,128)(2,1)} %copy-done.1, pred[]{:T(512)S(6)} %eq.39, pred[]{:T(512)S(6)} %eq.38, pred[]{:T(512)S(6)} %eq.37), kind=kLoop, calls=%fused_computation.21 | loop fusion | flops 3670016 | bytes 7340035 | tf_op jit(solution)/shard_map/convert_element_type | solution.py:231
  103.8 5.4 %collective-permute-start.24 = (bf16[512,1024]{1,0:T(8,128)(2,1)S(1)}, bf16[512,1024]{1,0:T(8,128)(2,1)S(1)}, u32[]{:S(2)}, u32[]{:S(2)}) collective-permute-start(bf16[512,1024]{1,0:T(8,128)(2,1)S(1)} %get-tuple-element.22), channel_id=1, source_target_pairs={{0,2},{7,5},{8,10},{15,13},{16,18},{23,21},{24,26},{31,29}} | collective-permute-start | bytes 3145736 | tf_op jit(solution)/shard_map/ppermute | solution.py:209
  111.0 1.6 collective-permute-start.10
  114.4 6.9 %collective-permute-done.24 = bf16[512,1024]{1,0:T(8,128)(2,1)S(1)} collective-permute-done((bf16[512,1024]{1,0:T(8,128)(2,1)S(1)}, bf16[512,1024]{1,0:T(8,128)(2,1)S(1)}, u32[]{:S(2)}, u32[]{:S(2)}) %collective-permute-start.24) | collective-permute-done | bytes 1048608 | tf_op jit(solution)/shard_map/ppermute | solution.py:209
  122.6 4.7 %collective-permute-start.26 = (bf16[512,1024]{1,0:T(8,128)(2,1)S(1)}, bf16[512,1024]{1,0:T(8,128)(2,1)S(1)}, u32[]{:S(2)}, u32[]{:S(2)}) collective-permute-start(bf16[512,1024]{1,0:T(8,128)(2,1)S(1)} %add_convert_fusion.3.refs_8_), channel_id=1, source_target_pairs={{0,2},{2,4},{5,3},{7,5},{8,10},{10,12},{13,11},{15,13},{16,18},{18... | collective-permute-start | bytes 3145736 | tf_op jit(solution)/shard_map/ppermute | solution.py:209
  128.3 4.5 %fusion.12.refs_0_ = bf16[1024,512]{1,0:T(8,128)(2,1)S(1)} fusion(bf16[4096,512]{1,0:T(8,128)(2,1)S(1)} %assemble.3.refs_1_, bf16[1,1024,4096]{2,1,0:T(8,128)(2,1)S(1)} %bitcast.62), kind=kOutput, calls=%fused_computation.24 | convolution fusion | flops 4295491584 | bytes 13631488 | tf_op jit(solution)/shard_map/dot_general | solution.py:291
  132.8 6.8 %collective-permute-done.26 = bf16[512,1024]{1,0:T(8,128)(2,1)S(1)} collective-permute-done((bf16[512,1024]{1,0:T(8,128)(2,1)S(1)}, bf16[512,1024]{1,0:T(8,128)(2,1)S(1)}, u32[]{:S(2)}, u32[]{:S(2)}) %collective-permute-start.26) | collective-permute-done | bytes 1048608 | tf_op jit(solution)/shard_map/ppermute | solution.py:209
  139.5 1.8 add_convert_fusion.2.refs_2_
  142.0 2.4 %convolution_convert_fusion.1 = bf16[256,4096]{1,0:T(8,128)(2,1)S(1)} fusion(bf16[1024,4096]{1,0:T(8,128)(2,1)S(1)} %bitcast.50, bf16[1024,512]{1,0:T(8,128)(2,1)S(1)} %fence.10.refs_2_), kind=kOutput, calls=%fused_computation.6 | convolution fusion | flops 2148532224 | bytes 11010048 | tf_op jit(solution)/shard_map/dot_general | solution.py:213
  145.9 2.4 %convolution_convert_fusion = bf16[256,4096]{1,0:T(8,128)(2,1)S(1)} fusion(bf16[1024,4096]{1,0:T(8,128)(2,1)S(1)} %bitcast.50, bf16[1024,512]{1,0:T(8,128)(2,1)S(1)} %fence.10.refs_2_), kind=kOutput, calls=%fused_computation.5 | convolution fusion | flops 2148532224 | bytes 11010048 | tf_op jit(solution)/shard_map/dot_general | solution.py:213
  148.3 1.3 copy-done.23
  151.0 4.7 %collective-permute-start.41 = (bf16[512,1024]{1,0:T(8,128)(2,1)S(1)}, bf16[512,1024]{1,0:T(8,128)(2,1)S(1)}, u32[]{:S(2)}, u32[]{:S(2)}) collective-permute-start(bf16[512,1024]{1,0:T(8,128)(2,1)S(1)} %add_convert_fusion.2.refs_2_), channel_id=1, source_target_pairs={{0,2},{2,4},{3,1},{4,6},{5,3},{7,5},{8,10},{10,12},{11,9},{12,14},... | collective-permute-start | bytes 3145736 | tf_op jit(solution)/shard_map/ppermute | solution.py:209
  155.8 3.0 %add_convert_fusion.10 = (bf16[256,1024]{1,0:T(8,128)(2,1)S(1)}, bf16[256,1024]{1,0:T(8,128)(2,1)}) fusion(bf16[256,1024]{1,0:T(8,128)(2,1)} %collective-permute-done.29, bf16[256,4096]{1,0:T(8,128)(2,1)} %copy-done.25, pred[]{:T(512)S(6)} %eq.39, pred[]{:T(512)S(6)} %eq.38, pred[]{:T(512)S(6)} %eq.37), kind=kLoop, calls=%fused_computation.35 | loop fusion | flops 1835008 | bytes 3670019 | tf_op jit(solution)/shard_map/convert_element_type | solution.py:231
  159.3 1.6 add_convert_fusion.7
  160.9 4.1 %collective-permute-start.30 = (bf16[256,1024]{1,0:T(8,128)(2,1)S(1)}, bf16[256,1024]{1,0:T(8,128)(2,1)}, u32[]{:S(2)}, u32[]{:S(2)}) collective-permute-start(bf16[256,1024]{1,0:T(8,128)(2,1)S(1)} %get-tuple-element.18.refs_3_), channel_id=1, source_target_pairs={{0,2},{7,5},{8,10},{15,13},{16,18},{23,21},{24,26},{31,29}} | collective-permute-start | bytes 1572872 | tf_op jit(solution)/shard_map/ppermute | solution.py:209
  165.0 2.1 %collective-permute-start.37 = (bf16[256,1024]{1,0:T(8,128)(2,1)S(1)}, bf16[256,1024]{1,0:T(8,128)(2,1)}, u32[]{:S(2)}, u32[]{:S(2)}) collective-permute-start(bf16[256,1024]{1,0:T(8,128)(2,1)S(1)} %get-tuple-element.20.refs_4_), channel_id=1, source_target_pairs={{0,2},{7,5},{8,10},{15,13},{16,18},{23,21},{24,26},{31,29}} | collective-permute-start | bytes 1572872 | tf_op jit(solution)/shard_map/ppermute | solution.py:209
  167.7 2.7 %convert_add_fusion = (f32[4096,128]{1,0:T(8,128)S(1)}, f32[4096,128]{1,0:T(8,128)S(1)}) fusion(bf16[4096,128]{1,0:T(8,128)(2,1)} %get-tuple-element.11, bf16[4096,128]{1,0:T(8,128)(2,1)} %add_convert_fusion, bf16[4096,128]{1,0:T(8,128)(2,1)} %get-tuple-element.10, bf16[4096,128]{1,0:T(8,128)(2,1)} %add_convert_fusion.1), kind=kLoop, calls=%fused_computation.14 | loop fusion | flops 3145728 | bytes 8388608 | tf_op jit(solution)/shard_map/add | solution.py:301
  171.8 3.9 %subtract_convert_fusion = (bf16[8192,128]{1,0:T(8,128)(2,1)}, f32[8192,128]{1,0:T(8,128)}) fusion(bf16[8192,128]{1,0:T(8,128)(2,1)S(1)} %copy-done.36, f32[4096,128]{1,0:T(8,128)S(1)} %get-tuple-element.34, f32[4096,128]{1,0:T(8,128)S(1)} %get-tuple-element.35, f32[8192,128]{1,0:T(8,128)S(1)} %copy-done.32), kind=kLoop, calls=%fused_computation.8 | loop fusion | flops 10485760 | bytes 16777216 | tf_op jit(solution)/shard_map/convert_element_type | solution.py:174
  176.2 1.7 add_convert_fusion.9
  177.9 1.8 collective-permute-start.31
  179.7 1.5 add_convert_fusion.6
  181.2 4.0 %collective-permute-start.38 = (bf16[256,1024]{1,0:T(8,128)(2,1)S(1)}, bf16[256,1024]{1,0:T(8,128)(2,1)S(1)}, u32[]{:S(2)}, u32[]{:S(2)}) collective-permute-start(bf16[256,1024]{1,0:T(8,128)(2,1)S(1)} %add_convert_fusion.6), channel_id=1, source_target_pairs={{0,2},{2,4},{5,3},{7,5},{8,10},{10,12},{13,11},{15,13},{16,18},{18... | collective-permute-start | bytes 1572872 | tf_op jit(solution)/shard_map/ppermute | solution.py:209
  186.7 4.5 %collective-permute-start.32 = (bf16[256,1024]{1,0:T(8,128)(2,1)S(1)}, bf16[256,1024]{1,0:T(8,128)(2,1)S(1)}, u32[]{:S(2)}, u32[]{:S(2)}) collective-permute-start(bf16[256,1024]{1,0:T(8,128)(2,1)S(1)} %add_convert_fusion.8), channel_id=1, source_target_pairs={{0,2},{2,4},{3,1},{4,6},{5,3},{7,5},{8,10},{10,12},{11,9},{12,14},... | collective-permute-start | bytes 1572872 | tf_op jit(solution)/shard_map/ppermute | solution.py:209
  192.3 4.4 %collective-permute-start.39 = (bf16[256,1024]{1,0:T(8,128)(2,1)S(1)}, bf16[256,1024]{1,0:T(8,128)(2,1)S(1)}, u32[]{:S(2)}, u32[]{:S(2)}) collective-permute-start(bf16[256,1024]{1,0:T(8,128)(2,1)S(1)} %add_convert_fusion.5), channel_id=1, source_target_pairs={{0,2},{2,4},{3,1},{4,6},{5,3},{7,5},{8,10},{10,12},{11,9},{12,14},... | collective-permute-start | bytes 1572872 | tf_op jit(solution)/shard_map/ppermute | solution.py:209
  198.9 4.6 %collective-permute-done.39 = bf16[256,1024]{1,0:T(8,128)(2,1)S(1)} collective-permute-done((bf16[256,1024]{1,0:T(8,128)(2,1)S(1)}, bf16[256,1024]{1,0:T(8,128)(2,1)S(1)}, u32[]{:S(2)}, u32[]{:S(2)}) %collective-permute-start.39) | collective-permute-done | bytes 524320 | tf_op jit(solution)/shard_map/ppermute | solution.py:209
  (186 shorter events, 42.0 us)
Async XLA Ops:
  1.4 2.2 %collective-permute-start = (bf16[512,512]{1,0:T(8,128)(2,1)}, bf16[512,512]{1,0:T(8,128)(2,1)S(1)}, u32[]{:S(2)}, u32[]{:S(2)}) collective-permute-start(bf16[512,512]{1,0:T(8,128)(2,1)} %bitcast.54), channel_id=1, source_target_pairs={{0,1},{1,0},{2,3},{3,2},{4,5},{5,4},{6,7},{7,6},{8,9},{9,8},{10,11... | collective-permute-start | bytes 1572872 | tf_op jit(solution)/shard_map/ppermute | solution.py:206
  1.9 2.5 %collective-permute-start.1 = (bf16[512,512]{1,0:T(8,128)(2,1)}, bf16[512,512]{1,0:T(8,128)(2,1)S(1)}, u32[]{:S(2)}, u32[]{:S(2)}) collective-permute-start(bf16[512,512]{1,0:T(8,128)(2,1)} %bitcast.52), channel_id=1, source_target_pairs={{0,1},{1,0},{2,3},{3,2},{4,5},{5,4},{6,7},{7,6},{8,9},{9,8},{10,11... | collective-permute-start | bytes 1572872 | tf_op jit(solution)/shard_map/ppermute | solution.py:206
  6.1 17.3 %copy-start.10 = (bf16[1024,256]{1,0:T(8,128)(2,1)}, bf16[1024,256]{1,0:T(8,128)(2,1)S(1)}, u32[]{:S(2)}) copy-start(bf16[1024,256]{1,0:T(8,128)(2,1)S(1)} %get-tuple-element.9.refs_1_) | copy-start | bytes 1572868
  6.1 26.8 %collective-permute-start.2 = (bf16[1024,256]{1,0:T(8,128)(2,1)S(1)}, bf16[1024,256]{1,0:T(8,128)(2,1)S(1)}, u32[]{:S(2)}, u32[]{:S(2)}) collective-permute-start(bf16[1024,256]{1,0:T(8,128)(2,1)S(1)} %get-tuple-element.8.refs_2_.refs_0_), channel_id=1, source_target_pairs={{0,2},{2,4},{3,1},{4,6},{5,3},{7,5},{8,10},{10,12},{11,9},{12,14},... | collective-permute-start | bytes 1572872 | tf_op jit(solution)/shard_map/ppermute | solution.py:209
  23.4 11.5 %collective-permute-start.11 = (bf16[1024,256]{1,0:T(8,128)(2,1)S(1)}, bf16[1024,256]{1,0:T(8,128)(2,1)}, u32[]{:S(2)}, u32[]{:S(2)}) collective-permute-start(bf16[1024,256]{1,0:T(8,128)(2,1)S(1)} %get-tuple-element.9.refs_1_), channel_id=1, source_target_pairs={{0,2},{2,4},{3,1},{4,6},{5,3},{7,5},{8,10},{10,12},{11,9},{12,14},... | collective-permute-start | bytes 1572872 | tf_op jit(solution)/shard_map/ppermute | solution.py:209
  29.8 21.4 %copy-start.27 = (bf16[4096,128]{1,0:T(8,128)(2,1)}, bf16[4096,128]{1,0:T(8,128)(2,1)S(1)}, u32[]{:S(2)}) copy-start(bf16[4096,128]{1,0:T(8,128)(2,1)S(1)} %get-tuple-element.30) | copy-start | bytes 3145732
  29.8 22.7 %copy-start.29 = (bf16[4096,128]{1,0:T(8,128)(2,1)}, bf16[4096,128]{1,0:T(8,128)(2,1)S(1)}, u32[]{:S(2)}) copy-start(bf16[4096,128]{1,0:T(8,128)(2,1)S(1)} %get-tuple-element.31) | copy-start | bytes 3145732
  29.8 19.9 %collective-permute-start.20 = (bf16[4096,128]{1,0:T(8,128)(2,1)S(1)}, bf16[4096,128]{1,0:T(8,128)(2,1)S(1)}, u32[]{:S(2)}, u32[]{:S(2)}) collective-permute-start(bf16[4096,128]{1,0:T(8,128)(2,1)S(1)} %get-tuple-element.31), channel_id=1, source_target_pairs={{0,8},{8,0},{16,24},{24,16},{1,9},{9,1},{17,25},{25,17},{2,10},{10... | collective-permute-start | bytes 3145736 | tf_op jit(solution)/shard_map/ppermute | solution.py:274
  31.4 19.8 %collective-permute-start.21 = (bf16[4096,128]{1,0:T(8,128)(2,1)S(1)}, bf16[4096,128]{1,0:T(8,128)(2,1)S(1)}, u32[]{:S(2)}, u32[]{:S(2)}) collective-permute-start(bf16[4096,128]{1,0:T(8,128)(2,1)S(1)} %get-tuple-element.30), channel_id=1, source_target_pairs={{0,16},{8,24},{16,0},{24,8},{1,17},{9,25},{17,1},{25,9},{2,18},{10... | collective-permute-start | bytes 3145736 | tf_op jit(solution)/shard_map/ppermute | solution.py:274
  33.4 3.7 %collective-permute-start.3 = (bf16[1024,256]{1,0:T(8,128)(2,1)S(1)}, bf16[1024,256]{1,0:T(8,128)(2,1)}, u32[]{:S(2)}, u32[]{:S(2)}) collective-permute-start(bf16[1024,256]{1,0:T(8,128)(2,1)S(1)} %fence.7.refs_2_), channel_id=1, source_target_pairs={{2,4},{3,1},{4,6},{5,3},{10,12},{11,9},{12,14},{13,11},{18,20},{19... | collective-permute-start | bytes 1572872 | tf_op jit(solution)/shard_map/ppermute | solution.py:209
  34.9 3.7 %collective-permute-start.12 = (bf16[1024,256]{1,0:T(8,128)(2,1)}, bf16[1024,256]{1,0:T(8,128)(2,1)}, u32[]{:S(2)}, u32[]{:S(2)}) collective-permute-start(bf16[1024,256]{1,0:T(8,128)(2,1)} %collective-permute-done.11.refs_3_), channel_id=1, source_target_pairs={{2,4},{3,1},{4,6},{5,3},{10,12},{11,9},{12,14},{13,11},{18,20},{19... | collective-permute-start | bytes 1572872 | tf_op jit(solution)/shard_map/ppermute | solution.py:209
  36.4 14.8 %collective-permute-start.14 = (bf16[1024,256]{1,0:T(8,128)(2,1)S(1)}, bf16[1024,256]{1,0:T(8,128)(2,1)S(1)}, u32[]{:S(2)}, u32[]{:S(2)}) collective-permute-start(bf16[1024,256]{1,0:T(8,128)(2,1)S(1)} %fence.7.refs_2_), channel_id=1, source_target_pairs={{0,1},{1,0},{2,3},{3,2},{4,5},{5,4},{6,7},{7,6},{8,9},{9,8},{10,11... | collective-permute-start | bytes 1572872 | tf_op jit(solution)/shard_map/ppermute | solution.py:206
  37.2 15.3 %collective-permute-start.4 = (bf16[1024,256]{1,0:T(8,128)(2,1)}, bf16[1024,256]{1,0:T(8,128)(2,1)}, u32[]{:S(2)}, u32[]{:S(2)}) collective-permute-start(bf16[1024,256]{1,0:T(8,128)(2,1)} %collective-permute-done.3.refs_4_), channel_id=1, source_target_pairs={{3,1},{4,6},{11,9},{12,14},{19,17},{20,22},{27,25},{28,30}} | collective-permute-start | bytes 1572872 | tf_op jit(solution)/shard_map/ppermute | solution.py:209
  38.6 13.9 %collective-permute-start.13 = (bf16[1024,256]{1,0:T(8,128)(2,1)}, bf16[1024,256]{1,0:T(8,128)(2,1)}, u32[]{:S(2)}, u32[]{:S(2)}) collective-permute-start(bf16[1024,256]{1,0:T(8,128)(2,1)} %collective-permute-done.12.refs_5_), channel_id=1, source_target_pairs={{3,1},{4,6},{11,9},{12,14},{19,17},{20,22},{27,25},{28,30}} | collective-permute-start | bytes 1572872 | tf_op jit(solution)/shard_map/ppermute | solution.py:209
  49.7 10.1 %collective-permute-start.15 = (bf16[1024,256]{1,0:T(8,128)(2,1)}, bf16[1024,256]{1,0:T(8,128)(2,1)}, u32[]{:S(2)}, u32[]{:S(2)}) collective-permute-start(bf16[1024,256]{1,0:T(8,128)(2,1)} %collective-permute-done.11.refs_3_), channel_id=1, source_target_pairs={{0,1},{1,0},{2,3},{3,2},{4,5},{5,4},{6,7},{7,6},{8,9},{9,8},{10,11... | collective-permute-start | bytes 1572872 | tf_op jit(solution)/shard_map/ppermute | solution.py:206
  51.1 11.0 %collective-permute-start.16 = (bf16[1024,256]{1,0:T(8,128)(2,1)}, bf16[1024,256]{1,0:T(8,128)(2,1)}, u32[]{:S(2)}, u32[]{:S(2)}) collective-permute-start(bf16[1024,256]{1,0:T(8,128)(2,1)} %collective-permute-done.3.refs_4_), channel_id=1, source_target_pairs={{0,1},{1,0},{2,3},{3,2},{4,5},{5,4},{6,7},{7,6},{8,9},{9,8},{10,11... | collective-permute-start | bytes 1572872 | tf_op jit(solution)/shard_map/ppermute | solution.py:206
  52.0 10.2 %collective-permute-start.17 = (bf16[1024,256]{1,0:T(8,128)(2,1)}, bf16[1024,256]{1,0:T(8,128)(2,1)}, u32[]{:S(2)}, u32[]{:S(2)}) collective-permute-start(bf16[1024,256]{1,0:T(8,128)(2,1)} %collective-permute-done.12.refs_5_), channel_id=1, source_target_pairs={{0,1},{1,0},{2,3},{3,2},{4,5},{5,4},{6,7},{7,6},{8,9},{9,8},{10,11... | collective-permute-start | bytes 1572872 | tf_op jit(solution)/shard_map/ppermute | solution.py:206
  52.5 9.7 %collective-permute-start.18 = (bf16[1024,256]{1,0:T(8,128)(2,1)}, bf16[1024,256]{1,0:T(8,128)(2,1)}, u32[]{:S(2)}, u32[]{:S(2)}) collective-permute-start(bf16[1024,256]{1,0:T(8,128)(2,1)} %collective-permute-done.4.refs_3_.refs_6_), channel_id=1, source_target_pairs={{0,1},{1,0},{2,3},{3,2},{4,5},{5,4},{6,7},{7,6},{8,9},{9,8},{10,11... | collective-permute-start | bytes 1572872 | tf_op jit(solution)/shard_map/ppermute | solution.py:206
  52.5 9.6 %collective-permute-start.19 = (bf16[1024,256]{1,0:T(8,128)(2,1)}, bf16[1024,256]{1,0:T(8,128)(2,1)}, u32[]{:S(2)}, u32[]{:S(2)}) collective-permute-start(bf16[1024,256]{1,0:T(8,128)(2,1)} %collective-permute-done.13.refs_7_), channel_id=1, source_target_pairs={{0,1},{1,0},{2,3},{3,2},{4,5},{5,4},{6,7},{7,6},{8,9},{9,8},{10,11... | collective-permute-start | bytes 1572872 | tf_op jit(solution)/shard_map/ppermute | solution.py:206
  59.8 14.6 %collective-permute-start.5 = (bf16[1024,512]{1,0:T(8,128)(2,1)S(1)}, bf16[1024,512]{1,0:T(8,128)(2,1)S(1)}, u32[]{:S(2)}, u32[]{:S(2)}) collective-permute-start(bf16[1024,512]{1,0:T(8,128)(2,1)S(1)} %join_cores.3.refs_14_.refs_0_), channel_id=1, source_target_pairs={{0,2},{2,4},{3,1},{4,6},{5,3},{7,5},{8,10},{10,12},{11,9},{12,14},... | collective-permute-start | bytes 3145736 | tf_op jit(solution)/shard_map/ppermute | solution.py:209
  74.4 6.3 %collective-permute-start.6 = (bf16[1024,512]{1,0:T(8,128)(2,1)S(1)}, bf16[1024,512]{1,0:T(8,128)(2,1)S(1)}, u32[]{:S(2)}, u32[]{:S(2)}) collective-permute-start(bf16[1024,512]{1,0:T(8,128)(2,1)S(1)} %collective-permute-done.5.refs_2_.refs_1_), channel_id=1, source_target_pairs={{2,4},{3,1},{4,6},{5,3},{10,12},{11,9},{12,14},{13,11},{18,20},{19... | collective-permute-start | bytes 3145736 | tf_op jit(solution)/shard_map/ppermute | solution.py:209
  84.3 15.7 %collective-permute-start.23 = (bf16[512,1024]{1,0:T(8,128)(2,1)}, bf16[512,1024]{1,0:T(8,128)(2,1)}, u32[]{:S(2)}, u32[]{:S(2)}) collective-permute-start(bf16[512,1024]{1,0:T(8,128)(2,1)} %get-tuple-element.25), channel_id=1, source_target_pairs={{0,1},{1,0},{2,3},{3,2},{4,5},{5,4},{6,7},{7,6},{8,9},{9,8},{10,11... | collective-permute-start | bytes 3145736 | tf_op jit(solution)/shard_map/ppermute | solution.py:206
  95.9 17.9 %collective-permute-start.22 = (bf16[512,1024]{1,0:T(8,128)(2,1)}, bf16[512,1024]{1,0:T(8,128)(2,1)S(1)}, u32[]{:S(2)}, u32[]{:S(2)}) collective-permute-start(bf16[512,1024]{1,0:T(8,128)(2,1)} %get-tuple-element.24), channel_id=1, source_target_pairs={{0,1},{1,0},{2,3},{3,2},{4,5},{5,4},{6,7},{7,6},{8,9},{9,8},{10,11... | collective-permute-start | bytes 3145736 | tf_op jit(solution)/shard_map/ppermute | solution.py:206
  95.9 15.1 %collective-permute-start.7 = (bf16[1024,512]{1,0:T(8,128)(2,1)}, bf16[1024,512]{1,0:T(8,128)(2,1)S(1)}, u32[]{:S(2)}, u32[]{:S(2)}) collective-permute-start(bf16[1024,512]{1,0:T(8,128)(2,1)} %copy-done.6), channel_id=1, source_target_pairs={{3,1},{4,6},{11,9},{12,14},{19,17},{20,22},{27,25},{28,30}} | collective-permute-start | bytes 3145736 | tf_op jit(solution)/shard_map/ppermute | solution.py:209
  103.8 17.5 %collective-permute-start.24 = (bf16[512,1024]{1,0:T(8,128)(2,1)S(1)}, bf16[512,1024]{1,0:T(8,128)(2,1)S(1)}, u32[]{:S(2)}, u32[]{:S(2)}) collective-permute-start(bf16[512,1024]{1,0:T(8,128)(2,1)S(1)} %get-tuple-element.22), channel_id=1, source_target_pairs={{0,2},{7,5},{8,10},{15,13},{16,18},{23,21},{24,26},{31,29}} | collective-permute-start | bytes 3145736 | tf_op jit(solution)/shard_map/ppermute | solution.py:209
  110.5 11.9 %collective-permute-start.8 = (bf16[1024,512]{1,0:T(8,128)(2,1)S(1)}, bf16[1024,512]{1,0:T(8,128)(2,1)S(1)}, u32[]{:S(2)}, u32[]{:S(2)}) collective-permute-start(bf16[1024,512]{1,0:T(8,128)(2,1)S(1)} %copy-done.5), channel_id=1, source_target_pairs={{0,1},{1,0},{2,3},{3,2},{4,5},{5,4},{6,7},{7,6},{8,9},{9,8},{10,11... | collective-permute-start | bytes 3145736 | tf_op jit(solution)/shard_map/ppermute | solution.py:206
  110.5 12.0 %collective-permute-start.9 = (bf16[1024,512]{1,0:T(8,128)(2,1)S(1)}, bf16[1024,512]{1,0:T(8,128)(2,1)S(1)}, u32[]{:S(2)}, u32[]{:S(2)}) collective-permute-start(bf16[1024,512]{1,0:T(8,128)(2,1)S(1)} %copy-done.7), channel_id=1, source_target_pairs={{0,1},{1,0},{2,3},{3,2},{4,5},{5,4},{6,7},{7,6},{8,9},{9,8},{10,11... | collective-permute-start | bytes 3145736 | tf_op jit(solution)/shard_map/ppermute | solution.py:206
  111.0 16.3 %collective-permute-start.10 = (bf16[1024,512]{1,0:T(8,128)(2,1)S(1)}, bf16[1024,512]{1,0:T(8,128)(2,1)S(1)}, u32[]{:S(2)}, u32[]{:S(2)}) collective-permute-start(bf16[1024,512]{1,0:T(8,128)(2,1)S(1)} %collective-permute-done.7.refs_3_), channel_id=1, source_target_pairs={{0,1},{1,0},{2,3},{3,2},{4,5},{5,4},{6,7},{7,6},{8,9},{9,8},{10,11... | collective-permute-start | bytes 3145736 | tf_op jit(solution)/shard_map/ppermute | solution.py:206
  113.9 47.0 %collective-permute-start.43 = (bf16[4096,128]{1,0:T(8,128)(2,1)}, bf16[4096,128]{1,0:T(8,128)(2,1)}, u32[]{:S(2)}, u32[]{:S(2)}) collective-permute-start(bf16[4096,128]{1,0:T(8,128)(2,1)} %add_convert_fusion.1), channel_id=1, source_target_pairs={{0,16},{8,24},{16,0},{24,8},{1,17},{9,25},{17,1},{25,9},{2,18},{10... | collective-permute-start | bytes 3145736 | tf_op jit(solution)/shard_map/ppermute | solution.py:274
  121.3 43.7 %collective-permute-start.44 = (bf16[4096,128]{1,0:T(8,128)(2,1)}, bf16[4096,128]{1,0:T(8,128)(2,1)}, u32[]{:S(2)}, u32[]{:S(2)}) collective-permute-start(bf16[4096,128]{1,0:T(8,128)(2,1)} %add_convert_fusion), channel_id=1, source_target_pairs={{0,8},{8,0},{16,24},{24,16},{1,9},{9,1},{17,25},{25,17},{2,10},{10... | collective-permute-start | bytes 3145736 | tf_op jit(solution)/shard_map/ppermute | solution.py:274
  122.5 10.3 %collective-permute-start.25 = (bf16[512,1024]{1,0:T(8,128)(2,1)S(1)}, bf16[512,1024]{1,0:T(8,128)(2,1)S(1)}, u32[]{:S(2)}, u32[]{:S(2)}) collective-permute-start(bf16[512,1024]{1,0:T(8,128)(2,1)S(1)} %get-tuple-element.23), channel_id=1, source_target_pairs={{0,1},{1,0},{2,3},{3,2},{4,5},{5,4},{6,7},{7,6},{8,9},{9,8},{10,11... | collective-permute-start | bytes 3145736 | tf_op jit(solution)/shard_map/ppermute | solution.py:206
  122.6 17.0 %collective-permute-start.26 = (bf16[512,1024]{1,0:T(8,128)(2,1)S(1)}, bf16[512,1024]{1,0:T(8,128)(2,1)S(1)}, u32[]{:S(2)}, u32[]{:S(2)}) collective-permute-start(bf16[512,1024]{1,0:T(8,128)(2,1)S(1)} %add_convert_fusion.3.refs_8_), channel_id=1, source_target_pairs={{0,2},{2,4},{5,3},{7,5},{8,10},{10,12},{13,11},{15,13},{16,18},{18... | collective-permute-start | bytes 3145736 | tf_op jit(solution)/shard_map/ppermute | solution.py:209
  145.8 9.9 %collective-permute-start.29 = (bf16[256,1024]{1,0:T(8,128)(2,1)S(1)}, bf16[256,1024]{1,0:T(8,128)(2,1)}, u32[]{:S(2)}, u32[]{:S(2)}) collective-permute-start(bf16[256,1024]{1,0:T(8,128)(2,1)S(1)} %get-tuple-element.27), channel_id=1, source_target_pairs={{0,1},{1,0},{2,3},{3,2},{4,5},{5,4},{6,7},{7,6},{8,9},{9,8},{10,11... | collective-permute-start | bytes 1572872 | tf_op jit(solution)/shard_map/ppermute | solution.py:206
  150.5 8.3 %collective-permute-start.36 = (bf16[256,1024]{1,0:T(8,128)(2,1)S(1)}, bf16[256,1024]{1,0:T(8,128)(2,1)}, u32[]{:S(2)}, u32[]{:S(2)}) collective-permute-start(bf16[256,1024]{1,0:T(8,128)(2,1)S(1)} %get-tuple-element.29), channel_id=1, source_target_pairs={{0,1},{1,0},{2,3},{3,2},{4,5},{5,4},{6,7},{7,6},{8,9},{9,8},{10,11... | collective-permute-start | bytes 1572872 | tf_op jit(solution)/shard_map/ppermute | solution.py:206
  151.0 34.2 %collective-permute-start.41 = (bf16[512,1024]{1,0:T(8,128)(2,1)S(1)}, bf16[512,1024]{1,0:T(8,128)(2,1)S(1)}, u32[]{:S(2)}, u32[]{:S(2)}) collective-permute-start(bf16[512,1024]{1,0:T(8,128)(2,1)S(1)} %add_convert_fusion.2.refs_2_), channel_id=1, source_target_pairs={{0,2},{2,4},{3,1},{4,6},{5,3},{7,5},{8,10},{10,12},{11,9},{12,14},... | collective-permute-start | bytes 3145736 | tf_op jit(solution)/shard_map/ppermute | solution.py:209
  155.7 20.0 %collective-permute-start.28 = (bf16[256,1024]{1,0:T(8,128)(2,1)}, bf16[256,1024]{1,0:T(8,128)(2,1)}, u32[]{:S(2)}, u32[]{:S(2)}) collective-permute-start(bf16[256,1024]{1,0:T(8,128)(2,1)} %get-tuple-element.26), channel_id=1, source_target_pairs={{0,1},{1,0},{2,3},{3,2},{4,5},{5,4},{6,7},{7,6},{8,9},{9,8},{10,11... | collective-permute-start | bytes 1572872 | tf_op jit(solution)/shard_map/ppermute | solution.py:206
  158.8 19.1 %collective-permute-start.35 = (bf16[256,1024]{1,0:T(8,128)(2,1)S(1)}, bf16[256,1024]{1,0:T(8,128)(2,1)}, u32[]{:S(2)}, u32[]{:S(2)}) collective-permute-start(bf16[256,1024]{1,0:T(8,128)(2,1)S(1)} %copy-done.34), channel_id=1, source_target_pairs={{0,1},{1,0},{2,3},{3,2},{4,5},{5,4},{6,7},{7,6},{8,9},{9,8},{10,11... | collective-permute-start | bytes 1572872 | tf_op jit(solution)/shard_map/ppermute | solution.py:206
  160.9 14.8 %collective-permute-start.30 = (bf16[256,1024]{1,0:T(8,128)(2,1)S(1)}, bf16[256,1024]{1,0:T(8,128)(2,1)}, u32[]{:S(2)}, u32[]{:S(2)}) collective-permute-start(bf16[256,1024]{1,0:T(8,128)(2,1)S(1)} %get-tuple-element.18.refs_3_), channel_id=1, source_target_pairs={{0,2},{7,5},{8,10},{15,13},{16,18},{23,21},{24,26},{31,29}} | collective-permute-start | bytes 1572872 | tf_op jit(solution)/shard_map/ppermute | solution.py:209
  165.0 14.8 %collective-permute-start.37 = (bf16[256,1024]{1,0:T(8,128)(2,1)S(1)}, bf16[256,1024]{1,0:T(8,128)(2,1)}, u32[]{:S(2)}, u32[]{:S(2)}) collective-permute-start(bf16[256,1024]{1,0:T(8,128)(2,1)S(1)} %get-tuple-element.20.refs_4_), channel_id=1, source_target_pairs={{0,2},{7,5},{8,10},{15,13},{16,18},{23,21},{24,26},{31,29}} | collective-permute-start | bytes 1572872 | tf_op jit(solution)/shard_map/ppermute | solution.py:209
  175.7 9.8 %collective-permute-start.27 = (bf16[256,1024]{1,0:T(8,128)(2,1)S(1)}, bf16[256,1024]{1,0:T(8,128)(2,1)S(1)}, u32[]{:S(2)}, u32[]{:S(2)}) collective-permute-start(bf16[256,1024]{1,0:T(8,128)(2,1)S(1)} %copy-done.37), channel_id=1, source_target_pairs={{0,1},{1,0},{2,3},{3,2},{4,5},{5,4},{6,7},{7,6},{8,9},{9,8},{10,11... | collective-permute-start | bytes 1572872 | tf_op jit(solution)/shard_map/ppermute | solution.py:206
  175.7 15.5 %collective-permute-start.34 = (bf16[256,1024]{1,0:T(8,128)(2,1)S(1)}, bf16[256,1024]{1,0:T(8,128)(2,1)S(1)}, u32[]{:S(2)}, u32[]{:S(2)}) collective-permute-start(bf16[256,1024]{1,0:T(8,128)(2,1)S(1)} %get-tuple-element.21), channel_id=1, source_target_pairs={{0,1},{1,0},{2,3},{3,2},{4,5},{5,4},{6,7},{7,6},{8,9},{9,8},{10,11... | collective-permute-start | bytes 1572872 | tf_op jit(solution)/shard_map/ppermute | solution.py:206
  177.9 8.4 %collective-permute-start.31 = (bf16[256,1024]{1,0:T(8,128)(2,1)S(1)}, bf16[256,1024]{1,0:T(8,128)(2,1)S(1)}, u32[]{:S(2)}, u32[]{:S(2)}) collective-permute-start(bf16[256,1024]{1,0:T(8,128)(2,1)S(1)} %add_convert_fusion.9), channel_id=1, source_target_pairs={{0,2},{2,4},{5,3},{7,5},{8,10},{10,12},{13,11},{15,13},{16,18},{18... | collective-permute-start | bytes 1572872 | tf_op jit(solution)/shard_map/ppermute | solution.py:209
  181.2 10.8 %collective-permute-start.38 = (bf16[256,1024]{1,0:T(8,128)(2,1)S(1)}, bf16[256,1024]{1,0:T(8,128)(2,1)S(1)}, u32[]{:S(2)}, u32[]{:S(2)}) collective-permute-start(bf16[256,1024]{1,0:T(8,128)(2,1)S(1)} %add_convert_fusion.6), channel_id=1, source_target_pairs={{0,2},{2,4},{5,3},{7,5},{8,10},{10,12},{13,11},{15,13},{16,18},{18... | collective-permute-start | bytes 1572872 | tf_op jit(solution)/shard_map/ppermute | solution.py:209
  186.7 11.2 %collective-permute-start.32 = (bf16[256,1024]{1,0:T(8,128)(2,1)S(1)}, bf16[256,1024]{1,0:T(8,128)(2,1)S(1)}, u32[]{:S(2)}, u32[]{:S(2)}) collective-permute-start(bf16[256,1024]{1,0:T(8,128)(2,1)S(1)} %add_convert_fusion.8), channel_id=1, source_target_pairs={{0,2},{2,4},{3,1},{4,6},{5,3},{7,5},{8,10},{10,12},{11,9},{12,14},... | collective-permute-start | bytes 1572872 | tf_op jit(solution)/shard_map/ppermute | solution.py:209
  192.3 11.2 %collective-permute-start.39 = (bf16[256,1024]{1,0:T(8,128)(2,1)S(1)}, bf16[256,1024]{1,0:T(8,128)(2,1)S(1)}, u32[]{:S(2)}, u32[]{:S(2)}) collective-permute-start(bf16[256,1024]{1,0:T(8,128)(2,1)S(1)} %add_convert_fusion.5), channel_id=1, source_target_pairs={{0,2},{2,4},{3,1},{4,6},{5,3},{7,5},{8,10},{10,12},{11,9},{12,14},... | collective-permute-start | bytes 1572872 | tf_op jit(solution)/shard_map/ppermute | solution.py:209
  196.8 7.6 %collective-permute-start.42 = (bf16[512,512]{1,0:T(8,128)(2,1)S(1)}, bf16[512,512]{1,0:T(8,128)(2,1)S(1)}, u32[]{:S(2)}, u32[]{:S(2)}) collective-permute-start(bf16[512,512]{1,0:T(8,128)(2,1)S(1)} %select_convert_fusion), channel_id=1, source_target_pairs={{0,1},{1,0},{2,3},{3,2},{4,5},{5,4},{6,7},{7,6},{8,9},{9,8},{10,11... | collective-permute-start | bytes 1572872 | tf_op jit(solution)/shard_map/ppermute | solution.py:206
  198.9 7.1 %collective-permute-start.33 = (bf16[256,512]{1,0:T(8,128)(2,1)}, bf16[256,512]{1,0:T(8,128)(2,1)S(1)}, u32[]{:S(2)}, u32[]{:S(2)}) collective-permute-start(bf16[256,512]{1,0:T(8,128)(2,1)} %select_convert_fusion.2), channel_id=1, source_target_pairs={{0,1},{1,0},{2,3},{3,2},{4,5},{5,4},{6,7},{7,6},{8,9},{9,8},{10,11... | collective-permute-start | bytes 786440 | tf_op jit(solution)/shard_map/ppermute | solution.py:206
  204.4 1.9 collective-permute-start.40
  (43 other events, 260.8 us)

commit v7 on v6

--- a/solution.py
+++ b/solution.py
@@ -71,27 +71,33 @@
     return order(fence, values, [ANY] * len(values), shapes, [], 4, after, aliases)
 
 
-def normalise(order, tokens, gain, after=()):
+def prepare(order, tokens, cotangent, gain, chips, after=()):
     rows, model = tokens.shape
-
-    def run(_, tokens_ref, gain_ref, out_ref):
+    block = model // chips
+
+    def run(place_ref, tokens_ref, cot_ref, gain_ref, normed_out, cot_out):
         xf = tokens_ref[...].astype(jnp.float32)
         scale = lax.rsqrt(jnp.mean(xf * xf, axis=1, keepdims=True) + 1e-05)
-        out_ref[...] = (xf * scale * gain_ref[...]).astype(jnp.bfloat16)
+        for p in range(chips):
+            cols = pl.ds(pl.multiple_of(place_ref[p] * block, block), block)
+            to = slice(p * block, (p + 1) * block)
+            part = tokens_ref[:, cols].astype(jnp.float32)
+            normed_out[:, to] = (part * scale * gain_ref[:, cols]).astype(jnp.bfloat16)
+            cot_out[:, to] = cot_ref[:, cols]
 
     tile = pl.BlockSpec((ROW_TILE, model), lambda i, _: (i, 0))
     return order(
         run,
-        (tokens, gain[None]),
-        [tile, pl.BlockSpec((1, model), lambda i, _: (0, 0))],
-        [jax.ShapeDtypeStruct((rows, model), jnp.bfloat16)],
+        (tokens, cotangent, gain[None]),
+        [tile, tile, pl.BlockSpec((1, model), lambda i, _: (0, 0))],
+        [jax.ShapeDtypeStruct((rows, model), jnp.bfloat16)] * 2,
         [],
-        16,
+        24,
         after,
         grid=rows // ROW_TILE,
-        out_specs=[tile],
+        out_specs=[tile, tile],
         us=20.0,
-    )[0]
+    )
 
 
 def join_cores(order, own, partner, parts, after=()):
@@ -118,54 +124,6 @@
         [pltpu.SemaphoreType.DMA((2 * parts,))],
         4,
         after,
-    )
-
-
-def assemble(order, pieces, others, parts, after=()):
-    chips, held = len(pieces), len(pieces[0])
-    block, width = pieces[0][0].shape
-    features = held * width
-    count = max(parts, held)
-    piece = features // count
-    wide = features // parts
-
-    def run(place_ref, *refs):
-        piece_refs = [refs[p * held : (p + 1) * held] for p in range(chips)]
-        rest = refs[chips * held :]
-        other_refs = [rest[p * held : (p + 1) * held] for p in range(chips - 1)]
-        out_refs, sems = rest[(chips - 1) * held : -1], rest[-1]
-        position = place_ref[chips]
-
-        def moves(p, source):
-            rows = pl.ds(pl.multiple_of(place_ref[p] * block, block), block)
-            for j in range(count):
-                at = j * piece
-                taken = source[at // width].at[:, pl.ds(at % width, piece)]
-                target = out_refs[at // wide].at[rows, pl.ds(at % wide, piece)]
-                yield pltpu.make_async_copy(taken, target, sems.at[p * count + j])
-
-        def begin(p, source):
-            for copy in moves(p, source):
-                copy.start()
-
-        begin(0, piece_refs[0])
-        for p in range(1, chips):
-            pl.when(position >= p)(lambda p=p: begin(p, piece_refs[p]))
-            pl.when(position < p)(lambda p=p: begin(p, other_refs[chips - p - 1]))
-        for p in range(chips):
-            for copy in moves(p, piece_refs[0]):
-                copy.wait()
-
-    arrays = [part for shard in (*pieces, *others) for part in shard]
-    return order(
-        run,
-        tuple(arrays),
-        [ANY] * len(arrays),
-        [jax.ShapeDtypeStruct((chips * block, wide), jnp.bfloat16)] * parts,
-        [pltpu.SemaphoreType.DMA((chips * count,))],
-        4,
-        after,
-        us=2.4,
     )
 
 
@@ -199,7 +157,6 @@
     order = Order(jnp.stack([*behind, position, core]).astype(jnp.int32))
     shard = value_weight.shape[1]
     block = 2 * shard
-    cotangent = out_cotangent[0]
     bf16, f32 = jnp.bfloat16, jnp.float32
 
     def swap(value):
@@ -214,18 +171,14 @@
             self.terms = terms.astype(bf16)
             if after:
                 self.terms = fence(order, self.terms, after=after)[0]
-            self.across = [None] + [swap(self.block(behind[chips - s])) for s in range(1, chips)]
+            self.across = [None] + [swap(self.block(chips - s)) for s in range(1, chips)]
             self.arrived = None
 
-        def block(self, where):
-            chosen = self.terms[:, :block]
-            for at in range(1, chips):
-                part = self.terms[:, at * block : (at + 1) * block]
-                chosen = jnp.where(where == at, part, chosen)
-            return chosen
+        def block(self, place):
+            return self.terms[:, place * block : (place + 1) * block]
 
         def message(self, step):
-            term = self.block(behind[step]).astype(f32) + self.across[step].astype(f32)
+            term = self.block(step).astype(f32) + self.across[step].astype(f32)
             if self.arrived is not None:
                 term = term + self.arrived.astype(f32)
             return term.astype(bf16)
@@ -236,7 +189,7 @@
             return message
 
         def finish(self):
-            whole = self.block(chip).astype(f32) + self.arrived.astype(f32)
+            whole = self.block(0).astype(f32) + self.arrived.astype(f32)
             first, second = whole[:, :shard], whole[:, shard:]
             mine = jnp.where(core == 0, first, second)
             partners = jnp.where(core == 0, second, first)
@@ -253,11 +206,19 @@
             others.append([swap(part) for part in along])
         return pieces, others
 
+    def assemble(pieces, others):
+        shards = [jnp.concatenate(pieces[0], axis=1)]
+        for p in range(1, chips):
+            parts = zip(pieces[p], others[chips - p - 1])
+            chosen = [jnp.where(position >= p, here, there) for here, there in parts]
+            shards.append(jnp.concatenate(chosen, axis=1))
+        return jnp.concatenate(shards, axis=0)
+
     first_own, second_own = value_weight[0], output_weight[0]
     first_partner, second_partner = swap(first_own), swap(second_own)
 
     joined = join_cores(order, first_own, first_partner, HALVES, (second_partner,))
-    normed = normalise(order, tokens[0], norm_gain, ())
+    normed, cotangent = prepare(order, tokens[0], out_cotangent[0], norm_gain, chips)
     exponents = fence(order, delta_exponents)[0]
     bits = replicas.bit_length() - 1
     if replicas != 1 << bits or bits < 1:
@@ -280,14 +241,14 @@
     last = pieces[-1]
 
     joined = join_cores(order, second_own, second_partner, 1, (last[0],))
-    weight = assemble(order, pieces, others, 1, early)[0]
+    weight = assemble(pieces, others)
     values = jnp.dot(normed, weight, preferred_element_type=f32).astype(bf16)
     pieces, others = gather(joined)
-    values = fence(order, values, after=(pieces[1][0],))[0]
+    values = fence(order, values, after=(pieces[1][0], *early))[0]
     first = Gradient(values, cotangent, (pieces[2][0],))
     sent = [first.reduce(step) for step in range(1, chips)]
 
-    weight = assemble(order, pieces, others, 1, (sent[1],))[0]
+    weight = assemble(pieces, others)
     mid = jnp.dot(cotangent, weight, preferred_element_type=f32).astype(bf16)
     mid = fence(order, mid, after=(sent[-1],))[0]
     half = mid.shape[1] // HALVES

time: 210 us -> 202 us (0.962)
  waiting for transfers between devices: 38.5 us -> 15.6 us
  matrix products: 18.7 us -> 38.2 us
  starting transfers between devices: 78.7 us -> 95.1 us
  local copies, waits for them, and re-layouts: 24.4 us -> 12.8 us
  other arithmetic: 33.4 us -> 24.7 us
    unnamed x95 -> x35, local copies, waits for them, and re-layouts: 24.3 us -> 9.94 us
    ppermute x23, starting transfers between devices: 20 us -> 33 us  [swap(): return lax.ppermute(value, 'fsdp', [(i, i ^ 1) for i in range(devices)])]
    dot_general x1, matrix products: 4.47 us -> 17.1 us  [per_device(): values = jnp.dot(normed, weight, preferred_element_type=f32).astype(bf16)]
    ppermute x4, waiting for transfers between devices: 11.1 us -> 0.01 us  [per_device(): lax.ppermute(mine, 'replica', [(i, i ^ bit) for i in range(replicas)])]
    ppermute x18, waiting for transfers between devices: 21.7 us -> 11 us  [move(): return lax.ppermute(value, 'fsdp', move_perm(chips, active))]
    convert_element_type x9, other arithmetic: 14.5 us -> 7.96 us  [message(): return term.astype(bf16)]
    dot_general x3, matrix products: 9.74 us -> 13.3 us  [__init__(): lax.dot_general(mid, x, (((0,), (0,)), ((), ())), preferred_element_type=...]
    dot_general x1, matrix products: 4.48 us -> 7.88 us  [per_device(): mid = jnp.dot(cotangent, weight, preferred_element_type=f32).astype(bf16)]
  transfers between devices with their start and end apart: 45 -> 45, of which waited for: 13 -> 11; matrix products, arithmetic and copies ran while one was open for 24% -> 33% of each run, Pallas kernels for 6% -> 6%
where the time goes in v7:
time: 202 us; the launch traced here: 201 us
  starting transfers between devices  95.1 us (47%)
  matrix products  38.2 us (19%)
  other arithmetic  24.7 us (12%)
  waiting for transfers between devices  15.6 us (8%)
  Pallas kernels  13.5 us (7%)
  local copies, waits for them, and re-layouts  12.8 us (6%)
    ppermute x18, starting transfers between devices, move(): return lax.ppermute(value, 'fsdp', move_perm(chips, active))  55.9 us
    ppermute x23, starting transfers between devices, swap(): return lax.ppermute(value, 'fsdp', [(i, i ^ 1) for i in range(devices)])  33 us
    dot_general x1, matrix products, per_device(): values = jnp.dot(normed, weight, preferred_element_type=f32).astype(bf16)  17.1 us
    pallas_call x9, Pallas kernels, __call__(): pl.pallas_call(ordered, grid_spec=pltpu.PrefetchScalarGridSpec(num_scalar...  13.5 us
    dot_general x3, matrix products, __init__(): lax.dot_general(mid, x, (((0,), (0,)), ((), ())), preferred_element_type=...  13.3 us
    ppermute x18, waiting for transfers between devices, move(): return lax.ppermute(value, 'fsdp', move_perm(chips, active))  11 us
    unnamed x35, local copies, waits for them, and re-layouts  9.94 us
    convert_element_type x9, other arithmetic, message(): return term.astype(bf16)  7.96 us
  transfers between devices with their start and end apart: 45, of which 11 were waited for; matrix products, arithmetic and copies ran while one was open for 33% of the time, Pallas kernels for 6%

profile of v7, /device:TPU:0, one launch (start us, length us, event | category | flops | bytes accessed | tf_op | source)
XLA Modules:
  0.0 201.4 jit_solution(13426920485280485700)
XLA Ops:
  2.0 1.6 collective-permute-done.refs_1_
  4.3 1.0 copy-done.3
  6.1 4.9 %collective-permute-start.12 = (bf16[1024,256]{1,0:T(8,128)(2,1)S(1)}, bf16[1024,256]{1,0:T(8,128)(2,1)S(1)}, u32[]{:S(2)}, u32[]{:S(2)}) collective-permute-start(bf16[1024,256]{1,0:T(8,128)(2,1)S(1)} %get-tuple-element.13), channel_id=1, source_target_pairs={{0,2},{2,4},{3,1},{4,6},{5,3},{7,5},{8,10},{10,12},{11,9},{12,14},... | collective-permute-start | bytes 1572872 | tf_op jit(solution)/shard_map/ppermute | solution.py:166
  10.9 3.5 %collective-permute-start.2 = (bf16[1024,256]{1,0:T(8,128)(2,1)S(1)}, bf16[1024,256]{1,0:T(8,128)(2,1)S(1)}, u32[]{:S(2)}, u32[]{:S(2)}) collective-permute-start(bf16[1024,256]{1,0:T(8,128)(2,1)S(1)} %get-tuple-element.10.refs_3_), channel_id=1, source_target_pairs={{0,2},{2,4},{3,1},{4,6},{5,3},{7,5},{8,10},{10,12},{11,9},{12,14},... | collective-permute-start | bytes 1572872 | tf_op jit(solution)/shard_map/ppermute | solution.py:166
  14.4 3.4 %copy-done.2 = bf16[1,1024,4096]{2,1,0:T(8,128)(2,1)S(1)} copy-done((bf16[1,1024,4096]{2,1,0:T(8,128)(2,1)S(1)}, bf16[1,1024,4096]{2,1,0:T(8,128)(2,1)}, u32[]{:S(2)}) %copy-start.2) | copy-done | bytes 8388632
  18.5 8.9 %prepare.1 = (bf16[1024,4096]{1,0:T(8,128)(2,1)S(1)}, bf16[1024,4096]{1,0:T(8,128)(2,1)S(1)}) custom-call(s32[6]{0:T(128)S(1)} %stack.27.place_ref, bf16[1024,4096]{1,0:T(8,128)(2,1)S(1)} %bitcast.35, bf16[1024,4096]{1,0:T(8,128)(2,1)} %bitcast.43, f32[1,4096]{1,0:T(1,128)S(1)} %bitcast.40, bf16[1024,256]{1,0:T(8,128)(2,1)S(1)} %get-tuple-element.10.refs_3_), custom_call_target="tpu_custom_call" | custom-call | flops 20000000000 | bytes 1 | tf_op jit(solution)/shard_map/prepare/pallas_call | solution.py:39
  30.4 5.4 %collective-permute-start.16 = (bf16[1024,256]{1,0:T(8,128)(2,1)S(1)}, bf16[1024,256]{1,0:T(8,128)(2,1)S(1)}, u32[]{:S(2)}, u32[]{:S(2)}) collective-permute-start(bf16[1024,256]{1,0:T(8,128)(2,1)S(1)} %collective-permute-done.3), channel_id=1, source_target_pairs={{0,1},{1,0},{2,3},{3,2},{4,5},{5,4},{6,7},{7,6},{8,9},{9,8},{10,11... | collective-permute-start | bytes 1572872 | tf_op jit(solution)/shard_map/ppermute | solution.py:163
  36.5 4.9 %collective-permute-start.17 = (bf16[1024,256]{1,0:T(8,128)(2,1)S(1)}, bf16[1024,256]{1,0:T(8,128)(2,1)S(1)}, u32[]{:S(2)}, u32[]{:S(2)}) collective-permute-start(bf16[1024,256]{1,0:T(8,128)(2,1)S(1)} %collective-permute-done.13), channel_id=1, source_target_pairs={{0,1},{1,0},{2,3},{3,2},{4,5},{5,4},{6,7},{7,6},{8,9},{9,8},{10,11... | collective-permute-start | bytes 1572872 | tf_op jit(solution)/shard_map/ppermute | solution.py:163
  41.4 2.1 %fusion.24 = (bf16[4096,128]{1,0:T(8,128)(2,1)S(1)}, bf16[4096,128]{1,0:T(8,128)(2,1)S(1)}) fusion(f32[4096]{0:T(1024)S(1)} %bitcast.41, bf16[1,8192,128]{2,1,0:T(8,128)(2,1)S(1)} %copy-done.12, f32[4096]{0:T(1024)S(1)} %bitcast.42), kind=kLoop, calls=%fused_computation.31 | loop fusion | flops 3145728 | bytes 4227072 | tf_op jit(solution)/shard_map/convert_element_type | solution.py:233
  43.5 1.7 collective-permute-start.21
  45.3 1.5 collective-permute-start.20
  49.7 5.2 %collective-permute-start.5 = (bf16[1024,512]{1,0:T(8,128)(2,1)S(1)}, bf16[1024,512]{1,0:T(8,128)(2,1)S(1)}, u32[]{:S(2)}, u32[]{:S(2)}) collective-permute-start(bf16[1024,512]{1,0:T(8,128)(2,1)S(1)} %join_cores.3.refs_1_), channel_id=1, source_target_pairs={{0,2},{2,4},{3,1},{4,6},{5,3},{7,5},{8,10},{10,12},{11,9},{12,14},... | collective-permute-start | bytes 3145736 | tf_op jit(solution)/shard_map/ppermute | solution.py:166
  54.9 4.1 %collective-permute-start.15 = (bf16[1024,256]{1,0:T(8,128)(2,1)S(1)}, bf16[1024,256]{1,0:T(8,128)(2,1)S(1)}, u32[]{:S(2)}, u32[]{:S(2)}) collective-permute-start(bf16[1024,256]{1,0:T(8,128)(2,1)S(1)} %collective-permute-done.14), channel_id=1, source_target_pairs={{0,1},{1,0},{2,3},{3,2},{4,5},{5,4},{6,7},{7,6},{8,9},{9,8},{10,11... | collective-permute-start | bytes 1572872 | tf_op jit(solution)/shard_map/ppermute | solution.py:163
  59.3 1.3 collective-permute-done.15
  61.4 17.1 %fusion.26.refs_0_ = bf16[1024,512]{1,0:T(8,128)(2,1)S(1)} fusion(bf16[1024,4096]{1,0:T(8,128)(2,1)S(1)} %get-tuple-element.12.refs_1_, bf16[1024,256]{1,0:T(8,128)(2,1)S(1)} %broadcast_select_fusion.3, bf16[1024,256]{1,0:T(8,128)(2,1)S(1)} %broadcast_select_fusion.4, bf16[1024,256]{1,0:T(8,128)(2,1)S(1)} %broadcast_select_fusion.5, ...), kind=kOutput, calls=%fused_computation.42 | convolution fusion | flops 4329046016 | bytes 13631488 | tf_op jit(solution)/shard_map/dot_general | solution.py:245
  79.8 8.2 %convolution_convert_fusion.refs_0_ = bf16[512,4096]{1,0:T(8,128)(2,1)S(1)} fusion(bf16[1024,512]{1,0:T(8,128)(2,1)S(1)} %fence.8.refs_1_, bf16[1024,4096]{1,0:T(8,128)(2,1)} %copy-done.6), kind=kOutput, calls=%fused_computation | convolution fusion | flops 4297064448 | bytes 13631488 | tf_op jit(solution)/shard_map/dot_general | solution.py:170
  88.9 6.5 %collective-permute-start.24 = (bf16[512,1024]{1,0:T(8,128)(2,1)S(1)}, bf16[512,1024]{1,0:T(8,128)(2,1)S(1)}, u32[]{:S(2)}, u32[]{:S(2)}) collective-permute-start(bf16[512,1024]{1,0:T(8,128)(2,1)S(1)} %get-tuple-element.24), channel_id=1, source_target_pairs={{0,1},{1,0},{2,3},{3,2},{4,5},{5,4},{6,7},{7,6},{8,9},{9,8},{10,11... | collective-permute-start | bytes 3145736 | tf_op jit(solution)/shard_map/ppermute | solution.py:163
  96.3 1.2 add_convert_fusion
  99.1 4.4 %collective-permute-start.25 = (bf16[512,1024]{1,0:T(8,128)(2,1)S(1)}, bf16[512,1024]{1,0:T(8,128)(2,1)S(1)}, u32[]{:S(2)}, u32[]{:S(2)}) collective-permute-start(bf16[512,1024]{1,0:T(8,128)(2,1)S(1)} %add_convert_fusion.4), channel_id=1, source_target_pairs={{0,2},{7,5},{8,10},{15,13},{16,18},{23,21},{24,26},{31,29}} | collective-permute-start | bytes 3145736 | tf_op jit(solution)/shard_map/ppermute | solution.py:166
  103.5 7.4 %collective-permute-start.8 = (bf16[1024,512]{1,0:T(8,128)(2,1)S(1)}, bf16[1024,512]{1,0:T(8,128)(2,1)S(1)}, u32[]{:S(2)}, u32[]{:S(2)}) collective-permute-start(bf16[1024,512]{1,0:T(8,128)(2,1)S(1)} %collective-permute-done.7), channel_id=1, source_target_pairs={{0,1},{1,0},{2,3},{3,2},{4,5},{5,4},{6,7},{7,6},{8,9},{9,8},{10,11... | collective-permute-start | bytes 3145736 | tf_op jit(solution)/shard_map/ppermute | solution.py:163
  110.9 1.2 add_convert_fusion.1
  112.2 1.4 collective-permute-start.44
  113.7 1.6 collective-permute-start.43
  116.4 4.5 %collective-permute-start.26 = (bf16[512,1024]{1,0:T(8,128)(2,1)S(1)}, bf16[512,1024]{1,0:T(8,128)(2,1)S(1)}, u32[]{:S(2)}, u32[]{:S(2)}) collective-permute-start(bf16[512,1024]{1,0:T(8,128)(2,1)S(1)} %add_convert_fusion.3), channel_id=1, source_target_pairs={{0,2},{2,4},{5,3},{7,5},{8,10},{10,12},{13,11},{15,13},{16,18},{18... | collective-permute-start | bytes 3145736 | tf_op jit(solution)/shard_map/ppermute | solution.py:166
  121.0 7.9 %fusion.29.refs_0_ = bf16[1024,512]{1,0:T(8,128)(2,1)S(1)} fusion(bf16[1024,4096]{1,0:T(8,128)(2,1)} %copy-done.6, bf16[1024,512]{1,0:T(8,128)(2,1)S(1)} %broadcast_select_fusion, bf16[1024,512]{1,0:T(8,128)(2,1)S(1)} %broadcast_select_fusion.1, bf16[1024,512]{1,0:T(8,128)(2,1)S(1)} %broadcast_select_fusion.2, bf16[1024,512]{1,0:T(8,128)(2,1)S(1)} %join_cores.3.refs_1_), kind=kOutput, calls=%fused_computation.43 | convolution fusion | flops 4312268800 | bytes 13631488 | tf_op jit(solution)/shard_map/dot_general | solution.py:252
  128.9 4.2 %collective-permute-done.26 = bf16[512,1024]{1,0:T(8,128)(2,1)S(1)} collective-permute-done((bf16[512,1024]{1,0:T(8,128)(2,1)S(1)}, bf16[512,1024]{1,0:T(8,128)(2,1)S(1)}, u32[]{:S(2)}, u32[]{:S(2)}) %collective-permute-start.26) | collective-permute-done | bytes 1048608 | tf_op jit(solution)/shard_map/ppermute | solution.py:166
  134.3 2.5 %convolution_convert_fusion.1 = bf16[256,4096]{1,0:T(8,128)(2,1)S(1)} fusion(bf16[1024,4096]{1,0:T(8,128)(2,1)S(1)} %get-tuple-element.12.refs_1_, bf16[1024,512]{1,0:T(8,128)(2,1)S(1)} %fence.10.refs_2_), kind=kOutput, calls=%fused_computation.1 | convolution fusion | flops 2148532224 | bytes 11010048 | tf_op jit(solution)/shard_map/dot_general | solution.py:170
  136.9 2.5 %convolution_convert_fusion.2 = bf16[256,4096]{1,0:T(8,128)(2,1)S(1)} fusion(bf16[1024,4096]{1,0:T(8,128)(2,1)S(1)} %get-tuple-element.12.refs_1_, bf16[1024,512]{1,0:T(8,128)(2,1)S(1)} %fence.10.refs_2_), kind=kOutput, calls=%fused_computation.2 | convolution fusion | flops 2148532224 | bytes 11010048 | tf_op jit(solution)/shard_map/dot_general | solution.py:170
  139.4 1.3 fusion.41
  140.7 1.3 fusion.42
  142.4 7.0 %collective-permute-start.41 = (bf16[512,1024]{1,0:T(8,128)(2,1)}, bf16[512,1024]{1,0:T(8,128)(2,1)}, u32[]{:S(2)}, u32[]{:S(2)}) collective-permute-start(bf16[512,1024]{1,0:T(8,128)(2,1)} %copy-done.1), channel_id=1, source_target_pairs={{0,2},{2,4},{3,1},{4,6},{5,3},{7,5},{8,10},{10,12},{11,9},{12,14},... | collective-permute-start | bytes 3145736 | tf_op jit(solution)/shard_map/ppermute | solution.py:166
  149.4 1.4 add_convert_fusion.10.refs_3_
  151.4 1.4 add_convert_fusion.7.refs_4_
  152.8 3.5 %collective-permute-start.30 = (bf16[256,1024]{1,0:T(8,128)(2,1)S(1)}, bf16[256,1024]{1,0:T(8,128)(2,1)}, u32[]{:S(2)}, u32[]{:S(2)}) collective-permute-start(bf16[256,1024]{1,0:T(8,128)(2,1)S(1)} %add_convert_fusion.10.refs_3_), channel_id=1, source_target_pairs={{0,2},{7,5},{8,10},{15,13},{16,18},{23,21},{24,26},{31,29}} | collective-permute-start | bytes 1572872 | tf_op jit(solution)/shard_map/ppermute | solution.py:166
  156.3 2.1 %collective-permute-start.37 = (bf16[256,1024]{1,0:T(8,128)(2,1)S(1)}, bf16[256,1024]{1,0:T(8,128)(2,1)}, u32[]{:S(2)}, u32[]{:S(2)}) collective-permute-start(bf16[256,1024]{1,0:T(8,128)(2,1)S(1)} %add_convert_fusion.7.refs_4_), channel_id=1, source_target_pairs={{0,2},{7,5},{8,10},{15,13},{16,18},{23,21},{24,26},{31,29}} | collective-permute-start | bytes 1572872 | tf_op jit(solution)/shard_map/ppermute | solution.py:166
  159.0 2.1 %convert_add_fusion = (f32[4096,128]{1,0:T(8,128)S(1)}, f32[4096,128]{1,0:T(8,128)S(1)}) fusion(bf16[4096,128]{1,0:T(8,128)(2,1)S(1)} %get-tuple-element.15, bf16[4096,128]{1,0:T(8,128)(2,1)} %add_convert_fusion, bf16[4096,128]{1,0:T(8,128)(2,1)S(1)} %get-tuple-element.14, bf16[4096,128]{1,0:T(8,128)(2,1)} %add_convert_fusion.1), kind=kLoop, calls=%fused_computation.34 | loop fusion | flops 3145728 | bytes 8388608 | tf_op jit(solution)/shard_map/add | solution.py:262
  162.5 3.9 %subtract_convert_fusion = (bf16[8192,128]{1,0:T(8,128)(2,1)}, f32[8192,128]{1,0:T(8,128)}) fusion(bf16[8192,128]{1,0:T(8,128)(2,1)S(1)} %copy-done.13, f32[4096,128]{1,0:T(8,128)S(1)} %get-tuple-element.35, f32[4096,128]{1,0:T(8,128)S(1)} %get-tuple-element.36, f32[8192,128]{1,0:T(8,128)S(1)} %copy-done.11), kind=kLoop, calls=%fused_computation.28 | loop fusion | flops 10485760 | bytes 16777216 | tf_op jit(solution)/shard_map/convert_element_type | solution.py:132
  166.9 1.5 add_convert_fusion.9
  168.4 4.1 %collective-permute-start.31 = (bf16[256,1024]{1,0:T(8,128)(2,1)S(1)}, bf16[256,1024]{1,0:T(8,128)(2,1)S(1)}, u32[]{:S(2)}, u32[]{:S(2)}) collective-permute-start(bf16[256,1024]{1,0:T(8,128)(2,1)S(1)} %add_convert_fusion.9), channel_id=1, source_target_pairs={{0,2},{2,4},{5,3},{7,5},{8,10},{10,12},{13,11},{15,13},{16,18},{18... | collective-permute-start | bytes 1572872 | tf_op jit(solution)/shard_map/ppermute | solution.py:166
  172.5 1.5 add_convert_fusion.6
  174.0 4.1 %collective-permute-start.38 = (bf16[256,1024]{1,0:T(8,128)(2,1)S(1)}, bf16[256,1024]{1,0:T(8,128)(2,1)S(1)}, u32[]{:S(2)}, u32[]{:S(2)}) collective-permute-start(bf16[256,1024]{1,0:T(8,128)(2,1)S(1)} %add_convert_fusion.6), channel_id=1, source_target_pairs={{0,2},{2,4},{5,3},{7,5},{8,10},{10,12},{13,11},{15,13},{16,18},{18... | collective-permute-start | bytes 1572872 | tf_op jit(solution)/shard_map/ppermute | solution.py:166
  178.1 1.9 convert_add_fusion.2
  180.4 3.5 %collective-permute-start.32 = (bf16[256,1024]{1,0:T(8,128)(2,1)S(1)}, bf16[256,1024]{1,0:T(8,128)(2,1)S(1)}, u32[]{:S(2)}, u32[]{:S(2)}) collective-permute-start(bf16[256,1024]{1,0:T(8,128)(2,1)S(1)} %add_convert_fusion.8), channel_id=1, source_target_pairs={{0,2},{2,4},{3,1},{4,6},{5,3},{7,5},{8,10},{10,12},{11,9},{12,14},... | collective-permute-start | bytes 1572872 | tf_op jit(solution)/shard_map/ppermute | solution.py:166
  185.1 4.4 %collective-permute-start.39 = (bf16[256,1024]{1,0:T(8,128)(2,1)S(1)}, bf16[256,1024]{1,0:T(8,128)(2,1)S(1)}, u32[]{:S(2)}, u32[]{:S(2)}) collective-permute-start(bf16[256,1024]{1,0:T(8,128)(2,1)S(1)} %add_convert_fusion.5), channel_id=1, source_target_pairs={{0,2},{2,4},{3,1},{4,6},{5,3},{7,5},{8,10},{10,12},{11,9},{12,14},... | collective-permute-start | bytes 1572872 | tf_op jit(solution)/shard_map/ppermute | solution.py:166
  191.5 4.7 %collective-permute-done.39 = bf16[256,1024]{1,0:T(8,128)(2,1)S(1)} collective-permute-done((bf16[256,1024]{1,0:T(8,128)(2,1)S(1)}, bf16[256,1024]{1,0:T(8,128)(2,1)S(1)}, u32[]{:S(2)}, u32[]{:S(2)}) %collective-permute-start.39) | collective-permute-done | bytes 524320 | tf_op jit(solution)/shard_map/ppermute | solution.py:166
  197.4 1.3 copy.21
  199.0 1.1 add_bitcast_fusion.1
  200.1 1.3 copy.20
  (129 shorter events, 26.4 us)
Async XLA Ops:
  1.4 2.2 %collective-permute-start = (bf16[512,512]{1,0:T(8,128)(2,1)}, bf16[512,512]{1,0:T(8,128)(2,1)S(1)}, u32[]{:S(2)}, u32[]{:S(2)}) collective-permute-start(bf16[512,512]{1,0:T(8,128)(2,1)} %bitcast.36), channel_id=1, source_target_pairs={{0,1},{1,0},{2,3},{3,2},{4,5},{5,4},{6,7},{7,6},{8,9},{9,8},{10,11... | collective-permute-start | bytes 1572872 | tf_op jit(solution)/shard_map/ppermute | solution.py:163
  1.8 2.5 %collective-permute-start.1 = (bf16[512,512]{1,0:T(8,128)(2,1)}, bf16[512,512]{1,0:T(8,128)(2,1)S(1)}, u32[]{:S(2)}, u32[]{:S(2)}) collective-permute-start(bf16[512,512]{1,0:T(8,128)(2,1)} %bitcast.38), channel_id=1, source_target_pairs={{0,1},{1,0},{2,3},{3,2},{4,5},{5,4},{6,7},{7,6},{8,9},{9,8},{10,11... | collective-permute-start | bytes 1572872 | tf_op jit(solution)/shard_map/ppermute | solution.py:163
  6.1 23.4 %collective-permute-start.12 = (bf16[1024,256]{1,0:T(8,128)(2,1)S(1)}, bf16[1024,256]{1,0:T(8,128)(2,1)S(1)}, u32[]{:S(2)}, u32[]{:S(2)}) collective-permute-start(bf16[1024,256]{1,0:T(8,128)(2,1)S(1)} %get-tuple-element.13), channel_id=1, source_target_pairs={{0,2},{2,4},{3,1},{4,6},{5,3},{7,5},{8,10},{10,12},{11,9},{12,14},... | collective-permute-start | bytes 1572872 | tf_op jit(solution)/shard_map/ppermute | solution.py:166
  10.9 17.1 %collective-permute-start.2 = (bf16[1024,256]{1,0:T(8,128)(2,1)S(1)}, bf16[1024,256]{1,0:T(8,128)(2,1)S(1)}, u32[]{:S(2)}, u32[]{:S(2)}) collective-permute-start(bf16[1024,256]{1,0:T(8,128)(2,1)S(1)} %get-tuple-element.10.refs_3_), channel_id=1, source_target_pairs={{0,2},{2,4},{3,1},{4,6},{5,3},{7,5},{8,10},{10,12},{11,9},{12,14},... | collective-permute-start | bytes 1572872 | tf_op jit(solution)/shard_map/ppermute | solution.py:166
  27.5 31.8 %copy-start.6 = (bf16[1024,4096]{1,0:T(8,128)(2,1)}, bf16[1024,4096]{1,0:T(8,128)(2,1)S(1)}, u32[]{:S(2)}) copy-start(bf16[1024,4096]{1,0:T(8,128)(2,1)S(1)} %get-tuple-element.11) | copy-start | bytes 25165828
  28.0 19.5 %copy-start.4 = (bf16[1,512,512]{2,1,0:T(8,128)(2,1)S(1)}, bf16[1,512,512]{2,1,0:T(8,128)(2,1)}, u32[]{:S(2)}) copy-start(bf16[1,512,512]{2,1,0:T(8,128)(2,1)} %param.12) | copy-start | bytes 1572868
  28.6 1.7 collective-permute-start.3
  29.5 7.0 %collective-permute-start.13 = (bf16[1024,256]{1,0:T(8,128)(2,1)S(1)}, bf16[1024,256]{1,0:T(8,128)(2,1)S(1)}, u32[]{:S(2)}, u32[]{:S(2)}) collective-permute-start(bf16[1024,256]{1,0:T(8,128)(2,1)S(1)} %collective-permute-done.12), channel_id=1, source_target_pairs={{2,4},{3,1},{4,6},{5,3},{10,12},{11,9},{12,14},{13,11},{18,20},{19... | collective-permute-start | bytes 1572872 | tf_op jit(solution)/shard_map/ppermute | solution.py:166
  30.4 18.6 %collective-permute-start.16 = (bf16[1024,256]{1,0:T(8,128)(2,1)S(1)}, bf16[1024,256]{1,0:T(8,128)(2,1)S(1)}, u32[]{:S(2)}, u32[]{:S(2)}) collective-permute-start(bf16[1024,256]{1,0:T(8,128)(2,1)S(1)} %collective-permute-done.3), channel_id=1, source_target_pairs={{0,1},{1,0},{2,3},{3,2},{4,5},{5,4},{6,7},{7,6},{8,9},{9,8},{10,11... | collective-permute-start | bytes 1572872 | tf_op jit(solution)/shard_map/ppermute | solution.py:163
  35.8 11.0 %collective-permute-start.4 = (bf16[1024,256]{1,0:T(8,128)(2,1)S(1)}, bf16[1024,256]{1,0:T(8,128)(2,1)S(1)}, u32[]{:S(2)}, u32[]{:S(2)}) collective-permute-start(bf16[1024,256]{1,0:T(8,128)(2,1)S(1)} %collective-permute-done.3), channel_id=1, source_target_pairs={{3,1},{4,6},{11,9},{12,14},{19,17},{20,22},{27,25},{28,30}} | collective-permute-start | bytes 1572872 | tf_op jit(solution)/shard_map/ppermute | solution.py:166
  36.5 11.7 %collective-permute-start.17 = (bf16[1024,256]{1,0:T(8,128)(2,1)S(1)}, bf16[1024,256]{1,0:T(8,128)(2,1)S(1)}, u32[]{:S(2)}, u32[]{:S(2)}) collective-permute-start(bf16[1024,256]{1,0:T(8,128)(2,1)S(1)} %collective-permute-done.13), channel_id=1, source_target_pairs={{0,1},{1,0},{2,3},{3,2},{4,5},{5,4},{6,7},{7,6},{8,9},{9,8},{10,11... | collective-permute-start | bytes 1572872 | tf_op jit(solution)/shard_map/ppermute | solution.py:163
  43.5 35.7 %collective-permute-start.21 = (bf16[4096,128]{1,0:T(8,128)(2,1)S(1)}, bf16[4096,128]{1,0:T(8,128)(2,1)S(1)}, u32[]{:S(2)}, u32[]{:S(2)}) collective-permute-start(bf16[4096,128]{1,0:T(8,128)(2,1)S(1)} %get-tuple-element.31), channel_id=1, source_target_pairs={{0,16},{8,24},{16,0},{24,8},{1,17},{9,25},{17,1},{25,9},{2,18},{10... | collective-permute-start | bytes 3145736 | tf_op jit(solution)/shard_map/ppermute | solution.py:235
  45.3 34.0 %collective-permute-start.20 = (bf16[4096,128]{1,0:T(8,128)(2,1)S(1)}, bf16[4096,128]{1,0:T(8,128)(2,1)S(1)}, u32[]{:S(2)}, u32[]{:S(2)}) collective-permute-start(bf16[4096,128]{1,0:T(8,128)(2,1)S(1)} %get-tuple-element.32), channel_id=1, source_target_pairs={{0,8},{8,0},{16,24},{24,16},{1,9},{9,1},{17,25},{25,17},{2,10},{10... | collective-permute-start | bytes 3145736 | tf_op jit(solution)/shard_map/ppermute | solution.py:235
  46.8 2.9 %collective-permute-start.19 = (bf16[1024,256]{1,0:T(8,128)(2,1)S(1)}, bf16[1024,256]{1,0:T(8,128)(2,1)S(1)}, u32[]{:S(2)}, u32[]{:S(2)}) collective-permute-start(bf16[1024,256]{1,0:T(8,128)(2,1)S(1)} %collective-permute-done.12), channel_id=1, source_target_pairs={{0,1},{1,0},{2,3},{3,2},{4,5},{5,4},{6,7},{7,6},{8,9},{9,8},{10,11... | collective-permute-start | bytes 1572872 | tf_op jit(solution)/shard_map/ppermute | solution.py:163
  48.2 6.7 %collective-permute-start.14 = (bf16[1024,256]{1,0:T(8,128)(2,1)S(1)}, bf16[1024,256]{1,0:T(8,128)(2,1)S(1)}, u32[]{:S(2)}, u32[]{:S(2)}) collective-permute-start(bf16[1024,256]{1,0:T(8,128)(2,1)S(1)} %collective-permute-done.13), channel_id=1, source_target_pairs={{3,1},{4,6},{11,9},{12,14},{19,17},{20,22},{27,25},{28,30}} | collective-permute-start | bytes 1572872 | tf_op jit(solution)/shard_map/ppermute | solution.py:166
  49.0 10.1 %collective-permute-start.18 = (bf16[1024,256]{1,0:T(8,128)(2,1)S(1)}, bf16[1024,256]{1,0:T(8,128)(2,1)S(1)}, u32[]{:S(2)}, u32[]{:S(2)}) collective-permute-start(bf16[1024,256]{1,0:T(8,128)(2,1)S(1)} %fence.7.refs_2_), channel_id=1, source_target_pairs={{0,1},{1,0},{2,3},{3,2},{4,5},{5,4},{6,7},{7,6},{8,9},{9,8},{10,11... | collective-permute-start | bytes 1572872 | tf_op jit(solution)/shard_map/ppermute | solution.py:163
  49.7 28.8 %collective-permute-start.5 = (bf16[1024,512]{1,0:T(8,128)(2,1)S(1)}, bf16[1024,512]{1,0:T(8,128)(2,1)S(1)}, u32[]{:S(2)}, u32[]{:S(2)}) collective-permute-start(bf16[1024,512]{1,0:T(8,128)(2,1)S(1)} %join_cores.3.refs_1_), channel_id=1, source_target_pairs={{0,2},{2,4},{3,1},{4,6},{5,3},{7,5},{8,10},{10,12},{11,9},{12,14},... | collective-permute-start | bytes 3145736 | tf_op jit(solution)/shard_map/ppermute | solution.py:166
  54.9 5.7 %collective-permute-start.15 = (bf16[1024,256]{1,0:T(8,128)(2,1)S(1)}, bf16[1024,256]{1,0:T(8,128)(2,1)S(1)}, u32[]{:S(2)}, u32[]{:S(2)}) collective-permute-start(bf16[1024,256]{1,0:T(8,128)(2,1)S(1)} %collective-permute-done.14), channel_id=1, source_target_pairs={{0,1},{1,0},{2,3},{3,2},{4,5},{5,4},{6,7},{7,6},{8,9},{9,8},{10,11... | collective-permute-start | bytes 1572872 | tf_op jit(solution)/shard_map/ppermute | solution.py:163
  59.1 2.2 %collective-permute-start.11 = (bf16[1024,256]{1,0:T(8,128)(2,1)S(1)}, bf16[1024,256]{1,0:T(8,128)(2,1)S(1)}, u32[]{:S(2)}, u32[]{:S(2)}) collective-permute-start(bf16[1024,256]{1,0:T(8,128)(2,1)S(1)} %collective-permute-done.4.refs_3_), channel_id=1, source_target_pairs={{0,1},{1,0},{2,3},{3,2},{4,5},{5,4},{6,7},{7,6},{8,9},{9,8},{10,11... | collective-permute-start | bytes 1572872 | tf_op jit(solution)/shard_map/ppermute | solution.py:163
  78.5 9.5 %collective-permute-start.6 = (bf16[1024,512]{1,0:T(8,128)(2,1)S(1)}, bf16[1024,512]{1,0:T(8,128)(2,1)S(1)}, u32[]{:S(2)}, u32[]{:S(2)}) collective-permute-start(bf16[1024,512]{1,0:T(8,128)(2,1)S(1)} %collective-permute-done.5.refs_2_), channel_id=1, source_target_pairs={{2,4},{3,1},{4,6},{5,3},{10,12},{11,9},{12,14},{13,11},{18,20},{19... | collective-permute-start | bytes 3145736 | tf_op jit(solution)/shard_map/ppermute | solution.py:166
  88.6 45.1 %copy-start = (bf16[512,4096]{1,0:T(8,128)(2,1)}, bf16[512,4096]{1,0:T(8,128)(2,1)S(1)}, u32[]{:S(2)}) copy-start(bf16[512,4096]{1,0:T(8,128)(2,1)S(1)} %fence.9.refs_1_) | copy-start | bytes 12582916
  88.9 9.8 %collective-permute-start.24 = (bf16[512,1024]{1,0:T(8,128)(2,1)S(1)}, bf16[512,1024]{1,0:T(8,128)(2,1)S(1)}, u32[]{:S(2)}, u32[]{:S(2)}) collective-permute-start(bf16[512,1024]{1,0:T(8,128)(2,1)S(1)} %get-tuple-element.24), channel_id=1, source_target_pairs={{0,1},{1,0},{2,3},{3,2},{4,5},{5,4},{6,7},{7,6},{8,9},{9,8},{10,11... | collective-permute-start | bytes 3145736 | tf_op jit(solution)/shard_map/ppermute | solution.py:163
  95.4 8.1 %collective-permute-start.7 = (bf16[1024,512]{1,0:T(8,128)(2,1)S(1)}, bf16[1024,512]{1,0:T(8,128)(2,1)S(1)}, u32[]{:S(2)}, u32[]{:S(2)}) collective-permute-start(bf16[1024,512]{1,0:T(8,128)(2,1)S(1)} %collective-permute-done.6.refs_2_), channel_id=1, source_target_pairs={{3,1},{4,6},{11,9},{12,14},{19,17},{20,22},{27,25},{28,30}} | collective-permute-start | bytes 3145736 | tf_op jit(solution)/shard_map/ppermute | solution.py:166
  97.6 16.1 %collective-permute-start.10 = (bf16[1024,512]{1,0:T(8,128)(2,1)S(1)}, bf16[1024,512]{1,0:T(8,128)(2,1)S(1)}, u32[]{:S(2)}, u32[]{:S(2)}) collective-permute-start(bf16[1024,512]{1,0:T(8,128)(2,1)S(1)} %collective-permute-done.5.refs_2_), channel_id=1, source_target_pairs={{0,1},{1,0},{2,3},{3,2},{4,5},{5,4},{6,7},{7,6},{8,9},{9,8},{10,11... | collective-permute-start | bytes 3145736 | tf_op jit(solution)/shard_map/ppermute | solution.py:163
  98.2 17.3 %collective-permute-start.23 = (bf16[512,1024]{1,0:T(8,128)(2,1)S(1)}, bf16[512,1024]{1,0:T(8,128)(2,1)S(1)}, u32[]{:S(2)}, u32[]{:S(2)}) collective-permute-start(bf16[512,1024]{1,0:T(8,128)(2,1)S(1)} %get-tuple-element.23), channel_id=1, source_target_pairs={{0,1},{1,0},{2,3},{3,2},{4,5},{5,4},{6,7},{7,6},{8,9},{9,8},{10,11... | collective-permute-start | bytes 3145736 | tf_op jit(solution)/shard_map/ppermute | solution.py:163
  98.2 14.0 %collective-permute-start.9 = (bf16[1024,512]{1,0:T(8,128)(2,1)S(1)}, bf16[1024,512]{1,0:T(8,128)(2,1)S(1)}, u32[]{:S(2)}, u32[]{:S(2)}) collective-permute-start(bf16[1024,512]{1,0:T(8,128)(2,1)S(1)} %collective-permute-done.6.refs_2_), channel_id=1, source_target_pairs={{0,1},{1,0},{2,3},{3,2},{4,5},{5,4},{6,7},{7,6},{8,9},{9,8},{10,11... | collective-permute-start | bytes 3145736 | tf_op jit(solution)/shard_map/ppermute | solution.py:163
  99.1 16.6 %collective-permute-start.25 = (bf16[512,1024]{1,0:T(8,128)(2,1)S(1)}, bf16[512,1024]{1,0:T(8,128)(2,1)S(1)}, u32[]{:S(2)}, u32[]{:S(2)}) collective-permute-start(bf16[512,1024]{1,0:T(8,128)(2,1)S(1)} %add_convert_fusion.4), channel_id=1, source_target_pairs={{0,2},{7,5},{8,10},{15,13},{16,18},{23,21},{24,26},{31,29}} | collective-permute-start | bytes 3145736 | tf_op jit(solution)/shard_map/ppermute | solution.py:166
  103.5 17.3 %collective-permute-start.8 = (bf16[1024,512]{1,0:T(8,128)(2,1)S(1)}, bf16[1024,512]{1,0:T(8,128)(2,1)S(1)}, u32[]{:S(2)}, u32[]{:S(2)}) collective-permute-start(bf16[1024,512]{1,0:T(8,128)(2,1)S(1)} %collective-permute-done.7), channel_id=1, source_target_pairs={{0,1},{1,0},{2,3},{3,2},{4,5},{5,4},{6,7},{7,6},{8,9},{9,8},{10,11... | collective-permute-start | bytes 3145736 | tf_op jit(solution)/shard_map/ppermute | solution.py:163
  112.2 40.6 %collective-permute-start.44 = (bf16[4096,128]{1,0:T(8,128)(2,1)}, bf16[4096,128]{1,0:T(8,128)(2,1)S(1)}, u32[]{:S(2)}, u32[]{:S(2)}) collective-permute-start(bf16[4096,128]{1,0:T(8,128)(2,1)} %add_convert_fusion), channel_id=1, source_target_pairs={{0,8},{8,0},{16,24},{24,16},{1,9},{9,1},{17,25},{25,17},{2,10},{10... | collective-permute-start | bytes 3145736 | tf_op jit(solution)/shard_map/ppermute | solution.py:235
  113.7 42.6 %collective-permute-start.43 = (bf16[4096,128]{1,0:T(8,128)(2,1)}, bf16[4096,128]{1,0:T(8,128)(2,1)S(1)}, u32[]{:S(2)}, u32[]{:S(2)}) collective-permute-start(bf16[4096,128]{1,0:T(8,128)(2,1)} %add_convert_fusion.1), channel_id=1, source_target_pairs={{0,16},{8,24},{16,0},{24,8},{1,17},{9,25},{17,1},{25,9},{2,18},{10... | collective-permute-start | bytes 3145736 | tf_op jit(solution)/shard_map/ppermute | solution.py:235
  115.4 13.4 %collective-permute-start.22 = (bf16[512,1024]{1,0:T(8,128)(2,1)S(1)}, bf16[512,1024]{1,0:T(8,128)(2,1)S(1)}, u32[]{:S(2)}, u32[]{:S(2)}) collective-permute-start(bf16[512,1024]{1,0:T(8,128)(2,1)S(1)} %get-tuple-element.22), channel_id=1, source_target_pairs={{0,1},{1,0},{2,3},{3,2},{4,5},{5,4},{6,7},{7,6},{8,9},{9,8},{10,11... | collective-permute-start | bytes 3145736 | tf_op jit(solution)/shard_map/ppermute | solution.py:163
  116.4 16.7 %collective-permute-start.26 = (bf16[512,1024]{1,0:T(8,128)(2,1)S(1)}, bf16[512,1024]{1,0:T(8,128)(2,1)S(1)}, u32[]{:S(2)}, u32[]{:S(2)}) collective-permute-start(bf16[512,1024]{1,0:T(8,128)(2,1)S(1)} %add_convert_fusion.3), channel_id=1, source_target_pairs={{0,2},{2,4},{5,3},{7,5},{8,10},{10,12},{13,11},{15,13},{16,18},{18... | collective-permute-start | bytes 3145736 | tf_op jit(solution)/shard_map/ppermute | solution.py:166
  140.7 8.7 %collective-permute-start.29 = (bf16[256,1024]{1,0:T(8,128)(2,1)}, bf16[256,1024]{1,0:T(8,128)(2,1)}, u32[]{:S(2)}, u32[]{:S(2)}) collective-permute-start(bf16[256,1024]{1,0:T(8,128)(2,1)} %get-tuple-element.27), channel_id=1, source_target_pairs={{0,1},{1,0},{2,3},{3,2},{4,5},{5,4},{6,7},{7,6},{8,9},{9,8},{10,11... | collective-permute-start | bytes 1572872 | tf_op jit(solution)/shard_map/ppermute | solution.py:163
  141.9 8.8 %collective-permute-start.36 = (bf16[256,1024]{1,0:T(8,128)(2,1)}, bf16[256,1024]{1,0:T(8,128)(2,1)}, u32[]{:S(2)}, u32[]{:S(2)}) collective-permute-start(bf16[256,1024]{1,0:T(8,128)(2,1)} %get-tuple-element.30), channel_id=1, source_target_pairs={{0,1},{1,0},{2,3},{3,2},{4,5},{5,4},{6,7},{7,6},{8,9},{9,8},{10,11... | collective-permute-start | bytes 1572872 | tf_op jit(solution)/shard_map/ppermute | solution.py:163
  142.4 35.8 %collective-permute-start.41 = (bf16[512,1024]{1,0:T(8,128)(2,1)}, bf16[512,1024]{1,0:T(8,128)(2,1)}, u32[]{:S(2)}, u32[]{:S(2)}) collective-permute-start(bf16[512,1024]{1,0:T(8,128)(2,1)} %copy-done.1), channel_id=1, source_target_pairs={{0,2},{2,4},{3,1},{4,6},{5,3},{7,5},{8,10},{10,12},{11,9},{12,14},... | collective-permute-start | bytes 3145736 | tf_op jit(solution)/shard_map/ppermute | solution.py:166
  149.4 17.0 %collective-permute-start.28 = (bf16[256,1024]{1,0:T(8,128)(2,1)}, bf16[256,1024]{1,0:T(8,128)(2,1)}, u32[]{:S(2)}, u32[]{:S(2)}) collective-permute-start(bf16[256,1024]{1,0:T(8,128)(2,1)} %get-tuple-element.26), channel_id=1, source_target_pairs={{0,1},{1,0},{2,3},{3,2},{4,5},{5,4},{6,7},{7,6},{8,9},{9,8},{10,11... | collective-permute-start | bytes 1572872 | tf_op jit(solution)/shard_map/ppermute | solution.py:163
  150.8 17.6 %collective-permute-start.35 = (bf16[256,1024]{1,0:T(8,128)(2,1)}, bf16[256,1024]{1,0:T(8,128)(2,1)}, u32[]{:S(2)}, u32[]{:S(2)}) collective-permute-start(bf16[256,1024]{1,0:T(8,128)(2,1)} %get-tuple-element.29), channel_id=1, source_target_pairs={{0,1},{1,0},{2,3},{3,2},{4,5},{5,4},{6,7},{7,6},{8,9},{9,8},{10,11... | collective-permute-start | bytes 1572872 | tf_op jit(solution)/shard_map/ppermute | solution.py:163
  152.8 13.7 %collective-permute-start.30 = (bf16[256,1024]{1,0:T(8,128)(2,1)S(1)}, bf16[256,1024]{1,0:T(8,128)(2,1)}, u32[]{:S(2)}, u32[]{:S(2)}) collective-permute-start(bf16[256,1024]{1,0:T(8,128)(2,1)S(1)} %add_convert_fusion.10.refs_3_), channel_id=1, source_target_pairs={{0,2},{7,5},{8,10},{15,13},{16,18},{23,21},{24,26},{31,29}} | collective-permute-start | bytes 1572872 | tf_op jit(solution)/shard_map/ppermute | solution.py:166
  156.3 16.3 %collective-permute-start.37 = (bf16[256,1024]{1,0:T(8,128)(2,1)S(1)}, bf16[256,1024]{1,0:T(8,128)(2,1)}, u32[]{:S(2)}, u32[]{:S(2)}) collective-permute-start(bf16[256,1024]{1,0:T(8,128)(2,1)S(1)} %add_convert_fusion.7.refs_4_), channel_id=1, source_target_pairs={{0,2},{7,5},{8,10},{15,13},{16,18},{23,21},{24,26},{31,29}} | collective-permute-start | bytes 1572872 | tf_op jit(solution)/shard_map/ppermute | solution.py:166
  166.4 13.7 %collective-permute-start.27 = (bf16[256,1024]{1,0:T(8,128)(2,1)S(1)}, bf16[256,1024]{1,0:T(8,128)(2,1)S(1)}, u32[]{:S(2)}, u32[]{:S(2)}) collective-permute-start(bf16[256,1024]{1,0:T(8,128)(2,1)S(1)} %copy-done.15), channel_id=1, source_target_pairs={{0,1},{1,0},{2,3},{3,2},{4,5},{5,4},{6,7},{7,6},{8,9},{9,8},{10,11... | collective-permute-start | bytes 1572872 | tf_op jit(solution)/shard_map/ppermute | solution.py:163
  166.5 17.4 %collective-permute-start.34 = (bf16[256,1024]{1,0:T(8,128)(2,1)S(1)}, bf16[256,1024]{1,0:T(8,128)(2,1)S(1)}, u32[]{:S(2)}, u32[]{:S(2)}) collective-permute-start(bf16[256,1024]{1,0:T(8,128)(2,1)S(1)} %copy-done.14), channel_id=1, source_target_pairs={{0,1},{1,0},{2,3},{3,2},{4,5},{5,4},{6,7},{7,6},{8,9},{9,8},{10,11... | collective-permute-start | bytes 1572872 | tf_op jit(solution)/shard_map/ppermute | solution.py:163
  168.4 11.7 %collective-permute-start.31 = (bf16[256,1024]{1,0:T(8,128)(2,1)S(1)}, bf16[256,1024]{1,0:T(8,128)(2,1)S(1)}, u32[]{:S(2)}, u32[]{:S(2)}) collective-permute-start(bf16[256,1024]{1,0:T(8,128)(2,1)S(1)} %add_convert_fusion.9), channel_id=1, source_target_pairs={{0,2},{2,4},{5,3},{7,5},{8,10},{10,12},{13,11},{15,13},{16,18},{18... | collective-permute-start | bytes 1572872 | tf_op jit(solution)/shard_map/ppermute | solution.py:166
  174.0 10.8 %collective-permute-start.38 = (bf16[256,1024]{1,0:T(8,128)(2,1)S(1)}, bf16[256,1024]{1,0:T(8,128)(2,1)S(1)}, u32[]{:S(2)}, u32[]{:S(2)}) collective-permute-start(bf16[256,1024]{1,0:T(8,128)(2,1)S(1)} %add_convert_fusion.6), channel_id=1, source_target_pairs={{0,2},{2,4},{5,3},{7,5},{8,10},{10,12},{13,11},{15,13},{16,18},{18... | collective-permute-start | bytes 1572872 | tf_op jit(solution)/shard_map/ppermute | solution.py:166
  180.4 10.2 %collective-permute-start.32 = (bf16[256,1024]{1,0:T(8,128)(2,1)S(1)}, bf16[256,1024]{1,0:T(8,128)(2,1)S(1)}, u32[]{:S(2)}, u32[]{:S(2)}) collective-permute-start(bf16[256,1024]{1,0:T(8,128)(2,1)S(1)} %add_convert_fusion.8), channel_id=1, source_target_pairs={{0,2},{2,4},{3,1},{4,6},{5,3},{7,5},{8,10},{10,12},{11,9},{12,14},... | collective-permute-start | bytes 1572872 | tf_op jit(solution)/shard_map/ppermute | solution.py:166
  185.1 11.1 %collective-permute-start.39 = (bf16[256,1024]{1,0:T(8,128)(2,1)S(1)}, bf16[256,1024]{1,0:T(8,128)(2,1)S(1)}, u32[]{:S(2)}, u32[]{:S(2)}) collective-permute-start(bf16[256,1024]{1,0:T(8,128)(2,1)S(1)} %add_convert_fusion.5), channel_id=1, source_target_pairs={{0,2},{2,4},{3,1},{4,6},{5,3},{7,5},{8,10},{10,12},{11,9},{12,14},... | collective-permute-start | bytes 1572872 | tf_op jit(solution)/shard_map/ppermute | solution.py:166
  189.6 7.5 %collective-permute-start.42 = (bf16[512,512]{1,0:T(8,128)(2,1)S(1)}, bf16[512,512]{1,0:T(8,128)(2,1)S(1)}, u32[]{:S(2)}, u32[]{:S(2)}) collective-permute-start(bf16[512,512]{1,0:T(8,128)(2,1)S(1)} %select_convert_fusion), channel_id=1, source_target_pairs={{0,1},{1,0},{2,3},{3,2},{4,5},{5,4},{6,7},{7,6},{8,9},{9,8},{10,11... | collective-permute-start | bytes 1572872 | tf_op jit(solution)/shard_map/ppermute | solution.py:163
  191.4 7.2 %collective-permute-start.33 = (bf16[256,512]{1,0:T(8,128)(2,1)}, bf16[256,512]{1,0:T(8,128)(2,1)S(1)}, u32[]{:S(2)}, u32[]{:S(2)}) collective-permute-start(bf16[256,512]{1,0:T(8,128)(2,1)} %select_convert_fusion.2), channel_id=1, source_target_pairs={{0,1},{1,0},{2,3},{3,2},{4,5},{5,4},{6,7},{7,6},{8,9},{9,8},{10,11... | collective-permute-start | bytes 786440 | tf_op jit(solution)/shard_map/ppermute | solution.py:163
  197.1 1.9 collective-permute-start.40
  (13 other events, 57.3 us)

commit v8 on v7

--- a/solution.py
+++ b/solution.py
@@ -242,6 +242,7 @@
 
     joined = join_cores(order, second_own, second_partner, 1, (last[0],))
     weight = assemble(pieces, others)
+    weight = fence(order, weight)[0]
     values = jnp.dot(normed, weight, preferred_element_type=f32).astype(bf16)
     pieces, others = gather(joined)
     values = fence(order, values, after=(pieces[1][0], *early))[0]
@@ -249,10 +250,14 @@
     sent = [first.reduce(step) for step in range(1, chips)]
 
     weight = assemble(pieces, others)
+    weight = fence(order, weight)[0]
     mid = jnp.dot(cotangent, weight, preferred_element_type=f32).astype(bf16)
     mid = fence(order, mid, after=(sent[-1],))[0]
     half = mid.shape[1] // HALVES
-    second = [Gradient(mid[:, j * half : (j + 1) * half], normed) for j in range(HALVES)]
+    second = []
+    for j in range(HALVES):
+        after = () if j else ()
+        second.append(Gradient(mid[:, j * half : (j + 1) * half], normed, after))
     for step in range(1, chips):
         sent = tuple(gradient.reduce(step) for gradient in second)
         if step == 1:

time: 202 us -> 210 us (1.040)
  matrix products: 38.2 us -> 19 us
  other arithmetic: 24.7 us -> 40.2 us
  local copies, waits for them, and re-layouts: 12.8 us -> 19.5 us
  starting transfers between devices: 95.1 us -> 98.6 us
    concatenate x0 -> x2, other arithmetic: none -> 15.4 us  [assemble(): return jnp.concatenate(shards, axis=0)]
    dot_general x1, matrix products: 17.1 us -> 4.48 us  [per_device(): values = jnp.dot(normed, weight, preferred_element_type=f32).astype(bf16)]
    unnamed x35 -> x43, local copies, waits for them, and re-layouts: 9.94 us -> 16.5 us
    ppermute x23, starting transfers between devices: 33 us -> 37.1 us  [swap(): return lax.ppermute(value, 'fsdp', [(i, i ^ 1) for i in range(devices)])]
    dot_general x1, matrix products: 7.88 us -> 4.49 us  [per_device(): mid = jnp.dot(cotangent, weight, preferred_element_type=f32).astype(bf16)]
    dot_general x3, matrix products: 13.3 us -> 10.1 us  [__init__(): lax.dot_general(mid, x, (((0,), (0,)), ((), ())), preferred_element_type=...]
    pallas_call x9 -> x11, Pallas kernels: 13.5 us -> 14.5 us  [__call__(): pl.pallas_call(ordered, grid_spec=pltpu.PrefetchScalarGridSpec(num_scalar...]
  transfers between devices with their start and end apart: 45 -> 45, of which waited for: 11 -> 11; matrix products, arithmetic and copies ran while one was open for 33% -> 30% of each run, Pallas kernels for 6% -> 6%
where the time goes in v8:
time: 210 us; the launch traced here: 209 us
  starting transfers between devices  98.6 us (47%)
  other arithmetic  40.2 us (19%)
  local copies, waits for them, and re-layouts  19.5 us (9%)
  matrix products  19 us (9%)
  waiting for transfers between devices  16.1 us (8%)
  Pallas kernels  14.5 us (7%)
    ppermute x18, starting transfers between devices, move(): return lax.ppermute(value, 'fsdp', move_perm(chips, active))  56.2 us
    ppermute x23, starting transfers between devices, swap(): return lax.ppermute(value, 'fsdp', [(i, i ^ 1) for i in range(devices)])  37.1 us
    unnamed x43, local copies, waits for them, and re-layouts  16.5 us
    concatenate x2, other arithmetic, assemble(): return jnp.concatenate(shards, axis=0)  15.4 us
    pallas_call x11, Pallas kernels, __call__(): pl.pallas_call(ordered, grid_spec=pltpu.PrefetchScalarGridSpec(num_scalar...  14.5 us
    ppermute x18, waiting for transfers between devices, move(): return lax.ppermute(value, 'fsdp', move_perm(chips, active))  11.5 us
    dot_general x3, matrix products, __init__(): lax.dot_general(mid, x, (((0,), (0,)), ((), ())), preferred_element_type=...  10.1 us
    convert_element_type x9, other arithmetic, message(): return term.astype(bf16)  7.96 us
  transfers between devices with their start and end apart: 45, of which 11 were waited for; matrix products, arithmetic and copies ran while one was open for 30% of the time, Pallas kernels for 6%

profile of v8, /device:TPU:0, one launch (start us, length us, event | category | flops | bytes accessed | tf_op | source)
XLA Modules:
  0.0 209.4 jit_solution(6253536347095055421)
XLA Ops:
  2.0 1.6 collective-permute-done.1.refs_2_.refs_1_
  6.1 4.9 %collective-permute-start.2 = (bf16[1024,256]{1,0:T(8,128)(2,1)S(1)}, bf16[1024,256]{1,0:T(8,128)(2,1)S(1)}, u32[]{:S(2)}, u32[]{:S(2)}) collective-permute-start(bf16[1024,256]{1,0:T(8,128)(2,1)S(1)} %get-tuple-element.10.refs_3_), channel_id=1, source_target_pairs={{0,2},{2,4},{3,1},{4,6},{5,3},{7,5},{8,10},{10,12},{11,9},{12,14},... | collective-permute-start | bytes 1572872 | tf_op jit(solution)/shard_map/ppermute | solution.py:166
  10.9 3.5 %collective-permute-start.12 = (bf16[1024,256]{1,0:T(8,128)(2,1)S(1)}, bf16[1024,256]{1,0:T(8,128)(2,1)S(1)}, u32[]{:S(2)}, u32[]{:S(2)}) collective-permute-start(bf16[1024,256]{1,0:T(8,128)(2,1)S(1)} %get-tuple-element.13), channel_id=1, source_target_pairs={{0,2},{2,4},{3,1},{4,6},{5,3},{7,5},{8,10},{10,12},{11,9},{12,14},... | collective-permute-start | bytes 1572872 | tf_op jit(solution)/shard_map/ppermute | solution.py:166
  14.4 3.4 %copy-done.2 = bf16[1,1024,4096]{2,1,0:T(8,128)(2,1)S(1)} copy-done((bf16[1,1024,4096]{2,1,0:T(8,128)(2,1)S(1)}, bf16[1,1024,4096]{2,1,0:T(8,128)(2,1)}, u32[]{:S(2)}) %copy-start.2) | copy-done | bytes 8388632
  18.5 8.9 %prepare.1 = (bf16[1024,4096]{1,0:T(8,128)(2,1)S(1)}, bf16[1024,4096]{1,0:T(8,128)(2,1)S(1)}) custom-call(s32[6]{0:T(128)S(1)} %stack.27.place_ref, bf16[1024,4096]{1,0:T(8,128)(2,1)S(1)} %bitcast.37, bf16[1024,4096]{1,0:T(8,128)(2,1)} %bitcast.49, f32[1,4096]{1,0:T(1,128)S(1)} %bitcast.42, bf16[1024,256]{1,0:T(8,128)(2,1)S(1)} %get-tuple-element.10.refs_3_), custom_call_target="tpu_custom_call" | custom-call | flops 20000000000 | bytes 1 | tf_op jit(solution)/shard_map/prepare/pallas_call | solution.py:39
  27.5 3.3 %copy-done.6 = bf16[1024,4096]{1,0:T(8,128)(2,1)} copy-done((bf16[1024,4096]{1,0:T(8,128)(2,1)}, bf16[1024,4096]{1,0:T(8,128)(2,1)S(1)}, u32[]{:S(2)}) %copy-start.6) | copy-done | bytes 8388632
  34.2 5.8 %collective-permute-start.16 = (bf16[1024,256]{1,0:T(8,128)(2,1)S(1)}, bf16[1024,256]{1,0:T(8,128)(2,1)S(1)}, u32[]{:S(2)}, u32[]{:S(2)}) collective-permute-start(bf16[1024,256]{1,0:T(8,128)(2,1)S(1)} %collective-permute-done.3), channel_id=1, source_target_pairs={{0,1},{1,0},{2,3},{3,2},{4,5},{5,4},{6,7},{7,6},{8,9},{9,8},{10,11... | collective-permute-start | bytes 1572872 | tf_op jit(solution)/shard_map/ppermute | solution.py:163
  40.1 2.1 %fusion = (bf16[4096,128]{1,0:T(8,128)(2,1)S(1)}, bf16[4096,128]{1,0:T(8,128)(2,1)S(1)}) fusion(f32[4096]{0:T(1024)S(1)} %bitcast.47, bf16[1,8192,128]{2,1,0:T(8,128)(2,1)S(1)} %copy-done.12, f32[4096]{0:T(1024)S(1)} %bitcast.48), kind=kLoop, calls=%fused_computation.9 | loop fusion | flops 3145728 | bytes 4227072 | tf_op jit(solution)/shard_map/convert_element_type | solution.py:233
  42.2 1.7 collective-permute-start.20
  43.9 1.5 collective-permute-start.21
  46.1 6.3 %collective-permute-start.19 = (bf16[1024,256]{1,0:T(8,128)(2,1)S(1)}, bf16[1024,256]{1,0:T(8,128)(2,1)S(1)}, u32[]{:S(2)}, u32[]{:S(2)}) collective-permute-start(bf16[1024,256]{1,0:T(8,128)(2,1)S(1)} %collective-permute-done.12), channel_id=1, source_target_pairs={{0,1},{1,0},{2,3},{3,2},{4,5},{5,4},{6,7},{7,6},{8,9},{9,8},{10,11... | collective-permute-start | bytes 1572872 | tf_op jit(solution)/shard_map/ppermute | solution.py:163
  53.9 4.4 %collective-permute-start.5 = (bf16[1024,512]{1,0:T(8,128)(2,1)S(1)}, bf16[1024,512]{1,0:T(8,128)(2,1)S(1)}, u32[]{:S(2)}, u32[]{:S(2)}) collective-permute-start(bf16[1024,512]{1,0:T(8,128)(2,1)S(1)} %join_cores.3.refs_1_), channel_id=1, source_target_pairs={{0,2},{2,4},{3,1},{4,6},{5,3},{7,5},{8,10},{10,12},{11,9},{12,14},... | collective-permute-start | bytes 3145736 | tf_op jit(solution)/shard_map/ppermute | solution.py:166
  58.3 4.3 %collective-permute-start.11 = (bf16[1024,256]{1,0:T(8,128)(2,1)S(1)}, bf16[1024,256]{1,0:T(8,128)(2,1)S(1)}, u32[]{:S(2)}, u32[]{:S(2)}) collective-permute-start(bf16[1024,256]{1,0:T(8,128)(2,1)S(1)} %collective-permute-done.4.refs_3_), channel_id=1, source_target_pairs={{0,1},{1,0},{2,3},{3,2},{4,5},{5,4},{6,7},{7,6},{8,9},{9,8},{10,11... | collective-permute-start | bytes 1572872 | tf_op jit(solution)/shard_map/ppermute | solution.py:163
  62.8 1.3 collective-permute-done.11
  64.9 15.1 %maximum_maximum_fusion.refs_0_ = bf16[4096,512]{1,0:T(8,128)(2,1)S(1)} fusion(bf16[1024,256]{1,0:T(8,128)(2,1)S(1)} %broadcast_select_fusion.3, bf16[1024,256]{1,0:T(8,128)(2,1)S(1)} %broadcast_select_fusion.4, bf16[1024,256]{1,0:T(8,128)(2,1)S(1)} %broadcast_select_fusion.5, bf16[1024,256]{1,0:T(8,128)(2,1)S(1)} %broadcast_select_fusion.6, ...), kind=kLoop, calls=%fused_computation.4 | loop fusion | flops 33554432 | bytes 8388608 | tf_op jit(solution)/shard_map/concatenate | solution.py:215
  80.6 4.5 %convolution_convert_fusion.4.refs_0_ = bf16[1024,512]{1,0:T(8,128)(2,1)S(1)} fusion(bf16[1024,4096]{1,0:T(8,128)(2,1)S(1)} %get-tuple-element.12.refs_1_, bf16[4096,512]{1,0:T(8,128)(2,1)S(1)} %fence.10.refs_1_), kind=kOutput, calls=%fused_computation.21 | convolution fusion | flops 4295491584 | bytes 13631488 | tf_op jit(solution)/shard_map/dot_general | solution.py:246
  86.6 5.0 %convolution_convert_fusion.refs_0_ = bf16[512,4096]{1,0:T(8,128)(2,1)S(1)} fusion(bf16[1024,512]{1,0:T(8,128)(2,1)S(1)} %fence.11.refs_1_, bf16[1024,4096]{1,0:T(8,128)(2,1)S(1)} %bitcast.44), kind=kOutput, calls=%fused_computation | convolution fusion | flops 4297064448 | bytes 13631488 | tf_op jit(solution)/shard_map/dot_general | solution.py:170
  92.6 9.5 %collective-permute-start.24 = (bf16[512,1024]{1,0:T(8,128)(2,1)S(1)}, bf16[512,1024]{1,0:T(8,128)(2,1)S(1)}, u32[]{:S(2)}, u32[]{:S(2)}) collective-permute-start(bf16[512,1024]{1,0:T(8,128)(2,1)S(1)} %get-tuple-element.24), channel_id=1, source_target_pairs={{0,1},{1,0},{2,3},{3,2},{4,5},{5,4},{6,7},{7,6},{8,9},{9,8},{10,11... | collective-permute-start | bytes 3145736 | tf_op jit(solution)/shard_map/ppermute | solution.py:163
  102.8 1.2 add_convert_fusion.1
  105.6 5.3 %collective-permute-start.25 = (bf16[512,1024]{1,0:T(8,128)(2,1)S(1)}, bf16[512,1024]{1,0:T(8,128)(2,1)S(1)}, u32[]{:S(2)}, u32[]{:S(2)}) collective-permute-start(bf16[512,1024]{1,0:T(8,128)(2,1)S(1)} %add_convert_fusion.4), channel_id=1, source_target_pairs={{0,2},{7,5},{8,10},{15,13},{16,18},{23,21},{24,26},{31,29}} | collective-permute-start | bytes 3145736 | tf_op jit(solution)/shard_map/ppermute | solution.py:166
  110.9 7.7 %collective-permute-start.8 = (bf16[1024,512]{1,0:T(8,128)(2,1)S(1)}, bf16[1024,512]{1,0:T(8,128)(2,1)S(1)}, u32[]{:S(2)}, u32[]{:S(2)}) collective-permute-start(bf16[1024,512]{1,0:T(8,128)(2,1)S(1)} %collective-permute-done.7), channel_id=1, source_target_pairs={{0,1},{1,0},{2,3},{3,2},{4,5},{5,4},{6,7},{7,6},{8,9},{9,8},{10,11... | collective-permute-start | bytes 3145736 | tf_op jit(solution)/shard_map/ppermute | solution.py:163
  118.5 1.2 add_convert_fusion
  120.4 1.5 collective-permute-start.44
  123.7 4.5 %collective-permute-start.26 = (bf16[512,1024]{1,0:T(8,128)(2,1)S(1)}, bf16[512,1024]{1,0:T(8,128)(2,1)S(1)}, u32[]{:S(2)}, u32[]{:S(2)}) collective-permute-start(bf16[512,1024]{1,0:T(8,128)(2,1)S(1)} %add_convert_fusion.3), channel_id=1, source_target_pairs={{0,2},{2,4},{5,3},{7,5},{8,10},{10,12},{13,11},{15,13},{16,18},{18... | collective-permute-start | bytes 3145736 | tf_op jit(solution)/shard_map/ppermute | solution.py:166
  129.3 1.3 slice-done.2
  130.6 1.4 slice-done.3
  131.9 4.5 %convolution_convert_fusion.3.refs_0_ = bf16[1024,512]{1,0:T(8,128)(2,1)S(1)} fusion(bf16[1024,4096]{1,0:T(8,128)(2,1)S(1)} %bitcast.46, bf16[4096,512]{1,0:T(8,128)(2,1)S(1)} %fence.13.refs_1_), kind=kOutput, calls=%fused_computation.20 | convolution fusion | flops 4295491584 | bytes 13631488 | tf_op jit(solution)/shard_map/dot_general | solution.py:254
  136.4 4.0 %collective-permute-done.26 = bf16[512,1024]{1,0:T(8,128)(2,1)S(1)} collective-permute-done((bf16[512,1024]{1,0:T(8,128)(2,1)S(1)}, bf16[512,1024]{1,0:T(8,128)(2,1)S(1)}, u32[]{:S(2)}, u32[]{:S(2)}) %collective-permute-start.26) | collective-permute-done | bytes 1048608 | tf_op jit(solution)/shard_map/ppermute | solution.py:166
  141.7 2.5 %convolution_convert_fusion.2 = bf16[256,4096]{1,0:T(8,128)(2,1)S(1)} fusion(bf16[1024,4096]{1,0:T(8,128)(2,1)S(1)} %get-tuple-element.12.refs_1_, bf16[1024,512]{1,0:T(8,128)(2,1)S(1)} %fence.14.refs_2_), kind=kOutput, calls=%fused_computation.2 | convolution fusion | flops 2148532224 | bytes 11010048 | tf_op jit(solution)/shard_map/dot_general | solution.py:170
  144.2 2.5 %convolution_convert_fusion.1 = bf16[256,4096]{1,0:T(8,128)(2,1)S(1)} fusion(bf16[1024,4096]{1,0:T(8,128)(2,1)S(1)} %get-tuple-element.12.refs_1_, bf16[1024,512]{1,0:T(8,128)(2,1)S(1)} %fence.14.refs_2_), kind=kOutput, calls=%fused_computation.1 | convolution fusion | flops 2148532224 | bytes 11010048 | tf_op jit(solution)/shard_map/dot_general | solution.py:170
  146.8 1.3 fusion.9
  149.8 7.5 %collective-permute-start.41 = (bf16[512,1024]{1,0:T(8,128)(2,1)}, bf16[512,1024]{1,0:T(8,128)(2,1)}, u32[]{:S(2)}, u32[]{:S(2)}) collective-permute-start(bf16[512,1024]{1,0:T(8,128)(2,1)} %copy-done.1), channel_id=1, source_target_pairs={{0,2},{2,4},{3,1},{4,6},{5,3},{7,5},{8,10},{10,12},{11,9},{12,14},... | collective-permute-start | bytes 3145736 | tf_op jit(solution)/shard_map/ppermute | solution.py:166
  157.3 1.4 add_convert_fusion.10.refs_3_
  159.3 1.4 add_convert_fusion.7.refs_4_
  160.7 3.5 %collective-permute-start.30 = (bf16[256,1024]{1,0:T(8,128)(2,1)S(1)}, bf16[256,1024]{1,0:T(8,128)(2,1)}, u32[]{:S(2)}, u32[]{:S(2)}) collective-permute-start(bf16[256,1024]{1,0:T(8,128)(2,1)S(1)} %add_convert_fusion.10.refs_3_), channel_id=1, source_target_pairs={{0,2},{7,5},{8,10},{15,13},{16,18},{23,21},{24,26},{31,29}} | collective-permute-start | bytes 1572872 | tf_op jit(solution)/shard_map/ppermute | solution.py:166
  164.2 2.1 %collective-permute-start.37 = (bf16[256,1024]{1,0:T(8,128)(2,1)S(1)}, bf16[256,1024]{1,0:T(8,128)(2,1)}, u32[]{:S(2)}, u32[]{:S(2)}) collective-permute-start(bf16[256,1024]{1,0:T(8,128)(2,1)S(1)} %add_convert_fusion.7.refs_4_), channel_id=1, source_target_pairs={{0,2},{7,5},{8,10},{15,13},{16,18},{23,21},{24,26},{31,29}} | collective-permute-start | bytes 1572872 | tf_op jit(solution)/shard_map/ppermute | solution.py:166
  166.9 2.1 %convert_add_fusion = (f32[4096,128]{1,0:T(8,128)S(1)}, f32[4096,128]{1,0:T(8,128)S(1)}) fusion(bf16[4096,128]{1,0:T(8,128)(2,1)S(1)} %get-tuple-element.15, bf16[4096,128]{1,0:T(8,128)(2,1)} %add_convert_fusion, bf16[4096,128]{1,0:T(8,128)(2,1)S(1)} %get-tuple-element.14, bf16[4096,128]{1,0:T(8,128)(2,1)} %add_convert_fusion.1), kind=kLoop, calls=%fused_computation.12 | loop fusion | flops 3145728 | bytes 8388608 | tf_op jit(solution)/shard_map/add | solution.py:267
  170.4 3.9 %subtract_convert_fusion = (bf16[8192,128]{1,0:T(8,128)(2,1)}, f32[8192,128]{1,0:T(8,128)}) fusion(bf16[8192,128]{1,0:T(8,128)(2,1)S(1)} %copy-done.13, f32[4096,128]{1,0:T(8,128)S(1)} %get-tuple-element.35, f32[4096,128]{1,0:T(8,128)S(1)} %get-tuple-element.36, f32[8192,128]{1,0:T(8,128)S(1)} %copy-done.11), kind=kLoop, calls=%fused_computation.6 | loop fusion | flops 10485760 | bytes 16777216 | tf_op jit(solution)/shard_map/convert_element_type | solution.py:132
  174.9 1.5 add_convert_fusion.9
  176.3 4.1 %collective-permute-start.31 = (bf16[256,1024]{1,0:T(8,128)(2,1)S(1)}, bf16[256,1024]{1,0:T(8,128)(2,1)S(1)}, u32[]{:S(2)}, u32[]{:S(2)}) collective-permute-start(bf16[256,1024]{1,0:T(8,128)(2,1)S(1)} %add_convert_fusion.9), channel_id=1, source_target_pairs={{0,2},{2,4},{5,3},{7,5},{8,10},{10,12},{13,11},{15,13},{16,18},{18... | collective-permute-start | bytes 1572872 | tf_op jit(solution)/shard_map/ppermute | solution.py:166
  180.5 1.5 add_convert_fusion.6
  182.0 4.3 %collective-permute-start.38 = (bf16[256,1024]{1,0:T(8,128)(2,1)S(1)}, bf16[256,1024]{1,0:T(8,128)(2,1)S(1)}, u32[]{:S(2)}, u32[]{:S(2)}) collective-permute-start(bf16[256,1024]{1,0:T(8,128)(2,1)S(1)} %add_convert_fusion.6), channel_id=1, source_target_pairs={{0,2},{2,4},{5,3},{7,5},{8,10},{10,12},{13,11},{15,13},{16,18},{18... | collective-permute-start | bytes 1572872 | tf_op jit(solution)/shard_map/ppermute | solution.py:166
  186.3 1.9 convert_add_fusion.2
  188.5 3.3 %collective-permute-start.32 = (bf16[256,1024]{1,0:T(8,128)(2,1)S(1)}, bf16[256,1024]{1,0:T(8,128)(2,1)S(1)}, u32[]{:S(2)}, u32[]{:S(2)}) collective-permute-start(bf16[256,1024]{1,0:T(8,128)(2,1)S(1)} %add_convert_fusion.8), channel_id=1, source_target_pairs={{0,2},{2,4},{3,1},{4,6},{5,3},{7,5},{8,10},{10,12},{11,9},{12,14},... | collective-permute-start | bytes 1572872 | tf_op jit(solution)/shard_map/ppermute | solution.py:166
  193.0 4.4 %collective-permute-start.39 = (bf16[256,1024]{1,0:T(8,128)(2,1)S(1)}, bf16[256,1024]{1,0:T(8,128)(2,1)S(1)}, u32[]{:S(2)}, u32[]{:S(2)}) collective-permute-start(bf16[256,1024]{1,0:T(8,128)(2,1)S(1)} %add_convert_fusion.5), channel_id=1, source_target_pairs={{0,2},{2,4},{3,1},{4,6},{5,3},{7,5},{8,10},{10,12},{11,9},{12,14},... | collective-permute-start | bytes 1572872 | tf_op jit(solution)/shard_map/ppermute | solution.py:166
  199.4 4.7 %collective-permute-done.39 = bf16[256,1024]{1,0:T(8,128)(2,1)S(1)} collective-permute-done((bf16[256,1024]{1,0:T(8,128)(2,1)S(1)}, bf16[256,1024]{1,0:T(8,128)(2,1)S(1)}, u32[]{:S(2)}, u32[]{:S(2)}) %collective-permute-start.39) | collective-permute-done | bytes 524320 | tf_op jit(solution)/shard_map/ppermute | solution.py:166
  205.3 1.3 copy.23
  208.1 1.3 copy.22
  (143 shorter events, 31.6 us)
Async XLA Ops:
  1.4 2.2 %collective-permute-start.1 = (bf16[512,512]{1,0:T(8,128)(2,1)}, bf16[512,512]{1,0:T(8,128)(2,1)S(1)}, u32[]{:S(2)}, u32[]{:S(2)}) collective-permute-start(bf16[512,512]{1,0:T(8,128)(2,1)} %bitcast.40), channel_id=1, source_target_pairs={{0,1},{1,0},{2,3},{3,2},{4,5},{5,4},{6,7},{7,6},{8,9},{9,8},{10,11... | collective-permute-start | bytes 1572872 | tf_op jit(solution)/shard_map/ppermute | solution.py:163
  1.8 2.5 %collective-permute-start = (bf16[512,512]{1,0:T(8,128)(2,1)}, bf16[512,512]{1,0:T(8,128)(2,1)S(1)}, u32[]{:S(2)}, u32[]{:S(2)}) collective-permute-start(bf16[512,512]{1,0:T(8,128)(2,1)} %bitcast.38), channel_id=1, source_target_pairs={{0,1},{1,0},{2,3},{3,2},{4,5},{5,4},{6,7},{7,6},{8,9},{9,8},{10,11... | collective-permute-start | bytes 1572872 | tf_op jit(solution)/shard_map/ppermute | solution.py:163
  6.1 25.3 %collective-permute-start.2 = (bf16[1024,256]{1,0:T(8,128)(2,1)S(1)}, bf16[1024,256]{1,0:T(8,128)(2,1)S(1)}, u32[]{:S(2)}, u32[]{:S(2)}) collective-permute-start(bf16[1024,256]{1,0:T(8,128)(2,1)S(1)} %get-tuple-element.10.refs_3_), channel_id=1, source_target_pairs={{0,2},{2,4},{3,1},{4,6},{5,3},{7,5},{8,10},{10,12},{11,9},{12,14},... | collective-permute-start | bytes 1572872 | tf_op jit(solution)/shard_map/ppermute | solution.py:166
  10.9 21.8 %collective-permute-start.12 = (bf16[1024,256]{1,0:T(8,128)(2,1)S(1)}, bf16[1024,256]{1,0:T(8,128)(2,1)S(1)}, u32[]{:S(2)}, u32[]{:S(2)}) collective-permute-start(bf16[1024,256]{1,0:T(8,128)(2,1)S(1)} %get-tuple-element.13), channel_id=1, source_target_pairs={{0,2},{2,4},{3,1},{4,6},{5,3},{7,5},{8,10},{10,12},{11,9},{12,14},... | collective-permute-start | bytes 1572872 | tf_op jit(solution)/shard_map/ppermute | solution.py:166
  31.4 14.1 %copy-start.4 = (bf16[1,512,512]{2,1,0:T(8,128)(2,1)S(1)}, bf16[1,512,512]{2,1,0:T(8,128)(2,1)}, u32[]{:S(2)}) copy-start(bf16[1,512,512]{2,1,0:T(8,128)(2,1)} %param.12) | copy-start | bytes 1572868
  31.9 1.6 collective-permute-start.3
  32.7 20.4 %collective-permute-start.18 = (bf16[1024,256]{1,0:T(8,128)(2,1)S(1)}, bf16[1024,256]{1,0:T(8,128)(2,1)S(1)}, u32[]{:S(2)}, u32[]{:S(2)}) collective-permute-start(bf16[1024,256]{1,0:T(8,128)(2,1)S(1)} %fence.9.refs_2_), channel_id=1, source_target_pairs={{0,1},{1,0},{2,3},{3,2},{4,5},{5,4},{6,7},{7,6},{8,9},{9,8},{10,11... | collective-permute-start | bytes 1572872 | tf_op jit(solution)/shard_map/ppermute | solution.py:163
  32.8 13.3 %collective-permute-start.13 = (bf16[1024,256]{1,0:T(8,128)(2,1)S(1)}, bf16[1024,256]{1,0:T(8,128)(2,1)S(1)}, u32[]{:S(2)}, u32[]{:S(2)}) collective-permute-start(bf16[1024,256]{1,0:T(8,128)(2,1)S(1)} %collective-permute-done.12), channel_id=1, source_target_pairs={{2,4},{3,1},{4,6},{5,3},{10,12},{11,9},{12,14},{13,11},{18,20},{19... | collective-permute-start | bytes 1572872 | tf_op jit(solution)/shard_map/ppermute | solution.py:166
  33.5 10.4 %collective-permute-start.4 = (bf16[1024,256]{1,0:T(8,128)(2,1)S(1)}, bf16[1024,256]{1,0:T(8,128)(2,1)S(1)}, u32[]{:S(2)}, u32[]{:S(2)}) collective-permute-start(bf16[1024,256]{1,0:T(8,128)(2,1)S(1)} %collective-permute-done.3), channel_id=1, source_target_pairs={{3,1},{4,6},{11,9},{12,14},{19,17},{20,22},{27,25},{28,30}} | collective-permute-start | bytes 1572872 | tf_op jit(solution)/shard_map/ppermute | solution.py:166
  34.2 18.1 %collective-permute-start.16 = (bf16[1024,256]{1,0:T(8,128)(2,1)S(1)}, bf16[1024,256]{1,0:T(8,128)(2,1)S(1)}, u32[]{:S(2)}, u32[]{:S(2)}) collective-permute-start(bf16[1024,256]{1,0:T(8,128)(2,1)S(1)} %collective-permute-done.3), channel_id=1, source_target_pairs={{0,1},{1,0},{2,3},{3,2},{4,5},{5,4},{6,7},{7,6},{8,9},{9,8},{10,11... | collective-permute-start | bytes 1572872 | tf_op jit(solution)/shard_map/ppermute | solution.py:163
  42.2 43.8 %collective-permute-start.20 = (bf16[4096,128]{1,0:T(8,128)(2,1)S(1)}, bf16[4096,128]{1,0:T(8,128)(2,1)S(1)}, u32[]{:S(2)}, u32[]{:S(2)}) collective-permute-start(bf16[4096,128]{1,0:T(8,128)(2,1)S(1)} %get-tuple-element.32), channel_id=1, source_target_pairs={{0,8},{8,0},{16,24},{24,16},{1,9},{9,1},{17,25},{25,17},{2,10},{10... | collective-permute-start | bytes 3145736 | tf_op jit(solution)/shard_map/ppermute | solution.py:235
  43.9 42.1 %collective-permute-start.21 = (bf16[4096,128]{1,0:T(8,128)(2,1)S(1)}, bf16[4096,128]{1,0:T(8,128)(2,1)S(1)}, u32[]{:S(2)}, u32[]{:S(2)}) collective-permute-start(bf16[4096,128]{1,0:T(8,128)(2,1)S(1)} %get-tuple-element.31), channel_id=1, source_target_pairs={{0,16},{8,24},{16,0},{24,8},{1,17},{9,25},{17,1},{25,9},{2,18},{10... | collective-permute-start | bytes 3145736 | tf_op jit(solution)/shard_map/ppermute | solution.py:235
  46.1 7.8 %collective-permute-start.19 = (bf16[1024,256]{1,0:T(8,128)(2,1)S(1)}, bf16[1024,256]{1,0:T(8,128)(2,1)S(1)}, u32[]{:S(2)}, u32[]{:S(2)}) collective-permute-start(bf16[1024,256]{1,0:T(8,128)(2,1)S(1)} %collective-permute-done.12), channel_id=1, source_target_pairs={{0,1},{1,0},{2,3},{3,2},{4,5},{5,4},{6,7},{7,6},{8,9},{9,8},{10,11... | collective-permute-start | bytes 1572872 | tf_op jit(solution)/shard_map/ppermute | solution.py:163
  52.3 5.9 %collective-permute-start.14 = (bf16[1024,256]{1,0:T(8,128)(2,1)S(1)}, bf16[1024,256]{1,0:T(8,128)(2,1)S(1)}, u32[]{:S(2)}, u32[]{:S(2)}) collective-permute-start(bf16[1024,256]{1,0:T(8,128)(2,1)S(1)} %collective-permute-done.13), channel_id=1, source_target_pairs={{3,1},{4,6},{11,9},{12,14},{19,17},{20,22},{27,25},{28,30}} | collective-permute-start | bytes 1572872 | tf_op jit(solution)/shard_map/ppermute | solution.py:166
  53.1 9.5 %collective-permute-start.17 = (bf16[1024,256]{1,0:T(8,128)(2,1)S(1)}, bf16[1024,256]{1,0:T(8,128)(2,1)S(1)}, u32[]{:S(2)}, u32[]{:S(2)}) collective-permute-start(bf16[1024,256]{1,0:T(8,128)(2,1)S(1)} %collective-permute-done.13), channel_id=1, source_target_pairs={{0,1},{1,0},{2,3},{3,2},{4,5},{5,4},{6,7},{7,6},{8,9},{9,8},{10,11... | collective-permute-start | bytes 1572872 | tf_op jit(solution)/shard_map/ppermute | solution.py:163
  53.9 31.2 %collective-permute-start.5 = (bf16[1024,512]{1,0:T(8,128)(2,1)S(1)}, bf16[1024,512]{1,0:T(8,128)(2,1)S(1)}, u32[]{:S(2)}, u32[]{:S(2)}) collective-permute-start(bf16[1024,512]{1,0:T(8,128)(2,1)S(1)} %join_cores.3.refs_1_), channel_id=1, source_target_pairs={{0,2},{2,4},{3,1},{4,6},{5,3},{7,5},{8,10},{10,12},{11,9},{12,14},... | collective-permute-start | bytes 3145736 | tf_op jit(solution)/shard_map/ppermute | solution.py:166
  58.3 5.9 %collective-permute-start.11 = (bf16[1024,256]{1,0:T(8,128)(2,1)S(1)}, bf16[1024,256]{1,0:T(8,128)(2,1)S(1)}, u32[]{:S(2)}, u32[]{:S(2)}) collective-permute-start(bf16[1024,256]{1,0:T(8,128)(2,1)S(1)} %collective-permute-done.4.refs_3_), channel_id=1, source_target_pairs={{0,1},{1,0},{2,3},{3,2},{4,5},{5,4},{6,7},{7,6},{8,9},{9,8},{10,11... | collective-permute-start | bytes 1572872 | tf_op jit(solution)/shard_map/ppermute | solution.py:163
  62.7 2.2 %collective-permute-start.15 = (bf16[1024,256]{1,0:T(8,128)(2,1)S(1)}, bf16[1024,256]{1,0:T(8,128)(2,1)S(1)}, u32[]{:S(2)}, u32[]{:S(2)}) collective-permute-start(bf16[1024,256]{1,0:T(8,128)(2,1)S(1)} %collective-permute-done.14), channel_id=1, source_target_pairs={{0,1},{1,0},{2,3},{3,2},{4,5},{5,4},{6,7},{7,6},{8,9},{9,8},{10,11... | collective-permute-start | bytes 1572872 | tf_op jit(solution)/shard_map/ppermute | solution.py:163
  85.1 6.5 %collective-permute-start.6 = (bf16[1024,512]{1,0:T(8,128)(2,1)S(1)}, bf16[1024,512]{1,0:T(8,128)(2,1)S(1)}, u32[]{:S(2)}, u32[]{:S(2)}) collective-permute-start(bf16[1024,512]{1,0:T(8,128)(2,1)S(1)} %collective-permute-done.5.refs_2_), channel_id=1, source_target_pairs={{2,4},{3,1},{4,6},{5,3},{10,12},{11,9},{12,14},{13,11},{18,20},{19... | collective-permute-start | bytes 3145736 | tf_op jit(solution)/shard_map/ppermute | solution.py:166
  92.2 48.3 %copy-start = (bf16[512,4096]{1,0:T(8,128)(2,1)}, bf16[512,4096]{1,0:T(8,128)(2,1)S(1)}, u32[]{:S(2)}) copy-start(bf16[512,4096]{1,0:T(8,128)(2,1)S(1)} %fence.12.refs_1_) | copy-start | bytes 12582916
  92.6 12.5 %collective-permute-start.24 = (bf16[512,1024]{1,0:T(8,128)(2,1)S(1)}, bf16[512,1024]{1,0:T(8,128)(2,1)S(1)}, u32[]{:S(2)}, u32[]{:S(2)}) collective-permute-start(bf16[512,1024]{1,0:T(8,128)(2,1)S(1)} %get-tuple-element.24), channel_id=1, source_target_pairs={{0,1},{1,0},{2,3},{3,2},{4,5},{5,4},{6,7},{7,6},{8,9},{9,8},{10,11... | collective-permute-start | bytes 3145736 | tf_op jit(solution)/shard_map/ppermute | solution.py:163
  102.1 8.8 %collective-permute-start.7 = (bf16[1024,512]{1,0:T(8,128)(2,1)S(1)}, bf16[1024,512]{1,0:T(8,128)(2,1)S(1)}, u32[]{:S(2)}, u32[]{:S(2)}) collective-permute-start(bf16[1024,512]{1,0:T(8,128)(2,1)S(1)} %collective-permute-done.6.refs_2_), channel_id=1, source_target_pairs={{3,1},{4,6},{11,9},{12,14},{19,17},{20,22},{27,25},{28,30}} | collective-permute-start | bytes 3145736 | tf_op jit(solution)/shard_map/ppermute | solution.py:166
  104.0 16.4 %collective-permute-start.10 = (bf16[1024,512]{1,0:T(8,128)(2,1)S(1)}, bf16[1024,512]{1,0:T(8,128)(2,1)S(1)}, u32[]{:S(2)}, u32[]{:S(2)}) collective-permute-start(bf16[1024,512]{1,0:T(8,128)(2,1)S(1)} %collective-permute-done.5.refs_2_), channel_id=1, source_target_pairs={{0,1},{1,0},{2,3},{3,2},{4,5},{5,4},{6,7},{7,6},{8,9},{9,8},{10,11... | collective-permute-start | bytes 3145736 | tf_op jit(solution)/shard_map/ppermute | solution.py:163
  104.6 17.4 %collective-permute-start.23 = (bf16[512,1024]{1,0:T(8,128)(2,1)S(1)}, bf16[512,1024]{1,0:T(8,128)(2,1)S(1)}, u32[]{:S(2)}, u32[]{:S(2)}) collective-permute-start(bf16[512,1024]{1,0:T(8,128)(2,1)S(1)} %get-tuple-element.23), channel_id=1, source_target_pairs={{0,1},{1,0},{2,3},{3,2},{4,5},{5,4},{6,7},{7,6},{8,9},{9,8},{10,11... | collective-permute-start | bytes 3145736 | tf_op jit(solution)/shard_map/ppermute | solution.py:163
  104.6 15.1 %collective-permute-start.9 = (bf16[1024,512]{1,0:T(8,128)(2,1)S(1)}, bf16[1024,512]{1,0:T(8,128)(2,1)S(1)}, u32[]{:S(2)}, u32[]{:S(2)}) collective-permute-start(bf16[1024,512]{1,0:T(8,128)(2,1)S(1)} %collective-permute-done.6.refs_2_), channel_id=1, source_target_pairs={{0,1},{1,0},{2,3},{3,2},{4,5},{5,4},{6,7},{7,6},{8,9},{9,8},{10,11... | collective-permute-start | bytes 3145736 | tf_op jit(solution)/shard_map/ppermute | solution.py:163
  105.6 17.5 %collective-permute-start.25 = (bf16[512,1024]{1,0:T(8,128)(2,1)S(1)}, bf16[512,1024]{1,0:T(8,128)(2,1)S(1)}, u32[]{:S(2)}, u32[]{:S(2)}) collective-permute-start(bf16[512,1024]{1,0:T(8,128)(2,1)S(1)} %add_convert_fusion.4), channel_id=1, source_target_pairs={{0,2},{7,5},{8,10},{15,13},{16,18},{23,21},{24,26},{31,29}} | collective-permute-start | bytes 3145736 | tf_op jit(solution)/shard_map/ppermute | solution.py:166
  110.9 17.3 %collective-permute-start.8 = (bf16[1024,512]{1,0:T(8,128)(2,1)S(1)}, bf16[1024,512]{1,0:T(8,128)(2,1)S(1)}, u32[]{:S(2)}, u32[]{:S(2)}) collective-permute-start(bf16[1024,512]{1,0:T(8,128)(2,1)S(1)} %collective-permute-done.7), channel_id=1, source_target_pairs={{0,1},{1,0},{2,3},{3,2},{4,5},{5,4},{6,7},{7,6},{8,9},{9,8},{10,11... | collective-permute-start | bytes 3145736 | tf_op jit(solution)/shard_map/ppermute | solution.py:163
  119.8 40.9 %collective-permute-start.43 = (bf16[4096,128]{1,0:T(8,128)(2,1)}, bf16[4096,128]{1,0:T(8,128)(2,1)S(1)}, u32[]{:S(2)}, u32[]{:S(2)}) collective-permute-start(bf16[4096,128]{1,0:T(8,128)(2,1)} %add_convert_fusion.1), channel_id=1, source_target_pairs={{0,16},{8,24},{16,0},{24,8},{1,17},{9,25},{17,1},{25,9},{2,18},{10... | collective-permute-start | bytes 3145736 | tf_op jit(solution)/shard_map/ppermute | solution.py:235
  120.4 43.8 %collective-permute-start.44 = (bf16[4096,128]{1,0:T(8,128)(2,1)}, bf16[4096,128]{1,0:T(8,128)(2,1)S(1)}, u32[]{:S(2)}, u32[]{:S(2)}) collective-permute-start(bf16[4096,128]{1,0:T(8,128)(2,1)} %add_convert_fusion), channel_id=1, source_target_pairs={{0,8},{8,0},{16,24},{24,16},{1,9},{9,1},{17,25},{25,17},{2,10},{10... | collective-permute-start | bytes 3145736 | tf_op jit(solution)/shard_map/ppermute | solution.py:235
  122.1 14.3 %collective-permute-start.22 = (bf16[512,1024]{1,0:T(8,128)(2,1)S(1)}, bf16[512,1024]{1,0:T(8,128)(2,1)S(1)}, u32[]{:S(2)}, u32[]{:S(2)}) collective-permute-start(bf16[512,1024]{1,0:T(8,128)(2,1)S(1)} %get-tuple-element.22), channel_id=1, source_target_pairs={{0,1},{1,0},{2,3},{3,2},{4,5},{5,4},{6,7},{7,6},{8,9},{9,8},{10,11... | collective-permute-start | bytes 3145736 | tf_op jit(solution)/shard_map/ppermute | solution.py:163
  123.7 16.7 %collective-permute-start.26 = (bf16[512,1024]{1,0:T(8,128)(2,1)S(1)}, bf16[512,1024]{1,0:T(8,128)(2,1)S(1)}, u32[]{:S(2)}, u32[]{:S(2)}) collective-permute-start(bf16[512,1024]{1,0:T(8,128)(2,1)S(1)} %add_convert_fusion.3), channel_id=1, source_target_pairs={{0,2},{2,4},{5,3},{7,5},{8,10},{10,12},{13,11},{15,13},{16,18},{18... | collective-permute-start | bytes 3145736 | tf_op jit(solution)/shard_map/ppermute | solution.py:166
  148.1 9.3 %collective-permute-start.29 = (bf16[256,1024]{1,0:T(8,128)(2,1)}, bf16[256,1024]{1,0:T(8,128)(2,1)}, u32[]{:S(2)}, u32[]{:S(2)}) collective-permute-start(bf16[256,1024]{1,0:T(8,128)(2,1)} %get-tuple-element.27), channel_id=1, source_target_pairs={{0,1},{1,0},{2,3},{3,2},{4,5},{5,4},{6,7},{7,6},{8,9},{9,8},{10,11... | collective-permute-start | bytes 1572872 | tf_op jit(solution)/shard_map/ppermute | solution.py:163
  149.8 9.0 %collective-permute-start.36 = (bf16[256,1024]{1,0:T(8,128)(2,1)}, bf16[256,1024]{1,0:T(8,128)(2,1)}, u32[]{:S(2)}, u32[]{:S(2)}) collective-permute-start(bf16[256,1024]{1,0:T(8,128)(2,1)} %get-tuple-element.30), channel_id=1, source_target_pairs={{0,1},{1,0},{2,3},{3,2},{4,5},{5,4},{6,7},{7,6},{8,9},{9,8},{10,11... | collective-permute-start | bytes 1572872 | tf_op jit(solution)/shard_map/ppermute | solution.py:163
  149.8 36.5 %collective-permute-start.41 = (bf16[512,1024]{1,0:T(8,128)(2,1)}, bf16[512,1024]{1,0:T(8,128)(2,1)}, u32[]{:S(2)}, u32[]{:S(2)}) collective-permute-start(bf16[512,1024]{1,0:T(8,128)(2,1)} %copy-done.1), channel_id=1, source_target_pairs={{0,2},{2,4},{3,1},{4,6},{5,3},{7,5},{8,10},{10,12},{11,9},{12,14},... | collective-permute-start | bytes 3145736 | tf_op jit(solution)/shard_map/ppermute | solution.py:166
  157.3 17.0 %collective-permute-start.28 = (bf16[256,1024]{1,0:T(8,128)(2,1)}, bf16[256,1024]{1,0:T(8,128)(2,1)}, u32[]{:S(2)}, u32[]{:S(2)}) collective-permute-start(bf16[256,1024]{1,0:T(8,128)(2,1)} %get-tuple-element.26), channel_id=1, source_target_pairs={{0,1},{1,0},{2,3},{3,2},{4,5},{5,4},{6,7},{7,6},{8,9},{9,8},{10,11... | collective-permute-start | bytes 1572872 | tf_op jit(solution)/shard_map/ppermute | solution.py:163
  158.7 17.6 %collective-permute-start.35 = (bf16[256,1024]{1,0:T(8,128)(2,1)}, bf16[256,1024]{1,0:T(8,128)(2,1)}, u32[]{:S(2)}, u32[]{:S(2)}) collective-permute-start(bf16[256,1024]{1,0:T(8,128)(2,1)} %get-tuple-element.29), channel_id=1, source_target_pairs={{0,1},{1,0},{2,3},{3,2},{4,5},{5,4},{6,7},{7,6},{8,9},{9,8},{10,11... | collective-permute-start | bytes 1572872 | tf_op jit(solution)/shard_map/ppermute | solution.py:163
  160.7 13.7 %collective-permute-start.30 = (bf16[256,1024]{1,0:T(8,128)(2,1)S(1)}, bf16[256,1024]{1,0:T(8,128)(2,1)}, u32[]{:S(2)}, u32[]{:S(2)}) collective-permute-start(bf16[256,1024]{1,0:T(8,128)(2,1)S(1)} %add_convert_fusion.10.refs_3_), channel_id=1, source_target_pairs={{0,2},{7,5},{8,10},{15,13},{16,18},{23,21},{24,26},{31,29}} | collective-permute-start | bytes 1572872 | tf_op jit(solution)/shard_map/ppermute | solution.py:166
  164.2 16.2 %collective-permute-start.37 = (bf16[256,1024]{1,0:T(8,128)(2,1)S(1)}, bf16[256,1024]{1,0:T(8,128)(2,1)}, u32[]{:S(2)}, u32[]{:S(2)}) collective-permute-start(bf16[256,1024]{1,0:T(8,128)(2,1)S(1)} %add_convert_fusion.7.refs_4_), channel_id=1, source_target_pairs={{0,2},{7,5},{8,10},{15,13},{16,18},{23,21},{24,26},{31,29}} | collective-permute-start | bytes 1572872 | tf_op jit(solution)/shard_map/ppermute | solution.py:166
  170.4 10.1 %copy-start.8 = (bf16[256,4096]{1,0:T(8,128)(2,1)S(1)}, bf16[256,4096]{1,0:T(8,128)(2,1)}, u32[]{:S(2)}) copy-start(bf16[256,4096]{1,0:T(8,128)(2,1)} %copy-done.7) | copy-start | bytes 6291460
  174.3 13.9 %collective-permute-start.27 = (bf16[256,1024]{1,0:T(8,128)(2,1)S(1)}, bf16[256,1024]{1,0:T(8,128)(2,1)S(1)}, u32[]{:S(2)}, u32[]{:S(2)}) collective-permute-start(bf16[256,1024]{1,0:T(8,128)(2,1)S(1)} %copy-done.15), channel_id=1, source_target_pairs={{0,1},{1,0},{2,3},{3,2},{4,5},{5,4},{6,7},{7,6},{8,9},{9,8},{10,11... | collective-permute-start | bytes 1572872 | tf_op jit(solution)/shard_map/ppermute | solution.py:163
  174.4 17.4 %collective-permute-start.34 = (bf16[256,1024]{1,0:T(8,128)(2,1)S(1)}, bf16[256,1024]{1,0:T(8,128)(2,1)S(1)}, u32[]{:S(2)}, u32[]{:S(2)}) collective-permute-start(bf16[256,1024]{1,0:T(8,128)(2,1)S(1)} %copy-done.14), channel_id=1, source_target_pairs={{0,1},{1,0},{2,3},{3,2},{4,5},{5,4},{6,7},{7,6},{8,9},{9,8},{10,11... | collective-permute-start | bytes 1572872 | tf_op jit(solution)/shard_map/ppermute | solution.py:163
  176.3 11.9 %collective-permute-start.31 = (bf16[256,1024]{1,0:T(8,128)(2,1)S(1)}, bf16[256,1024]{1,0:T(8,128)(2,1)S(1)}, u32[]{:S(2)}, u32[]{:S(2)}) collective-permute-start(bf16[256,1024]{1,0:T(8,128)(2,1)S(1)} %add_convert_fusion.9), channel_id=1, source_target_pairs={{0,2},{2,4},{5,3},{7,5},{8,10},{10,12},{13,11},{15,13},{16,18},{18... | collective-permute-start | bytes 1572872 | tf_op jit(solution)/shard_map/ppermute | solution.py:166
  182.0 10.8 %collective-permute-start.38 = (bf16[256,1024]{1,0:T(8,128)(2,1)S(1)}, bf16[256,1024]{1,0:T(8,128)(2,1)S(1)}, u32[]{:S(2)}, u32[]{:S(2)}) collective-permute-start(bf16[256,1024]{1,0:T(8,128)(2,1)S(1)} %add_convert_fusion.6), channel_id=1, source_target_pairs={{0,2},{2,4},{5,3},{7,5},{8,10},{10,12},{13,11},{15,13},{16,18},{18... | collective-permute-start | bytes 1572872 | tf_op jit(solution)/shard_map/ppermute | solution.py:166
  188.5 9.9 %collective-permute-start.32 = (bf16[256,1024]{1,0:T(8,128)(2,1)S(1)}, bf16[256,1024]{1,0:T(8,128)(2,1)S(1)}, u32[]{:S(2)}, u32[]{:S(2)}) collective-permute-start(bf16[256,1024]{1,0:T(8,128)(2,1)S(1)} %add_convert_fusion.8), channel_id=1, source_target_pairs={{0,2},{2,4},{3,1},{4,6},{5,3},{7,5},{8,10},{10,12},{11,9},{12,14},... | collective-permute-start | bytes 1572872 | tf_op jit(solution)/shard_map/ppermute | solution.py:166
  193.0 11.1 %collective-permute-start.39 = (bf16[256,1024]{1,0:T(8,128)(2,1)S(1)}, bf16[256,1024]{1,0:T(8,128)(2,1)S(1)}, u32[]{:S(2)}, u32[]{:S(2)}) collective-permute-start(bf16[256,1024]{1,0:T(8,128)(2,1)S(1)} %add_convert_fusion.5), channel_id=1, source_target_pairs={{0,2},{2,4},{3,1},{4,6},{5,3},{7,5},{8,10},{10,12},{11,9},{12,14},... | collective-permute-start | bytes 1572872 | tf_op jit(solution)/shard_map/ppermute | solution.py:166
  197.5 7.5 %collective-permute-start.42 = (bf16[512,512]{1,0:T(8,128)(2,1)S(1)}, bf16[512,512]{1,0:T(8,128)(2,1)S(1)}, u32[]{:S(2)}, u32[]{:S(2)}) collective-permute-start(bf16[512,512]{1,0:T(8,128)(2,1)S(1)} %select_convert_fusion), channel_id=1, source_target_pairs={{0,1},{1,0},{2,3},{3,2},{4,5},{5,4},{6,7},{7,6},{8,9},{9,8},{10,11... | collective-permute-start | bytes 1572872 | tf_op jit(solution)/shard_map/ppermute | solution.py:163
  199.4 7.2 %collective-permute-start.33 = (bf16[256,512]{1,0:T(8,128)(2,1)}, bf16[256,512]{1,0:T(8,128)(2,1)S(1)}, u32[]{:S(2)}, u32[]{:S(2)}) collective-permute-start(bf16[256,512]{1,0:T(8,128)(2,1)} %select_convert_fusion.2), channel_id=1, source_target_pairs={{0,1},{1,0},{2,3},{3,2},{4,5},{5,4},{6,7},{7,6},{8,9},{9,8},{10,11... | collective-permute-start | bytes 786440 | tf_op jit(solution)/shard_map/ppermute | solution.py:163
  205.0 1.9 collective-permute-start.40
  (17 other events, 64.9 us)

commit v9 on v8

--- a/solution.py
+++ b/solution.py
@@ -207,19 +207,24 @@
         return pieces, others
 
     def assemble(pieces, others):
-        shards = [jnp.concatenate(pieces[0], axis=1)]
-        for p in range(1, chips):
-            parts = zip(pieces[p], others[chips - p - 1])
-            chosen = [jnp.where(position >= p, here, there) for here, there in parts]
-            shards.append(jnp.concatenate(chosen, axis=1))
-        return jnp.concatenate(shards, axis=0)
+        parts = []
+        for j, first in enumerate(pieces[0]):
+            shards = [first]
+            for p in range(1, chips):
+                here, there = pieces[p][j], others[chips - p - 1][j]
+                shards.append(jnp.where(position >= p, here, there))
+            parts.append(jnp.concatenate(shards, axis=0))
+        return fence(order, *parts)
 
     first_own, second_own = value_weight[0], output_weight[0]
     first_partner, second_partner = swap(first_own), swap(second_own)
 
     joined = join_cores(order, first_own, first_partner, HALVES, (second_partner,))
     normed, cotangent = prepare(order, tokens[0], out_cotangent[0], norm_gain, chips)
-    exponents = fence(order, delta_exponents)[0]
+    pieces, others = gather(joined, at_first=True)
+    last = pieces[-1]
+
+    exponents = fence(order, delta_exponents, after=(pieces[2][1],))[0]
     bits = replicas.bit_length() - 1
     if replicas != 1 << bits or bits < 1:
         raise ValueError("replicas")
@@ -237,20 +242,21 @@
                 early.append(theirs)
             total = mine.astype(f32) + theirs.astype(f32)
         sums.append((mine, theirs))
-    pieces, others = gather(joined, at_first=True)
-    last = pieces[-1]
 
     joined = join_cores(order, second_own, second_partner, 1, (last[0],))
-    weight = assemble(pieces, others)
-    weight = fence(order, weight)[0]
-    values = jnp.dot(normed, weight, preferred_element_type=f32).astype(bf16)
+    values = jnp.concatenate(
+        [
+            jnp.dot(normed, part, preferred_element_type=f32).astype(bf16)
+            for part in assemble(pieces, others)
+        ],
+        axis=1,
+    )
     pieces, others = gather(joined)
     values = fence(order, values, after=(pieces[1][0], *early))[0]
     first = Gradient(values, cotangent, (pieces[2][0],))
     sent = [first.reduce(step) for step in range(1, chips)]
 
-    weight = assemble(pieces, others)
-    weight = fence(order, weight)[0]
+    weight = assemble(pieces, others)[0]
     mid = jnp.dot(cotangent, weight, preferred_element_type=f32).astype(bf16)
     mid = fence(order, mid, after=(sent[-1],))[0]
     half = mid.shape[1] // HALVES

time: 210 us -> 205 us (0.976)
  other arithmetic: 40.2 us -> 26.5 us
  starting transfers between devices: 98.6 us -> 108 us
  local copies, waits for them, and re-layouts: 19.5 us -> 13.4 us
  waiting for transfers between devices: 16.1 us -> 20.9 us
    concatenate x2 -> x4, other arithmetic: 15.4 us -> 0.68 us  [the longest x3 0.6 us: assemble(): parts.append(jnp.concatenate(shards, axis=0))]
    ppermute x23, starting transfers between devices: 37.1 us -> 45.1 us  [swap(): return lax.ppermute(value, 'fsdp', [(i, i ^ 1) for i in range(devices)])]
    unnamed x43 -> x37, local copies, waits for them, and re-layouts: 16.5 us -> 9.52 us
    ppermute x18, waiting for transfers between devices: 11.5 us -> 16.4 us  [move(): return lax.ppermute(value, 'fsdp', move_perm(chips, active))]
    dot_general x1 -> x2, matrix products: 4.48 us -> 4.67 us  [per_device(): jnp.dot(normed, part, preferred_element_type=f32).astype(bf16)]
  transfers between devices with their start and end apart: 45 -> 45, of which waited for: 11 -> 12; matrix products, arithmetic and copies ran while one was open for 30% -> 24% of each run, Pallas kernels for 6% -> 7%
where the time goes in v9:
time: 205 us; the launch traced here: 204 us
  starting transfers between devices  108 us (53%)
  other arithmetic  26.5 us (13%)
  waiting for transfers between devices  20.9 us (10%)
  matrix products  19.2 us (9%)
  Pallas kernels  14.6 us (7%)
  local copies, waits for them, and re-layouts  13.4 us (7%)
    ppermute x18, starting transfers between devices, move(): return lax.ppermute(value, 'fsdp', move_perm(chips, active))  57.9 us
    ppermute x23, starting transfers between devices, swap(): return lax.ppermute(value, 'fsdp', [(i, i ^ 1) for i in range(devices)])  45.1 us
    ppermute x18, waiting for transfers between devices, move(): return lax.ppermute(value, 'fsdp', move_perm(chips, active))  16.4 us
    pallas_call x11, Pallas kernels, __call__(): pl.pallas_call(ordered, grid_spec=pltpu.PrefetchScalarGridSpec(num_scalar...  14.6 us
    dot_general x3, matrix products, __init__(): lax.dot_general(mid, x, (((0,), (0,)), ((), ())), preferred_element_type=...  10 us
    unnamed x37, local copies, waits for them, and re-layouts  9.52 us
    convert_element_type x9, other arithmetic, message(): return term.astype(bf16)  9.21 us
    ppermute x4, starting transfers between devices, per_device(): lax.ppermute(mine, 'replica', [(i, i ^ bit) for i in range(replicas)])  5.14 us
  transfers between devices with their start and end apart: 45, of which 12 were waited for; matrix products, arithmetic and copies ran while one was open for 24% of the time, Pallas kernels for 7%

profile of v9, /device:TPU:0, one launch (start us, length us, event | category | flops | bytes accessed | tf_op | source)
XLA Modules:
  0.0 204.1 jit_solution(11881012955820565387)
XLA Ops:
  2.0 1.6 collective-permute-done.1.refs_2_.refs_1_
  6.1 5.7 %collective-permute-start.3 = (bf16[1024,256]{1,0:T(8,128)(2,1)S(1)}, bf16[1024,256]{1,0:T(8,128)(2,1)}, u32[]{:S(2)}, u32[]{:S(2)}) collective-permute-start(bf16[1024,256]{1,0:T(8,128)(2,1)S(1)} %get-tuple-element.15), channel_id=1, source_target_pairs={{0,2},{2,4},{3,1},{4,6},{5,3},{7,5},{8,10},{10,12},{11,9},{12,14},... | collective-permute-start | bytes 1572872 | tf_op jit(solution)/shard_map/ppermute | solution.py:166
  11.7 2.7 %collective-permute-start.2 = (bf16[1024,256]{1,0:T(8,128)(2,1)S(1)}, bf16[1024,256]{1,0:T(8,128)(2,1)S(1)}, u32[]{:S(2)}, u32[]{:S(2)}) collective-permute-start(bf16[1024,256]{1,0:T(8,128)(2,1)S(1)} %get-tuple-element.12.refs_3_), channel_id=1, source_target_pairs={{0,2},{2,4},{3,1},{4,6},{5,3},{7,5},{8,10},{10,12},{11,9},{12,14},... | collective-permute-start | bytes 1572872 | tf_op jit(solution)/shard_map/ppermute | solution.py:166
  14.5 3.1 %collective-permute-done.3 = bf16[1024,256]{1,0:T(8,128)(2,1)} collective-permute-done((bf16[1024,256]{1,0:T(8,128)(2,1)S(1)}, bf16[1024,256]{1,0:T(8,128)(2,1)}, u32[]{:S(2)}, u32[]{:S(2)}) %collective-permute-start.3) | collective-permute-done | bytes 524320 | tf_op jit(solution)/shard_map/ppermute | solution.py:166
  18.3 3.4 %copy-done.2 = bf16[1,1024,4096]{2,1,0:T(8,128)(2,1)S(1)} copy-done((bf16[1,1024,4096]{2,1,0:T(8,128)(2,1)S(1)}, bf16[1,1024,4096]{2,1,0:T(8,128)(2,1)}, u32[]{:S(2)}) %copy-start.2) | copy-done | bytes 8388632
  21.7 8.9 %prepare.1 = (bf16[1024,4096]{1,0:T(8,128)(2,1)S(1)}, bf16[1024,4096]{1,0:T(8,128)(2,1)S(1)}) custom-call(s32[6]{0:T(128)S(1)} %stack.27.place_ref, bf16[1024,4096]{1,0:T(8,128)(2,1)S(1)} %bitcast.39, bf16[1024,4096]{1,0:T(8,128)(2,1)} %bitcast.47, f32[1,4096]{1,0:T(1,128)S(1)} %bitcast.44, bf16[1024,256]{1,0:T(8,128)(2,1)S(1)} %get-tuple-element.12.refs_3_), custom_call_target="tpu_custom_call" | custom-call | flops 20000000000 | bytes 1 | tf_op jit(solution)/shard_map/prepare/pallas_call | solution.py:39
  34.5 9.4 %collective-permute-start.14 = (bf16[1024,256]{1,0:T(8,128)(2,1)S(1)}, bf16[1024,256]{1,0:T(8,128)(2,1)S(1)}, u32[]{:S(2)}, u32[]{:S(2)}) collective-permute-start(bf16[1024,256]{1,0:T(8,128)(2,1)S(1)} %collective-permute-done.5), channel_id=1, source_target_pairs={{0,1},{1,0},{2,3},{3,2},{4,5},{5,4},{6,7},{7,6},{8,9},{9,8},{10,11... | collective-permute-start | bytes 1572872 | tf_op jit(solution)/shard_map/ppermute | solution.py:163
  44.0 2.1 %fusion = (bf16[4096,128]{1,0:T(8,128)(2,1)S(1)}, bf16[4096,128]{1,0:T(8,128)(2,1)S(1)}) fusion(f32[4096]{0:T(1024)S(1)} %bitcast.45, bf16[1,8192,128]{2,1,0:T(8,128)(2,1)S(1)} %copy-done.13, f32[4096]{0:T(1024)S(1)} %bitcast.46), kind=kLoop, calls=%fused_computation.10 | loop fusion | flops 3145728 | bytes 4227072 | tf_op jit(solution)/shard_map/convert_element_type | solution.py:238
  46.1 1.6 collective-permute-start.20
  47.7 1.5 collective-permute-start.21
  50.7 5.5 %collective-permute-start.18 = (bf16[1024,256]{1,0:T(8,128)(2,1)S(1)}, bf16[1024,256]{1,0:T(8,128)(2,1)S(1)}, u32[]{:S(2)}, u32[]{:S(2)}) collective-permute-start(bf16[1024,256]{1,0:T(8,128)(2,1)S(1)} %collective-permute-done.4.refs_2_), channel_id=1, source_target_pairs={{0,1},{1,0},{2,3},{3,2},{4,5},{5,4},{6,7},{7,6},{8,9},{9,8},{10,11... | collective-permute-start | bytes 1572872 | tf_op jit(solution)/shard_map/ppermute | solution.py:163
  56.3 4.4 %collective-permute-start.7 = (bf16[1024,512]{1,0:T(8,128)(2,1)S(1)}, bf16[1024,512]{1,0:T(8,128)(2,1)S(1)}, u32[]{:S(2)}, u32[]{:S(2)}) collective-permute-start(bf16[1024,512]{1,0:T(8,128)(2,1)S(1)} %join_cores.3.refs_2_), channel_id=1, source_target_pairs={{0,2},{2,4},{3,1},{4,6},{5,3},{7,5},{8,10},{10,12},{11,9},{12,14},... | collective-permute-start | bytes 3145736 | tf_op jit(solution)/shard_map/ppermute | solution.py:166
  60.6 4.3 %collective-permute-start.13 = (bf16[1024,256]{1,0:T(8,128)(2,1)S(1)}, bf16[1024,256]{1,0:T(8,128)(2,1)S(1)}, u32[]{:S(2)}, u32[]{:S(2)}) collective-permute-start(bf16[1024,256]{1,0:T(8,128)(2,1)S(1)} %collective-permute-done.6.refs_3_), channel_id=1, source_target_pairs={{0,1},{1,0},{2,3},{3,2},{4,5},{5,4},{6,7},{7,6},{8,9},{9,8},{10,11... | collective-permute-start | bytes 1572872 | tf_op jit(solution)/shard_map/ppermute | solution.py:163
  65.2 1.3 collective-permute-done.13
  68.0 2.3 %convolution_convert_fusion.5 = bf16[1024,256]{1,0:T(8,128)(2,1)S(1)} fusion(bf16[1024,4096]{1,0:T(8,128)(2,1)S(1)} %get-tuple-element.14.refs_1_, bf16[4096,256]{1,0:T(8,128)(2,1)S(1)} %get-tuple-element.16.refs_1_), kind=kOutput, calls=%fused_computation.23 | convolution fusion | flops 2147745792 | bytes 11010048 | tf_op jit(solution)/shard_map/dot_general | solution.py:249
  70.3 2.3 %convolution_convert_fusion.4 = bf16[1024,256]{1,0:T(8,128)(2,1)S(1)} fusion(bf16[1024,4096]{1,0:T(8,128)(2,1)S(1)} %get-tuple-element.14.refs_1_, bf16[4096,256]{1,0:T(8,128)(2,1)S(1)} %get-tuple-element.17), kind=kOutput, calls=%fused_computation.22 | convolution fusion | flops 2147745792 | bytes 11010048 | tf_op jit(solution)/shard_map/dot_general | solution.py:249
  74.2 5.0 %convolution_convert_fusion.refs_0_ = bf16[512,4096]{1,0:T(8,128)(2,1)S(1)} fusion(bf16[1024,512]{1,0:T(8,128)(2,1)S(1)} %fence.11.refs_1_, bf16[1024,4096]{1,0:T(8,128)(2,1)S(1)} %get-tuple-element.13), kind=kOutput, calls=%fused_computation | convolution fusion | flops 4297064448 | bytes 13631488 | tf_op jit(solution)/shard_map/dot_general | solution.py:170
  79.7 1.3 fusion.8
  81.0 13.8 %collective-permute-start.24 = (bf16[512,1024]{1,0:T(8,128)(2,1)S(1)}, bf16[512,1024]{1,0:T(8,128)(2,1)S(1)}, u32[]{:S(2)}, u32[]{:S(2)}) collective-permute-start(bf16[512,1024]{1,0:T(8,128)(2,1)S(1)} %get-tuple-element.28), channel_id=1, source_target_pairs={{0,1},{1,0},{2,3},{3,2},{4,5},{5,4},{6,7},{7,6},{8,9},{9,8},{10,11... | collective-permute-start | bytes 3145736 | tf_op jit(solution)/shard_map/ppermute | solution.py:163
  95.5 1.2 add_convert_fusion.1
  98.2 6.5 %collective-permute-start.25 = (bf16[512,1024]{1,0:T(8,128)(2,1)S(1)}, bf16[512,1024]{1,0:T(8,128)(2,1)S(1)}, u32[]{:S(2)}, u32[]{:S(2)}) collective-permute-start(bf16[512,1024]{1,0:T(8,128)(2,1)S(1)} %add_convert_fusion.4), channel_id=1, source_target_pairs={{0,2},{7,5},{8,10},{15,13},{16,18},{23,21},{24,26},{31,29}} | collective-permute-start | bytes 3145736 | tf_op jit(solution)/shard_map/ppermute | solution.py:166
  104.7 7.5 %collective-permute-start.10 = (bf16[1024,512]{1,0:T(8,128)(2,1)S(1)}, bf16[1024,512]{1,0:T(8,128)(2,1)S(1)}, u32[]{:S(2)}, u32[]{:S(2)}) collective-permute-start(bf16[1024,512]{1,0:T(8,128)(2,1)S(1)} %collective-permute-done.9), channel_id=1, source_target_pairs={{0,1},{1,0},{2,3},{3,2},{4,5},{5,4},{6,7},{7,6},{8,9},{9,8},{10,11... | collective-permute-start | bytes 3145736 | tf_op jit(solution)/shard_map/ppermute | solution.py:163
  112.2 1.2 add_convert_fusion
  114.1 1.6 collective-permute-start.44
  117.4 5.4 %collective-permute-start.26 = (bf16[512,1024]{1,0:T(8,128)(2,1)S(1)}, bf16[512,1024]{1,0:T(8,128)(2,1)}, u32[]{:S(2)}, u32[]{:S(2)}) collective-permute-start(bf16[512,1024]{1,0:T(8,128)(2,1)S(1)} %add_convert_fusion.3), channel_id=1, source_target_pairs={{0,2},{2,4},{5,3},{7,5},{8,10},{10,12},{13,11},{15,13},{16,18},{18... | collective-permute-start | bytes 3145736 | tf_op jit(solution)/shard_map/ppermute | solution.py:166
  123.8 4.5 %convolution_convert_fusion.3.refs_0_ = bf16[1024,512]{1,0:T(8,128)(2,1)S(1)} fusion(bf16[1024,4096]{1,0:T(8,128)(2,1)S(1)} %get-tuple-element.13, bf16[4096,512]{1,0:T(8,128)(2,1)S(1)} %fence.13.refs_1_), kind=kOutput, calls=%fused_computation.21 | convolution fusion | flops 4295491584 | bytes 13631488 | tf_op jit(solution)/shard_map/dot_general | solution.py:260
  128.3 5.8 %collective-permute-done.26 = bf16[512,1024]{1,0:T(8,128)(2,1)} collective-permute-done((bf16[512,1024]{1,0:T(8,128)(2,1)S(1)}, bf16[512,1024]{1,0:T(8,128)(2,1)}, u32[]{:S(2)}, u32[]{:S(2)}) %collective-permute-start.26) | collective-permute-done | bytes 1048608 | tf_op jit(solution)/shard_map/ppermute | solution.py:166
  134.1 1.9 add_convert_fusion.2.refs_2_
  137.0 2.5 %convolution_convert_fusion.2 = bf16[256,4096]{1,0:T(8,128)(2,1)S(1)} fusion(bf16[1024,4096]{1,0:T(8,128)(2,1)S(1)} %get-tuple-element.14.refs_1_, bf16[1024,512]{1,0:T(8,128)(2,1)S(1)} %fence.14.refs_2_), kind=kOutput, calls=%fused_computation.2 | convolution fusion | flops 2148532224 | bytes 11010048 | tf_op jit(solution)/shard_map/dot_general | solution.py:170
  139.5 2.5 %convolution_convert_fusion.1 = bf16[256,4096]{1,0:T(8,128)(2,1)S(1)} fusion(bf16[1024,4096]{1,0:T(8,128)(2,1)S(1)} %get-tuple-element.14.refs_1_, bf16[1024,512]{1,0:T(8,128)(2,1)S(1)} %fence.14.refs_2_), kind=kOutput, calls=%fused_computation.1 | convolution fusion | flops 2148532224 | bytes 11010048 | tf_op jit(solution)/shard_map/dot_general | solution.py:170
  142.1 1.3 fusion.9
  145.1 6.1 %collective-permute-start.41 = (bf16[512,1024]{1,0:T(8,128)(2,1)}, bf16[512,1024]{1,0:T(8,128)(2,1)S(1)}, u32[]{:S(2)}, u32[]{:S(2)}) collective-permute-start(bf16[512,1024]{1,0:T(8,128)(2,1)} %copy-done.1), channel_id=1, source_target_pairs={{0,2},{2,4},{3,1},{4,6},{5,3},{7,5},{8,10},{10,12},{11,9},{12,14},... | collective-permute-start | bytes 3145736 | tf_op jit(solution)/shard_map/ppermute | solution.py:166
  151.2 1.4 add_convert_fusion.10.refs_3_
  153.2 1.4 add_convert_fusion.7.refs_4_
  154.6 4.4 %collective-permute-start.30 = (bf16[256,1024]{1,0:T(8,128)(2,1)S(1)}, bf16[256,1024]{1,0:T(8,128)(2,1)}, u32[]{:S(2)}, u32[]{:S(2)}) collective-permute-start(bf16[256,1024]{1,0:T(8,128)(2,1)S(1)} %add_convert_fusion.10.refs_3_), channel_id=1, source_target_pairs={{0,2},{7,5},{8,10},{15,13},{16,18},{23,21},{24,26},{31,29}} | collective-permute-start | bytes 1572872 | tf_op jit(solution)/shard_map/ppermute | solution.py:166
  159.0 2.1 %collective-permute-start.37 = (bf16[256,1024]{1,0:T(8,128)(2,1)S(1)}, bf16[256,1024]{1,0:T(8,128)(2,1)}, u32[]{:S(2)}, u32[]{:S(2)}) collective-permute-start(bf16[256,1024]{1,0:T(8,128)(2,1)S(1)} %add_convert_fusion.7.refs_4_), channel_id=1, source_target_pairs={{0,2},{7,5},{8,10},{15,13},{16,18},{23,21},{24,26},{31,29}} | collective-permute-start | bytes 1572872 | tf_op jit(solution)/shard_map/ppermute | solution.py:166
  161.7 2.2 %convert_add_fusion = (f32[4096,128]{1,0:T(8,128)S(1)}, f32[4096,128]{1,0:T(8,128)S(1)}) fusion(bf16[4096,128]{1,0:T(8,128)(2,1)S(1)} %get-tuple-element.19, bf16[4096,128]{1,0:T(8,128)(2,1)} %add_convert_fusion, bf16[4096,128]{1,0:T(8,128)(2,1)S(1)} %get-tuple-element.18, bf16[4096,128]{1,0:T(8,128)(2,1)} %add_convert_fusion.1), kind=kLoop, calls=%fused_computation.13 | loop fusion | flops 3145728 | bytes 8388608 | tf_op jit(solution)/shard_map/add | solution.py:273
  165.2 3.9 %subtract_convert_fusion = (bf16[8192,128]{1,0:T(8,128)(2,1)}, f32[8192,128]{1,0:T(8,128)}) fusion(bf16[8192,128]{1,0:T(8,128)(2,1)S(1)} %copy-done.14, f32[4096,128]{1,0:T(8,128)S(1)} %get-tuple-element.39, f32[4096,128]{1,0:T(8,128)S(1)} %get-tuple-element.40, f32[8192,128]{1,0:T(8,128)S(1)} %copy-done.12), kind=kLoop, calls=%fused_computation.5 | loop fusion | flops 10485760 | bytes 16777216 | tf_op jit(solution)/shard_map/convert_element_type | solution.py:132
  169.7 1.5 add_convert_fusion.9
  171.2 4.0 %collective-permute-start.31 = (bf16[256,1024]{1,0:T(8,128)(2,1)S(1)}, bf16[256,1024]{1,0:T(8,128)(2,1)S(1)}, u32[]{:S(2)}, u32[]{:S(2)}) collective-permute-start(bf16[256,1024]{1,0:T(8,128)(2,1)S(1)} %add_convert_fusion.9), channel_id=1, source_target_pairs={{0,2},{2,4},{5,3},{7,5},{8,10},{10,12},{13,11},{15,13},{16,18},{18... | collective-permute-start | bytes 1572872 | tf_op jit(solution)/shard_map/ppermute | solution.py:166
  175.3 1.5 add_convert_fusion.6
  176.7 4.1 %collective-permute-start.38 = (bf16[256,1024]{1,0:T(8,128)(2,1)S(1)}, bf16[256,1024]{1,0:T(8,128)(2,1)S(1)}, u32[]{:S(2)}, u32[]{:S(2)}) collective-permute-start(bf16[256,1024]{1,0:T(8,128)(2,1)S(1)} %add_convert_fusion.6), channel_id=1, source_target_pairs={{0,2},{2,4},{5,3},{7,5},{8,10},{10,12},{13,11},{15,13},{16,18},{18... | collective-permute-start | bytes 1572872 | tf_op jit(solution)/shard_map/ppermute | solution.py:166
  180.8 1.6 convert_add_fusion.2
  182.8 3.8 %collective-permute-start.32 = (bf16[256,1024]{1,0:T(8,128)(2,1)S(1)}, bf16[256,1024]{1,0:T(8,128)(2,1)S(1)}, u32[]{:S(2)}, u32[]{:S(2)}) collective-permute-start(bf16[256,1024]{1,0:T(8,128)(2,1)S(1)} %add_convert_fusion.8), channel_id=1, source_target_pairs={{0,2},{2,4},{3,1},{4,6},{5,3},{7,5},{8,10},{10,12},{11,9},{12,14},... | collective-permute-start | bytes 1572872 | tf_op jit(solution)/shard_map/ppermute | solution.py:166
  187.8 4.4 %collective-permute-start.39 = (bf16[256,1024]{1,0:T(8,128)(2,1)S(1)}, bf16[256,1024]{1,0:T(8,128)(2,1)S(1)}, u32[]{:S(2)}, u32[]{:S(2)}) collective-permute-start(bf16[256,1024]{1,0:T(8,128)(2,1)S(1)} %add_convert_fusion.5), channel_id=1, source_target_pairs={{0,2},{2,4},{3,1},{4,6},{5,3},{7,5},{8,10},{10,12},{11,9},{12,14},... | collective-permute-start | bytes 1572872 | tf_op jit(solution)/shard_map/ppermute | solution.py:166
  194.2 4.7 %collective-permute-done.39 = bf16[256,1024]{1,0:T(8,128)(2,1)S(1)} collective-permute-done((bf16[256,1024]{1,0:T(8,128)(2,1)S(1)}, bf16[256,1024]{1,0:T(8,128)(2,1)S(1)}, u32[]{:S(2)}, u32[]{:S(2)}) %collective-permute-start.39) | collective-permute-done | bytes 524320 | tf_op jit(solution)/shard_map/ppermute | solution.py:166
  200.1 1.3 copy.26
  202.8 1.3 copy.25
  (138 shorter events, 30.8 us)
Async XLA Ops:
  0.6 17.7 %copy-start.5 = (f32[4096]{0:T(1024)S(1)}, f32[4096]{0:T(1024)}, u32[]{:S(2)}) copy-start(f32[4096]{0:T(1024)} %param.10) | copy-start | bytes 49156
  1.4 2.2 %collective-permute-start.1 = (bf16[512,512]{1,0:T(8,128)(2,1)}, bf16[512,512]{1,0:T(8,128)(2,1)S(1)}, u32[]{:S(2)}, u32[]{:S(2)}) collective-permute-start(bf16[512,512]{1,0:T(8,128)(2,1)} %bitcast.42), channel_id=1, source_target_pairs={{0,1},{1,0},{2,3},{3,2},{4,5},{5,4},{6,7},{7,6},{8,9},{9,8},{10,11... | collective-permute-start | bytes 1572872 | tf_op jit(solution)/shard_map/ppermute | solution.py:163
  1.9 2.5 %collective-permute-start = (bf16[512,512]{1,0:T(8,128)(2,1)}, bf16[512,512]{1,0:T(8,128)(2,1)S(1)}, u32[]{:S(2)}, u32[]{:S(2)}) collective-permute-start(bf16[512,512]{1,0:T(8,128)(2,1)} %bitcast.40), channel_id=1, source_target_pairs={{0,1},{1,0},{2,3},{3,2},{4,5},{5,4},{6,7},{7,6},{8,9},{9,8},{10,11... | collective-permute-start | bytes 1572872 | tf_op jit(solution)/shard_map/ppermute | solution.py:163
  6.1 11.5 %collective-permute-start.3 = (bf16[1024,256]{1,0:T(8,128)(2,1)S(1)}, bf16[1024,256]{1,0:T(8,128)(2,1)}, u32[]{:S(2)}, u32[]{:S(2)}) collective-permute-start(bf16[1024,256]{1,0:T(8,128)(2,1)S(1)} %get-tuple-element.15), channel_id=1, source_target_pairs={{0,2},{2,4},{3,1},{4,6},{5,3},{7,5},{8,10},{10,12},{11,9},{12,14},... | collective-permute-start | bytes 1572872 | tf_op jit(solution)/shard_map/ppermute | solution.py:166
  11.7 18.9 %collective-permute-start.2 = (bf16[1024,256]{1,0:T(8,128)(2,1)S(1)}, bf16[1024,256]{1,0:T(8,128)(2,1)S(1)}, u32[]{:S(2)}, u32[]{:S(2)}) collective-permute-start(bf16[1024,256]{1,0:T(8,128)(2,1)S(1)} %get-tuple-element.12.refs_3_), channel_id=1, source_target_pairs={{0,2},{2,4},{3,1},{4,6},{5,3},{7,5},{8,10},{10,12},{11,9},{12,14},... | collective-permute-start | bytes 1572872 | tf_op jit(solution)/shard_map/ppermute | solution.py:166
  17.6 15.6 %collective-permute-start.4 = (bf16[1024,256]{1,0:T(8,128)(2,1)}, bf16[1024,256]{1,0:T(8,128)(2,1)S(1)}, u32[]{:S(2)}, u32[]{:S(2)}) collective-permute-start(bf16[1024,256]{1,0:T(8,128)(2,1)} %collective-permute-done.3), channel_id=1, source_target_pairs={{2,4},{3,1},{4,6},{5,3},{10,12},{11,9},{12,14},{13,11},{18,20},{19... | collective-permute-start | bytes 1572872 | tf_op jit(solution)/shard_map/ppermute | solution.py:166
  31.2 2.6 %collective-permute-start.5 = (bf16[1024,256]{1,0:T(8,128)(2,1)S(1)}, bf16[1024,256]{1,0:T(8,128)(2,1)S(1)}, u32[]{:S(2)}, u32[]{:S(2)}) collective-permute-start(bf16[1024,256]{1,0:T(8,128)(2,1)S(1)} %fence.8.refs_1_), channel_id=1, source_target_pairs={{2,4},{3,1},{4,6},{5,3},{10,12},{11,9},{12,14},{13,11},{18,20},{19... | collective-permute-start | bytes 1572872 | tf_op jit(solution)/shard_map/ppermute | solution.py:166
  32.0 18.6 %collective-permute-start.15 = (bf16[1024,256]{1,0:T(8,128)(2,1)S(1)}, bf16[1024,256]{1,0:T(8,128)(2,1)S(1)}, u32[]{:S(2)}, u32[]{:S(2)}) collective-permute-start(bf16[1024,256]{1,0:T(8,128)(2,1)S(1)} %fence.8.refs_1_), channel_id=1, source_target_pairs={{0,1},{1,0},{2,3},{3,2},{4,5},{5,4},{6,7},{7,6},{8,9},{9,8},{10,11... | collective-permute-start | bytes 1572872 | tf_op jit(solution)/shard_map/ppermute | solution.py:163
  33.1 23.1 %collective-permute-start.19 = (bf16[1024,256]{1,0:T(8,128)(2,1)}, bf16[1024,256]{1,0:T(8,128)(2,1)S(1)}, u32[]{:S(2)}, u32[]{:S(2)}) collective-permute-start(bf16[1024,256]{1,0:T(8,128)(2,1)} %collective-permute-done.3), channel_id=1, source_target_pairs={{0,1},{1,0},{2,3},{3,2},{4,5},{5,4},{6,7},{7,6},{8,9},{9,8},{10,11... | collective-permute-start | bytes 1572872 | tf_op jit(solution)/shard_map/ppermute | solution.py:163
  33.8 13.9 %collective-permute-start.6 = (bf16[1024,256]{1,0:T(8,128)(2,1)S(1)}, bf16[1024,256]{1,0:T(8,128)(2,1)S(1)}, u32[]{:S(2)}, u32[]{:S(2)}) collective-permute-start(bf16[1024,256]{1,0:T(8,128)(2,1)S(1)} %collective-permute-done.5), channel_id=1, source_target_pairs={{3,1},{4,6},{11,9},{12,14},{19,17},{20,22},{27,25},{28,30}} | collective-permute-start | bytes 1572872 | tf_op jit(solution)/shard_map/ppermute | solution.py:166
  34.5 15.3 %collective-permute-start.14 = (bf16[1024,256]{1,0:T(8,128)(2,1)S(1)}, bf16[1024,256]{1,0:T(8,128)(2,1)S(1)}, u32[]{:S(2)}, u32[]{:S(2)}) collective-permute-start(bf16[1024,256]{1,0:T(8,128)(2,1)S(1)} %collective-permute-done.5), channel_id=1, source_target_pairs={{0,1},{1,0},{2,3},{3,2},{4,5},{5,4},{6,7},{7,6},{8,9},{9,8},{10,11... | collective-permute-start | bytes 1572872 | tf_op jit(solution)/shard_map/ppermute | solution.py:163
  46.1 27.4 %collective-permute-start.20 = (bf16[4096,128]{1,0:T(8,128)(2,1)S(1)}, bf16[4096,128]{1,0:T(8,128)(2,1)S(1)}, u32[]{:S(2)}, u32[]{:S(2)}) collective-permute-start(bf16[4096,128]{1,0:T(8,128)(2,1)S(1)} %get-tuple-element.36), channel_id=1, source_target_pairs={{0,8},{8,0},{16,24},{24,16},{1,9},{9,1},{17,25},{25,17},{2,10},{10... | collective-permute-start | bytes 3145736 | tf_op jit(solution)/shard_map/ppermute | solution.py:240
  47.7 25.9 %collective-permute-start.21 = (bf16[4096,128]{1,0:T(8,128)(2,1)S(1)}, bf16[4096,128]{1,0:T(8,128)(2,1)S(1)}, u32[]{:S(2)}, u32[]{:S(2)}) collective-permute-start(bf16[4096,128]{1,0:T(8,128)(2,1)S(1)} %get-tuple-element.35), channel_id=1, source_target_pairs={{0,16},{8,24},{16,0},{24,8},{1,17},{9,25},{17,1},{25,9},{2,18},{10... | collective-permute-start | bytes 3145736 | tf_op jit(solution)/shard_map/ppermute | solution.py:240
  49.9 10.7 %collective-permute-start.16 = (bf16[1024,256]{1,0:T(8,128)(2,1)S(1)}, bf16[1024,256]{1,0:T(8,128)(2,1)S(1)}, u32[]{:S(2)}, u32[]{:S(2)}) collective-permute-start(bf16[1024,256]{1,0:T(8,128)(2,1)S(1)} %collective-permute-done.4.refs_2_), channel_id=1, source_target_pairs={{3,1},{4,6},{11,9},{12,14},{19,17},{20,22},{27,25},{28,30}} | collective-permute-start | bytes 1572872 | tf_op jit(solution)/shard_map/ppermute | solution.py:166
  50.7 14.4 %collective-permute-start.18 = (bf16[1024,256]{1,0:T(8,128)(2,1)S(1)}, bf16[1024,256]{1,0:T(8,128)(2,1)S(1)}, u32[]{:S(2)}, u32[]{:S(2)}) collective-permute-start(bf16[1024,256]{1,0:T(8,128)(2,1)S(1)} %collective-permute-done.4.refs_2_), channel_id=1, source_target_pairs={{0,1},{1,0},{2,3},{3,2},{4,5},{5,4},{6,7},{7,6},{8,9},{9,8},{10,11... | collective-permute-start | bytes 1572872 | tf_op jit(solution)/shard_map/ppermute | solution.py:163
  56.3 16.6 %collective-permute-start.7 = (bf16[1024,512]{1,0:T(8,128)(2,1)S(1)}, bf16[1024,512]{1,0:T(8,128)(2,1)S(1)}, u32[]{:S(2)}, u32[]{:S(2)}) collective-permute-start(bf16[1024,512]{1,0:T(8,128)(2,1)S(1)} %join_cores.3.refs_2_), channel_id=1, source_target_pairs={{0,2},{2,4},{3,1},{4,6},{5,3},{7,5},{8,10},{10,12},{11,9},{12,14},... | collective-permute-start | bytes 3145736 | tf_op jit(solution)/shard_map/ppermute | solution.py:166
  60.6 5.9 %collective-permute-start.13 = (bf16[1024,256]{1,0:T(8,128)(2,1)S(1)}, bf16[1024,256]{1,0:T(8,128)(2,1)S(1)}, u32[]{:S(2)}, u32[]{:S(2)}) collective-permute-start(bf16[1024,256]{1,0:T(8,128)(2,1)S(1)} %collective-permute-done.6.refs_3_), channel_id=1, source_target_pairs={{0,1},{1,0},{2,3},{3,2},{4,5},{5,4},{6,7},{7,6},{8,9},{9,8},{10,11... | collective-permute-start | bytes 1572872 | tf_op jit(solution)/shard_map/ppermute | solution.py:163
  65.0 2.2 %collective-permute-start.17 = (bf16[1024,256]{1,0:T(8,128)(2,1)S(1)}, bf16[1024,256]{1,0:T(8,128)(2,1)S(1)}, u32[]{:S(2)}, u32[]{:S(2)}) collective-permute-start(bf16[1024,256]{1,0:T(8,128)(2,1)S(1)} %collective-permute-done.16), channel_id=1, source_target_pairs={{0,1},{1,0},{2,3},{3,2},{4,5},{5,4},{6,7},{7,6},{8,9},{9,8},{10,11... | collective-permute-start | bytes 1572872 | tf_op jit(solution)/shard_map/ppermute | solution.py:163
  72.9 6.3 %collective-permute-start.8 = (bf16[1024,512]{1,0:T(8,128)(2,1)S(1)}, bf16[1024,512]{1,0:T(8,128)(2,1)S(1)}, u32[]{:S(2)}, u32[]{:S(2)}) collective-permute-start(bf16[1024,512]{1,0:T(8,128)(2,1)S(1)} %collective-permute-done.7.refs_2_), channel_id=1, source_target_pairs={{2,4},{3,1},{4,6},{5,3},{10,12},{11,9},{12,14},{13,11},{18,20},{19... | collective-permute-start | bytes 3145736 | tf_op jit(solution)/shard_map/ppermute | solution.py:166
  79.7 54.4 %copy-start = (bf16[512,4096]{1,0:T(8,128)(2,1)}, bf16[512,4096]{1,0:T(8,128)(2,1)S(1)}, u32[]{:S(2)}) copy-start(bf16[512,4096]{1,0:T(8,128)(2,1)S(1)} %fence.12.refs_1_) | copy-start | bytes 12582916
  79.7 15.8 %copy-start.11 = (bf16[4096,128]{1,0:T(8,128)(2,1)S(1)}, bf16[4096,128]{1,0:T(8,128)(2,1)}, u32[]{:S(2)}) copy-start(bf16[4096,128]{1,0:T(8,128)(2,1)} %copy-done.10) | copy-start | bytes 3145732
  81.0 16.8 %collective-permute-start.24 = (bf16[512,1024]{1,0:T(8,128)(2,1)S(1)}, bf16[512,1024]{1,0:T(8,128)(2,1)S(1)}, u32[]{:S(2)}, u32[]{:S(2)}) collective-permute-start(bf16[512,1024]{1,0:T(8,128)(2,1)S(1)} %get-tuple-element.28), channel_id=1, source_target_pairs={{0,1},{1,0},{2,3},{3,2},{4,5},{5,4},{6,7},{7,6},{8,9},{9,8},{10,11... | collective-permute-start | bytes 3145736 | tf_op jit(solution)/shard_map/ppermute | solution.py:163
  94.8 10.0 %collective-permute-start.9 = (bf16[1024,512]{1,0:T(8,128)(2,1)S(1)}, bf16[1024,512]{1,0:T(8,128)(2,1)S(1)}, u32[]{:S(2)}, u32[]{:S(2)}) collective-permute-start(bf16[1024,512]{1,0:T(8,128)(2,1)S(1)} %collective-permute-done.8.refs_2_), channel_id=1, source_target_pairs={{3,1},{4,6},{11,9},{12,14},{19,17},{20,22},{27,25},{28,30}} | collective-permute-start | bytes 3145736 | tf_op jit(solution)/shard_map/ppermute | solution.py:166
  96.7 17.3 %collective-permute-start.12 = (bf16[1024,512]{1,0:T(8,128)(2,1)S(1)}, bf16[1024,512]{1,0:T(8,128)(2,1)S(1)}, u32[]{:S(2)}, u32[]{:S(2)}) collective-permute-start(bf16[1024,512]{1,0:T(8,128)(2,1)S(1)} %collective-permute-done.7.refs_2_), channel_id=1, source_target_pairs={{0,1},{1,0},{2,3},{3,2},{4,5},{5,4},{6,7},{7,6},{8,9},{9,8},{10,11... | collective-permute-start | bytes 3145736 | tf_op jit(solution)/shard_map/ppermute | solution.py:163
  97.3 18.5 %collective-permute-start.23 = (bf16[512,1024]{1,0:T(8,128)(2,1)S(1)}, bf16[512,1024]{1,0:T(8,128)(2,1)S(1)}, u32[]{:S(2)}, u32[]{:S(2)}) collective-permute-start(bf16[512,1024]{1,0:T(8,128)(2,1)S(1)} %get-tuple-element.27), channel_id=1, source_target_pairs={{0,1},{1,0},{2,3},{3,2},{4,5},{5,4},{6,7},{7,6},{8,9},{9,8},{10,11... | collective-permute-start | bytes 3145736 | tf_op jit(solution)/shard_map/ppermute | solution.py:163
  97.3 16.1 %collective-permute-start.11 = (bf16[1024,512]{1,0:T(8,128)(2,1)S(1)}, bf16[1024,512]{1,0:T(8,128)(2,1)S(1)}, u32[]{:S(2)}, u32[]{:S(2)}) collective-permute-start(bf16[1024,512]{1,0:T(8,128)(2,1)S(1)} %collective-permute-done.8.refs_2_), channel_id=1, source_target_pairs={{0,1},{1,0},{2,3},{3,2},{4,5},{5,4},{6,7},{7,6},{8,9},{9,8},{10,11... | collective-permute-start | bytes 3145736 | tf_op jit(solution)/shard_map/ppermute | solution.py:163
  98.2 18.5 %collective-permute-start.25 = (bf16[512,1024]{1,0:T(8,128)(2,1)S(1)}, bf16[512,1024]{1,0:T(8,128)(2,1)S(1)}, u32[]{:S(2)}, u32[]{:S(2)}) collective-permute-start(bf16[512,1024]{1,0:T(8,128)(2,1)S(1)} %add_convert_fusion.4), channel_id=1, source_target_pairs={{0,2},{7,5},{8,10},{15,13},{16,18},{23,21},{24,26},{31,29}} | collective-permute-start | bytes 3145736 | tf_op jit(solution)/shard_map/ppermute | solution.py:166
  104.7 18.1 %collective-permute-start.10 = (bf16[1024,512]{1,0:T(8,128)(2,1)S(1)}, bf16[1024,512]{1,0:T(8,128)(2,1)S(1)}, u32[]{:S(2)}, u32[]{:S(2)}) collective-permute-start(bf16[1024,512]{1,0:T(8,128)(2,1)S(1)} %collective-permute-done.9), channel_id=1, source_target_pairs={{0,1},{1,0},{2,3},{3,2},{4,5},{5,4},{6,7},{7,6},{8,9},{9,8},{10,11... | collective-permute-start | bytes 3145736 | tf_op jit(solution)/shard_map/ppermute | solution.py:163
  113.4 41.2 %collective-permute-start.43 = (bf16[4096,128]{1,0:T(8,128)(2,1)}, bf16[4096,128]{1,0:T(8,128)(2,1)S(1)}, u32[]{:S(2)}, u32[]{:S(2)}) collective-permute-start(bf16[4096,128]{1,0:T(8,128)(2,1)} %add_convert_fusion.1), channel_id=1, source_target_pairs={{0,16},{8,24},{16,0},{24,8},{1,17},{9,25},{17,1},{25,9},{2,18},{10... | collective-permute-start | bytes 3145736 | tf_op jit(solution)/shard_map/ppermute | solution.py:240
  114.1 45.0 %collective-permute-start.44 = (bf16[4096,128]{1,0:T(8,128)(2,1)}, bf16[4096,128]{1,0:T(8,128)(2,1)S(1)}, u32[]{:S(2)}, u32[]{:S(2)}) collective-permute-start(bf16[4096,128]{1,0:T(8,128)(2,1)} %add_convert_fusion), channel_id=1, source_target_pairs={{0,8},{8,0},{16,24},{24,16},{1,9},{9,1},{17,25},{25,17},{2,10},{10... | collective-permute-start | bytes 3145736 | tf_op jit(solution)/shard_map/ppermute | solution.py:240
  115.8 12.5 %collective-permute-start.22 = (bf16[512,1024]{1,0:T(8,128)(2,1)}, bf16[512,1024]{1,0:T(8,128)(2,1)S(1)}, u32[]{:S(2)}, u32[]{:S(2)}) collective-permute-start(bf16[512,1024]{1,0:T(8,128)(2,1)} %get-tuple-element.26), channel_id=1, source_target_pairs={{0,1},{1,0},{2,3},{3,2},{4,5},{5,4},{6,7},{7,6},{8,9},{9,8},{10,11... | collective-permute-start | bytes 3145736 | tf_op jit(solution)/shard_map/ppermute | solution.py:163
  117.4 16.7 %collective-permute-start.26 = (bf16[512,1024]{1,0:T(8,128)(2,1)S(1)}, bf16[512,1024]{1,0:T(8,128)(2,1)}, u32[]{:S(2)}, u32[]{:S(2)}) collective-permute-start(bf16[512,1024]{1,0:T(8,128)(2,1)S(1)} %add_convert_fusion.3), channel_id=1, source_target_pairs={{0,2},{2,4},{5,3},{7,5},{8,10},{10,12},{13,11},{15,13},{16,18},{18... | collective-permute-start | bytes 3145736 | tf_op jit(solution)/shard_map/ppermute | solution.py:166
  143.4 7.8 %collective-permute-start.29 = (bf16[256,1024]{1,0:T(8,128)(2,1)}, bf16[256,1024]{1,0:T(8,128)(2,1)}, u32[]{:S(2)}, u32[]{:S(2)}) collective-permute-start(bf16[256,1024]{1,0:T(8,128)(2,1)} %get-tuple-element.31), channel_id=1, source_target_pairs={{0,1},{1,0},{2,3},{3,2},{4,5},{5,4},{6,7},{7,6},{8,9},{9,8},{10,11... | collective-permute-start | bytes 1572872 | tf_op jit(solution)/shard_map/ppermute | solution.py:163
  144.6 8.1 %collective-permute-start.36 = (bf16[256,1024]{1,0:T(8,128)(2,1)}, bf16[256,1024]{1,0:T(8,128)(2,1)}, u32[]{:S(2)}, u32[]{:S(2)}) collective-permute-start(bf16[256,1024]{1,0:T(8,128)(2,1)} %get-tuple-element.34), channel_id=1, source_target_pairs={{0,1},{1,0},{2,3},{3,2},{4,5},{5,4},{6,7},{7,6},{8,9},{9,8},{10,11... | collective-permute-start | bytes 1572872 | tf_op jit(solution)/shard_map/ppermute | solution.py:163
  145.1 35.8 %collective-permute-start.41 = (bf16[512,1024]{1,0:T(8,128)(2,1)}, bf16[512,1024]{1,0:T(8,128)(2,1)S(1)}, u32[]{:S(2)}, u32[]{:S(2)}) collective-permute-start(bf16[512,1024]{1,0:T(8,128)(2,1)} %copy-done.1), channel_id=1, source_target_pairs={{0,2},{2,4},{3,1},{4,6},{5,3},{7,5},{8,10},{10,12},{11,9},{12,14},... | collective-permute-start | bytes 3145736 | tf_op jit(solution)/shard_map/ppermute | solution.py:166
  151.2 17.9 %collective-permute-start.28 = (bf16[256,1024]{1,0:T(8,128)(2,1)}, bf16[256,1024]{1,0:T(8,128)(2,1)}, u32[]{:S(2)}, u32[]{:S(2)}) collective-permute-start(bf16[256,1024]{1,0:T(8,128)(2,1)} %get-tuple-element.30), channel_id=1, source_target_pairs={{0,1},{1,0},{2,3},{3,2},{4,5},{5,4},{6,7},{7,6},{8,9},{9,8},{10,11... | collective-permute-start | bytes 1572872 | tf_op jit(solution)/shard_map/ppermute | solution.py:163
  152.7 18.5 %collective-permute-start.35 = (bf16[256,1024]{1,0:T(8,128)(2,1)}, bf16[256,1024]{1,0:T(8,128)(2,1)}, u32[]{:S(2)}, u32[]{:S(2)}) collective-permute-start(bf16[256,1024]{1,0:T(8,128)(2,1)} %get-tuple-element.33), channel_id=1, source_target_pairs={{0,1},{1,0},{2,3},{3,2},{4,5},{5,4},{6,7},{7,6},{8,9},{9,8},{10,11... | collective-permute-start | bytes 1572872 | tf_op jit(solution)/shard_map/ppermute | solution.py:163
  154.6 14.6 %collective-permute-start.30 = (bf16[256,1024]{1,0:T(8,128)(2,1)S(1)}, bf16[256,1024]{1,0:T(8,128)(2,1)}, u32[]{:S(2)}, u32[]{:S(2)}) collective-permute-start(bf16[256,1024]{1,0:T(8,128)(2,1)S(1)} %add_convert_fusion.10.refs_3_), channel_id=1, source_target_pairs={{0,2},{7,5},{8,10},{15,13},{16,18},{23,21},{24,26},{31,29}} | collective-permute-start | bytes 1572872 | tf_op jit(solution)/shard_map/ppermute | solution.py:166
  159.0 16.2 %collective-permute-start.37 = (bf16[256,1024]{1,0:T(8,128)(2,1)S(1)}, bf16[256,1024]{1,0:T(8,128)(2,1)}, u32[]{:S(2)}, u32[]{:S(2)}) collective-permute-start(bf16[256,1024]{1,0:T(8,128)(2,1)S(1)} %add_convert_fusion.7.refs_4_), channel_id=1, source_target_pairs={{0,2},{7,5},{8,10},{15,13},{16,18},{23,21},{24,26},{31,29}} | collective-permute-start | bytes 1572872 | tf_op jit(solution)/shard_map/ppermute | solution.py:166
  169.1 13.4 %collective-permute-start.27 = (bf16[256,1024]{1,0:T(8,128)(2,1)S(1)}, bf16[256,1024]{1,0:T(8,128)(2,1)S(1)}, u32[]{:S(2)}, u32[]{:S(2)}) collective-permute-start(bf16[256,1024]{1,0:T(8,128)(2,1)S(1)} %copy-done.16), channel_id=1, source_target_pairs={{0,1},{1,0},{2,3},{3,2},{4,5},{5,4},{6,7},{7,6},{8,9},{9,8},{10,11... | collective-permute-start | bytes 1572872 | tf_op jit(solution)/shard_map/ppermute | solution.py:163
  169.2 17.4 %collective-permute-start.34 = (bf16[256,1024]{1,0:T(8,128)(2,1)S(1)}, bf16[256,1024]{1,0:T(8,128)(2,1)S(1)}, u32[]{:S(2)}, u32[]{:S(2)}) collective-permute-start(bf16[256,1024]{1,0:T(8,128)(2,1)S(1)} %copy-done.15), channel_id=1, source_target_pairs={{0,1},{1,0},{2,3},{3,2},{4,5},{5,4},{6,7},{7,6},{8,9},{9,8},{10,11... | collective-permute-start | bytes 1572872 | tf_op jit(solution)/shard_map/ppermute | solution.py:163
  171.2 11.3 %collective-permute-start.31 = (bf16[256,1024]{1,0:T(8,128)(2,1)S(1)}, bf16[256,1024]{1,0:T(8,128)(2,1)S(1)}, u32[]{:S(2)}, u32[]{:S(2)}) collective-permute-start(bf16[256,1024]{1,0:T(8,128)(2,1)S(1)} %add_convert_fusion.9), channel_id=1, source_target_pairs={{0,2},{2,4},{5,3},{7,5},{8,10},{10,12},{13,11},{15,13},{16,18},{18... | collective-permute-start | bytes 1572872 | tf_op jit(solution)/shard_map/ppermute | solution.py:166
  176.7 10.8 %collective-permute-start.38 = (bf16[256,1024]{1,0:T(8,128)(2,1)S(1)}, bf16[256,1024]{1,0:T(8,128)(2,1)S(1)}, u32[]{:S(2)}, u32[]{:S(2)}) collective-permute-start(bf16[256,1024]{1,0:T(8,128)(2,1)S(1)} %add_convert_fusion.6), channel_id=1, source_target_pairs={{0,2},{2,4},{5,3},{7,5},{8,10},{10,12},{13,11},{15,13},{16,18},{18... | collective-permute-start | bytes 1572872 | tf_op jit(solution)/shard_map/ppermute | solution.py:166
  182.8 10.5 %collective-permute-start.32 = (bf16[256,1024]{1,0:T(8,128)(2,1)S(1)}, bf16[256,1024]{1,0:T(8,128)(2,1)S(1)}, u32[]{:S(2)}, u32[]{:S(2)}) collective-permute-start(bf16[256,1024]{1,0:T(8,128)(2,1)S(1)} %add_convert_fusion.8), channel_id=1, source_target_pairs={{0,2},{2,4},{3,1},{4,6},{5,3},{7,5},{8,10},{10,12},{11,9},{12,14},... | collective-permute-start | bytes 1572872 | tf_op jit(solution)/shard_map/ppermute | solution.py:166
  187.8 11.1 %collective-permute-start.39 = (bf16[256,1024]{1,0:T(8,128)(2,1)S(1)}, bf16[256,1024]{1,0:T(8,128)(2,1)S(1)}, u32[]{:S(2)}, u32[]{:S(2)}) collective-permute-start(bf16[256,1024]{1,0:T(8,128)(2,1)S(1)} %add_convert_fusion.5), channel_id=1, source_target_pairs={{0,2},{2,4},{3,1},{4,6},{5,3},{7,5},{8,10},{10,12},{11,9},{12,14},... | collective-permute-start | bytes 1572872 | tf_op jit(solution)/shard_map/ppermute | solution.py:166
  192.3 7.5 %collective-permute-start.42 = (bf16[512,512]{1,0:T(8,128)(2,1)S(1)}, bf16[512,512]{1,0:T(8,128)(2,1)S(1)}, u32[]{:S(2)}, u32[]{:S(2)}) collective-permute-start(bf16[512,512]{1,0:T(8,128)(2,1)S(1)} %select_convert_fusion), channel_id=1, source_target_pairs={{0,1},{1,0},{2,3},{3,2},{4,5},{5,4},{6,7},{7,6},{8,9},{9,8},{10,11... | collective-permute-start | bytes 1572872 | tf_op jit(solution)/shard_map/ppermute | solution.py:163
  194.2 7.2 %collective-permute-start.33 = (bf16[256,512]{1,0:T(8,128)(2,1)}, bf16[256,512]{1,0:T(8,128)(2,1)S(1)}, u32[]{:S(2)}, u32[]{:S(2)}) collective-permute-start(bf16[256,512]{1,0:T(8,128)(2,1)} %select_convert_fusion.2), channel_id=1, source_target_pairs={{0,1},{1,0},{2,3},{3,2},{4,5},{5,4},{6,7},{7,6},{8,9},{9,8},{10,11... | collective-permute-start | bytes 786440 | tf_op jit(solution)/shard_map/ppermute | solution.py:163
  199.8 1.9 collective-permute-start.40
  (14 other events, 58.0 us)

commit v10 on v9

--- a/solution.py
+++ b/solution.py
@@ -195,18 +195,16 @@
             partners = jnp.where(core == 0, second, first)
             return (mine + swap(partners.astype(bf16)).astype(f32)).T
 
-    def gather(own, at_first=False):
+    def gather(own):
         along = list(own)
         pieces, others = [list(along)], []
         for step in range(1, chips):
             along = [move(part, lambda y: y >= step - 1) for part in along]
-            if at_first and step == 1:
-                along[:1] = fence(order, along[0])
             pieces.append(list(along))
             others.append([swap(part) for part in along])
         return pieces, others
 
-    def assemble(pieces, others):
+    def assemble(pieces, others, after=()):
         parts = []
         for j, first in enumerate(pieces[0]):
             shards = [first]
@@ -214,14 +212,13 @@
                 here, there = pieces[p][j], others[chips - p - 1][j]
                 shards.append(jnp.where(position >= p, here, there))
             parts.append(jnp.concatenate(shards, axis=0))
-        return fence(order, *parts)
+        return fence(order, *parts, after=after)
 
     first_own, second_own = value_weight[0], output_weight[0]
     first_partner, second_partner = swap(first_own), swap(second_own)
 
     joined = join_cores(order, first_own, first_partner, HALVES, (second_partner,))
-    normed, cotangent = prepare(order, tokens[0], out_cotangent[0], norm_gain, chips)
-    pieces, others = gather(joined, at_first=True)
+    pieces, others = gather(joined)
     last = pieces[-1]
 
     exponents = fence(order, delta_exponents, after=(pieces[2][1],))[0]
@@ -244,14 +241,16 @@
         sums.append((mine, theirs))
 
     joined = join_cores(order, second_own, second_partner, 1, (last[0],))
+    ahead = gather(joined)
+    normed, cotangent = prepare(order, tokens[0], out_cotangent[0], norm_gain, chips, (*others[-1], *others[-2]))
     values = jnp.concatenate(
         [
             jnp.dot(normed, part, preferred_element_type=f32).astype(bf16)
-            for part in assemble(pieces, others)
+            for part in assemble(pieces, others, (ahead[0][1][0],))
         ],
         axis=1,
     )
-    pieces, others = gather(joined)
+    pieces, others = ahead
     values = fence(order, values, after=(pieces[1][0], *early))[0]
     first = Gradient(values, cotangent, (pieces[2][0],))
     sent = [first.reduce(step) for step in range(1, chips)]

time: 205 us -> 204 us (level)
  starting transfers between devices: 108 us -> 104 us
    ppermute x23, starting transfers between devices: 45.1 us -> 39.8 us  [swap(): return lax.ppermute(value, 'fsdp', [(i, i ^ 1) for i in range(devices)])]
    unnamed x37 -> x45, local copies, waits for them, and re-layouts: 9.52 us -> 12.1 us
    pallas_call x11 -> x10, Pallas kernels: 14.6 us -> 14 us  [__call__(): pl.pallas_call(ordered, grid_spec=pltpu.PrefetchScalarGridSpec(num_scalar...]
  transfers between devices with their start and end apart: 45 -> 45, of which waited for: 12 -> 12; matrix products, arithmetic and copies ran while one was open for 24% -> 24% of each run, Pallas kernels for 7% -> 6%
where the time goes in v10:
time: 204 us; the launch traced here: 203 us
  starting transfers between devices  104 us (51%)
  other arithmetic  26.5 us (13%)
  waiting for transfers between devices  22.3 us (11%)
  matrix products  19.1 us (9%)
  local copies, waits for them, and re-layouts  15.1 us (7%)
  Pallas kernels  14 us (7%)
    ppermute x18, starting transfers between devices, move(): return lax.ppermute(value, 'fsdp', move_perm(chips, active))  58.8 us
    ppermute x23, starting transfers between devices, swap(): return lax.ppermute(value, 'fsdp', [(i, i ^ 1) for i in range(devices)])  39.8 us
    ppermute x18, waiting for transfers between devices, move(): return lax.ppermute(value, 'fsdp', move_perm(chips, active))  17.7 us
    pallas_call x10, Pallas kernels, __call__(): pl.pallas_call(ordered, grid_spec=pltpu.PrefetchScalarGridSpec(num_scalar...  14 us
    unnamed x45, local copies, waits for them, and re-layouts  12.1 us
    dot_general x3, matrix products, __init__(): lax.dot_general(mid, x, (((0,), (0,)), ((), ())), preferred_element_type=...  10 us
    convert_element_type x9, other arithmetic, message(): return term.astype(bf16)  9.2 us
    ppermute x4, starting transfers between devices, per_device(): lax.ppermute(mine, 'replica', [(i, i ^ bit) for i in range(replicas)])  5.44 us
  transfers between devices with their start and end apart: 45, of which 12 were waited for; matrix products, arithmetic and copies ran while one was open for 24% of the time, Pallas kernels for 6%

profile of v10, /device:TPU:0, one launch (start us, length us, event | category | flops | bytes accessed | tf_op | source)
XLA Modules:
  0.0 202.6 jit_solution(9105620919327731823)
XLA Ops:
  2.0 1.6 collective-permute-done.refs_2_.refs_1_
  6.1 5.7 %collective-permute-start.2 = (bf16[1024,256]{1,0:T(8,128)(2,1)S(1)}, bf16[1024,256]{1,0:T(8,128)(2,1)}, u32[]{:S(2)}, u32[]{:S(2)}) collective-permute-start(bf16[1024,256]{1,0:T(8,128)(2,1)S(1)} %get-tuple-element.13), channel_id=1, source_target_pairs={{0,2},{2,4},{3,1},{4,6},{5,3},{7,5},{8,10},{10,12},{11,9},{12,14},... | collective-permute-start | bytes 1572872 | tf_op jit(solution)/shard_map/ppermute | solution.py:166
  11.7 3.5 %collective-permute-start.4 = (bf16[1024,256]{1,0:T(8,128)(2,1)S(1)}, bf16[1024,256]{1,0:T(8,128)(2,1)}, u32[]{:S(2)}, u32[]{:S(2)}) collective-permute-start(bf16[1024,256]{1,0:T(8,128)(2,1)S(1)} %get-tuple-element.12.refs_1_), channel_id=1, source_target_pairs={{0,2},{2,4},{3,1},{4,6},{5,3},{7,5},{8,10},{10,12},{11,9},{12,14},... | collective-permute-start | bytes 1572872 | tf_op jit(solution)/shard_map/ppermute | solution.py:166
  15.2 2.4 %collective-permute-done.2 = bf16[1024,256]{1,0:T(8,128)(2,1)} collective-permute-done((bf16[1024,256]{1,0:T(8,128)(2,1)S(1)}, bf16[1024,256]{1,0:T(8,128)(2,1)}, u32[]{:S(2)}, u32[]{:S(2)}) %collective-permute-start.2) | collective-permute-done | bytes 524320 | tf_op jit(solution)/shard_map/ppermute | solution.py:166
  18.3 4.9 %collective-permute-done.4 = bf16[1024,256]{1,0:T(8,128)(2,1)} collective-permute-done((bf16[1024,256]{1,0:T(8,128)(2,1)S(1)}, bf16[1024,256]{1,0:T(8,128)(2,1)}, u32[]{:S(2)}, u32[]{:S(2)}) %collective-permute-start.4) | collective-permute-done | bytes 524320 | tf_op jit(solution)/shard_map/ppermute | solution.py:166
  25.8 9.7 %collective-permute-start.10 = (bf16[1024,256]{1,0:T(8,128)(2,1)S(1)}, bf16[1024,256]{1,0:T(8,128)(2,1)S(1)}, u32[]{:S(2)}, u32[]{:S(2)}) collective-permute-start(bf16[1024,256]{1,0:T(8,128)(2,1)S(1)} %collective-permute-done.5), channel_id=1, source_target_pairs={{0,1},{1,0},{2,3},{3,2},{4,5},{5,4},{6,7},{7,6},{8,9},{9,8},{10,11... | collective-permute-start | bytes 1572872 | tf_op jit(solution)/shard_map/ppermute | solution.py:163
  35.5 2.1 %fusion = (bf16[4096,128]{1,0:T(8,128)(2,1)S(1)}, bf16[4096,128]{1,0:T(8,128)(2,1)S(1)}) fusion(f32[4096]{0:T(1024)S(1)} %bitcast.51, bf16[1,8192,128]{2,1,0:T(8,128)(2,1)S(1)} %copy-done.11, f32[4096]{0:T(1024)S(1)} %bitcast.52), kind=kLoop, calls=%fused_computation.10 | loop fusion | flops 3145728 | bytes 4227072 | tf_op jit(solution)/shard_map/convert_element_type | solution.py:235
  37.7 1.7 collective-permute-start.20
  39.4 1.5 collective-permute-start.21
  42.4 5.5 %collective-permute-start.11 = (bf16[1024,256]{1,0:T(8,128)(2,1)S(1)}, bf16[1024,256]{1,0:T(8,128)(2,1)S(1)}, u32[]{:S(2)}, u32[]{:S(2)}) collective-permute-start(bf16[1024,256]{1,0:T(8,128)(2,1)S(1)} %collective-permute-done.3.refs_2_), channel_id=1, source_target_pairs={{0,1},{1,0},{2,3},{3,2},{4,5},{5,4},{6,7},{7,6},{8,9},{9,8},{10,11... | collective-permute-start | bytes 1572872 | tf_op jit(solution)/shard_map/ppermute | solution.py:163
  48.0 4.4 %collective-permute-start.12 = (bf16[1024,512]{1,0:T(8,128)(2,1)S(1)}, bf16[1024,512]{1,0:T(8,128)(2,1)S(1)}, u32[]{:S(2)}, u32[]{:S(2)}) collective-permute-start(bf16[1024,512]{1,0:T(8,128)(2,1)S(1)} %join_cores.3.refs_3_), channel_id=1, source_target_pairs={{0,2},{2,4},{3,1},{4,6},{5,3},{7,5},{8,10},{10,12},{11,9},{12,14},... | collective-permute-start | bytes 3145736 | tf_op jit(solution)/shard_map/ppermute | solution.py:166
  52.4 4.3 %collective-permute-start.7 = (bf16[1024,256]{1,0:T(8,128)(2,1)S(1)}, bf16[1024,256]{1,0:T(8,128)(2,1)S(1)}, u32[]{:S(2)}, u32[]{:S(2)}) collective-permute-start(bf16[1024,256]{1,0:T(8,128)(2,1)S(1)} %collective-permute-done.6.refs_3_), channel_id=1, source_target_pairs={{0,1},{1,0},{2,3},{3,2},{4,5},{5,4},{6,7},{7,6},{8,9},{9,8},{10,11... | collective-permute-start | bytes 1572872 | tf_op jit(solution)/shard_map/ppermute | solution.py:163
  56.9 1.3 collective-permute-done.7.refs_4_
  59.0 8.9 %prepare.1 = (bf16[1024,4096]{1,0:T(8,128)(2,1)S(1)}, bf16[1024,4096]{1,0:T(8,128)(2,1)S(1)}) custom-call(s32[6]{0:T(128)S(1)} %stack.27.place_ref, bf16[1024,4096]{1,0:T(8,128)(2,1)S(1)} %bitcast.41, bf16[1024,4096]{1,0:T(8,128)(2,1)} %bitcast.53, f32[1,4096]{1,0:T(1,128)S(1)} %bitcast.46, bf16[1024,512]{1,0:T(8,128)(2,1)S(1)} %join_cores.3.refs_3_, ...), custom_call_target="tpu_custom_call" | custom-call | flops 20000000000 | bytes 1 | tf_op jit(solution)/shard_map/prepare/pallas_call | solution.py:39
  67.9 3.3 %copy-done.5 = bf16[1024,4096]{1,0:T(8,128)(2,1)} copy-done((bf16[1024,4096]{1,0:T(8,128)(2,1)}, bf16[1024,4096]{1,0:T(8,128)(2,1)S(1)}, u32[]{:S(2)}) %copy-start.5) | copy-done | bytes 8388632
  72.2 2.3 %convolution_convert_fusion.5 = bf16[1024,256]{1,0:T(8,128)(2,1)S(1)} fusion(bf16[1024,4096]{1,0:T(8,128)(2,1)S(1)} %get-tuple-element.15.refs_2_, bf16[4096,256]{1,0:T(8,128)(2,1)S(1)} %get-tuple-element.16.refs_1_), kind=kOutput, calls=%fused_computation.23 | convolution fusion | flops 2147745792 | bytes 11010048 | tf_op jit(solution)/shard_map/dot_general | solution.py:248
  75.3 2.3 %convolution_convert_fusion.4 = bf16[1024,256]{1,0:T(8,128)(2,1)S(1)} fusion(bf16[1024,4096]{1,0:T(8,128)(2,1)S(1)} %get-tuple-element.15.refs_2_, bf16[4096,256]{1,0:T(8,128)(2,1)S(1)} %get-tuple-element.17), kind=kOutput, calls=%fused_computation.22 | convolution fusion | flops 2147745792 | bytes 11010048 | tf_op jit(solution)/shard_map/dot_general | solution.py:248
  78.3 4.9 %convolution_convert_fusion.refs_0_ = bf16[512,4096]{1,0:T(8,128)(2,1)S(1)} fusion(bf16[1024,512]{1,0:T(8,128)(2,1)S(1)} %fence.9.refs_1_, bf16[1024,4096]{1,0:T(8,128)(2,1)S(1)} %bitcast.48), kind=kOutput, calls=%fused_computation | convolution fusion | flops 4297064448 | bytes 13631488 | tf_op jit(solution)/shard_map/dot_general | solution.py:170
  84.3 8.7 %collective-permute-start.24 = (bf16[512,1024]{1,0:T(8,128)(2,1)S(1)}, bf16[512,1024]{1,0:T(8,128)(2,1)S(1)}, u32[]{:S(2)}, u32[]{:S(2)}) collective-permute-start(bf16[512,1024]{1,0:T(8,128)(2,1)S(1)} %get-tuple-element.28), channel_id=1, source_target_pairs={{0,1},{1,0},{2,3},{3,2},{4,5},{5,4},{6,7},{7,6},{8,9},{9,8},{10,11... | collective-permute-start | bytes 3145736 | tf_op jit(solution)/shard_map/ppermute | solution.py:163
  96.4 6.8 %collective-permute-start.25 = (bf16[512,1024]{1,0:T(8,128)(2,1)S(1)}, bf16[512,1024]{1,0:T(8,128)(2,1)S(1)}, u32[]{:S(2)}, u32[]{:S(2)}) collective-permute-start(bf16[512,1024]{1,0:T(8,128)(2,1)S(1)} %add_convert_fusion.4), channel_id=1, source_target_pairs={{0,2},{7,5},{8,10},{15,13},{16,18},{23,21},{24,26},{31,29}} | collective-permute-start | bytes 3145736 | tf_op jit(solution)/shard_map/ppermute | solution.py:166
  103.2 7.5 %collective-permute-start.15 = (bf16[1024,512]{1,0:T(8,128)(2,1)S(1)}, bf16[1024,512]{1,0:T(8,128)(2,1)S(1)}, u32[]{:S(2)}, u32[]{:S(2)}) collective-permute-start(bf16[1024,512]{1,0:T(8,128)(2,1)S(1)} %collective-permute-done.14), channel_id=1, source_target_pairs={{0,1},{1,0},{2,3},{3,2},{4,5},{5,4},{6,7},{7,6},{8,9},{9,8},{10,11... | collective-permute-start | bytes 3145736 | tf_op jit(solution)/shard_map/ppermute | solution.py:163
  112.7 1.6 collective-permute-start.44
  115.9 5.4 %collective-permute-start.26 = (bf16[512,1024]{1,0:T(8,128)(2,1)S(1)}, bf16[512,1024]{1,0:T(8,128)(2,1)}, u32[]{:S(2)}, u32[]{:S(2)}) collective-permute-start(bf16[512,1024]{1,0:T(8,128)(2,1)S(1)} %add_convert_fusion.3), channel_id=1, source_target_pairs={{0,2},{2,4},{5,3},{7,5},{8,10},{10,12},{13,11},{15,13},{16,18},{18... | collective-permute-start | bytes 3145736 | tf_op jit(solution)/shard_map/ppermute | solution.py:166
  122.3 1.3 slice-done.4
  123.6 1.4 slice-done.5
  125.0 4.5 %convolution_convert_fusion.3.refs_0_ = bf16[1024,512]{1,0:T(8,128)(2,1)S(1)} fusion(bf16[1024,4096]{1,0:T(8,128)(2,1)S(1)} %bitcast.50, bf16[4096,512]{1,0:T(8,128)(2,1)S(1)} %fence.11.refs_1_), kind=kOutput, calls=%fused_computation.21 | convolution fusion | flops 4295491584 | bytes 13631488 | tf_op jit(solution)/shard_map/dot_general | solution.py:259
  129.5 3.1 %collective-permute-done.26 = bf16[512,1024]{1,0:T(8,128)(2,1)} collective-permute-done((bf16[512,1024]{1,0:T(8,128)(2,1)S(1)}, bf16[512,1024]{1,0:T(8,128)(2,1)}, u32[]{:S(2)}, u32[]{:S(2)}) %collective-permute-start.26) | collective-permute-done | bytes 1048608 | tf_op jit(solution)/shard_map/ppermute | solution.py:166
  132.6 1.9 add_convert_fusion.2.refs_2_
  135.5 2.5 %convolution_convert_fusion.2 = bf16[256,4096]{1,0:T(8,128)(2,1)S(1)} fusion(bf16[1024,4096]{1,0:T(8,128)(2,1)S(1)} %get-tuple-element.15.refs_2_, bf16[1024,512]{1,0:T(8,128)(2,1)S(1)} %fence.12.refs_2_), kind=kOutput, calls=%fused_computation.2 | convolution fusion | flops 2148532224 | bytes 11010048 | tf_op jit(solution)/shard_map/dot_general | solution.py:170
  138.0 2.5 %convolution_convert_fusion.1 = bf16[256,4096]{1,0:T(8,128)(2,1)S(1)} fusion(bf16[1024,4096]{1,0:T(8,128)(2,1)S(1)} %get-tuple-element.15.refs_2_, bf16[1024,512]{1,0:T(8,128)(2,1)S(1)} %fence.12.refs_2_), kind=kOutput, calls=%fused_computation.1 | convolution fusion | flops 2148532224 | bytes 11010048 | tf_op jit(solution)/shard_map/dot_general | solution.py:170
  140.6 1.2 fusion.9
  143.5 6.1 %collective-permute-start.41 = (bf16[512,1024]{1,0:T(8,128)(2,1)}, bf16[512,1024]{1,0:T(8,128)(2,1)S(1)}, u32[]{:S(2)}, u32[]{:S(2)}) collective-permute-start(bf16[512,1024]{1,0:T(8,128)(2,1)} %copy-done.1), channel_id=1, source_target_pairs={{0,2},{2,4},{3,1},{4,6},{5,3},{7,5},{8,10},{10,12},{11,9},{12,14},... | collective-permute-start | bytes 3145736 | tf_op jit(solution)/shard_map/ppermute | solution.py:166
  149.7 1.4 add_convert_fusion.10.refs_3_
  151.7 1.4 add_convert_fusion.7.refs_4_
  153.1 4.4 %collective-permute-start.30 = (bf16[256,1024]{1,0:T(8,128)(2,1)S(1)}, bf16[256,1024]{1,0:T(8,128)(2,1)}, u32[]{:S(2)}, u32[]{:S(2)}) collective-permute-start(bf16[256,1024]{1,0:T(8,128)(2,1)S(1)} %add_convert_fusion.10.refs_3_), channel_id=1, source_target_pairs={{0,2},{7,5},{8,10},{15,13},{16,18},{23,21},{24,26},{31,29}} | collective-permute-start | bytes 1572872 | tf_op jit(solution)/shard_map/ppermute | solution.py:166
  157.5 2.1 %collective-permute-start.37 = (bf16[256,1024]{1,0:T(8,128)(2,1)S(1)}, bf16[256,1024]{1,0:T(8,128)(2,1)}, u32[]{:S(2)}, u32[]{:S(2)}) collective-permute-start(bf16[256,1024]{1,0:T(8,128)(2,1)S(1)} %add_convert_fusion.7.refs_4_), channel_id=1, source_target_pairs={{0,2},{7,5},{8,10},{15,13},{16,18},{23,21},{24,26},{31,29}} | collective-permute-start | bytes 1572872 | tf_op jit(solution)/shard_map/ppermute | solution.py:166
  160.2 2.2 %convert_add_fusion = (f32[4096,128]{1,0:T(8,128)S(1)}, f32[4096,128]{1,0:T(8,128)S(1)}) fusion(bf16[4096,128]{1,0:T(8,128)(2,1)S(1)} %get-tuple-element.19, bf16[4096,128]{1,0:T(8,128)(2,1)} %add_convert_fusion, bf16[4096,128]{1,0:T(8,128)(2,1)S(1)} %get-tuple-element.18, bf16[4096,128]{1,0:T(8,128)(2,1)} %add_convert_fusion.1), kind=kLoop, calls=%fused_computation.13 | loop fusion | flops 3145728 | bytes 8388608 | tf_op jit(solution)/shard_map/add | solution.py:272
  163.7 3.9 %subtract_convert_fusion = (bf16[8192,128]{1,0:T(8,128)(2,1)}, f32[8192,128]{1,0:T(8,128)}) fusion(bf16[8192,128]{1,0:T(8,128)(2,1)S(1)} %copy-done.12, f32[4096,128]{1,0:T(8,128)S(1)} %get-tuple-element.39, f32[4096,128]{1,0:T(8,128)S(1)} %get-tuple-element.40, f32[8192,128]{1,0:T(8,128)S(1)} %copy-done.10), kind=kLoop, calls=%fused_computation.5 | loop fusion | flops 10485760 | bytes 16777216 | tf_op jit(solution)/shard_map/convert_element_type | solution.py:132
  168.2 1.5 add_convert_fusion.9
  169.7 4.0 %collective-permute-start.31 = (bf16[256,1024]{1,0:T(8,128)(2,1)S(1)}, bf16[256,1024]{1,0:T(8,128)(2,1)S(1)}, u32[]{:S(2)}, u32[]{:S(2)}) collective-permute-start(bf16[256,1024]{1,0:T(8,128)(2,1)S(1)} %add_convert_fusion.9), channel_id=1, source_target_pairs={{0,2},{2,4},{5,3},{7,5},{8,10},{10,12},{13,11},{15,13},{16,18},{18... | collective-permute-start | bytes 1572872 | tf_op jit(solution)/shard_map/ppermute | solution.py:166
  173.7 1.5 add_convert_fusion.6
  175.2 4.1 %collective-permute-start.38 = (bf16[256,1024]{1,0:T(8,128)(2,1)S(1)}, bf16[256,1024]{1,0:T(8,128)(2,1)S(1)}, u32[]{:S(2)}, u32[]{:S(2)}) collective-permute-start(bf16[256,1024]{1,0:T(8,128)(2,1)S(1)} %add_convert_fusion.6), channel_id=1, source_target_pairs={{0,2},{2,4},{5,3},{7,5},{8,10},{10,12},{13,11},{15,13},{16,18},{18... | collective-permute-start | bytes 1572872 | tf_op jit(solution)/shard_map/ppermute | solution.py:166
  179.3 1.6 convert_add_fusion.2
  181.2 3.8 %collective-permute-start.32 = (bf16[256,1024]{1,0:T(8,128)(2,1)S(1)}, bf16[256,1024]{1,0:T(8,128)(2,1)S(1)}, u32[]{:S(2)}, u32[]{:S(2)}) collective-permute-start(bf16[256,1024]{1,0:T(8,128)(2,1)S(1)} %add_convert_fusion.8), channel_id=1, source_target_pairs={{0,2},{2,4},{3,1},{4,6},{5,3},{7,5},{8,10},{10,12},{11,9},{12,14},... | collective-permute-start | bytes 1572872 | tf_op jit(solution)/shard_map/ppermute | solution.py:166
  186.3 4.4 %collective-permute-start.39 = (bf16[256,1024]{1,0:T(8,128)(2,1)S(1)}, bf16[256,1024]{1,0:T(8,128)(2,1)S(1)}, u32[]{:S(2)}, u32[]{:S(2)}) collective-permute-start(bf16[256,1024]{1,0:T(8,128)(2,1)S(1)} %add_convert_fusion.5), channel_id=1, source_target_pairs={{0,2},{2,4},{3,1},{4,6},{5,3},{7,5},{8,10},{10,12},{11,9},{12,14},... | collective-permute-start | bytes 1572872 | tf_op jit(solution)/shard_map/ppermute | solution.py:166
  192.6 4.7 %collective-permute-done.39 = bf16[256,1024]{1,0:T(8,128)(2,1)S(1)} collective-permute-done((bf16[256,1024]{1,0:T(8,128)(2,1)S(1)}, bf16[256,1024]{1,0:T(8,128)(2,1)S(1)}, u32[]{:S(2)}, u32[]{:S(2)}) %collective-permute-start.39) | collective-permute-done | bytes 524320 | tf_op jit(solution)/shard_map/ppermute | solution.py:166
  198.5 1.3 copy.25
  201.3 1.3 copy.24
  (148 shorter events, 32.5 us)
Async XLA Ops:
  1.4 2.2 %collective-permute-start = (bf16[512,512]{1,0:T(8,128)(2,1)}, bf16[512,512]{1,0:T(8,128)(2,1)S(1)}, u32[]{:S(2)}, u32[]{:S(2)}) collective-permute-start(bf16[512,512]{1,0:T(8,128)(2,1)} %bitcast.44), channel_id=1, source_target_pairs={{0,1},{1,0},{2,3},{3,2},{4,5},{5,4},{6,7},{7,6},{8,9},{9,8},{10,11... | collective-permute-start | bytes 1572872 | tf_op jit(solution)/shard_map/ppermute | solution.py:163
  1.8 2.5 %collective-permute-start.1 = (bf16[512,512]{1,0:T(8,128)(2,1)}, bf16[512,512]{1,0:T(8,128)(2,1)S(1)}, u32[]{:S(2)}, u32[]{:S(2)}) collective-permute-start(bf16[512,512]{1,0:T(8,128)(2,1)} %bitcast.42), channel_id=1, source_target_pairs={{0,1},{1,0},{2,3},{3,2},{4,5},{5,4},{6,7},{7,6},{8,9},{9,8},{10,11... | collective-permute-start | bytes 1572872 | tf_op jit(solution)/shard_map/ppermute | solution.py:163
  6.1 11.5 %collective-permute-start.2 = (bf16[1024,256]{1,0:T(8,128)(2,1)S(1)}, bf16[1024,256]{1,0:T(8,128)(2,1)}, u32[]{:S(2)}, u32[]{:S(2)}) collective-permute-start(bf16[1024,256]{1,0:T(8,128)(2,1)S(1)} %get-tuple-element.13), channel_id=1, source_target_pairs={{0,2},{2,4},{3,1},{4,6},{5,3},{7,5},{8,10},{10,12},{11,9},{12,14},... | collective-permute-start | bytes 1572872 | tf_op jit(solution)/shard_map/ppermute | solution.py:166
  11.7 11.5 %collective-permute-start.4 = (bf16[1024,256]{1,0:T(8,128)(2,1)S(1)}, bf16[1024,256]{1,0:T(8,128)(2,1)}, u32[]{:S(2)}, u32[]{:S(2)}) collective-permute-start(bf16[1024,256]{1,0:T(8,128)(2,1)S(1)} %get-tuple-element.12.refs_1_), channel_id=1, source_target_pairs={{0,2},{2,4},{3,1},{4,6},{5,3},{7,5},{8,10},{10,12},{11,9},{12,14},... | collective-permute-start | bytes 1572872 | tf_op jit(solution)/shard_map/ppermute | solution.py:166
  17.6 6.9 %collective-permute-start.3 = (bf16[1024,256]{1,0:T(8,128)(2,1)}, bf16[1024,256]{1,0:T(8,128)(2,1)S(1)}, u32[]{:S(2)}, u32[]{:S(2)}) collective-permute-start(bf16[1024,256]{1,0:T(8,128)(2,1)} %collective-permute-done.2), channel_id=1, source_target_pairs={{2,4},{3,1},{4,6},{5,3},{10,12},{11,9},{12,14},{13,11},{18,20},{19... | collective-permute-start | bytes 1572872 | tf_op jit(solution)/shard_map/ppermute | solution.py:166
  23.2 1.9 collective-permute-start.5
  23.9 17.7 %collective-permute-start.18 = (bf16[1024,256]{1,0:T(8,128)(2,1)}, bf16[1024,256]{1,0:T(8,128)(2,1)S(1)}, u32[]{:S(2)}, u32[]{:S(2)}) collective-permute-start(bf16[1024,256]{1,0:T(8,128)(2,1)} %collective-permute-done.4), channel_id=1, source_target_pairs={{0,1},{1,0},{2,3},{3,2},{4,5},{5,4},{6,7},{7,6},{8,9},{9,8},{10,11... | collective-permute-start | bytes 1572872 | tf_op jit(solution)/shard_map/ppermute | solution.py:163
  24.4 23.6 %collective-permute-start.19 = (bf16[1024,256]{1,0:T(8,128)(2,1)}, bf16[1024,256]{1,0:T(8,128)(2,1)S(1)}, u32[]{:S(2)}, u32[]{:S(2)}) collective-permute-start(bf16[1024,256]{1,0:T(8,128)(2,1)} %collective-permute-done.2), channel_id=1, source_target_pairs={{0,1},{1,0},{2,3},{3,2},{4,5},{5,4},{6,7},{7,6},{8,9},{9,8},{10,11... | collective-permute-start | bytes 1572872 | tf_op jit(solution)/shard_map/ppermute | solution.py:163
  25.1 14.3 %collective-permute-start.6 = (bf16[1024,256]{1,0:T(8,128)(2,1)S(1)}, bf16[1024,256]{1,0:T(8,128)(2,1)S(1)}, u32[]{:S(2)}, u32[]{:S(2)}) collective-permute-start(bf16[1024,256]{1,0:T(8,128)(2,1)S(1)} %collective-permute-done.5), channel_id=1, source_target_pairs={{3,1},{4,6},{11,9},{12,14},{19,17},{20,22},{27,25},{28,30}} | collective-permute-start | bytes 1572872 | tf_op jit(solution)/shard_map/ppermute | solution.py:166
  25.8 16.6 %collective-permute-start.10 = (bf16[1024,256]{1,0:T(8,128)(2,1)S(1)}, bf16[1024,256]{1,0:T(8,128)(2,1)S(1)}, u32[]{:S(2)}, u32[]{:S(2)}) collective-permute-start(bf16[1024,256]{1,0:T(8,128)(2,1)S(1)} %collective-permute-done.5), channel_id=1, source_target_pairs={{0,1},{1,0},{2,3},{3,2},{4,5},{5,4},{6,7},{7,6},{8,9},{9,8},{10,11... | collective-permute-start | bytes 1572872 | tf_op jit(solution)/shard_map/ppermute | solution.py:163
  35.5 23.4 %slice-start = ((s8[8388608]{0:T(1024)(128)(4,1)}), s8[4194304]{0:T(1024)(128)(4,1)S(1)}, s32[]{:S(2)}) async-start(s8[8388608]{0:T(1024)(128)(4,1)} %bitcast.39), calls=%async_computation | async-start | bytes 8388608
  37.7 40.0 %collective-permute-start.20 = (bf16[4096,128]{1,0:T(8,128)(2,1)S(1)}, bf16[4096,128]{1,0:T(8,128)(2,1)S(1)}, u32[]{:S(2)}, u32[]{:S(2)}) collective-permute-start(bf16[4096,128]{1,0:T(8,128)(2,1)S(1)} %get-tuple-element.36), channel_id=1, source_target_pairs={{0,8},{8,0},{16,24},{24,16},{1,9},{9,1},{17,25},{25,17},{2,10},{10... | collective-permute-start | bytes 3145736 | tf_op jit(solution)/shard_map/ppermute | solution.py:237
  39.4 19.6 %slice-start.1 = ((s8[8388608]{0:T(1024)(128)(4,1)}), s8[4194304]{0:T(1024)(128)(4,1)S(1)}, s32[]{:S(2)}) async-start(s8[8388608]{0:T(1024)(128)(4,1)} %bitcast.39), calls=%async_computation.1 | async-start | bytes 8388608
  39.4 38.3 %collective-permute-start.21 = (bf16[4096,128]{1,0:T(8,128)(2,1)S(1)}, bf16[4096,128]{1,0:T(8,128)(2,1)S(1)}, u32[]{:S(2)}, u32[]{:S(2)}) collective-permute-start(bf16[4096,128]{1,0:T(8,128)(2,1)S(1)} %get-tuple-element.35), channel_id=1, source_target_pairs={{0,16},{8,24},{16,0},{24,8},{1,17},{9,25},{17,1},{25,9},{2,18},{10... | collective-permute-start | bytes 3145736 | tf_op jit(solution)/shard_map/ppermute | solution.py:237
  41.6 10.8 %collective-permute-start.8 = (bf16[1024,256]{1,0:T(8,128)(2,1)S(1)}, bf16[1024,256]{1,0:T(8,128)(2,1)S(1)}, u32[]{:S(2)}, u32[]{:S(2)}) collective-permute-start(bf16[1024,256]{1,0:T(8,128)(2,1)S(1)} %collective-permute-done.3.refs_2_), channel_id=1, source_target_pairs={{3,1},{4,6},{11,9},{12,14},{19,17},{20,22},{27,25},{28,30}} | collective-permute-start | bytes 1572872 | tf_op jit(solution)/shard_map/ppermute | solution.py:166
  42.4 14.4 %collective-permute-start.11 = (bf16[1024,256]{1,0:T(8,128)(2,1)S(1)}, bf16[1024,256]{1,0:T(8,128)(2,1)S(1)}, u32[]{:S(2)}, u32[]{:S(2)}) collective-permute-start(bf16[1024,256]{1,0:T(8,128)(2,1)S(1)} %collective-permute-done.3.refs_2_), channel_id=1, source_target_pairs={{0,1},{1,0},{2,3},{3,2},{4,5},{5,4},{6,7},{7,6},{8,9},{9,8},{10,11... | collective-permute-start | bytes 1572872 | tf_op jit(solution)/shard_map/ppermute | solution.py:163
  48.0 23.6 %collective-permute-start.12 = (bf16[1024,512]{1,0:T(8,128)(2,1)S(1)}, bf16[1024,512]{1,0:T(8,128)(2,1)S(1)}, u32[]{:S(2)}, u32[]{:S(2)}) collective-permute-start(bf16[1024,512]{1,0:T(8,128)(2,1)S(1)} %join_cores.3.refs_3_), channel_id=1, source_target_pairs={{0,2},{2,4},{3,1},{4,6},{5,3},{7,5},{8,10},{10,12},{11,9},{12,14},... | collective-permute-start | bytes 3145736 | tf_op jit(solution)/shard_map/ppermute | solution.py:166
  52.4 5.8 %collective-permute-start.7 = (bf16[1024,256]{1,0:T(8,128)(2,1)S(1)}, bf16[1024,256]{1,0:T(8,128)(2,1)S(1)}, u32[]{:S(2)}, u32[]{:S(2)}) collective-permute-start(bf16[1024,256]{1,0:T(8,128)(2,1)S(1)} %collective-permute-done.6.refs_3_), channel_id=1, source_target_pairs={{0,1},{1,0},{2,3},{3,2},{4,5},{5,4},{6,7},{7,6},{8,9},{9,8},{10,11... | collective-permute-start | bytes 1572872 | tf_op jit(solution)/shard_map/ppermute | solution.py:163
  56.7 2.2 %collective-permute-start.9 = (bf16[1024,256]{1,0:T(8,128)(2,1)S(1)}, bf16[1024,256]{1,0:T(8,128)(2,1)S(1)}, u32[]{:S(2)}, u32[]{:S(2)}) collective-permute-start(bf16[1024,256]{1,0:T(8,128)(2,1)S(1)} %collective-permute-done.8), channel_id=1, source_target_pairs={{0,1},{1,0},{2,3},{3,2},{4,5},{5,4},{6,7},{7,6},{8,9},{9,8},{10,11... | collective-permute-start | bytes 1572872 | tf_op jit(solution)/shard_map/ppermute | solution.py:163
  74.5 8.7 %collective-permute-start.13 = (bf16[1024,512]{1,0:T(8,128)(2,1)S(1)}, bf16[1024,512]{1,0:T(8,128)(2,1)S(1)}, u32[]{:S(2)}, u32[]{:S(2)}) collective-permute-start(bf16[1024,512]{1,0:T(8,128)(2,1)S(1)} %collective-permute-done.12.refs_3_.refs_2_), channel_id=1, source_target_pairs={{2,4},{3,1},{4,6},{5,3},{10,12},{11,9},{12,14},{13,11},{18,20},{19... | collective-permute-start | bytes 3145736 | tf_op jit(solution)/shard_map/ppermute | solution.py:166
  83.8 48.8 %copy-start = (bf16[512,4096]{1,0:T(8,128)(2,1)}, bf16[512,4096]{1,0:T(8,128)(2,1)S(1)}, u32[]{:S(2)}) copy-start(bf16[512,4096]{1,0:T(8,128)(2,1)S(1)} %fence.10.refs_1_) | copy-start | bytes 12582916
  84.3 11.8 %collective-permute-start.24 = (bf16[512,1024]{1,0:T(8,128)(2,1)S(1)}, bf16[512,1024]{1,0:T(8,128)(2,1)S(1)}, u32[]{:S(2)}, u32[]{:S(2)}) collective-permute-start(bf16[512,1024]{1,0:T(8,128)(2,1)S(1)} %get-tuple-element.28), channel_id=1, source_target_pairs={{0,1},{1,0},{2,3},{3,2},{4,5},{5,4},{6,7},{7,6},{8,9},{9,8},{10,11... | collective-permute-start | bytes 3145736 | tf_op jit(solution)/shard_map/ppermute | solution.py:163
  93.0 10.3 %collective-permute-start.14 = (bf16[1024,512]{1,0:T(8,128)(2,1)S(1)}, bf16[1024,512]{1,0:T(8,128)(2,1)S(1)}, u32[]{:S(2)}, u32[]{:S(2)}) collective-permute-start(bf16[1024,512]{1,0:T(8,128)(2,1)S(1)} %collective-permute-done.13.refs_2_), channel_id=1, source_target_pairs={{3,1},{4,6},{11,9},{12,14},{19,17},{20,22},{27,25},{28,30}} | collective-permute-start | bytes 3145736 | tf_op jit(solution)/shard_map/ppermute | solution.py:166
  94.9 17.0 %collective-permute-start.17 = (bf16[1024,512]{1,0:T(8,128)(2,1)S(1)}, bf16[1024,512]{1,0:T(8,128)(2,1)S(1)}, u32[]{:S(2)}, u32[]{:S(2)}) collective-permute-start(bf16[1024,512]{1,0:T(8,128)(2,1)S(1)} %collective-permute-done.12.refs_3_.refs_2_), channel_id=1, source_target_pairs={{0,1},{1,0},{2,3},{3,2},{4,5},{5,4},{6,7},{7,6},{8,9},{9,8},{10,11... | collective-permute-start | bytes 3145736 | tf_op jit(solution)/shard_map/ppermute | solution.py:163
  95.5 18.9 %collective-permute-start.23 = (bf16[512,1024]{1,0:T(8,128)(2,1)S(1)}, bf16[512,1024]{1,0:T(8,128)(2,1)S(1)}, u32[]{:S(2)}, u32[]{:S(2)}) collective-permute-start(bf16[512,1024]{1,0:T(8,128)(2,1)S(1)} %get-tuple-element.27), channel_id=1, source_target_pairs={{0,1},{1,0},{2,3},{3,2},{4,5},{5,4},{6,7},{7,6},{8,9},{9,8},{10,11... | collective-permute-start | bytes 3145736 | tf_op jit(solution)/shard_map/ppermute | solution.py:163
  95.5 17.2 %collective-permute-start.16 = (bf16[1024,512]{1,0:T(8,128)(2,1)S(1)}, bf16[1024,512]{1,0:T(8,128)(2,1)S(1)}, u32[]{:S(2)}, u32[]{:S(2)}) collective-permute-start(bf16[1024,512]{1,0:T(8,128)(2,1)S(1)} %collective-permute-done.13.refs_2_), channel_id=1, source_target_pairs={{0,1},{1,0},{2,3},{3,2},{4,5},{5,4},{6,7},{7,6},{8,9},{9,8},{10,11... | collective-permute-start | bytes 3145736 | tf_op jit(solution)/shard_map/ppermute | solution.py:163
  96.4 18.8 %collective-permute-start.25 = (bf16[512,1024]{1,0:T(8,128)(2,1)S(1)}, bf16[512,1024]{1,0:T(8,128)(2,1)S(1)}, u32[]{:S(2)}, u32[]{:S(2)}) collective-permute-start(bf16[512,1024]{1,0:T(8,128)(2,1)S(1)} %add_convert_fusion.4), channel_id=1, source_target_pairs={{0,2},{7,5},{8,10},{15,13},{16,18},{23,21},{24,26},{31,29}} | collective-permute-start | bytes 3145736 | tf_op jit(solution)/shard_map/ppermute | solution.py:166
  103.2 18.1 %collective-permute-start.15 = (bf16[1024,512]{1,0:T(8,128)(2,1)S(1)}, bf16[1024,512]{1,0:T(8,128)(2,1)S(1)}, u32[]{:S(2)}, u32[]{:S(2)}) collective-permute-start(bf16[1024,512]{1,0:T(8,128)(2,1)S(1)} %collective-permute-done.14), channel_id=1, source_target_pairs={{0,1},{1,0},{2,3},{3,2},{4,5},{5,4},{6,7},{7,6},{8,9},{9,8},{10,11... | collective-permute-start | bytes 3145736 | tf_op jit(solution)/shard_map/ppermute | solution.py:163
  112.0 41.1 %collective-permute-start.43 = (bf16[4096,128]{1,0:T(8,128)(2,1)}, bf16[4096,128]{1,0:T(8,128)(2,1)S(1)}, u32[]{:S(2)}, u32[]{:S(2)}) collective-permute-start(bf16[4096,128]{1,0:T(8,128)(2,1)} %add_convert_fusion.1), channel_id=1, source_target_pairs={{0,16},{8,24},{16,0},{24,8},{1,17},{9,25},{17,1},{25,9},{2,18},{10... | collective-permute-start | bytes 3145736 | tf_op jit(solution)/shard_map/ppermute | solution.py:237
  112.7 44.8 %collective-permute-start.44 = (bf16[4096,128]{1,0:T(8,128)(2,1)}, bf16[4096,128]{1,0:T(8,128)(2,1)S(1)}, u32[]{:S(2)}, u32[]{:S(2)}) collective-permute-start(bf16[4096,128]{1,0:T(8,128)(2,1)} %add_convert_fusion), channel_id=1, source_target_pairs={{0,8},{8,0},{16,24},{24,16},{1,9},{9,1},{17,25},{25,17},{2,10},{10... | collective-permute-start | bytes 3145736 | tf_op jit(solution)/shard_map/ppermute | solution.py:237
  114.4 15.1 %collective-permute-start.22 = (bf16[512,1024]{1,0:T(8,128)(2,1)S(1)}, bf16[512,1024]{1,0:T(8,128)(2,1)S(1)}, u32[]{:S(2)}, u32[]{:S(2)}) collective-permute-start(bf16[512,1024]{1,0:T(8,128)(2,1)S(1)} %get-tuple-element.26), channel_id=1, source_target_pairs={{0,1},{1,0},{2,3},{3,2},{4,5},{5,4},{6,7},{7,6},{8,9},{9,8},{10,11... | collective-permute-start | bytes 3145736 | tf_op jit(solution)/shard_map/ppermute | solution.py:163
  115.9 16.7 %collective-permute-start.26 = (bf16[512,1024]{1,0:T(8,128)(2,1)S(1)}, bf16[512,1024]{1,0:T(8,128)(2,1)}, u32[]{:S(2)}, u32[]{:S(2)}) collective-permute-start(bf16[512,1024]{1,0:T(8,128)(2,1)S(1)} %add_convert_fusion.3), channel_id=1, source_target_pairs={{0,2},{2,4},{5,3},{7,5},{8,10},{10,12},{13,11},{15,13},{16,18},{18... | collective-permute-start | bytes 3145736 | tf_op jit(solution)/shard_map/ppermute | solution.py:166
  141.8 7.8 %collective-permute-start.29 = (bf16[256,1024]{1,0:T(8,128)(2,1)}, bf16[256,1024]{1,0:T(8,128)(2,1)}, u32[]{:S(2)}, u32[]{:S(2)}) collective-permute-start(bf16[256,1024]{1,0:T(8,128)(2,1)} %get-tuple-element.31), channel_id=1, source_target_pairs={{0,1},{1,0},{2,3},{3,2},{4,5},{5,4},{6,7},{7,6},{8,9},{9,8},{10,11... | collective-permute-start | bytes 1572872 | tf_op jit(solution)/shard_map/ppermute | solution.py:163
  143.0 8.1 %collective-permute-start.36 = (bf16[256,1024]{1,0:T(8,128)(2,1)}, bf16[256,1024]{1,0:T(8,128)(2,1)}, u32[]{:S(2)}, u32[]{:S(2)}) collective-permute-start(bf16[256,1024]{1,0:T(8,128)(2,1)} %get-tuple-element.34), channel_id=1, source_target_pairs={{0,1},{1,0},{2,3},{3,2},{4,5},{5,4},{6,7},{7,6},{8,9},{9,8},{10,11... | collective-permute-start | bytes 1572872 | tf_op jit(solution)/shard_map/ppermute | solution.py:163
  143.5 35.8 %collective-permute-start.41 = (bf16[512,1024]{1,0:T(8,128)(2,1)}, bf16[512,1024]{1,0:T(8,128)(2,1)S(1)}, u32[]{:S(2)}, u32[]{:S(2)}) collective-permute-start(bf16[512,1024]{1,0:T(8,128)(2,1)} %copy-done.1), channel_id=1, source_target_pairs={{0,2},{2,4},{3,1},{4,6},{5,3},{7,5},{8,10},{10,12},{11,9},{12,14},... | collective-permute-start | bytes 3145736 | tf_op jit(solution)/shard_map/ppermute | solution.py:166
  149.6 18.0 %collective-permute-start.28 = (bf16[256,1024]{1,0:T(8,128)(2,1)}, bf16[256,1024]{1,0:T(8,128)(2,1)}, u32[]{:S(2)}, u32[]{:S(2)}) collective-permute-start(bf16[256,1024]{1,0:T(8,128)(2,1)} %get-tuple-element.30), channel_id=1, source_target_pairs={{0,1},{1,0},{2,3},{3,2},{4,5},{5,4},{6,7},{7,6},{8,9},{9,8},{10,11... | collective-permute-start | bytes 1572872 | tf_op jit(solution)/shard_map/ppermute | solution.py:163
  151.1 18.6 %collective-permute-start.35 = (bf16[256,1024]{1,0:T(8,128)(2,1)}, bf16[256,1024]{1,0:T(8,128)(2,1)}, u32[]{:S(2)}, u32[]{:S(2)}) collective-permute-start(bf16[256,1024]{1,0:T(8,128)(2,1)} %get-tuple-element.33), channel_id=1, source_target_pairs={{0,1},{1,0},{2,3},{3,2},{4,5},{5,4},{6,7},{7,6},{8,9},{9,8},{10,11... | collective-permute-start | bytes 1572872 | tf_op jit(solution)/shard_map/ppermute | solution.py:163
  153.1 14.6 %collective-permute-start.30 = (bf16[256,1024]{1,0:T(8,128)(2,1)S(1)}, bf16[256,1024]{1,0:T(8,128)(2,1)}, u32[]{:S(2)}, u32[]{:S(2)}) collective-permute-start(bf16[256,1024]{1,0:T(8,128)(2,1)S(1)} %add_convert_fusion.10.refs_3_), channel_id=1, source_target_pairs={{0,2},{7,5},{8,10},{15,13},{16,18},{23,21},{24,26},{31,29}} | collective-permute-start | bytes 1572872 | tf_op jit(solution)/shard_map/ppermute | solution.py:166
  157.5 16.2 %collective-permute-start.37 = (bf16[256,1024]{1,0:T(8,128)(2,1)S(1)}, bf16[256,1024]{1,0:T(8,128)(2,1)}, u32[]{:S(2)}, u32[]{:S(2)}) collective-permute-start(bf16[256,1024]{1,0:T(8,128)(2,1)S(1)} %add_convert_fusion.7.refs_4_), channel_id=1, source_target_pairs={{0,2},{7,5},{8,10},{15,13},{16,18},{23,21},{24,26},{31,29}} | collective-permute-start | bytes 1572872 | tf_op jit(solution)/shard_map/ppermute | solution.py:166
  167.6 13.3 %collective-permute-start.27 = (bf16[256,1024]{1,0:T(8,128)(2,1)S(1)}, bf16[256,1024]{1,0:T(8,128)(2,1)S(1)}, u32[]{:S(2)}, u32[]{:S(2)}) collective-permute-start(bf16[256,1024]{1,0:T(8,128)(2,1)S(1)} %copy-done.14), channel_id=1, source_target_pairs={{0,1},{1,0},{2,3},{3,2},{4,5},{5,4},{6,7},{7,6},{8,9},{9,8},{10,11... | collective-permute-start | bytes 1572872 | tf_op jit(solution)/shard_map/ppermute | solution.py:163
  167.7 17.4 %collective-permute-start.34 = (bf16[256,1024]{1,0:T(8,128)(2,1)S(1)}, bf16[256,1024]{1,0:T(8,128)(2,1)S(1)}, u32[]{:S(2)}, u32[]{:S(2)}) collective-permute-start(bf16[256,1024]{1,0:T(8,128)(2,1)S(1)} %copy-done.13), channel_id=1, source_target_pairs={{0,1},{1,0},{2,3},{3,2},{4,5},{5,4},{6,7},{7,6},{8,9},{9,8},{10,11... | collective-permute-start | bytes 1572872 | tf_op jit(solution)/shard_map/ppermute | solution.py:163
  169.7 11.2 %collective-permute-start.31 = (bf16[256,1024]{1,0:T(8,128)(2,1)S(1)}, bf16[256,1024]{1,0:T(8,128)(2,1)S(1)}, u32[]{:S(2)}, u32[]{:S(2)}) collective-permute-start(bf16[256,1024]{1,0:T(8,128)(2,1)S(1)} %add_convert_fusion.9), channel_id=1, source_target_pairs={{0,2},{2,4},{5,3},{7,5},{8,10},{10,12},{13,11},{15,13},{16,18},{18... | collective-permute-start | bytes 1572872 | tf_op jit(solution)/shard_map/ppermute | solution.py:166
  175.2 10.8 %collective-permute-start.38 = (bf16[256,1024]{1,0:T(8,128)(2,1)S(1)}, bf16[256,1024]{1,0:T(8,128)(2,1)S(1)}, u32[]{:S(2)}, u32[]{:S(2)}) collective-permute-start(bf16[256,1024]{1,0:T(8,128)(2,1)S(1)} %add_convert_fusion.6), channel_id=1, source_target_pairs={{0,2},{2,4},{5,3},{7,5},{8,10},{10,12},{13,11},{15,13},{16,18},{18... | collective-permute-start | bytes 1572872 | tf_op jit(solution)/shard_map/ppermute | solution.py:166
  181.2 10.5 %collective-permute-start.32 = (bf16[256,1024]{1,0:T(8,128)(2,1)S(1)}, bf16[256,1024]{1,0:T(8,128)(2,1)S(1)}, u32[]{:S(2)}, u32[]{:S(2)}) collective-permute-start(bf16[256,1024]{1,0:T(8,128)(2,1)S(1)} %add_convert_fusion.8), channel_id=1, source_target_pairs={{0,2},{2,4},{3,1},{4,6},{5,3},{7,5},{8,10},{10,12},{11,9},{12,14},... | collective-permute-start | bytes 1572872 | tf_op jit(solution)/shard_map/ppermute | solution.py:166
  186.3 11.1 %collective-permute-start.39 = (bf16[256,1024]{1,0:T(8,128)(2,1)S(1)}, bf16[256,1024]{1,0:T(8,128)(2,1)S(1)}, u32[]{:S(2)}, u32[]{:S(2)}) collective-permute-start(bf16[256,1024]{1,0:T(8,128)(2,1)S(1)} %add_convert_fusion.5), channel_id=1, source_target_pairs={{0,2},{2,4},{3,1},{4,6},{5,3},{7,5},{8,10},{10,12},{11,9},{12,14},... | collective-permute-start | bytes 1572872 | tf_op jit(solution)/shard_map/ppermute | solution.py:166
  190.8 7.5 %collective-permute-start.42 = (bf16[512,512]{1,0:T(8,128)(2,1)S(1)}, bf16[512,512]{1,0:T(8,128)(2,1)S(1)}, u32[]{:S(2)}, u32[]{:S(2)}) collective-permute-start(bf16[512,512]{1,0:T(8,128)(2,1)S(1)} %select_convert_fusion), channel_id=1, source_target_pairs={{0,1},{1,0},{2,3},{3,2},{4,5},{5,4},{6,7},{7,6},{8,9},{9,8},{10,11... | collective-permute-start | bytes 1572872 | tf_op jit(solution)/shard_map/ppermute | solution.py:163
  192.6 7.2 %collective-permute-start.33 = (bf16[256,512]{1,0:T(8,128)(2,1)}, bf16[256,512]{1,0:T(8,128)(2,1)S(1)}, u32[]{:S(2)}, u32[]{:S(2)}) collective-permute-start(bf16[256,512]{1,0:T(8,128)(2,1)} %select_convert_fusion.2), channel_id=1, source_target_pairs={{0,1},{1,0},{2,3},{3,2},{4,5},{5,4},{6,7},{7,6},{8,9},{9,8},{10,11... | collective-permute-start | bytes 786440 | tf_op jit(solution)/shard_map/ppermute | solution.py:163
  198.3 1.9 collective-permute-start.40
  (18 other events, 94.4 us)

commit v11 on v10

--- a/solution.py
+++ b/solution.py
@@ -261,7 +261,7 @@
     half = mid.shape[1] // HALVES
     second = []
     for j in range(HALVES):
-        after = () if j else ()
+        after = (first.arrived,) if j else ()
         second.append(Gradient(mid[:, j * half : (j + 1) * half], normed, after))
     for step in range(1, chips):
         sent = tuple(gradient.reduce(step) for gradient in second)

time: 204 us -> 207 us (1.015)
  waiting for transfers between devices: 22.3 us -> 32.1 us
  other arithmetic: 26.5 us -> 22.1 us
    ppermute x18, waiting for transfers between devices: 17.7 us -> 27.7 us  [move(): return lax.ppermute(value, 'fsdp', move_perm(chips, active))]
    convert_element_type x9, other arithmetic: 9.2 us -> 4.66 us  [message(): return term.astype(bf16)]
    pallas_call x10 -> x11, Pallas kernels: 14 us -> 14.6 us  [__call__(): pl.pallas_call(ordered, grid_spec=pltpu.PrefetchScalarGridSpec(num_scalar...]
    unnamed x45 -> x63, local copies, waits for them, and re-layouts: 12.1 us -> 11.7 us
  transfers between devices with their start and end apart: 45 -> 45, of which waited for: 12 -> 13; matrix products, arithmetic and copies ran while one was open for 24% -> 20% of each run, Pallas kernels for 6% -> 7%
where the time goes in v11:
time: 207 us; the launch traced here: 205 us
  starting transfers between devices  102 us (49%)
  waiting for transfers between devices  32.1 us (16%)
  other arithmetic  22.1 us (11%)
  matrix products  19.1 us (9%)
  Pallas kernels  14.6 us (7%)
  local copies, waits for them, and re-layouts  14 us (7%)
    ppermute x18, starting transfers between devices, move(): return lax.ppermute(value, 'fsdp', move_perm(chips, active))  58.2 us
    ppermute x23, starting transfers between devices, swap(): return lax.ppermute(value, 'fsdp', [(i, i ^ 1) for i in range(devices)])  38.1 us
    ppermute x18, waiting for transfers between devices, move(): return lax.ppermute(value, 'fsdp', move_perm(chips, active))  27.7 us
    pallas_call x11, Pallas kernels, __call__(): pl.pallas_call(ordered, grid_spec=pltpu.PrefetchScalarGridSpec(num_scalar...  14.6 us
    unnamed x63, local copies, waits for them, and re-layouts  11.7 us
    dot_general x3, matrix products, __init__(): lax.dot_general(mid, x, (((0,), (0,)), ((), ())), preferred_element_type=...  10 us
    ppermute x4, starting transfers between devices, per_device(): lax.ppermute(mine, 'replica', [(i, i ^ bit) for i in range(replicas)])  5.61 us
    convert_element_type x3, other arithmetic, per_device(): mine = total.astype(bf16)  5.58 us
  transfers between devices with their start and end apart: 45, of which 13 were waited for; matrix products, arithmetic and copies ran while one was open for 20% of the time, Pallas kernels for 7%

profile of v11, /device:TPU:0, one launch (start us, length us, event | category | flops | bytes accessed | tf_op | source)
XLA Modules:
  0.0 205.3 jit_solution(5114358815193152079)
XLA Ops:
  2.0 1.6 collective-permute-done.refs_2_.refs_1_
  6.8 5.6 %collective-permute-start.2 = (bf16[1024,256]{1,0:T(8,128)(2,1)S(1)}, bf16[1024,256]{1,0:T(8,128)(2,1)}, u32[]{:S(2)}, u32[]{:S(2)}) collective-permute-start(bf16[1024,256]{1,0:T(8,128)(2,1)S(1)} %get-tuple-element.13), channel_id=1, source_target_pairs={{0,2},{2,4},{3,1},{4,6},{5,3},{7,5},{8,10},{10,12},{11,9},{12,14},... | collective-permute-start | bytes 1572872 | tf_op jit(solution)/shard_map/ppermute | solution.py:166
  12.5 3.5 %collective-permute-start.4 = (bf16[1024,256]{1,0:T(8,128)(2,1)S(1)}, bf16[1024,256]{1,0:T(8,128)(2,1)}, u32[]{:S(2)}, u32[]{:S(2)}) collective-permute-start(bf16[1024,256]{1,0:T(8,128)(2,1)S(1)} %get-tuple-element.12.refs_1_), channel_id=1, source_target_pairs={{0,2},{2,4},{3,1},{4,6},{5,3},{7,5},{8,10},{10,12},{11,9},{12,14},... | collective-permute-start | bytes 1572872 | tf_op jit(solution)/shard_map/ppermute | solution.py:166
  16.0 2.4 %collective-permute-done.2 = bf16[1024,256]{1,0:T(8,128)(2,1)} collective-permute-done((bf16[1024,256]{1,0:T(8,128)(2,1)S(1)}, bf16[1024,256]{1,0:T(8,128)(2,1)}, u32[]{:S(2)}, u32[]{:S(2)}) %collective-permute-start.2) | collective-permute-done | bytes 524320 | tf_op jit(solution)/shard_map/ppermute | solution.py:166
  18.4 1.4 collective-permute-start.3
  19.8 4.2 %collective-permute-done.4 = bf16[1024,256]{1,0:T(8,128)(2,1)} collective-permute-done((bf16[1024,256]{1,0:T(8,128)(2,1)S(1)}, bf16[1024,256]{1,0:T(8,128)(2,1)}, u32[]{:S(2)}, u32[]{:S(2)}) %collective-permute-start.4) | collective-permute-done | bytes 524320 | tf_op jit(solution)/shard_map/ppermute | solution.py:166
  26.6 9.7 %collective-permute-start.10 = (bf16[1024,256]{1,0:T(8,128)(2,1)S(1)}, bf16[1024,256]{1,0:T(8,128)(2,1)S(1)}, u32[]{:S(2)}, u32[]{:S(2)}) collective-permute-start(bf16[1024,256]{1,0:T(8,128)(2,1)S(1)} %collective-permute-done.5), channel_id=1, source_target_pairs={{0,1},{1,0},{2,3},{3,2},{4,5},{5,4},{6,7},{7,6},{8,9},{9,8},{10,11... | collective-permute-start | bytes 1572872 | tf_op jit(solution)/shard_map/ppermute | solution.py:163
  36.3 3.8 %fusion = (bf16[4096,128]{1,0:T(8,128)(2,1)S(1)}, bf16[4096,128]{1,0:T(8,128)(2,1)S(1)}) fusion(f32[4096]{0:T(1024)S(1)} %bitcast.51, bf16[1,8192,128]{2,1,0:T(8,128)(2,1)} %param.16, f32[4096]{0:T(1024)S(1)} %bitcast.52), kind=kLoop, calls=%fused_computation.10 | loop fusion | flops 3145728 | bytes 4227072 | tf_op jit(solution)/shard_map/convert_element_type | solution.py:235
  40.1 1.7 collective-permute-start.20
  41.8 1.5 collective-permute-start.21
  45.9 3.9 %collective-permute-start.11 = (bf16[1024,256]{1,0:T(8,128)(2,1)}, bf16[1024,256]{1,0:T(8,128)(2,1)S(1)}, u32[]{:S(2)}, u32[]{:S(2)}) collective-permute-start(bf16[1024,256]{1,0:T(8,128)(2,1)} %collective-permute-done.3.refs_2_), channel_id=1, source_target_pairs={{0,1},{1,0},{2,3},{3,2},{4,5},{5,4},{6,7},{7,6},{8,9},{9,8},{10,11... | collective-permute-start | bytes 1572872 | tf_op jit(solution)/shard_map/ppermute | solution.py:163
  49.8 4.4 %collective-permute-start.12 = (bf16[1024,512]{1,0:T(8,128)(2,1)S(1)}, bf16[1024,512]{1,0:T(8,128)(2,1)S(1)}, u32[]{:S(2)}, u32[]{:S(2)}) collective-permute-start(bf16[1024,512]{1,0:T(8,128)(2,1)S(1)} %join_cores.3.refs_3_), channel_id=1, source_target_pairs={{0,2},{2,4},{3,1},{4,6},{5,3},{7,5},{8,10},{10,12},{11,9},{12,14},... | collective-permute-start | bytes 3145736 | tf_op jit(solution)/shard_map/ppermute | solution.py:166
  54.2 4.5 %collective-permute-start.7 = (bf16[1024,256]{1,0:T(8,128)(2,1)S(1)}, bf16[1024,256]{1,0:T(8,128)(2,1)S(1)}, u32[]{:S(2)}, u32[]{:S(2)}) collective-permute-start(bf16[1024,256]{1,0:T(8,128)(2,1)S(1)} %collective-permute-done.6.refs_3_), channel_id=1, source_target_pairs={{0,1},{1,0},{2,3},{3,2},{4,5},{5,4},{6,7},{7,6},{8,9},{9,8},{10,11... | collective-permute-start | bytes 1572872 | tf_op jit(solution)/shard_map/ppermute | solution.py:163
  59.0 1.3 collective-permute-done.7.refs_4_
  61.0 9.0 %prepare.1 = (bf16[1024,4096]{1,0:T(8,128)(2,1)S(1)}, bf16[1024,4096]{1,0:T(8,128)(2,1)S(1)}) custom-call(s32[6]{0:T(128)S(1)} %stack.27.place_ref, bf16[1024,4096]{1,0:T(8,128)(2,1)S(1)} %bitcast.43, bf16[1024,4096]{1,0:T(8,128)(2,1)} %bitcast.53, f32[1,4096]{1,0:T(1,128)S(1)} %bitcast.48, bf16[1024,512]{1,0:T(8,128)(2,1)S(1)} %join_cores.3.refs_3_, ...), custom_call_target="tpu_custom_call" | custom-call | flops 20000000000 | bytes 1 | tf_op jit(solution)/shard_map/prepare/pallas_call | solution.py:39
  72.3 2.3 %convolution_convert_fusion.5 = bf16[1024,256]{1,0:T(8,128)(2,1)S(1)} fusion(bf16[1024,4096]{1,0:T(8,128)(2,1)S(1)} %get-tuple-element.15.refs_2_, bf16[4096,256]{1,0:T(8,128)(2,1)S(1)} %get-tuple-element.16.refs_1_), kind=kOutput, calls=%fused_computation.23 | convolution fusion | flops 2147745792 | bytes 11010048 | tf_op jit(solution)/shard_map/dot_general | solution.py:248
  75.3 2.3 %convolution_convert_fusion.4 = bf16[1024,256]{1,0:T(8,128)(2,1)S(1)} fusion(bf16[1024,4096]{1,0:T(8,128)(2,1)S(1)} %get-tuple-element.15.refs_2_, bf16[4096,256]{1,0:T(8,128)(2,1)S(1)} %get-tuple-element.17), kind=kOutput, calls=%fused_computation.22 | convolution fusion | flops 2147745792 | bytes 11010048 | tf_op jit(solution)/shard_map/dot_general | solution.py:248
  78.3 4.9 %convolution_convert_fusion.refs_0_ = bf16[512,4096]{1,0:T(8,128)(2,1)S(1)} fusion(bf16[1024,512]{1,0:T(8,128)(2,1)S(1)} %fence.10.refs_1_, bf16[1024,4096]{1,0:T(8,128)(2,1)S(1)} %get-tuple-element.14), kind=kOutput, calls=%fused_computation | convolution fusion | flops 4297064448 | bytes 13631488 | tf_op jit(solution)/shard_map/dot_general | solution.py:170
  84.3 1.9 fusion.8
  87.2 9.1 %collective-permute-start.24 = (bf16[512,1024]{1,0:T(8,128)(2,1)}, bf16[512,1024]{1,0:T(8,128)(2,1)}, u32[]{:S(2)}, u32[]{:S(2)}) collective-permute-start(bf16[512,1024]{1,0:T(8,128)(2,1)} %get-tuple-element.28), channel_id=1, source_target_pairs={{0,1},{1,0},{2,3},{3,2},{4,5},{5,4},{6,7},{7,6},{8,9},{9,8},{10,11... | collective-permute-start | bytes 3145736 | tf_op jit(solution)/shard_map/ppermute | solution.py:163
  97.2 1.5 add_convert_fusion.1
  99.9 1.9 add_convert_fusion.4
  101.8 6.9 %collective-permute-start.25 = (bf16[512,1024]{1,0:T(8,128)(2,1)S(1)}, bf16[512,1024]{1,0:T(8,128)(2,1)S(1)}, u32[]{:S(2)}, u32[]{:S(2)}) collective-permute-start(bf16[512,1024]{1,0:T(8,128)(2,1)S(1)} %add_convert_fusion.4), channel_id=1, source_target_pairs={{0,2},{7,5},{8,10},{15,13},{16,18},{23,21},{24,26},{31,29}} | collective-permute-start | bytes 3145736 | tf_op jit(solution)/shard_map/ppermute | solution.py:166
  108.7 5.8 %collective-permute-start.15 = (bf16[1024,512]{1,0:T(8,128)(2,1)S(1)}, bf16[1024,512]{1,0:T(8,128)(2,1)S(1)}, u32[]{:S(2)}, u32[]{:S(2)}) collective-permute-start(bf16[1024,512]{1,0:T(8,128)(2,1)S(1)} %collective-permute-done.14), channel_id=1, source_target_pairs={{0,1},{1,0},{2,3},{3,2},{4,5},{5,4},{6,7},{7,6},{8,9},{9,8},{10,11... | collective-permute-start | bytes 3145736 | tf_op jit(solution)/shard_map/ppermute | solution.py:163
  115.8 1.6 collective-permute-start.44
  117.6 3.2 %collective-permute-done.25 = bf16[512,1024]{1,0:T(8,128)(2,1)S(1)} collective-permute-done((bf16[512,1024]{1,0:T(8,128)(2,1)S(1)}, bf16[512,1024]{1,0:T(8,128)(2,1)S(1)}, u32[]{:S(2)}, u32[]{:S(2)}) %collective-permute-start.25) | collective-permute-done | bytes 1048608 | tf_op jit(solution)/shard_map/ppermute | solution.py:166
  121.5 4.6 %collective-permute-start.26 = (bf16[512,1024]{1,0:T(8,128)(2,1)S(1)}, bf16[512,1024]{1,0:T(8,128)(2,1)S(1)}, u32[]{:S(2)}, u32[]{:S(2)}) collective-permute-start(bf16[512,1024]{1,0:T(8,128)(2,1)S(1)} %add_convert_fusion.3), channel_id=1, source_target_pairs={{0,2},{2,4},{5,3},{7,5},{8,10},{10,12},{13,11},{15,13},{16,18},{18... | collective-permute-start | bytes 3145736 | tf_op jit(solution)/shard_map/ppermute | solution.py:166
  127.1 1.3 slice-done.4
  128.4 1.4 slice-done.5
  129.8 4.5 %convolution_convert_fusion.3.refs_0_ = bf16[1024,512]{1,0:T(8,128)(2,1)S(1)} fusion(bf16[1024,4096]{1,0:T(8,128)(2,1)S(1)} %bitcast.50, bf16[4096,512]{1,0:T(8,128)(2,1)S(1)} %fence.12.refs_1_), kind=kOutput, calls=%fused_computation.21 | convolution fusion | flops 4295491584 | bytes 13631488 | tf_op jit(solution)/shard_map/dot_general | solution.py:259
  134.2 4.0 %collective-permute-done.26 = bf16[512,1024]{1,0:T(8,128)(2,1)S(1)} collective-permute-done((bf16[512,1024]{1,0:T(8,128)(2,1)S(1)}, bf16[512,1024]{1,0:T(8,128)(2,1)S(1)}, u32[]{:S(2)}, u32[]{:S(2)}) %collective-permute-start.26) | collective-permute-done | bytes 1048608 | tf_op jit(solution)/shard_map/ppermute | solution.py:166
  138.9 4.5 %collective-permute-start.34 = (bf16[512,1024]{1,0:T(8,128)(2,1)S(1)}, bf16[512,1024]{1,0:T(8,128)(2,1)S(1)}, u32[]{:S(2)}, u32[]{:S(2)}) collective-permute-start(bf16[512,1024]{1,0:T(8,128)(2,1)S(1)} %add_convert_fusion.2.refs_2_), channel_id=1, source_target_pairs={{0,2},{2,4},{3,1},{4,6},{5,3},{7,5},{8,10},{10,12},{11,9},{12,14},... | collective-permute-start | bytes 3145736 | tf_op jit(solution)/shard_map/ppermute | solution.py:166
  144.0 2.5 %convolution_convert_fusion.2 = bf16[256,4096]{1,0:T(8,128)(2,1)S(1)} fusion(bf16[1024,4096]{1,0:T(8,128)(2,1)S(1)} %bitcast.40, bf16[1024,512]{1,0:T(8,128)(2,1)S(1)} %fence.13.refs_1_), kind=kOutput, calls=%fused_computation.2 | convolution fusion | flops 2148532224 | bytes 11010048 | tf_op jit(solution)/shard_map/dot_general | solution.py:170
  146.7 2.5 %convolution_convert_fusion.1.refs_0_ = bf16[256,4096]{1,0:T(8,128)(2,1)S(1)} fusion(bf16[1024,4096]{1,0:T(8,128)(2,1)S(1)} %bitcast.40, bf16[1024,512]{1,0:T(8,128)(2,1)S(1)} %fence.13.refs_1_), kind=kOutput, calls=%fused_computation.1 | convolution fusion | flops 2148532224 | bytes 11010048 | tf_op jit(solution)/shard_map/dot_general | solution.py:170
  149.8 5.8 %collective-permute-done.34.refs_2_ = bf16[512,1024]{1,0:T(8,128)(2,1)S(1)} collective-permute-done((bf16[512,1024]{1,0:T(8,128)(2,1)S(1)}, bf16[512,1024]{1,0:T(8,128)(2,1)S(1)}, u32[]{:S(2)}, u32[]{:S(2)}) %collective-permute-start.34) | collective-permute-done | bytes 1048608 | tf_op jit(solution)/shard_map/ppermute | solution.py:166
  156.3 1.4 collective-permute-start.37
  157.9 4.0 %collective-permute-start.30 = (bf16[256,1024]{1,0:T(8,128)(2,1)S(1)}, bf16[256,1024]{1,0:T(8,128)(2,1)S(1)}, u32[]{:S(2)}, u32[]{:S(2)}) collective-permute-start(bf16[256,1024]{1,0:T(8,128)(2,1)S(1)} %add_convert_fusion.10.refs_3_), channel_id=1, source_target_pairs={{0,2},{7,5},{8,10},{15,13},{16,18},{23,21},{24,26},{31,29}} | collective-permute-start | bytes 1572872 | tf_op jit(solution)/shard_map/ppermute | solution.py:166
  162.5 1.5 collective-permute-start.38
  164.2 4.3 %collective-permute-done.30 = bf16[256,1024]{1,0:T(8,128)(2,1)S(1)} collective-permute-done((bf16[256,1024]{1,0:T(8,128)(2,1)S(1)}, bf16[256,1024]{1,0:T(8,128)(2,1)S(1)}, u32[]{:S(2)}, u32[]{:S(2)}) %collective-permute-start.30) | collective-permute-done | bytes 524320 | tf_op jit(solution)/shard_map/ppermute | solution.py:166
  170.0 4.4 %collective-permute-start.31 = (bf16[256,1024]{1,0:T(8,128)(2,1)S(1)}, bf16[256,1024]{1,0:T(8,128)(2,1)S(1)}, u32[]{:S(2)}, u32[]{:S(2)}) collective-permute-start(bf16[256,1024]{1,0:T(8,128)(2,1)S(1)} %add_convert_fusion.9), channel_id=1, source_target_pairs={{0,2},{2,4},{5,3},{7,5},{8,10},{10,12},{13,11},{15,13},{16,18},{18... | collective-permute-start | bytes 1572872 | tf_op jit(solution)/shard_map/ppermute | solution.py:166
  174.7 4.1 %collective-permute-start.39 = (bf16[256,1024]{1,0:T(8,128)(2,1)S(1)}, bf16[256,1024]{1,0:T(8,128)(2,1)S(1)}, u32[]{:S(2)}, u32[]{:S(2)}) collective-permute-start(bf16[256,1024]{1,0:T(8,128)(2,1)S(1)} %add_convert_fusion.6), channel_id=1, source_target_pairs={{0,2},{2,4},{5,3},{7,5},{8,10},{10,12},{13,11},{15,13},{16,18},{18... | collective-permute-start | bytes 1572872 | tf_op jit(solution)/shard_map/ppermute | solution.py:166
  179.3 1.8 collective-permute-done.31
  181.4 4.4 %collective-permute-start.32 = (bf16[256,1024]{1,0:T(8,128)(2,1)S(1)}, bf16[256,1024]{1,0:T(8,128)(2,1)S(1)}, u32[]{:S(2)}, u32[]{:S(2)}) collective-permute-start(bf16[256,1024]{1,0:T(8,128)(2,1)S(1)} %add_convert_fusion.8), channel_id=1, source_target_pairs={{0,2},{2,4},{3,1},{4,6},{5,3},{7,5},{8,10},{10,12},{11,9},{12,14},... | collective-permute-start | bytes 1572872 | tf_op jit(solution)/shard_map/ppermute | solution.py:166
  187.0 5.2 %collective-permute-start.40 = (bf16[256,1024]{1,0:T(8,128)(2,1)S(1)}, bf16[256,1024]{1,0:T(8,128)(2,1)}, u32[]{:S(2)}, u32[]{:S(2)}) collective-permute-start(bf16[256,1024]{1,0:T(8,128)(2,1)S(1)} %add_convert_fusion.5), channel_id=1, source_target_pairs={{0,2},{2,4},{3,1},{4,6},{5,3},{7,5},{8,10},{10,12},{11,9},{12,14},... | collective-permute-start | bytes 1572872 | tf_op jit(solution)/shard_map/ppermute | solution.py:166
  192.2 3.9 %subtract_convert_fusion = (bf16[8192,128]{1,0:T(8,128)(2,1)}, f32[8192,128]{1,0:T(8,128)}) fusion(bf16[8192,128]{1,0:T(8,128)(2,1)S(1)} %copy-done.21, f32[4096,128]{1,0:T(8,128)S(1)} %get-tuple-element.39, f32[4096,128]{1,0:T(8,128)S(1)} %get-tuple-element.40, f32[8192,128]{1,0:T(8,128)S(1)} %copy-done.20), kind=kLoop, calls=%fused_computation.5 | loop fusion | flops 10485760 | bytes 16777216 | tf_op jit(solution)/shard_map/convert_element_type | solution.py:132
  200.0 1.4 add_bitcast_fusion
  201.3 1.3 copy.26
  204.0 1.3 copy.25
  (167 shorter events, 33.6 us)
Async XLA Ops:
  1.4 2.2 %collective-permute-start = (bf16[512,512]{1,0:T(8,128)(2,1)}, bf16[512,512]{1,0:T(8,128)(2,1)S(1)}, u32[]{:S(2)}, u32[]{:S(2)}) collective-permute-start(bf16[512,512]{1,0:T(8,128)(2,1)} %bitcast.46), channel_id=1, source_target_pairs={{0,1},{1,0},{2,3},{3,2},{4,5},{5,4},{6,7},{7,6},{8,9},{9,8},{10,11... | collective-permute-start | bytes 1572872 | tf_op jit(solution)/shard_map/ppermute | solution.py:163
  1.8 2.5 %collective-permute-start.1 = (bf16[512,512]{1,0:T(8,128)(2,1)}, bf16[512,512]{1,0:T(8,128)(2,1)S(1)}, u32[]{:S(2)}, u32[]{:S(2)}) collective-permute-start(bf16[512,512]{1,0:T(8,128)(2,1)} %bitcast.44), channel_id=1, source_target_pairs={{0,1},{1,0},{2,3},{3,2},{4,5},{5,4},{6,7},{7,6},{8,9},{9,8},{10,11... | collective-permute-start | bytes 1572872 | tf_op jit(solution)/shard_map/ppermute | solution.py:163
  3.6 22.2 %copy-start.13 = (bf16[512,512]{1,0:T(8,128)(2,1)}, bf16[512,512]{1,0:T(8,128)(2,1)S(1)}, u32[]{:S(2)}) copy-start(bf16[512,512]{1,0:T(8,128)(2,1)S(1)} %collective-permute-done.refs_2_.refs_1_) | copy-start | bytes 1572868
  6.1 34.0 %copy-start.9 = (bf16[1024,256]{1,0:T(8,128)(2,1)}, bf16[1024,256]{1,0:T(8,128)(2,1)S(1)}, u32[]{:S(2)}) copy-start(bf16[1024,256]{1,0:T(8,128)(2,1)S(1)} %get-tuple-element.12.refs_1_) | copy-start | bytes 1572868
  6.8 11.5 %collective-permute-start.2 = (bf16[1024,256]{1,0:T(8,128)(2,1)S(1)}, bf16[1024,256]{1,0:T(8,128)(2,1)}, u32[]{:S(2)}, u32[]{:S(2)}) collective-permute-start(bf16[1024,256]{1,0:T(8,128)(2,1)S(1)} %get-tuple-element.13), channel_id=1, source_target_pairs={{0,2},{2,4},{3,1},{4,6},{5,3},{7,5},{8,10},{10,12},{11,9},{12,14},... | collective-permute-start | bytes 1572872 | tf_op jit(solution)/shard_map/ppermute | solution.py:166
  12.5 11.5 %collective-permute-start.4 = (bf16[1024,256]{1,0:T(8,128)(2,1)S(1)}, bf16[1024,256]{1,0:T(8,128)(2,1)}, u32[]{:S(2)}, u32[]{:S(2)}) collective-permute-start(bf16[1024,256]{1,0:T(8,128)(2,1)S(1)} %get-tuple-element.12.refs_1_), channel_id=1, source_target_pairs={{0,2},{2,4},{3,1},{4,6},{5,3},{7,5},{8,10},{10,12},{11,9},{12,14},... | collective-permute-start | bytes 1572872 | tf_op jit(solution)/shard_map/ppermute | solution.py:166
  18.4 6.9 %collective-permute-start.3 = (bf16[1024,256]{1,0:T(8,128)(2,1)}, bf16[1024,256]{1,0:T(8,128)(2,1)}, u32[]{:S(2)}, u32[]{:S(2)}) collective-permute-start(bf16[1024,256]{1,0:T(8,128)(2,1)} %collective-permute-done.2), channel_id=1, source_target_pairs={{2,4},{3,1},{4,6},{5,3},{10,12},{11,9},{12,14},{13,11},{18,20},{19... | collective-permute-start | bytes 1572872 | tf_op jit(solution)/shard_map/ppermute | solution.py:166
  24.0 1.9 collective-permute-start.5
  24.7 20.4 %collective-permute-start.18 = (bf16[1024,256]{1,0:T(8,128)(2,1)}, bf16[1024,256]{1,0:T(8,128)(2,1)S(1)}, u32[]{:S(2)}, u32[]{:S(2)}) collective-permute-start(bf16[1024,256]{1,0:T(8,128)(2,1)} %collective-permute-done.4), channel_id=1, source_target_pairs={{0,1},{1,0},{2,3},{3,2},{4,5},{5,4},{6,7},{7,6},{8,9},{9,8},{10,11... | collective-permute-start | bytes 1572872 | tf_op jit(solution)/shard_map/ppermute | solution.py:163
  25.2 24.6 %collective-permute-start.19 = (bf16[1024,256]{1,0:T(8,128)(2,1)}, bf16[1024,256]{1,0:T(8,128)(2,1)S(1)}, u32[]{:S(2)}, u32[]{:S(2)}) collective-permute-start(bf16[1024,256]{1,0:T(8,128)(2,1)} %collective-permute-done.2), channel_id=1, source_target_pairs={{0,1},{1,0},{2,3},{3,2},{4,5},{5,4},{6,7},{7,6},{8,9},{9,8},{10,11... | collective-permute-start | bytes 1572872 | tf_op jit(solution)/shard_map/ppermute | solution.py:163
  25.9 15.9 %collective-permute-start.6 = (bf16[1024,256]{1,0:T(8,128)(2,1)S(1)}, bf16[1024,256]{1,0:T(8,128)(2,1)S(1)}, u32[]{:S(2)}, u32[]{:S(2)}) collective-permute-start(bf16[1024,256]{1,0:T(8,128)(2,1)S(1)} %collective-permute-done.5), channel_id=1, source_target_pairs={{3,1},{4,6},{11,9},{12,14},{19,17},{20,22},{27,25},{28,30}} | collective-permute-start | bytes 1572872 | tf_op jit(solution)/shard_map/ppermute | solution.py:166
  26.6 19.3 %collective-permute-start.10 = (bf16[1024,256]{1,0:T(8,128)(2,1)S(1)}, bf16[1024,256]{1,0:T(8,128)(2,1)S(1)}, u32[]{:S(2)}, u32[]{:S(2)}) collective-permute-start(bf16[1024,256]{1,0:T(8,128)(2,1)S(1)} %collective-permute-done.5), channel_id=1, source_target_pairs={{0,1},{1,0},{2,3},{3,2},{4,5},{5,4},{6,7},{7,6},{8,9},{9,8},{10,11... | collective-permute-start | bytes 1572872 | tf_op jit(solution)/shard_map/ppermute | solution.py:163
  36.3 24.7 %slice-start.2 = ((s8[8388608]{0:T(1024)(128)(4,1)}), s8[4194304]{0:T(1024)(128)(4,1)S(1)}, s32[]{:S(2)}) async-start(s8[8388608]{0:T(1024)(128)(4,1)} %bitcast.41), calls=%async_computation.2 | async-start | bytes 8388608
  40.1 37.6 %collective-permute-start.20 = (bf16[4096,128]{1,0:T(8,128)(2,1)S(1)}, bf16[4096,128]{1,0:T(8,128)(2,1)S(1)}, u32[]{:S(2)}, u32[]{:S(2)}) collective-permute-start(bf16[4096,128]{1,0:T(8,128)(2,1)S(1)} %get-tuple-element.36), channel_id=1, source_target_pairs={{0,8},{8,0},{16,24},{24,16},{1,9},{9,1},{17,25},{25,17},{2,10},{10... | collective-permute-start | bytes 3145736 | tf_op jit(solution)/shard_map/ppermute | solution.py:237
  41.8 35.9 %collective-permute-start.21 = (bf16[4096,128]{1,0:T(8,128)(2,1)S(1)}, bf16[4096,128]{1,0:T(8,128)(2,1)S(1)}, u32[]{:S(2)}, u32[]{:S(2)}) collective-permute-start(bf16[4096,128]{1,0:T(8,128)(2,1)S(1)} %get-tuple-element.35), channel_id=1, source_target_pairs={{0,16},{8,24},{16,0},{24,8},{1,17},{9,25},{17,1},{25,9},{2,18},{10... | collective-permute-start | bytes 3145736 | tf_op jit(solution)/shard_map/ppermute | solution.py:237
  45.1 9.1 %collective-permute-start.8 = (bf16[1024,256]{1,0:T(8,128)(2,1)}, bf16[1024,256]{1,0:T(8,128)(2,1)S(1)}, u32[]{:S(2)}, u32[]{:S(2)}) collective-permute-start(bf16[1024,256]{1,0:T(8,128)(2,1)} %collective-permute-done.3.refs_2_), channel_id=1, source_target_pairs={{3,1},{4,6},{11,9},{12,14},{19,17},{20,22},{27,25},{28,30}} | collective-permute-start | bytes 1572872 | tf_op jit(solution)/shard_map/ppermute | solution.py:166
  45.9 12.9 %collective-permute-start.11 = (bf16[1024,256]{1,0:T(8,128)(2,1)}, bf16[1024,256]{1,0:T(8,128)(2,1)S(1)}, u32[]{:S(2)}, u32[]{:S(2)}) collective-permute-start(bf16[1024,256]{1,0:T(8,128)(2,1)} %collective-permute-done.3.refs_2_), channel_id=1, source_target_pairs={{0,1},{1,0},{2,3},{3,2},{4,5},{5,4},{6,7},{7,6},{8,9},{9,8},{10,11... | collective-permute-start | bytes 1572872 | tf_op jit(solution)/shard_map/ppermute | solution.py:163
  49.8 21.9 %collective-permute-start.12 = (bf16[1024,512]{1,0:T(8,128)(2,1)S(1)}, bf16[1024,512]{1,0:T(8,128)(2,1)S(1)}, u32[]{:S(2)}, u32[]{:S(2)}) collective-permute-start(bf16[1024,512]{1,0:T(8,128)(2,1)S(1)} %join_cores.3.refs_3_), channel_id=1, source_target_pairs={{0,2},{2,4},{3,1},{4,6},{5,3},{7,5},{8,10},{10,12},{11,9},{12,14},... | collective-permute-start | bytes 3145736 | tf_op jit(solution)/shard_map/ppermute | solution.py:166
  54.2 6.0 %collective-permute-start.7 = (bf16[1024,256]{1,0:T(8,128)(2,1)S(1)}, bf16[1024,256]{1,0:T(8,128)(2,1)S(1)}, u32[]{:S(2)}, u32[]{:S(2)}) collective-permute-start(bf16[1024,256]{1,0:T(8,128)(2,1)S(1)} %collective-permute-done.6.refs_3_), channel_id=1, source_target_pairs={{0,1},{1,0},{2,3},{3,2},{4,5},{5,4},{6,7},{7,6},{8,9},{9,8},{10,11... | collective-permute-start | bytes 1572872 | tf_op jit(solution)/shard_map/ppermute | solution.py:163
  58.8 2.2 %collective-permute-start.9 = (bf16[1024,256]{1,0:T(8,128)(2,1)S(1)}, bf16[1024,256]{1,0:T(8,128)(2,1)S(1)}, u32[]{:S(2)}, u32[]{:S(2)}) collective-permute-start(bf16[1024,256]{1,0:T(8,128)(2,1)S(1)} %collective-permute-done.8), channel_id=1, source_target_pairs={{0,1},{1,0},{2,3},{3,2},{4,5},{5,4},{6,7},{7,6},{8,9},{9,8},{10,11... | collective-permute-start | bytes 1572872 | tf_op jit(solution)/shard_map/ppermute | solution.py:163
  74.6 8.7 %collective-permute-start.13 = (bf16[1024,512]{1,0:T(8,128)(2,1)S(1)}, bf16[1024,512]{1,0:T(8,128)(2,1)S(1)}, u32[]{:S(2)}, u32[]{:S(2)}) collective-permute-start(bf16[1024,512]{1,0:T(8,128)(2,1)S(1)} %collective-permute-done.12.refs_3_.refs_2_), channel_id=1, source_target_pairs={{2,4},{3,1},{4,6},{5,3},{10,12},{11,9},{12,14},{13,11},{18,20},{19... | collective-permute-start | bytes 3145736 | tf_op jit(solution)/shard_map/ppermute | solution.py:166
  87.2 12.6 %collective-permute-start.24 = (bf16[512,1024]{1,0:T(8,128)(2,1)}, bf16[512,1024]{1,0:T(8,128)(2,1)}, u32[]{:S(2)}, u32[]{:S(2)}) collective-permute-start(bf16[512,1024]{1,0:T(8,128)(2,1)} %get-tuple-element.28), channel_id=1, source_target_pairs={{0,1},{1,0},{2,3},{3,2},{4,5},{5,4},{6,7},{7,6},{8,9},{9,8},{10,11... | collective-permute-start | bytes 3145736 | tf_op jit(solution)/shard_map/ppermute | solution.py:163
  96.3 12.4 %collective-permute-start.14 = (bf16[1024,512]{1,0:T(8,128)(2,1)}, bf16[1024,512]{1,0:T(8,128)(2,1)S(1)}, u32[]{:S(2)}, u32[]{:S(2)}) collective-permute-start(bf16[1024,512]{1,0:T(8,128)(2,1)} %copy-done.3), channel_id=1, source_target_pairs={{3,1},{4,6},{11,9},{12,14},{19,17},{20,22},{27,25},{28,30}} | collective-permute-start | bytes 3145736 | tf_op jit(solution)/shard_map/ppermute | solution.py:166
  98.7 16.1 %collective-permute-start.17 = (bf16[1024,512]{1,0:T(8,128)(2,1)S(1)}, bf16[1024,512]{1,0:T(8,128)(2,1)S(1)}, u32[]{:S(2)}, u32[]{:S(2)}) collective-permute-start(bf16[1024,512]{1,0:T(8,128)(2,1)S(1)} %collective-permute-done.12.refs_3_.refs_2_), channel_id=1, source_target_pairs={{0,1},{1,0},{2,3},{3,2},{4,5},{5,4},{6,7},{7,6},{8,9},{9,8},{10,11... | collective-permute-start | bytes 3145736 | tf_op jit(solution)/shard_map/ppermute | solution.py:163
  99.4 18.1 %collective-permute-start.23 = (bf16[512,1024]{1,0:T(8,128)(2,1)S(1)}, bf16[512,1024]{1,0:T(8,128)(2,1)S(1)}, u32[]{:S(2)}, u32[]{:S(2)}) collective-permute-start(bf16[512,1024]{1,0:T(8,128)(2,1)S(1)} %copy-done.23), channel_id=1, source_target_pairs={{0,1},{1,0},{2,3},{3,2},{4,5},{5,4},{6,7},{7,6},{8,9},{9,8},{10,11... | collective-permute-start | bytes 3145736 | tf_op jit(solution)/shard_map/ppermute | solution.py:163
  99.4 16.3 %collective-permute-start.16 = (bf16[1024,512]{1,0:T(8,128)(2,1)S(1)}, bf16[1024,512]{1,0:T(8,128)(2,1)S(1)}, u32[]{:S(2)}, u32[]{:S(2)}) collective-permute-start(bf16[1024,512]{1,0:T(8,128)(2,1)S(1)} %copy-done.4), channel_id=1, source_target_pairs={{0,1},{1,0},{2,3},{3,2},{4,5},{5,4},{6,7},{7,6},{8,9},{9,8},{10,11... | collective-permute-start | bytes 3145736 | tf_op jit(solution)/shard_map/ppermute | solution.py:163
  101.8 19.0 %collective-permute-start.25 = (bf16[512,1024]{1,0:T(8,128)(2,1)S(1)}, bf16[512,1024]{1,0:T(8,128)(2,1)S(1)}, u32[]{:S(2)}, u32[]{:S(2)}) collective-permute-start(bf16[512,1024]{1,0:T(8,128)(2,1)S(1)} %add_convert_fusion.4), channel_id=1, source_target_pairs={{0,2},{7,5},{8,10},{15,13},{16,18},{23,21},{24,26},{31,29}} | collective-permute-start | bytes 3145736 | tf_op jit(solution)/shard_map/ppermute | solution.py:166
  108.7 17.3 %collective-permute-start.15 = (bf16[1024,512]{1,0:T(8,128)(2,1)S(1)}, bf16[1024,512]{1,0:T(8,128)(2,1)S(1)}, u32[]{:S(2)}, u32[]{:S(2)}) collective-permute-start(bf16[1024,512]{1,0:T(8,128)(2,1)S(1)} %collective-permute-done.14), channel_id=1, source_target_pairs={{0,1},{1,0},{2,3},{3,2},{4,5},{5,4},{6,7},{7,6},{8,9},{9,8},{10,11... | collective-permute-start | bytes 3145736 | tf_op jit(solution)/shard_map/ppermute | solution.py:163
  114.8 54.0 %collective-permute-start.43 = (bf16[4096,128]{1,0:T(8,128)(2,1)S(1)}, bf16[4096,128]{1,0:T(8,128)(2,1)S(1)}, u32[]{:S(2)}, u32[]{:S(2)}) collective-permute-start(bf16[4096,128]{1,0:T(8,128)(2,1)S(1)} %add_convert_fusion.1), channel_id=1, source_target_pairs={{0,16},{8,24},{16,0},{24,8},{1,17},{9,25},{17,1},{25,9},{2,18},{10... | collective-permute-start | bytes 3145736 | tf_op jit(solution)/shard_map/ppermute | solution.py:237
  115.8 53.6 %collective-permute-start.44 = (bf16[4096,128]{1,0:T(8,128)(2,1)S(1)}, bf16[4096,128]{1,0:T(8,128)(2,1)S(1)}, u32[]{:S(2)}, u32[]{:S(2)}) collective-permute-start(bf16[4096,128]{1,0:T(8,128)(2,1)S(1)} %add_convert_fusion), channel_id=1, source_target_pairs={{0,8},{8,0},{16,24},{24,16},{1,9},{9,1},{17,25},{25,17},{2,10},{10... | collective-permute-start | bytes 3145736 | tf_op jit(solution)/shard_map/ppermute | solution.py:237
  117.5 16.7 %collective-permute-start.22 = (bf16[512,1024]{1,0:T(8,128)(2,1)S(1)}, bf16[512,1024]{1,0:T(8,128)(2,1)S(1)}, u32[]{:S(2)}, u32[]{:S(2)}) collective-permute-start(bf16[512,1024]{1,0:T(8,128)(2,1)S(1)} %copy-done.22), channel_id=1, source_target_pairs={{0,1},{1,0},{2,3},{3,2},{4,5},{5,4},{6,7},{7,6},{8,9},{9,8},{10,11... | collective-permute-start | bytes 3145736 | tf_op jit(solution)/shard_map/ppermute | solution.py:163
  121.5 16.8 %collective-permute-start.26 = (bf16[512,1024]{1,0:T(8,128)(2,1)S(1)}, bf16[512,1024]{1,0:T(8,128)(2,1)S(1)}, u32[]{:S(2)}, u32[]{:S(2)}) collective-permute-start(bf16[512,1024]{1,0:T(8,128)(2,1)S(1)} %add_convert_fusion.3), channel_id=1, source_target_pairs={{0,2},{2,4},{5,3},{7,5},{8,10},{10,12},{13,11},{15,13},{16,18},{18... | collective-permute-start | bytes 3145736 | tf_op jit(solution)/shard_map/ppermute | solution.py:166
  138.9 16.7 %collective-permute-start.34 = (bf16[512,1024]{1,0:T(8,128)(2,1)S(1)}, bf16[512,1024]{1,0:T(8,128)(2,1)S(1)}, u32[]{:S(2)}, u32[]{:S(2)}) collective-permute-start(bf16[512,1024]{1,0:T(8,128)(2,1)S(1)} %add_convert_fusion.2.refs_2_), channel_id=1, source_target_pairs={{0,2},{2,4},{3,1},{4,6},{5,3},{7,5},{8,10},{10,12},{11,9},{12,14},... | collective-permute-start | bytes 3145736 | tf_op jit(solution)/shard_map/ppermute | solution.py:166
  146.6 11.0 %collective-permute-start.29 = (bf16[256,1024]{1,0:T(8,128)(2,1)S(1)}, bf16[256,1024]{1,0:T(8,128)(2,1)S(1)}, u32[]{:S(2)}, u32[]{:S(2)}) collective-permute-start(bf16[256,1024]{1,0:T(8,128)(2,1)S(1)} %get-tuple-element.31), channel_id=1, source_target_pairs={{0,1},{1,0},{2,3},{3,2},{4,5},{5,4},{6,7},{7,6},{8,9},{9,8},{10,11... | collective-permute-start | bytes 1572872 | tf_op jit(solution)/shard_map/ppermute | solution.py:163
  149.3 13.3 %collective-permute-start.28 = (bf16[256,1024]{1,0:T(8,128)(2,1)S(1)}, bf16[256,1024]{1,0:T(8,128)(2,1)S(1)}, u32[]{:S(2)}, u32[]{:S(2)}) collective-permute-start(bf16[256,1024]{1,0:T(8,128)(2,1)S(1)} %get-tuple-element.30), channel_id=1, source_target_pairs={{0,1},{1,0},{2,3},{3,2},{4,5},{5,4},{6,7},{7,6},{8,9},{9,8},{10,11... | collective-permute-start | bytes 1572872 | tf_op jit(solution)/shard_map/ppermute | solution.py:163
  156.3 5.9 %collective-permute-start.37 = (bf16[256,1024]{1,0:T(8,128)(2,1)S(1)}, bf16[256,1024]{1,0:T(8,128)(2,1)S(1)}, u32[]{:S(2)}, u32[]{:S(2)}) collective-permute-start(bf16[256,1024]{1,0:T(8,128)(2,1)S(1)} %get-tuple-element.34), channel_id=1, source_target_pairs={{0,1},{1,0},{2,3},{3,2},{4,5},{5,4},{6,7},{7,6},{8,9},{9,8},{10,11... | collective-permute-start | bytes 1572872 | tf_op jit(solution)/shard_map/ppermute | solution.py:163
  157.9 10.6 %collective-permute-start.30 = (bf16[256,1024]{1,0:T(8,128)(2,1)S(1)}, bf16[256,1024]{1,0:T(8,128)(2,1)S(1)}, u32[]{:S(2)}, u32[]{:S(2)}) collective-permute-start(bf16[256,1024]{1,0:T(8,128)(2,1)S(1)} %add_convert_fusion.10.refs_3_), channel_id=1, source_target_pairs={{0,2},{7,5},{8,10},{15,13},{16,18},{23,21},{24,26},{31,29}} | collective-permute-start | bytes 1572872 | tf_op jit(solution)/shard_map/ppermute | solution.py:166
  162.3 7.7 %collective-permute-start.36 = (bf16[256,1024]{1,0:T(8,128)(2,1)S(1)}, bf16[256,1024]{1,0:T(8,128)(2,1)S(1)}, u32[]{:S(2)}, u32[]{:S(2)}) collective-permute-start(bf16[256,1024]{1,0:T(8,128)(2,1)S(1)} %get-tuple-element.33), channel_id=1, source_target_pairs={{0,1},{1,0},{2,3},{3,2},{4,5},{5,4},{6,7},{7,6},{8,9},{9,8},{10,11... | collective-permute-start | bytes 1572872 | tf_op jit(solution)/shard_map/ppermute | solution.py:163
  162.5 11.9 %collective-permute-start.38 = (bf16[256,1024]{1,0:T(8,128)(2,1)S(1)}, bf16[256,1024]{1,0:T(8,128)(2,1)S(1)}, u32[]{:S(2)}, u32[]{:S(2)}) collective-permute-start(bf16[256,1024]{1,0:T(8,128)(2,1)S(1)} %add_convert_fusion.7.refs_4_), channel_id=1, source_target_pairs={{0,2},{7,5},{8,10},{15,13},{16,18},{23,21},{24,26},{31,29}} | collective-permute-start | bytes 1572872 | tf_op jit(solution)/shard_map/ppermute | solution.py:166
  168.5 10.8 %collective-permute-start.27 = (bf16[256,1024]{1,0:T(8,128)(2,1)S(1)}, bf16[256,1024]{1,0:T(8,128)(2,1)S(1)}, u32[]{:S(2)}, u32[]{:S(2)}) collective-permute-start(bf16[256,1024]{1,0:T(8,128)(2,1)S(1)} %get-tuple-element.29), channel_id=1, source_target_pairs={{0,1},{1,0},{2,3},{3,2},{4,5},{5,4},{6,7},{7,6},{8,9},{9,8},{10,11... | collective-permute-start | bytes 1572872 | tf_op jit(solution)/shard_map/ppermute | solution.py:163
  168.8 31.2 %collective-permute-start.42 = (bf16[512,512]{1,0:T(8,128)(2,1)S(1)}, bf16[512,512]{1,0:T(8,128)(2,1)}, u32[]{:S(2)}, u32[]{:S(2)}) collective-permute-start(bf16[512,512]{1,0:T(8,128)(2,1)S(1)} %select_convert_fusion), channel_id=1, source_target_pairs={{0,1},{1,0},{2,3},{3,2},{4,5},{5,4},{6,7},{7,6},{8,9},{9,8},{10,11... | collective-permute-start | bytes 1572872 | tf_op jit(solution)/shard_map/ppermute | solution.py:163
  169.4 16.4 %collective-permute-start.35 = (bf16[256,1024]{1,0:T(8,128)(2,1)S(1)}, bf16[256,1024]{1,0:T(8,128)(2,1)S(1)}, u32[]{:S(2)}, u32[]{:S(2)}) collective-permute-start(bf16[256,1024]{1,0:T(8,128)(2,1)S(1)} %get-tuple-element.32), channel_id=1, source_target_pairs={{0,1},{1,0},{2,3},{3,2},{4,5},{5,4},{6,7},{7,6},{8,9},{9,8},{10,11... | collective-permute-start | bytes 1572872 | tf_op jit(solution)/shard_map/ppermute | solution.py:163
  170.0 11.1 %collective-permute-start.31 = (bf16[256,1024]{1,0:T(8,128)(2,1)S(1)}, bf16[256,1024]{1,0:T(8,128)(2,1)S(1)}, u32[]{:S(2)}, u32[]{:S(2)}) collective-permute-start(bf16[256,1024]{1,0:T(8,128)(2,1)S(1)} %add_convert_fusion.9), channel_id=1, source_target_pairs={{0,2},{2,4},{5,3},{7,5},{8,10},{10,12},{13,11},{15,13},{16,18},{18... | collective-permute-start | bytes 1572872 | tf_op jit(solution)/shard_map/ppermute | solution.py:166
  174.7 12.0 %collective-permute-start.39 = (bf16[256,1024]{1,0:T(8,128)(2,1)S(1)}, bf16[256,1024]{1,0:T(8,128)(2,1)S(1)}, u32[]{:S(2)}, u32[]{:S(2)}) collective-permute-start(bf16[256,1024]{1,0:T(8,128)(2,1)S(1)} %add_convert_fusion.6), channel_id=1, source_target_pairs={{0,2},{2,4},{5,3},{7,5},{8,10},{10,12},{13,11},{15,13},{16,18},{18... | collective-permute-start | bytes 1572872 | tf_op jit(solution)/shard_map/ppermute | solution.py:166
  181.4 14.7 %collective-permute-start.32 = (bf16[256,1024]{1,0:T(8,128)(2,1)S(1)}, bf16[256,1024]{1,0:T(8,128)(2,1)S(1)}, u32[]{:S(2)}, u32[]{:S(2)}) collective-permute-start(bf16[256,1024]{1,0:T(8,128)(2,1)S(1)} %add_convert_fusion.8), channel_id=1, source_target_pairs={{0,2},{2,4},{3,1},{4,6},{5,3},{7,5},{8,10},{10,12},{11,9},{12,14},... | collective-permute-start | bytes 1572872 | tf_op jit(solution)/shard_map/ppermute | solution.py:166
  187.0 11.1 %collective-permute-start.40 = (bf16[256,1024]{1,0:T(8,128)(2,1)S(1)}, bf16[256,1024]{1,0:T(8,128)(2,1)}, u32[]{:S(2)}, u32[]{:S(2)}) collective-permute-start(bf16[256,1024]{1,0:T(8,128)(2,1)S(1)} %add_convert_fusion.5), channel_id=1, source_target_pairs={{0,2},{2,4},{3,1},{4,6},{5,3},{7,5},{8,10},{10,12},{11,9},{12,14},... | collective-permute-start | bytes 1572872 | tf_op jit(solution)/shard_map/ppermute | solution.py:166
  197.0 5.7 %collective-permute-start.33 = (bf16[256,512]{1,0:T(8,128)(2,1)}, bf16[256,512]{1,0:T(8,128)(2,1)S(1)}, u32[]{:S(2)}, u32[]{:S(2)}) collective-permute-start(bf16[256,512]{1,0:T(8,128)(2,1)} %select_convert_fusion.2), channel_id=1, source_target_pairs={{0,1},{1,0},{2,3},{3,2},{4,5},{5,4},{6,7},{7,6},{8,9},{9,8},{10,11... | collective-permute-start | bytes 786440 | tf_op jit(solution)/shard_map/ppermute | solution.py:163
  200.0 2.8 %collective-permute-start.41 = (bf16[256,512]{1,0:T(8,128)(2,1)}, bf16[256,512]{1,0:T(8,128)(2,1)}, u32[]{:S(2)}, u32[]{:S(2)}) collective-permute-start(bf16[256,512]{1,0:T(8,128)(2,1)} %select_convert_fusion.1), channel_id=1, source_target_pairs={{0,1},{1,0},{2,3},{3,2},{4,5},{5,4},{6,7},{7,6},{8,9},{9,8},{10,11... | collective-permute-start | bytes 786440 | tf_op jit(solution)/shard_map/ppermute | solution.py:163
  (27 other events, 203.8 us)

commit v12 on v11

--- a/solution.py
+++ b/solution.py
@@ -71,33 +71,36 @@
     return order(fence, values, [ANY] * len(values), shapes, [], 4, after, aliases)
 
 
-def prepare(order, tokens, cotangent, gain, chips, after=()):
-    rows, model = tokens.shape
+def in_places(order, x, gain, chips, after=()):
+    rows, model = x.shape
     block = model // chips
 
-    def run(place_ref, tokens_ref, cot_ref, gain_ref, normed_out, cot_out):
-        xf = tokens_ref[...].astype(jnp.float32)
-        scale = lax.rsqrt(jnp.mean(xf * xf, axis=1, keepdims=True) + 1e-05)
+    def run(place_ref, x_ref, *refs):
+        out_ref = refs[-1]
+        if gain is not None:
+            xf = x_ref[...].astype(jnp.float32)
+            scale = lax.rsqrt(jnp.mean(xf * xf, axis=1, keepdims=True) + 1e-05)
         for p in range(chips):
             cols = pl.ds(pl.multiple_of(place_ref[p] * block, block), block)
-            to = slice(p * block, (p + 1) * block)
-            part = tokens_ref[:, cols].astype(jnp.float32)
-            normed_out[:, to] = (part * scale * gain_ref[:, cols]).astype(jnp.bfloat16)
-            cot_out[:, to] = cot_ref[:, cols]
+            part = x_ref[:, cols]
+            if gain is not None:
+                part = part.astype(jnp.float32) * scale * refs[0][:, cols]
+            out_ref[:, p * block : (p + 1) * block] = part.astype(jnp.bfloat16)
 
     tile = pl.BlockSpec((ROW_TILE, model), lambda i, _: (i, 0))
+    gains = () if gain is None else (gain[None],)
     return order(
         run,
-        (tokens, cotangent, gain[None]),
-        [tile, tile, pl.BlockSpec((1, model), lambda i, _: (0, 0))],
-        [jax.ShapeDtypeStruct((rows, model), jnp.bfloat16)] * 2,
+        (x, *gains),
+        [tile] + [pl.BlockSpec((1, model), lambda i, _: (0, 0))] * len(gains),
+        [jax.ShapeDtypeStruct((rows, model), jnp.bfloat16)],
         [],
-        24,
+        16,
         after,
         grid=rows // ROW_TILE,
-        out_specs=[tile, tile],
-        us=20.0,
-    )
+        out_specs=[tile],
+        us=5.0,
+    )[0]
 
 
 def join_cores(order, own, partner, parts, after=()):
@@ -166,13 +169,15 @@
         return lax.ppermute(value, "fsdp", move_perm(chips, active))
 
     class Gradient:
-        def __init__(self, mid, x, after=()):
+        def __init__(self, mid, x, after=(), late=()):
             terms = lax.dot_general(mid, x, (((0,), (0,)), ((), ())), preferred_element_type=f32)
             self.terms = terms.astype(bf16)
             if after:
                 self.terms = fence(order, self.terms, after=after)[0]
             self.across = [None] + [swap(self.block(chips - s)) for s in range(1, chips)]
             self.arrived = None
+            if late:
+                self.across[1] = fence(order, self.across[1], after=late)[0]
 
         def block(self, place):
             return self.terms[:, place * block : (place + 1) * block]
@@ -242,7 +247,7 @@
 
     joined = join_cores(order, second_own, second_partner, 1, (last[0],))
     ahead = gather(joined)
-    normed, cotangent = prepare(order, tokens[0], out_cotangent[0], norm_gain, chips, (*others[-1], *others[-2]))
+    normed = in_places(order, tokens[0], norm_gain, chips, (*others[-1], *others[-2]))
     values = jnp.concatenate(
         [
             jnp.dot(normed, part, preferred_element_type=f32).astype(bf16)
@@ -250,6 +255,7 @@
         ],
         axis=1,
     )
+    cotangent = in_places(order, out_cotangent[0], None, chips)
     pieces, others = ahead
     values = fence(order, values, after=(pieces[1][0], *early))[0]
     first = Gradient(values, cotangent, (pieces[2][0],))
@@ -261,8 +267,8 @@
     half = mid.shape[1] // HALVES
     second = []
     for j in range(HALVES):
-        after = (first.arrived,) if j else ()
-        second.append(Gradient(mid[:, j * half : (j + 1) * half], normed, after))
+        late = () if j else ()
+        second.append(Gradient(mid[:, j * half : (j + 1) * half], normed, (), late))
     for step in range(1, chips):
         sent = tuple(gradient.reduce(step) for gradient in second)
         if step == 1:

time: 207 us -> 194 us (0.937)
  starting transfers between devices: 102 us -> 95.2 us
  other arithmetic: 22.1 us -> 26.6 us
  local copies, waits for them, and re-layouts: 14 us -> 9.98 us
  waiting for transfers between devices: 32.1 us -> 29 us
  Pallas kernels: 14.6 us -> 11.6 us
    unnamed x63 -> x43, local copies, waits for them, and re-layouts: 11.7 us -> 6.17 us
    convert_element_type x9, other arithmetic: 4.66 us -> 9.2 us  [message(): return term.astype(bf16)]
    ppermute x18, starting transfers between devices: 58.2 us -> 54.2 us  [move(): return lax.ppermute(value, 'fsdp', move_perm(chips, active))]
    ppermute x18, waiting for transfers between devices: 27.7 us -> 24.6 us  [move(): return lax.ppermute(value, 'fsdp', move_perm(chips, active))]
    pallas_call x11, Pallas kernels: 14.6 us -> 11.6 us  [__call__(): pl.pallas_call(ordered, grid_spec=pltpu.PrefetchScalarGridSpec(num_scalar...]
    ppermute x23, starting transfers between devices: 38.1 us -> 35.7 us  [swap(): return lax.ppermute(value, 'fsdp', [(i, i ^ 1) for i in range(devices)])]
  transfers between devices with their start and end apart: 45 -> 45, of which waited for: 13 -> 15; matrix products, arithmetic and copies ran while one was open for 20% -> 25% of each run, Pallas kernels for 7% -> 5%
where the time goes in v12:
time: 194 us; the launch traced here: 193 us
  starting transfers between devices  95.2 us (49%)
  waiting for transfers between devices  29 us (15%)
  other arithmetic  26.6 us (14%)
  matrix products  19.2 us (10%)
  Pallas kernels  11.6 us (6%)
  local copies, waits for them, and re-layouts  9.98 us (5%)
    ppermute x18, starting transfers between devices, move(): return lax.ppermute(value, 'fsdp', move_perm(chips, active))  54.2 us
    ppermute x23, starting transfers between devices, swap(): return lax.ppermute(value, 'fsdp', [(i, i ^ 1) for i in range(devices)])  35.7 us
    ppermute x18, waiting for transfers between devices, move(): return lax.ppermute(value, 'fsdp', move_perm(chips, active))  24.6 us
    pallas_call x11, Pallas kernels, __call__(): pl.pallas_call(ordered, grid_spec=pltpu.PrefetchScalarGridSpec(num_scalar...  11.6 us
    dot_general x3, matrix products, __init__(): lax.dot_general(mid, x, (((0,), (0,)), ((), ())), preferred_element_type=...  10.1 us
    convert_element_type x9, other arithmetic, message(): return term.astype(bf16)  9.2 us
    unnamed x43, local copies, waits for them, and re-layouts  6.17 us
    ppermute x4, starting transfers between devices, per_device(): lax.ppermute(mine, 'replica', [(i, i ^ bit) for i in range(replicas)])  5.3 us
  transfers between devices with their start and end apart: 45, of which 15 were waited for; matrix products, arithmetic and copies ran while one was open for 25% of the time, Pallas kernels for 5%

profile of v12, /device:TPU:0, one launch (start us, length us, event | category | flops | bytes accessed | tf_op | source)
XLA Modules:
  0.0 193.1 jit_solution(11202279852536483178)
XLA Ops:
  2.0 1.6 collective-permute-done.1.refs_2_.refs_1_
  6.1 5.7 %collective-permute-start.8 = (bf16[1024,256]{1,0:T(8,128)(2,1)S(1)}, bf16[1024,256]{1,0:T(8,128)(2,1)}, u32[]{:S(2)}, u32[]{:S(2)}) collective-permute-start(bf16[1024,256]{1,0:T(8,128)(2,1)S(1)} %get-tuple-element.11), channel_id=1, source_target_pairs={{0,2},{2,4},{3,1},{4,6},{5,3},{7,5},{8,10},{10,12},{11,9},{12,14},... | collective-permute-start | bytes 1572872 | tf_op jit(solution)/shard_map/ppermute | solution.py:169
  11.7 3.5 %collective-permute-start.2 = (bf16[1024,256]{1,0:T(8,128)(2,1)S(1)}, bf16[1024,256]{1,0:T(8,128)(2,1)}, u32[]{:S(2)}, u32[]{:S(2)}) collective-permute-start(bf16[1024,256]{1,0:T(8,128)(2,1)S(1)} %get-tuple-element.10.refs_1_), channel_id=1, source_target_pairs={{0,2},{2,4},{3,1},{4,6},{5,3},{7,5},{8,10},{10,12},{11,9},{12,14},... | collective-permute-start | bytes 1572872 | tf_op jit(solution)/shard_map/ppermute | solution.py:169
  15.2 2.4 %collective-permute-done.8 = bf16[1024,256]{1,0:T(8,128)(2,1)} collective-permute-done((bf16[1024,256]{1,0:T(8,128)(2,1)S(1)}, bf16[1024,256]{1,0:T(8,128)(2,1)}, u32[]{:S(2)}, u32[]{:S(2)}) %collective-permute-start.8) | collective-permute-done | bytes 524320 | tf_op jit(solution)/shard_map/ppermute | solution.py:169
  18.8 4.4 %collective-permute-done.2 = bf16[1024,256]{1,0:T(8,128)(2,1)} collective-permute-done((bf16[1024,256]{1,0:T(8,128)(2,1)S(1)}, bf16[1024,256]{1,0:T(8,128)(2,1)}, u32[]{:S(2)}, u32[]{:S(2)}) %collective-permute-start.2) | collective-permute-done | bytes 524320 | tf_op jit(solution)/shard_map/ppermute | solution.py:169
  26.5 2.2 %fusion = (bf16[4096,128]{1,0:T(8,128)(2,1)S(1)}, bf16[4096,128]{1,0:T(8,128)(2,1)S(1)}) fusion(f32[4096]{0:T(1024)S(1)} %bitcast.50, bf16[1,8192,128]{2,1,0:T(8,128)(2,1)S(1)} %copy-done.12, f32[4096]{0:T(1024)S(1)} %bitcast.51), kind=kLoop, calls=%fused_computation.10 | loop fusion | flops 3145728 | bytes 4227072 | tf_op jit(solution)/shard_map/convert_element_type | solution.py:240
  28.6 1.7 collective-permute-start.20
  30.4 1.5 collective-permute-start.21
  32.5 15.3 %collective-permute-start.12 = (bf16[1024,256]{1,0:T(8,128)(2,1)S(1)}, bf16[1024,256]{1,0:T(8,128)(2,1)S(1)}, u32[]{:S(2)}, u32[]{:S(2)}) collective-permute-start(bf16[1024,256]{1,0:T(8,128)(2,1)S(1)} %collective-permute-done.9.refs_2_), channel_id=1, source_target_pairs={{0,1},{1,0},{2,3},{3,2},{4,5},{5,4},{6,7},{7,6},{8,9},{9,8},{10,11... | collective-permute-start | bytes 1572872 | tf_op jit(solution)/shard_map/ppermute | solution.py:166
  48.0 1.5 collective-permute-start.14
  52.4 5.3 %in_places.2.refs_2_ = bf16[1024,4096]{1,0:T(8,128)(2,1)S(1)} custom-call(s32[6]{0:T(128)S(1)} %stack.27.place_ref, bf16[1024,4096]{1,0:T(8,128)(2,1)S(1)} %bitcast.41, f32[1,4096]{1,0:T(1,128)S(1)} %bitcast.45, bf16[1024,512]{1,0:T(8,128)(2,1)S(1)} %join_cores.3.refs_2_, bf16[1024,256]{1,0:T(8,128)(2,1)S(1)} %collective-permute-done.5.refs_3_, ...), custom_call_target="tpu_custom_call" | custom-call | flops 5000000000 | bytes 1 | tf_op jit(solution)/shard_map/in_places/pallas_call | solution.py:39
  58.1 3.7 %collective-permute-done.14.refs_3_.refs_2_ = bf16[1024,512]{1,0:T(8,128)(2,1)S(1)} collective-permute-done((bf16[1024,512]{1,0:T(8,128)(2,1)S(1)}, bf16[1024,512]{1,0:T(8,128)(2,1)S(1)}, u32[]{:S(2)}, u32[]{:S(2)}) %collective-permute-start.14) | collective-permute-done | bytes 1048608 | tf_op jit(solution)/shard_map/ppermute | solution.py:169
  62.3 2.3 %convolution_convert_fusion.4 = bf16[1024,256]{1,0:T(8,128)(2,1)S(1)} fusion(bf16[1024,4096]{1,0:T(8,128)(2,1)S(1)} %in_places.2.refs_2_, bf16[4096,256]{1,0:T(8,128)(2,1)S(1)} %get-tuple-element.13), kind=kOutput, calls=%fused_computation.22 | convolution fusion | flops 2147745792 | bytes 11010048 | tf_op jit(solution)/shard_map/dot_general | solution.py:253
  65.4 2.3 %convolution_convert_fusion.5 = bf16[1024,256]{1,0:T(8,128)(2,1)S(1)} fusion(bf16[1024,4096]{1,0:T(8,128)(2,1)S(1)} %in_places.2.refs_2_, bf16[4096,256]{1,0:T(8,128)(2,1)S(1)} %get-tuple-element.12.refs_1_), kind=kOutput, calls=%fused_computation.23 | convolution fusion | flops 2147745792 | bytes 11010048 | tf_op jit(solution)/shard_map/dot_general | solution.py:253
  67.9 1.2 in_places.3.refs_1_
  69.7 5.0 %convolution_convert_fusion.refs_0_ = bf16[512,4096]{1,0:T(8,128)(2,1)S(1)} fusion(bf16[1024,512]{1,0:T(8,128)(2,1)S(1)} %fence.9.refs_1_, bf16[1024,4096]{1,0:T(8,128)(2,1)S(1)} %in_places.3.refs_1_), kind=kOutput, calls=%fused_computation | convolution fusion | flops 4297064448 | bytes 13631488 | tf_op jit(solution)/shard_map/dot_general | solution.py:173
  75.3 1.3 fusion.8
  76.6 7.8 %collective-permute-start.24 = (bf16[512,1024]{1,0:T(8,128)(2,1)S(1)}, bf16[512,1024]{1,0:T(8,128)(2,1)S(1)}, u32[]{:S(2)}, u32[]{:S(2)}) collective-permute-start(bf16[512,1024]{1,0:T(8,128)(2,1)S(1)} %get-tuple-element.24), channel_id=1, source_target_pairs={{0,1},{1,0},{2,3},{3,2},{4,5},{5,4},{6,7},{7,6},{8,9},{9,8},{10,11... | collective-permute-start | bytes 3145736 | tf_op jit(solution)/shard_map/ppermute | solution.py:166
  85.1 1.2 add_convert_fusion.1
  87.8 5.9 %collective-permute-start.25 = (bf16[512,1024]{1,0:T(8,128)(2,1)S(1)}, bf16[512,1024]{1,0:T(8,128)(2,1)S(1)}, u32[]{:S(2)}, u32[]{:S(2)}) collective-permute-start(bf16[512,1024]{1,0:T(8,128)(2,1)S(1)} %add_convert_fusion.4), channel_id=1, source_target_pairs={{0,2},{7,5},{8,10},{15,13},{16,18},{23,21},{24,26},{31,29}} | collective-permute-start | bytes 3145736 | tf_op jit(solution)/shard_map/ppermute | solution.py:169
  93.7 7.5 %collective-permute-start.17 = (bf16[1024,512]{1,0:T(8,128)(2,1)S(1)}, bf16[1024,512]{1,0:T(8,128)(2,1)S(1)}, u32[]{:S(2)}, u32[]{:S(2)}) collective-permute-start(bf16[1024,512]{1,0:T(8,128)(2,1)S(1)} %collective-permute-done.16), channel_id=1, source_target_pairs={{0,1},{1,0},{2,3},{3,2},{4,5},{5,4},{6,7},{7,6},{8,9},{9,8},{10,11... | collective-permute-start | bytes 3145736 | tf_op jit(solution)/shard_map/ppermute | solution.py:166
  101.2 1.2 add_convert_fusion
  103.1 1.6 collective-permute-start.44
  106.4 4.5 %collective-permute-start.26 = (bf16[512,1024]{1,0:T(8,128)(2,1)S(1)}, bf16[512,1024]{1,0:T(8,128)(2,1)S(1)}, u32[]{:S(2)}, u32[]{:S(2)}) collective-permute-start(bf16[512,1024]{1,0:T(8,128)(2,1)S(1)} %add_convert_fusion.3), channel_id=1, source_target_pairs={{0,2},{2,4},{5,3},{7,5},{8,10},{10,12},{13,11},{15,13},{16,18},{18... | collective-permute-start | bytes 3145736 | tf_op jit(solution)/shard_map/ppermute | solution.py:169
  111.9 4.5 %convolution_convert_fusion.3.refs_0_ = bf16[1024,512]{1,0:T(8,128)(2,1)S(1)} fusion(bf16[1024,4096]{1,0:T(8,128)(2,1)S(1)} %in_places.3.refs_1_, bf16[4096,512]{1,0:T(8,128)(2,1)S(1)} %fence.11.refs_1_), kind=kOutput, calls=%fused_computation.21 | convolution fusion | flops 4295491584 | bytes 13631488 | tf_op jit(solution)/shard_map/dot_general | solution.py:265
  116.4 6.7 %collective-permute-done.26 = bf16[512,1024]{1,0:T(8,128)(2,1)S(1)} collective-permute-done((bf16[512,1024]{1,0:T(8,128)(2,1)S(1)}, bf16[512,1024]{1,0:T(8,128)(2,1)S(1)}, u32[]{:S(2)}, u32[]{:S(2)}) %collective-permute-start.26) | collective-permute-done | bytes 1048608 | tf_op jit(solution)/shard_map/ppermute | solution.py:169
  123.1 1.9 add_convert_fusion.2.refs_2_
  126.0 2.5 %convolution_convert_fusion.2 = bf16[256,4096]{1,0:T(8,128)(2,1)S(1)} fusion(bf16[1024,4096]{1,0:T(8,128)(2,1)S(1)} %in_places.2.refs_2_, bf16[1024,512]{1,0:T(8,128)(2,1)S(1)} %fence.12.refs_2_), kind=kOutput, calls=%fused_computation.2 | convolution fusion | flops 2148532224 | bytes 11010048 | tf_op jit(solution)/shard_map/dot_general | solution.py:173
  128.5 2.5 %convolution_convert_fusion.1 = bf16[256,4096]{1,0:T(8,128)(2,1)S(1)} fusion(bf16[1024,4096]{1,0:T(8,128)(2,1)S(1)} %in_places.2.refs_2_, bf16[1024,512]{1,0:T(8,128)(2,1)S(1)} %fence.12.refs_2_), kind=kOutput, calls=%fused_computation.1 | convolution fusion | flops 2148532224 | bytes 11010048 | tf_op jit(solution)/shard_map/dot_general | solution.py:173
  131.1 1.2 fusion.9
  132.3 1.2 fusion.10
  134.0 6.1 %collective-permute-start.41 = (bf16[512,1024]{1,0:T(8,128)(2,1)}, bf16[512,1024]{1,0:T(8,128)(2,1)S(1)}, u32[]{:S(2)}, u32[]{:S(2)}) collective-permute-start(bf16[512,1024]{1,0:T(8,128)(2,1)} %copy-done.1), channel_id=1, source_target_pairs={{0,2},{2,4},{3,1},{4,6},{5,3},{7,5},{8,10},{10,12},{11,9},{12,14},... | collective-permute-start | bytes 3145736 | tf_op jit(solution)/shard_map/ppermute | solution.py:169
  140.2 1.4 add_convert_fusion.10.refs_3_
  142.2 1.4 add_convert_fusion.7.refs_4_
  143.6 4.4 %collective-permute-start.30 = (bf16[256,1024]{1,0:T(8,128)(2,1)S(1)}, bf16[256,1024]{1,0:T(8,128)(2,1)}, u32[]{:S(2)}, u32[]{:S(2)}) collective-permute-start(bf16[256,1024]{1,0:T(8,128)(2,1)S(1)} %add_convert_fusion.10.refs_3_), channel_id=1, source_target_pairs={{0,2},{7,5},{8,10},{15,13},{16,18},{23,21},{24,26},{31,29}} | collective-permute-start | bytes 1572872 | tf_op jit(solution)/shard_map/ppermute | solution.py:169
  148.0 2.1 %collective-permute-start.37 = (bf16[256,1024]{1,0:T(8,128)(2,1)S(1)}, bf16[256,1024]{1,0:T(8,128)(2,1)}, u32[]{:S(2)}, u32[]{:S(2)}) collective-permute-start(bf16[256,1024]{1,0:T(8,128)(2,1)S(1)} %add_convert_fusion.7.refs_4_), channel_id=1, source_target_pairs={{0,2},{7,5},{8,10},{15,13},{16,18},{23,21},{24,26},{31,29}} | collective-permute-start | bytes 1572872 | tf_op jit(solution)/shard_map/ppermute | solution.py:169
  150.7 2.2 %convert_add_fusion = (f32[4096,128]{1,0:T(8,128)S(1)}, f32[4096,128]{1,0:T(8,128)S(1)}) fusion(bf16[4096,128]{1,0:T(8,128)(2,1)S(1)} %get-tuple-element.15, bf16[4096,128]{1,0:T(8,128)(2,1)} %add_convert_fusion, bf16[4096,128]{1,0:T(8,128)(2,1)S(1)} %get-tuple-element.14, bf16[4096,128]{1,0:T(8,128)(2,1)} %add_convert_fusion.1), kind=kLoop, calls=%fused_computation.13 | loop fusion | flops 3145728 | bytes 8388608 | tf_op jit(solution)/shard_map/add | solution.py:278
  154.1 3.9 %subtract_convert_fusion = (bf16[8192,128]{1,0:T(8,128)(2,1)}, f32[8192,128]{1,0:T(8,128)}) fusion(bf16[8192,128]{1,0:T(8,128)(2,1)S(1)} %copy-done.13, f32[4096,128]{1,0:T(8,128)S(1)} %get-tuple-element.35, f32[4096,128]{1,0:T(8,128)S(1)} %get-tuple-element.36, f32[8192,128]{1,0:T(8,128)S(1)} %copy-done.11), kind=kLoop, calls=%fused_computation.5 | loop fusion | flops 10485760 | bytes 16777216 | tf_op jit(solution)/shard_map/convert_element_type | solution.py:135
  158.7 1.5 add_convert_fusion.9
  160.2 4.0 %collective-permute-start.31 = (bf16[256,1024]{1,0:T(8,128)(2,1)S(1)}, bf16[256,1024]{1,0:T(8,128)(2,1)S(1)}, u32[]{:S(2)}, u32[]{:S(2)}) collective-permute-start(bf16[256,1024]{1,0:T(8,128)(2,1)S(1)} %add_convert_fusion.9), channel_id=1, source_target_pairs={{0,2},{2,4},{5,3},{7,5},{8,10},{10,12},{13,11},{15,13},{16,18},{18... | collective-permute-start | bytes 1572872 | tf_op jit(solution)/shard_map/ppermute | solution.py:169
  164.2 1.5 add_convert_fusion.6
  165.7 4.1 %collective-permute-start.38 = (bf16[256,1024]{1,0:T(8,128)(2,1)S(1)}, bf16[256,1024]{1,0:T(8,128)(2,1)S(1)}, u32[]{:S(2)}, u32[]{:S(2)}) collective-permute-start(bf16[256,1024]{1,0:T(8,128)(2,1)S(1)} %add_convert_fusion.6), channel_id=1, source_target_pairs={{0,2},{2,4},{5,3},{7,5},{8,10},{10,12},{13,11},{15,13},{16,18},{18... | collective-permute-start | bytes 1572872 | tf_op jit(solution)/shard_map/ppermute | solution.py:169
  169.8 1.6 convert_add_fusion.2
  171.7 3.8 %collective-permute-start.32 = (bf16[256,1024]{1,0:T(8,128)(2,1)S(1)}, bf16[256,1024]{1,0:T(8,128)(2,1)S(1)}, u32[]{:S(2)}, u32[]{:S(2)}) collective-permute-start(bf16[256,1024]{1,0:T(8,128)(2,1)S(1)} %add_convert_fusion.8), channel_id=1, source_target_pairs={{0,2},{2,4},{3,1},{4,6},{5,3},{7,5},{8,10},{10,12},{11,9},{12,14},... | collective-permute-start | bytes 1572872 | tf_op jit(solution)/shard_map/ppermute | solution.py:169
  176.8 4.4 %collective-permute-start.39 = (bf16[256,1024]{1,0:T(8,128)(2,1)S(1)}, bf16[256,1024]{1,0:T(8,128)(2,1)S(1)}, u32[]{:S(2)}, u32[]{:S(2)}) collective-permute-start(bf16[256,1024]{1,0:T(8,128)(2,1)S(1)} %add_convert_fusion.5), channel_id=1, source_target_pairs={{0,2},{2,4},{3,1},{4,6},{5,3},{7,5},{8,10},{10,12},{11,9},{12,14},... | collective-permute-start | bytes 1572872 | tf_op jit(solution)/shard_map/ppermute | solution.py:169
  183.2 4.7 %collective-permute-done.39 = bf16[256,1024]{1,0:T(8,128)(2,1)S(1)} collective-permute-done((bf16[256,1024]{1,0:T(8,128)(2,1)S(1)}, bf16[256,1024]{1,0:T(8,128)(2,1)S(1)}, u32[]{:S(2)}, u32[]{:S(2)}) %collective-permute-start.39) | collective-permute-done | bytes 524320 | tf_op jit(solution)/shard_map/ppermute | solution.py:169
  189.1 1.3 copy.25
  191.8 1.3 copy.24
  (146 shorter events, 30.7 us)
Async XLA Ops:
  1.4 2.2 %collective-permute-start.1 = (bf16[512,512]{1,0:T(8,128)(2,1)}, bf16[512,512]{1,0:T(8,128)(2,1)S(1)}, u32[]{:S(2)}, u32[]{:S(2)}) collective-permute-start(bf16[512,512]{1,0:T(8,128)(2,1)} %bitcast.48), channel_id=1, source_target_pairs={{0,1},{1,0},{2,3},{3,2},{4,5},{5,4},{6,7},{7,6},{8,9},{9,8},{10,11... | collective-permute-start | bytes 1572872 | tf_op jit(solution)/shard_map/ppermute | solution.py:166
  1.8 2.5 %collective-permute-start = (bf16[512,512]{1,0:T(8,128)(2,1)}, bf16[512,512]{1,0:T(8,128)(2,1)S(1)}, u32[]{:S(2)}, u32[]{:S(2)}) collective-permute-start(bf16[512,512]{1,0:T(8,128)(2,1)} %bitcast.46), channel_id=1, source_target_pairs={{0,1},{1,0},{2,3},{3,2},{4,5},{5,4},{6,7},{7,6},{8,9},{9,8},{10,11... | collective-permute-start | bytes 1572872 | tf_op jit(solution)/shard_map/ppermute | solution.py:166
  6.1 11.5 %collective-permute-start.8 = (bf16[1024,256]{1,0:T(8,128)(2,1)S(1)}, bf16[1024,256]{1,0:T(8,128)(2,1)}, u32[]{:S(2)}, u32[]{:S(2)}) collective-permute-start(bf16[1024,256]{1,0:T(8,128)(2,1)S(1)} %get-tuple-element.11), channel_id=1, source_target_pairs={{0,2},{2,4},{3,1},{4,6},{5,3},{7,5},{8,10},{10,12},{11,9},{12,14},... | collective-permute-start | bytes 1572872 | tf_op jit(solution)/shard_map/ppermute | solution.py:169
  11.7 11.5 %collective-permute-start.2 = (bf16[1024,256]{1,0:T(8,128)(2,1)S(1)}, bf16[1024,256]{1,0:T(8,128)(2,1)}, u32[]{:S(2)}, u32[]{:S(2)}) collective-permute-start(bf16[1024,256]{1,0:T(8,128)(2,1)S(1)} %get-tuple-element.10.refs_1_), channel_id=1, source_target_pairs={{0,2},{2,4},{3,1},{4,6},{5,3},{7,5},{8,10},{10,12},{11,9},{12,14},... | collective-permute-start | bytes 1572872 | tf_op jit(solution)/shard_map/ppermute | solution.py:169
  17.6 6.8 %collective-permute-start.9 = (bf16[1024,256]{1,0:T(8,128)(2,1)}, bf16[1024,256]{1,0:T(8,128)(2,1)S(1)}, u32[]{:S(2)}, u32[]{:S(2)}) collective-permute-start(bf16[1024,256]{1,0:T(8,128)(2,1)} %collective-permute-done.8), channel_id=1, source_target_pairs={{2,4},{3,1},{4,6},{5,3},{10,12},{11,9},{12,14},{13,11},{18,20},{19... | collective-permute-start | bytes 1572872 | tf_op jit(solution)/shard_map/ppermute | solution.py:169
  18.3 29.6 %collective-permute-start.13 = (bf16[1024,256]{1,0:T(8,128)(2,1)}, bf16[1024,256]{1,0:T(8,128)(2,1)S(1)}, u32[]{:S(2)}, u32[]{:S(2)}) collective-permute-start(bf16[1024,256]{1,0:T(8,128)(2,1)} %collective-permute-done.8), channel_id=1, source_target_pairs={{0,1},{1,0},{2,3},{3,2},{4,5},{5,4},{6,7},{7,6},{8,9},{9,8},{10,11... | collective-permute-start | bytes 1572872 | tf_op jit(solution)/shard_map/ppermute | solution.py:166
  23.2 2.5 %collective-permute-start.3 = (bf16[1024,256]{1,0:T(8,128)(2,1)}, bf16[1024,256]{1,0:T(8,128)(2,1)S(1)}, u32[]{:S(2)}, u32[]{:S(2)}) collective-permute-start(bf16[1024,256]{1,0:T(8,128)(2,1)} %collective-permute-done.2), channel_id=1, source_target_pairs={{2,4},{3,1},{4,6},{5,3},{10,12},{11,9},{12,14},{13,11},{18,20},{19... | collective-permute-start | bytes 1572872 | tf_op jit(solution)/shard_map/ppermute | solution.py:169
  23.9 8.6 %collective-permute-start.7 = (bf16[1024,256]{1,0:T(8,128)(2,1)}, bf16[1024,256]{1,0:T(8,128)(2,1)S(1)}, u32[]{:S(2)}, u32[]{:S(2)}) collective-permute-start(bf16[1024,256]{1,0:T(8,128)(2,1)} %collective-permute-done.2), channel_id=1, source_target_pairs={{0,1},{1,0},{2,3},{3,2},{4,5},{5,4},{6,7},{7,6},{8,9},{9,8},{10,11... | collective-permute-start | bytes 1572872 | tf_op jit(solution)/shard_map/ppermute | solution.py:166
  24.4 23.6 %collective-permute-start.10 = (bf16[1024,256]{1,0:T(8,128)(2,1)S(1)}, bf16[1024,256]{1,0:T(8,128)(2,1)S(1)}, u32[]{:S(2)}, u32[]{:S(2)}) collective-permute-start(bf16[1024,256]{1,0:T(8,128)(2,1)S(1)} %collective-permute-done.9.refs_2_), channel_id=1, source_target_pairs={{3,1},{4,6},{11,9},{12,14},{19,17},{20,22},{27,25},{28,30}} | collective-permute-start | bytes 1572872 | tf_op jit(solution)/shard_map/ppermute | solution.py:169
  25.7 4.6 %collective-permute-start.4 = (bf16[1024,256]{1,0:T(8,128)(2,1)S(1)}, bf16[1024,256]{1,0:T(8,128)(2,1)S(1)}, u32[]{:S(2)}, u32[]{:S(2)}) collective-permute-start(bf16[1024,256]{1,0:T(8,128)(2,1)S(1)} %collective-permute-done.3), channel_id=1, source_target_pairs={{3,1},{4,6},{11,9},{12,14},{19,17},{20,22},{27,25},{28,30}} | collective-permute-start | bytes 1572872 | tf_op jit(solution)/shard_map/ppermute | solution.py:169
  26.4 25.9 %slice-start = ((s8[8388608]{0:T(1024)(128)(4,1)}), s8[4194304]{0:T(1024)(128)(4,1)S(1)}, s32[]{:S(2)}) async-start(s8[8388608]{0:T(1024)(128)(4,1)} %bitcast.39), calls=%async_computation | async-start | bytes 8388608
  28.6 40.4 %collective-permute-start.20 = (bf16[4096,128]{1,0:T(8,128)(2,1)S(1)}, bf16[4096,128]{1,0:T(8,128)(2,1)S(1)}, u32[]{:S(2)}, u32[]{:S(2)}) collective-permute-start(bf16[4096,128]{1,0:T(8,128)(2,1)S(1)} %get-tuple-element.32), channel_id=1, source_target_pairs={{0,8},{8,0},{16,24},{24,16},{1,9},{9,1},{17,25},{25,17},{2,10},{10... | collective-permute-start | bytes 3145736 | tf_op jit(solution)/shard_map/ppermute | solution.py:242
  30.4 22.0 %slice-start.1 = ((s8[8388608]{0:T(1024)(128)(4,1)}), s8[4194304]{0:T(1024)(128)(4,1)S(1)}, s32[]{:S(2)}) async-start(s8[8388608]{0:T(1024)(128)(4,1)} %bitcast.39), calls=%async_computation.1 | async-start | bytes 8388608
  30.4 38.7 %collective-permute-start.21 = (bf16[4096,128]{1,0:T(8,128)(2,1)S(1)}, bf16[4096,128]{1,0:T(8,128)(2,1)S(1)}, u32[]{:S(2)}, u32[]{:S(2)}) collective-permute-start(bf16[4096,128]{1,0:T(8,128)(2,1)S(1)} %get-tuple-element.31), channel_id=1, source_target_pairs={{0,16},{8,24},{16,0},{24,8},{1,17},{9,25},{17,1},{25,9},{2,18},{10... | collective-permute-start | bytes 3145736 | tf_op jit(solution)/shard_map/ppermute | solution.py:242
  32.5 17.1 %collective-permute-start.12 = (bf16[1024,256]{1,0:T(8,128)(2,1)S(1)}, bf16[1024,256]{1,0:T(8,128)(2,1)S(1)}, u32[]{:S(2)}, u32[]{:S(2)}) collective-permute-start(bf16[1024,256]{1,0:T(8,128)(2,1)S(1)} %collective-permute-done.9.refs_2_), channel_id=1, source_target_pairs={{0,1},{1,0},{2,3},{3,2},{4,5},{5,4},{6,7},{7,6},{8,9},{9,8},{10,11... | collective-permute-start | bytes 1572872 | tf_op jit(solution)/shard_map/ppermute | solution.py:166
  47.9 2.2 %collective-permute-start.6 = (bf16[1024,256]{1,0:T(8,128)(2,1)S(1)}, bf16[1024,256]{1,0:T(8,128)(2,1)S(1)}, u32[]{:S(2)}, u32[]{:S(2)}) collective-permute-start(bf16[1024,256]{1,0:T(8,128)(2,1)S(1)} %collective-permute-done.3), channel_id=1, source_target_pairs={{0,1},{1,0},{2,3},{3,2},{4,5},{5,4},{6,7},{7,6},{8,9},{9,8},{10,11... | collective-permute-start | bytes 1572872 | tf_op jit(solution)/shard_map/ppermute | solution.py:166
  48.0 13.8 %collective-permute-start.14 = (bf16[1024,512]{1,0:T(8,128)(2,1)S(1)}, bf16[1024,512]{1,0:T(8,128)(2,1)S(1)}, u32[]{:S(2)}, u32[]{:S(2)}) collective-permute-start(bf16[1024,512]{1,0:T(8,128)(2,1)S(1)} %join_cores.3.refs_2_), channel_id=1, source_target_pairs={{0,2},{2,4},{3,1},{4,6},{5,3},{7,5},{8,10},{10,12},{11,9},{12,14},... | collective-permute-start | bytes 3145736 | tf_op jit(solution)/shard_map/ppermute | solution.py:169
  49.6 2.0 %collective-permute-start.11 = (bf16[1024,256]{1,0:T(8,128)(2,1)S(1)}, bf16[1024,256]{1,0:T(8,128)(2,1)S(1)}, u32[]{:S(2)}, u32[]{:S(2)}) collective-permute-start(bf16[1024,256]{1,0:T(8,128)(2,1)S(1)} %collective-permute-done.10), channel_id=1, source_target_pairs={{0,1},{1,0},{2,3},{3,2},{4,5},{5,4},{6,7},{7,6},{8,9},{9,8},{10,11... | collective-permute-start | bytes 1572872 | tf_op jit(solution)/shard_map/ppermute | solution.py:166
  50.1 2.2 %collective-permute-start.5 = (bf16[1024,256]{1,0:T(8,128)(2,1)S(1)}, bf16[1024,256]{1,0:T(8,128)(2,1)S(1)}, u32[]{:S(2)}, u32[]{:S(2)}) collective-permute-start(bf16[1024,256]{1,0:T(8,128)(2,1)S(1)} %collective-permute-done.4.refs_3_), channel_id=1, source_target_pairs={{0,1},{1,0},{2,3},{3,2},{4,5},{5,4},{6,7},{7,6},{8,9},{9,8},{10,11... | collective-permute-start | bytes 1572872 | tf_op jit(solution)/shard_map/ppermute | solution.py:166
  64.7 10.0 %collective-permute-start.15 = (bf16[1024,512]{1,0:T(8,128)(2,1)S(1)}, bf16[1024,512]{1,0:T(8,128)(2,1)S(1)}, u32[]{:S(2)}, u32[]{:S(2)}) collective-permute-start(bf16[1024,512]{1,0:T(8,128)(2,1)S(1)} %collective-permute-done.14.refs_3_.refs_2_), channel_id=1, source_target_pairs={{2,4},{3,1},{4,6},{5,3},{10,12},{11,9},{12,14},{13,11},{18,20},{19... | collective-permute-start | bytes 3145736 | tf_op jit(solution)/shard_map/ppermute | solution.py:169
  75.3 47.9 %copy-start = (bf16[512,4096]{1,0:T(8,128)(2,1)}, bf16[512,4096]{1,0:T(8,128)(2,1)S(1)}, u32[]{:S(2)}) copy-start(bf16[512,4096]{1,0:T(8,128)(2,1)S(1)} %fence.10.refs_1_) | copy-start | bytes 12582916
  76.6 10.8 %collective-permute-start.24 = (bf16[512,1024]{1,0:T(8,128)(2,1)S(1)}, bf16[512,1024]{1,0:T(8,128)(2,1)S(1)}, u32[]{:S(2)}, u32[]{:S(2)}) collective-permute-start(bf16[512,1024]{1,0:T(8,128)(2,1)S(1)} %get-tuple-element.24), channel_id=1, source_target_pairs={{0,1},{1,0},{2,3},{3,2},{4,5},{5,4},{6,7},{7,6},{8,9},{9,8},{10,11... | collective-permute-start | bytes 3145736 | tf_op jit(solution)/shard_map/ppermute | solution.py:166
  84.3 9.4 %collective-permute-start.16 = (bf16[1024,512]{1,0:T(8,128)(2,1)S(1)}, bf16[1024,512]{1,0:T(8,128)(2,1)S(1)}, u32[]{:S(2)}, u32[]{:S(2)}) collective-permute-start(bf16[1024,512]{1,0:T(8,128)(2,1)S(1)} %collective-permute-done.15.refs_2_), channel_id=1, source_target_pairs={{3,1},{4,6},{11,9},{12,14},{19,17},{20,22},{27,25},{28,30}} | collective-permute-start | bytes 3145736 | tf_op jit(solution)/shard_map/ppermute | solution.py:169
  86.3 16.2 %collective-permute-start.19 = (bf16[1024,512]{1,0:T(8,128)(2,1)S(1)}, bf16[1024,512]{1,0:T(8,128)(2,1)S(1)}, u32[]{:S(2)}, u32[]{:S(2)}) collective-permute-start(bf16[1024,512]{1,0:T(8,128)(2,1)S(1)} %collective-permute-done.14.refs_3_.refs_2_), channel_id=1, source_target_pairs={{0,1},{1,0},{2,3},{3,2},{4,5},{5,4},{6,7},{7,6},{8,9},{9,8},{10,11... | collective-permute-start | bytes 3145736 | tf_op jit(solution)/shard_map/ppermute | solution.py:166
  86.9 17.9 %collective-permute-start.23 = (bf16[512,1024]{1,0:T(8,128)(2,1)S(1)}, bf16[512,1024]{1,0:T(8,128)(2,1)S(1)}, u32[]{:S(2)}, u32[]{:S(2)}) collective-permute-start(bf16[512,1024]{1,0:T(8,128)(2,1)S(1)} %get-tuple-element.23), channel_id=1, source_target_pairs={{0,1},{1,0},{2,3},{3,2},{4,5},{5,4},{6,7},{7,6},{8,9},{9,8},{10,11... | collective-permute-start | bytes 3145736 | tf_op jit(solution)/shard_map/ppermute | solution.py:166
  86.9 16.2 %collective-permute-start.18 = (bf16[1024,512]{1,0:T(8,128)(2,1)S(1)}, bf16[1024,512]{1,0:T(8,128)(2,1)S(1)}, u32[]{:S(2)}, u32[]{:S(2)}) collective-permute-start(bf16[1024,512]{1,0:T(8,128)(2,1)S(1)} %collective-permute-done.15.refs_2_), channel_id=1, source_target_pairs={{0,1},{1,0},{2,3},{3,2},{4,5},{5,4},{6,7},{7,6},{8,9},{9,8},{10,11... | collective-permute-start | bytes 3145736 | tf_op jit(solution)/shard_map/ppermute | solution.py:166
  87.8 18.0 %collective-permute-start.25 = (bf16[512,1024]{1,0:T(8,128)(2,1)S(1)}, bf16[512,1024]{1,0:T(8,128)(2,1)S(1)}, u32[]{:S(2)}, u32[]{:S(2)}) collective-permute-start(bf16[512,1024]{1,0:T(8,128)(2,1)S(1)} %add_convert_fusion.4), channel_id=1, source_target_pairs={{0,2},{7,5},{8,10},{15,13},{16,18},{23,21},{24,26},{31,29}} | collective-permute-start | bytes 3145736 | tf_op jit(solution)/shard_map/ppermute | solution.py:169
  93.7 17.2 %collective-permute-start.17 = (bf16[1024,512]{1,0:T(8,128)(2,1)S(1)}, bf16[1024,512]{1,0:T(8,128)(2,1)S(1)}, u32[]{:S(2)}, u32[]{:S(2)}) collective-permute-start(bf16[1024,512]{1,0:T(8,128)(2,1)S(1)} %collective-permute-done.16), channel_id=1, source_target_pairs={{0,1},{1,0},{2,3},{3,2},{4,5},{5,4},{6,7},{7,6},{8,9},{9,8},{10,11... | collective-permute-start | bytes 3145736 | tf_op jit(solution)/shard_map/ppermute | solution.py:166
  102.5 41.1 %collective-permute-start.43 = (bf16[4096,128]{1,0:T(8,128)(2,1)}, bf16[4096,128]{1,0:T(8,128)(2,1)S(1)}, u32[]{:S(2)}, u32[]{:S(2)}) collective-permute-start(bf16[4096,128]{1,0:T(8,128)(2,1)} %add_convert_fusion.1), channel_id=1, source_target_pairs={{0,16},{8,24},{16,0},{24,8},{1,17},{9,25},{17,1},{25,9},{2,18},{10... | collective-permute-start | bytes 3145736 | tf_op jit(solution)/shard_map/ppermute | solution.py:242
  103.1 44.9 %collective-permute-start.44 = (bf16[4096,128]{1,0:T(8,128)(2,1)}, bf16[4096,128]{1,0:T(8,128)(2,1)S(1)}, u32[]{:S(2)}, u32[]{:S(2)}) collective-permute-start(bf16[4096,128]{1,0:T(8,128)(2,1)} %add_convert_fusion), channel_id=1, source_target_pairs={{0,8},{8,0},{16,24},{24,16},{1,9},{9,1},{17,25},{25,17},{2,10},{10... | collective-permute-start | bytes 3145736 | tf_op jit(solution)/shard_map/ppermute | solution.py:242
  104.8 11.6 %collective-permute-start.22 = (bf16[512,1024]{1,0:T(8,128)(2,1)}, bf16[512,1024]{1,0:T(8,128)(2,1)}, u32[]{:S(2)}, u32[]{:S(2)}) collective-permute-start(bf16[512,1024]{1,0:T(8,128)(2,1)} %get-tuple-element.22), channel_id=1, source_target_pairs={{0,1},{1,0},{2,3},{3,2},{4,5},{5,4},{6,7},{7,6},{8,9},{9,8},{10,11... | collective-permute-start | bytes 3145736 | tf_op jit(solution)/shard_map/ppermute | solution.py:166
  106.4 16.7 %collective-permute-start.26 = (bf16[512,1024]{1,0:T(8,128)(2,1)S(1)}, bf16[512,1024]{1,0:T(8,128)(2,1)S(1)}, u32[]{:S(2)}, u32[]{:S(2)}) collective-permute-start(bf16[512,1024]{1,0:T(8,128)(2,1)S(1)} %add_convert_fusion.3), channel_id=1, source_target_pairs={{0,2},{2,4},{5,3},{7,5},{8,10},{10,12},{13,11},{15,13},{16,18},{18... | collective-permute-start | bytes 3145736 | tf_op jit(solution)/shard_map/ppermute | solution.py:169
  132.3 7.8 %collective-permute-start.29 = (bf16[256,1024]{1,0:T(8,128)(2,1)}, bf16[256,1024]{1,0:T(8,128)(2,1)}, u32[]{:S(2)}, u32[]{:S(2)}) collective-permute-start(bf16[256,1024]{1,0:T(8,128)(2,1)} %get-tuple-element.27), channel_id=1, source_target_pairs={{0,1},{1,0},{2,3},{3,2},{4,5},{5,4},{6,7},{7,6},{8,9},{9,8},{10,11... | collective-permute-start | bytes 1572872 | tf_op jit(solution)/shard_map/ppermute | solution.py:166
  133.6 8.1 %collective-permute-start.36 = (bf16[256,1024]{1,0:T(8,128)(2,1)}, bf16[256,1024]{1,0:T(8,128)(2,1)}, u32[]{:S(2)}, u32[]{:S(2)}) collective-permute-start(bf16[256,1024]{1,0:T(8,128)(2,1)} %get-tuple-element.30), channel_id=1, source_target_pairs={{0,1},{1,0},{2,3},{3,2},{4,5},{5,4},{6,7},{7,6},{8,9},{9,8},{10,11... | collective-permute-start | bytes 1572872 | tf_op jit(solution)/shard_map/ppermute | solution.py:166
  134.0 35.8 %collective-permute-start.41 = (bf16[512,1024]{1,0:T(8,128)(2,1)}, bf16[512,1024]{1,0:T(8,128)(2,1)S(1)}, u32[]{:S(2)}, u32[]{:S(2)}) collective-permute-start(bf16[512,1024]{1,0:T(8,128)(2,1)} %copy-done.1), channel_id=1, source_target_pairs={{0,2},{2,4},{3,1},{4,6},{5,3},{7,5},{8,10},{10,12},{11,9},{12,14},... | collective-permute-start | bytes 3145736 | tf_op jit(solution)/shard_map/ppermute | solution.py:169
  140.1 17.9 %collective-permute-start.28 = (bf16[256,1024]{1,0:T(8,128)(2,1)}, bf16[256,1024]{1,0:T(8,128)(2,1)}, u32[]{:S(2)}, u32[]{:S(2)}) collective-permute-start(bf16[256,1024]{1,0:T(8,128)(2,1)} %get-tuple-element.26), channel_id=1, source_target_pairs={{0,1},{1,0},{2,3},{3,2},{4,5},{5,4},{6,7},{7,6},{8,9},{9,8},{10,11... | collective-permute-start | bytes 1572872 | tf_op jit(solution)/shard_map/ppermute | solution.py:166
  141.6 18.5 %collective-permute-start.35 = (bf16[256,1024]{1,0:T(8,128)(2,1)}, bf16[256,1024]{1,0:T(8,128)(2,1)}, u32[]{:S(2)}, u32[]{:S(2)}) collective-permute-start(bf16[256,1024]{1,0:T(8,128)(2,1)} %get-tuple-element.29), channel_id=1, source_target_pairs={{0,1},{1,0},{2,3},{3,2},{4,5},{5,4},{6,7},{7,6},{8,9},{9,8},{10,11... | collective-permute-start | bytes 1572872 | tf_op jit(solution)/shard_map/ppermute | solution.py:166
  143.6 14.6 %collective-permute-start.30 = (bf16[256,1024]{1,0:T(8,128)(2,1)S(1)}, bf16[256,1024]{1,0:T(8,128)(2,1)}, u32[]{:S(2)}, u32[]{:S(2)}) collective-permute-start(bf16[256,1024]{1,0:T(8,128)(2,1)S(1)} %add_convert_fusion.10.refs_3_), channel_id=1, source_target_pairs={{0,2},{7,5},{8,10},{15,13},{16,18},{23,21},{24,26},{31,29}} | collective-permute-start | bytes 1572872 | tf_op jit(solution)/shard_map/ppermute | solution.py:169
  148.0 16.2 %collective-permute-start.37 = (bf16[256,1024]{1,0:T(8,128)(2,1)S(1)}, bf16[256,1024]{1,0:T(8,128)(2,1)}, u32[]{:S(2)}, u32[]{:S(2)}) collective-permute-start(bf16[256,1024]{1,0:T(8,128)(2,1)S(1)} %add_convert_fusion.7.refs_4_), channel_id=1, source_target_pairs={{0,2},{7,5},{8,10},{15,13},{16,18},{23,21},{24,26},{31,29}} | collective-permute-start | bytes 1572872 | tf_op jit(solution)/shard_map/ppermute | solution.py:169
  158.1 13.4 %collective-permute-start.27 = (bf16[256,1024]{1,0:T(8,128)(2,1)S(1)}, bf16[256,1024]{1,0:T(8,128)(2,1)S(1)}, u32[]{:S(2)}, u32[]{:S(2)}) collective-permute-start(bf16[256,1024]{1,0:T(8,128)(2,1)S(1)} %copy-done.15), channel_id=1, source_target_pairs={{0,1},{1,0},{2,3},{3,2},{4,5},{5,4},{6,7},{7,6},{8,9},{9,8},{10,11... | collective-permute-start | bytes 1572872 | tf_op jit(solution)/shard_map/ppermute | solution.py:166
  158.2 17.4 %collective-permute-start.34 = (bf16[256,1024]{1,0:T(8,128)(2,1)S(1)}, bf16[256,1024]{1,0:T(8,128)(2,1)S(1)}, u32[]{:S(2)}, u32[]{:S(2)}) collective-permute-start(bf16[256,1024]{1,0:T(8,128)(2,1)S(1)} %copy-done.14), channel_id=1, source_target_pairs={{0,1},{1,0},{2,3},{3,2},{4,5},{5,4},{6,7},{7,6},{8,9},{9,8},{10,11... | collective-permute-start | bytes 1572872 | tf_op jit(solution)/shard_map/ppermute | solution.py:166
  160.2 11.3 %collective-permute-start.31 = (bf16[256,1024]{1,0:T(8,128)(2,1)S(1)}, bf16[256,1024]{1,0:T(8,128)(2,1)S(1)}, u32[]{:S(2)}, u32[]{:S(2)}) collective-permute-start(bf16[256,1024]{1,0:T(8,128)(2,1)S(1)} %add_convert_fusion.9), channel_id=1, source_target_pairs={{0,2},{2,4},{5,3},{7,5},{8,10},{10,12},{13,11},{15,13},{16,18},{18... | collective-permute-start | bytes 1572872 | tf_op jit(solution)/shard_map/ppermute | solution.py:169
  165.7 10.8 %collective-permute-start.38 = (bf16[256,1024]{1,0:T(8,128)(2,1)S(1)}, bf16[256,1024]{1,0:T(8,128)(2,1)S(1)}, u32[]{:S(2)}, u32[]{:S(2)}) collective-permute-start(bf16[256,1024]{1,0:T(8,128)(2,1)S(1)} %add_convert_fusion.6), channel_id=1, source_target_pairs={{0,2},{2,4},{5,3},{7,5},{8,10},{10,12},{13,11},{15,13},{16,18},{18... | collective-permute-start | bytes 1572872 | tf_op jit(solution)/shard_map/ppermute | solution.py:169
  171.7 10.5 %collective-permute-start.32 = (bf16[256,1024]{1,0:T(8,128)(2,1)S(1)}, bf16[256,1024]{1,0:T(8,128)(2,1)S(1)}, u32[]{:S(2)}, u32[]{:S(2)}) collective-permute-start(bf16[256,1024]{1,0:T(8,128)(2,1)S(1)} %add_convert_fusion.8), channel_id=1, source_target_pairs={{0,2},{2,4},{3,1},{4,6},{5,3},{7,5},{8,10},{10,12},{11,9},{12,14},... | collective-permute-start | bytes 1572872 | tf_op jit(solution)/shard_map/ppermute | solution.py:169
  176.8 11.1 %collective-permute-start.39 = (bf16[256,1024]{1,0:T(8,128)(2,1)S(1)}, bf16[256,1024]{1,0:T(8,128)(2,1)S(1)}, u32[]{:S(2)}, u32[]{:S(2)}) collective-permute-start(bf16[256,1024]{1,0:T(8,128)(2,1)S(1)} %add_convert_fusion.5), channel_id=1, source_target_pairs={{0,2},{2,4},{3,1},{4,6},{5,3},{7,5},{8,10},{10,12},{11,9},{12,14},... | collective-permute-start | bytes 1572872 | tf_op jit(solution)/shard_map/ppermute | solution.py:169
  181.3 7.5 %collective-permute-start.42 = (bf16[512,512]{1,0:T(8,128)(2,1)S(1)}, bf16[512,512]{1,0:T(8,128)(2,1)S(1)}, u32[]{:S(2)}, u32[]{:S(2)}) collective-permute-start(bf16[512,512]{1,0:T(8,128)(2,1)S(1)} %select_convert_fusion), channel_id=1, source_target_pairs={{0,1},{1,0},{2,3},{3,2},{4,5},{5,4},{6,7},{7,6},{8,9},{9,8},{10,11... | collective-permute-start | bytes 1572872 | tf_op jit(solution)/shard_map/ppermute | solution.py:166
  183.2 7.2 %collective-permute-start.33 = (bf16[256,512]{1,0:T(8,128)(2,1)}, bf16[256,512]{1,0:T(8,128)(2,1)S(1)}, u32[]{:S(2)}, u32[]{:S(2)}) collective-permute-start(bf16[256,512]{1,0:T(8,128)(2,1)} %select_convert_fusion.2), channel_id=1, source_target_pairs={{0,1},{1,0},{2,3},{3,2},{4,5},{5,4},{6,7},{7,6},{8,9},{9,8},{10,11... | collective-permute-start | bytes 786440 | tf_op jit(solution)/shard_map/ppermute | solution.py:166
  188.8 1.9 collective-permute-start.40
  (17 other events, 86.7 us)

commit v13 on v12

--- a/solution.py
+++ b/solution.py
@@ -247,7 +247,7 @@
 
     joined = join_cores(order, second_own, second_partner, 1, (last[0],))
     ahead = gather(joined)
-    normed = in_places(order, tokens[0], norm_gain, chips, (*others[-1], *others[-2]))
+    normed = in_places(order, tokens[0], norm_gain, chips, (*others[-1],*others[-2]))
     values = jnp.concatenate(
         [
             jnp.dot(normed, part, preferred_element_type=f32).astype(bf16)
@@ -261,13 +261,13 @@
     first = Gradient(values, cotangent, (pieces[2][0],))
     sent = [first.reduce(step) for step in range(1, chips)]
 
-    weight = assemble(pieces, others)[0]
+    weight = assemble(pieces, others, (sent[1],))[0]
     mid = jnp.dot(cotangent, weight, preferred_element_type=f32).astype(bf16)
-    mid = fence(order, mid, after=(sent[-1],))[0]
+    mid = fence(order, mid, after=())[0]
     half = mid.shape[1] // HALVES
     second = []
     for j in range(HALVES):
-        late = () if j else ()
+        late = (sent[-1],) if j else ()
         second.append(Gradient(mid[:, j * half : (j + 1) * half], normed, (), late))
     for step in range(1, chips):
         sent = tuple(gradient.reduce(step) for gradient in second)

time: 194 us -> 204 us (1.052)
  waiting for transfers between devices: 29 us -> 37.6 us
  local copies, waits for them, and re-layouts: 9.98 us -> 17.4 us
  starting transfers between devices: 95.2 us -> 90.4 us
    ppermute x18, waiting for transfers between devices: 24.6 us -> 32.3 us  [move(): return lax.ppermute(value, 'fsdp', move_perm(chips, active))]
    unnamed x43 -> x55, local copies, waits for them, and re-layouts: 6.17 us -> 13.6 us
    convert_element_type x1, other arithmetic: 3.91 us -> 6.94 us  [nesterov(): (base_part.astype(jnp.float32) - 0.7 * (delta + 0.9 * momentum_next)).ast...]
    ppermute x18, starting transfers between devices: 54.2 us -> 51.4 us  [move(): return lax.ppermute(value, 'fsdp', move_perm(chips, active))]
    pallas_call x11 -> x12, Pallas kernels: 11.6 us -> 12.2 us  [__call__(): pl.pallas_call(ordered, grid_spec=pltpu.PrefetchScalarGridSpec(num_scalar...]
  transfers between devices with their start and end apart: 45 -> 45, of which waited for: 15 -> 13; matrix products, arithmetic and copies ran while one was open for 25% -> 23% of each run, Pallas kernels for 5% -> 5%
where the time goes in v13:
time: 204 us; the launch traced here: 203 us
  starting transfers between devices  90.4 us (44%)
  waiting for transfers between devices  37.6 us (18%)
  other arithmetic  24.7 us (12%)
  matrix products  18.7 us (9%)
  local copies, waits for them, and re-layouts  17.4 us (9%)
  Pallas kernels  12.2 us (6%)
    ppermute x18, starting transfers between devices, move(): return lax.ppermute(value, 'fsdp', move_perm(chips, active))  51.4 us
    ppermute x23, starting transfers between devices, swap(): return lax.ppermute(value, 'fsdp', [(i, i ^ 1) for i in range(devices)])  34.6 us
    ppermute x18, waiting for transfers between devices, move(): return lax.ppermute(value, 'fsdp', move_perm(chips, active))  32.3 us
    unnamed x55, local copies, waits for them, and re-layouts  13.6 us
    pallas_call x12, Pallas kernels, __call__(): pl.pallas_call(ordered, grid_spec=pltpu.PrefetchScalarGridSpec(num_scalar...  12.2 us
    dot_general x3, matrix products, __init__(): lax.dot_general(mid, x, (((0,), (0,)), ((), ())), preferred_element_type=...  9.53 us
    convert_element_type x9, other arithmetic, message(): return term.astype(bf16)  8.45 us
    convert_element_type x1, other arithmetic, nesterov(): (base_part.astype(jnp.float32) - 0.7 * (delta + 0.9 * momentum_next)).ast...  6.94 us
  transfers between devices with their start and end apart: 45, of which 13 were waited for; matrix products, arithmetic and copies ran while one was open for 23% of the time, Pallas kernels for 5%

profile of v13, /device:TPU:0, one launch (start us, length us, event | category | flops | bytes accessed | tf_op | source)
XLA Modules:
  0.0 202.6 jit_solution(2529479620004331886)
XLA Ops:
  2.0 1.6 collective-permute-done.refs_1_
  6.1 5.7 %collective-permute-start.8 = (bf16[1024,256]{1,0:T(8,128)(2,1)S(1)}, bf16[1024,256]{1,0:T(8,128)(2,1)}, u32[]{:S(2)}, u32[]{:S(2)}) collective-permute-start(bf16[1024,256]{1,0:T(8,128)(2,1)S(1)} %get-tuple-element.11), channel_id=1, source_target_pairs={{0,2},{2,4},{3,1},{4,6},{5,3},{7,5},{8,10},{10,12},{11,9},{12,14},... | collective-permute-start | bytes 1572872 | tf_op jit(solution)/shard_map/ppermute | solution.py:169
  11.8 3.5 %collective-permute-start.2 = (bf16[1024,256]{1,0:T(8,128)(2,1)S(1)}, bf16[1024,256]{1,0:T(8,128)(2,1)}, u32[]{:S(2)}, u32[]{:S(2)}) collective-permute-start(bf16[1024,256]{1,0:T(8,128)(2,1)S(1)} %get-tuple-element.10.refs_1_), channel_id=1, source_target_pairs={{0,2},{2,4},{3,1},{4,6},{5,3},{7,5},{8,10},{10,12},{11,9},{12,14},... | collective-permute-start | bytes 1572872 | tf_op jit(solution)/shard_map/ppermute | solution.py:169
  15.2 2.4 %collective-permute-done.8 = bf16[1024,256]{1,0:T(8,128)(2,1)} collective-permute-done((bf16[1024,256]{1,0:T(8,128)(2,1)S(1)}, bf16[1024,256]{1,0:T(8,128)(2,1)}, u32[]{:S(2)}, u32[]{:S(2)}) %collective-permute-start.8) | collective-permute-done | bytes 524320 | tf_op jit(solution)/shard_map/ppermute | solution.py:169
  17.6 1.5 collective-permute-start.9
  19.1 4.2 %collective-permute-done.2 = bf16[1024,256]{1,0:T(8,128)(2,1)} collective-permute-done((bf16[1024,256]{1,0:T(8,128)(2,1)S(1)}, bf16[1024,256]{1,0:T(8,128)(2,1)}, u32[]{:S(2)}, u32[]{:S(2)}) %collective-permute-start.2) | collective-permute-done | bytes 524320 | tf_op jit(solution)/shard_map/ppermute | solution.py:169
  23.9 4.8 %collective-permute-start.12 = (bf16[1024,256]{1,0:T(8,128)(2,1)}, bf16[1024,256]{1,0:T(8,128)(2,1)S(1)}, u32[]{:S(2)}, u32[]{:S(2)}) collective-permute-start(bf16[1024,256]{1,0:T(8,128)(2,1)} %collective-permute-done.9.refs_2_), channel_id=1, source_target_pairs={{0,1},{1,0},{2,3},{3,2},{4,5},{5,4},{6,7},{7,6},{8,9},{9,8},{10,11... | collective-permute-start | bytes 1572872 | tf_op jit(solution)/shard_map/ppermute | solution.py:166
  29.3 5.4 %collective-permute-start.6 = (bf16[1024,256]{1,0:T(8,128)(2,1)S(1)}, bf16[1024,256]{1,0:T(8,128)(2,1)S(1)}, u32[]{:S(2)}, u32[]{:S(2)}) collective-permute-start(bf16[1024,256]{1,0:T(8,128)(2,1)S(1)} %collective-permute-done.3), channel_id=1, source_target_pairs={{0,1},{1,0},{2,3},{3,2},{4,5},{5,4},{6,7},{7,6},{8,9},{9,8},{10,11... | collective-permute-start | bytes 1572872 | tf_op jit(solution)/shard_map/ppermute | solution.py:166
  35.4 3.8 %fusion = (bf16[4096,128]{1,0:T(8,128)(2,1)S(1)}, bf16[4096,128]{1,0:T(8,128)(2,1)S(1)}) fusion(f32[4096]{0:T(1024)S(1)} %bitcast.54, bf16[1,8192,128]{2,1,0:T(8,128)(2,1)} %param.16, f32[4096]{0:T(1024)S(1)} %bitcast.55), kind=kLoop, calls=%fused_computation.10 | loop fusion | flops 3145728 | bytes 4227072 | tf_op jit(solution)/shard_map/convert_element_type | solution.py:240
  39.3 1.6 collective-permute-start.21
  42.3 1.6 collective-permute-start.20
  44.0 3.7 %collective-permute-start.14 = (bf16[1024,512]{1,0:T(8,128)(2,1)S(1)}, bf16[1024,512]{1,0:T(8,128)(2,1)S(1)}, u32[]{:S(2)}, u32[]{:S(2)}) collective-permute-start(bf16[1024,512]{1,0:T(8,128)(2,1)S(1)} %join_cores.3.refs_2_), channel_id=1, source_target_pairs={{0,2},{2,4},{3,1},{4,6},{5,3},{7,5},{8,10},{10,12},{11,9},{12,14},... | collective-permute-start | bytes 3145736 | tf_op jit(solution)/shard_map/ppermute | solution.py:169
  47.7 9.6 %collective-permute-start.11 = (bf16[1024,256]{1,0:T(8,128)(2,1)S(1)}, bf16[1024,256]{1,0:T(8,128)(2,1)S(1)}, u32[]{:S(2)}, u32[]{:S(2)}) collective-permute-start(bf16[1024,256]{1,0:T(8,128)(2,1)S(1)} %collective-permute-done.10), channel_id=1, source_target_pairs={{0,1},{1,0},{2,3},{3,2},{4,5},{5,4},{6,7},{7,6},{8,9},{9,8},{10,11... | collective-permute-start | bytes 1572872 | tf_op jit(solution)/shard_map/ppermute | solution.py:166
  57.5 1.3 collective-permute-done.11.refs_4_
  59.6 5.3 %in_places.2.refs_2_ = bf16[1024,4096]{1,0:T(8,128)(2,1)S(1)} custom-call(s32[6]{0:T(128)S(1)} %stack.27.place_ref, bf16[1024,4096]{1,0:T(8,128)(2,1)S(1)} %bitcast.45, f32[1,4096]{1,0:T(1,128)S(1)} %bitcast.49, bf16[1024,512]{1,0:T(8,128)(2,1)S(1)} %join_cores.3.refs_2_, bf16[1024,256]{1,0:T(8,128)(2,1)S(1)} %collective-permute-done.5.refs_3_, ...), custom_call_target="tpu_custom_call" | custom-call | flops 5000000000 | bytes 1 | tf_op jit(solution)/shard_map/in_places/pallas_call | solution.py:39
  67.2 2.3 %convolution_convert_fusion.4 = bf16[1024,256]{1,0:T(8,128)(2,1)S(1)} fusion(bf16[1024,4096]{1,0:T(8,128)(2,1)S(1)} %in_places.2.refs_2_, bf16[4096,256]{1,0:T(8,128)(2,1)S(1)} %get-tuple-element.13), kind=kOutput, calls=%fused_computation.22 | convolution fusion | flops 2147745792 | bytes 11010048 | tf_op jit(solution)/shard_map/dot_general | solution.py:253
  70.2 2.3 %convolution_convert_fusion.5 = bf16[1024,256]{1,0:T(8,128)(2,1)S(1)} fusion(bf16[1024,4096]{1,0:T(8,128)(2,1)S(1)} %in_places.2.refs_2_, bf16[4096,256]{1,0:T(8,128)(2,1)S(1)} %get-tuple-element.12.refs_1_), kind=kOutput, calls=%fused_computation.23 | convolution fusion | flops 2147745792 | bytes 11010048 | tf_op jit(solution)/shard_map/dot_general | solution.py:253
  74.5 2.7 %copy-done.3 = bf16[1024,4096]{1,0:T(8,128)(2,1)} copy-done((bf16[1024,4096]{1,0:T(8,128)(2,1)}, bf16[1024,4096]{1,0:T(8,128)(2,1)S(1)}, u32[]{:S(2)}) %copy-start.3) | copy-done | bytes 8388632
  78.2 4.8 %convolution_convert_fusion.refs_0_ = bf16[512,4096]{1,0:T(8,128)(2,1)S(1)} fusion(bf16[1024,512]{1,0:T(8,128)(2,1)S(1)} %fence.10.refs_1_, bf16[1024,4096]{1,0:T(8,128)(2,1)S(1)} %in_places.3.refs_1_), kind=kOutput, calls=%fused_computation | convolution fusion | flops 4297064448 | bytes 13631488 | tf_op jit(solution)/shard_map/dot_general | solution.py:173
  84.0 1.9 fusion.8
  86.9 5.6 %collective-permute-start.23 = (bf16[512,1024]{1,0:T(8,128)(2,1)}, bf16[512,1024]{1,0:T(8,128)(2,1)}, u32[]{:S(2)}, u32[]{:S(2)}) collective-permute-start(bf16[512,1024]{1,0:T(8,128)(2,1)} %get-tuple-element.23), channel_id=1, source_target_pairs={{0,1},{1,0},{2,3},{3,2},{4,5},{5,4},{6,7},{7,6},{8,9},{9,8},{10,11... | collective-permute-start | bytes 3145736 | tf_op jit(solution)/shard_map/ppermute | solution.py:166
  93.4 1.8 add_convert_fusion
  96.4 1.9 add_convert_fusion.4
  98.3 6.7 %collective-permute-start.24 = (bf16[512,1024]{1,0:T(8,128)(2,1)S(1)}, bf16[512,1024]{1,0:T(8,128)(2,1)S(1)}, u32[]{:S(2)}, u32[]{:S(2)}) collective-permute-start(bf16[512,1024]{1,0:T(8,128)(2,1)S(1)} %add_convert_fusion.4), channel_id=1, source_target_pairs={{0,2},{7,5},{8,10},{15,13},{16,18},{23,21},{24,26},{31,29}} | collective-permute-start | bytes 3145736 | tf_op jit(solution)/shard_map/ppermute | solution.py:169
  105.0 5.5 %collective-permute-start.17 = (bf16[1024,512]{1,0:T(8,128)(2,1)S(1)}, bf16[1024,512]{1,0:T(8,128)(2,1)S(1)}, u32[]{:S(2)}, u32[]{:S(2)}) collective-permute-start(bf16[1024,512]{1,0:T(8,128)(2,1)S(1)} %collective-permute-done.16), channel_id=1, source_target_pairs={{0,1},{1,0},{2,3},{3,2},{4,5},{5,4},{6,7},{7,6},{8,9},{9,8},{10,11... | collective-permute-start | bytes 3145736 | tf_op jit(solution)/shard_map/ppermute | solution.py:166
  112.5 4.6 %collective-permute-done.24 = bf16[512,1024]{1,0:T(8,128)(2,1)S(1)} collective-permute-done((bf16[512,1024]{1,0:T(8,128)(2,1)S(1)}, bf16[512,1024]{1,0:T(8,128)(2,1)S(1)}, u32[]{:S(2)}, u32[]{:S(2)}) %collective-permute-start.24) | collective-permute-done | bytes 1048608 | tf_op jit(solution)/shard_map/ppermute | solution.py:169
  117.7 5.4 %collective-permute-start.36 = (bf16[512,1024]{1,0:T(8,128)(2,1)S(1)}, bf16[512,1024]{1,0:T(8,128)(2,1)}, u32[]{:S(2)}, u32[]{:S(2)}) collective-permute-start(bf16[512,1024]{1,0:T(8,128)(2,1)S(1)} %add_convert_fusion.3.refs_2_), channel_id=1, source_target_pairs={{0,2},{2,4},{5,3},{7,5},{8,10},{10,12},{13,11},{15,13},{16,18},{18... | collective-permute-start | bytes 3145736 | tf_op jit(solution)/shard_map/ppermute | solution.py:169
  125.5 1.4 slice-done.3
  126.8 4.5 %convolution_convert_fusion.3.refs_0_ = bf16[1024,512]{1,0:T(8,128)(2,1)S(1)} fusion(bf16[1024,4096]{1,0:T(8,128)(2,1)S(1)} %bitcast.42, bf16[4096,512]{1,0:T(8,128)(2,1)S(1)} %fence.12.refs_1_), kind=kOutput, calls=%fused_computation.21 | convolution fusion | flops 4295491584 | bytes 13631488 | tf_op jit(solution)/shard_map/dot_general | solution.py:265
  131.9 2.4 %convolution_convert_fusion.2 = bf16[256,4096]{1,0:T(8,128)(2,1)S(1)} fusion(bf16[1024,4096]{1,0:T(8,128)(2,1)S(1)} %bitcast.40, bf16[1024,512]{1,0:T(8,128)(2,1)S(1)} %fence.13.refs_1_), kind=kOutput, calls=%fused_computation.2 | convolution fusion | flops 2148532224 | bytes 11010048 | tf_op jit(solution)/shard_map/dot_general | solution.py:173
  135.2 2.4 %convolution_convert_fusion.1 = bf16[256,4096]{1,0:T(8,128)(2,1)S(1)} fusion(bf16[1024,4096]{1,0:T(8,128)(2,1)S(1)} %bitcast.40, bf16[1024,512]{1,0:T(8,128)(2,1)S(1)} %fence.13.refs_1_), kind=kOutput, calls=%fused_computation.1 | convolution fusion | flops 2148532224 | bytes 11010048 | tf_op jit(solution)/shard_map/dot_general | solution.py:173
  139.3 1.3 collective-permute-start.28
  140.6 2.2 %add_convert_fusion.2.refs_2_ = bf16[512,1024]{1,0:T(8,128)(2,1)S(1)} fusion(bf16[512,1024]{1,0:T(8,128)(2,1)} %collective-permute-done.36, bf16[512,1024]{1,0:T(8,128)(2,1)} %collective-permute-done.35, bf16[512,4096]{1,0:T(8,128)(2,1)S(1)} %copy-done.2), kind=kLoop, calls=%fused_computation.18 | loop fusion | flops 3145728 | bytes 4194304 | tf_op jit(solution)/shard_map/convert_element_type | solution.py:189
  144.2 3.1 %collective-permute-done.28 = bf16[256,1024]{1,0:T(8,128)(2,1)S(1)} collective-permute-done((bf16[256,1024]{1,0:T(8,128)(2,1)S(1)}, bf16[256,1024]{1,0:T(8,128)(2,1)S(1)}, u32[]{:S(2)}, u32[]{:S(2)}) %collective-permute-start.28) | collective-permute-done | bytes 524320 | tf_op jit(solution)/shard_map/ppermute | solution.py:169
  147.3 4.4 %collective-permute-start.41 = (bf16[512,1024]{1,0:T(8,128)(2,1)S(1)}, bf16[512,1024]{1,0:T(8,128)(2,1)S(1)}, u32[]{:S(2)}, u32[]{:S(2)}) collective-permute-start(bf16[512,1024]{1,0:T(8,128)(2,1)S(1)} %add_convert_fusion.2.refs_2_), channel_id=1, source_target_pairs={{0,2},{2,4},{3,1},{4,6},{5,3},{7,5},{8,10},{10,12},{11,9},{12,14},... | collective-permute-start | bytes 3145736 | tf_op jit(solution)/shard_map/ppermute | solution.py:169
  152.0 2.7 %collective-permute-start.29 = (bf16[256,1024]{1,0:T(8,128)(2,1)S(1)}, bf16[256,1024]{1,0:T(8,128)(2,1)}, u32[]{:S(2)}, u32[]{:S(2)}) collective-permute-start(bf16[256,1024]{1,0:T(8,128)(2,1)S(1)} %add_convert_fusion.9), channel_id=1, source_target_pairs={{0,2},{2,4},{5,3},{7,5},{8,10},{10,12},{13,11},{15,13},{16,18},{18... | collective-permute-start | bytes 1572872 | tf_op jit(solution)/shard_map/ppermute | solution.py:169
  154.7 2.1 %collective-permute-start.37 = (bf16[256,1024]{1,0:T(8,128)(2,1)S(1)}, bf16[256,1024]{1,0:T(8,128)(2,1)}, u32[]{:S(2)}, u32[]{:S(2)}) collective-permute-start(bf16[256,1024]{1,0:T(8,128)(2,1)S(1)} %add_convert_fusion.7.refs_4_), channel_id=1, source_target_pairs={{0,2},{7,5},{8,10},{15,13},{16,18},{23,21},{24,26},{31,29}} | collective-permute-start | bytes 1572872 | tf_op jit(solution)/shard_map/ppermute | solution.py:169
  157.7 6.9 %subtract_convert_fusion = (bf16[8192,128]{1,0:T(8,128)(2,1)}, f32[8192,128]{1,0:T(8,128)}) fusion(bf16[8192,128]{1,0:T(8,128)(2,1)} %param.14, f32[4096,128]{1,0:T(8,128)S(1)} %get-tuple-element.35, f32[4096,128]{1,0:T(8,128)S(1)} %get-tuple-element.36, f32[8192,128]{1,0:T(8,128)} %param.15), kind=kLoop, calls=%fused_computation.5 | loop fusion | flops 10485760 | bytes 16777216 | tf_op jit(solution)/shard_map/convert_element_type | solution.py:135
  164.7 10.5 %collective-permute-done.37 = bf16[256,1024]{1,0:T(8,128)(2,1)} collective-permute-done((bf16[256,1024]{1,0:T(8,128)(2,1)S(1)}, bf16[256,1024]{1,0:T(8,128)(2,1)}, u32[]{:S(2)}, u32[]{:S(2)}) %collective-permute-start.37) | collective-permute-done | bytes 524320 | tf_op jit(solution)/shard_map/ppermute | solution.py:169
  175.2 1.5 add_convert_fusion.6
  176.7 4.5 %collective-permute-start.38 = (bf16[256,1024]{1,0:T(8,128)(2,1)S(1)}, bf16[256,1024]{1,0:T(8,128)(2,1)S(1)}, u32[]{:S(2)}, u32[]{:S(2)}) collective-permute-start(bf16[256,1024]{1,0:T(8,128)(2,1)S(1)} %add_convert_fusion.6), channel_id=1, source_target_pairs={{0,2},{2,4},{5,3},{7,5},{8,10},{10,12},{13,11},{15,13},{16,18},{18... | collective-permute-start | bytes 1572872 | tf_op jit(solution)/shard_map/ppermute | solution.py:169
  181.2 1.3 add_convert_fusion.8
  182.5 1.9 collective-permute-start.30
  184.9 2.9 %collective-permute-done.38 = bf16[256,1024]{1,0:T(8,128)(2,1)S(1)} collective-permute-done((bf16[256,1024]{1,0:T(8,128)(2,1)S(1)}, bf16[256,1024]{1,0:T(8,128)(2,1)S(1)}, u32[]{:S(2)}, u32[]{:S(2)}) %collective-permute-start.38) | collective-permute-done | bytes 524320 | tf_op jit(solution)/shard_map/ppermute | solution.py:169
  188.1 4.4 %collective-permute-start.39 = (bf16[256,1024]{1,0:T(8,128)(2,1)S(1)}, bf16[256,1024]{1,0:T(8,128)(2,1)S(1)}, u32[]{:S(2)}, u32[]{:S(2)}) collective-permute-start(bf16[256,1024]{1,0:T(8,128)(2,1)S(1)} %add_convert_fusion.5), channel_id=1, source_target_pairs={{0,2},{2,4},{3,1},{4,6},{5,3},{7,5},{8,10},{10,12},{11,9},{12,14},... | collective-permute-start | bytes 1572872 | tf_op jit(solution)/shard_map/ppermute | solution.py:169
  195.4 3.8 %collective-permute-done.39 = bf16[256,1024]{1,0:T(8,128)(2,1)S(1)} collective-permute-done((bf16[256,1024]{1,0:T(8,128)(2,1)S(1)}, bf16[256,1024]{1,0:T(8,128)(2,1)S(1)}, u32[]{:S(2)}, u32[]{:S(2)}) %collective-permute-start.39) | collective-permute-done | bytes 524320 | tf_op jit(solution)/shard_map/ppermute | solution.py:169
  199.8 1.3 copy.26
  201.3 1.3 copy.25
  (161 shorter events, 32.9 us)
Async XLA Ops:
  1.4 2.2 %collective-permute-start = (bf16[512,512]{1,0:T(8,128)(2,1)}, bf16[512,512]{1,0:T(8,128)(2,1)S(1)}, u32[]{:S(2)}, u32[]{:S(2)}) collective-permute-start(bf16[512,512]{1,0:T(8,128)(2,1)} %bitcast.50), channel_id=1, source_target_pairs={{0,1},{1,0},{2,3},{3,2},{4,5},{5,4},{6,7},{7,6},{8,9},{9,8},{10,11... | collective-permute-start | bytes 1572872 | tf_op jit(solution)/shard_map/ppermute | solution.py:166
  1.8 2.5 %collective-permute-start.1 = (bf16[512,512]{1,0:T(8,128)(2,1)}, bf16[512,512]{1,0:T(8,128)(2,1)S(1)}, u32[]{:S(2)}, u32[]{:S(2)}) collective-permute-start(bf16[512,512]{1,0:T(8,128)(2,1)} %bitcast.52), channel_id=1, source_target_pairs={{0,1},{1,0},{2,3},{3,2},{4,5},{5,4},{6,7},{7,6},{8,9},{9,8},{10,11... | collective-permute-start | bytes 1572872 | tf_op jit(solution)/shard_map/ppermute | solution.py:166
  6.1 33.1 %copy-start.7 = (bf16[1024,256]{1,0:T(8,128)(2,1)}, bf16[1024,256]{1,0:T(8,128)(2,1)S(1)}, u32[]{:S(2)}) copy-start(bf16[1024,256]{1,0:T(8,128)(2,1)S(1)} %get-tuple-element.10.refs_1_) | copy-start | bytes 1572868
  6.1 11.5 %collective-permute-start.8 = (bf16[1024,256]{1,0:T(8,128)(2,1)S(1)}, bf16[1024,256]{1,0:T(8,128)(2,1)}, u32[]{:S(2)}, u32[]{:S(2)}) collective-permute-start(bf16[1024,256]{1,0:T(8,128)(2,1)S(1)} %get-tuple-element.11), channel_id=1, source_target_pairs={{0,2},{2,4},{3,1},{4,6},{5,3},{7,5},{8,10},{10,12},{11,9},{12,14},... | collective-permute-start | bytes 1572872 | tf_op jit(solution)/shard_map/ppermute | solution.py:169
  11.8 11.5 %collective-permute-start.2 = (bf16[1024,256]{1,0:T(8,128)(2,1)S(1)}, bf16[1024,256]{1,0:T(8,128)(2,1)}, u32[]{:S(2)}, u32[]{:S(2)}) collective-permute-start(bf16[1024,256]{1,0:T(8,128)(2,1)S(1)} %get-tuple-element.10.refs_1_), channel_id=1, source_target_pairs={{0,2},{2,4},{3,1},{4,6},{5,3},{7,5},{8,10},{10,12},{11,9},{12,14},... | collective-permute-start | bytes 1572872 | tf_op jit(solution)/shard_map/ppermute | solution.py:169
  17.6 6.3 %collective-permute-start.9 = (bf16[1024,256]{1,0:T(8,128)(2,1)}, bf16[1024,256]{1,0:T(8,128)(2,1)}, u32[]{:S(2)}, u32[]{:S(2)}) collective-permute-start(bf16[1024,256]{1,0:T(8,128)(2,1)} %collective-permute-done.8), channel_id=1, source_target_pairs={{2,4},{3,1},{4,6},{5,3},{10,12},{11,9},{12,14},{13,11},{18,20},{19... | collective-permute-start | bytes 1572872 | tf_op jit(solution)/shard_map/ppermute | solution.py:169
  19.1 24.9 %collective-permute-start.13 = (bf16[1024,256]{1,0:T(8,128)(2,1)}, bf16[1024,256]{1,0:T(8,128)(2,1)S(1)}, u32[]{:S(2)}, u32[]{:S(2)}) collective-permute-start(bf16[1024,256]{1,0:T(8,128)(2,1)} %collective-permute-done.8), channel_id=1, source_target_pairs={{0,1},{1,0},{2,3},{3,2},{4,5},{5,4},{6,7},{7,6},{8,9},{9,8},{10,11... | collective-permute-start | bytes 1572872 | tf_op jit(solution)/shard_map/ppermute | solution.py:166
  23.2 34.1 %collective-permute-start.7 = (bf16[1024,256]{1,0:T(8,128)(2,1)}, bf16[1024,256]{1,0:T(8,128)(2,1)S(1)}, u32[]{:S(2)}, u32[]{:S(2)}) collective-permute-start(bf16[1024,256]{1,0:T(8,128)(2,1)} %collective-permute-done.2), channel_id=1, source_target_pairs={{0,1},{1,0},{2,3},{3,2},{4,5},{5,4},{6,7},{7,6},{8,9},{9,8},{10,11... | collective-permute-start | bytes 1572872 | tf_op jit(solution)/shard_map/ppermute | solution.py:166
  23.2 6.1 %collective-permute-start.3 = (bf16[1024,256]{1,0:T(8,128)(2,1)}, bf16[1024,256]{1,0:T(8,128)(2,1)S(1)}, u32[]{:S(2)}, u32[]{:S(2)}) collective-permute-start(bf16[1024,256]{1,0:T(8,128)(2,1)} %collective-permute-done.2), channel_id=1, source_target_pairs={{2,4},{3,1},{4,6},{5,3},{10,12},{11,9},{12,14},{13,11},{18,20},{19... | collective-permute-start | bytes 1572872 | tf_op jit(solution)/shard_map/ppermute | solution.py:169
  23.9 17.6 %collective-permute-start.12 = (bf16[1024,256]{1,0:T(8,128)(2,1)}, bf16[1024,256]{1,0:T(8,128)(2,1)S(1)}, u32[]{:S(2)}, u32[]{:S(2)}) collective-permute-start(bf16[1024,256]{1,0:T(8,128)(2,1)} %collective-permute-done.9.refs_2_), channel_id=1, source_target_pairs={{0,1},{1,0},{2,3},{3,2},{4,5},{5,4},{6,7},{7,6},{8,9},{9,8},{10,11... | collective-permute-start | bytes 1572872 | tf_op jit(solution)/shard_map/ppermute | solution.py:166
  29.3 13.0 %collective-permute-start.6 = (bf16[1024,256]{1,0:T(8,128)(2,1)S(1)}, bf16[1024,256]{1,0:T(8,128)(2,1)S(1)}, u32[]{:S(2)}, u32[]{:S(2)}) collective-permute-start(bf16[1024,256]{1,0:T(8,128)(2,1)S(1)} %collective-permute-done.3), channel_id=1, source_target_pairs={{0,1},{1,0},{2,3},{3,2},{4,5},{5,4},{6,7},{7,6},{8,9},{9,8},{10,11... | collective-permute-start | bytes 1572872 | tf_op jit(solution)/shard_map/ppermute | solution.py:166
  34.7 4.5 %collective-permute-start.4 = (bf16[1024,256]{1,0:T(8,128)(2,1)S(1)}, bf16[1024,256]{1,0:T(8,128)(2,1)S(1)}, u32[]{:S(2)}, u32[]{:S(2)}) collective-permute-start(bf16[1024,256]{1,0:T(8,128)(2,1)S(1)} %collective-permute-done.3), channel_id=1, source_target_pairs={{3,1},{4,6},{11,9},{12,14},{19,17},{20,22},{27,25},{28,30}} | collective-permute-start | bytes 1572872 | tf_op jit(solution)/shard_map/ppermute | solution.py:169
  35.4 24.1 %slice-start.4 = ((s8[8388608]{0:T(1024)(128)(4,1)}), s8[4194304]{0:T(1024)(128)(4,1)S(1)}, s32[]{:S(2)}) async-start(s8[8388608]{0:T(1024)(128)(4,1)} %bitcast.43), calls=%async_computation.4 | async-start | bytes 8388608
  39.2 25.7 %copy-start.16 = (bf16[4096,128]{1,0:T(8,128)(2,1)}, bf16[4096,128]{1,0:T(8,128)(2,1)S(1)}, u32[]{:S(2)}) copy-start(bf16[4096,128]{1,0:T(8,128)(2,1)S(1)} %get-tuple-element.31) | copy-start | bytes 3145732
  39.3 34.7 %collective-permute-start.21 = (bf16[4096,128]{1,0:T(8,128)(2,1)S(1)}, bf16[4096,128]{1,0:T(8,128)(2,1)S(1)}, u32[]{:S(2)}, u32[]{:S(2)}) collective-permute-start(bf16[4096,128]{1,0:T(8,128)(2,1)S(1)} %get-tuple-element.31), channel_id=1, source_target_pairs={{0,16},{8,24},{16,0},{24,8},{1,17},{9,25},{17,1},{25,9},{2,18},{10... | collective-permute-start | bytes 3145736 | tf_op jit(solution)/shard_map/ppermute | solution.py:242
  41.5 6.2 %collective-permute-start.10 = (bf16[1024,256]{1,0:T(8,128)(2,1)}, bf16[1024,256]{1,0:T(8,128)(2,1)S(1)}, u32[]{:S(2)}, u32[]{:S(2)}) collective-permute-start(bf16[1024,256]{1,0:T(8,128)(2,1)} %collective-permute-done.9.refs_2_), channel_id=1, source_target_pairs={{3,1},{4,6},{11,9},{12,14},{19,17},{20,22},{27,25},{28,30}} | collective-permute-start | bytes 1572872 | tf_op jit(solution)/shard_map/ppermute | solution.py:169
  42.3 31.6 %collective-permute-start.20 = (bf16[4096,128]{1,0:T(8,128)(2,1)S(1)}, bf16[4096,128]{1,0:T(8,128)(2,1)S(1)}, u32[]{:S(2)}, u32[]{:S(2)}) collective-permute-start(bf16[4096,128]{1,0:T(8,128)(2,1)S(1)} %get-tuple-element.32), channel_id=1, source_target_pairs={{0,8},{8,0},{16,24},{24,16},{1,9},{9,1},{17,25},{25,17},{2,10},{10... | collective-permute-start | bytes 3145736 | tf_op jit(solution)/shard_map/ppermute | solution.py:242
  44.0 22.6 %collective-permute-start.14 = (bf16[1024,512]{1,0:T(8,128)(2,1)S(1)}, bf16[1024,512]{1,0:T(8,128)(2,1)S(1)}, u32[]{:S(2)}, u32[]{:S(2)}) collective-permute-start(bf16[1024,512]{1,0:T(8,128)(2,1)S(1)} %join_cores.3.refs_2_), channel_id=1, source_target_pairs={{0,2},{2,4},{3,1},{4,6},{5,3},{7,5},{8,10},{10,12},{11,9},{12,14},... | collective-permute-start | bytes 3145736 | tf_op jit(solution)/shard_map/ppermute | solution.py:169
  47.7 11.1 %collective-permute-start.11 = (bf16[1024,256]{1,0:T(8,128)(2,1)S(1)}, bf16[1024,256]{1,0:T(8,128)(2,1)S(1)}, u32[]{:S(2)}, u32[]{:S(2)}) collective-permute-start(bf16[1024,256]{1,0:T(8,128)(2,1)S(1)} %collective-permute-done.10), channel_id=1, source_target_pairs={{0,1},{1,0},{2,3},{3,2},{4,5},{5,4},{6,7},{7,6},{8,9},{9,8},{10,11... | collective-permute-start | bytes 1572872 | tf_op jit(solution)/shard_map/ppermute | solution.py:166
  57.3 2.2 %collective-permute-start.5 = (bf16[1024,256]{1,0:T(8,128)(2,1)S(1)}, bf16[1024,256]{1,0:T(8,128)(2,1)S(1)}, u32[]{:S(2)}, u32[]{:S(2)}) collective-permute-start(bf16[1024,256]{1,0:T(8,128)(2,1)S(1)} %collective-permute-done.4.refs_3_), channel_id=1, source_target_pairs={{0,1},{1,0},{2,3},{3,2},{4,5},{5,4},{6,7},{7,6},{8,9},{9,8},{10,11... | collective-permute-start | bytes 1572872 | tf_op jit(solution)/shard_map/ppermute | solution.py:166
  69.5 13.5 %collective-permute-start.15 = (bf16[1024,512]{1,0:T(8,128)(2,1)S(1)}, bf16[1024,512]{1,0:T(8,128)(2,1)S(1)}, u32[]{:S(2)}, u32[]{:S(2)}) collective-permute-start(bf16[1024,512]{1,0:T(8,128)(2,1)S(1)} %collective-permute-done.14.refs_3_.refs_2_), channel_id=1, source_target_pairs={{2,4},{3,1},{4,6},{5,3},{10,12},{11,9},{12,14},{13,11},{18,20},{19... | collective-permute-start | bytes 3145736 | tf_op jit(solution)/shard_map/ppermute | solution.py:169
  86.9 9.5 %collective-permute-start.23 = (bf16[512,1024]{1,0:T(8,128)(2,1)}, bf16[512,1024]{1,0:T(8,128)(2,1)}, u32[]{:S(2)}, u32[]{:S(2)}) collective-permute-start(bf16[512,1024]{1,0:T(8,128)(2,1)} %get-tuple-element.23), channel_id=1, source_target_pairs={{0,1},{1,0},{2,3},{3,2},{4,5},{5,4},{6,7},{7,6},{8,9},{9,8},{10,11... | collective-permute-start | bytes 3145736 | tf_op jit(solution)/shard_map/ppermute | solution.py:166
  92.6 12.5 %collective-permute-start.16 = (bf16[1024,512]{1,0:T(8,128)(2,1)}, bf16[1024,512]{1,0:T(8,128)(2,1)S(1)}, u32[]{:S(2)}, u32[]{:S(2)}) collective-permute-start(bf16[1024,512]{1,0:T(8,128)(2,1)} %copy-done.5), channel_id=1, source_target_pairs={{3,1},{4,6},{11,9},{12,14},{19,17},{20,22},{27,25},{28,30}} | collective-permute-start | bytes 3145736 | tf_op jit(solution)/shard_map/ppermute | solution.py:169
  95.2 16.3 %collective-permute-start.19 = (bf16[1024,512]{1,0:T(8,128)(2,1)S(1)}, bf16[1024,512]{1,0:T(8,128)(2,1)S(1)}, u32[]{:S(2)}, u32[]{:S(2)}) collective-permute-start(bf16[1024,512]{1,0:T(8,128)(2,1)S(1)} %collective-permute-done.14.refs_3_.refs_2_), channel_id=1, source_target_pairs={{0,1},{1,0},{2,3},{3,2},{4,5},{5,4},{6,7},{7,6},{8,9},{9,8},{10,11... | collective-permute-start | bytes 3145736 | tf_op jit(solution)/shard_map/ppermute | solution.py:166
  95.9 16.5 %collective-permute-start.22 = (bf16[512,1024]{1,0:T(8,128)(2,1)S(1)}, bf16[512,1024]{1,0:T(8,128)(2,1)S(1)}, u32[]{:S(2)}, u32[]{:S(2)}) collective-permute-start(bf16[512,1024]{1,0:T(8,128)(2,1)S(1)} %copy-done.17), channel_id=1, source_target_pairs={{0,1},{1,0},{2,3},{3,2},{4,5},{5,4},{6,7},{7,6},{8,9},{9,8},{10,11... | collective-permute-start | bytes 3145736 | tf_op jit(solution)/shard_map/ppermute | solution.py:166
  96.0 14.9 %collective-permute-start.18 = (bf16[1024,512]{1,0:T(8,128)(2,1)S(1)}, bf16[1024,512]{1,0:T(8,128)(2,1)S(1)}, u32[]{:S(2)}, u32[]{:S(2)}) collective-permute-start(bf16[1024,512]{1,0:T(8,128)(2,1)S(1)} %copy-done.6), channel_id=1, source_target_pairs={{0,1},{1,0},{2,3},{3,2},{4,5},{5,4},{6,7},{7,6},{8,9},{9,8},{10,11... | collective-permute-start | bytes 3145736 | tf_op jit(solution)/shard_map/ppermute | solution.py:166
  98.3 18.7 %collective-permute-start.24 = (bf16[512,1024]{1,0:T(8,128)(2,1)S(1)}, bf16[512,1024]{1,0:T(8,128)(2,1)S(1)}, u32[]{:S(2)}, u32[]{:S(2)}) collective-permute-start(bf16[512,1024]{1,0:T(8,128)(2,1)S(1)} %add_convert_fusion.4), channel_id=1, source_target_pairs={{0,2},{7,5},{8,10},{15,13},{16,18},{23,21},{24,26},{31,29}} | collective-permute-start | bytes 3145736 | tf_op jit(solution)/shard_map/ppermute | solution.py:169
  105.0 18.1 %collective-permute-start.17 = (bf16[1024,512]{1,0:T(8,128)(2,1)S(1)}, bf16[1024,512]{1,0:T(8,128)(2,1)S(1)}, u32[]{:S(2)}, u32[]{:S(2)}) collective-permute-start(bf16[1024,512]{1,0:T(8,128)(2,1)S(1)} %collective-permute-done.16), channel_id=1, source_target_pairs={{0,1},{1,0},{2,3},{3,2},{4,5},{5,4},{6,7},{7,6},{8,9},{9,8},{10,11... | collective-permute-start | bytes 3145736 | tf_op jit(solution)/shard_map/ppermute | solution.py:166
  110.8 41.2 %collective-permute-start.44 = (bf16[4096,128]{1,0:T(8,128)(2,1)S(1)}, bf16[4096,128]{1,0:T(8,128)(2,1)S(1)}, u32[]{:S(2)}, u32[]{:S(2)}) collective-permute-start(bf16[4096,128]{1,0:T(8,128)(2,1)S(1)} %add_convert_fusion), channel_id=1, source_target_pairs={{0,8},{8,0},{16,24},{24,16},{1,9},{9,1},{17,25},{25,17},{2,10},{10... | collective-permute-start | bytes 3145736 | tf_op jit(solution)/shard_map/ppermute | solution.py:242
  111.6 43.1 %collective-permute-start.43 = (bf16[4096,128]{1,0:T(8,128)(2,1)S(1)}, bf16[4096,128]{1,0:T(8,128)(2,1)S(1)}, u32[]{:S(2)}, u32[]{:S(2)}) collective-permute-start(bf16[4096,128]{1,0:T(8,128)(2,1)S(1)} %add_convert_fusion.1), channel_id=1, source_target_pairs={{0,16},{8,24},{16,0},{24,8},{1,17},{9,25},{17,1},{25,9},{2,18},{10... | collective-permute-start | bytes 3145736 | tf_op jit(solution)/shard_map/ppermute | solution.py:242
  112.4 26.8 %collective-permute-start.35 = (bf16[512,1024]{1,0:T(8,128)(2,1)}, bf16[512,1024]{1,0:T(8,128)(2,1)}, u32[]{:S(2)}, u32[]{:S(2)}) collective-permute-start(bf16[512,1024]{1,0:T(8,128)(2,1)} %get-tuple-element.22), channel_id=1, source_target_pairs={{0,1},{1,0},{2,3},{3,2},{4,5},{5,4},{6,7},{7,6},{8,9},{9,8},{10,11... | collective-permute-start | bytes 3145736 | tf_op jit(solution)/shard_map/ppermute | solution.py:166
  117.7 21.5 %collective-permute-start.36 = (bf16[512,1024]{1,0:T(8,128)(2,1)S(1)}, bf16[512,1024]{1,0:T(8,128)(2,1)}, u32[]{:S(2)}, u32[]{:S(2)}) collective-permute-start(bf16[512,1024]{1,0:T(8,128)(2,1)S(1)} %add_convert_fusion.3.refs_2_), channel_id=1, source_target_pairs={{0,2},{2,4},{5,3},{7,5},{8,10},{10,12},{13,11},{15,13},{16,18},{18... | collective-permute-start | bytes 3145736 | tf_op jit(solution)/shard_map/ppermute | solution.py:169
  135.2 3.3 %collective-permute-start.27 = (bf16[256,1024]{1,0:T(8,128)(2,1)S(1)}, bf16[256,1024]{1,0:T(8,128)(2,1)S(1)}, u32[]{:S(2)}, u32[]{:S(2)}) collective-permute-start(bf16[256,1024]{1,0:T(8,128)(2,1)S(1)} %get-tuple-element.27), channel_id=1, source_target_pairs={{0,1},{1,0},{2,3},{3,2},{4,5},{5,4},{6,7},{7,6},{8,9},{9,8},{10,11... | collective-permute-start | bytes 1572872 | tf_op jit(solution)/shard_map/ppermute | solution.py:166
  138.5 4.3 %collective-permute-start.34 = (bf16[256,1024]{1,0:T(8,128)(2,1)S(1)}, bf16[256,1024]{1,0:T(8,128)(2,1)S(1)}, u32[]{:S(2)}, u32[]{:S(2)}) collective-permute-start(bf16[256,1024]{1,0:T(8,128)(2,1)S(1)} %get-tuple-element.30), channel_id=1, source_target_pairs={{0,1},{1,0},{2,3},{3,2},{4,5},{5,4},{6,7},{7,6},{8,9},{9,8},{10,11... | collective-permute-start | bytes 1572872 | tf_op jit(solution)/shard_map/ppermute | solution.py:166
  139.2 4.4 %collective-permute-start.26 = (bf16[256,1024]{1,0:T(8,128)(2,1)S(1)}, bf16[256,1024]{1,0:T(8,128)(2,1)S(1)}, u32[]{:S(2)}, u32[]{:S(2)}) collective-permute-start(bf16[256,1024]{1,0:T(8,128)(2,1)S(1)} %get-tuple-element.26), channel_id=1, source_target_pairs={{0,1},{1,0},{2,3},{3,2},{4,5},{5,4},{6,7},{7,6},{8,9},{9,8},{10,11... | collective-permute-start | bytes 1572872 | tf_op jit(solution)/shard_map/ppermute | solution.py:166
  139.3 8.0 %collective-permute-start.28 = (bf16[256,1024]{1,0:T(8,128)(2,1)S(1)}, bf16[256,1024]{1,0:T(8,128)(2,1)S(1)}, u32[]{:S(2)}, u32[]{:S(2)}) collective-permute-start(bf16[256,1024]{1,0:T(8,128)(2,1)S(1)} %add_convert_fusion.10.refs_3_), channel_id=1, source_target_pairs={{0,2},{7,5},{8,10},{15,13},{16,18},{23,21},{24,26},{31,29}} | collective-permute-start | bytes 1572872 | tf_op jit(solution)/shard_map/ppermute | solution.py:169
  142.8 38.4 %collective-permute-start.25 = (bf16[256,1024]{1,0:T(8,128)(2,1)}, bf16[256,1024]{1,0:T(8,128)(2,1)S(1)}, u32[]{:S(2)}, u32[]{:S(2)}) collective-permute-start(bf16[256,1024]{1,0:T(8,128)(2,1)} %get-tuple-element.25), channel_id=1, source_target_pairs={{0,1},{1,0},{2,3},{3,2},{4,5},{5,4},{6,7},{7,6},{8,9},{9,8},{10,11... | collective-permute-start | bytes 1572872 | tf_op jit(solution)/shard_map/ppermute | solution.py:166
  143.7 21.0 %collective-permute-start.33 = (bf16[256,1024]{1,0:T(8,128)(2,1)}, bf16[256,1024]{1,0:T(8,128)(2,1)}, u32[]{:S(2)}, u32[]{:S(2)}) collective-permute-start(bf16[256,1024]{1,0:T(8,128)(2,1)} %get-tuple-element.29), channel_id=1, source_target_pairs={{0,1},{1,0},{2,3},{3,2},{4,5},{5,4},{6,7},{7,6},{8,9},{9,8},{10,11... | collective-permute-start | bytes 1572872 | tf_op jit(solution)/shard_map/ppermute | solution.py:166
  147.3 37.2 %collective-permute-start.41 = (bf16[512,1024]{1,0:T(8,128)(2,1)S(1)}, bf16[512,1024]{1,0:T(8,128)(2,1)S(1)}, u32[]{:S(2)}, u32[]{:S(2)}) collective-permute-start(bf16[512,1024]{1,0:T(8,128)(2,1)S(1)} %add_convert_fusion.2.refs_2_), channel_id=1, source_target_pairs={{0,2},{2,4},{3,1},{4,6},{5,3},{7,5},{8,10},{10,12},{11,9},{12,14},... | collective-permute-start | bytes 3145736 | tf_op jit(solution)/shard_map/ppermute | solution.py:169
  152.0 29.2 %collective-permute-start.29 = (bf16[256,1024]{1,0:T(8,128)(2,1)S(1)}, bf16[256,1024]{1,0:T(8,128)(2,1)}, u32[]{:S(2)}, u32[]{:S(2)}) collective-permute-start(bf16[256,1024]{1,0:T(8,128)(2,1)S(1)} %add_convert_fusion.9), channel_id=1, source_target_pairs={{0,2},{2,4},{5,3},{7,5},{8,10},{10,12},{13,11},{15,13},{16,18},{18... | collective-permute-start | bytes 1572872 | tf_op jit(solution)/shard_map/ppermute | solution.py:169
  154.7 20.5 %collective-permute-start.37 = (bf16[256,1024]{1,0:T(8,128)(2,1)S(1)}, bf16[256,1024]{1,0:T(8,128)(2,1)}, u32[]{:S(2)}, u32[]{:S(2)}) collective-permute-start(bf16[256,1024]{1,0:T(8,128)(2,1)S(1)} %add_convert_fusion.7.refs_4_), channel_id=1, source_target_pairs={{0,2},{7,5},{8,10},{15,13},{16,18},{23,21},{24,26},{31,29}} | collective-permute-start | bytes 1572872 | tf_op jit(solution)/shard_map/ppermute | solution.py:169
  164.7 20.2 %collective-permute-start.32 = (bf16[256,1024]{1,0:T(8,128)(2,1)S(1)}, bf16[256,1024]{1,0:T(8,128)(2,1)S(1)}, u32[]{:S(2)}, u32[]{:S(2)}) collective-permute-start(bf16[256,1024]{1,0:T(8,128)(2,1)S(1)} %get-tuple-element.28), channel_id=1, source_target_pairs={{0,1},{1,0},{2,3},{3,2},{4,5},{5,4},{6,7},{7,6},{8,9},{9,8},{10,11... | collective-permute-start | bytes 1572872 | tf_op jit(solution)/shard_map/ppermute | solution.py:166
  176.7 11.2 %collective-permute-start.38 = (bf16[256,1024]{1,0:T(8,128)(2,1)S(1)}, bf16[256,1024]{1,0:T(8,128)(2,1)S(1)}, u32[]{:S(2)}, u32[]{:S(2)}) collective-permute-start(bf16[256,1024]{1,0:T(8,128)(2,1)S(1)} %add_convert_fusion.6), channel_id=1, source_target_pairs={{0,2},{2,4},{5,3},{7,5},{8,10},{10,12},{13,11},{15,13},{16,18},{18... | collective-permute-start | bytes 1572872 | tf_op jit(solution)/shard_map/ppermute | solution.py:169
  182.5 10.9 %collective-permute-start.30 = (bf16[256,1024]{1,0:T(8,128)(2,1)S(1)}, bf16[256,1024]{1,0:T(8,128)(2,1)S(1)}, u32[]{:S(2)}, u32[]{:S(2)}) collective-permute-start(bf16[256,1024]{1,0:T(8,128)(2,1)S(1)} %add_convert_fusion.8), channel_id=1, source_target_pairs={{0,2},{2,4},{3,1},{4,6},{5,3},{7,5},{8,10},{10,12},{11,9},{12,14},... | collective-permute-start | bytes 1572872 | tf_op jit(solution)/shard_map/ppermute | solution.py:169
  188.1 11.1 %collective-permute-start.39 = (bf16[256,1024]{1,0:T(8,128)(2,1)S(1)}, bf16[256,1024]{1,0:T(8,128)(2,1)S(1)}, u32[]{:S(2)}, u32[]{:S(2)}) collective-permute-start(bf16[256,1024]{1,0:T(8,128)(2,1)S(1)} %add_convert_fusion.5), channel_id=1, source_target_pairs={{0,2},{2,4},{3,1},{4,6},{5,3},{7,5},{8,10},{10,12},{11,9},{12,14},... | collective-permute-start | bytes 1572872 | tf_op jit(solution)/shard_map/ppermute | solution.py:169
  193.7 1.6 collective-permute-start.31
  193.9 5.6 %collective-permute-start.42 = (bf16[512,512]{1,0:T(8,128)(2,1)S(1)}, bf16[512,512]{1,0:T(8,128)(2,1)S(1)}, u32[]{:S(2)}, u32[]{:S(2)}) collective-permute-start(bf16[512,512]{1,0:T(8,128)(2,1)S(1)} %select_convert_fusion), channel_id=1, source_target_pairs={{0,1},{1,0},{2,3},{3,2},{4,5},{5,4},{6,7},{7,6},{8,9},{9,8},{10,11... | collective-permute-start | bytes 1572872 | tf_op jit(solution)/shard_map/ppermute | solution.py:166
  199.4 1.7 collective-permute-start.40
  (23 other events, 132.7 us)

commit v14 on v12

--- a/solution.py
+++ b/solution.py
@@ -169,15 +169,13 @@
         return lax.ppermute(value, "fsdp", move_perm(chips, active))
 
     class Gradient:
-        def __init__(self, mid, x, after=(), late=()):
+        def __init__(self, mid, x, after=()):
             terms = lax.dot_general(mid, x, (((0,), (0,)), ((), ())), preferred_element_type=f32)
             self.terms = terms.astype(bf16)
             if after:
                 self.terms = fence(order, self.terms, after=after)[0]
             self.across = [None] + [swap(self.block(chips - s)) for s in range(1, chips)]
             self.arrived = None
-            if late:
-                self.across[1] = fence(order, self.across[1], after=late)[0]
 
         def block(self, place):
             return self.terms[:, place * block : (place + 1) * block]
@@ -261,14 +259,14 @@
     first = Gradient(values, cotangent, (pieces[2][0],))
     sent = [first.reduce(step) for step in range(1, chips)]
 
-    weight = assemble(pieces, others)[0]
+    weight = assemble(pieces, others, ())[0]
     mid = jnp.dot(cotangent, weight, preferred_element_type=f32).astype(bf16)
     mid = fence(order, mid, after=(sent[-1],))[0]
     half = mid.shape[1] // HALVES
     second = []
     for j in range(HALVES):
-        late = () if j else ()
-        second.append(Gradient(mid[:, j * half : (j + 1) * half], normed, (), late))
+        after = (first.arrived,) if j else ()
+        second.append(Gradient(mid[:, j * half : (j + 1) * half], normed, after))
     for step in range(1, chips):
         sent = tuple(gradient.reduce(step) for gradient in second)
         if step == 1:

time: 194 us -> 197 us (1.015)
  local copies, waits for them, and re-layouts: 9.98 us -> 16.9 us
  starting transfers between devices: 95.2 us -> 90 us
  waiting for transfers between devices: 29 us -> 31.3 us
    unnamed x43 -> x65, local copies, waits for them, and re-layouts: 6.17 us -> 14.8 us
    ppermute x23, starting transfers between devices: 35.7 us -> 29.8 us  [swap(): return lax.ppermute(value, 'fsdp', [(i, i ^ 1) for i in range(devices)])]
    convert_element_type x9, other arithmetic: 9.2 us -> 4.66 us  [message(): return term.astype(bf16)]
    ppermute x18, waiting for transfers between devices: 24.6 us -> 27.4 us  [move(): return lax.ppermute(value, 'fsdp', move_perm(chips, active))]
    convert_element_type x3, other arithmetic: 4.65 us -> 6.83 us  [per_device(): mine = total.astype(bf16)]
    pallas_call x11 -> x12, Pallas kernels: 11.6 us -> 12.2 us  [__call__(): pl.pallas_call(ordered, grid_spec=pltpu.PrefetchScalarGridSpec(num_scalar...]
  transfers between devices with their start and end apart: 45 -> 45, of which waited for: 15 -> 15; matrix products, arithmetic and copies ran while one was open for 25% -> 23% of each run, Pallas kernels for 5% -> 6%
where the time goes in v14:
time: 197 us; the launch traced here: 196 us
  starting transfers between devices  90 us (46%)
  waiting for transfers between devices  31.3 us (16%)
  other arithmetic  24.7 us (13%)
  matrix products  19.2 us (10%)
  local copies, waits for them, and re-layouts  16.9 us (9%)
  Pallas kernels  12.2 us (6%)
    ppermute x18, starting transfers between devices, move(): return lax.ppermute(value, 'fsdp', move_perm(chips, active))  54.6 us
    ppermute x23, starting transfers between devices, swap(): return lax.ppermute(value, 'fsdp', [(i, i ^ 1) for i in range(devices)])  29.8 us
    ppermute x18, waiting for transfers between devices, move(): return lax.ppermute(value, 'fsdp', move_perm(chips, active))  27.4 us
    unnamed x65, local copies, waits for them, and re-layouts  14.8 us
    pallas_call x12, Pallas kernels, __call__(): pl.pallas_call(ordered, grid_spec=pltpu.PrefetchScalarGridSpec(num_scalar...  12.2 us
    dot_general x3, matrix products, __init__(): lax.dot_general(mid, x, (((0,), (0,)), ((), ())), preferred_element_type=...  10 us
    convert_element_type x3, other arithmetic, per_device(): mine = total.astype(bf16)  6.83 us
    ppermute x4, starting transfers between devices, per_device(): lax.ppermute(mine, 'replica', [(i, i ^ bit) for i in range(replicas)])  5.55 us
  transfers between devices with their start and end apart: 45, of which 15 were waited for; matrix products, arithmetic and copies ran while one was open for 23% of the time, Pallas kernels for 6%

profile of v14, /device:TPU:0, one launch (start us, length us, event | category | flops | bytes accessed | tf_op | source)
XLA Modules:
  0.0 195.9 jit_solution(18404038643966828800)
XLA Ops:
  2.0 1.6 collective-permute-done.1.refs_2_.refs_1_
  6.1 5.7 %collective-permute-start.8 = (bf16[1024,256]{1,0:T(8,128)(2,1)S(1)}, bf16[1024,256]{1,0:T(8,128)(2,1)}, u32[]{:S(2)}, u32[]{:S(2)}) collective-permute-start(bf16[1024,256]{1,0:T(8,128)(2,1)S(1)} %get-tuple-element.11), channel_id=1, source_target_pairs={{0,2},{2,4},{3,1},{4,6},{5,3},{7,5},{8,10},{10,12},{11,9},{12,14},... | collective-permute-start | bytes 1572872 | tf_op jit(solution)/shard_map/ppermute | solution.py:169
  11.8 3.5 %collective-permute-start.2 = (bf16[1024,256]{1,0:T(8,128)(2,1)S(1)}, bf16[1024,256]{1,0:T(8,128)(2,1)}, u32[]{:S(2)}, u32[]{:S(2)}) collective-permute-start(bf16[1024,256]{1,0:T(8,128)(2,1)S(1)} %get-tuple-element.10.refs_1_), channel_id=1, source_target_pairs={{0,2},{2,4},{3,1},{4,6},{5,3},{7,5},{8,10},{10,12},{11,9},{12,14},... | collective-permute-start | bytes 1572872 | tf_op jit(solution)/shard_map/ppermute | solution.py:169
  15.2 2.4 %collective-permute-done.8 = bf16[1024,256]{1,0:T(8,128)(2,1)} collective-permute-done((bf16[1024,256]{1,0:T(8,128)(2,1)S(1)}, bf16[1024,256]{1,0:T(8,128)(2,1)}, u32[]{:S(2)}, u32[]{:S(2)}) %collective-permute-start.8) | collective-permute-done | bytes 524320 | tf_op jit(solution)/shard_map/ppermute | solution.py:169
  17.6 1.5 collective-permute-start.9
  19.1 4.1 %collective-permute-done.2 = bf16[1024,256]{1,0:T(8,128)(2,1)} collective-permute-done((bf16[1024,256]{1,0:T(8,128)(2,1)S(1)}, bf16[1024,256]{1,0:T(8,128)(2,1)}, u32[]{:S(2)}, u32[]{:S(2)}) %collective-permute-start.2) | collective-permute-done | bytes 524320 | tf_op jit(solution)/shard_map/ppermute | solution.py:169
  26.5 3.8 %fusion = (bf16[4096,128]{1,0:T(8,128)(2,1)S(1)}, bf16[4096,128]{1,0:T(8,128)(2,1)S(1)}) fusion(f32[4096]{0:T(1024)S(1)} %bitcast.54, bf16[1,8192,128]{2,1,0:T(8,128)(2,1)} %param.16, f32[4096]{0:T(1024)S(1)} %bitcast.55), kind=kLoop, calls=%fused_computation.10 | loop fusion | flops 3145728 | bytes 4227072 | tf_op jit(solution)/shard_map/convert_element_type | solution.py:238
  30.3 1.7 collective-permute-start.20
  32.0 1.5 collective-permute-start.21
  35.2 13.7 %collective-permute-start.12 = (bf16[1024,256]{1,0:T(8,128)(2,1)}, bf16[1024,256]{1,0:T(8,128)(2,1)S(1)}, u32[]{:S(2)}, u32[]{:S(2)}) collective-permute-start(bf16[1024,256]{1,0:T(8,128)(2,1)} %collective-permute-done.9.refs_2_), channel_id=1, source_target_pairs={{0,1},{1,0},{2,3},{3,2},{4,5},{5,4},{6,7},{7,6},{8,9},{9,8},{10,11... | collective-permute-start | bytes 1572872 | tf_op jit(solution)/shard_map/ppermute | solution.py:166
  49.1 1.5 collective-permute-start.14
  51.2 1.3 collective-permute-start.5
  54.0 5.3 %in_places.2.refs_2_ = bf16[1024,4096]{1,0:T(8,128)(2,1)S(1)} custom-call(s32[6]{0:T(128)S(1)} %stack.27.place_ref, bf16[1024,4096]{1,0:T(8,128)(2,1)S(1)} %bitcast.45, f32[1,4096]{1,0:T(1,128)S(1)} %bitcast.49, bf16[1024,512]{1,0:T(8,128)(2,1)S(1)} %join_cores.3.refs_2_, bf16[1024,256]{1,0:T(8,128)(2,1)S(1)} %collective-permute-done.5.refs_3_, ...), custom_call_target="tpu_custom_call" | custom-call | flops 5000000000 | bytes 1 | tf_op jit(solution)/shard_map/in_places/pallas_call | solution.py:39
  59.7 1.3 copy-done.8
  61.1 1.8 collective-permute-done.14.refs_3_.refs_2_
  63.4 2.3 %convolution_convert_fusion.4 = bf16[1024,256]{1,0:T(8,128)(2,1)S(1)} fusion(bf16[1024,4096]{1,0:T(8,128)(2,1)S(1)} %in_places.2.refs_2_, bf16[4096,256]{1,0:T(8,128)(2,1)S(1)} %get-tuple-element.13), kind=kOutput, calls=%fused_computation.22 | convolution fusion | flops 2147745792 | bytes 11010048 | tf_op jit(solution)/shard_map/dot_general | solution.py:251
  66.5 2.3 %convolution_convert_fusion.5 = bf16[1024,256]{1,0:T(8,128)(2,1)S(1)} fusion(bf16[1024,4096]{1,0:T(8,128)(2,1)S(1)} %in_places.2.refs_2_, bf16[4096,256]{1,0:T(8,128)(2,1)S(1)} %get-tuple-element.12.refs_1_), kind=kOutput, calls=%fused_computation.23 | convolution fusion | flops 2147745792 | bytes 11010048 | tf_op jit(solution)/shard_map/dot_general | solution.py:251
  70.8 2.7 %copy-done.3 = bf16[1024,4096]{1,0:T(8,128)(2,1)} copy-done((bf16[1024,4096]{1,0:T(8,128)(2,1)}, bf16[1024,4096]{1,0:T(8,128)(2,1)S(1)}, u32[]{:S(2)}) %copy-start.3) | copy-done | bytes 8388632
  74.5 4.9 %convolution_convert_fusion.refs_0_ = bf16[512,4096]{1,0:T(8,128)(2,1)S(1)} fusion(bf16[1024,512]{1,0:T(8,128)(2,1)S(1)} %fence.10.refs_1_, bf16[1024,4096]{1,0:T(8,128)(2,1)S(1)} %in_places.3.refs_1_), kind=kOutput, calls=%fused_computation | convolution fusion | flops 4297064448 | bytes 13631488 | tf_op jit(solution)/shard_map/dot_general | solution.py:173
  80.4 1.8 fusion.8
  83.4 4.6 %collective-permute-start.24 = (bf16[512,1024]{1,0:T(8,128)(2,1)}, bf16[512,1024]{1,0:T(8,128)(2,1)}, u32[]{:S(2)}, u32[]{:S(2)}) collective-permute-start(bf16[512,1024]{1,0:T(8,128)(2,1)} %get-tuple-element.24), channel_id=1, source_target_pairs={{0,1},{1,0},{2,3},{3,2},{4,5},{5,4},{6,7},{7,6},{8,9},{9,8},{10,11... | collective-permute-start | bytes 3145736 | tf_op jit(solution)/shard_map/ppermute | solution.py:166
  88.8 1.8 add_convert_fusion.1
  91.8 1.9 add_convert_fusion.4
  93.8 6.3 %collective-permute-start.25 = (bf16[512,1024]{1,0:T(8,128)(2,1)S(1)}, bf16[512,1024]{1,0:T(8,128)(2,1)S(1)}, u32[]{:S(2)}, u32[]{:S(2)}) collective-permute-start(bf16[512,1024]{1,0:T(8,128)(2,1)S(1)} %add_convert_fusion.4), channel_id=1, source_target_pairs={{0,2},{7,5},{8,10},{15,13},{16,18},{23,21},{24,26},{31,29}} | collective-permute-start | bytes 3145736 | tf_op jit(solution)/shard_map/ppermute | solution.py:169
  100.1 5.5 %collective-permute-start.17 = (bf16[1024,512]{1,0:T(8,128)(2,1)S(1)}, bf16[1024,512]{1,0:T(8,128)(2,1)S(1)}, u32[]{:S(2)}, u32[]{:S(2)}) collective-permute-start(bf16[1024,512]{1,0:T(8,128)(2,1)S(1)} %collective-permute-done.16), channel_id=1, source_target_pairs={{0,1},{1,0},{2,3},{3,2},{4,5},{5,4},{6,7},{7,6},{8,9},{9,8},{10,11... | collective-permute-start | bytes 3145736 | tf_op jit(solution)/shard_map/ppermute | solution.py:166
  107.8 1.6 collective-permute-start.44
  109.6 2.6 %collective-permute-done.25 = bf16[512,1024]{1,0:T(8,128)(2,1)S(1)} collective-permute-done((bf16[512,1024]{1,0:T(8,128)(2,1)S(1)}, bf16[512,1024]{1,0:T(8,128)(2,1)S(1)}, u32[]{:S(2)}, u32[]{:S(2)}) %collective-permute-start.25) | collective-permute-done | bytes 1048608 | tf_op jit(solution)/shard_map/ppermute | solution.py:169
  112.8 4.5 %collective-permute-start.26 = (bf16[512,1024]{1,0:T(8,128)(2,1)S(1)}, bf16[512,1024]{1,0:T(8,128)(2,1)S(1)}, u32[]{:S(2)}, u32[]{:S(2)}) collective-permute-start(bf16[512,1024]{1,0:T(8,128)(2,1)S(1)} %add_convert_fusion.3), channel_id=1, source_target_pairs={{0,2},{2,4},{5,3},{7,5},{8,10},{10,12},{13,11},{15,13},{16,18},{18... | collective-permute-start | bytes 3145736 | tf_op jit(solution)/shard_map/ppermute | solution.py:169
  118.3 1.3 slice-done.2
  119.6 1.4 slice-done.3
  121.0 4.5 %convolution_convert_fusion.3.refs_0_ = bf16[1024,512]{1,0:T(8,128)(2,1)S(1)} fusion(bf16[1024,4096]{1,0:T(8,128)(2,1)S(1)} %bitcast.42, bf16[4096,512]{1,0:T(8,128)(2,1)S(1)} %fence.12.refs_1_), kind=kOutput, calls=%fused_computation.21 | convolution fusion | flops 4295491584 | bytes 13631488 | tf_op jit(solution)/shard_map/dot_general | solution.py:263
  125.5 4.0 %collective-permute-done.26 = bf16[512,1024]{1,0:T(8,128)(2,1)S(1)} collective-permute-done((bf16[512,1024]{1,0:T(8,128)(2,1)S(1)}, bf16[512,1024]{1,0:T(8,128)(2,1)S(1)}, u32[]{:S(2)}, u32[]{:S(2)}) %collective-permute-start.26) | collective-permute-done | bytes 1048608 | tf_op jit(solution)/shard_map/ppermute | solution.py:169
  130.1 4.5 %collective-permute-start.34 = (bf16[512,1024]{1,0:T(8,128)(2,1)S(1)}, bf16[512,1024]{1,0:T(8,128)(2,1)S(1)}, u32[]{:S(2)}, u32[]{:S(2)}) collective-permute-start(bf16[512,1024]{1,0:T(8,128)(2,1)S(1)} %add_convert_fusion.2.refs_2_), channel_id=1, source_target_pairs={{0,2},{2,4},{3,1},{4,6},{5,3},{7,5},{8,10},{10,12},{11,9},{12,14},... | collective-permute-start | bytes 3145736 | tf_op jit(solution)/shard_map/ppermute | solution.py:169
  135.2 2.5 %convolution_convert_fusion.2 = bf16[256,4096]{1,0:T(8,128)(2,1)S(1)} fusion(bf16[1024,4096]{1,0:T(8,128)(2,1)S(1)} %bitcast.40, bf16[1024,512]{1,0:T(8,128)(2,1)S(1)} %fence.13.refs_1_), kind=kOutput, calls=%fused_computation.2 | convolution fusion | flops 2148532224 | bytes 11010048 | tf_op jit(solution)/shard_map/dot_general | solution.py:173
  137.9 2.5 %convolution_convert_fusion.1.refs_0_ = bf16[256,4096]{1,0:T(8,128)(2,1)S(1)} fusion(bf16[1024,4096]{1,0:T(8,128)(2,1)S(1)} %bitcast.40, bf16[1024,512]{1,0:T(8,128)(2,1)S(1)} %fence.13.refs_1_), kind=kOutput, calls=%fused_computation.1 | convolution fusion | flops 2148532224 | bytes 11010048 | tf_op jit(solution)/shard_map/dot_general | solution.py:173
  141.0 5.8 %collective-permute-done.34.refs_2_ = bf16[512,1024]{1,0:T(8,128)(2,1)S(1)} collective-permute-done((bf16[512,1024]{1,0:T(8,128)(2,1)S(1)}, bf16[512,1024]{1,0:T(8,128)(2,1)S(1)}, u32[]{:S(2)}, u32[]{:S(2)}) %collective-permute-start.34) | collective-permute-done | bytes 1048608 | tf_op jit(solution)/shard_map/ppermute | solution.py:169
  148.5 4.0 %collective-permute-start.30 = (bf16[256,1024]{1,0:T(8,128)(2,1)S(1)}, bf16[256,1024]{1,0:T(8,128)(2,1)S(1)}, u32[]{:S(2)}, u32[]{:S(2)}) collective-permute-start(bf16[256,1024]{1,0:T(8,128)(2,1)S(1)} %add_convert_fusion.10.refs_3_), channel_id=1, source_target_pairs={{0,2},{7,5},{8,10},{15,13},{16,18},{23,21},{24,26},{31,29}} | collective-permute-start | bytes 1572872 | tf_op jit(solution)/shard_map/ppermute | solution.py:169
  153.1 1.5 collective-permute-start.38
  154.8 4.3 %collective-permute-done.30 = bf16[256,1024]{1,0:T(8,128)(2,1)S(1)} collective-permute-done((bf16[256,1024]{1,0:T(8,128)(2,1)S(1)}, bf16[256,1024]{1,0:T(8,128)(2,1)S(1)}, u32[]{:S(2)}, u32[]{:S(2)}) %collective-permute-start.30) | collective-permute-done | bytes 524320 | tf_op jit(solution)/shard_map/ppermute | solution.py:169
  160.6 4.4 %collective-permute-start.31 = (bf16[256,1024]{1,0:T(8,128)(2,1)S(1)}, bf16[256,1024]{1,0:T(8,128)(2,1)S(1)}, u32[]{:S(2)}, u32[]{:S(2)}) collective-permute-start(bf16[256,1024]{1,0:T(8,128)(2,1)S(1)} %add_convert_fusion.9), channel_id=1, source_target_pairs={{0,2},{2,4},{5,3},{7,5},{8,10},{10,12},{13,11},{15,13},{16,18},{18... | collective-permute-start | bytes 1572872 | tf_op jit(solution)/shard_map/ppermute | solution.py:169
  165.3 4.1 %collective-permute-start.39 = (bf16[256,1024]{1,0:T(8,128)(2,1)S(1)}, bf16[256,1024]{1,0:T(8,128)(2,1)S(1)}, u32[]{:S(2)}, u32[]{:S(2)}) collective-permute-start(bf16[256,1024]{1,0:T(8,128)(2,1)S(1)} %add_convert_fusion.6), channel_id=1, source_target_pairs={{0,2},{2,4},{5,3},{7,5},{8,10},{10,12},{13,11},{15,13},{16,18},{18... | collective-permute-start | bytes 1572872 | tf_op jit(solution)/shard_map/ppermute | solution.py:169
  169.4 1.8 convert_add_fusion
  172.0 4.4 %collective-permute-start.32 = (bf16[256,1024]{1,0:T(8,128)(2,1)S(1)}, bf16[256,1024]{1,0:T(8,128)(2,1)S(1)}, u32[]{:S(2)}, u32[]{:S(2)}) collective-permute-start(bf16[256,1024]{1,0:T(8,128)(2,1)S(1)} %add_convert_fusion.8), channel_id=1, source_target_pairs={{0,2},{2,4},{3,1},{4,6},{5,3},{7,5},{8,10},{10,12},{11,9},{12,14},... | collective-permute-start | bytes 1572872 | tf_op jit(solution)/shard_map/ppermute | solution.py:169
  177.6 5.2 %collective-permute-start.40 = (bf16[256,1024]{1,0:T(8,128)(2,1)S(1)}, bf16[256,1024]{1,0:T(8,128)(2,1)}, u32[]{:S(2)}, u32[]{:S(2)}) collective-permute-start(bf16[256,1024]{1,0:T(8,128)(2,1)S(1)} %add_convert_fusion.5), channel_id=1, source_target_pairs={{0,2},{2,4},{3,1},{4,6},{5,3},{7,5},{8,10},{10,12},{11,9},{12,14},... | collective-permute-start | bytes 1572872 | tf_op jit(solution)/shard_map/ppermute | solution.py:169
  182.8 3.9 %subtract_convert_fusion = (bf16[8192,128]{1,0:T(8,128)(2,1)}, f32[8192,128]{1,0:T(8,128)}) fusion(bf16[8192,128]{1,0:T(8,128)(2,1)S(1)} %copy-done.20, f32[4096,128]{1,0:T(8,128)S(1)} %get-tuple-element.35, f32[4096,128]{1,0:T(8,128)S(1)} %get-tuple-element.36, f32[8192,128]{1,0:T(8,128)S(1)} %copy-done.19), kind=kLoop, calls=%fused_computation.5 | loop fusion | flops 10485760 | bytes 16777216 | tf_op jit(solution)/shard_map/convert_element_type | solution.py:135
  190.6 1.4 add_bitcast_fusion
  192.0 1.3 copy.26
  194.6 1.3 copy.25
  (171 shorter events, 36.7 us)
Async XLA Ops:
  1.4 2.2 %collective-permute-start.1 = (bf16[512,512]{1,0:T(8,128)(2,1)}, bf16[512,512]{1,0:T(8,128)(2,1)S(1)}, u32[]{:S(2)}, u32[]{:S(2)}) collective-permute-start(bf16[512,512]{1,0:T(8,128)(2,1)} %bitcast.52), channel_id=1, source_target_pairs={{0,1},{1,0},{2,3},{3,2},{4,5},{5,4},{6,7},{7,6},{8,9},{9,8},{10,11... | collective-permute-start | bytes 1572872 | tf_op jit(solution)/shard_map/ppermute | solution.py:166
  1.8 2.5 %collective-permute-start = (bf16[512,512]{1,0:T(8,128)(2,1)}, bf16[512,512]{1,0:T(8,128)(2,1)S(1)}, u32[]{:S(2)}, u32[]{:S(2)}) collective-permute-start(bf16[512,512]{1,0:T(8,128)(2,1)} %bitcast.50), channel_id=1, source_target_pairs={{0,1},{1,0},{2,3},{3,2},{4,5},{5,4},{6,7},{7,6},{8,9},{9,8},{10,11... | collective-permute-start | bytes 1572872 | tf_op jit(solution)/shard_map/ppermute | solution.py:166
  3.6 22.1 %copy-start.14 = (bf16[512,512]{1,0:T(8,128)(2,1)}, bf16[512,512]{1,0:T(8,128)(2,1)S(1)}, u32[]{:S(2)}) copy-start(bf16[512,512]{1,0:T(8,128)(2,1)S(1)} %collective-permute-done.1.refs_2_.refs_1_) | copy-start | bytes 1572868
  6.1 24.2 %copy-start.7 = (bf16[1024,256]{1,0:T(8,128)(2,1)}, bf16[1024,256]{1,0:T(8,128)(2,1)S(1)}, u32[]{:S(2)}) copy-start(bf16[1024,256]{1,0:T(8,128)(2,1)S(1)} %get-tuple-element.10.refs_1_) | copy-start | bytes 1572868
  6.1 11.5 %collective-permute-start.8 = (bf16[1024,256]{1,0:T(8,128)(2,1)S(1)}, bf16[1024,256]{1,0:T(8,128)(2,1)}, u32[]{:S(2)}, u32[]{:S(2)}) collective-permute-start(bf16[1024,256]{1,0:T(8,128)(2,1)S(1)} %get-tuple-element.11), channel_id=1, source_target_pairs={{0,2},{2,4},{3,1},{4,6},{5,3},{7,5},{8,10},{10,12},{11,9},{12,14},... | collective-permute-start | bytes 1572872 | tf_op jit(solution)/shard_map/ppermute | solution.py:169
  11.8 11.5 %collective-permute-start.2 = (bf16[1024,256]{1,0:T(8,128)(2,1)S(1)}, bf16[1024,256]{1,0:T(8,128)(2,1)}, u32[]{:S(2)}, u32[]{:S(2)}) collective-permute-start(bf16[1024,256]{1,0:T(8,128)(2,1)S(1)} %get-tuple-element.10.refs_1_), channel_id=1, source_target_pairs={{0,2},{2,4},{3,1},{4,6},{5,3},{7,5},{8,10},{10,12},{11,9},{12,14},... | collective-permute-start | bytes 1572872 | tf_op jit(solution)/shard_map/ppermute | solution.py:169
  17.6 6.8 %collective-permute-start.9 = (bf16[1024,256]{1,0:T(8,128)(2,1)}, bf16[1024,256]{1,0:T(8,128)(2,1)}, u32[]{:S(2)}, u32[]{:S(2)}) collective-permute-start(bf16[1024,256]{1,0:T(8,128)(2,1)} %collective-permute-done.8), channel_id=1, source_target_pairs={{2,4},{3,1},{4,6},{5,3},{10,12},{11,9},{12,14},{13,11},{18,20},{19... | collective-permute-start | bytes 1572872 | tf_op jit(solution)/shard_map/ppermute | solution.py:169
  19.1 29.9 %collective-permute-start.13 = (bf16[1024,256]{1,0:T(8,128)(2,1)}, bf16[1024,256]{1,0:T(8,128)(2,1)S(1)}, u32[]{:S(2)}, u32[]{:S(2)}) collective-permute-start(bf16[1024,256]{1,0:T(8,128)(2,1)} %collective-permute-done.8), channel_id=1, source_target_pairs={{0,1},{1,0},{2,3},{3,2},{4,5},{5,4},{6,7},{7,6},{8,9},{9,8},{10,11... | collective-permute-start | bytes 1572872 | tf_op jit(solution)/shard_map/ppermute | solution.py:166
  23.2 2.5 %collective-permute-start.3 = (bf16[1024,256]{1,0:T(8,128)(2,1)}, bf16[1024,256]{1,0:T(8,128)(2,1)S(1)}, u32[]{:S(2)}, u32[]{:S(2)}) collective-permute-start(bf16[1024,256]{1,0:T(8,128)(2,1)} %collective-permute-done.2), channel_id=1, source_target_pairs={{2,4},{3,1},{4,6},{5,3},{10,12},{11,9},{12,14},{13,11},{18,20},{19... | collective-permute-start | bytes 1572872 | tf_op jit(solution)/shard_map/ppermute | solution.py:169
  23.9 11.3 %collective-permute-start.7 = (bf16[1024,256]{1,0:T(8,128)(2,1)}, bf16[1024,256]{1,0:T(8,128)(2,1)S(1)}, u32[]{:S(2)}, u32[]{:S(2)}) collective-permute-start(bf16[1024,256]{1,0:T(8,128)(2,1)} %collective-permute-done.2), channel_id=1, source_target_pairs={{0,1},{1,0},{2,3},{3,2},{4,5},{5,4},{6,7},{7,6},{8,9},{9,8},{10,11... | collective-permute-start | bytes 1572872 | tf_op jit(solution)/shard_map/ppermute | solution.py:166
  24.4 24.6 %collective-permute-start.10 = (bf16[1024,256]{1,0:T(8,128)(2,1)}, bf16[1024,256]{1,0:T(8,128)(2,1)S(1)}, u32[]{:S(2)}, u32[]{:S(2)}) collective-permute-start(bf16[1024,256]{1,0:T(8,128)(2,1)} %collective-permute-done.9.refs_2_), channel_id=1, source_target_pairs={{3,1},{4,6},{11,9},{12,14},{19,17},{20,22},{27,25},{28,30}} | collective-permute-start | bytes 1572872 | tf_op jit(solution)/shard_map/ppermute | solution.py:169
  25.8 6.2 %collective-permute-start.4 = (bf16[1024,256]{1,0:T(8,128)(2,1)S(1)}, bf16[1024,256]{1,0:T(8,128)(2,1)S(1)}, u32[]{:S(2)}, u32[]{:S(2)}) collective-permute-start(bf16[1024,256]{1,0:T(8,128)(2,1)S(1)} %collective-permute-done.3), channel_id=1, source_target_pairs={{3,1},{4,6},{11,9},{12,14},{19,17},{20,22},{27,25},{28,30}} | collective-permute-start | bytes 1572872 | tf_op jit(solution)/shard_map/ppermute | solution.py:169
  26.5 27.5 %slice-start.4 = ((s8[8388608]{0:T(1024)(128)(4,1)}), s8[4194304]{0:T(1024)(128)(4,1)S(1)}, s32[]{:S(2)}) async-start(s8[8388608]{0:T(1024)(128)(4,1)} %bitcast.43), calls=%async_computation.4 | async-start | bytes 8388608
  30.3 39.9 %collective-permute-start.20 = (bf16[4096,128]{1,0:T(8,128)(2,1)S(1)}, bf16[4096,128]{1,0:T(8,128)(2,1)S(1)}, u32[]{:S(2)}, u32[]{:S(2)}) collective-permute-start(bf16[4096,128]{1,0:T(8,128)(2,1)S(1)} %get-tuple-element.32), channel_id=1, source_target_pairs={{0,8},{8,0},{16,24},{24,16},{1,9},{9,1},{17,25},{25,17},{2,10},{10... | collective-permute-start | bytes 3145736 | tf_op jit(solution)/shard_map/ppermute | solution.py:240
  32.0 38.2 %collective-permute-start.21 = (bf16[4096,128]{1,0:T(8,128)(2,1)S(1)}, bf16[4096,128]{1,0:T(8,128)(2,1)S(1)}, u32[]{:S(2)}, u32[]{:S(2)}) collective-permute-start(bf16[4096,128]{1,0:T(8,128)(2,1)S(1)} %get-tuple-element.31), channel_id=1, source_target_pairs={{0,16},{8,24},{16,0},{24,8},{1,17},{9,25},{17,1},{25,9},{2,18},{10... | collective-permute-start | bytes 3145736 | tf_op jit(solution)/shard_map/ppermute | solution.py:240
  35.2 15.5 %collective-permute-start.12 = (bf16[1024,256]{1,0:T(8,128)(2,1)}, bf16[1024,256]{1,0:T(8,128)(2,1)S(1)}, u32[]{:S(2)}, u32[]{:S(2)}) collective-permute-start(bf16[1024,256]{1,0:T(8,128)(2,1)} %collective-permute-done.9.refs_2_), channel_id=1, source_target_pairs={{0,1},{1,0},{2,3},{3,2},{4,5},{5,4},{6,7},{7,6},{8,9},{9,8},{10,11... | collective-permute-start | bytes 1572872 | tf_op jit(solution)/shard_map/ppermute | solution.py:166
  49.0 2.2 %collective-permute-start.6 = (bf16[1024,256]{1,0:T(8,128)(2,1)S(1)}, bf16[1024,256]{1,0:T(8,128)(2,1)S(1)}, u32[]{:S(2)}, u32[]{:S(2)}) collective-permute-start(bf16[1024,256]{1,0:T(8,128)(2,1)S(1)} %collective-permute-done.3), channel_id=1, source_target_pairs={{0,1},{1,0},{2,3},{3,2},{4,5},{5,4},{6,7},{7,6},{8,9},{9,8},{10,11... | collective-permute-start | bytes 1572872 | tf_op jit(solution)/shard_map/ppermute | solution.py:166
  49.1 13.8 %collective-permute-start.14 = (bf16[1024,512]{1,0:T(8,128)(2,1)S(1)}, bf16[1024,512]{1,0:T(8,128)(2,1)S(1)}, u32[]{:S(2)}, u32[]{:S(2)}) collective-permute-start(bf16[1024,512]{1,0:T(8,128)(2,1)S(1)} %join_cores.3.refs_2_), channel_id=1, source_target_pairs={{0,2},{2,4},{3,1},{4,6},{5,3},{7,5},{8,10},{10,12},{11,9},{12,14},... | collective-permute-start | bytes 3145736 | tf_op jit(solution)/shard_map/ppermute | solution.py:169
  50.7 2.0 %collective-permute-start.11 = (bf16[1024,256]{1,0:T(8,128)(2,1)S(1)}, bf16[1024,256]{1,0:T(8,128)(2,1)S(1)}, u32[]{:S(2)}, u32[]{:S(2)}) collective-permute-start(bf16[1024,256]{1,0:T(8,128)(2,1)S(1)} %collective-permute-done.10), channel_id=1, source_target_pairs={{0,1},{1,0},{2,3},{3,2},{4,5},{5,4},{6,7},{7,6},{8,9},{9,8},{10,11... | collective-permute-start | bytes 1572872 | tf_op jit(solution)/shard_map/ppermute | solution.py:166
  51.2 2.8 %collective-permute-start.5 = (bf16[1024,256]{1,0:T(8,128)(2,1)S(1)}, bf16[1024,256]{1,0:T(8,128)(2,1)S(1)}, u32[]{:S(2)}, u32[]{:S(2)}) collective-permute-start(bf16[1024,256]{1,0:T(8,128)(2,1)S(1)} %collective-permute-done.4.refs_3_), channel_id=1, source_target_pairs={{0,1},{1,0},{2,3},{3,2},{4,5},{5,4},{6,7},{7,6},{8,9},{9,8},{10,11... | collective-permute-start | bytes 1572872 | tf_op jit(solution)/shard_map/ppermute | solution.py:166
  65.8 13.7 %collective-permute-start.15 = (bf16[1024,512]{1,0:T(8,128)(2,1)S(1)}, bf16[1024,512]{1,0:T(8,128)(2,1)S(1)}, u32[]{:S(2)}, u32[]{:S(2)}) collective-permute-start(bf16[1024,512]{1,0:T(8,128)(2,1)S(1)} %collective-permute-done.14.refs_3_.refs_2_), channel_id=1, source_target_pairs={{2,4},{3,1},{4,6},{5,3},{10,12},{11,9},{12,14},{13,11},{18,20},{19... | collective-permute-start | bytes 3145736 | tf_op jit(solution)/shard_map/ppermute | solution.py:169
  83.4 8.4 %collective-permute-start.24 = (bf16[512,1024]{1,0:T(8,128)(2,1)}, bf16[512,1024]{1,0:T(8,128)(2,1)}, u32[]{:S(2)}, u32[]{:S(2)}) collective-permute-start(bf16[512,1024]{1,0:T(8,128)(2,1)} %get-tuple-element.24), channel_id=1, source_target_pairs={{0,1},{1,0},{2,3},{3,2},{4,5},{5,4},{6,7},{7,6},{8,9},{9,8},{10,11... | collective-permute-start | bytes 3145736 | tf_op jit(solution)/shard_map/ppermute | solution.py:166
  88.0 12.1 %collective-permute-start.16 = (bf16[1024,512]{1,0:T(8,128)(2,1)}, bf16[1024,512]{1,0:T(8,128)(2,1)S(1)}, u32[]{:S(2)}, u32[]{:S(2)}) collective-permute-start(bf16[1024,512]{1,0:T(8,128)(2,1)} %copy-done.5), channel_id=1, source_target_pairs={{3,1},{4,6},{11,9},{12,14},{19,17},{20,22},{27,25},{28,30}} | collective-permute-start | bytes 3145736 | tf_op jit(solution)/shard_map/ppermute | solution.py:169
  90.7 16.2 %collective-permute-start.19 = (bf16[1024,512]{1,0:T(8,128)(2,1)S(1)}, bf16[1024,512]{1,0:T(8,128)(2,1)S(1)}, u32[]{:S(2)}, u32[]{:S(2)}) collective-permute-start(bf16[1024,512]{1,0:T(8,128)(2,1)S(1)} %collective-permute-done.14.refs_3_.refs_2_), channel_id=1, source_target_pairs={{0,1},{1,0},{2,3},{3,2},{4,5},{5,4},{6,7},{7,6},{8,9},{9,8},{10,11... | collective-permute-start | bytes 3145736 | tf_op jit(solution)/shard_map/ppermute | solution.py:166
  91.3 18.2 %collective-permute-start.23 = (bf16[512,1024]{1,0:T(8,128)(2,1)S(1)}, bf16[512,1024]{1,0:T(8,128)(2,1)S(1)}, u32[]{:S(2)}, u32[]{:S(2)}) collective-permute-start(bf16[512,1024]{1,0:T(8,128)(2,1)S(1)} %copy-done.22), channel_id=1, source_target_pairs={{0,1},{1,0},{2,3},{3,2},{4,5},{5,4},{6,7},{7,6},{8,9},{9,8},{10,11... | collective-permute-start | bytes 3145736 | tf_op jit(solution)/shard_map/ppermute | solution.py:166
  91.4 16.4 %collective-permute-start.18 = (bf16[1024,512]{1,0:T(8,128)(2,1)S(1)}, bf16[1024,512]{1,0:T(8,128)(2,1)S(1)}, u32[]{:S(2)}, u32[]{:S(2)}) collective-permute-start(bf16[1024,512]{1,0:T(8,128)(2,1)S(1)} %copy-done.6), channel_id=1, source_target_pairs={{0,1},{1,0},{2,3},{3,2},{4,5},{5,4},{6,7},{7,6},{8,9},{9,8},{10,11... | collective-permute-start | bytes 3145736 | tf_op jit(solution)/shard_map/ppermute | solution.py:166
  93.8 18.4 %collective-permute-start.25 = (bf16[512,1024]{1,0:T(8,128)(2,1)S(1)}, bf16[512,1024]{1,0:T(8,128)(2,1)S(1)}, u32[]{:S(2)}, u32[]{:S(2)}) collective-permute-start(bf16[512,1024]{1,0:T(8,128)(2,1)S(1)} %add_convert_fusion.4), channel_id=1, source_target_pairs={{0,2},{7,5},{8,10},{15,13},{16,18},{23,21},{24,26},{31,29}} | collective-permute-start | bytes 3145736 | tf_op jit(solution)/shard_map/ppermute | solution.py:169
  100.1 17.2 %collective-permute-start.17 = (bf16[1024,512]{1,0:T(8,128)(2,1)S(1)}, bf16[1024,512]{1,0:T(8,128)(2,1)S(1)}, u32[]{:S(2)}, u32[]{:S(2)}) collective-permute-start(bf16[1024,512]{1,0:T(8,128)(2,1)S(1)} %collective-permute-done.16), channel_id=1, source_target_pairs={{0,1},{1,0},{2,3},{3,2},{4,5},{5,4},{6,7},{7,6},{8,9},{9,8},{10,11... | collective-permute-start | bytes 3145736 | tf_op jit(solution)/shard_map/ppermute | solution.py:166
  106.9 52.5 %collective-permute-start.43 = (bf16[4096,128]{1,0:T(8,128)(2,1)S(1)}, bf16[4096,128]{1,0:T(8,128)(2,1)S(1)}, u32[]{:S(2)}, u32[]{:S(2)}) collective-permute-start(bf16[4096,128]{1,0:T(8,128)(2,1)S(1)} %add_convert_fusion.1), channel_id=1, source_target_pairs={{0,16},{8,24},{16,0},{24,8},{1,17},{9,25},{17,1},{25,9},{2,18},{10... | collective-permute-start | bytes 3145736 | tf_op jit(solution)/shard_map/ppermute | solution.py:240
  107.8 52.2 %collective-permute-start.44 = (bf16[4096,128]{1,0:T(8,128)(2,1)}, bf16[4096,128]{1,0:T(8,128)(2,1)S(1)}, u32[]{:S(2)}, u32[]{:S(2)}) collective-permute-start(bf16[4096,128]{1,0:T(8,128)(2,1)} %add_convert_fusion), channel_id=1, source_target_pairs={{0,8},{8,0},{16,24},{24,16},{1,9},{9,1},{17,25},{25,17},{2,10},{10... | collective-permute-start | bytes 3145736 | tf_op jit(solution)/shard_map/ppermute | solution.py:240
  109.5 15.9 %collective-permute-start.22 = (bf16[512,1024]{1,0:T(8,128)(2,1)S(1)}, bf16[512,1024]{1,0:T(8,128)(2,1)S(1)}, u32[]{:S(2)}, u32[]{:S(2)}) collective-permute-start(bf16[512,1024]{1,0:T(8,128)(2,1)S(1)} %copy-done.21), channel_id=1, source_target_pairs={{0,1},{1,0},{2,3},{3,2},{4,5},{5,4},{6,7},{7,6},{8,9},{9,8},{10,11... | collective-permute-start | bytes 3145736 | tf_op jit(solution)/shard_map/ppermute | solution.py:166
  112.8 16.7 %collective-permute-start.26 = (bf16[512,1024]{1,0:T(8,128)(2,1)S(1)}, bf16[512,1024]{1,0:T(8,128)(2,1)S(1)}, u32[]{:S(2)}, u32[]{:S(2)}) collective-permute-start(bf16[512,1024]{1,0:T(8,128)(2,1)S(1)} %add_convert_fusion.3), channel_id=1, source_target_pairs={{0,2},{2,4},{5,3},{7,5},{8,10},{10,12},{13,11},{15,13},{16,18},{18... | collective-permute-start | bytes 3145736 | tf_op jit(solution)/shard_map/ppermute | solution.py:169
  130.1 16.7 %collective-permute-start.34 = (bf16[512,1024]{1,0:T(8,128)(2,1)S(1)}, bf16[512,1024]{1,0:T(8,128)(2,1)S(1)}, u32[]{:S(2)}, u32[]{:S(2)}) collective-permute-start(bf16[512,1024]{1,0:T(8,128)(2,1)S(1)} %add_convert_fusion.2.refs_2_), channel_id=1, source_target_pairs={{0,2},{2,4},{3,1},{4,6},{5,3},{7,5},{8,10},{10,12},{11,9},{12,14},... | collective-permute-start | bytes 3145736 | tf_op jit(solution)/shard_map/ppermute | solution.py:169
  137.8 10.4 %collective-permute-start.29 = (bf16[256,1024]{1,0:T(8,128)(2,1)S(1)}, bf16[256,1024]{1,0:T(8,128)(2,1)S(1)}, u32[]{:S(2)}, u32[]{:S(2)}) collective-permute-start(bf16[256,1024]{1,0:T(8,128)(2,1)S(1)} %get-tuple-element.27), channel_id=1, source_target_pairs={{0,1},{1,0},{2,3},{3,2},{4,5},{5,4},{6,7},{7,6},{8,9},{9,8},{10,11... | collective-permute-start | bytes 1572872 | tf_op jit(solution)/shard_map/ppermute | solution.py:166
  140.5 12.7 %collective-permute-start.28 = (bf16[256,1024]{1,0:T(8,128)(2,1)S(1)}, bf16[256,1024]{1,0:T(8,128)(2,1)S(1)}, u32[]{:S(2)}, u32[]{:S(2)}) collective-permute-start(bf16[256,1024]{1,0:T(8,128)(2,1)S(1)} %get-tuple-element.26), channel_id=1, source_target_pairs={{0,1},{1,0},{2,3},{3,2},{4,5},{5,4},{6,7},{7,6},{8,9},{9,8},{10,11... | collective-permute-start | bytes 1572872 | tf_op jit(solution)/shard_map/ppermute | solution.py:166
  147.5 5.3 %collective-permute-start.37 = (bf16[256,1024]{1,0:T(8,128)(2,1)S(1)}, bf16[256,1024]{1,0:T(8,128)(2,1)S(1)}, u32[]{:S(2)}, u32[]{:S(2)}) collective-permute-start(bf16[256,1024]{1,0:T(8,128)(2,1)S(1)} %get-tuple-element.30), channel_id=1, source_target_pairs={{0,1},{1,0},{2,3},{3,2},{4,5},{5,4},{6,7},{7,6},{8,9},{9,8},{10,11... | collective-permute-start | bytes 1572872 | tf_op jit(solution)/shard_map/ppermute | solution.py:166
  148.5 10.6 %collective-permute-start.30 = (bf16[256,1024]{1,0:T(8,128)(2,1)S(1)}, bf16[256,1024]{1,0:T(8,128)(2,1)S(1)}, u32[]{:S(2)}, u32[]{:S(2)}) collective-permute-start(bf16[256,1024]{1,0:T(8,128)(2,1)S(1)} %add_convert_fusion.10.refs_3_), channel_id=1, source_target_pairs={{0,2},{7,5},{8,10},{15,13},{16,18},{23,21},{24,26},{31,29}} | collective-permute-start | bytes 1572872 | tf_op jit(solution)/shard_map/ppermute | solution.py:169
  152.9 7.7 %collective-permute-start.36 = (bf16[256,1024]{1,0:T(8,128)(2,1)S(1)}, bf16[256,1024]{1,0:T(8,128)(2,1)S(1)}, u32[]{:S(2)}, u32[]{:S(2)}) collective-permute-start(bf16[256,1024]{1,0:T(8,128)(2,1)S(1)} %get-tuple-element.29), channel_id=1, source_target_pairs={{0,1},{1,0},{2,3},{3,2},{4,5},{5,4},{6,7},{7,6},{8,9},{9,8},{10,11... | collective-permute-start | bytes 1572872 | tf_op jit(solution)/shard_map/ppermute | solution.py:166
  153.1 11.9 %collective-permute-start.38 = (bf16[256,1024]{1,0:T(8,128)(2,1)S(1)}, bf16[256,1024]{1,0:T(8,128)(2,1)S(1)}, u32[]{:S(2)}, u32[]{:S(2)}) collective-permute-start(bf16[256,1024]{1,0:T(8,128)(2,1)S(1)} %add_convert_fusion.7.refs_4_), channel_id=1, source_target_pairs={{0,2},{7,5},{8,10},{15,13},{16,18},{23,21},{24,26},{31,29}} | collective-permute-start | bytes 1572872 | tf_op jit(solution)/shard_map/ppermute | solution.py:169
  159.1 12.1 %collective-permute-start.27 = (bf16[256,1024]{1,0:T(8,128)(2,1)S(1)}, bf16[256,1024]{1,0:T(8,128)(2,1)S(1)}, u32[]{:S(2)}, u32[]{:S(2)}) collective-permute-start(bf16[256,1024]{1,0:T(8,128)(2,1)S(1)} %get-tuple-element.25), channel_id=1, source_target_pairs={{0,1},{1,0},{2,3},{3,2},{4,5},{5,4},{6,7},{7,6},{8,9},{9,8},{10,11... | collective-permute-start | bytes 1572872 | tf_op jit(solution)/shard_map/ppermute | solution.py:166
  159.4 31.2 %collective-permute-start.42 = (bf16[512,512]{1,0:T(8,128)(2,1)S(1)}, bf16[512,512]{1,0:T(8,128)(2,1)}, u32[]{:S(2)}, u32[]{:S(2)}) collective-permute-start(bf16[512,512]{1,0:T(8,128)(2,1)S(1)} %select_convert_fusion), channel_id=1, source_target_pairs={{0,1},{1,0},{2,3},{3,2},{4,5},{5,4},{6,7},{7,6},{8,9},{9,8},{10,11... | collective-permute-start | bytes 1572872 | tf_op jit(solution)/shard_map/ppermute | solution.py:166
  160.0 16.4 %collective-permute-start.35 = (bf16[256,1024]{1,0:T(8,128)(2,1)S(1)}, bf16[256,1024]{1,0:T(8,128)(2,1)S(1)}, u32[]{:S(2)}, u32[]{:S(2)}) collective-permute-start(bf16[256,1024]{1,0:T(8,128)(2,1)S(1)} %get-tuple-element.28), channel_id=1, source_target_pairs={{0,1},{1,0},{2,3},{3,2},{4,5},{5,4},{6,7},{7,6},{8,9},{9,8},{10,11... | collective-permute-start | bytes 1572872 | tf_op jit(solution)/shard_map/ppermute | solution.py:166
  160.6 11.1 %collective-permute-start.31 = (bf16[256,1024]{1,0:T(8,128)(2,1)S(1)}, bf16[256,1024]{1,0:T(8,128)(2,1)S(1)}, u32[]{:S(2)}, u32[]{:S(2)}) collective-permute-start(bf16[256,1024]{1,0:T(8,128)(2,1)S(1)} %add_convert_fusion.9), channel_id=1, source_target_pairs={{0,2},{2,4},{5,3},{7,5},{8,10},{10,12},{13,11},{15,13},{16,18},{18... | collective-permute-start | bytes 1572872 | tf_op jit(solution)/shard_map/ppermute | solution.py:169
  165.3 12.0 %collective-permute-start.39 = (bf16[256,1024]{1,0:T(8,128)(2,1)S(1)}, bf16[256,1024]{1,0:T(8,128)(2,1)S(1)}, u32[]{:S(2)}, u32[]{:S(2)}) collective-permute-start(bf16[256,1024]{1,0:T(8,128)(2,1)S(1)} %add_convert_fusion.6), channel_id=1, source_target_pairs={{0,2},{2,4},{5,3},{7,5},{8,10},{10,12},{13,11},{15,13},{16,18},{18... | collective-permute-start | bytes 1572872 | tf_op jit(solution)/shard_map/ppermute | solution.py:169
  172.0 14.7 %collective-permute-start.32 = (bf16[256,1024]{1,0:T(8,128)(2,1)S(1)}, bf16[256,1024]{1,0:T(8,128)(2,1)S(1)}, u32[]{:S(2)}, u32[]{:S(2)}) collective-permute-start(bf16[256,1024]{1,0:T(8,128)(2,1)S(1)} %add_convert_fusion.8), channel_id=1, source_target_pairs={{0,2},{2,4},{3,1},{4,6},{5,3},{7,5},{8,10},{10,12},{11,9},{12,14},... | collective-permute-start | bytes 1572872 | tf_op jit(solution)/shard_map/ppermute | solution.py:169
  177.6 11.1 %collective-permute-start.40 = (bf16[256,1024]{1,0:T(8,128)(2,1)S(1)}, bf16[256,1024]{1,0:T(8,128)(2,1)}, u32[]{:S(2)}, u32[]{:S(2)}) collective-permute-start(bf16[256,1024]{1,0:T(8,128)(2,1)S(1)} %add_convert_fusion.5), channel_id=1, source_target_pairs={{0,2},{2,4},{3,1},{4,6},{5,3},{7,5},{8,10},{10,12},{11,9},{12,14},... | collective-permute-start | bytes 1572872 | tf_op jit(solution)/shard_map/ppermute | solution.py:169
  187.6 5.7 %collective-permute-start.33 = (bf16[256,512]{1,0:T(8,128)(2,1)}, bf16[256,512]{1,0:T(8,128)(2,1)S(1)}, u32[]{:S(2)}, u32[]{:S(2)}) collective-permute-start(bf16[256,512]{1,0:T(8,128)(2,1)} %select_convert_fusion.2), channel_id=1, source_target_pairs={{0,1},{1,0},{2,3},{3,2},{4,5},{5,4},{6,7},{7,6},{8,9},{9,8},{10,11... | collective-permute-start | bytes 786440 | tf_op jit(solution)/shard_map/ppermute | solution.py:166
  190.6 2.8 %collective-permute-start.41 = (bf16[256,512]{1,0:T(8,128)(2,1)}, bf16[256,512]{1,0:T(8,128)(2,1)}, u32[]{:S(2)}, u32[]{:S(2)}) collective-permute-start(bf16[256,512]{1,0:T(8,128)(2,1)} %select_convert_fusion.1), channel_id=1, source_target_pairs={{0,1},{1,0},{2,3},{3,2},{4,5},{5,4},{6,7},{7,6},{8,9},{9,8},{10,11... | collective-permute-start | bytes 786440 | tf_op jit(solution)/shard_map/ppermute | solution.py:166
  (28 other events, 199.1 us)

commit v15 on v12

--- a/solution.py
+++ b/solution.py
@@ -226,7 +226,7 @@
     pieces, others = gather(joined)
     last = pieces[-1]
 
-    exponents = fence(order, delta_exponents, after=(pieces[2][1],))[0]
+    exponents = fence(order, delta_exponents, after=(pieces[-1][1],))[0]
     bits = replicas.bit_length() - 1
     if replicas != 1 << bits or bits < 1:
         raise ValueError("replicas")

time: 194 us -> 191 us (0.985)
    ppermute x18, waiting for transfers between devices: 24.6 us -> 22.2 us  [move(): return lax.ppermute(value, 'fsdp', move_perm(chips, active))]
    ppermute x23, starting transfers between devices: 35.7 us -> 37.8 us  [swap(): return lax.ppermute(value, 'fsdp', [(i, i ^ 1) for i in range(devices)])]
    unnamed x43 -> x47, local copies, waits for them, and re-layouts: 6.17 us -> 6.18 us
  transfers between devices with their start and end apart: 45 -> 45, of which waited for: 15 -> 14; matrix products, arithmetic and copies ran while one was open for 25% -> 25% of each run, Pallas kernels for 5% -> 5%
where the time goes in v15:
time: 191 us; the launch traced here: 190 us
  starting transfers between devices  95.1 us (50%)
  waiting for transfers between devices  28 us (15%)
  other arithmetic  25.4 us (13%)
  matrix products  19.2 us (10%)
  Pallas kernels  11.6 us (6%)
  local copies, waits for them, and re-layouts  9.03 us (5%)
    ppermute x18, starting transfers between devices, move(): return lax.ppermute(value, 'fsdp', move_perm(chips, active))  52.9 us
    ppermute x23, starting transfers between devices, swap(): return lax.ppermute(value, 'fsdp', [(i, i ^ 1) for i in range(devices)])  37.8 us
    ppermute x18, waiting for transfers between devices, move(): return lax.ppermute(value, 'fsdp', move_perm(chips, active))  22.2 us
    pallas_call x11, Pallas kernels, __call__(): pl.pallas_call(ordered, grid_spec=pltpu.PrefetchScalarGridSpec(num_scalar...  11.6 us
    dot_general x3, matrix products, __init__(): lax.dot_general(mid, x, (((0,), (0,)), ((), ())), preferred_element_type=...  10 us
    convert_element_type x9, other arithmetic, message(): return term.astype(bf16)  7.97 us
    unnamed x47, local copies, waits for them, and re-layouts  6.18 us
    dot_general x2, matrix products, per_device(): jnp.dot(normed, part, preferred_element_type=f32).astype(bf16)  4.66 us
  transfers between devices with their start and end apart: 45, of which 14 were waited for; matrix products, arithmetic and copies ran while one was open for 25% of the time, Pallas kernels for 5%

profile of v15, /device:TPU:0, one launch (start us, length us, event | category | flops | bytes accessed | tf_op | source)
XLA Modules:
  0.0 189.9 jit_solution(4173119226067494571)
XLA Ops:
  2.0 1.6 collective-permute-done.1.refs_2_.refs_1_
  6.1 5.8 %collective-permute-start.8 = (bf16[1024,256]{1,0:T(8,128)(2,1)S(1)}, bf16[1024,256]{1,0:T(8,128)(2,1)}, u32[]{:S(2)}, u32[]{:S(2)}) collective-permute-start(bf16[1024,256]{1,0:T(8,128)(2,1)S(1)} %get-tuple-element.11), channel_id=1, source_target_pairs={{0,2},{2,4},{3,1},{4,6},{5,3},{7,5},{8,10},{10,12},{11,9},{12,14},... | collective-permute-start | bytes 1572872 | tf_op jit(solution)/shard_map/ppermute | solution.py:169
  11.9 2.7 %collective-permute-start.2 = (bf16[1024,256]{1,0:T(8,128)(2,1)S(1)}, bf16[1024,256]{1,0:T(8,128)(2,1)S(1)}, u32[]{:S(2)}, u32[]{:S(2)}) collective-permute-start(bf16[1024,256]{1,0:T(8,128)(2,1)S(1)} %get-tuple-element.10.refs_1_), channel_id=1, source_target_pairs={{0,2},{2,4},{3,1},{4,6},{5,3},{7,5},{8,10},{10,12},{11,9},{12,14},... | collective-permute-start | bytes 1572872 | tf_op jit(solution)/shard_map/ppermute | solution.py:169
  14.6 3.2 %collective-permute-done.8 = bf16[1024,256]{1,0:T(8,128)(2,1)} collective-permute-done((bf16[1024,256]{1,0:T(8,128)(2,1)S(1)}, bf16[1024,256]{1,0:T(8,128)(2,1)}, u32[]{:S(2)}, u32[]{:S(2)}) %collective-permute-start.8) | collective-permute-done | bytes 524320 | tf_op jit(solution)/shard_map/ppermute | solution.py:169
  17.7 1.5 collective-permute-start.9
  19.2 4.1 %collective-permute-done.2 = bf16[1024,256]{1,0:T(8,128)(2,1)S(1)} collective-permute-done((bf16[1024,256]{1,0:T(8,128)(2,1)S(1)}, bf16[1024,256]{1,0:T(8,128)(2,1)S(1)}, u32[]{:S(2)}, u32[]{:S(2)}) %collective-permute-start.2) | collective-permute-done | bytes 524320 | tf_op jit(solution)/shard_map/ppermute | solution.py:169
  23.4 1.5 collective-permute-start.3
  25.5 4.6 %collective-permute-start.13 = (bf16[1024,256]{1,0:T(8,128)(2,1)}, bf16[1024,256]{1,0:T(8,128)(2,1)S(1)}, u32[]{:S(2)}, u32[]{:S(2)}) collective-permute-start(bf16[1024,256]{1,0:T(8,128)(2,1)} %collective-permute-done.8), channel_id=1, source_target_pairs={{0,1},{1,0},{2,3},{3,2},{4,5},{5,4},{6,7},{7,6},{8,9},{9,8},{10,11... | collective-permute-start | bytes 1572872 | tf_op jit(solution)/shard_map/ppermute | solution.py:166
  31.4 8.6 %collective-permute-start.6 = (bf16[1024,256]{1,0:T(8,128)(2,1)}, bf16[1024,256]{1,0:T(8,128)(2,1)S(1)}, u32[]{:S(2)}, u32[]{:S(2)}) collective-permute-start(bf16[1024,256]{1,0:T(8,128)(2,1)} %collective-permute-done.3), channel_id=1, source_target_pairs={{0,1},{1,0},{2,3},{3,2},{4,5},{5,4},{6,7},{7,6},{8,9},{9,8},{10,11... | collective-permute-start | bytes 1572872 | tf_op jit(solution)/shard_map/ppermute | solution.py:166
  41.2 2.2 %collective-permute-start.14 = (bf16[1024,512]{1,0:T(8,128)(2,1)S(1)}, bf16[1024,512]{1,0:T(8,128)(2,1)S(1)}, u32[]{:S(2)}, u32[]{:S(2)}) collective-permute-start(bf16[1024,512]{1,0:T(8,128)(2,1)S(1)} %join_cores.3.refs_2_), channel_id=1, source_target_pairs={{0,2},{2,4},{3,1},{4,6},{5,3},{7,5},{8,10},{10,12},{11,9},{12,14},... | collective-permute-start | bytes 3145736 | tf_op jit(solution)/shard_map/ppermute | solution.py:169
  43.5 2.2 %fusion = (bf16[4096,128]{1,0:T(8,128)(2,1)S(1)}, bf16[4096,128]{1,0:T(8,128)(2,1)S(1)}) fusion(f32[4096]{0:T(1024)S(1)} %bitcast.50, bf16[1,8192,128]{2,1,0:T(8,128)(2,1)S(1)} %copy-done.14, f32[4096]{0:T(1024)S(1)} %bitcast.51), kind=kLoop, calls=%fused_computation.10 | loop fusion | flops 3145728 | bytes 4227072 | tf_op jit(solution)/shard_map/convert_element_type | solution.py:240
  45.7 1.7 collective-permute-start.20
  47.5 1.6 collective-permute-start.21
  49.1 3.7 %collective-permute-start.11 = (bf16[1024,256]{1,0:T(8,128)(2,1)S(1)}, bf16[1024,256]{1,0:T(8,128)(2,1)S(1)}, u32[]{:S(2)}, u32[]{:S(2)}) collective-permute-start(bf16[1024,256]{1,0:T(8,128)(2,1)S(1)} %collective-permute-done.10.refs_2_), channel_id=1, source_target_pairs={{0,1},{1,0},{2,3},{3,2},{4,5},{5,4},{6,7},{7,6},{8,9},{9,8},{10,11... | collective-permute-start | bytes 1572872 | tf_op jit(solution)/shard_map/ppermute | solution.py:166
  55.6 5.3 %in_places.2.refs_2_ = bf16[1024,4096]{1,0:T(8,128)(2,1)S(1)} custom-call(s32[6]{0:T(128)S(1)} %stack.27.place_ref, bf16[1024,4096]{1,0:T(8,128)(2,1)S(1)} %bitcast.41, f32[1,4096]{1,0:T(1,128)S(1)} %bitcast.45, bf16[1024,512]{1,0:T(8,128)(2,1)S(1)} %join_cores.3.refs_2_, bf16[1024,256]{1,0:T(8,128)(2,1)S(1)} %collective-permute-done.5.refs_3_, ...), custom_call_target="tpu_custom_call" | custom-call | flops 5000000000 | bytes 1 | tf_op jit(solution)/shard_map/in_places/pallas_call | solution.py:39
  61.9 2.3 %convolution_convert_fusion.4 = bf16[1024,256]{1,0:T(8,128)(2,1)S(1)} fusion(bf16[1024,4096]{1,0:T(8,128)(2,1)S(1)} %in_places.2.refs_2_, bf16[4096,256]{1,0:T(8,128)(2,1)S(1)} %get-tuple-element.13), kind=kOutput, calls=%fused_computation.22 | convolution fusion | flops 2147745792 | bytes 11010048 | tf_op jit(solution)/shard_map/dot_general | solution.py:253
  65.0 2.3 %convolution_convert_fusion.5 = bf16[1024,256]{1,0:T(8,128)(2,1)S(1)} fusion(bf16[1024,4096]{1,0:T(8,128)(2,1)S(1)} %in_places.2.refs_2_, bf16[4096,256]{1,0:T(8,128)(2,1)S(1)} %get-tuple-element.12.refs_1_), kind=kOutput, calls=%fused_computation.23 | convolution fusion | flops 2147745792 | bytes 11010048 | tf_op jit(solution)/shard_map/dot_general | solution.py:253
  68.7 1.8 collective-permute-done.21.refs_4_
  71.1 4.9 %convolution_convert_fusion.refs_0_ = bf16[512,4096]{1,0:T(8,128)(2,1)S(1)} fusion(bf16[1024,512]{1,0:T(8,128)(2,1)S(1)} %fence.9.refs_1_, bf16[1024,4096]{1,0:T(8,128)(2,1)S(1)} %in_places.3.refs_1_), kind=kOutput, calls=%fused_computation | convolution fusion | flops 4297064448 | bytes 13631488 | tf_op jit(solution)/shard_map/dot_general | solution.py:173
  76.9 8.2 %collective-permute-start.24 = (bf16[512,1024]{1,0:T(8,128)(2,1)S(1)}, bf16[512,1024]{1,0:T(8,128)(2,1)S(1)}, u32[]{:S(2)}, u32[]{:S(2)}) collective-permute-start(bf16[512,1024]{1,0:T(8,128)(2,1)S(1)} %get-tuple-element.24), channel_id=1, source_target_pairs={{0,1},{1,0},{2,3},{3,2},{4,5},{5,4},{6,7},{7,6},{8,9},{9,8},{10,11... | collective-permute-start | bytes 3145736 | tf_op jit(solution)/shard_map/ppermute | solution.py:166
  85.9 1.2 add_convert_fusion.1
  88.7 4.6 %collective-permute-start.25 = (bf16[512,1024]{1,0:T(8,128)(2,1)S(1)}, bf16[512,1024]{1,0:T(8,128)(2,1)S(1)}, u32[]{:S(2)}, u32[]{:S(2)}) collective-permute-start(bf16[512,1024]{1,0:T(8,128)(2,1)S(1)} %add_convert_fusion.4), channel_id=1, source_target_pairs={{0,2},{7,5},{8,10},{15,13},{16,18},{23,21},{24,26},{31,29}} | collective-permute-start | bytes 3145736 | tf_op jit(solution)/shard_map/ppermute | solution.py:169
  93.4 7.9 %collective-permute-start.17 = (bf16[1024,512]{1,0:T(8,128)(2,1)S(1)}, bf16[1024,512]{1,0:T(8,128)(2,1)S(1)}, u32[]{:S(2)}, u32[]{:S(2)}) collective-permute-start(bf16[1024,512]{1,0:T(8,128)(2,1)S(1)} %collective-permute-done.16), channel_id=1, source_target_pairs={{0,1},{1,0},{2,3},{3,2},{4,5},{5,4},{6,7},{7,6},{8,9},{9,8},{10,11... | collective-permute-start | bytes 3145736 | tf_op jit(solution)/shard_map/ppermute | solution.py:166
  101.3 1.2 add_convert_fusion
  104.0 1.4 collective-permute-done.25
  106.1 4.5 %collective-permute-start.26 = (bf16[512,1024]{1,0:T(8,128)(2,1)S(1)}, bf16[512,1024]{1,0:T(8,128)(2,1)S(1)}, u32[]{:S(2)}, u32[]{:S(2)}) collective-permute-start(bf16[512,1024]{1,0:T(8,128)(2,1)S(1)} %add_convert_fusion.3), channel_id=1, source_target_pairs={{0,2},{2,4},{5,3},{7,5},{8,10},{10,12},{13,11},{15,13},{16,18},{18... | collective-permute-start | bytes 3145736 | tf_op jit(solution)/shard_map/ppermute | solution.py:169
  111.5 4.5 %convolution_convert_fusion.3.refs_0_ = bf16[1024,512]{1,0:T(8,128)(2,1)S(1)} fusion(bf16[1024,4096]{1,0:T(8,128)(2,1)S(1)} %in_places.3.refs_1_, bf16[4096,512]{1,0:T(8,128)(2,1)S(1)} %fence.11.refs_1_), kind=kOutput, calls=%fused_computation.21 | convolution fusion | flops 4295491584 | bytes 13631488 | tf_op jit(solution)/shard_map/dot_general | solution.py:265
  116.0 6.7 %collective-permute-done.26 = bf16[512,1024]{1,0:T(8,128)(2,1)S(1)} collective-permute-done((bf16[512,1024]{1,0:T(8,128)(2,1)S(1)}, bf16[512,1024]{1,0:T(8,128)(2,1)S(1)}, u32[]{:S(2)}, u32[]{:S(2)}) %collective-permute-start.26) | collective-permute-done | bytes 1048608 | tf_op jit(solution)/shard_map/ppermute | solution.py:169
  124.4 2.5 %convolution_convert_fusion.2 = bf16[256,4096]{1,0:T(8,128)(2,1)S(1)} fusion(bf16[1024,4096]{1,0:T(8,128)(2,1)S(1)} %in_places.2.refs_2_, bf16[1024,512]{1,0:T(8,128)(2,1)S(1)} %fence.12.refs_2_), kind=kOutput, calls=%fused_computation.2 | convolution fusion | flops 2148532224 | bytes 11010048 | tf_op jit(solution)/shard_map/dot_general | solution.py:173
  126.9 2.5 %convolution_convert_fusion.1 = bf16[256,4096]{1,0:T(8,128)(2,1)S(1)} fusion(bf16[1024,4096]{1,0:T(8,128)(2,1)S(1)} %in_places.2.refs_2_, bf16[1024,512]{1,0:T(8,128)(2,1)S(1)} %fence.12.refs_2_), kind=kOutput, calls=%fused_computation.1 | convolution fusion | flops 2148532224 | bytes 11010048 | tf_op jit(solution)/shard_map/dot_general | solution.py:173
  129.5 1.2 fusion.9
  132.4 4.5 %collective-permute-start.41 = (bf16[512,1024]{1,0:T(8,128)(2,1)}, bf16[512,1024]{1,0:T(8,128)(2,1)S(1)}, u32[]{:S(2)}, u32[]{:S(2)}) collective-permute-start(bf16[512,1024]{1,0:T(8,128)(2,1)} %copy-done.1), channel_id=1, source_target_pairs={{0,2},{2,4},{3,1},{4,6},{5,3},{7,5},{8,10},{10,12},{11,9},{12,14},... | collective-permute-start | bytes 3145736 | tf_op jit(solution)/shard_map/ppermute | solution.py:169
  137.0 1.4 add_convert_fusion.10.refs_3_
  139.0 1.4 add_convert_fusion.7.refs_4_
  140.4 4.1 %collective-permute-start.30 = (bf16[256,1024]{1,0:T(8,128)(2,1)S(1)}, bf16[256,1024]{1,0:T(8,128)(2,1)}, u32[]{:S(2)}, u32[]{:S(2)}) collective-permute-start(bf16[256,1024]{1,0:T(8,128)(2,1)S(1)} %add_convert_fusion.10.refs_3_), channel_id=1, source_target_pairs={{0,2},{7,5},{8,10},{15,13},{16,18},{23,21},{24,26},{31,29}} | collective-permute-start | bytes 1572872 | tf_op jit(solution)/shard_map/ppermute | solution.py:169
  144.5 2.1 %collective-permute-start.37 = (bf16[256,1024]{1,0:T(8,128)(2,1)S(1)}, bf16[256,1024]{1,0:T(8,128)(2,1)}, u32[]{:S(2)}, u32[]{:S(2)}) collective-permute-start(bf16[256,1024]{1,0:T(8,128)(2,1)S(1)} %add_convert_fusion.7.refs_4_), channel_id=1, source_target_pairs={{0,2},{7,5},{8,10},{15,13},{16,18},{23,21},{24,26},{31,29}} | collective-permute-start | bytes 1572872 | tf_op jit(solution)/shard_map/ppermute | solution.py:169
  147.1 2.2 %convert_add_fusion = (f32[4096,128]{1,0:T(8,128)S(1)}, f32[4096,128]{1,0:T(8,128)S(1)}) fusion(bf16[4096,128]{1,0:T(8,128)(2,1)S(1)} %get-tuple-element.15, bf16[4096,128]{1,0:T(8,128)(2,1)} %add_convert_fusion, bf16[4096,128]{1,0:T(8,128)(2,1)S(1)} %get-tuple-element.14, bf16[4096,128]{1,0:T(8,128)(2,1)} %add_convert_fusion.1), kind=kLoop, calls=%fused_computation.13 | loop fusion | flops 3145728 | bytes 8388608 | tf_op jit(solution)/shard_map/add | solution.py:278
  150.6 3.9 %subtract_convert_fusion = (bf16[8192,128]{1,0:T(8,128)(2,1)}, f32[8192,128]{1,0:T(8,128)}) fusion(bf16[8192,128]{1,0:T(8,128)(2,1)S(1)} %copy-done.15, f32[4096,128]{1,0:T(8,128)S(1)} %get-tuple-element.35, f32[4096,128]{1,0:T(8,128)S(1)} %get-tuple-element.36, f32[8192,128]{1,0:T(8,128)S(1)} %copy-done.13), kind=kLoop, calls=%fused_computation.5 | loop fusion | flops 10485760 | bytes 16777216 | tf_op jit(solution)/shard_map/convert_element_type | solution.py:135
  155.1 1.5 add_convert_fusion.9
  156.7 4.3 %collective-permute-start.31 = (bf16[256,1024]{1,0:T(8,128)(2,1)S(1)}, bf16[256,1024]{1,0:T(8,128)(2,1)S(1)}, u32[]{:S(2)}, u32[]{:S(2)}) collective-permute-start(bf16[256,1024]{1,0:T(8,128)(2,1)S(1)} %add_convert_fusion.9), channel_id=1, source_target_pairs={{0,2},{2,4},{5,3},{7,5},{8,10},{10,12},{13,11},{15,13},{16,18},{18... | collective-permute-start | bytes 1572872 | tf_op jit(solution)/shard_map/ppermute | solution.py:169
  161.0 1.5 add_convert_fusion.6
  162.5 4.1 %collective-permute-start.38 = (bf16[256,1024]{1,0:T(8,128)(2,1)S(1)}, bf16[256,1024]{1,0:T(8,128)(2,1)S(1)}, u32[]{:S(2)}, u32[]{:S(2)}) collective-permute-start(bf16[256,1024]{1,0:T(8,128)(2,1)S(1)} %add_convert_fusion.6), channel_id=1, source_target_pairs={{0,2},{2,4},{5,3},{7,5},{8,10},{10,12},{13,11},{15,13},{16,18},{18... | collective-permute-start | bytes 1572872 | tf_op jit(solution)/shard_map/ppermute | solution.py:169
  166.6 1.6 convert_add_fusion.2
  168.5 3.8 %collective-permute-start.32 = (bf16[256,1024]{1,0:T(8,128)(2,1)S(1)}, bf16[256,1024]{1,0:T(8,128)(2,1)S(1)}, u32[]{:S(2)}, u32[]{:S(2)}) collective-permute-start(bf16[256,1024]{1,0:T(8,128)(2,1)S(1)} %add_convert_fusion.8), channel_id=1, source_target_pairs={{0,2},{2,4},{3,1},{4,6},{5,3},{7,5},{8,10},{10,12},{11,9},{12,14},... | collective-permute-start | bytes 1572872 | tf_op jit(solution)/shard_map/ppermute | solution.py:169
  173.5 4.4 %collective-permute-start.39 = (bf16[256,1024]{1,0:T(8,128)(2,1)S(1)}, bf16[256,1024]{1,0:T(8,128)(2,1)S(1)}, u32[]{:S(2)}, u32[]{:S(2)}) collective-permute-start(bf16[256,1024]{1,0:T(8,128)(2,1)S(1)} %add_convert_fusion.5), channel_id=1, source_target_pairs={{0,2},{2,4},{3,1},{4,6},{5,3},{7,5},{8,10},{10,12},{11,9},{12,14},... | collective-permute-start | bytes 1572872 | tf_op jit(solution)/shard_map/ppermute | solution.py:169
  179.9 4.7 %collective-permute-done.39 = bf16[256,1024]{1,0:T(8,128)(2,1)S(1)} collective-permute-done((bf16[256,1024]{1,0:T(8,128)(2,1)S(1)}, bf16[256,1024]{1,0:T(8,128)(2,1)S(1)}, u32[]{:S(2)}, u32[]{:S(2)}) %collective-permute-start.39) | collective-permute-done | bytes 524320 | tf_op jit(solution)/shard_map/ppermute | solution.py:169
  185.8 1.3 copy.25
  188.6 1.3 copy.24
  (150 shorter events, 31.9 us)
Async XLA Ops:
  1.4 2.2 %collective-permute-start.1 = (bf16[512,512]{1,0:T(8,128)(2,1)}, bf16[512,512]{1,0:T(8,128)(2,1)S(1)}, u32[]{:S(2)}, u32[]{:S(2)}) collective-permute-start(bf16[512,512]{1,0:T(8,128)(2,1)} %bitcast.48), channel_id=1, source_target_pairs={{0,1},{1,0},{2,3},{3,2},{4,5},{5,4},{6,7},{7,6},{8,9},{9,8},{10,11... | collective-permute-start | bytes 1572872 | tf_op jit(solution)/shard_map/ppermute | solution.py:166
  1.8 2.5 %collective-permute-start = (bf16[512,512]{1,0:T(8,128)(2,1)}, bf16[512,512]{1,0:T(8,128)(2,1)S(1)}, u32[]{:S(2)}, u32[]{:S(2)}) collective-permute-start(bf16[512,512]{1,0:T(8,128)(2,1)} %bitcast.46), channel_id=1, source_target_pairs={{0,1},{1,0},{2,3},{3,2},{4,5},{5,4},{6,7},{7,6},{8,9},{9,8},{10,11... | collective-permute-start | bytes 1572872 | tf_op jit(solution)/shard_map/ppermute | solution.py:166
  6.1 34.5 %copy-start.4 = (bf16[1,512,512]{2,1,0:T(8,128)(2,1)S(1)}, bf16[1,512,512]{2,1,0:T(8,128)(2,1)}, u32[]{:S(2)}) copy-start(bf16[1,512,512]{2,1,0:T(8,128)(2,1)} %param.12) | copy-start | bytes 1572868
  6.1 11.7 %collective-permute-start.8 = (bf16[1024,256]{1,0:T(8,128)(2,1)S(1)}, bf16[1024,256]{1,0:T(8,128)(2,1)}, u32[]{:S(2)}, u32[]{:S(2)}) collective-permute-start(bf16[1024,256]{1,0:T(8,128)(2,1)S(1)} %get-tuple-element.11), channel_id=1, source_target_pairs={{0,2},{2,4},{3,1},{4,6},{5,3},{7,5},{8,10},{10,12},{11,9},{12,14},... | collective-permute-start | bytes 1572872 | tf_op jit(solution)/shard_map/ppermute | solution.py:169
  11.9 11.5 %collective-permute-start.2 = (bf16[1024,256]{1,0:T(8,128)(2,1)S(1)}, bf16[1024,256]{1,0:T(8,128)(2,1)S(1)}, u32[]{:S(2)}, u32[]{:S(2)}) collective-permute-start(bf16[1024,256]{1,0:T(8,128)(2,1)S(1)} %get-tuple-element.10.refs_1_), channel_id=1, source_target_pairs={{0,2},{2,4},{3,1},{4,6},{5,3},{7,5},{8,10},{10,12},{11,9},{12,14},... | collective-permute-start | bytes 1572872 | tf_op jit(solution)/shard_map/ppermute | solution.py:169
  17.7 7.1 %collective-permute-start.9 = (bf16[1024,256]{1,0:T(8,128)(2,1)}, bf16[1024,256]{1,0:T(8,128)(2,1)}, u32[]{:S(2)}, u32[]{:S(2)}) collective-permute-start(bf16[1024,256]{1,0:T(8,128)(2,1)} %collective-permute-done.8), channel_id=1, source_target_pairs={{2,4},{3,1},{4,6},{5,3},{10,12},{11,9},{12,14},{13,11},{18,20},{19... | collective-permute-start | bytes 1572872 | tf_op jit(solution)/shard_map/ppermute | solution.py:169
  23.4 7.3 %collective-permute-start.3 = (bf16[1024,256]{1,0:T(8,128)(2,1)S(1)}, bf16[1024,256]{1,0:T(8,128)(2,1)}, u32[]{:S(2)}, u32[]{:S(2)}) collective-permute-start(bf16[1024,256]{1,0:T(8,128)(2,1)S(1)} %collective-permute-done.2), channel_id=1, source_target_pairs={{2,4},{3,1},{4,6},{5,3},{10,12},{11,9},{12,14},{13,11},{18,20},{19... | collective-permute-start | bytes 1572872 | tf_op jit(solution)/shard_map/ppermute | solution.py:169
  24.8 6.5 %collective-permute-start.10 = (bf16[1024,256]{1,0:T(8,128)(2,1)}, bf16[1024,256]{1,0:T(8,128)(2,1)S(1)}, u32[]{:S(2)}, u32[]{:S(2)}) collective-permute-start(bf16[1024,256]{1,0:T(8,128)(2,1)} %collective-permute-done.9), channel_id=1, source_target_pairs={{3,1},{4,6},{11,9},{12,14},{19,17},{20,22},{27,25},{28,30}} | collective-permute-start | bytes 1572872 | tf_op jit(solution)/shard_map/ppermute | solution.py:169
  25.5 20.1 %collective-permute-start.13 = (bf16[1024,256]{1,0:T(8,128)(2,1)}, bf16[1024,256]{1,0:T(8,128)(2,1)S(1)}, u32[]{:S(2)}, u32[]{:S(2)}) collective-permute-start(bf16[1024,256]{1,0:T(8,128)(2,1)} %collective-permute-done.8), channel_id=1, source_target_pairs={{0,1},{1,0},{2,3},{3,2},{4,5},{5,4},{6,7},{7,6},{8,9},{9,8},{10,11... | collective-permute-start | bytes 1572872 | tf_op jit(solution)/shard_map/ppermute | solution.py:166
  30.2 17.3 %collective-permute-start.7 = (bf16[1024,256]{1,0:T(8,128)(2,1)S(1)}, bf16[1024,256]{1,0:T(8,128)(2,1)S(1)}, u32[]{:S(2)}, u32[]{:S(2)}) collective-permute-start(bf16[1024,256]{1,0:T(8,128)(2,1)S(1)} %collective-permute-done.2), channel_id=1, source_target_pairs={{0,1},{1,0},{2,3},{3,2},{4,5},{5,4},{6,7},{7,6},{8,9},{9,8},{10,11... | collective-permute-start | bytes 1572872 | tf_op jit(solution)/shard_map/ppermute | solution.py:166
  30.3 18.9 %collective-permute-start.12 = (bf16[1024,256]{1,0:T(8,128)(2,1)}, bf16[1024,256]{1,0:T(8,128)(2,1)S(1)}, u32[]{:S(2)}, u32[]{:S(2)}) collective-permute-start(bf16[1024,256]{1,0:T(8,128)(2,1)} %collective-permute-done.9), channel_id=1, source_target_pairs={{0,1},{1,0},{2,3},{3,2},{4,5},{5,4},{6,7},{7,6},{8,9},{9,8},{10,11... | collective-permute-start | bytes 1572872 | tf_op jit(solution)/shard_map/ppermute | solution.py:166
  30.7 9.9 %collective-permute-start.4 = (bf16[1024,256]{1,0:T(8,128)(2,1)}, bf16[1024,256]{1,0:T(8,128)(2,1)S(1)}, u32[]{:S(2)}, u32[]{:S(2)}) collective-permute-start(bf16[1024,256]{1,0:T(8,128)(2,1)} %collective-permute-done.3), channel_id=1, source_target_pairs={{3,1},{4,6},{11,9},{12,14},{19,17},{20,22},{27,25},{28,30}} | collective-permute-start | bytes 1572872 | tf_op jit(solution)/shard_map/ppermute | solution.py:169
  31.4 21.6 %collective-permute-start.6 = (bf16[1024,256]{1,0:T(8,128)(2,1)}, bf16[1024,256]{1,0:T(8,128)(2,1)S(1)}, u32[]{:S(2)}, u32[]{:S(2)}) collective-permute-start(bf16[1024,256]{1,0:T(8,128)(2,1)} %collective-permute-done.3), channel_id=1, source_target_pairs={{0,1},{1,0},{2,3},{3,2},{4,5},{5,4},{6,7},{7,6},{8,9},{9,8},{10,11... | collective-permute-start | bytes 1572872 | tf_op jit(solution)/shard_map/ppermute | solution.py:166
  40.6 15.0 %slice-start = ((s8[8388608]{0:T(1024)(128)(4,1)}), s8[4194304]{0:T(1024)(128)(4,1)S(1)}, s32[]{:S(2)}) async-start(s8[8388608]{0:T(1024)(128)(4,1)} %bitcast.39), calls=%async_computation | async-start | bytes 8388608
  41.2 20.1 %collective-permute-start.14 = (bf16[1024,512]{1,0:T(8,128)(2,1)S(1)}, bf16[1024,512]{1,0:T(8,128)(2,1)S(1)}, u32[]{:S(2)}, u32[]{:S(2)}) collective-permute-start(bf16[1024,512]{1,0:T(8,128)(2,1)S(1)} %join_cores.3.refs_2_), channel_id=1, source_target_pairs={{0,2},{2,4},{3,1},{4,6},{5,3},{7,5},{8,10},{10,12},{11,9},{12,14},... | collective-permute-start | bytes 3145736 | tf_op jit(solution)/shard_map/ppermute | solution.py:169
  45.7 23.0 %collective-permute-start.20 = (bf16[4096,128]{1,0:T(8,128)(2,1)S(1)}, bf16[4096,128]{1,0:T(8,128)(2,1)S(1)}, u32[]{:S(2)}, u32[]{:S(2)}) collective-permute-start(bf16[4096,128]{1,0:T(8,128)(2,1)S(1)} %get-tuple-element.32), channel_id=1, source_target_pairs={{0,8},{8,0},{16,24},{24,16},{1,9},{9,1},{17,25},{25,17},{2,10},{10... | collective-permute-start | bytes 3145736 | tf_op jit(solution)/shard_map/ppermute | solution.py:242
  47.5 23.1 %collective-permute-start.21 = (bf16[4096,128]{1,0:T(8,128)(2,1)S(1)}, bf16[4096,128]{1,0:T(8,128)(2,1)S(1)}, u32[]{:S(2)}, u32[]{:S(2)}) collective-permute-start(bf16[4096,128]{1,0:T(8,128)(2,1)S(1)} %get-tuple-element.31), channel_id=1, source_target_pairs={{0,16},{8,24},{16,0},{24,8},{1,17},{9,25},{17,1},{25,9},{2,18},{10... | collective-permute-start | bytes 3145736 | tf_op jit(solution)/shard_map/ppermute | solution.py:242
  49.1 5.3 %collective-permute-start.11 = (bf16[1024,256]{1,0:T(8,128)(2,1)S(1)}, bf16[1024,256]{1,0:T(8,128)(2,1)S(1)}, u32[]{:S(2)}, u32[]{:S(2)}) collective-permute-start(bf16[1024,256]{1,0:T(8,128)(2,1)S(1)} %collective-permute-done.10.refs_2_), channel_id=1, source_target_pairs={{0,1},{1,0},{2,3},{3,2},{4,5},{5,4},{6,7},{7,6},{8,9},{9,8},{10,11... | collective-permute-start | bytes 1572872 | tf_op jit(solution)/shard_map/ppermute | solution.py:166
  52.9 2.7 %collective-permute-start.5 = (bf16[1024,256]{1,0:T(8,128)(2,1)S(1)}, bf16[1024,256]{1,0:T(8,128)(2,1)S(1)}, u32[]{:S(2)}, u32[]{:S(2)}) collective-permute-start(bf16[1024,256]{1,0:T(8,128)(2,1)S(1)} %collective-permute-done.4.refs_3_), channel_id=1, source_target_pairs={{0,1},{1,0},{2,3},{3,2},{4,5},{5,4},{6,7},{7,6},{8,9},{9,8},{10,11... | collective-permute-start | bytes 1572872 | tf_op jit(solution)/shard_map/ppermute | solution.py:166
  64.3 11.8 %collective-permute-start.15 = (bf16[1024,512]{1,0:T(8,128)(2,1)S(1)}, bf16[1024,512]{1,0:T(8,128)(2,1)S(1)}, u32[]{:S(2)}, u32[]{:S(2)}) collective-permute-start(bf16[1024,512]{1,0:T(8,128)(2,1)S(1)} %collective-permute-done.14.refs_3_.refs_2_), channel_id=1, source_target_pairs={{2,4},{3,1},{4,6},{5,3},{10,12},{11,9},{12,14},{13,11},{18,20},{19... | collective-permute-start | bytes 3145736 | tf_op jit(solution)/shard_map/ppermute | solution.py:169
  76.6 46.2 %copy-start = (bf16[512,4096]{1,0:T(8,128)(2,1)}, bf16[512,4096]{1,0:T(8,128)(2,1)S(1)}, u32[]{:S(2)}) copy-start(bf16[512,4096]{1,0:T(8,128)(2,1)S(1)} %fence.10.refs_1_) | copy-start | bytes 12582916
  76.9 11.4 %collective-permute-start.24 = (bf16[512,1024]{1,0:T(8,128)(2,1)S(1)}, bf16[512,1024]{1,0:T(8,128)(2,1)S(1)}, u32[]{:S(2)}, u32[]{:S(2)}) collective-permute-start(bf16[512,1024]{1,0:T(8,128)(2,1)S(1)} %get-tuple-element.24), channel_id=1, source_target_pairs={{0,1},{1,0},{2,3},{3,2},{4,5},{5,4},{6,7},{7,6},{8,9},{9,8},{10,11... | collective-permute-start | bytes 3145736 | tf_op jit(solution)/shard_map/ppermute | solution.py:166
  85.1 17.4 %collective-permute-start.19 = (bf16[1024,512]{1,0:T(8,128)(2,1)S(1)}, bf16[1024,512]{1,0:T(8,128)(2,1)S(1)}, u32[]{:S(2)}, u32[]{:S(2)}) collective-permute-start(bf16[1024,512]{1,0:T(8,128)(2,1)S(1)} %collective-permute-done.14.refs_3_.refs_2_), channel_id=1, source_target_pairs={{0,1},{1,0},{2,3},{3,2},{4,5},{5,4},{6,7},{7,6},{8,9},{9,8},{10,11... | collective-permute-start | bytes 3145736 | tf_op jit(solution)/shard_map/ppermute | solution.py:166
  85.2 8.2 %collective-permute-start.16 = (bf16[1024,512]{1,0:T(8,128)(2,1)S(1)}, bf16[1024,512]{1,0:T(8,128)(2,1)S(1)}, u32[]{:S(2)}, u32[]{:S(2)}) collective-permute-start(bf16[1024,512]{1,0:T(8,128)(2,1)S(1)} %collective-permute-done.15.refs_2_), channel_id=1, source_target_pairs={{3,1},{4,6},{11,9},{12,14},{19,17},{20,22},{27,25},{28,30}} | collective-permute-start | bytes 3145736 | tf_op jit(solution)/shard_map/ppermute | solution.py:169
  87.2 16.8 %collective-permute-start.23 = (bf16[512,1024]{1,0:T(8,128)(2,1)S(1)}, bf16[512,1024]{1,0:T(8,128)(2,1)S(1)}, u32[]{:S(2)}, u32[]{:S(2)}) collective-permute-start(bf16[512,1024]{1,0:T(8,128)(2,1)S(1)} %get-tuple-element.23), channel_id=1, source_target_pairs={{0,1},{1,0},{2,3},{3,2},{4,5},{5,4},{6,7},{7,6},{8,9},{9,8},{10,11... | collective-permute-start | bytes 3145736 | tf_op jit(solution)/shard_map/ppermute | solution.py:166
  88.3 14.9 %collective-permute-start.18 = (bf16[1024,512]{1,0:T(8,128)(2,1)S(1)}, bf16[1024,512]{1,0:T(8,128)(2,1)S(1)}, u32[]{:S(2)}, u32[]{:S(2)}) collective-permute-start(bf16[1024,512]{1,0:T(8,128)(2,1)S(1)} %collective-permute-done.15.refs_2_), channel_id=1, source_target_pairs={{0,1},{1,0},{2,3},{3,2},{4,5},{5,4},{6,7},{7,6},{8,9},{9,8},{10,11... | collective-permute-start | bytes 3145736 | tf_op jit(solution)/shard_map/ppermute | solution.py:166
  88.7 16.7 %collective-permute-start.25 = (bf16[512,1024]{1,0:T(8,128)(2,1)S(1)}, bf16[512,1024]{1,0:T(8,128)(2,1)S(1)}, u32[]{:S(2)}, u32[]{:S(2)}) collective-permute-start(bf16[512,1024]{1,0:T(8,128)(2,1)S(1)} %add_convert_fusion.4), channel_id=1, source_target_pairs={{0,2},{7,5},{8,10},{15,13},{16,18},{23,21},{24,26},{31,29}} | collective-permute-start | bytes 3145736 | tf_op jit(solution)/shard_map/ppermute | solution.py:169
  93.4 17.2 %collective-permute-start.17 = (bf16[1024,512]{1,0:T(8,128)(2,1)S(1)}, bf16[1024,512]{1,0:T(8,128)(2,1)S(1)}, u32[]{:S(2)}, u32[]{:S(2)}) collective-permute-start(bf16[1024,512]{1,0:T(8,128)(2,1)S(1)} %collective-permute-done.16), channel_id=1, source_target_pairs={{0,1},{1,0},{2,3},{3,2},{4,5},{5,4},{6,7},{7,6},{8,9},{9,8},{10,11... | collective-permute-start | bytes 3145736 | tf_op jit(solution)/shard_map/ppermute | solution.py:166
  102.5 37.8 %collective-permute-start.43 = (bf16[4096,128]{1,0:T(8,128)(2,1)}, bf16[4096,128]{1,0:T(8,128)(2,1)S(1)}, u32[]{:S(2)}, u32[]{:S(2)}) collective-permute-start(bf16[4096,128]{1,0:T(8,128)(2,1)} %add_convert_fusion.1), channel_id=1, source_target_pairs={{0,16},{8,24},{16,0},{24,8},{1,17},{9,25},{17,1},{25,9},{2,18},{10... | collective-permute-start | bytes 3145736 | tf_op jit(solution)/shard_map/ppermute | solution.py:242
  103.2 41.3 %collective-permute-start.44 = (bf16[4096,128]{1,0:T(8,128)(2,1)}, bf16[4096,128]{1,0:T(8,128)(2,1)S(1)}, u32[]{:S(2)}, u32[]{:S(2)}) collective-permute-start(bf16[4096,128]{1,0:T(8,128)(2,1)} %add_convert_fusion), channel_id=1, source_target_pairs={{0,8},{8,0},{16,24},{24,16},{1,9},{9,1},{17,25},{25,17},{2,10},{10... | collective-permute-start | bytes 3145736 | tf_op jit(solution)/shard_map/ppermute | solution.py:242
  103.9 12.1 %collective-permute-start.22 = (bf16[512,1024]{1,0:T(8,128)(2,1)S(1)}, bf16[512,1024]{1,0:T(8,128)(2,1)S(1)}, u32[]{:S(2)}, u32[]{:S(2)}) collective-permute-start(bf16[512,1024]{1,0:T(8,128)(2,1)S(1)} %get-tuple-element.22), channel_id=1, source_target_pairs={{0,1},{1,0},{2,3},{3,2},{4,5},{5,4},{6,7},{7,6},{8,9},{9,8},{10,11... | collective-permute-start | bytes 3145736 | tf_op jit(solution)/shard_map/ppermute | solution.py:166
  106.1 16.7 %collective-permute-start.26 = (bf16[512,1024]{1,0:T(8,128)(2,1)S(1)}, bf16[512,1024]{1,0:T(8,128)(2,1)S(1)}, u32[]{:S(2)}, u32[]{:S(2)}) collective-permute-start(bf16[512,1024]{1,0:T(8,128)(2,1)S(1)} %add_convert_fusion.3), channel_id=1, source_target_pairs={{0,2},{2,4},{5,3},{7,5},{8,10},{10,12},{13,11},{15,13},{16,18},{18... | collective-permute-start | bytes 3145736 | tf_op jit(solution)/shard_map/ppermute | solution.py:169
  130.7 6.2 %collective-permute-start.29 = (bf16[256,1024]{1,0:T(8,128)(2,1)}, bf16[256,1024]{1,0:T(8,128)(2,1)}, u32[]{:S(2)}, u32[]{:S(2)}) collective-permute-start(bf16[256,1024]{1,0:T(8,128)(2,1)} %get-tuple-element.27), channel_id=1, source_target_pairs={{0,1},{1,0},{2,3},{3,2},{4,5},{5,4},{6,7},{7,6},{8,9},{9,8},{10,11... | collective-permute-start | bytes 1572872 | tf_op jit(solution)/shard_map/ppermute | solution.py:166
  132.0 6.4 %collective-permute-start.36 = (bf16[256,1024]{1,0:T(8,128)(2,1)}, bf16[256,1024]{1,0:T(8,128)(2,1)}, u32[]{:S(2)}, u32[]{:S(2)}) collective-permute-start(bf16[256,1024]{1,0:T(8,128)(2,1)} %get-tuple-element.30), channel_id=1, source_target_pairs={{0,1},{1,0},{2,3},{3,2},{4,5},{5,4},{6,7},{7,6},{8,9},{9,8},{10,11... | collective-permute-start | bytes 1572872 | tf_op jit(solution)/shard_map/ppermute | solution.py:166
  132.4 34.2 %collective-permute-start.41 = (bf16[512,1024]{1,0:T(8,128)(2,1)}, bf16[512,1024]{1,0:T(8,128)(2,1)S(1)}, u32[]{:S(2)}, u32[]{:S(2)}) collective-permute-start(bf16[512,1024]{1,0:T(8,128)(2,1)} %copy-done.1), channel_id=1, source_target_pairs={{0,2},{2,4},{3,1},{4,6},{5,3},{7,5},{8,10},{10,12},{11,9},{12,14},... | collective-permute-start | bytes 3145736 | tf_op jit(solution)/shard_map/ppermute | solution.py:169
  136.9 17.6 %collective-permute-start.28 = (bf16[256,1024]{1,0:T(8,128)(2,1)}, bf16[256,1024]{1,0:T(8,128)(2,1)}, u32[]{:S(2)}, u32[]{:S(2)}) collective-permute-start(bf16[256,1024]{1,0:T(8,128)(2,1)} %get-tuple-element.26), channel_id=1, source_target_pairs={{0,1},{1,0},{2,3},{3,2},{4,5},{5,4},{6,7},{7,6},{8,9},{9,8},{10,11... | collective-permute-start | bytes 1572872 | tf_op jit(solution)/shard_map/ppermute | solution.py:166
  138.4 18.2 %collective-permute-start.35 = (bf16[256,1024]{1,0:T(8,128)(2,1)}, bf16[256,1024]{1,0:T(8,128)(2,1)}, u32[]{:S(2)}, u32[]{:S(2)}) collective-permute-start(bf16[256,1024]{1,0:T(8,128)(2,1)} %get-tuple-element.29), channel_id=1, source_target_pairs={{0,1},{1,0},{2,3},{3,2},{4,5},{5,4},{6,7},{7,6},{8,9},{9,8},{10,11... | collective-permute-start | bytes 1572872 | tf_op jit(solution)/shard_map/ppermute | solution.py:166
  140.4 14.6 %collective-permute-start.30 = (bf16[256,1024]{1,0:T(8,128)(2,1)S(1)}, bf16[256,1024]{1,0:T(8,128)(2,1)}, u32[]{:S(2)}, u32[]{:S(2)}) collective-permute-start(bf16[256,1024]{1,0:T(8,128)(2,1)S(1)} %add_convert_fusion.10.refs_3_), channel_id=1, source_target_pairs={{0,2},{7,5},{8,10},{15,13},{16,18},{23,21},{24,26},{31,29}} | collective-permute-start | bytes 1572872 | tf_op jit(solution)/shard_map/ppermute | solution.py:169
  144.5 16.5 %collective-permute-start.37 = (bf16[256,1024]{1,0:T(8,128)(2,1)S(1)}, bf16[256,1024]{1,0:T(8,128)(2,1)}, u32[]{:S(2)}, u32[]{:S(2)}) collective-permute-start(bf16[256,1024]{1,0:T(8,128)(2,1)S(1)} %add_convert_fusion.7.refs_4_), channel_id=1, source_target_pairs={{0,2},{7,5},{8,10},{15,13},{16,18},{23,21},{24,26},{31,29}} | collective-permute-start | bytes 1572872 | tf_op jit(solution)/shard_map/ppermute | solution.py:169
  154.5 13.7 %collective-permute-start.27 = (bf16[256,1024]{1,0:T(8,128)(2,1)S(1)}, bf16[256,1024]{1,0:T(8,128)(2,1)S(1)}, u32[]{:S(2)}, u32[]{:S(2)}) collective-permute-start(bf16[256,1024]{1,0:T(8,128)(2,1)S(1)} %copy-done.17), channel_id=1, source_target_pairs={{0,1},{1,0},{2,3},{3,2},{4,5},{5,4},{6,7},{7,6},{8,9},{9,8},{10,11... | collective-permute-start | bytes 1572872 | tf_op jit(solution)/shard_map/ppermute | solution.py:166
  155.0 17.4 %collective-permute-start.34 = (bf16[256,1024]{1,0:T(8,128)(2,1)S(1)}, bf16[256,1024]{1,0:T(8,128)(2,1)S(1)}, u32[]{:S(2)}, u32[]{:S(2)}) collective-permute-start(bf16[256,1024]{1,0:T(8,128)(2,1)S(1)} %copy-done.16), channel_id=1, source_target_pairs={{0,1},{1,0},{2,3},{3,2},{4,5},{5,4},{6,7},{7,6},{8,9},{9,8},{10,11... | collective-permute-start | bytes 1572872 | tf_op jit(solution)/shard_map/ppermute | solution.py:166
  156.7 11.6 %collective-permute-start.31 = (bf16[256,1024]{1,0:T(8,128)(2,1)S(1)}, bf16[256,1024]{1,0:T(8,128)(2,1)S(1)}, u32[]{:S(2)}, u32[]{:S(2)}) collective-permute-start(bf16[256,1024]{1,0:T(8,128)(2,1)S(1)} %add_convert_fusion.9), channel_id=1, source_target_pairs={{0,2},{2,4},{5,3},{7,5},{8,10},{10,12},{13,11},{15,13},{16,18},{18... | collective-permute-start | bytes 1572872 | tf_op jit(solution)/shard_map/ppermute | solution.py:169
  162.5 10.8 %collective-permute-start.38 = (bf16[256,1024]{1,0:T(8,128)(2,1)S(1)}, bf16[256,1024]{1,0:T(8,128)(2,1)S(1)}, u32[]{:S(2)}, u32[]{:S(2)}) collective-permute-start(bf16[256,1024]{1,0:T(8,128)(2,1)S(1)} %add_convert_fusion.6), channel_id=1, source_target_pairs={{0,2},{2,4},{5,3},{7,5},{8,10},{10,12},{13,11},{15,13},{16,18},{18... | collective-permute-start | bytes 1572872 | tf_op jit(solution)/shard_map/ppermute | solution.py:169
  168.5 10.5 %collective-permute-start.32 = (bf16[256,1024]{1,0:T(8,128)(2,1)S(1)}, bf16[256,1024]{1,0:T(8,128)(2,1)S(1)}, u32[]{:S(2)}, u32[]{:S(2)}) collective-permute-start(bf16[256,1024]{1,0:T(8,128)(2,1)S(1)} %add_convert_fusion.8), channel_id=1, source_target_pairs={{0,2},{2,4},{3,1},{4,6},{5,3},{7,5},{8,10},{10,12},{11,9},{12,14},... | collective-permute-start | bytes 1572872 | tf_op jit(solution)/shard_map/ppermute | solution.py:169
  173.5 11.1 %collective-permute-start.39 = (bf16[256,1024]{1,0:T(8,128)(2,1)S(1)}, bf16[256,1024]{1,0:T(8,128)(2,1)S(1)}, u32[]{:S(2)}, u32[]{:S(2)}) collective-permute-start(bf16[256,1024]{1,0:T(8,128)(2,1)S(1)} %add_convert_fusion.5), channel_id=1, source_target_pairs={{0,2},{2,4},{3,1},{4,6},{5,3},{7,5},{8,10},{10,12},{11,9},{12,14},... | collective-permute-start | bytes 1572872 | tf_op jit(solution)/shard_map/ppermute | solution.py:169
  178.1 7.5 %collective-permute-start.42 = (bf16[512,512]{1,0:T(8,128)(2,1)S(1)}, bf16[512,512]{1,0:T(8,128)(2,1)S(1)}, u32[]{:S(2)}, u32[]{:S(2)}) collective-permute-start(bf16[512,512]{1,0:T(8,128)(2,1)S(1)} %select_convert_fusion), channel_id=1, source_target_pairs={{0,1},{1,0},{2,3},{3,2},{4,5},{5,4},{6,7},{7,6},{8,9},{9,8},{10,11... | collective-permute-start | bytes 1572872 | tf_op jit(solution)/shard_map/ppermute | solution.py:166
  179.9 7.2 %collective-permute-start.33 = (bf16[256,512]{1,0:T(8,128)(2,1)}, bf16[256,512]{1,0:T(8,128)(2,1)S(1)}, u32[]{:S(2)}, u32[]{:S(2)}) collective-permute-start(bf16[256,512]{1,0:T(8,128)(2,1)} %select_convert_fusion.2), channel_id=1, source_target_pairs={{0,1},{1,0},{2,3},{3,2},{4,5},{5,4},{6,7},{7,6},{8,9},{9,8},{10,11... | collective-permute-start | bytes 786440 | tf_op jit(solution)/shard_map/ppermute | solution.py:166
  185.5 1.9 collective-permute-start.40
  (19 other events, 100.2 us)
